TPU v7x, 32 devices: a whole 2x2x4 slice. The times are simulated.
32 devices in a mesh: groups: 2 (over y), slab: 4 (over z), probe: 2 (over x), sub: 2 (over core).
Axes of the slice: x: 2, y: 2, z: 4, core: 2. Of those that a mesh axis runs over, the one named last changes fastest.
Arguments:
- probes: bfloat16 [64, 16, 48, 512], P(('groups', 'slab'), 'sub', None, 'probe'), parts along dimension 0, may hold values from -6 to 6
- courant: float32 [32, 16, 48], P('slab', 'sub'), may hold values from 0.05 to 0.19
- source: float32 [4, 64, 16, 48], P(None, ('groups', 'slab'), 'sub'), parts along dimension 1, may hold values from -48 to 48, as said below
Outputs:
- coupling: float32 [1024, 512], P(('groups', 'slab')), parts along dimension 0
- norms: float32 [1024], P(('groups', 'slab')), parts along dimension 0
There are 2 independent parts, one for each index of `groups`. A program takes and returns all parts, laid end to end along the dimension named above; an argument that names none is the same for every part. Nothing has to cross between parts.
Inputs may be any that keep to these rules, and one draw needn't show every extreme that they name: A signed background source, of a scale that varies smoothly over the grid.
All inputs are finite; a program needn't handle non-finite values.
Results may differ from a plain program's by a relative error of at most 0.003.
Values may be sent and summed in bfloat16 or wider, within the bound.
No kernel may reach another device: no remote copies, remote signals or barrier semaphores. Data moves between devices by JAX's collectives and lax.ppermute only.
A program may use at most 128 MiB of HBM per device.

v0:
```python
import math

import jax
import jax.numpy as jnp
from jax import lax
from jax.sharding import PartitionSpec as P

COEFFICIENTS = (-205.0 / 72.0, 8.0 / 5.0, -1.0 / 5.0, 8.0 / 315.0, -1.0 / 560.0)
EPSILON = 1e-06


def extended(x, sides, width):
    for axis, dim in sides:
        count, length = (lax.axis_size(axis), x.shape[dim])
        up = [(i, (i + 1) % count) for i in range(count - 1)]
        down = [(j, i) for i, j in up]
        last = lax.slice_in_dim(x, length - width, length, axis=dim)
        first = lax.slice_in_dim(x, 0, width, axis=dim)
        before = lax.ppermute(last, axis, up)
        after = lax.ppermute(first, axis, down)
        x = jnp.concatenate([before, x, after], axis=dim)
    return x


def stencil(current, padded):
    depth_cells, across, along_cells = (current.shape[0], current.shape[1], current.shape[2])
    sideways = jnp.pad(current, ((0, 0), (0, 0), (4, 4), (0, 0)))
    summed = 3.0 * COEFFICIENTS[0] * current
    for distance in range(1, 5):
        pair_deep = (
            padded[4 + distance : 4 + distance + depth_cells, 4 : 4 + across]
            + padded[4 - distance : 4 - distance + depth_cells, 4 : 4 + across]
        )
        pair_wide = (
            padded[4 : 4 + depth_cells, 4 + distance : 4 + distance + across]
            + padded[4 : 4 + depth_cells, 4 - distance : 4 - distance + across]
        )
        pair_long = (
            sideways[:, :, 4 + distance : 4 + distance + along_cells]
            + sideways[:, :, 4 - distance : 4 - distance + along_cells]
        )
        summed = summed + COEFFICIENTS[distance] * (pair_deep + pair_wide + pair_long)
    return summed


def laplace_shared(current):
    padded = extended(current, (("slab", 0), ("sub", 1)), 4)
    return stencil(current, padded)


def propagate(probe_block, courant, source, operator):
    previous = jnp.zeros(probe_block.shape, jnp.float32)
    current = source[0][..., None] * probe_block
    for moment in range(1, source.shape[0]):
        upcoming = (
            2.0 * current
            - previous
            + courant[..., None] * operator(current)
            + source[moment][..., None] * probe_block
        )
        previous, current = (current, upcoming)
    return current.astype(jnp.bfloat16)


def shards(probes, courant, source):
    depth_cells, across, along_cells, batch_size = probes.shape
    fields = propagate(probes, courant, source, laplace_shared)
    local_rows = depth_cells * across * along_cells
    transposed = jnp.transpose(fields, (3, 2, 0, 1)).reshape(batch_size, local_rows)
    quarters = lax.all_to_all(transposed, "probe", split_axis=1, concat_axis=0, tiled=True)
    all_probes = quarters.shape[0]
    rows_out = all_probes // lax.axis_size("slab")
    own_panel = lax.all_to_all(quarters, "slab", split_axis=0, concat_axis=1, tiled=True)
    product_tile = lax.dot_general(
        own_panel,
        lax.all_gather(own_panel, "slab", axis=0, tiled=True),
        (((1,), (1,)), ((), ())),
        preferred_element_type=jnp.float32,
    )
    gram_rows = lax.psum(product_tile, ("probe", "sub"))
    own_start = lax.axis_index("slab") * rows_out
    own_block = lax.dynamic_slice_in_dim(gram_rows, own_start, rows_out, 1)
    cell_count = local_rows * lax.axis_size("slab") * lax.axis_size("sub")
    own_norms = jnp.sqrt(jnp.diagonal(own_block) / cell_count + EPSILON)
    all_norms = lax.all_gather(own_norms, "slab", axis=0, tiled=True)
    coupling = gram_rows / math.sqrt(cell_count) / (own_norms[:, None] * all_norms[None, :])
    row_ids = own_start + lax.broadcasted_iota(jnp.int32, coupling.shape, 0)
    col_ids = lax.broadcasted_iota(jnp.int32, coupling.shape, 1)
    coupling = jnp.where(row_ids == col_ids, 0.0, coupling)
    return (coupling, own_norms)


def solution(mesh):
    placed = (
        P(("groups", "slab"), "sub", None, "probe"),
        P("slab", "sub", None),
        P(None, ("groups", "slab"), "sub", None),
    )
    return jax.shard_map(
        shards,
        mesh=mesh,
        in_specs=placed,
        out_specs=(P(("groups", "slab"), None), P(("groups", "slab"))),
        check_vma=False,
    )
```

profile of v0, /device:TPU:0, one launch (start us, length us, event | category | flops | bytes accessed | tf_op | source)
XLA Modules:
  0.0 570.9 jit_solution(8756280232743605682)
XLA Ops:
  12.5 5.7 collective-permute-start.1
  18.2 32.4 %collective-permute-done = f32[4,8,48,256]{3,1,0,2:T(8,128)S(1)} collective-permute-done((f32[4,8,48,256]{3,1,0,2:T(8,128)S(1)}, f32[4,8,48,256]{3,1,0,2:T(8,128)S(1)}, u32[]{:S(2)}, u32[]{:S(2)}) %collective-permute-start) | collective-permute-done | bytes 1572896 | tf_op jit(solution)/shard_map/ppermute | solution.py:20
  52.9 4.4 fusion.102
  58.6 6.3 %collective-permute-start.3 = (f32[16,4,48,256]{3,1,0,2:T(4,128)}, f32[16,4,48,256]{3,1,0,2:T(4,128)}, u32[]{:S(2)}, u32[]{:S(2)}) collective-permute-start(f32[16,4,48,256]{3,1,0,2:T(4,128)} %get-tuple-element.13), channel_id=1, source_target_pairs={{0,1},{2,3},{4,5},{6,7},{8,9},{10,11},{12,13},{14,15},{16,17},{18,... | collective-permute-start | bytes 9437192 | tf_op jit(solution)/shard_map/ppermute | solution.py:19
  68.9 13.9 %pad_maximum_fusion = (f32[16,12,48,256]{3,1,0,2:T(8,128)}, f32[16,12,48,256]{3,1,0,2:T(8,128)}) fusion(f32[16,4,48,256]{3,1,0,2:T(4,128)} %collective-permute-done.2, f32[4,8,48,256]{3,1,0,2:T(8,128)} %copy-done.3, f32[8,8,48,256]{3,1,0,2:T(8,128)S(1)} %convert_multiply_fusion.3, f32[4,8,48,256]{3,1,0,2:T(8,128)} %copy-done.6, ...), kind=kLoop, calls=%fused_computation.1 | loop fusion | flops 14155776 | bytes 31457280 | tf_op jit(solution)/shard_map/concatenate | solution.py:21
  82.8 37.6 %fusion.9 = f32[8,8,48,256]{3,1,0,2:T(8,128)S(1)} fusion(f32[8,8,48,256]{3,1,0,2:T(8,128)} %copy-done.1, f32[4,8,48,256]{3,1,0,2:T(8,128)} %copy-done.6, f32[4,8,48,256]{3,1,0,2:T(8,128)} %copy-done.3, f32[16,12,48,256]{3,1,0,2:T(8,128)} %get-tuple-element.11, f32[16,12,48,256]{3,1,0,2:T(8,128)} %get-tuple-element.10, f32[8,8,48]{1,0,2:T(8,128)} %copy.16, ...), kind=kLoop, calls=%fused_computation.83 | loop fusion | flops 33816576 | bytes 36200448 | tf_op jit(solution)/shard_map/add | solution.py:56
  122.1 5.1 collective-permute-start.5
  127.2 32.9 %collective-permute-done.4 = f32[4,8,48,256]{3,1,0,2:T(8,128)S(1)} collective-permute-done((f32[4,8,48,256]{3,1,0,2:T(8,128)S(1)}, f32[4,8,48,256]{3,1,0,2:T(8,128)S(1)}, u32[]{:S(2)}, u32[]{:S(2)}) %collective-permute-start.4) | collective-permute-done | bytes 1572896 | tf_op jit(solution)/shard_map/ppermute | solution.py:20
  162.5 4.4 fusion.101
  168.2 6.4 %collective-permute-start.7 = (f32[16,4,48,256]{3,1,0,2:T(4,128)}, f32[16,4,48,256]{3,1,0,2:T(4,128)}, u32[]{:S(2)}, u32[]{:S(2)}) collective-permute-start(f32[16,4,48,256]{3,1,0,2:T(4,128)} %get-tuple-element.9), channel_id=1, source_target_pairs={{0,1},{2,3},{4,5},{6,7},{8,9},{10,11},{12,13},{14,15},{16,17},{18,... | collective-permute-start | bytes 9437192 | tf_op jit(solution)/shard_map/ppermute | solution.py:19
  178.4 13.8 %pad_maximum_fusion.1 = (f32[16,12,48,256]{3,1,0,2:T(8,128)}, f32[16,12,48,256]{3,1,0,2:T(8,128)}) fusion(f32[16,4,48,256]{3,1,0,2:T(4,128)} %collective-permute-done.6, f32[4,8,48,256]{3,1,0,2:T(8,128)} %copy-done.4, f32[8,8,48,256]{3,1,0,2:T(8,128)S(1)} %fusion.9, f32[4,8,48,256]{3,1,0,2:T(8,128)} %copy-done.7, f32[16,4,48,256]{3,1,0,2:T(4,128)} %collective-permute-done.7), kind=kLoop, calls=%fused_computation.3 | loop fusion | flops 14155776 | bytes 31457280 | tf_op jit(solution)/shard_map/concatenate | solution.py:21
  192.2 23.1 %fusion.28 = f32[8,8,48,256]{3,1,0,2:T(8,128)} fusion(f32[8,8,48,256]{3,1,0,2:T(8,128)S(1)} %fusion.9, f32[4,8,48,256]{3,1,0,2:T(8,128)} %copy-done.7, f32[4,8,48,256]{3,1,0,2:T(8,128)} %copy-done.4, f32[16,12,48,256]{3,1,0,2:T(8,128)} %get-tuple-element.7, f32[16,12,48,256]{3,1,0,2:T(8,128)} %get-tuple-element.6, f32[8,8,48]{1,0,2:T(8,128)} %copy.17, ...), kind=kLoop, calls=%fused_computation.102 | loop fusion | flops 35389440 | bytes 36212736 | tf_op jit(solution)/shard_map/add | solution.py:56
  219.1 5.1 collective-permute-start.9
  224.2 32.9 %collective-permute-done.8 = f32[4,8,48,256]{3,1,0,2:T(8,128)S(1)} collective-permute-done((f32[4,8,48,256]{3,1,0,2:T(8,128)S(1)}, f32[4,8,48,256]{3,1,0,2:T(8,128)S(1)}, u32[]{:S(2)}, u32[]{:S(2)}) %collective-permute-start.8) | collective-permute-done | bytes 1572896 | tf_op jit(solution)/shard_map/ppermute | solution.py:20
  260.1 4.4 fusion.100
  265.8 6.3 %collective-permute-start.11 = (f32[16,4,48,256]{3,1,0,2:T(4,128)}, f32[16,4,48,256]{3,1,0,2:T(4,128)}, u32[]{:S(2)}, u32[]{:S(2)}) collective-permute-start(f32[16,4,48,256]{3,1,0,2:T(4,128)} %get-tuple-element.5), channel_id=1, source_target_pairs={{0,1},{2,3},{4,5},{6,7},{8,9},{10,11},{12,13},{14,15},{16,17},{18,... | collective-permute-start | bytes 9437192 | tf_op jit(solution)/shard_map/ppermute | solution.py:19
  276.1 17.6 %pad_maximum_fusion.2 = (f32[16,12,48,256]{3,1,0,2:T(8,128)}, f32[16,12,48,256]{3,1,0,2:T(8,128)}) fusion(f32[16,4,48,256]{3,1,0,2:T(4,128)} %collective-permute-done.10, f32[4,8,48,256]{3,1,0,2:T(8,128)} %copy-done.2, f32[8,8,48,256]{3,1,0,2:T(8,128)} %fusion.28, f32[4,8,48,256]{3,1,0,2:T(8,128)} %copy-done.5, f32[16,4,48,256]{3,1,0,2:T(4,128)} %collective-permute-done.11), kind=kLoop, calls=%fused_computation.5 | loop fusion | flops 14155776 | bytes 31457280 | tf_op jit(solution)/shard_map/concatenate | solution.py:21
  293.7 38.3 %fusion.48 = bf16[8,8,48,256]{3,1,0,2:T(8,128)(2,1)} fusion(f32[8,8,48,256]{3,1,0,2:T(8,128)} %fusion.28, f32[4,8,48,256]{3,1,0,2:T(8,128)} %copy-done.5, f32[4,8,48,256]{3,1,0,2:T(8,128)} %copy-done.2, f32[16,12,48,256]{3,1,0,2:T(8,128)} %get-tuple-element.3, f32[16,12,48,256]{3,1,0,2:T(8,128)} %get-tuple-element.2, f32[8,8,48,256]{3,1,0,2:T(8,128)S(1)} %fusion.9, ...), kind=kLoop, calls=%fused_computation.122 | loop fusion | flops 35389440 | bytes 37773312 | tf_op jit(solution)/shard_map/convert_element_type | solution.py:62
  332.0 23.7 %all_to_all.35 = bf16[256,2,1536]{0,2,1:T(8,128)(2,1)S(1)} all-to-all(bf16[256,2,1536]{0,2,1:T(8,128)(2,1)} %bitcast.24), channel_id=1, replica_groups=mesh['groups'=2,'slab'=4,'probe'=2,'sub'=2] {'probe'}, dimensions={1} | all-to-all | bytes 3145728 | tf_op jit(solution)/shard_map/all_to_all | solution.py:70
  356.4 42.7 %all_to_all.36 = bf16[4,128,1536]{2,1,0:T(8,128)(2,1)S(1)} all-to-all(bf16[4,128,1536]{2,1,0:T(8,128)(2,1)S(1)} %bitcast.26), channel_id=1, replica_groups=mesh['groups'=2,'slab'=4,'probe'=2,'sub'=2] {'slab'}, dimensions={0} | all-to-all | bytes 3145728 | tf_op jit(solution)/shard_map/all_to_all | solution.py:73
  400.7 113.3 %all-gather.3.cloned.1.call-done = bf16[512,6144]{0,1:T(8,128)(2,1)} async-done(((bf16[128,6144]{0,1:T(8,128)(2,1)}), bf16[512,6144]{0,1:T(8,128)(2,1)}) %all-gather.3.cloned.1.call-update) | async-done | bytes 6291472 | tf_op jit(solution)/shard_map/all_gather | solution.py:76
  514.0 5.0 fusion.106
  519.1 30.3 %all-reduce.5.cloned.1.call-done = f32[128,512]{1,0:T(8,128)} async-done(((f32[128,512]{1,0:T(8,128)}), f32[128,512]{1,0:T(8,128)}) %all-reduce.5.cloned.1.call-update) | async-done | bytes 262160 | tf_op jit(solution)/shard_map/psum | solution.py:80
  551.5 10.8 %all-gather = f32[4,1,128]{2,1,0:T(1,128)S(1)} all-gather(f32[1,1,128]{2,1,0:T(1,128)S(1)} %fusion.109), channel_id=1, replica_groups=mesh['groups'=2,'slab'=4,'probe'=2,'sub'=2] {'slab'}, dimensions={0}, use_global_device_ids=true | all-gather | bytes 2560 | tf_op jit(solution)/shard_map/all_gather | solution.py:85
  (59 shorter events, 40.5 us)
Async XLA Ops:
  7.2 506.9 %all-gather.3.cloned.1.call-start = ((), (), s32[]{:S(2)}) async-start(), calls=%async_computation.2 | async-start | bytes 7864320 | tf_op jit(solution)/shard_map/all_gather | solution.py:76
  10.8 58.1 %copy-start.1 = (f32[8,8,48,256]{3,1,0,2:T(8,128)}, f32[8,8,48,256]{3,1,0,2:T(8,128)S(1)}, u32[]{:S(2)}) copy-start(f32[8,8,48,256]{3,1,0,2:T(8,128)S(1)} %convert_multiply_fusion.3) | copy-start | bytes 9437188
  11.2 39.3 %collective-permute-start = (f32[4,8,48,256]{3,1,0,2:T(8,128)S(1)}, f32[4,8,48,256]{3,1,0,2:T(8,128)S(1)}, u32[]{:S(2)}, u32[]{:S(2)}) collective-permute-start(f32[4,8,48,256]{3,1,0,2:T(8,128)S(1)} %get-tuple-element.18), channel_id=1, source_target_pairs={{4,0},{8,4},{12,8},{5,1},{9,5},{13,9},{6,2},{10,6},{14,10},{7,3},{... | collective-permute-start | bytes 4718600 | tf_op jit(solution)/shard_map/ppermute | solution.py:20
  12.5 39.2 %collective-permute-start.1 = (f32[4,8,48,256]{3,1,0,2:T(8,128)S(1)}, f32[4,8,48,256]{3,1,0,2:T(8,128)S(1)}, u32[]{:S(2)}, u32[]{:S(2)}) collective-permute-start(f32[4,8,48,256]{3,1,0,2:T(8,128)S(1)} %get-tuple-element.19), channel_id=1, source_target_pairs={{0,4},{4,8},{8,12},{1,5},{5,9},{9,13},{2,6},{6,10},{10,14},{3,7},{... | collective-permute-start | bytes 4718600 | tf_op jit(solution)/shard_map/ppermute | solution.py:19
  50.5 1.8 copy-start.3
  51.7 1.2 copy-start.6
  57.3 9.3 %collective-permute-start.2 = (f32[16,4,48,256]{3,1,0,2:T(4,128)}, f32[16,4,48,256]{3,1,0,2:T(4,128)}, u32[]{:S(2)}, u32[]{:S(2)}) collective-permute-start(f32[16,4,48,256]{3,1,0,2:T(4,128)} %get-tuple-element.12), channel_id=1, source_target_pairs={{1,0},{3,2},{5,4},{7,6},{9,8},{11,10},{13,12},{15,14},{17,16},{19,... | collective-permute-start | bytes 9437192 | tf_op jit(solution)/shard_map/ppermute | solution.py:20
  58.6 10.3 %collective-permute-start.3 = (f32[16,4,48,256]{3,1,0,2:T(4,128)}, f32[16,4,48,256]{3,1,0,2:T(4,128)}, u32[]{:S(2)}, u32[]{:S(2)}) collective-permute-start(f32[16,4,48,256]{3,1,0,2:T(4,128)} %get-tuple-element.13), channel_id=1, source_target_pairs={{0,1},{2,3},{4,5},{6,7},{8,9},{10,11},{12,13},{14,15},{16,17},{18,... | collective-permute-start | bytes 9437192 | tf_op jit(solution)/shard_map/ppermute | solution.py:19
  120.8 39.3 %collective-permute-start.4 = (f32[4,8,48,256]{3,1,0,2:T(8,128)S(1)}, f32[4,8,48,256]{3,1,0,2:T(8,128)S(1)}, u32[]{:S(2)}, u32[]{:S(2)}) collective-permute-start(f32[4,8,48,256]{3,1,0,2:T(8,128)S(1)} %get-tuple-element.16), channel_id=1, source_target_pairs={{4,0},{8,4},{12,8},{5,1},{9,5},{13,9},{6,2},{10,6},{14,10},{7,3},{... | collective-permute-start | bytes 4718600 | tf_op jit(solution)/shard_map/ppermute | solution.py:20
  122.1 39.2 %collective-permute-start.5 = (f32[4,8,48,256]{3,1,0,2:T(8,128)S(1)}, f32[4,8,48,256]{3,1,0,2:T(8,128)S(1)}, u32[]{:S(2)}, u32[]{:S(2)}) collective-permute-start(f32[4,8,48,256]{3,1,0,2:T(8,128)S(1)} %get-tuple-element.17), channel_id=1, source_target_pairs={{0,4},{4,8},{8,12},{1,5},{5,9},{9,13},{2,6},{6,10},{10,14},{3,7},{... | collective-permute-start | bytes 4718600 | tf_op jit(solution)/shard_map/ppermute | solution.py:19
  160.1 1.8 copy-start.4
  161.3 1.2 copy-start.7
  166.9 9.2 %collective-permute-start.6 = (f32[16,4,48,256]{3,1,0,2:T(4,128)}, f32[16,4,48,256]{3,1,0,2:T(4,128)}, u32[]{:S(2)}, u32[]{:S(2)}) collective-permute-start(f32[16,4,48,256]{3,1,0,2:T(4,128)} %get-tuple-element.8), channel_id=1, source_target_pairs={{1,0},{3,2},{5,4},{7,6},{9,8},{11,10},{13,12},{15,14},{17,16},{19,... | collective-permute-start | bytes 9437192 | tf_op jit(solution)/shard_map/ppermute | solution.py:20
  168.2 10.3 %collective-permute-start.7 = (f32[16,4,48,256]{3,1,0,2:T(4,128)}, f32[16,4,48,256]{3,1,0,2:T(4,128)}, u32[]{:S(2)}, u32[]{:S(2)}) collective-permute-start(f32[16,4,48,256]{3,1,0,2:T(4,128)} %get-tuple-element.9), channel_id=1, source_target_pairs={{0,1},{2,3},{4,5},{6,7},{8,9},{10,11},{12,13},{14,15},{16,17},{18,... | collective-permute-start | bytes 9437192 | tf_op jit(solution)/shard_map/ppermute | solution.py:19
  215.3 44.1 %copy-start = (f32[8,8,48,256]{3,1,0,2:T(8,128)S(1)}, f32[8,8,48,256]{3,1,0,2:T(8,128)}, u32[]{:S(2)}) copy-start(f32[8,8,48,256]{3,1,0,2:T(8,128)} %fusion.28) | copy-start | bytes 9437188
  217.8 39.3 %collective-permute-start.8 = (f32[4,8,48,256]{3,1,0,2:T(8,128)S(1)}, f32[4,8,48,256]{3,1,0,2:T(8,128)S(1)}, u32[]{:S(2)}, u32[]{:S(2)}) collective-permute-start(f32[4,8,48,256]{3,1,0,2:T(8,128)S(1)} %get-tuple-element.14), channel_id=1, source_target_pairs={{4,0},{8,4},{12,8},{5,1},{9,5},{13,9},{6,2},{10,6},{14,10},{7,3},{... | collective-permute-start | bytes 4718600 | tf_op jit(solution)/shard_map/ppermute | solution.py:20
  219.1 39.2 %collective-permute-start.9 = (f32[4,8,48,256]{3,1,0,2:T(8,128)S(1)}, f32[4,8,48,256]{3,1,0,2:T(8,128)S(1)}, u32[]{:S(2)}, u32[]{:S(2)}) collective-permute-start(f32[4,8,48,256]{3,1,0,2:T(8,128)S(1)} %get-tuple-element.15), channel_id=1, source_target_pairs={{0,4},{4,8},{8,12},{1,5},{5,9},{9,13},{2,6},{6,10},{10,14},{3,7},{... | collective-permute-start | bytes 4718600 | tf_op jit(solution)/shard_map/ppermute | solution.py:19
  257.1 1.2 copy-start.2
  258.2 1.1 copy-start.5
  264.5 8.5 %collective-permute-start.10 = (f32[16,4,48,256]{3,1,0,2:T(4,128)}, f32[16,4,48,256]{3,1,0,2:T(4,128)}, u32[]{:S(2)}, u32[]{:S(2)}) collective-permute-start(f32[16,4,48,256]{3,1,0,2:T(4,128)} %get-tuple-element.4), channel_id=1, source_target_pairs={{1,0},{3,2},{5,4},{7,6},{9,8},{11,10},{13,12},{15,14},{17,16},{19,... | collective-permute-start | bytes 9437192 | tf_op jit(solution)/shard_map/ppermute | solution.py:20
  265.8 10.3 %collective-permute-start.11 = (f32[16,4,48,256]{3,1,0,2:T(4,128)}, f32[16,4,48,256]{3,1,0,2:T(4,128)}, u32[]{:S(2)}, u32[]{:S(2)}) collective-permute-start(f32[16,4,48,256]{3,1,0,2:T(4,128)} %get-tuple-element.5), channel_id=1, source_target_pairs={{0,1},{2,3},{4,5},{6,7},{8,9},{10,11},{12,13},{14,15},{16,17},{18,... | collective-permute-start | bytes 9437192 | tf_op jit(solution)/shard_map/ppermute | solution.py:19
  400.7 148.7 %all-reduce.5.cloned.1.call-start = ((), (), s32[]{:S(2)}) async-start(), calls=%async_computation.3 | async-start | bytes 524288 | tf_op jit(solution)/shard_map/psum | solution.py:80
  551.5 12.6 %copy-start.8 = (f32[128]{0:T(128)}, f32[128]{0:T(128)S(1)}, u32[]{:S(2)}) copy-start(f32[128]{0:T(128)S(1)} %add_sqrt_fusion) | copy-start | bytes 1540
Sparse Core Ops, SparseCore 0:
  400.8 113.1 all-gather.2
  519.2 30.1 all-reduce.4
where the time goes:
time: 572 us; the launch traced here: 571 us
  waiting for transfers between devices  253 us (44%)
  other arithmetic  150 us (26%)
  blocking collectives  77.2 us (13%)
  starting transfers between devices  42.7 us (7%)
  local copies, waits for them, and re-layouts  28.7 us (5%)
  between operations  14.3 us (2%)
    all_gather x1, waiting for transfers between devices, shards(): lax.all_gather(own_panel, 'slab', axis=0, tiled=True)  113 us
    ppermute x6, waiting for transfers between devices, extended(): after = lax.ppermute(first, axis, down)  98.1 us
    add x2, other arithmetic, propagate(): 2.0 * current - previous + courant[..., None] * operator(current)  60.7 us
    concatenate x6, other arithmetic, extended(): x = jnp.concatenate([before, x, after], axis=dim)  47.2 us
    all_to_all x1, blocking collectives, shards(): lax.all_to_all(quarters, 'slab', split_axis=0, concat_axis=1, tiled=True)  42.7 us
    convert_element_type x1, other arithmetic, propagate(): return current.astype(jnp.bfloat16)  38.3 us
    ppermute x6, starting transfers between devices, extended(): before = lax.ppermute(last, axis, up)  34.9 us
    psum x1, waiting for transfers between devices, shards(): gram_rows = lax.psum(product_tile, ('probe', 'sub'))  30.3 us
  transfers between devices with their start and end apart: 14, of which 11 were waited for; matrix products, arithmetic and copies ran while one was open for 1% of the time, Pallas kernels for 0%

commit v1 on v0

v1 whole, which is shorter than its diff:
```python
import functools
import math

import jax
import jax.numpy as jnp
from jax import lax
from jax.experimental import pallas as pl
from jax.experimental.pallas import tpu as pltpu
from jax.sharding import PartitionSpec as P

COEFFICIENTS = (-205.0 / 72.0, 8.0 / 5.0, -1.0 / 5.0, 8.0 / 315.0, -1.0 / 560.0)
EPSILON = 1e-06
LANES = 128
RADIUS = 4
EDGE = 8
TILE = 16
F32 = jnp.float32
BF16 = jnp.bfloat16
VMEM_LIMIT = 32 * 1024 * 1024


def params(*semantics):
    return pltpu.CompilerParams(
        dimension_semantics=semantics or None, vmem_limit_bytes=VMEM_LIMIT
    )


def edge_store(i, across, edge_ref, value_of):
    core = lax.axis_index("sub")
    first = (across - RADIUS) * (1 - core)
    slot = i - first

    @pl.when((slot >= 0) & (slot < RADIUS))
    def _():
        edge_ref[:, pl.ds(jnp.clip(slot, 0, RADIUS - 1), 1)] = value_of().astype(BF16)


def first_body(p_ref, s_ref, u_ref, low_ref, high_ref, edge_ref):
    i = pl.program_id(0)
    depth = u_ref.shape[0]
    u = s_ref[...] * p_ref[...].astype(F32)
    u_ref[...] = u
    low_ref[...] = u[:RADIUS].astype(BF16)
    high_ref[...] = u[depth - RADIUS :].astype(BF16)
    edge_store(i, pl.num_programs(0), edge_ref, lambda: u_ref[...])


def first_field(probes, chunk, source0):
    depth, across, along, _ = probes.shape
    column = lambda n: pl.BlockSpec((n, 1, along, LANES), lambda i: (0, i, 0, 0))
    shape = lambda n, m, dtype: jax.ShapeDtypeStruct((n, m, along, LANES), dtype)
    return pl.pallas_call(
        first_body,
        grid=(across,),
        in_specs=[
            pl.BlockSpec((depth, 1, along, LANES), lambda i: (0, i, 0, chunk)),
            column(depth),
        ],
        out_specs=[
            column(depth),
            column(RADIUS),
            column(RADIUS),
            pl.BlockSpec((depth, RADIUS, along, LANES), lambda i: (0, 0, 0, 0)),
        ],
        out_shape=[
            shape(depth, across, F32),
            shape(RADIUS, across, BF16),
            shape(RADIUS, across, BF16),
            shape(depth, RADIUS, BF16),
        ],
        compiler_params=params("arbitrary"),
    )(probes, source0)


def fill(wide, u_ref, below_ref, above_ref, beside_ref):
    depth, across, along, _ = u_ref.shape
    core = lax.axis_index("sub")
    far = across + RADIUS
    inner = pl.ds(RADIUS, across)
    rows = pl.ds(EDGE, along)
    blank = jnp.zeros((across, EDGE, LANES), F32)

    def plane(z, _):
        wide[RADIUS + z, inner, rows] = u_ref[z]
        wide[RADIUS + z, inner, pl.ds(0, EDGE)] = blank
        wide[RADIUS + z, inner, pl.ds(EDGE + along, EDGE)] = blank
        wide[RADIUS + z, pl.ds(far * (1 - core), RADIUS), rows] = beside_ref[z].astype(F32)
        wide[RADIUS + z, pl.ds(far * core, RADIUS), rows] = jnp.zeros(
            (RADIUS, along, LANES), F32
        )
        return 0

    def outer(z, _):
        wide[z, inner, rows] = below_ref[z].astype(F32)
        wide[RADIUS + depth + z, inner, rows] = above_ref[z].astype(F32)
        return 0

    lax.fori_loop(0, depth, plane, 0)
    lax.fori_loop(0, RADIUS, outer, 0)


def step_body(has_previous, last, *refs):
    refs = list(refs)
    u_ref, below_ref, above_ref, beside_ref, p_ref, c_ref, s_ref = refs[:7]
    refs = refs[7:]
    prev_ref = refs.pop(0) if has_previous else None
    wide = refs.pop()
    i = pl.program_id(0)
    depth, across, along, _ = u_ref.shape

    @pl.when(i == 0)
    def _():
        fill(wide, u_ref, below_ref, above_ref, beside_ref)

    x = RADIUS + i

    def update(z, start, column):
        here = RADIUS + z
        rows = EDGE + start
        total = (3.0 * COEFFICIENTS[0]) * column[here]
        for r in range(1, RADIUS + 1):
            deep = column[here + r] + column[here - r]
            wide_pair = wide[here, x + r, pl.ds(rows, TILE)] + wide[here, x - r, pl.ds(rows, TILE)]
            long = wide[here, x, pl.ds(rows + r, TILE)] + wide[here, x, pl.ds(rows - r, TILE)]
            total = total + COEFFICIENTS[r] * (deep + wide_pair + long)
        span = pl.ds(start, TILE)
        new = 2.0 * column[here]
        if has_previous:
            new = new - prev_ref[z, 0, span]
        new = new + c_ref[z, 0, span] * total
        return new + s_ref[z, 0, span] * p_ref[z, 0, span].astype(F32)

    for start in range(0, along, TILE):
        span = pl.ds(start, TILE)
        column = [wide[z, x, pl.ds(EDGE + start, TILE)] for z in range(depth + 2 * RADIUS)]
        if last == "half":
            keep_ref, send_ref = refs
            lower = lax.axis_index("probe") == 0
            for z in range(depth // 2):
                one = update(z, start, column)
                two = update(z + depth // 2, start, column)
                keep_ref[z, 0, span] = jnp.where(lower, one, two).astype(BF16)
                send_ref[z, 0, span] = jnp.where(lower, two, one).astype(BF16)
        elif last:
            for z in range(depth):
                refs[0][z, 0, span] = update(z, start, column).astype(BF16)
        else:
            out_ref, low_ref, high_ref, edge_ref = refs
            for z in range(depth):
                new = update(z, start, column)
                out_ref[z, 0, span] = new
                if z < RADIUS:
                    low_ref[z, 0, span] = new.astype(BF16)
                if z >= depth - RADIUS:
                    high_ref[z - depth + RADIUS, 0, span] = new.astype(BF16)
    if not last:
        edge_store(i, across, refs[3], lambda: refs[0][...])


def step(u, halos, probes, chunk, courant, source, previous, last):
    depth, across, along, _ = u.shape
    below, above, beside = halos
    whole = lambda a: pl.BlockSpec(a.shape, lambda i: (0, 0, 0, 0))
    column = lambda n: pl.BlockSpec((n, 1, along, LANES), lambda i: (0, i, 0, 0))
    shape = lambda n, m, dtype: jax.ShapeDtypeStruct((n, m, along, LANES), dtype)
    operands = [u, below, above, beside, probes, courant, source]
    in_specs = [
        whole(u),
        whole(below),
        whole(above),
        whole(beside),
        pl.BlockSpec((depth, 1, along, LANES), lambda i: (0, i, 0, chunk)),
        column(depth),
        column(depth),
    ]
    if previous is not None:
        operands.append(previous)
        in_specs.append(column(depth))
    if last == "half":
        out_specs = [column(depth // 2)] * 2
        out_shape = [shape(depth // 2, across, BF16)] * 2
    elif last:
        out_specs = [column(depth)]
        out_shape = [shape(depth, across, BF16)]
    else:
        out_specs = [
            column(depth),
            column(RADIUS),
            column(RADIUS),
            pl.BlockSpec((depth, RADIUS, along, LANES), lambda i: (0, 0, 0, 0)),
        ]
        out_shape = [
            shape(depth, across, F32),
            shape(RADIUS, across, BF16),
            shape(RADIUS, across, BF16),
            shape(depth, RADIUS, BF16),
        ]
    return pl.pallas_call(
        functools.partial(step_body, previous is not None, last),
        grid=(across,),
        in_specs=in_specs,
        out_specs=out_specs,
        out_shape=out_shape,
        scratch_shapes=[
            pltpu.VMEM(
                (depth + 2 * RADIUS, across + 2 * RADIUS, along + 2 * EDGE, LANES), F32
            )
        ],
        compiler_params=params("arbitrary"),
    )(*operands)


def exchange(low, high, edge):
    slabs = lax.axis_size("slab")
    up = [(i, i + 1) for i in range(slabs - 1)]
    down = [(i + 1, i) for i in range(slabs - 1)]
    below = lax.ppermute(high, "slab", up)
    above = lax.ppermute(low, "slab", down)
    beside = lax.ppermute(edge, "sub", [(0, 1), (1, 0)])
    return below, above, beside


def gram_body(parts, *refs):
    ins, (keep_ref, send_ref), panel = refs[:parts], refs[parts : parts + 2], refs[-1]
    half = parts // 2
    chip = lax.axis_index("probe")
    core = lax.axis_index("sub")
    for n in range(half):
        mine = pl.multiple_of((chip * half + n) * LANES, LANES)
        other = pl.multiple_of(((1 - chip) * half + n) * LANES, LANES)
        panel[:, pl.ds(mine, LANES)] = ins[2 * n][...]
        panel[:, pl.ds(other, LANES)] = ins[2 * n + 1][...]
    size = parts * LANES
    everything = panel[...]

    def columns(which):
        one = panel[:, pl.ds(pl.multiple_of(which * LANES, LANES), LANES)]
        two = panel[:, pl.ds(pl.multiple_of((2 + which) * LANES, LANES), LANES)]
        return lax.dot_general(
            everything,
            jnp.concatenate([one, two], axis=1),
            (((0,), (0,)), ((), ())),
            preferred_element_type=F32,
        )

    rows = lax.broadcasted_iota(jnp.int32, (LANES, LANES), 0)
    cols = lax.broadcasted_iota(jnp.int32, (LANES, LANES), 1)
    eye = rows == cols
    keep = columns(core)
    send = columns(1 - core)
    keep_ref[:size] = keep
    send_ref[:size] = send

    def diagonal(which, first):
        side = which // 2
        a = keep_ref[which * LANES : (which + 1) * LANES, side * LANES : (side + 1) * LANES]
        b = send_ref[which * LANES : (which + 1) * LANES, side * LANES : (side + 1) * LANES]
        block = jnp.where(core == which % 2, a, b)
        return jnp.sum(jnp.where(eye, block, 0.0), axis=0, keepdims=True)

    diag = [diagonal(n, None) for n in range(parts)]
    row0 = jnp.concatenate(diag[:2], axis=1)
    row1 = jnp.concatenate(diag[2:], axis=1)
    tail = jnp.concatenate([row0, row1, jnp.zeros((6, 2 * LANES), F32)], axis=0)
    keep_ref[size:] = tail
    send_ref[size:] = tail


def gram(fields):
    parts = len(fields)
    size = parts * LANES
    shape = jax.ShapeDtypeStruct((size + 8, 2 * LANES), F32)
    return pl.pallas_call(
        functools.partial(gram_body, parts),
        out_shape=[shape, shape],
        scratch_shapes=[pltpu.VMEM((fields[0].shape[0], size), BF16)],
        compiler_params=params(),
    )(*fields)


def rows_body(slabs, count, keep_ref, got_ref, *outs):
    slab = lax.axis_index("slab")
    size = slabs * count
    tail = keep_ref[pl.ds(size, 8)] + got_ref[pl.ds(size, 8)]
    for d in range(slabs):
        owner = lax.rem(slab + d, slabs)
        span = pl.ds(pl.multiple_of(owner * count, count), count)
        outs[d][:count] = keep_ref[span] + got_ref[span]
        outs[d][count:] = tail


def split_rows(keep, got, slabs):
    count = (keep.shape[0] - 8) // slabs
    shape = jax.ShapeDtypeStruct((count + 8, keep.shape[1]), F32)
    return pl.pallas_call(
        functools.partial(rows_body, slabs, count),
        out_shape=[shape] * slabs,
        compiler_params=params(),
    )(keep, got)


def sum_body(*refs):
    total = refs[0][...]
    for ref in refs[1:-1]:
        total = total + ref[...]
    refs[-1][...] = total


def sum_all(pieces):
    return pl.pallas_call(
        sum_body,
        out_shape=jax.ShapeDtypeStruct(pieces[0].shape, F32),
        compiler_params=params(),
    )(*pieces)


def finish_body(cell_count, a_ref, b_ref, c_ref, d_ref, out_ref, norms_ref):
    slab = lax.axis_index("slab")
    core = lax.axis_index("sub")
    count = out_ref.shape[0]
    near = a_ref[...] + b_ref[...]
    far = c_ref[:count] + d_ref[:count]
    squares = near[count : count + 2]
    norms = jnp.sqrt(squares / cell_count + EPSILON)
    blocks = [norms[n // 2 : n // 2 + 1, (n % 2) * LANES : (n % 2 + 1) * LANES] for n in range(4)]
    own = blocks[0]
    for n in range(1, 4):
        own = jnp.where(slab == n, blocks[n], own)
    norms_ref[...] = own
    rows = lax.broadcasted_iota(jnp.int32, (LANES, LANES), 0)
    cols = lax.broadcasted_iota(jnp.int32, (LANES, LANES), 1)
    eye = rows == cols
    own_column = jnp.sum(
        jnp.where(eye, jnp.broadcast_to(own, (LANES, LANES)), 0.0), axis=1, keepdims=True
    )
    for side in range(2):
        for block, which in ((near, core), (far, 1 - core)):
            index = 2 * side + which
            others = jnp.where(which == 0, blocks[2 * side], blocks[2 * side + 1])
            value = block[:count, side * LANES : (side + 1) * LANES]
            value = value / math.sqrt(cell_count) / (own_column * others)
            value = jnp.where(eye & (index == slab), 0.0, value)
            out_ref[:, pl.ds(pl.multiple_of(index * LANES, LANES), LANES)] = value


def finish(pieces, cell_count):
    count = pieces[0].shape[0] - 8
    return pl.pallas_call(
        functools.partial(finish_body, cell_count),
        out_shape=[
            jax.ShapeDtypeStruct((count, 4 * LANES), F32),
            jax.ShapeDtypeStruct((1, LANES), F32),
        ],
        compiler_params=params(),
    )(*pieces)


def coupled(keeps, gots, cell_count):
    slabs = 4
    flat = lambda a: a.reshape(-1, LANES)
    fields = []
    for keep, got in zip(keeps, gots):
        fields += [flat(keep), flat(got)]
    keep, send = gram(fields)
    got = lax.ppermute(send, "sub", [(0, 1), (1, 0)])
    pieces = split_rows(keep, got, slabs)
    arrived = [pieces[0]]
    for d in range(1, slabs):
        arrived.append(
            lax.ppermute(pieces[d], "slab", [(i, (i + d) % slabs) for i in range(slabs)])
        )
    mine = sum_all(arrived)
    both = ("probe", "sub")
    others = [
        lax.ppermute(mine, both, [(i, i ^ flip) for i in range(4)]) for flip in (2, 1, 3)
    ]
    coupling, norms = finish([mine] + others, cell_count)
    return coupling, norms.reshape(-1)


def coupled_general(fields, cell_count):
    chips = lax.axis_size("probe")
    sketch = jnp.concatenate(fields, axis=-1)
    sketch = sketch.reshape(-1, sketch.shape[-1])
    if chips > 1:
        sketch = lax.all_to_all(sketch, "probe", split_axis=0, concat_axis=1, tiled=True)
    partial_gram = lax.dot_general(
        sketch, sketch, (((0,), (0,)), ((), ())), preferred_element_type=F32
    )
    rows = lax.psum_scatter(partial_gram, "slab", scatter_dimension=0, tiled=True)
    rows = lax.psum(rows, ("probe", "sub"))
    count = rows.shape[0]
    start = lax.axis_index("slab") * count
    own = jnp.diagonal(lax.dynamic_slice_in_dim(rows, start, count, 1))
    own_norms = jnp.sqrt(own / cell_count + EPSILON)
    norms = lax.all_gather(own_norms, "slab", axis=0, tiled=True)
    coupling = rows / math.sqrt(cell_count) / (own_norms[:, None] * norms[None, :])
    row_ids = start + lax.broadcasted_iota(jnp.int32, coupling.shape, 0)
    col_ids = lax.broadcasted_iota(jnp.int32, coupling.shape, 1)
    return jnp.where(row_ids == col_ids, 0.0, coupling), own_norms


def shards(probes, courant, source):
    depth, across, along, count = probes.shape
    chunks = count // LANES
    slabs, chips = lax.axis_size("slab"), lax.axis_size("probe")
    cell_count = depth * across * along * slabs * lax.axis_size("sub")
    paired = chips == 2 and slabs == 4 and chunks == 2
    spread = lambda a: jnp.broadcast_to(a[..., None], a.shape + (LANES,))
    steps = source.shape[0]
    wide_source = [spread(source[n]) for n in range(steps)]
    wide_courant = spread(courant)

    now, previous, halos = [], [None] * chunks, []
    for c in range(chunks):
        u, low, high, edge = first_field(probes, c, wide_source[0])
        now.append(u)
        halos.append(exchange(low, high, edge))
    done = []
    for n in range(1, steps):
        last = n == steps - 1
        for c in range(chunks):
            kind = "half" if last and paired else last
            out = step(
                now[c], halos[c], probes, c, wide_courant, wide_source[n], previous[c], kind
            )
            if last and paired:
                done.append((out[0], lax.ppermute(out[1], "probe", [(0, 1), (1, 0)])))
            elif last:
                done.append(out[0])
            else:
                previous[c], now[c] = now[c], out[0]
                halos[c] = exchange(*out[1:])
    if paired:
        return coupled([a for a, _ in done], [b for _, b in done], cell_count)
    return coupled_general(done, cell_count)


def solution(mesh):
    placed = (
        P(("groups", "slab"), "sub", None, "probe"),
        P("slab", "sub", None),
        P(None, ("groups", "slab"), "sub", None),
    )
    return jax.shard_map(
        shards,
        mesh=mesh,
        in_specs=placed,
        out_specs=(P(("groups", "slab"), None), P(("groups", "slab"))),
        check_vma=False,
    )
```

time: 572 us -> 112 us (0.20)
  waiting for transfers between devices: 253 us -> 36.6 us
  other arithmetic: 150 us -> 0 us
  blocking collectives: 77.2 us -> 0 us
  local copies, waits for them, and re-layouts: 28.7 us -> 3.34 us
  Pallas kernels: 0 us -> 25 us
  between operations: 14.3 us -> 0.92 us
    all_gather x1 -> x0, waiting for transfers between devices: 113 us -> none  [shards(): lax.all_gather(own_panel, 'slab', axis=0, tiled=True)]
    ppermute x12 -> x27, waiting for transfers between devices: 109 us -> 36.6 us  [the longest x6 11.3 us: exchange(): above = lax.ppermute(low, 'slab', down)]
    all_to_all x2 -> x0, blocking collectives: 66.4 us -> none  [the longest x1 42.7 us: shards(): lax.all_to_all(quarters, 'slab', split_axis=0, concat_axis=1, tiled=True)]
    add x3 -> x0, other arithmetic: 60.7 us -> none  [the longest x2 60.7 us: propagate(): 2.0 * current - previous + courant[..., None] * operator(current)]
    concatenate x7 -> x0, other arithmetic: 47.2 us -> none  [the longest x6 47.2 us: extended(): x = jnp.concatenate([before, x, after], axis=dim)]
    convert_element_type x1 -> x0, other arithmetic: 38.3 us -> none  [propagate(): return current.astype(jnp.bfloat16)]
    psum x1 -> x0, waiting for transfers between devices: 30.3 us -> none  [shards(): gram_rows = lax.psum(product_tile, ('probe', 'sub'))]
    pallas_call x0 -> x12, Pallas kernels: none -> 25 us  [the longest x6 21 us: step(): pl.pallas_call(functools.partial(step_body, previous is not None, last),...]
  transfers between devices with their start and end apart: 14 -> 27, of which waited for: 11 -> 12; matrix products, arithmetic and copies ran while one was open for 1% -> 2% of each run, Pallas kernels for 0% -> 20%
where the time goes in v1:
time: 112 us; the launch traced here: 111 us
  starting transfers between devices  44.7 us (40%)
  waiting for transfers between devices  36.6 us (33%)
  Pallas kernels  25 us (22%)
  local copies, waits for them, and re-layouts  3.34 us (3%)
    ppermute x6, starting transfers between devices, exchange(): below = lax.ppermute(high, 'slab', up)  25.5 us
    pallas_call x6, Pallas kernels, step(): pl.pallas_call(functools.partial(step_body, previous is not None, last),...  21 us
    ppermute x6, waiting for transfers between devices, exchange(): above = lax.ppermute(low, 'slab', down)  11.3 us
    ppermute x2, waiting for transfers between devices, shards(): done.append((out[0], lax.ppermute(out[1], 'probe', [(0, 1), (1, 0)])))  8.46 us
    ppermute x3, waiting for transfers between devices, coupled(): lax.ppermute(pieces[d], 'slab', [(i, (i + d) % slabs) for i in range(slab...  8.34 us
    ppermute x6, starting transfers between devices, exchange(): above = lax.ppermute(low, 'slab', down)  7.75 us
    ppermute x3, waiting for transfers between devices, coupled(): lax.ppermute(mine, both, [(i, i ^ flip) for i in range(4)])  5.35 us
    ppermute x3, starting transfers between devices, coupled(): lax.ppermute(pieces[d], 'slab', [(i, (i + d) % slabs) for i in range(slab...  5.33 us
  transfers between devices with their start and end apart: 27, of which 12 were waited for; matrix products, arithmetic and copies ran while one was open for 2% of the time, Pallas kernels for 20%

profile of v1, /device:TPU:0, one launch (start us, length us, event | category | flops | bytes accessed | tf_op | source)
XLA Modules:
  0.0 110.5 jit_solution(12210405203907844402)
XLA Ops:
  3.0 5.0 %collective-permute-start.10 = (bf16[4,8,48,128]{3,2,1,0:T(8,128)(2,1)S(1)}, bf16[4,8,48,128]{3,2,1,0:T(8,128)(2,1)S(1)}, u32[]{:S(2)}, u32[]{:S(2)}) collective-permute-start(bf16[4,8,48,128]{3,2,1,0:T(8,128)(2,1)S(1)} %get-tuple-element.53), channel_id=1, source_target_pairs={{0,4},{4,8},{8,12},{1,5},{5,9},{9,13},{2,6},{6,10},{10,14},{3,7},{... | collective-permute-start | bytes 1179656 | tf_op jit(solution)/shard_map/ppermute | solution.py:217
  10.2 4.6 %collective-permute-start = (bf16[4,8,48,128]{3,2,1,0:T(8,128)(2,1)S(1)}, bf16[4,8,48,128]{3,2,1,0:T(8,128)(2,1)S(1)}, u32[]{:S(2)}, u32[]{:S(2)}) collective-permute-start(bf16[4,8,48,128]{3,2,1,0:T(8,128)(2,1)S(1)} %get-tuple-element.39), channel_id=1, source_target_pairs={{0,4},{4,8},{8,12},{1,5},{5,9},{9,13},{2,6},{6,10},{10,14},{3,7},{... | collective-permute-start | bytes 1179656 | tf_op jit(solution)/shard_map/ppermute | solution.py:217
  17.1 4.1 %collective-permute-done.11.refs_2_ = bf16[4,8,48,128]{3,2,1,0:T(8,128)(2,1)S(1)} collective-permute-done((bf16[4,8,48,128]{3,2,1,0:T(8,128)(2,1)S(1)}, bf16[4,8,48,128]{3,2,1,0:T(8,128)(2,1)S(1)}, u32[]{:S(2)}, u32[]{:S(2)}) %collective-permute-start.11) | collective-permute-done | bytes 393248 | tf_op jit(solution)/shard_map/ppermute | solution.py:218
  22.2 3.5 %shard_map.55 = (f32[8,8,48,128]{3,2,1,0:T(8,128)S(1)}, bf16[4,8,48,128]{3,2,1,0:T(8,128)(2,1)S(1)}, bf16[4,8,48,128]{3,2,1,0:T(8,128)(2,1)S(1)}, bf16[8,4,48,128]{3,2,1,0:T(8,128)(2,1)S(1)}) custom-call(f32[8,8,48,128]{3,2,1,0:T(8,128)S(1)} %get-tuple-element.52.refs_0_.refs_7_, bf16[4,8,48,128]{3,2,1,0:T(8,128)(2,1)S(1)} %collective-permute-done.10.refs_1_, ...), custom_call_target="tpu_custom_call" | custom-call | tf_op jit(solution)/shard_map/pallas_call | solution.py:198
  25.7 3.5 %collective-permute-start.13 = (bf16[4,8,48,128]{3,2,1,0:T(8,128)(2,1)S(1)}, bf16[4,8,48,128]{3,2,1,0:T(8,128)(2,1)S(1)}, u32[]{:S(2)}, u32[]{:S(2)}) collective-permute-start(bf16[4,8,48,128]{3,2,1,0:T(8,128)(2,1)S(1)} %get-tuple-element.57), channel_id=1, source_target_pairs={{0,4},{4,8},{8,12},{1,5},{5,9},{9,13},{2,6},{6,10},{10,14},{3,7},{... | collective-permute-start | bytes 1179656 | tf_op jit(solution)/shard_map/ppermute | solution.py:217
  30.6 3.5 %shard_map.51 = (f32[8,8,48,128]{3,2,1,0:T(8,128)S(1)}, bf16[4,8,48,128]{3,2,1,0:T(8,128)(2,1)S(1)}, bf16[4,8,48,128]{3,2,1,0:T(8,128)(2,1)S(1)}, bf16[8,4,48,128]{3,2,1,0:T(8,128)(2,1)S(1)}) custom-call(f32[8,8,48,128]{3,2,1,0:T(8,128)S(1)} %get-tuple-element.38.refs_0_.refs_7_, bf16[4,8,48,128]{3,2,1,0:T(8,128)(2,1)S(1)} %collective-permute-done.refs_1_, ...), custom_call_target="tpu_custom_call" | custom-call | tf_op jit(solution)/shard_map/pallas_call | solution.py:198
  34.1 4.6 %collective-permute-start.3 = (bf16[4,8,48,128]{3,2,1,0:T(8,128)(2,1)S(1)}, bf16[4,8,48,128]{3,2,1,0:T(8,128)(2,1)S(1)}, u32[]{:S(2)}, u32[]{:S(2)}) collective-permute-start(bf16[4,8,48,128]{3,2,1,0:T(8,128)(2,1)S(1)} %get-tuple-element.43), channel_id=1, source_target_pairs={{0,4},{4,8},{8,12},{1,5},{5,9},{9,13},{2,6},{6,10},{10,14},{3,7},{... | collective-permute-start | bytes 1179656 | tf_op jit(solution)/shard_map/ppermute | solution.py:217
  40.7 3.7 %shard_map.56 = (f32[8,8,48,128]{3,2,1,0:T(8,128)S(1)}, bf16[4,8,48,128]{3,2,1,0:T(8,128)(2,1)S(1)}, bf16[4,8,48,128]{3,2,1,0:T(8,128)(2,1)S(1)}, bf16[8,4,48,128]{3,2,1,0:T(8,128)(2,1)S(1)}) custom-call(f32[8,8,48,128]{3,2,1,0:T(8,128)S(1)} %get-tuple-element.56.refs_0_.refs_7_, bf16[4,8,48,128]{3,2,1,0:T(8,128)(2,1)S(1)} %collective-permute-done.13.refs_1_, ...), custom_call_target="tpu_custom_call" | custom-call | tf_op jit(solution)/shard_map/pallas_call | solution.py:198
  44.4 4.4 %collective-permute-start.16 = (bf16[4,8,48,128]{3,2,1,0:T(8,128)(2,1)S(1)}, bf16[4,8,48,128]{3,2,1,0:T(8,128)(2,1)S(1)}, u32[]{:S(2)}, u32[]{:S(2)}) collective-permute-start(bf16[4,8,48,128]{3,2,1,0:T(8,128)(2,1)S(1)} %get-tuple-element.61), channel_id=1, source_target_pairs={{0,4},{4,8},{8,12},{1,5},{5,9},{9,13},{2,6},{6,10},{10,14},{3,7},{... | collective-permute-start | bytes 1179656 | tf_op jit(solution)/shard_map/ppermute | solution.py:217
  51.8 3.7 %shard_map.52 = (f32[8,8,48,128]{3,2,1,0:T(8,128)S(1)}, bf16[4,8,48,128]{3,2,1,0:T(8,128)(2,1)S(1)}, bf16[4,8,48,128]{3,2,1,0:T(8,128)(2,1)S(1)}, bf16[8,4,48,128]{3,2,1,0:T(8,128)(2,1)S(1)}) custom-call(f32[8,8,48,128]{3,2,1,0:T(8,128)S(1)} %get-tuple-element.42.refs_0_.refs_7_, bf16[4,8,48,128]{3,2,1,0:T(8,128)(2,1)S(1)} %collective-permute-done.3.refs_1_, ...), custom_call_target="tpu_custom_call" | custom-call | tf_op jit(solution)/shard_map/pallas_call | solution.py:198
  55.5 3.4 %collective-permute-start.6 = (bf16[4,8,48,128]{3,2,1,0:T(8,128)(2,1)S(1)}, bf16[4,8,48,128]{3,2,1,0:T(8,128)(2,1)S(1)}, u32[]{:S(2)}, u32[]{:S(2)}) collective-permute-start(bf16[4,8,48,128]{3,2,1,0:T(8,128)(2,1)S(1)} %get-tuple-element.47), channel_id=1, source_target_pairs={{0,4},{4,8},{8,12},{1,5},{5,9},{9,13},{2,6},{6,10},{10,14},{3,7},{... | collective-permute-start | bytes 1179656 | tf_op jit(solution)/shard_map/ppermute | solution.py:217
  60.3 1.6 %collective-permute-done.17.refs_2_ = bf16[4,8,48,128]{3,2,1,0:T(8,128)(2,1)S(1)} collective-permute-done((bf16[4,8,48,128]{3,2,1,0:T(8,128)(2,1)S(1)}, bf16[4,8,48,128]{3,2,1,0:T(8,128)(2,1)S(1)}, u32[]{:S(2)}, u32[]{:S(2)}) %collective-permute-start.17) | collective-permute-done | bytes 393248 | tf_op jit(solution)/shard_map/ppermute | solution.py:218
  62.5 3.3 %shard_map.57 = (bf16[4,8,48,128]{3,2,1,0:T(8,128)(2,1)S(1)}, bf16[4,8,48,128]{3,2,1,0:T(8,128)(2,1)S(1)}) custom-call(f32[8,8,48,128]{3,2,1,0:T(8,128)S(1)} %get-tuple-element.60.refs_0_, bf16[4,8,48,128]{3,2,1,0:T(8,128)(2,1)S(1)} %collective-permute-done.16.refs_1_, bf16[4,8,48,128]{3,2,1,0:T(8,128)(2,1)S(1)} %collective-permute-done.17.refs_2_, ...), custom_call_target="tpu_custom_call" | custom-call | tf_op jit(solution)/shard_map/pallas_call | solution.py:198
  65.8 1.6 %collective-permute-start.19 = (bf16[4,8,48,128]{3,2,1,0:T(8,128)(2,1)S(1)}, bf16[4,8,48,128]{3,2,1,0:T(8,128)(2,1)S(1)}, u32[]{:S(2)}, u32[]{:S(2)}) collective-permute-start(bf16[4,8,48,128]{3,2,1,0:T(8,128)(2,1)S(1)} %get-tuple-element.65), channel_id=1, source_target_pairs={{0,2},{2,0},{1,3},{3,1},{4,6},{6,4},{5,7},{7,5},{8,10},{10,8},{9,1... | collective-permute-start | bytes 1179656 | tf_op jit(solution)/shard_map/ppermute | solution.py:428
  67.5 4.1 %collective-permute-done.7.refs_2_ = bf16[4,8,48,128]{3,2,1,0:T(8,128)(2,1)S(1)} collective-permute-done((bf16[4,8,48,128]{3,2,1,0:T(8,128)(2,1)S(1)}, bf16[4,8,48,128]{3,2,1,0:T(8,128)(2,1)S(1)}, u32[]{:S(2)}, u32[]{:S(2)}) %collective-permute-start.7) | collective-permute-done | bytes 393248 | tf_op jit(solution)/shard_map/ppermute | solution.py:218
  71.7 3.3 %shard_map.53 = (bf16[4,8,48,128]{3,2,1,0:T(8,128)(2,1)S(1)}, bf16[4,8,48,128]{3,2,1,0:T(8,128)(2,1)S(1)}) custom-call(f32[8,8,48,128]{3,2,1,0:T(8,128)S(1)} %get-tuple-element.46.refs_0_, bf16[4,8,48,128]{3,2,1,0:T(8,128)(2,1)S(1)} %collective-permute-done.6.refs_1_, bf16[4,8,48,128]{3,2,1,0:T(8,128)(2,1)S(1)} %collective-permute-done.7.refs_2_, ...), custom_call_target="tpu_custom_call" | custom-call | tf_op jit(solution)/shard_map/pallas_call | solution.py:198
  76.6 8.5 %collective-permute-done.9 = bf16[4,8,48,128]{3,2,1,0:T(8,128)(2,1)S(1)} collective-permute-done((bf16[4,8,48,128]{3,2,1,0:T(8,128)(2,1)S(1)}, bf16[4,8,48,128]{3,2,1,0:T(8,128)(2,1)S(1)}, u32[]{:S(2)}, u32[]{:S(2)}) %collective-permute-start.9) | collective-permute-done | bytes 393248 | tf_op jit(solution)/shard_map/ppermute | solution.py:428
  86.4 1.9 %collective-permute-done.20.got_ref = f32[520,256]{1,0:T(8,128)S(1)} collective-permute-done((f32[520,256]{1,0:T(8,128)S(1)}, f32[520,256]{1,0:T(8,128)S(1)}, u32[]{:S(2)}, u32[]{:S(2)}) %collective-permute-start.20) | collective-permute-done | bytes 532512 | tf_op jit(solution)/shard_map/ppermute | solution.py:365
  88.4 2.0 %collective-permute-start.21 = (f32[136,256]{1,0:T(8,128)S(1)}, f32[136,256]{1,0:T(8,128)S(1)}, u32[]{:S(2)}, u32[]{:S(2)}) collective-permute-start(f32[136,256]{1,0:T(8,128)S(1)} %get-tuple-element.69), channel_id=1, source_target_pairs={{0,4},{4,8},{8,12},{12,0},{1,5},{5,9},{9,13},{13,1},{2,6},{6,10},{... | collective-permute-start | bytes 417800 | tf_op jit(solution)/shard_map/ppermute | solution.py:370
  91.0 2.7 %collective-permute-start.23 = (f32[136,256]{1,0:T(8,128)S(1)}, f32[136,256]{1,0:T(8,128)S(1)}, u32[]{:S(2)}, u32[]{:S(2)}) collective-permute-start(f32[136,256]{1,0:T(8,128)S(1)} %get-tuple-element.71), channel_id=1, source_target_pairs={{0,12},{4,0},{8,4},{12,8},{1,13},{5,1},{9,5},{13,9},{2,14},{6,2},{... | collective-permute-start | bytes 417800 | tf_op jit(solution)/shard_map/ppermute | solution.py:370
  93.7 3.2 %collective-permute-done.21.refs_1_ = f32[136,256]{1,0:T(8,128)S(1)} collective-permute-done((f32[136,256]{1,0:T(8,128)S(1)}, f32[136,256]{1,0:T(8,128)S(1)}, u32[]{:S(2)}, u32[]{:S(2)}) %collective-permute-start.21) | collective-permute-done | bytes 139296 | tf_op jit(solution)/shard_map/ppermute | solution.py:370
  96.9 5.2 %collective-permute-done.22.refs_2_ = f32[136,256]{1,0:T(8,128)S(1)} collective-permute-done((f32[136,256]{1,0:T(8,128)S(1)}, f32[136,256]{1,0:T(8,128)S(1)}, u32[]{:S(2)}, u32[]{:S(2)}) %collective-permute-start.22) | collective-permute-done | bytes 139296 | tf_op jit(solution)/shard_map/ppermute | solution.py:370
  102.1 1.6 %collective-permute-start.24 = (f32[136,256]{1,0:T(8,128)S(1)}, f32[136,256]{1,0:T(8,128)S(1)}, u32[]{:S(2)}, u32[]{:S(2)}) collective-permute-start(f32[136,256]{1,0:T(8,128)S(1)} %shard_map.60.a_ref), channel_id=1, source_target_pairs={{0,2},{1,3},{2,0},{3,1},{4,6},{5,7},{6,4},{7,5},{8,10},{9,11},{10,... | collective-permute-start | bytes 417800 | tf_op jit(solution)/shard_map/ppermute | solution.py:375
  104.3 4.4 %collective-permute-done.24.b_ref = f32[136,256]{1,0:T(8,128)S(1)} collective-permute-done((f32[136,256]{1,0:T(8,128)S(1)}, f32[136,256]{1,0:T(8,128)S(1)}, u32[]{:S(2)}, u32[]{:S(2)}) %collective-permute-start.24) | collective-permute-done | bytes 139296 | tf_op jit(solution)/shard_map/ppermute | solution.py:375
  (52 shorter events, 22.3 us)
Async XLA Ops:
  3.0 14.2 %collective-permute-start.10 = (bf16[4,8,48,128]{3,2,1,0:T(8,128)(2,1)S(1)}, bf16[4,8,48,128]{3,2,1,0:T(8,128)(2,1)S(1)}, u32[]{:S(2)}, u32[]{:S(2)}) collective-permute-start(bf16[4,8,48,128]{3,2,1,0:T(8,128)(2,1)S(1)} %get-tuple-element.53), channel_id=1, source_target_pairs={{0,4},{4,8},{8,12},{1,5},{5,9},{9,13},{2,6},{6,10},{10,14},{3,7},{... | collective-permute-start | bytes 1179656 | tf_op jit(solution)/shard_map/ppermute | solution.py:217
  7.9 13.3 %collective-permute-start.11 = (bf16[4,8,48,128]{3,2,1,0:T(8,128)(2,1)S(1)}, bf16[4,8,48,128]{3,2,1,0:T(8,128)(2,1)S(1)}, u32[]{:S(2)}, u32[]{:S(2)}) collective-permute-start(bf16[4,8,48,128]{3,2,1,0:T(8,128)(2,1)S(1)} %get-tuple-element.54), channel_id=1, source_target_pairs={{4,0},{8,4},{12,8},{5,1},{9,5},{13,9},{6,2},{10,6},{14,10},{7,3},{... | collective-permute-start | bytes 1179656 | tf_op jit(solution)/shard_map/ppermute | solution.py:218
  9.2 12.0 %collective-permute-start.12 = (bf16[8,4,48,128]{3,2,1,0:T(8,128)(2,1)S(1)}, bf16[8,4,48,128]{3,2,1,0:T(8,128)(2,1)S(1)}, u32[]{:S(2)}, u32[]{:S(2)}) collective-permute-start(bf16[8,4,48,128]{3,2,1,0:T(8,128)(2,1)S(1)} %get-tuple-element.55), channel_id=1, source_target_pairs={{0,1},{1,0},{2,3},{3,2},{4,5},{5,4},{6,7},{7,6},{8,9},{9,8},{10,11... | collective-permute-start | bytes 1179656 | tf_op jit(solution)/shard_map/ppermute | solution.py:219
  10.2 20.3 %collective-permute-start = (bf16[4,8,48,128]{3,2,1,0:T(8,128)(2,1)S(1)}, bf16[4,8,48,128]{3,2,1,0:T(8,128)(2,1)S(1)}, u32[]{:S(2)}, u32[]{:S(2)}) collective-permute-start(bf16[4,8,48,128]{3,2,1,0:T(8,128)(2,1)S(1)} %get-tuple-element.39), channel_id=1, source_target_pairs={{0,4},{4,8},{8,12},{1,5},{5,9},{9,13},{2,6},{6,10},{10,14},{3,7},{... | collective-permute-start | bytes 1179656 | tf_op jit(solution)/shard_map/ppermute | solution.py:217
  14.8 15.8 %collective-permute-start.1 = (bf16[4,8,48,128]{3,2,1,0:T(8,128)(2,1)S(1)}, bf16[4,8,48,128]{3,2,1,0:T(8,128)(2,1)S(1)}, u32[]{:S(2)}, u32[]{:S(2)}) collective-permute-start(bf16[4,8,48,128]{3,2,1,0:T(8,128)(2,1)S(1)} %get-tuple-element.40), channel_id=1, source_target_pairs={{4,0},{8,4},{12,8},{5,1},{9,5},{13,9},{6,2},{10,6},{14,10},{7,3},{... | collective-permute-start | bytes 1179656 | tf_op jit(solution)/shard_map/ppermute | solution.py:218
  17.1 13.5 %collective-permute-start.2 = (bf16[8,4,48,128]{3,2,1,0:T(8,128)(2,1)S(1)}, bf16[8,4,48,128]{3,2,1,0:T(8,128)(2,1)S(1)}, u32[]{:S(2)}, u32[]{:S(2)}) collective-permute-start(bf16[8,4,48,128]{3,2,1,0:T(8,128)(2,1)S(1)} %get-tuple-element.41), channel_id=1, source_target_pairs={{0,1},{1,0},{2,3},{3,2},{4,5},{5,4},{6,7},{7,6},{8,9},{9,8},{10,11... | collective-permute-start | bytes 1179656 | tf_op jit(solution)/shard_map/ppermute | solution.py:219
  25.7 14.3 %collective-permute-start.13 = (bf16[4,8,48,128]{3,2,1,0:T(8,128)(2,1)S(1)}, bf16[4,8,48,128]{3,2,1,0:T(8,128)(2,1)S(1)}, u32[]{:S(2)}, u32[]{:S(2)}) collective-permute-start(bf16[4,8,48,128]{3,2,1,0:T(8,128)(2,1)S(1)} %get-tuple-element.57), channel_id=1, source_target_pairs={{0,4},{4,8},{8,12},{1,5},{5,9},{9,13},{2,6},{6,10},{10,14},{3,7},{... | collective-permute-start | bytes 1179656 | tf_op jit(solution)/shard_map/ppermute | solution.py:217
  29.2 11.0 %collective-permute-start.14 = (bf16[4,8,48,128]{3,2,1,0:T(8,128)(2,1)S(1)}, bf16[4,8,48,128]{3,2,1,0:T(8,128)(2,1)S(1)}, u32[]{:S(2)}, u32[]{:S(2)}) collective-permute-start(bf16[4,8,48,128]{3,2,1,0:T(8,128)(2,1)S(1)} %get-tuple-element.58), channel_id=1, source_target_pairs={{4,0},{8,4},{12,8},{5,1},{9,5},{13,9},{6,2},{10,6},{14,10},{7,3},{... | collective-permute-start | bytes 1179656 | tf_op jit(solution)/shard_map/ppermute | solution.py:218
  30.5 9.7 %collective-permute-start.15 = (bf16[8,4,48,128]{3,2,1,0:T(8,128)(2,1)S(1)}, bf16[8,4,48,128]{3,2,1,0:T(8,128)(2,1)S(1)}, u32[]{:S(2)}, u32[]{:S(2)}) collective-permute-start(bf16[8,4,48,128]{3,2,1,0:T(8,128)(2,1)S(1)} %get-tuple-element.59), channel_id=1, source_target_pairs={{0,1},{1,0},{2,3},{3,2},{4,5},{5,4},{6,7},{7,6},{8,9},{9,8},{10,11... | collective-permute-start | bytes 1179656 | tf_op jit(solution)/shard_map/ppermute | solution.py:219
  34.1 16.1 %collective-permute-start.3 = (bf16[4,8,48,128]{3,2,1,0:T(8,128)(2,1)S(1)}, bf16[4,8,48,128]{3,2,1,0:T(8,128)(2,1)S(1)}, u32[]{:S(2)}, u32[]{:S(2)}) collective-permute-start(bf16[4,8,48,128]{3,2,1,0:T(8,128)(2,1)S(1)} %get-tuple-element.43), channel_id=1, source_target_pairs={{0,4},{4,8},{8,12},{1,5},{5,9},{9,13},{2,6},{6,10},{10,14},{3,7},{... | collective-permute-start | bytes 1179656 | tf_op jit(solution)/shard_map/ppermute | solution.py:217
  38.7 13.1 %collective-permute-start.4 = (bf16[4,8,48,128]{3,2,1,0:T(8,128)(2,1)S(1)}, bf16[4,8,48,128]{3,2,1,0:T(8,128)(2,1)S(1)}, u32[]{:S(2)}, u32[]{:S(2)}) collective-permute-start(bf16[4,8,48,128]{3,2,1,0:T(8,128)(2,1)S(1)} %get-tuple-element.44), channel_id=1, source_target_pairs={{4,0},{8,4},{12,8},{5,1},{9,5},{13,9},{6,2},{10,6},{14,10},{7,3},{... | collective-permute-start | bytes 1179656 | tf_op jit(solution)/shard_map/ppermute | solution.py:218
  40.0 11.8 %collective-permute-start.5 = (bf16[8,4,48,128]{3,2,1,0:T(8,128)(2,1)S(1)}, bf16[8,4,48,128]{3,2,1,0:T(8,128)(2,1)S(1)}, u32[]{:S(2)}, u32[]{:S(2)}) collective-permute-start(bf16[8,4,48,128]{3,2,1,0:T(8,128)(2,1)S(1)} %get-tuple-element.45), channel_id=1, source_target_pairs={{0,1},{1,0},{2,3},{3,2},{4,5},{5,4},{6,7},{7,6},{8,9},{9,8},{10,11... | collective-permute-start | bytes 1179656 | tf_op jit(solution)/shard_map/ppermute | solution.py:219
  44.4 15.8 %collective-permute-start.16 = (bf16[4,8,48,128]{3,2,1,0:T(8,128)(2,1)S(1)}, bf16[4,8,48,128]{3,2,1,0:T(8,128)(2,1)S(1)}, u32[]{:S(2)}, u32[]{:S(2)}) collective-permute-start(bf16[4,8,48,128]{3,2,1,0:T(8,128)(2,1)S(1)} %get-tuple-element.61), channel_id=1, source_target_pairs={{0,4},{4,8},{8,12},{1,5},{5,9},{9,13},{2,6},{6,10},{10,14},{3,7},{... | collective-permute-start | bytes 1179656 | tf_op jit(solution)/shard_map/ppermute | solution.py:217
  48.9 13.1 %collective-permute-start.17 = (bf16[4,8,48,128]{3,2,1,0:T(8,128)(2,1)S(1)}, bf16[4,8,48,128]{3,2,1,0:T(8,128)(2,1)S(1)}, u32[]{:S(2)}, u32[]{:S(2)}) collective-permute-start(bf16[4,8,48,128]{3,2,1,0:T(8,128)(2,1)S(1)} %get-tuple-element.62), channel_id=1, source_target_pairs={{4,0},{8,4},{12,8},{5,1},{9,5},{13,9},{6,2},{10,6},{14,10},{7,3},{... | collective-permute-start | bytes 1179656 | tf_op jit(solution)/shard_map/ppermute | solution.py:218
  50.2 11.8 %collective-permute-start.18 = (bf16[8,4,48,128]{3,2,1,0:T(8,128)(2,1)S(1)}, bf16[8,4,48,128]{3,2,1,0:T(8,128)(2,1)S(1)}, u32[]{:S(2)}, u32[]{:S(2)}) collective-permute-start(bf16[8,4,48,128]{3,2,1,0:T(8,128)(2,1)S(1)} %get-tuple-element.63), channel_id=1, source_target_pairs={{0,1},{1,0},{2,3},{3,2},{4,5},{5,4},{6,7},{7,6},{8,9},{9,8},{10,11... | collective-permute-start | bytes 1179656 | tf_op jit(solution)/shard_map/ppermute | solution.py:219
  55.5 12.0 %collective-permute-start.6 = (bf16[4,8,48,128]{3,2,1,0:T(8,128)(2,1)S(1)}, bf16[4,8,48,128]{3,2,1,0:T(8,128)(2,1)S(1)}, u32[]{:S(2)}, u32[]{:S(2)}) collective-permute-start(bf16[4,8,48,128]{3,2,1,0:T(8,128)(2,1)S(1)} %get-tuple-element.47), channel_id=1, source_target_pairs={{0,4},{4,8},{8,12},{1,5},{5,9},{9,13},{2,6},{6,10},{10,14},{3,7},{... | collective-permute-start | bytes 1179656 | tf_op jit(solution)/shard_map/ppermute | solution.py:217
  59.0 12.7 %collective-permute-start.7 = (bf16[4,8,48,128]{3,2,1,0:T(8,128)(2,1)S(1)}, bf16[4,8,48,128]{3,2,1,0:T(8,128)(2,1)S(1)}, u32[]{:S(2)}, u32[]{:S(2)}) collective-permute-start(bf16[4,8,48,128]{3,2,1,0:T(8,128)(2,1)S(1)} %get-tuple-element.48), channel_id=1, source_target_pairs={{4,0},{8,4},{12,8},{5,1},{9,5},{13,9},{6,2},{10,6},{14,10},{7,3},{... | collective-permute-start | bytes 1179656 | tf_op jit(solution)/shard_map/ppermute | solution.py:218
  60.3 11.4 %collective-permute-start.8 = (bf16[8,4,48,128]{3,2,1,0:T(8,128)(2,1)S(1)}, bf16[8,4,48,128]{3,2,1,0:T(8,128)(2,1)S(1)}, u32[]{:S(2)}, u32[]{:S(2)}) collective-permute-start(bf16[8,4,48,128]{3,2,1,0:T(8,128)(2,1)S(1)} %get-tuple-element.49), channel_id=1, source_target_pairs={{0,1},{1,0},{2,3},{3,2},{4,5},{5,4},{6,7},{7,6},{8,9},{9,8},{10,11... | collective-permute-start | bytes 1179656 | tf_op jit(solution)/shard_map/ppermute | solution.py:219
  65.8 10.8 %collective-permute-start.19 = (bf16[4,8,48,128]{3,2,1,0:T(8,128)(2,1)S(1)}, bf16[4,8,48,128]{3,2,1,0:T(8,128)(2,1)S(1)}, u32[]{:S(2)}, u32[]{:S(2)}) collective-permute-start(bf16[4,8,48,128]{3,2,1,0:T(8,128)(2,1)S(1)} %get-tuple-element.65), channel_id=1, source_target_pairs={{0,2},{2,0},{1,3},{3,1},{4,6},{6,4},{5,7},{7,5},{8,10},{10,8},{9,1... | collective-permute-start | bytes 1179656 | tf_op jit(solution)/shard_map/ppermute | solution.py:428
  75.0 10.0 %collective-permute-start.9 = (bf16[4,8,48,128]{3,2,1,0:T(8,128)(2,1)S(1)}, bf16[4,8,48,128]{3,2,1,0:T(8,128)(2,1)S(1)}, u32[]{:S(2)}, u32[]{:S(2)}) collective-permute-start(bf16[4,8,48,128]{3,2,1,0:T(8,128)(2,1)S(1)} %get-tuple-element.51), channel_id=1, source_target_pairs={{0,2},{2,0},{1,3},{3,1},{4,6},{6,4},{5,7},{7,5},{8,10},{10,8},{9,1... | collective-permute-start | bytes 1179656 | tf_op jit(solution)/shard_map/ppermute | solution.py:428
  88.4 8.5 %collective-permute-start.21 = (f32[136,256]{1,0:T(8,128)S(1)}, f32[136,256]{1,0:T(8,128)S(1)}, u32[]{:S(2)}, u32[]{:S(2)}) collective-permute-start(f32[136,256]{1,0:T(8,128)S(1)} %get-tuple-element.69), channel_id=1, source_target_pairs={{0,4},{4,8},{8,12},{12,0},{1,5},{5,9},{9,13},{13,1},{2,6},{6,10},{... | collective-permute-start | bytes 417800 | tf_op jit(solution)/shard_map/ppermute | solution.py:370
  90.4 11.7 %collective-permute-start.22 = (f32[136,256]{1,0:T(8,128)S(1)}, f32[136,256]{1,0:T(8,128)S(1)}, u32[]{:S(2)}, u32[]{:S(2)}) collective-permute-start(f32[136,256]{1,0:T(8,128)S(1)} %get-tuple-element.70), channel_id=1, source_target_pairs={{0,8},{4,12},{8,0},{12,4},{1,9},{5,13},{9,1},{13,5},{2,10},{6,14},... | collective-permute-start | bytes 417800 | tf_op jit(solution)/shard_map/ppermute | solution.py:370
  91.0 11.0 %collective-permute-start.23 = (f32[136,256]{1,0:T(8,128)S(1)}, f32[136,256]{1,0:T(8,128)S(1)}, u32[]{:S(2)}, u32[]{:S(2)}) collective-permute-start(f32[136,256]{1,0:T(8,128)S(1)} %get-tuple-element.71), channel_id=1, source_target_pairs={{0,12},{4,0},{8,4},{12,8},{1,13},{5,1},{9,5},{13,9},{2,14},{6,2},{... | collective-permute-start | bytes 417800 | tf_op jit(solution)/shard_map/ppermute | solution.py:370
  102.1 6.6 %collective-permute-start.24 = (f32[136,256]{1,0:T(8,128)S(1)}, f32[136,256]{1,0:T(8,128)S(1)}, u32[]{:S(2)}, u32[]{:S(2)}) collective-permute-start(f32[136,256]{1,0:T(8,128)S(1)} %shard_map.60.a_ref), channel_id=1, source_target_pairs={{0,2},{1,3},{2,0},{3,1},{4,6},{5,7},{6,4},{7,5},{8,10},{9,11},{10,... | collective-permute-start | bytes 417800 | tf_op jit(solution)/shard_map/ppermute | solution.py:375
  (5 other events, 26.5 us)

commit v2 on v0

v2 whole, which is shorter than its diff:
```python
import functools
import math

import jax
import jax.numpy as jnp
from jax import lax
from jax.experimental import pallas as pl
from jax.experimental.pallas import tpu as pltpu
from jax.sharding import PartitionSpec as P

COEFFICIENTS = (-205.0 / 72.0, 8.0 / 5.0, -1.0 / 5.0, 8.0 / 315.0, -1.0 / 560.0)
EPSILON = 1e-06
LANES = 128
RADIUS = 4
EDGE = 8
TILE = 16
F32 = jnp.float32
BF16 = jnp.bfloat16
VMEM_LIMIT = 32 * 1024 * 1024


def params(*semantics):
    return pltpu.CompilerParams(
        dimension_semantics=semantics or None, vmem_limit_bytes=VMEM_LIMIT
    )


def whole_vmem(count):
    return [pl.BlockSpec(memory_space=pltpu.VMEM)] * count


def shape_of(depth, across, along, dtype):
    return jax.ShapeDtypeStruct((depth, across, along, LANES), dtype)


def turned(field, scratch):
    rows, along = field.shape
    scratch[:rows, :along] = field
    return jnp.transpose(scratch[...])


def lane(values, n):
    return jnp.broadcast_to(values[:, n : n + 1], (values.shape[0], LANES))


def store_edges(z, x, span, new, depth, across, core, refs):
    low_refs, high_refs, edge_ref = refs
    value = new.astype(BF16)
    width = across // len(low_refs)
    if z < RADIUS:
        low_refs[x // width][z, x % width, span] = value
    if z >= depth - RADIUS:
        high_refs[x // width][z - depth + RADIUS, x % width, span] = value

    for mine, first in ((0, across - RADIUS), (1, 0)):
        if first <= x < first + RADIUS:

            @pl.when(core == mine)
            def _():
                edge_ref[z, x - first, span] = value


def clear_pads(u_ref):
    depth, across, padded, _ = u_ref.shape

    def plane(z, _):
        blank = jnp.zeros((across, EDGE, LANES), F32)
        u_ref[z, :, pl.ds(0, EDGE)] = blank
        u_ref[z, :, pl.ds(padded - EDGE, EDGE)] = blank
        return 0

    lax.fori_loop(0, depth, plane, 0)


def tiles(along, body):
    def one(t, _):
        body(pl.multiple_of(t * TILE, TILE))
        return 0

    lax.fori_loop(0, along // TILE, one, 0)


def first_body(chunk, p_ref, s_ref, u_ref, low_ref, high_ref, edge_ref, square, turned_s):
    depth, across, padded, _ = u_ref.shape
    along = padded - 2 * EDGE
    core = lax.axis_index("sub")
    turned_s[...] = turned(s_ref[0], square)
    clear_pads(u_ref)

    def tile(start):
        span = pl.ds(start, TILE)
        source = turned_s[span]
        for z in range(depth):
            for x in range(across):
                p = p_ref[z, x, span, chunk * LANES : (chunk + 1) * LANES].astype(F32)
                new = lane(source, z * across + x) * p
                u_ref[z, x, pl.ds(start + EDGE, TILE)] = new
                store_edges(
                    z, x, span, new, depth, across, core, ([low_ref], [high_ref], edge_ref)
                )

    tiles(along, tile)


def square_scratch():
    return [pltpu.VMEM((LANES, LANES), F32)] * 2


def first_field(probes, chunk, source):
    depth, across, along, _ = probes.shape
    return pl.pallas_call(
        functools.partial(first_body, chunk),
        in_specs=whole_vmem(2),
        out_specs=whole_vmem(4),
        out_shape=[
            shape_of(depth, across, along + 2 * EDGE, F32),
            shape_of(RADIUS, across, along, BF16),
            shape_of(RADIUS, across, along, BF16),
            shape_of(depth, RADIUS, along, BF16),
        ],
        scratch_shapes=square_scratch(),
        compiler_params=params(),
    )(probes, source)


def local_body(chunk, moment, has_previous, *refs):
    refs = list(refs)
    u_ref, beside_ref, p_ref, c_ref, s_ref = refs[:5]
    prev_ref = refs[5] if has_previous else None
    base_ref, square, turned_c, turned_s = refs[-4:]
    depth, across, along, _ = base_ref.shape
    core = lax.axis_index("sub")
    left_on = (core == 1).astype(F32)
    right_on = (core == 0).astype(F32)
    turned_c[...] = turned(c_ref[...], square)
    turned_s[...] = turned(s_ref[moment], square)

    def tile(start):
        span = pl.ds(start, TILE)
        rows = start + EDGE
        courant = turned_c[span]
        source = turned_s[span]
        for z in range(depth):
            beside = [beside_ref[z, j, span].astype(F32) for j in range(RADIUS)]
            row = [v * left_on for v in beside]
            row += [u_ref[z, x, pl.ds(rows, TILE)] for x in range(across)]
            row += [v * right_on for v in beside]
            for x in range(across):
                here = row[RADIUS + x]
                total = (3.0 * COEFFICIENTS[0]) * here
                for r in range(1, RADIUS + 1):
                    near = row[RADIUS + x + r] + row[RADIUS + x - r]
                    near = near + (
                        u_ref[z, x, pl.ds(rows + r, TILE)] + u_ref[z, x, pl.ds(rows - r, TILE)]
                    )
                    if z + r < depth:
                        near = near + u_ref[z + r, x, pl.ds(rows, TILE)]
                    if z - r >= 0:
                        near = near + u_ref[z - r, x, pl.ds(rows, TILE)]
                    total = total + COEFFICIENTS[r] * near
                cell = z * across + x
                p = p_ref[z, x, span, chunk * LANES : (chunk + 1) * LANES].astype(F32)
                new = 2.0 * here
                if has_previous:
                    new = new - prev_ref[z, x, pl.ds(rows, TILE)]
                new = new + lane(courant, cell) * total + lane(source, cell) * p
                base_ref[z, x, span] = new

    tiles(along, tile)


def local_step(u, beside, probes, chunk, courant, source, moment, previous):
    depth, across, along, _ = probes.shape
    operands = [u, beside, probes, courant, source]
    if previous is not None:
        operands.append(previous)
    return pl.pallas_call(
        functools.partial(local_body, chunk, moment, previous is not None),
        in_specs=whole_vmem(len(operands)),
        out_specs=whole_vmem(1)[0],
        out_shape=shape_of(depth, across, along, F32),
        scratch_shapes=square_scratch() + square_scratch()[:1],
        compiler_params=params(),
    )(*operands)


def rim_body(first, kind, parts, *refs):
    base_ref, below_ref, above_ref, c_ref = refs[:4]
    outs, (square, turned_c) = refs[4:-2], refs[-2:]
    depth, all_across, along, _ = base_ref.shape
    across = below_ref.shape[1]
    core = lax.axis_index("sub")
    turned_c[...] = turned(c_ref[...], square)
    if kind == "middle":
        clear_pads(outs[0])

    def tile(start):
        span = pl.ds(start, TILE)
        courant = turned_c[span]
        for x in range(across):
            place = first + x
            below = [below_ref[j, x, span].astype(F32) for j in range(RADIUS)]
            above = [above_ref[j, x, span].astype(F32) for j in range(RADIUS)]
            news = []
            for z in range(depth):
                added = None
                for r in range(1, RADIUS + 1):
                    if z - r < 0:
                        term = COEFFICIENTS[r] * below[RADIUS + z - r]
                        added = term if added is None else added + term
                    if z + r >= depth:
                        term = COEFFICIENTS[r] * above[z + r - depth]
                        added = term if added is None else added + term
                new = base_ref[z, place, span]
                if added is not None:
                    new = new + lane(courant, z * all_across + place) * added
                news.append(new)
            if kind == "middle":
                for z, new in enumerate(news):
                    outs[0][z, place, pl.ds(start + EDGE, TILE)] = new
                    edges = (outs[1 : 1 + parts], outs[1 + parts : 1 + 2 * parts], outs[-1])
                    store_edges(z, place, span, new, depth, all_across, core, edges)
            elif kind == "half":
                keep_ref, send_ref = outs
                lower = lax.axis_index("probe") == 0
                for z in range(depth // 2):
                    one, two = news[z], news[z + depth // 2]
                    keep_ref[z, x, span] = jnp.where(lower, one, two).astype(BF16)
                    send_ref[z, x, span] = jnp.where(lower, two, one).astype(BF16)
            else:
                for z, new in enumerate(news):
                    outs[0][z, x, span] = new.astype(BF16)

    tiles(along, tile)


def rim_step(base, below, above, courant, kind, first=0, parts=1):
    depth, all_across, along, _ = base.shape
    across = below.shape[1]
    if kind == "middle":
        edge = [shape_of(RADIUS, across // parts, along, BF16)] * parts
        out_shape = [shape_of(depth, across, along + 2 * EDGE, F32)]
        out_shape += edge + edge + [shape_of(depth, RADIUS, along, BF16)]
    elif kind == "half":
        out_shape = [shape_of(depth // 2, across, along, BF16)] * 2
    else:
        out_shape = [shape_of(depth, across, along, BF16)]
    return pl.pallas_call(
        functools.partial(rim_body, first, kind, parts),
        in_specs=whole_vmem(4),
        out_specs=whole_vmem(len(out_shape)),
        out_shape=out_shape,
        scratch_shapes=square_scratch(),
        compiler_params=params(),
    )(base, below, above, courant)


def exchange(lows, highs, edge):
    slabs = lax.axis_size("slab")
    up = [(i, i + 1) for i in range(slabs - 1)]
    down = [(i + 1, i) for i in range(slabs - 1)]
    pairs = []
    for low, high in zip(lows, highs):
        pairs.append((lax.ppermute(high, "slab", up), lax.ppermute(low, "slab", down)))
    return pairs, lax.ppermute(edge, "sub", [(0, 1), (1, 0)])


def gram_body(parts, pieces, *refs):
    ins, (keep_ref, send_ref), panel = refs[: 2 * len(pieces)], refs[-3:-1], refs[-1]
    half = parts // 2
    chip = lax.axis_index("probe")
    core = lax.axis_index("sub")
    depth, _, along, _ = ins[0].shape
    across = panel.shape[0] // (depth * along)
    for (chunk, first), keep, got in zip(pieces, ins[0::2], ins[1::2]):
        mine = pl.multiple_of((chip * half + chunk) * LANES, LANES)
        other = pl.multiple_of(((1 - chip) * half + chunk) * LANES, LANES)
        width = keep.shape[1]
        for z in range(depth):
            rows = pl.ds((z * across + first) * along, width * along)
            panel[rows, pl.ds(mine, LANES)] = keep[z].reshape(width * along, LANES)
            panel[rows, pl.ds(other, LANES)] = got[z].reshape(width * along, LANES)
    size = parts * LANES
    everything = panel[...]

    def columns(which):
        one = panel[:, pl.ds(pl.multiple_of(which * LANES, LANES), LANES)]
        two = panel[:, pl.ds(pl.multiple_of((2 + which) * LANES, LANES), LANES)]
        return lax.dot_general(
            everything,
            jnp.concatenate([one, two], axis=1),
            (((0,), (0,)), ((), ())),
            preferred_element_type=F32,
        )

    rows = lax.broadcasted_iota(jnp.int32, (LANES, LANES), 0)
    cols = lax.broadcasted_iota(jnp.int32, (LANES, LANES), 1)
    eye = rows == cols
    keep = columns(core)
    send = columns(1 - core)
    keep_ref[:size] = keep
    send_ref[:size] = send

    def diagonal(which, first):
        side = which // 2
        a = keep_ref[which * LANES : (which + 1) * LANES, side * LANES : (side + 1) * LANES]
        b = send_ref[which * LANES : (which + 1) * LANES, side * LANES : (side + 1) * LANES]
        block = jnp.where(core == which % 2, a, b)
        return jnp.sum(jnp.where(eye, block, 0.0), axis=0, keepdims=True)

    diag = [diagonal(n, None) for n in range(parts)]
    row0 = jnp.concatenate(diag[:2], axis=1)
    row1 = jnp.concatenate(diag[2:], axis=1)
    tail = jnp.concatenate([row0, row1, jnp.zeros((6, 2 * LANES), F32)], axis=0)
    keep_ref[size:] = tail
    send_ref[size:] = tail


def gram(parts, pieces, fields, cells):
    size = parts * LANES
    shape = jax.ShapeDtypeStruct((size + 8, 2 * LANES), F32)
    return pl.pallas_call(
        functools.partial(gram_body, parts, pieces),
        in_specs=whole_vmem(len(fields)),
        out_specs=whole_vmem(2),
        out_shape=[shape, shape],
        scratch_shapes=[pltpu.VMEM((cells, size), BF16)],
        compiler_params=params(),
    )(*fields)


def rounded(ref, block, tail):
    count = block.shape[0]
    high = tail.astype(BF16)
    low = tail - high.astype(F32)
    ref[:count] = block.astype(BF16)
    ref[count:] = jnp.concatenate([high.astype(F32), low], axis=0).astype(BF16)


def opened(ref):
    count = ref.shape[0] - 16
    tail = ref[count:].astype(F32)
    return ref[:count].astype(F32), tail[:8] + tail[8:]


def rows_body(slabs, count, keep_ref, got_ref, own_ref, *outs):
    slab = lax.axis_index("slab")
    size = slabs * count
    tail = keep_ref[pl.ds(size, 8)] + got_ref[pl.ds(size, 8)]
    for d in range(slabs):
        owner = lax.rem(slab + d, slabs)
        span = pl.ds(pl.multiple_of(owner * count, count), count)
        block = keep_ref[span] + got_ref[span]
        if d == 0:
            own_ref[:count] = block
            own_ref[count:] = tail
        else:
            rounded(outs[d - 1], block, tail)


def split_rows(keep, got, slabs):
    count = (keep.shape[0] - 8) // slabs
    own = jax.ShapeDtypeStruct((count + 8, keep.shape[1]), F32)
    sent = jax.ShapeDtypeStruct((count + 16, keep.shape[1]), BF16)
    return pl.pallas_call(
        functools.partial(rows_body, slabs, count),
        in_specs=whole_vmem(2),
        out_specs=whole_vmem(slabs),
        out_shape=[own] + [sent] * (slabs - 1),
        compiler_params=params(),
    )(keep, got)


def sum_body(own_ref, *refs):
    count = own_ref.shape[0] - 8
    block, tail = own_ref[:count], own_ref[count:]
    for ref in refs[:-1]:
        more, more_tail = opened(ref)
        block, tail = block + more, tail + more_tail
    rounded(refs[-1], block, tail)


def sum_all(own, others):
    return pl.pallas_call(
        sum_body,
        in_specs=whole_vmem(1 + len(others)),
        out_specs=whole_vmem(1)[0],
        out_shape=jax.ShapeDtypeStruct(others[0].shape, BF16),
        compiler_params=params(),
    )(own, *others)


def finish_body(cell_count, a_ref, b_ref, c_ref, d_ref, out_ref, norms_ref):
    slab = lax.axis_index("slab")
    core = lax.axis_index("sub")
    count = out_ref.shape[0]
    near, tail = opened(a_ref)
    far, _ = opened(c_ref)
    more, more_tail = opened(b_ref)
    near = near + more
    far = far + opened(d_ref)[0]
    norms = jnp.sqrt((tail + more_tail)[:2] / cell_count + EPSILON)
    blocks = [norms[n // 2 : n // 2 + 1, (n % 2) * LANES : (n % 2 + 1) * LANES] for n in range(4)]
    own = blocks[0]
    for n in range(1, 4):
        own = jnp.where(slab == n, blocks[n], own)
    norms_ref[...] = own
    rows = lax.broadcasted_iota(jnp.int32, (LANES, LANES), 0)
    cols = lax.broadcasted_iota(jnp.int32, (LANES, LANES), 1)
    eye = rows == cols
    own_column = jnp.sum(
        jnp.where(eye, jnp.broadcast_to(own, (LANES, LANES)), 0.0), axis=1, keepdims=True
    )
    for side in range(2):
        for block, which in ((near, core), (far, 1 - core)):
            index = 2 * side + which
            others = jnp.where(which == 0, blocks[2 * side], blocks[2 * side + 1])
            value = block[:count, side * LANES : (side + 1) * LANES]
            value = value / math.sqrt(cell_count) / (own_column * others)
            value = jnp.where(eye & (index == slab), 0.0, value)
            out_ref[:, pl.ds(pl.multiple_of(index * LANES, LANES), LANES)] = value


def finish(pieces, cell_count):
    count = pieces[0].shape[0] - 16
    return pl.pallas_call(
        functools.partial(finish_body, cell_count),
        in_specs=whole_vmem(4),
        out_specs=whole_vmem(2),
        out_shape=[
            jax.ShapeDtypeStruct((count, 4 * LANES), F32),
            jax.ShapeDtypeStruct((1, LANES), F32),
        ],
        compiler_params=params(),
    )(*pieces)


def coupled(pieces, fields, cells, cell_count):
    slabs = 4
    keep, send = gram(4, pieces, fields, cells)
    got = lax.ppermute(send, "sub", [(0, 1), (1, 0)])
    own, *sent = split_rows(keep, got, slabs)
    arrived = [
        lax.ppermute(block, "slab", [(i, (i + d) % slabs) for i in range(slabs)])
        for d, block in enumerate(sent, 1)
    ]
    mine = sum_all(own, arrived)
    both = ("probe", "sub")
    others = [
        lax.ppermute(mine, both, [(i, i ^ flip) for i in range(4)]) for flip in (2, 1, 3)
    ]
    coupling, norms = finish([mine] + others, cell_count)
    return coupling, norms.reshape(-1)


def coupled_general(fields, cell_count):
    chips = lax.axis_size("probe")
    sketch = jnp.concatenate(fields, axis=-1)
    sketch = sketch.reshape(-1, sketch.shape[-1])
    if chips > 1:
        sketch = lax.all_to_all(sketch, "probe", split_axis=0, concat_axis=1, tiled=True)
    partial_gram = lax.dot_general(
        sketch, sketch, (((0,), (0,)), ((), ())), preferred_element_type=F32
    )
    rows = lax.psum_scatter(partial_gram, "slab", scatter_dimension=0, tiled=True)
    rows = lax.psum(rows, ("probe", "sub"))
    count = rows.shape[0]
    start = lax.axis_index("slab") * count
    own = jnp.diagonal(lax.dynamic_slice_in_dim(rows, start, count, 1))
    own_norms = jnp.sqrt(own / cell_count + EPSILON)
    norms = lax.all_gather(own_norms, "slab", axis=0, tiled=True)
    coupling = rows / math.sqrt(cell_count) / (own_norms[:, None] * norms[None, :])
    row_ids = start + lax.broadcasted_iota(jnp.int32, coupling.shape, 0)
    col_ids = lax.broadcasted_iota(jnp.int32, coupling.shape, 1)
    return jnp.where(row_ids == col_ids, 0.0, coupling), own_norms


def shards(probes, courant, source):
    depth, across, along, count = probes.shape
    chunks = count // LANES
    slabs, chips = lax.axis_size("slab"), lax.axis_size("probe")
    cell_count = depth * across * along * slabs * lax.axis_size("sub")
    paired = chips == 2 and slabs == 4 and chunks == 2
    steps = source.shape[0]
    courant = courant.reshape(depth * across, along)
    source = source.reshape(steps, depth * across, along)

    now, previous, halos = [], [None] * chunks, []
    for c in range(chunks):
        u, low, high, edge = first_field(probes, c, source)
        now.append(u)
        halos.append(exchange([low], [high], edge))
    pieces, fields = [], []
    for n in range(1, steps):
        for c in range(chunks):
            pairs, beside = halos[c]
            base = local_step(now[c], beside, probes, c, courant, source, n, previous[c])
            if n == steps - 1:
                width = across // len(pairs)
                for h, (below, above) in enumerate(pairs):
                    kind = "half" if paired else "all"
                    out = rim_step(base, below, above, courant, kind, h * width)
                    if paired:
                        pieces.append((c, h * width))
                        fields += [out[0], lax.ppermute(out[1], "probe", [(0, 1), (1, 0)])]
                    else:
                        fields.append(out[0])
            else:
                parts = 2 if paired and n == steps - 2 and c == chunks - 1 else 1
                ((below, above),) = pairs
                out = rim_step(base, below, above, courant, "middle", parts=parts)
                previous[c], now[c] = now[c], out[0]
                halos[c] = exchange(out[1 : 1 + parts], out[1 + parts : 1 + 2 * parts], out[-1])
    if paired:
        cells = depth // 2 * across * along
        return coupled(tuple(pieces), fields, cells, cell_count)
    return coupled_general(fields, cell_count)


def solution(mesh):
    placed = (
        P(("groups", "slab"), "sub", None, "probe"),
        P("slab", "sub", None),
        P(None, ("groups", "slab"), "sub", None),
    )
    return jax.shard_map(
        shards,
        mesh=mesh,
        in_specs=placed,
        out_specs=(P(("groups", "slab"), None), P(("groups", "slab"))),
        check_vma=False,
    )
```

time: 572 us -> 137 us (0.24)
  waiting for transfers between devices: 253 us -> 22.2 us
  other arithmetic: 150 us -> 0 us
  blocking collectives: 77.2 us -> 0 us
  Pallas kernels: 0 us -> 57.1 us
  local copies, waits for them, and re-layouts: 28.7 us -> 2.32 us
  between operations: 14.3 us -> 1.06 us
  starting transfers between devices: 42.7 us -> 54.1 us
    all_gather x1 -> x0, waiting for transfers between devices: 113 us -> none  [shards(): lax.all_gather(own_panel, 'slab', axis=0, tiled=True)]
    ppermute x12 -> x30, waiting for transfers between devices: 109 us -> 22.2 us  [the longest x3 10.9 us: shards(): fields += [out[0], lax.ppermute(out[1], 'probe', [(0, 1), (1, 0)])]]
    all_to_all x2 -> x0, blocking collectives: 66.4 us -> none  [the longest x1 42.7 us: shards(): lax.all_to_all(quarters, 'slab', split_axis=0, concat_axis=1, tiled=True)]
    add x3 -> x0, other arithmetic: 60.7 us -> none  [the longest x2 60.7 us: propagate(): 2.0 * current - previous + courant[..., None] * operator(current)]
    pallas_call x0 -> x19, Pallas kernels: none -> 57.1 us  [the longest x2 28.3 us: first_field(): pl.pallas_call(functools.partial(first_body, chunk), in_specs=whole_vmem(...]
    concatenate x7 -> x0, other arithmetic: 47.2 us -> none  [the longest x6 47.2 us: extended(): x = jnp.concatenate([before, x, after], axis=dim)]
    convert_element_type x1 -> x0, other arithmetic: 38.3 us -> none  [propagate(): return current.astype(jnp.bfloat16)]
    psum x1 -> x0, waiting for transfers between devices: 30.3 us -> none  [shards(): gram_rows = lax.psum(product_tile, ('probe', 'sub'))]
  transfers between devices with their start and end apart: 14 -> 30, of which waited for: 11 -> 9; matrix products, arithmetic and copies ran while one was open for 1% -> 0% of each run, Pallas kernels for 0% -> 30%
where the time goes in v2:
time: 137 us
  Pallas kernels  57.1 us (42%)
  starting transfers between devices  54.1 us (39%)
  waiting for transfers between devices  22.2 us (16%)
  local copies, waits for them, and re-layouts  2.32 us (2%)
    ppermute x7, starting transfers between devices, exchange(): lax.ppermute(high, 'slab', up)  30.9 us
    pallas_call x2, Pallas kernels, first_field(): pl.pallas_call(functools.partial(first_body, chunk), in_specs=whole_vmem(...  28.3 us
    pallas_call x6, Pallas kernels, local_step(): pl.pallas_call(functools.partial(local_body, chunk, moment, previous is n...  13.3 us
    pallas_call x7, Pallas kernels, rim_step(): pl.pallas_call(functools.partial(rim_body, first, kind, parts), in_specs=...  13.3 us
    ppermute x3, waiting for transfers between devices, shards(): fields += [out[0], lax.ppermute(out[1], 'probe', [(0, 1), (1, 0)])]  10.9 us
    ppermute x7, starting transfers between devices, exchange(): lax.ppermute(low, 'slab', down)  9.04 us
    ppermute x3, starting transfers between devices, coupled(): lax.ppermute(block, 'slab', [(i, (i + d) % slabs) for i in range(slabs)])  6.23 us
    ppermute x3, waiting for transfers between devices, coupled(): lax.ppermute(block, 'slab', [(i, (i + d) % slabs) for i in range(slabs)])  4.33 us
  transfers between devices with their start and end apart: 30, of which 9 were waited for; matrix products, arithmetic and copies ran while one was open for 0% of the time, Pallas kernels for 30%

profile of v2, /device:TPU:0, one launch (start us, length us, event | category | flops | bytes accessed | tf_op | source)
XLA Modules:
  0.0 136.7 jit_solution(14662819400820208241)
XLA Ops:
  2.9 14.1 %shard_map.50 = (f32[8,8,64,128]{3,2,1,0:T(8,128)S(1)}, bf16[4,8,48,128]{3,2,1,0:T(8,128)(2,1)S(1)}, bf16[4,8,48,128]{3,2,1,0:T(8,128)(2,1)S(1)}, bf16[8,4,48,128]{3,2,1,0:T(8,128)(2,1)S(1)}) custom-call(bf16[8,8,48,256]{3,2,1,0:T(8,128)(2,1)S(1)} %copy-done, f32[4,64,48]{2,1,0:T(8,128)S(1)} %bitcast.3), custom_call_target="tpu_custom_call" | custom-call | tf_op jit(solution)/shard_map/pallas_call | solution.py:111
  17.6 4.5 %collective-permute-start.1 = (bf16[4,8,48,128]{3,2,1,0:T(8,128)(2,1)S(1)}, bf16[4,8,48,128]{3,2,1,0:T(8,128)(2,1)S(1)}, u32[]{:S(2)}, u32[]{:S(2)}) collective-permute-start(bf16[4,8,48,128]{3,2,1,0:T(8,128)(2,1)S(1)} %get-tuple-element.44), channel_id=1, source_target_pairs={{0,4},{4,8},{8,12},{1,5},{5,9},{9,13},{2,6},{6,10},{10,14},{3,7},{... | collective-permute-start | bytes 1179656 | tf_op jit(solution)/shard_map/ppermute | solution.py:264
  23.4 14.1 %shard_map.57 = (f32[8,8,64,128]{3,2,1,0:T(8,128)S(1)}, bf16[4,8,48,128]{3,2,1,0:T(8,128)(2,1)S(1)}, bf16[4,8,48,128]{3,2,1,0:T(8,128)(2,1)S(1)}, bf16[8,4,48,128]{3,2,1,0:T(8,128)(2,1)S(1)}) custom-call(bf16[8,8,48,256]{3,2,1,0:T(8,128)(2,1)S(1)} %copy-done, f32[4,64,48]{2,1,0:T(8,128)S(1)} %bitcast.4), custom_call_target="tpu_custom_call" | custom-call | tf_op jit(solution)/shard_map/pallas_call | solution.py:111
  37.8 4.4 %collective-permute-start.11 = (bf16[4,8,48,128]{3,2,1,0:T(8,128)(2,1)S(1)}, bf16[4,8,48,128]{3,2,1,0:T(8,128)(2,1)S(1)}, u32[]{:S(2)}, u32[]{:S(2)}) collective-permute-start(bf16[4,8,48,128]{3,2,1,0:T(8,128)(2,1)S(1)} %get-tuple-element.58), channel_id=1, source_target_pairs={{0,4},{4,8},{8,12},{1,5},{5,9},{9,13},{2,6},{6,10},{10,14},{3,7},{... | collective-permute-start | bytes 1179656 | tf_op jit(solution)/shard_map/ppermute | solution.py:264
  45.7 2.8 %shard_map.52 = (f32[8,8,64,128]{3,2,1,0:T(8,128)S(1)}, bf16[4,8,48,128]{3,2,1,0:T(8,128)(2,1)S(1)}, bf16[4,8,48,128]{3,2,1,0:T(8,128)(2,1)S(1)}, bf16[8,4,48,128]{3,2,1,0:T(8,128)(2,1)S(1)}) custom-call(f32[8,8,48,128]{3,2,1,0:T(8,128)S(1)} %shard_map.51.refs_0_, bf16[4,8,48,128]{3,2,1,0:T(8,128)(2,1)S(1)} %collective-permute-done.1.refs_1_, ...), custom_call_target="tpu_custom_call" | custom-call | tf_op jit(solution)/shard_map/pallas_call | solution.py:248
  48.8 4.4 %collective-permute-start.4 = (bf16[4,8,48,128]{3,2,1,0:T(8,128)(2,1)S(1)}, bf16[4,8,48,128]{3,2,1,0:T(8,128)(2,1)S(1)}, u32[]{:S(2)}, u32[]{:S(2)}) collective-permute-start(bf16[4,8,48,128]{3,2,1,0:T(8,128)(2,1)S(1)} %get-tuple-element.48), channel_id=1, source_target_pairs={{0,4},{4,8},{8,12},{1,5},{5,9},{9,13},{2,6},{6,10},{10,14},{3,7},{... | collective-permute-start | bytes 1179656 | tf_op jit(solution)/shard_map/ppermute | solution.py:264
  54.5 2.2 %shard_map.58.refs_0_ = f32[8,8,48,128]{3,2,1,0:T(8,128)S(1)} custom-call(f32[8,8,64,128]{3,2,1,0:T(8,128)S(1)} %get-tuple-element.56.refs_0_.refs_5_, bf16[8,4,48,128]{3,2,1,0:T(8,128)(2,1)S(1)} %collective-permute-done.10.refs_1_, bf16[8,8,48,256]{3,2,1,0:T(8,128)(2,1)S(1)} %copy-done.1, f32[64,48]{1,0:T(8,128)S(1)} %bitcast.13, f32[4,64,48]{2,1,0:T(8,128)S(1)} %bitcast.6), custom_call_target="tpu_custom_call" | custom-call | tf_op jit(solution)/shard_map/pallas_call | solution.py:177
  56.6 2.8 %shard_map.59 = (f32[8,8,64,128]{3,2,1,0:T(8,128)S(1)}, bf16[4,8,48,128]{3,2,1,0:T(8,128)(2,1)S(1)}, bf16[4,8,48,128]{3,2,1,0:T(8,128)(2,1)S(1)}, bf16[8,4,48,128]{3,2,1,0:T(8,128)(2,1)S(1)}) custom-call(f32[8,8,48,128]{3,2,1,0:T(8,128)S(1)} %shard_map.58.refs_0_, bf16[4,8,48,128]{3,2,1,0:T(8,128)(2,1)S(1)} %collective-permute-done.11.refs_1_, ...), custom_call_target="tpu_custom_call" | custom-call | tf_op jit(solution)/shard_map/pallas_call | solution.py:248
  59.7 4.4 %collective-permute-start.14 = (bf16[4,8,48,128]{3,2,1,0:T(8,128)(2,1)S(1)}, bf16[4,8,48,128]{3,2,1,0:T(8,128)(2,1)S(1)}, u32[]{:S(2)}, u32[]{:S(2)}) collective-permute-start(bf16[4,8,48,128]{3,2,1,0:T(8,128)(2,1)S(1)} %get-tuple-element.62), channel_id=1, source_target_pairs={{0,4},{4,8},{8,12},{1,5},{5,9},{9,13},{2,6},{6,10},{10,14},{3,7},{... | collective-permute-start | bytes 1179656 | tf_op jit(solution)/shard_map/ppermute | solution.py:264
  65.4 2.3 %shard_map.53.refs_0_ = f32[8,8,48,128]{3,2,1,0:T(8,128)S(1)} custom-call(f32[8,8,64,128]{3,2,1,0:T(8,128)S(1)} %get-tuple-element.46.refs_0_.refs_5_, bf16[8,4,48,128]{3,2,1,0:T(8,128)(2,1)S(1)} %collective-permute-done.3.refs_1_, bf16[8,8,48,256]{3,2,1,0:T(8,128)(2,1)S(1)} %copy-done.1, f32[64,48]{1,0:T(8,128)S(1)} %bitcast.15, f32[4,64,48]{2,1,0:T(8,128)S(1)} %bitcast.7, ...), custom_call_target="tpu_custom_call" | custom-call | tf_op jit(solution)/shard_map/pallas_call | solution.py:177
  67.7 2.8 %shard_map.54 = (f32[8,8,64,128]{3,2,1,0:T(8,128)S(1)}, bf16[4,8,48,128]{3,2,1,0:T(8,128)(2,1)S(1)}, bf16[4,8,48,128]{3,2,1,0:T(8,128)(2,1)S(1)}, bf16[8,4,48,128]{3,2,1,0:T(8,128)(2,1)S(1)}) custom-call(f32[8,8,48,128]{3,2,1,0:T(8,128)S(1)} %shard_map.53.refs_0_, bf16[4,8,48,128]{3,2,1,0:T(8,128)(2,1)S(1)} %collective-permute-done.4.refs_1_, ...), custom_call_target="tpu_custom_call" | custom-call | tf_op jit(solution)/shard_map/pallas_call | solution.py:248
  70.7 4.4 %collective-permute-start.7 = (bf16[4,8,48,128]{3,2,1,0:T(8,128)(2,1)S(1)}, bf16[4,8,48,128]{3,2,1,0:T(8,128)(2,1)S(1)}, u32[]{:S(2)}, u32[]{:S(2)}) collective-permute-start(bf16[4,8,48,128]{3,2,1,0:T(8,128)(2,1)S(1)} %get-tuple-element.52), channel_id=1, source_target_pairs={{0,4},{4,8},{8,12},{1,5},{5,9},{9,13},{2,6},{6,10},{10,14},{3,7},{... | collective-permute-start | bytes 1179656 | tf_op jit(solution)/shard_map/ppermute | solution.py:264
  76.4 2.3 %shard_map.60.refs_0_ = f32[8,8,48,128]{3,2,1,0:T(8,128)S(1)} custom-call(f32[8,8,64,128]{3,2,1,0:T(8,128)S(1)} %get-tuple-element.60.refs_0_.refs_5_, bf16[8,4,48,128]{3,2,1,0:T(8,128)(2,1)S(1)} %collective-permute-done.13.refs_1_, bf16[8,8,48,256]{3,2,1,0:T(8,128)(2,1)S(1)} %copy-done.1, f32[64,48]{1,0:T(8,128)S(1)} %bitcast.17, f32[4,64,48]{2,1,0:T(8,128)S(1)} %bitcast.8, ...), custom_call_target="tpu_custom_call" | custom-call | tf_op jit(solution)/shard_map/pallas_call | solution.py:177
  78.7 2.8 %shard_map.61 = (f32[8,8,64,128]{3,2,1,0:T(8,128)S(1)}, bf16[4,4,48,128]{3,2,1,0:T(8,128)(2,1)S(1)}, bf16[4,4,48,128]{3,2,1,0:T(8,128)(2,1)S(1)}, bf16[4,4,48,12...) custom-call(f32[8,8,48,128]{3,2,1,0:T(8,128)S(1)} %shard_map.60.refs_0_, ...), custom_call_target="tpu_custom_call" | custom-call | tf_op jit(solution)/shard_map/pallas_call | solution.py:248
  81.7 4.4 %collective-permute-start.20 = (bf16[4,4,48,128]{3,2,1,0:T(8,128)(2,1)S(1)}, bf16[4,4,48,128]{3,2,1,0:T(8,128)(2,1)S(1)}, u32[]{:S(2)}, u32[]{:S(2)}) collective-permute-start(bf16[4,4,48,128]{3,2,1,0:T(8,128)(2,1)S(1)} %get-tuple-element.70), channel_id=1, source_target_pairs={{0,4},{4,8},{8,12},{1,5},{5,9},{9,13},{2,6},{6,10},{10,14},{3,7},{... | collective-permute-start | bytes 589832 | tf_op jit(solution)/shard_map/ppermute | solution.py:264
  87.4 2.3 %shard_map.55.refs_0_ = f32[8,8,48,128]{3,2,1,0:T(8,128)S(1)} custom-call(f32[8,8,64,128]{3,2,1,0:T(8,128)S(1)} %get-tuple-element.50.refs_0_, bf16[8,4,48,128]{3,2,1,0:T(8,128)(2,1)S(1)} %collective-permute-done.6.refs_1_, bf16[8,8,48,256]{3,2,1,0:T(8,128)(2,1)S(1)} %copy-done.1, f32[64,48]{1,0:T(8,128)S(1)} %bitcast.19, f32[4,64,48]{2,1,0:T(8,128)S(1)} %bitcast.9, ...), custom_call_target="tpu_custom_call" | custom-call | tf_op jit(solution)/shard_map/pallas_call | solution.py:177
  89.7 4.6 %collective-permute-start.17 = (bf16[4,4,48,128]{3,2,1,0:T(8,128)(2,1)S(1)}, bf16[4,4,48,128]{3,2,1,0:T(8,128)(2,1)S(1)}, u32[]{:S(2)}, u32[]{:S(2)}) collective-permute-start(bf16[4,4,48,128]{3,2,1,0:T(8,128)(2,1)S(1)} %get-tuple-element.66), channel_id=1, source_target_pairs={{0,4},{4,8},{8,12},{1,5},{5,9},{9,13},{2,6},{6,10},{10,14},{3,7},{... | collective-permute-start | bytes 589832 | tf_op jit(solution)/shard_map/ppermute | solution.py:264
  98.1 2.3 %shard_map.62.refs_0_ = f32[8,8,48,128]{3,2,1,0:T(8,128)S(1)} custom-call(f32[8,8,64,128]{3,2,1,0:T(8,128)S(1)} %get-tuple-element.64.refs_0_, bf16[8,4,48,128]{3,2,1,0:T(8,128)(2,1)S(1)} %collective-permute-done.16.refs_1_, bf16[8,8,48,256]{3,2,1,0:T(8,128)(2,1)S(1)} %copy-done.1, f32[64,48]{1,0:T(8,128)S(1)} %bitcast.21, f32[4,64,48]{2,1,0:T(8,128)S(1)} %bitcast.10, ...), custom_call_target="tpu_custom_call" | custom-call | tf_op jit(solution)/shard_map/pallas_call | solution.py:177
  104.8 8.0 %collective-permute-done.22.refs_5_ = bf16[4,4,48,128]{3,2,1,0:T(8,128)(2,1)S(1)} collective-permute-done((bf16[4,4,48,128]{3,2,1,0:T(8,128)(2,1)S(1)}, bf16[4,4,48,128]{3,2,1,0:T(8,128)(2,1)S(1)}, u32[]{:S(2)}, u32[]{:S(2)}) %collective-permute-start.22) | collective-permute-done | bytes 196640 | tf_op jit(solution)/shard_map/ppermute | solution.py:505
  112.8 2.8 %collective-permute-done.19.refs_3_ = bf16[4,4,48,128]{3,2,1,0:T(8,128)(2,1)S(1)} collective-permute-done((bf16[4,4,48,128]{3,2,1,0:T(8,128)(2,1)S(1)}, bf16[4,4,48,128]{3,2,1,0:T(8,128)(2,1)S(1)}, u32[]{:S(2)}, u32[]{:S(2)}) %collective-permute-start.19) | collective-permute-done | bytes 196640 | tf_op jit(solution)/shard_map/ppermute | solution.py:505
  119.1 2.4 %collective-permute-start.24 = (bf16[144,256]{1,0:T(8,128)(2,1)S(1)}, bf16[144,256]{1,0:T(8,128)(2,1)S(1)}, u32[]{:S(2)}, u32[]{:S(2)}) collective-permute-start(bf16[144,256]{1,0:T(8,128)(2,1)S(1)} %get-tuple-element.77), channel_id=1, source_target_pairs={{0,4},{4,8},{8,12},{12,0},{1,5},{5,9},{9,13},{13,1},{2,6},{6,10},{... | collective-permute-start | bytes 221192 | tf_op jit(solution)/shard_map/ppermute | solution.py:444
  121.5 2.6 %collective-permute-start.25 = (bf16[144,256]{1,0:T(8,128)(2,1)S(1)}, bf16[144,256]{1,0:T(8,128)(2,1)S(1)}, u32[]{:S(2)}, u32[]{:S(2)}) collective-permute-start(bf16[144,256]{1,0:T(8,128)(2,1)S(1)} %get-tuple-element.78), channel_id=1, source_target_pairs={{0,8},{4,12},{8,0},{12,4},{1,9},{5,13},{9,1},{13,5},{2,10},{6,14},... | collective-permute-start | bytes 221192 | tf_op jit(solution)/shard_map/ppermute | solution.py:444
  126.6 2.8 %collective-permute-done.25.refs_1_ = bf16[144,256]{1,0:T(8,128)(2,1)S(1)} collective-permute-done((bf16[144,256]{1,0:T(8,128)(2,1)S(1)}, bf16[144,256]{1,0:T(8,128)(2,1)S(1)}, u32[]{:S(2)}, u32[]{:S(2)}) %collective-permute-start.25) | collective-permute-done | bytes 73760 | tf_op jit(solution)/shard_map/ppermute | solution.py:444
  131.9 2.4 %collective-permute-done.29.d_ref = bf16[144,256]{1,0:T(8,128)(2,1)S(1)} collective-permute-done((bf16[144,256]{1,0:T(8,128)(2,1)S(1)}, bf16[144,256]{1,0:T(8,128)(2,1)S(1)}, u32[]{:S(2)}, u32[]{:S(2)}) %collective-permute-start.29) | collective-permute-done | bytes 73760 | tf_op jit(solution)/shard_map/ppermute | solution.py:450
  (65 shorter events, 33.3 us)
Async XLA Ops:
  17.1 25.1 %collective-permute-start = (bf16[8,4,48,128]{3,2,1,0:T(8,128)(2,1)S(1)}, bf16[8,4,48,128]{3,2,1,0:T(8,128)(2,1)S(1)}, u32[]{:S(2)}, u32[]{:S(2)}) collective-permute-start(bf16[8,4,48,128]{3,2,1,0:T(8,128)(2,1)S(1)} %get-tuple-element.43), channel_id=1, source_target_pairs={{0,1},{1,0},{2,3},{3,2},{4,5},{5,4},{6,7},{7,6},{8,9},{9,8},{10,11... | collective-permute-start | bytes 1179656 | tf_op jit(solution)/shard_map/ppermute | solution.py:265
  17.6 28.1 %collective-permute-start.1 = (bf16[4,8,48,128]{3,2,1,0:T(8,128)(2,1)S(1)}, bf16[4,8,48,128]{3,2,1,0:T(8,128)(2,1)S(1)}, u32[]{:S(2)}, u32[]{:S(2)}) collective-permute-start(bf16[4,8,48,128]{3,2,1,0:T(8,128)(2,1)S(1)} %get-tuple-element.44), channel_id=1, source_target_pairs={{0,4},{4,8},{8,12},{1,5},{5,9},{9,13},{2,6},{6,10},{10,14},{3,7},{... | collective-permute-start | bytes 1179656 | tf_op jit(solution)/shard_map/ppermute | solution.py:264
  22.1 23.6 %collective-permute-start.2 = (bf16[4,8,48,128]{3,2,1,0:T(8,128)(2,1)S(1)}, bf16[4,8,48,128]{3,2,1,0:T(8,128)(2,1)S(1)}, u32[]{:S(2)}, u32[]{:S(2)}) collective-permute-start(bf16[4,8,48,128]{3,2,1,0:T(8,128)(2,1)S(1)} %get-tuple-element.45), channel_id=1, source_target_pairs={{4,0},{8,4},{12,8},{5,1},{9,5},{13,9},{6,2},{10,6},{14,10},{7,3},{... | collective-permute-start | bytes 1179656 | tf_op jit(solution)/shard_map/ppermute | solution.py:264
  37.5 15.6 %collective-permute-start.10 = (bf16[8,4,48,128]{3,2,1,0:T(8,128)(2,1)S(1)}, bf16[8,4,48,128]{3,2,1,0:T(8,128)(2,1)S(1)}, u32[]{:S(2)}, u32[]{:S(2)}) collective-permute-start(bf16[8,4,48,128]{3,2,1,0:T(8,128)(2,1)S(1)} %get-tuple-element.57), channel_id=1, source_target_pairs={{0,1},{1,0},{2,3},{3,2},{4,5},{5,4},{6,7},{7,6},{8,9},{9,8},{10,11... | collective-permute-start | bytes 1179656 | tf_op jit(solution)/shard_map/ppermute | solution.py:265
  37.8 18.8 %collective-permute-start.11 = (bf16[4,8,48,128]{3,2,1,0:T(8,128)(2,1)S(1)}, bf16[4,8,48,128]{3,2,1,0:T(8,128)(2,1)S(1)}, u32[]{:S(2)}, u32[]{:S(2)}) collective-permute-start(bf16[4,8,48,128]{3,2,1,0:T(8,128)(2,1)S(1)} %get-tuple-element.58), channel_id=1, source_target_pairs={{0,4},{4,8},{8,12},{1,5},{5,9},{9,13},{2,6},{6,10},{10,14},{3,7},{... | collective-permute-start | bytes 1179656 | tf_op jit(solution)/shard_map/ppermute | solution.py:264
  42.2 14.4 %collective-permute-start.12 = (bf16[4,8,48,128]{3,2,1,0:T(8,128)(2,1)S(1)}, bf16[4,8,48,128]{3,2,1,0:T(8,128)(2,1)S(1)}, u32[]{:S(2)}, u32[]{:S(2)}) collective-permute-start(bf16[4,8,48,128]{3,2,1,0:T(8,128)(2,1)S(1)} %get-tuple-element.59), channel_id=1, source_target_pairs={{4,0},{8,4},{12,8},{5,1},{9,5},{13,9},{6,2},{10,6},{14,10},{7,3},{... | collective-permute-start | bytes 1179656 | tf_op jit(solution)/shard_map/ppermute | solution.py:264
  48.5 15.6 %collective-permute-start.3 = (bf16[8,4,48,128]{3,2,1,0:T(8,128)(2,1)S(1)}, bf16[8,4,48,128]{3,2,1,0:T(8,128)(2,1)S(1)}, u32[]{:S(2)}, u32[]{:S(2)}) collective-permute-start(bf16[8,4,48,128]{3,2,1,0:T(8,128)(2,1)S(1)} %get-tuple-element.47), channel_id=1, source_target_pairs={{0,1},{1,0},{2,3},{3,2},{4,5},{5,4},{6,7},{7,6},{8,9},{9,8},{10,11... | collective-permute-start | bytes 1179656 | tf_op jit(solution)/shard_map/ppermute | solution.py:265
  48.8 18.9 %collective-permute-start.4 = (bf16[4,8,48,128]{3,2,1,0:T(8,128)(2,1)S(1)}, bf16[4,8,48,128]{3,2,1,0:T(8,128)(2,1)S(1)}, u32[]{:S(2)}, u32[]{:S(2)}) collective-permute-start(bf16[4,8,48,128]{3,2,1,0:T(8,128)(2,1)S(1)} %get-tuple-element.48), channel_id=1, source_target_pairs={{0,4},{4,8},{8,12},{1,5},{5,9},{9,13},{2,6},{6,10},{10,14},{3,7},{... | collective-permute-start | bytes 1179656 | tf_op jit(solution)/shard_map/ppermute | solution.py:264
  53.1 14.5 %collective-permute-start.5 = (bf16[4,8,48,128]{3,2,1,0:T(8,128)(2,1)S(1)}, bf16[4,8,48,128]{3,2,1,0:T(8,128)(2,1)S(1)}, u32[]{:S(2)}, u32[]{:S(2)}) collective-permute-start(bf16[4,8,48,128]{3,2,1,0:T(8,128)(2,1)S(1)} %get-tuple-element.49), channel_id=1, source_target_pairs={{4,0},{8,4},{12,8},{5,1},{9,5},{13,9},{6,2},{10,6},{14,10},{7,3},{... | collective-permute-start | bytes 1179656 | tf_op jit(solution)/shard_map/ppermute | solution.py:264
  59.4 15.7 %collective-permute-start.13 = (bf16[8,4,48,128]{3,2,1,0:T(8,128)(2,1)S(1)}, bf16[8,4,48,128]{3,2,1,0:T(8,128)(2,1)S(1)}, u32[]{:S(2)}, u32[]{:S(2)}) collective-permute-start(bf16[8,4,48,128]{3,2,1,0:T(8,128)(2,1)S(1)} %get-tuple-element.61), channel_id=1, source_target_pairs={{0,1},{1,0},{2,3},{3,2},{4,5},{5,4},{6,7},{7,6},{8,9},{9,8},{10,11... | collective-permute-start | bytes 1179656 | tf_op jit(solution)/shard_map/ppermute | solution.py:265
  59.7 19.0 %collective-permute-start.14 = (bf16[4,8,48,128]{3,2,1,0:T(8,128)(2,1)S(1)}, bf16[4,8,48,128]{3,2,1,0:T(8,128)(2,1)S(1)}, u32[]{:S(2)}, u32[]{:S(2)}) collective-permute-start(bf16[4,8,48,128]{3,2,1,0:T(8,128)(2,1)S(1)} %get-tuple-element.62), channel_id=1, source_target_pairs={{0,4},{4,8},{8,12},{1,5},{5,9},{9,13},{2,6},{6,10},{10,14},{3,7},{... | collective-permute-start | bytes 1179656 | tf_op jit(solution)/shard_map/ppermute | solution.py:264
  64.1 14.6 %collective-permute-start.15 = (bf16[4,8,48,128]{3,2,1,0:T(8,128)(2,1)S(1)}, bf16[4,8,48,128]{3,2,1,0:T(8,128)(2,1)S(1)}, u32[]{:S(2)}, u32[]{:S(2)}) collective-permute-start(bf16[4,8,48,128]{3,2,1,0:T(8,128)(2,1)S(1)} %get-tuple-element.63), channel_id=1, source_target_pairs={{4,0},{8,4},{12,8},{5,1},{9,5},{13,9},{6,2},{10,6},{14,10},{7,3},{... | collective-permute-start | bytes 1179656 | tf_op jit(solution)/shard_map/ppermute | solution.py:264
  70.4 15.7 %collective-permute-start.6 = (bf16[8,4,48,128]{3,2,1,0:T(8,128)(2,1)S(1)}, bf16[8,4,48,128]{3,2,1,0:T(8,128)(2,1)S(1)}, u32[]{:S(2)}, u32[]{:S(2)}) collective-permute-start(bf16[8,4,48,128]{3,2,1,0:T(8,128)(2,1)S(1)} %get-tuple-element.51), channel_id=1, source_target_pairs={{0,1},{1,0},{2,3},{3,2},{4,5},{5,4},{6,7},{7,6},{8,9},{9,8},{10,11... | collective-permute-start | bytes 1179656 | tf_op jit(solution)/shard_map/ppermute | solution.py:265
  70.7 19.0 %collective-permute-start.7 = (bf16[4,8,48,128]{3,2,1,0:T(8,128)(2,1)S(1)}, bf16[4,8,48,128]{3,2,1,0:T(8,128)(2,1)S(1)}, u32[]{:S(2)}, u32[]{:S(2)}) collective-permute-start(bf16[4,8,48,128]{3,2,1,0:T(8,128)(2,1)S(1)} %get-tuple-element.52), channel_id=1, source_target_pairs={{0,4},{4,8},{8,12},{1,5},{5,9},{9,13},{2,6},{6,10},{10,14},{3,7},{... | collective-permute-start | bytes 1179656 | tf_op jit(solution)/shard_map/ppermute | solution.py:264
  75.1 19.1 %collective-permute-start.8 = (bf16[4,8,48,128]{3,2,1,0:T(8,128)(2,1)S(1)}, bf16[4,8,48,128]{3,2,1,0:T(8,128)(2,1)S(1)}, u32[]{:S(2)}, u32[]{:S(2)}) collective-permute-start(bf16[4,8,48,128]{3,2,1,0:T(8,128)(2,1)S(1)} %get-tuple-element.53), channel_id=1, source_target_pairs={{4,0},{8,4},{12,8},{5,1},{9,5},{13,9},{6,2},{10,6},{14,10},{7,3},{... | collective-permute-start | bytes 1179656 | tf_op jit(solution)/shard_map/ppermute | solution.py:264
  81.4 15.1 %collective-permute-start.16 = (bf16[8,4,48,128]{3,2,1,0:T(8,128)(2,1)S(1)}, bf16[8,4,48,128]{3,2,1,0:T(8,128)(2,1)S(1)}, u32[]{:S(2)}, u32[]{:S(2)}) collective-permute-start(bf16[8,4,48,128]{3,2,1,0:T(8,128)(2,1)S(1)} %get-tuple-element.65), channel_id=1, source_target_pairs={{0,1},{1,0},{2,3},{3,2},{4,5},{5,4},{6,7},{7,6},{8,9},{9,8},{10,11... | collective-permute-start | bytes 1179656 | tf_op jit(solution)/shard_map/ppermute | solution.py:265
  81.7 18.6 %collective-permute-start.20 = (bf16[4,4,48,128]{3,2,1,0:T(8,128)(2,1)S(1)}, bf16[4,4,48,128]{3,2,1,0:T(8,128)(2,1)S(1)}, u32[]{:S(2)}, u32[]{:S(2)}) collective-permute-start(bf16[4,4,48,128]{3,2,1,0:T(8,128)(2,1)S(1)} %get-tuple-element.70), channel_id=1, source_target_pairs={{0,4},{4,8},{8,12},{1,5},{5,9},{9,13},{2,6},{6,10},{10,14},{3,7},{... | collective-permute-start | bytes 589832 | tf_op jit(solution)/shard_map/ppermute | solution.py:264
  86.1 14.3 %collective-permute-start.21 = (bf16[4,4,48,128]{3,2,1,0:T(8,128)(2,1)S(1)}, bf16[4,4,48,128]{3,2,1,0:T(8,128)(2,1)S(1)}, u32[]{:S(2)}, u32[]{:S(2)}) collective-permute-start(bf16[4,4,48,128]{3,2,1,0:T(8,128)(2,1)S(1)} %get-tuple-element.71), channel_id=1, source_target_pairs={{4,0},{8,4},{12,8},{5,1},{9,5},{13,9},{6,2},{10,6},{14,10},{7,3},{... | collective-permute-start | bytes 589832 | tf_op jit(solution)/shard_map/ppermute | solution.py:264
  89.7 11.9 %collective-permute-start.17 = (bf16[4,4,48,128]{3,2,1,0:T(8,128)(2,1)S(1)}, bf16[4,4,48,128]{3,2,1,0:T(8,128)(2,1)S(1)}, u32[]{:S(2)}, u32[]{:S(2)}) collective-permute-start(bf16[4,4,48,128]{3,2,1,0:T(8,128)(2,1)S(1)} %get-tuple-element.66), channel_id=1, source_target_pairs={{0,4},{4,8},{8,12},{1,5},{5,9},{9,13},{2,6},{6,10},{10,14},{3,7},{... | collective-permute-start | bytes 589832 | tf_op jit(solution)/shard_map/ppermute | solution.py:264
  94.2 8.3 %collective-permute-start.18 = (bf16[4,4,48,128]{3,2,1,0:T(8,128)(2,1)S(1)}, bf16[4,4,48,128]{3,2,1,0:T(8,128)(2,1)S(1)}, u32[]{:S(2)}, u32[]{:S(2)}) collective-permute-start(bf16[4,4,48,128]{3,2,1,0:T(8,128)(2,1)S(1)} %get-tuple-element.67), channel_id=1, source_target_pairs={{4,0},{8,4},{12,8},{5,1},{9,5},{13,9},{6,2},{10,6},{14,10},{7,3},{... | collective-permute-start | bytes 589832 | tf_op jit(solution)/shard_map/ppermute | solution.py:264
  96.5 19.2 %collective-permute-start.9 = (bf16[4,8,48,128]{3,2,1,0:T(8,128)(2,1)S(1)}, bf16[4,8,48,128]{3,2,1,0:T(8,128)(2,1)S(1)}, u32[]{:S(2)}, u32[]{:S(2)}) collective-permute-start(bf16[4,8,48,128]{3,2,1,0:T(8,128)(2,1)S(1)} %get-tuple-element.55), channel_id=1, source_target_pairs={{0,2},{2,0},{1,3},{3,1},{4,6},{6,4},{5,7},{7,5},{8,10},{10,8},{9,1... | collective-permute-start | bytes 1179656 | tf_op jit(solution)/shard_map/ppermute | solution.py:505
  101.0 11.8 %collective-permute-start.22 = (bf16[4,4,48,128]{3,2,1,0:T(8,128)(2,1)S(1)}, bf16[4,4,48,128]{3,2,1,0:T(8,128)(2,1)S(1)}, u32[]{:S(2)}, u32[]{:S(2)}) collective-permute-start(bf16[4,4,48,128]{3,2,1,0:T(8,128)(2,1)S(1)} %get-tuple-element.73), channel_id=1, source_target_pairs={{0,2},{2,0},{1,3},{3,1},{4,6},{6,4},{5,7},{7,5},{8,10},{10,8},{9,1... | collective-permute-start | bytes 589832 | tf_op jit(solution)/shard_map/ppermute | solution.py:505
  103.2 12.4 %collective-permute-start.19 = (bf16[4,4,48,128]{3,2,1,0:T(8,128)(2,1)S(1)}, bf16[4,4,48,128]{3,2,1,0:T(8,128)(2,1)S(1)}, u32[]{:S(2)}, u32[]{:S(2)}) collective-permute-start(bf16[4,4,48,128]{3,2,1,0:T(8,128)(2,1)S(1)} %get-tuple-element.69), channel_id=1, source_target_pairs={{0,2},{2,0},{1,3},{3,1},{4,6},{6,4},{5,7},{7,5},{8,10},{10,8},{9,1... | collective-permute-start | bytes 589832 | tf_op jit(solution)/shard_map/ppermute | solution.py:505
  121.5 7.9 %collective-permute-start.25 = (bf16[144,256]{1,0:T(8,128)(2,1)S(1)}, bf16[144,256]{1,0:T(8,128)(2,1)S(1)}, u32[]{:S(2)}, u32[]{:S(2)}) collective-permute-start(bf16[144,256]{1,0:T(8,128)(2,1)S(1)} %get-tuple-element.78), channel_id=1, source_target_pairs={{0,8},{4,12},{8,0},{12,4},{1,9},{5,13},{9,1},{13,5},{2,10},{6,14},... | collective-permute-start | bytes 221192 | tf_op jit(solution)/shard_map/ppermute | solution.py:444
  (11 other events, 88.4 us)

commit v3 on v2

--- a/solution.py
+++ b/solution.py
@@ -43,21 +43,27 @@
     return jnp.broadcast_to(values[:, n : n + 1], (values.shape[0], LANES))
 
 
-def store_edges(z, x, span, new, depth, across, core, refs):
-    low_refs, high_refs, edge_ref = refs
-    value = new.astype(BF16)
-    width = across // len(low_refs)
-    if z < RADIUS:
-        low_refs[x // width][z, x % width, span] = value
-    if z >= depth - RADIUS:
-        high_refs[x // width][z - depth + RADIUS, x % width, span] = value
-
-    for mine, first in ((0, across - RADIUS), (1, 0)):
-        if first <= x < first + RADIUS:
-
-            @pl.when(core == mine)
-            def _():
-                edge_ref[z, x - first, span] = value
+def store_edges(x, span, news, even, refs):
+    even_refs, odd_refs = refs
+    width = even_refs[0].shape[1]
+    part, x = x // width, x % width
+    for j in range(RADIUS):
+        low = news[j].astype(BF16)
+        high = news[len(news) - RADIUS + j].astype(BF16)
+        even_refs[part][j, x, span] = jnp.where(even, high, low)
+        odd_refs[part][j, x, span] = jnp.where(even, low, high)
+
+
+def store_beside(span, rows, core, u_ref, edge_ref):
+    depth, across, _, _ = u_ref.shape
+    first = (across - RADIUS) * (1 - core)
+    for z in range(depth):
+        for j in range(RADIUS):
+            edge_ref[z, j, span] = u_ref[z, first + j, rows].astype(BF16)
+
+
+def slab_is_even():
+    return lax.rem(lax.axis_index("slab"), 2) == 0
 
 
 def clear_pads(u_ref):
@@ -80,24 +86,27 @@
     lax.fori_loop(0, along // TILE, one, 0)
 
 
-def first_body(chunk, p_ref, s_ref, u_ref, low_ref, high_ref, edge_ref, square, turned_s):
+def first_body(chunk, p_ref, s_ref, u_ref, even_ref, odd_ref, edge_ref, square, turned_s):
     depth, across, padded, _ = u_ref.shape
     along = padded - 2 * EDGE
     core = lax.axis_index("sub")
+    even = slab_is_even()
     turned_s[...] = turned(s_ref[0], square)
     clear_pads(u_ref)
 
     def tile(start):
         span = pl.ds(start, TILE)
+        rows = pl.ds(start + EDGE, TILE)
         source = turned_s[span]
-        for z in range(depth):
-            for x in range(across):
+        for x in range(across):
+            news = []
+            for z in range(depth):
                 p = p_ref[z, x, span, chunk * LANES : (chunk + 1) * LANES].astype(F32)
                 new = lane(source, z * across + x) * p
-                u_ref[z, x, pl.ds(start + EDGE, TILE)] = new
-                store_edges(
-                    z, x, span, new, depth, across, core, ([low_ref], [high_ref], edge_ref)
-                )
+                u_ref[z, x, rows] = new
+                news.append(new)
+            store_edges(x, span, news, even, ([even_ref], [odd_ref]))
+        store_beside(span, rows, core, u_ref, edge_ref)
 
     tiles(along, tile)
 
@@ -185,22 +194,27 @@
 
 
 def rim_body(first, kind, parts, *refs):
-    base_ref, below_ref, above_ref, c_ref = refs[:4]
+    base_ref, even_ref, odd_ref, c_ref = refs[:4]
     outs, (square, turned_c) = refs[4:-2], refs[-2:]
     depth, all_across, along, _ = base_ref.shape
-    across = below_ref.shape[1]
+    across = even_ref.shape[1]
     core = lax.axis_index("sub")
+    even = slab_is_even()
     turned_c[...] = turned(c_ref[...], square)
     if kind == "middle":
         clear_pads(outs[0])
 
     def tile(start):
         span = pl.ds(start, TILE)
+        rows = pl.ds(start + EDGE, TILE)
         courant = turned_c[span]
         for x in range(across):
             place = first + x
-            below = [below_ref[j, x, span].astype(F32) for j in range(RADIUS)]
-            above = [above_ref[j, x, span].astype(F32) for j in range(RADIUS)]
+            below, above = [], []
+            for j in range(RADIUS):
+                one, two = even_ref[j, x, span], odd_ref[j, x, span]
+                below.append(jnp.where(even, two, one).astype(F32))
+                above.append(jnp.where(even, one, two).astype(F32))
             news = []
             for z in range(depth):
                 added = None
@@ -217,26 +231,28 @@
                 news.append(new)
             if kind == "middle":
                 for z, new in enumerate(news):
-                    outs[0][z, place, pl.ds(start + EDGE, TILE)] = new
-                    edges = (outs[1 : 1 + parts], outs[1 + parts : 1 + 2 * parts], outs[-1])
-                    store_edges(z, place, span, new, depth, all_across, core, edges)
+                    outs[0][z, place, rows] = new
+                edges = (outs[1 : 1 + parts], outs[1 + parts : 1 + 2 * parts])
+                store_edges(place, span, news, even, edges)
             elif kind == "half":
                 keep_ref, send_ref = outs
                 lower = lax.axis_index("probe") == 0
                 for z in range(depth // 2):
-                    one, two = news[z], news[z + depth // 2]
-                    keep_ref[z, x, span] = jnp.where(lower, one, two).astype(BF16)
-                    send_ref[z, x, span] = jnp.where(lower, two, one).astype(BF16)
+                    one, two = news[z].astype(BF16), news[z + depth // 2].astype(BF16)
+                    keep_ref[z, x, span] = jnp.where(lower, one, two)
+                    send_ref[z, x, span] = jnp.where(lower, two, one)
             else:
                 for z, new in enumerate(news):
                     outs[0][z, x, span] = new.astype(BF16)
+        if kind == "middle":
+            store_beside(span, rows, core, outs[0], outs[-1])
 
     tiles(along, tile)
 
 
-def rim_step(base, below, above, courant, kind, first=0, parts=1):
+def rim_step(base, evens, odds, courant, kind, first=0, parts=1):
     depth, all_across, along, _ = base.shape
-    across = below.shape[1]
+    across = evens.shape[1]
     if kind == "middle":
         edge = [shape_of(RADIUS, across // parts, along, BF16)] * parts
         out_shape = [shape_of(depth, across, along + 2 * EDGE, F32)]
@@ -252,17 +268,24 @@
         out_shape=out_shape,
         scratch_shapes=square_scratch(),
         compiler_params=params(),
-    )(base, below, above, courant)
-
-
-def exchange(lows, highs, edge):
+    )(base, evens, odds, courant)
+
+
+def swap(x, axis, pairs):
+    return lax.ppermute(x, axis, [p for a, b in pairs for p in ((a, b), (b, a))])
+
+
+def exchange(evens, odds, edge):
     slabs = lax.axis_size("slab")
-    up = [(i, i + 1) for i in range(slabs - 1)]
-    down = [(i + 1, i) for i in range(slabs - 1)]
     pairs = []
-    for low, high in zip(lows, highs):
-        pairs.append((lax.ppermute(high, "slab", up), lax.ppermute(low, "slab", down)))
-    return pairs, lax.ppermute(edge, "sub", [(0, 1), (1, 0)])
+    for one, two in zip(evens, odds):
+        pairs.append(
+            (
+                swap(one, "slab", [(i, i + 1) for i in range(0, slabs - 1, 2)]),
+                swap(two, "slab", [(i, i + 1) for i in range(1, slabs - 1, 2)]),
+            )
+        )
+    return pairs, swap(edge, "sub", [(0, 1)])
 
 
 def gram_body(parts, pieces, *refs):
@@ -348,7 +371,7 @@
     size = slabs * count
     tail = keep_ref[pl.ds(size, 8)] + got_ref[pl.ds(size, 8)]
     for d in range(slabs):
-        owner = lax.rem(slab + d, slabs)
+        owner = slab ^ d
         span = pl.ds(pl.multiple_of(owner * count, count), count)
         block = keep_ref[span] + got_ref[span]
         if d == 0:
@@ -438,10 +461,10 @@
 def coupled(pieces, fields, cells, cell_count):
     slabs = 4
     keep, send = gram(4, pieces, fields, cells)
-    got = lax.ppermute(send, "sub", [(0, 1), (1, 0)])
+    got = swap(send, "sub", [(0, 1)])
     own, *sent = split_rows(keep, got, slabs)
     arrived = [
-        lax.ppermute(block, "slab", [(i, (i + d) % slabs) for i in range(slabs)])
+        lax.ppermute(block, "slab", [(i, i ^ d) for i in range(slabs)])
         for d, block in enumerate(sent, 1)
     ]
     mine = sum_all(own, arrived)
@@ -487,9 +510,9 @@
 
     now, previous, halos = [], [None] * chunks, []
     for c in range(chunks):
-        u, low, high, edge = first_field(probes, c, source)
+        u, one, two, edge = first_field(probes, c, source)
         now.append(u)
-        halos.append(exchange([low], [high], edge))
+        halos.append(exchange([one], [two], edge))
     pieces, fields = [], []
     for n in range(1, steps):
         for c in range(chunks):
@@ -497,18 +520,18 @@
             base = local_step(now[c], beside, probes, c, courant, source, n, previous[c])
             if n == steps - 1:
                 width = across // len(pairs)
-                for h, (below, above) in enumerate(pairs):
+                for h, (one, two) in enumerate(pairs):
                     kind = "half" if paired else "all"
-                    out = rim_step(base, below, above, courant, kind, h * width)
+                    out = rim_step(base, one, two, courant, kind, h * width)
                     if paired:
                         pieces.append((c, h * width))
-                        fields += [out[0], lax.ppermute(out[1], "probe", [(0, 1), (1, 0)])]
+                        fields += [out[0], swap(out[1], "probe", [(0, 1)])]
                     else:
                         fields.append(out[0])
             else:
-                parts = 2 if paired and n == steps - 2 and c == chunks - 1 else 1
-                ((below, above),) = pairs
-                out = rim_step(base, below, above, courant, "middle", parts=parts)
+                parts = 2 if paired and n == steps - 2 else 1
+                ((one, two),) = pairs
+                out = rim_step(base, one, two, courant, "middle", parts=parts)
                 previous[c], now[c] = now[c], out[0]
                 halos[c] = exchange(out[1 : 1 + parts], out[1 + parts : 1 + 2 * parts], out[-1])
     if paired:

time: 137 us -> 107 us (0.78)
  Pallas kernels: 57.1 us -> 24.7 us
  waiting for transfers between devices: 22.2 us -> 23.8 us
    pallas_call x2, Pallas kernels: 28.3 us -> 2.1 us  [first_field(): pl.pallas_call(functools.partial(first_body, chunk), in_specs=whole_vmem(...]
    pallas_call x7 -> x8, Pallas kernels: 13.3 us -> 6.97 us  [rim_step(): pl.pallas_call(functools.partial(rim_body, first, kind, parts), in_specs=...]
    ppermute x27 -> x30, waiting for transfers between devices: 18.2 us -> 19.8 us  [the longest x27 13.8 us: swap(): lax.ppermute(x, axis, [p for a, b in pairs for p in ((a, b), (b, a))])]
    ppermute x27 -> x30, starting transfers between devices: 51.9 us -> 52.7 us  [the longest x27 47.2 us: swap(): lax.ppermute(x, axis, [p for a, b in pairs for p in ((a, b), (b, a))])]
  transfers between devices with their start and end apart: 30 -> 33, of which waited for: 9 -> 9; matrix products, arithmetic and copies ran while one was open for 0% -> 0% of each run, Pallas kernels for 30% -> 20%
where the time goes in v3:
time: 107 us
  starting transfers between devices  54.9 us (51%)
  Pallas kernels  24.7 us (23%)
  waiting for transfers between devices  23.8 us (22%)
  local copies, waits for them, and re-layouts  2.32 us (2%)
    ppermute x27, starting transfers between devices, swap(): lax.ppermute(x, axis, [p for a, b in pairs for p in ((a, b), (b, a))])  47.2 us
    ppermute x27, waiting for transfers between devices, swap(): lax.ppermute(x, axis, [p for a, b in pairs for p in ((a, b), (b, a))])  13.8 us
    pallas_call x6, Pallas kernels, local_step(): pl.pallas_call(functools.partial(local_body, chunk, moment, previous is n...  13.3 us
    pallas_call x8, Pallas kernels, rim_step(): pl.pallas_call(functools.partial(rim_body, first, kind, parts), in_specs=...  6.97 us
    ppermute x3, waiting for transfers between devices, coupled(): lax.ppermute(block, 'slab', [(i, i ^ d) for i in range(slabs)])  5.92 us
    ppermute x3, starting transfers between devices, coupled(): lax.ppermute(block, 'slab', [(i, i ^ d) for i in range(slabs)])  5.48 us
    ppermute x3, waiting for transfers between devices, coupled(): lax.ppermute(mine, both, [(i, i ^ flip) for i in range(4)])  4 us
    unnamed x10, local copies, waits for them, and re-layouts  2.32 us
  transfers between devices with their start and end apart: 33, of which 9 were waited for; matrix products, arithmetic and copies ran while one was open for 0% of the time, Pallas kernels for 20%

profile of v3, /device:TPU:0, one launch (start us, length us, event | category | flops | bytes accessed | tf_op | source)
XLA Modules:
  0.0 106.6 jit_solution(13820322027406096030)
XLA Ops:
  4.5 2.7 %collective-permute-start.14 = (bf16[4,8,48,128]{3,2,1,0:T(8,128)(2,1)S(1)}, bf16[4,8,48,128]{3,2,1,0:T(8,128)(2,1)S(1)}, u32[]{:S(2)}, u32[]{:S(2)}) collective-permute-start(bf16[4,8,48,128]{3,2,1,0:T(8,128)(2,1)S(1)} %get-tuple-element.66), channel_id=1, source_target_pairs={{0,4},{4,0},{8,12},{12,8},{1,5},{5,1},{9,13},{13,9},{2,6},{6,2},{1... | collective-permute-start | bytes 1179656 | tf_op jit(solution)/shard_map/ppermute | solution.py:275
  9.1 4.3 %collective-permute-start.1 = (bf16[4,8,48,128]{3,2,1,0:T(8,128)(2,1)S(1)}, bf16[4,8,48,128]{3,2,1,0:T(8,128)(2,1)S(1)}, u32[]{:S(2)}, u32[]{:S(2)}) collective-permute-start(bf16[4,8,48,128]{3,2,1,0:T(8,128)(2,1)S(1)} %get-tuple-element.48), channel_id=1, source_target_pairs={{0,4},{4,0},{8,12},{12,8},{1,5},{5,1},{9,13},{13,9},{2,6},{6,2},{1... | collective-permute-start | bytes 1179656 | tf_op jit(solution)/shard_map/ppermute | solution.py:275
  14.1 2.2 %shard_map.59.refs_0_ = f32[8,8,48,128]{3,2,1,0:T(8,128)S(1)} custom-call(f32[8,8,64,128]{3,2,1,0:T(8,128)S(1)} %get-tuple-element.64.refs_0_.refs_5_, bf16[8,4,48,128]{3,2,1,0:T(8,128)(2,1)S(1)} %collective-permute-done.13.refs_1_, bf16[8,8,48,256]{3,2,1,0:T(8,128)(2,1)S(1)} %copy-done, f32[64,48]{1,0:T(8,128)S(1)} %bitcast.11, f32[4,64,48]{2,1,0:T(8,128)S(1)} %bitcast.5), custom_call_target="tpu_custom_call" | custom-call | tf_op jit(solution)/shard_map/pallas_call | solution.py:186
  18.3 5.0 %collective-permute-start.17 = (bf16[4,8,48,128]{3,2,1,0:T(8,128)(2,1)S(1)}, bf16[4,8,48,128]{3,2,1,0:T(8,128)(2,1)S(1)}, u32[]{:S(2)}, u32[]{:S(2)}) collective-permute-start(bf16[4,8,48,128]{3,2,1,0:T(8,128)(2,1)S(1)} %get-tuple-element.70), channel_id=1, source_target_pairs={{0,4},{4,0},{8,12},{12,8},{1,5},{5,1},{9,13},{13,9},{2,6},{6,2},{1... | collective-permute-start | bytes 1179656 | tf_op jit(solution)/shard_map/ppermute | solution.py:275
  24.1 2.1 %shard_map.51.refs_0_ = f32[8,8,48,128]{3,2,1,0:T(8,128)S(1)} custom-call(f32[8,8,64,128]{3,2,1,0:T(8,128)S(1)} %get-tuple-element.46.refs_0_.refs_5_, bf16[8,4,48,128]{3,2,1,0:T(8,128)(2,1)S(1)} %collective-permute-done.refs_1_, bf16[8,8,48,256]{3,2,1,0:T(8,128)(2,1)S(1)} %copy-done.1, f32[64,48]{1,0:T(8,128)S(1)} %bitcast.13, f32[4,64,48]{2,1,0:T(8,128)S(1)} %bitcast.6), custom_call_target="tpu_custom_call" | custom-call | tf_op jit(solution)/shard_map/pallas_call | solution.py:186
  27.6 4.2 %collective-permute-start.4 = (bf16[4,8,48,128]{3,2,1,0:T(8,128)(2,1)S(1)}, bf16[4,8,48,128]{3,2,1,0:T(8,128)(2,1)S(1)}, u32[]{:S(2)}, u32[]{:S(2)}) collective-permute-start(bf16[4,8,48,128]{3,2,1,0:T(8,128)(2,1)S(1)} %get-tuple-element.52), channel_id=1, source_target_pairs={{0,4},{4,0},{8,12},{12,8},{1,5},{5,1},{9,13},{13,9},{2,6},{6,2},{1... | collective-permute-start | bytes 1179656 | tf_op jit(solution)/shard_map/ppermute | solution.py:275
  32.5 2.3 %shard_map.61.refs_0_ = f32[8,8,48,128]{3,2,1,0:T(8,128)S(1)} custom-call(f32[8,8,64,128]{3,2,1,0:T(8,128)S(1)} %get-tuple-element.68.refs_0_.refs_5_, bf16[8,4,48,128]{3,2,1,0:T(8,128)(2,1)S(1)} %collective-permute-done.16.refs_1_, bf16[8,8,48,256]{3,2,1,0:T(8,128)(2,1)S(1)} %copy-done.1, f32[64,48]{1,0:T(8,128)S(1)} %bitcast.15, f32[4,64,48]{2,1,0:T(8,128)S(1)} %bitcast.7, ...), custom_call_target="tpu_custom_call" | custom-call | tf_op jit(solution)/shard_map/pallas_call | solution.py:186
  35.9 4.3 %collective-permute-start.20 = (bf16[4,4,48,128]{3,2,1,0:T(8,128)(2,1)S(1)}, bf16[4,4,48,128]{3,2,1,0:T(8,128)(2,1)S(1)}, u32[]{:S(2)}, u32[]{:S(2)}) collective-permute-start(bf16[4,4,48,128]{3,2,1,0:T(8,128)(2,1)S(1)} %get-tuple-element.74), channel_id=1, source_target_pairs={{0,4},{4,0},{8,12},{12,8},{1,5},{5,1},{9,13},{13,9},{2,6},{6,2},{1... | collective-permute-start | bytes 589832 | tf_op jit(solution)/shard_map/ppermute | solution.py:275
  40.1 2.3 %shard_map.53.refs_0_ = f32[8,8,48,128]{3,2,1,0:T(8,128)S(1)} custom-call(f32[8,8,64,128]{3,2,1,0:T(8,128)S(1)} %get-tuple-element.50.refs_0_.refs_5_, bf16[8,4,48,128]{3,2,1,0:T(8,128)(2,1)S(1)} %collective-permute-done.3.refs_1_, bf16[8,8,48,256]{3,2,1,0:T(8,128)(2,1)S(1)} %copy-done.1, f32[64,48]{1,0:T(8,128)S(1)} %bitcast.17, f32[4,64,48]{2,1,0:T(8,128)S(1)} %bitcast.8, ...), custom_call_target="tpu_custom_call" | custom-call | tf_op jit(solution)/shard_map/pallas_call | solution.py:186
  44.8 7.1 %collective-permute-start.23 = (bf16[4,4,48,128]{3,2,1,0:T(8,128)(2,1)S(1)}, bf16[4,4,48,128]{3,2,1,0:T(8,128)(2,1)S(1)}, u32[]{:S(2)}, u32[]{:S(2)}) collective-permute-start(bf16[4,4,48,128]{3,2,1,0:T(8,128)(2,1)S(1)} %get-tuple-element.78), channel_id=1, source_target_pairs={{0,4},{4,0},{8,12},{12,8},{1,5},{5,1},{9,13},{13,9},{2,6},{6,2},{1... | collective-permute-start | bytes 589832 | tf_op jit(solution)/shard_map/ppermute | solution.py:275
  52.5 5.2 %collective-permute-start.10 = (bf16[4,4,48,128]{3,2,1,0:T(8,128)(2,1)S(1)}, bf16[4,4,48,128]{3,2,1,0:T(8,128)(2,1)S(1)}, u32[]{:S(2)}, u32[]{:S(2)}) collective-permute-start(bf16[4,4,48,128]{3,2,1,0:T(8,128)(2,1)S(1)} %get-tuple-element.60), channel_id=1, source_target_pairs={{0,4},{4,0},{8,12},{12,8},{1,5},{5,1},{9,13},{13,9},{2,6},{6,2},{1... | collective-permute-start | bytes 589832 | tf_op jit(solution)/shard_map/ppermute | solution.py:275
  58.4 3.1 %collective-permute-start.7 = (bf16[4,4,48,128]{3,2,1,0:T(8,128)(2,1)S(1)}, bf16[4,4,48,128]{3,2,1,0:T(8,128)(2,1)S(1)}, u32[]{:S(2)}, u32[]{:S(2)}) collective-permute-start(bf16[4,4,48,128]{3,2,1,0:T(8,128)(2,1)S(1)} %get-tuple-element.56), channel_id=1, source_target_pairs={{0,4},{4,0},{8,12},{12,8},{1,5},{5,1},{9,13},{13,9},{2,6},{6,2},{1... | collective-permute-start | bytes 589832 | tf_op jit(solution)/shard_map/ppermute | solution.py:275
  62.2 2.3 %shard_map.63.refs_0_ = f32[8,8,48,128]{3,2,1,0:T(8,128)S(1)} custom-call(f32[8,8,64,128]{3,2,1,0:T(8,128)S(1)} %get-tuple-element.72.refs_0_, bf16[8,4,48,128]{3,2,1,0:T(8,128)(2,1)S(1)} %collective-permute-done.19.refs_1_, bf16[8,8,48,256]{3,2,1,0:T(8,128)(2,1)S(1)} %copy-done.1, f32[64,48]{1,0:T(8,128)S(1)} %bitcast.19, f32[4,64,48]{2,1,0:T(8,128)S(1)} %bitcast.9, ...), custom_call_target="tpu_custom_call" | custom-call | tf_op jit(solution)/shard_map/pallas_call | solution.py:186
  65.8 1.6 %collective-permute-start.25 = (bf16[4,4,48,128]{3,2,1,0:T(8,128)(2,1)S(1)}, bf16[4,4,48,128]{3,2,1,0:T(8,128)(2,1)S(1)}, u32[]{:S(2)}, u32[]{:S(2)}) collective-permute-start(bf16[4,4,48,128]{3,2,1,0:T(8,128)(2,1)S(1)} %get-tuple-element.81), channel_id=1, source_target_pairs={{0,2},{2,0},{1,3},{3,1},{4,6},{6,4},{5,7},{7,5},{8,10},{10,8},{9,1... | collective-permute-start | bytes 589832 | tf_op jit(solution)/shard_map/ppermute | solution.py:275
  67.3 2.2 %shard_map.55.refs_0_ = f32[8,8,48,128]{3,2,1,0:T(8,128)S(1)} custom-call(f32[8,8,64,128]{3,2,1,0:T(8,128)S(1)} %get-tuple-element.54.refs_0_, bf16[8,4,48,128]{3,2,1,0:T(8,128)(2,1)S(1)} %collective-permute-done.6.refs_1_, bf16[8,8,48,256]{3,2,1,0:T(8,128)(2,1)S(1)} %copy-done.1, f32[64,48]{1,0:T(8,128)S(1)} %bitcast.22, f32[4,64,48]{2,1,0:T(8,128)S(1)} %bitcast.10, ...), custom_call_target="tpu_custom_call" | custom-call | tf_op jit(solution)/shard_map/pallas_call | solution.py:186
  73.7 3.8 %collective-permute-done.22.refs_5_ = bf16[4,4,48,128]{3,2,1,0:T(8,128)(2,1)S(1)} collective-permute-done((bf16[4,4,48,128]{3,2,1,0:T(8,128)(2,1)S(1)}, bf16[4,4,48,128]{3,2,1,0:T(8,128)(2,1)S(1)}, u32[]{:S(2)}, u32[]{:S(2)}) %collective-permute-start.22) | collective-permute-done | bytes 196640 | tf_op jit(solution)/shard_map/ppermute | solution.py:275
  77.5 4.2 %collective-permute-done.12.refs_3_ = bf16[4,4,48,128]{3,2,1,0:T(8,128)(2,1)S(1)} collective-permute-done((bf16[4,4,48,128]{3,2,1,0:T(8,128)(2,1)S(1)}, bf16[4,4,48,128]{3,2,1,0:T(8,128)(2,1)S(1)}, u32[]{:S(2)}, u32[]{:S(2)}) %collective-permute-start.12) | collective-permute-done | bytes 196640 | tf_op jit(solution)/shard_map/ppermute | solution.py:275
  81.7 3.0 %collective-permute-done.9.refs_1_ = bf16[4,4,48,128]{3,2,1,0:T(8,128)(2,1)S(1)} collective-permute-done((bf16[4,4,48,128]{3,2,1,0:T(8,128)(2,1)S(1)}, bf16[4,4,48,128]{3,2,1,0:T(8,128)(2,1)S(1)}, u32[]{:S(2)}, u32[]{:S(2)}) %collective-permute-start.9) | collective-permute-done | bytes 196640 | tf_op jit(solution)/shard_map/ppermute | solution.py:275
  86.1 1.9 %collective-permute-done.26.got_ref = f32[520,256]{1,0:T(8,128)S(1)} collective-permute-done((f32[520,256]{1,0:T(8,128)S(1)}, f32[520,256]{1,0:T(8,128)S(1)}, u32[]{:S(2)}, u32[]{:S(2)}) %collective-permute-start.26) | collective-permute-done | bytes 532512 | tf_op jit(solution)/shard_map/ppermute | solution.py:275
  88.1 3.0 %collective-permute-start.27 = (bf16[144,256]{1,0:T(8,128)(2,1)S(1)}, bf16[144,256]{1,0:T(8,128)(2,1)S(1)}, u32[]{:S(2)}, u32[]{:S(2)}) collective-permute-start(bf16[144,256]{1,0:T(8,128)(2,1)S(1)} %get-tuple-element.85), channel_id=1, source_target_pairs={{0,4},{4,0},{8,12},{12,8},{1,5},{5,1},{9,13},{13,9},{2,6},{6,2},{1... | collective-permute-start | bytes 221192 | tf_op jit(solution)/shard_map/ppermute | solution.py:467
  91.4 2.2 %collective-permute-start.29 = (bf16[144,256]{1,0:T(8,128)(2,1)S(1)}, bf16[144,256]{1,0:T(8,128)(2,1)S(1)}, u32[]{:S(2)}, u32[]{:S(2)}) collective-permute-start(bf16[144,256]{1,0:T(8,128)(2,1)S(1)} %get-tuple-element.87), channel_id=1, source_target_pairs={{0,12},{4,8},{8,4},{12,0},{1,13},{5,9},{9,5},{13,1},{2,14},{6,10},... | collective-permute-start | bytes 221192 | tf_op jit(solution)/shard_map/ppermute | solution.py:467
  93.8 5.7 %collective-permute-done.28.refs_1_ = bf16[144,256]{1,0:T(8,128)(2,1)S(1)} collective-permute-done((bf16[144,256]{1,0:T(8,128)(2,1)S(1)}, bf16[144,256]{1,0:T(8,128)(2,1)S(1)}, u32[]{:S(2)}, u32[]{:S(2)}) %collective-permute-start.28) | collective-permute-done | bytes 73760 | tf_op jit(solution)/shard_map/ppermute | solution.py:467
  101.8 2.4 %collective-permute-done.32.d_ref = bf16[144,256]{1,0:T(8,128)(2,1)S(1)} collective-permute-done((bf16[144,256]{1,0:T(8,128)(2,1)S(1)}, bf16[144,256]{1,0:T(8,128)(2,1)S(1)}, u32[]{:S(2)}, u32[]{:S(2)}) %collective-permute-start.32) | collective-permute-done | bytes 73760 | tf_op jit(solution)/shard_map/ppermute | solution.py:473
  104.1 1.6 %collective-permute-done.30.b_ref = bf16[144,256]{1,0:T(8,128)(2,1)S(1)} collective-permute-done((bf16[144,256]{1,0:T(8,128)(2,1)S(1)}, bf16[144,256]{1,0:T(8,128)(2,1)S(1)}, u32[]{:S(2)}, u32[]{:S(2)}) %collective-permute-start.30) | collective-permute-done | bytes 73760 | tf_op jit(solution)/shard_map/ppermute | solution.py:473
  (72 shorter events, 27.0 us)
Async XLA Ops:
  4.0 9.4 %collective-permute-start.13 = (bf16[8,4,48,128]{3,2,1,0:T(8,128)(2,1)S(1)}, bf16[8,4,48,128]{3,2,1,0:T(8,128)(2,1)S(1)}, u32[]{:S(2)}, u32[]{:S(2)}) collective-permute-start(bf16[8,4,48,128]{3,2,1,0:T(8,128)(2,1)S(1)} %get-tuple-element.65), channel_id=1, source_target_pairs={{0,1},{1,0},{2,3},{3,2},{4,5},{5,4},{6,7},{7,6},{8,9},{9,8},{10,11... | collective-permute-start | bytes 1179656 | tf_op jit(solution)/shard_map/ppermute | solution.py:275
  4.5 12.6 %collective-permute-start.14 = (bf16[4,8,48,128]{3,2,1,0:T(8,128)(2,1)S(1)}, bf16[4,8,48,128]{3,2,1,0:T(8,128)(2,1)S(1)}, u32[]{:S(2)}, u32[]{:S(2)}) collective-permute-start(bf16[4,8,48,128]{3,2,1,0:T(8,128)(2,1)S(1)} %get-tuple-element.66), channel_id=1, source_target_pairs={{0,4},{4,0},{8,12},{12,8},{1,5},{5,1},{9,13},{13,9},{2,6},{6,2},{1... | collective-permute-start | bytes 1179656 | tf_op jit(solution)/shard_map/ppermute | solution.py:275
  7.2 10.0 %collective-permute-start.15 = (bf16[4,8,48,128]{3,2,1,0:T(8,128)(2,1)S(1)}, bf16[4,8,48,128]{3,2,1,0:T(8,128)(2,1)S(1)}, u32[]{:S(2)}, u32[]{:S(2)}) collective-permute-start(bf16[4,8,48,128]{3,2,1,0:T(8,128)(2,1)S(1)} %get-tuple-element.67), channel_id=1, source_target_pairs={{4,8},{8,4},{5,9},{9,5},{6,10},{10,6},{7,11},{11,7},{20,24},{24,20... | collective-permute-start | bytes 1179656 | tf_op jit(solution)/shard_map/ppermute | solution.py:275
  8.9 14.4 %collective-permute-start = (bf16[8,4,48,128]{3,2,1,0:T(8,128)(2,1)S(1)}, bf16[8,4,48,128]{3,2,1,0:T(8,128)(2,1)S(1)}, u32[]{:S(2)}, u32[]{:S(2)}) collective-permute-start(bf16[8,4,48,128]{3,2,1,0:T(8,128)(2,1)S(1)} %get-tuple-element.47), channel_id=1, source_target_pairs={{0,1},{1,0},{2,3},{3,2},{4,5},{5,4},{6,7},{7,6},{8,9},{9,8},{10,11... | collective-permute-start | bytes 1179656 | tf_op jit(solution)/shard_map/ppermute | solution.py:275
  9.1 17.1 %collective-permute-start.1 = (bf16[4,8,48,128]{3,2,1,0:T(8,128)(2,1)S(1)}, bf16[4,8,48,128]{3,2,1,0:T(8,128)(2,1)S(1)}, u32[]{:S(2)}, u32[]{:S(2)}) collective-permute-start(bf16[4,8,48,128]{3,2,1,0:T(8,128)(2,1)S(1)} %get-tuple-element.48), channel_id=1, source_target_pairs={{0,4},{4,0},{8,12},{12,8},{1,5},{5,1},{9,13},{13,9},{2,6},{6,2},{1... | collective-permute-start | bytes 1179656 | tf_op jit(solution)/shard_map/ppermute | solution.py:275
  13.4 12.8 %collective-permute-start.2 = (bf16[4,8,48,128]{3,2,1,0:T(8,128)(2,1)S(1)}, bf16[4,8,48,128]{3,2,1,0:T(8,128)(2,1)S(1)}, u32[]{:S(2)}, u32[]{:S(2)}) collective-permute-start(bf16[4,8,48,128]{3,2,1,0:T(8,128)(2,1)S(1)} %get-tuple-element.49), channel_id=1, source_target_pairs={{4,8},{8,4},{5,9},{9,5},{6,10},{10,6},{7,11},{11,7},{20,24},{24,20... | collective-permute-start | bytes 1179656 | tf_op jit(solution)/shard_map/ppermute | solution.py:275
  18.2 13.5 %collective-permute-start.16 = (bf16[8,4,48,128]{3,2,1,0:T(8,128)(2,1)S(1)}, bf16[8,4,48,128]{3,2,1,0:T(8,128)(2,1)S(1)}, u32[]{:S(2)}, u32[]{:S(2)}) collective-permute-start(bf16[8,4,48,128]{3,2,1,0:T(8,128)(2,1)S(1)} %get-tuple-element.69), channel_id=1, source_target_pairs={{0,1},{1,0},{2,3},{3,2},{4,5},{5,4},{6,7},{7,6},{8,9},{9,8},{10,11... | collective-permute-start | bytes 1179656 | tf_op jit(solution)/shard_map/ppermute | solution.py:275
  18.3 16.4 %collective-permute-start.17 = (bf16[4,8,48,128]{3,2,1,0:T(8,128)(2,1)S(1)}, bf16[4,8,48,128]{3,2,1,0:T(8,128)(2,1)S(1)}, u32[]{:S(2)}, u32[]{:S(2)}) collective-permute-start(bf16[4,8,48,128]{3,2,1,0:T(8,128)(2,1)S(1)} %get-tuple-element.70), channel_id=1, source_target_pairs={{0,4},{4,0},{8,12},{12,8},{1,5},{5,1},{9,13},{13,9},{2,6},{6,2},{1... | collective-permute-start | bytes 1179656 | tf_op jit(solution)/shard_map/ppermute | solution.py:275
  23.4 11.4 %collective-permute-start.18 = (bf16[4,8,48,128]{3,2,1,0:T(8,128)(2,1)S(1)}, bf16[4,8,48,128]{3,2,1,0:T(8,128)(2,1)S(1)}, u32[]{:S(2)}, u32[]{:S(2)}) collective-permute-start(bf16[4,8,48,128]{3,2,1,0:T(8,128)(2,1)S(1)} %get-tuple-element.71), channel_id=1, source_target_pairs={{4,8},{8,4},{5,9},{9,5},{6,10},{10,6},{7,11},{11,7},{20,24},{24,20... | collective-permute-start | bytes 1179656 | tf_op jit(solution)/shard_map/ppermute | solution.py:275
  27.3 12.8 %collective-permute-start.3 = (bf16[8,4,48,128]{3,2,1,0:T(8,128)(2,1)S(1)}, bf16[8,4,48,128]{3,2,1,0:T(8,128)(2,1)S(1)}, u32[]{:S(2)}, u32[]{:S(2)}) collective-permute-start(bf16[8,4,48,128]{3,2,1,0:T(8,128)(2,1)S(1)} %get-tuple-element.51), channel_id=1, source_target_pairs={{0,1},{1,0},{2,3},{3,2},{4,5},{5,4},{6,7},{7,6},{8,9},{9,8},{10,11... | collective-permute-start | bytes 1179656 | tf_op jit(solution)/shard_map/ppermute | solution.py:275
  27.6 14.8 %collective-permute-start.4 = (bf16[4,8,48,128]{3,2,1,0:T(8,128)(2,1)S(1)}, bf16[4,8,48,128]{3,2,1,0:T(8,128)(2,1)S(1)}, u32[]{:S(2)}, u32[]{:S(2)}) collective-permute-start(bf16[4,8,48,128]{3,2,1,0:T(8,128)(2,1)S(1)} %get-tuple-element.52), channel_id=1, source_target_pairs={{0,4},{4,0},{8,12},{12,8},{1,5},{5,1},{9,13},{13,9},{2,6},{6,2},{1... | collective-permute-start | bytes 1179656 | tf_op jit(solution)/shard_map/ppermute | solution.py:275
  31.8 10.6 %collective-permute-start.5 = (bf16[4,8,48,128]{3,2,1,0:T(8,128)(2,1)S(1)}, bf16[4,8,48,128]{3,2,1,0:T(8,128)(2,1)S(1)}, u32[]{:S(2)}, u32[]{:S(2)}) collective-permute-start(bf16[4,8,48,128]{3,2,1,0:T(8,128)(2,1)S(1)} %get-tuple-element.53), channel_id=1, source_target_pairs={{4,8},{8,4},{5,9},{9,5},{6,10},{10,6},{7,11},{11,7},{20,24},{24,20... | collective-permute-start | bytes 1179656 | tf_op jit(solution)/shard_map/ppermute | solution.py:275
  35.9 16.0 %collective-permute-start.20 = (bf16[4,4,48,128]{3,2,1,0:T(8,128)(2,1)S(1)}, bf16[4,4,48,128]{3,2,1,0:T(8,128)(2,1)S(1)}, u32[]{:S(2)}, u32[]{:S(2)}) collective-permute-start(bf16[4,4,48,128]{3,2,1,0:T(8,128)(2,1)S(1)} %get-tuple-element.74), channel_id=1, source_target_pairs={{0,4},{4,0},{8,12},{12,8},{1,5},{5,1},{9,13},{13,9},{2,6},{6,2},{1... | collective-permute-start | bytes 589832 | tf_op jit(solution)/shard_map/ppermute | solution.py:275
  40.1 21.4 %collective-permute-start.19 = (bf16[8,4,48,128]{3,2,1,0:T(8,128)(2,1)S(1)}, bf16[8,4,48,128]{3,2,1,0:T(8,128)(2,1)S(1)}, u32[]{:S(2)}, u32[]{:S(2)}) collective-permute-start(bf16[8,4,48,128]{3,2,1,0:T(8,128)(2,1)S(1)} %get-tuple-element.73), channel_id=1, source_target_pairs={{0,1},{1,0},{2,3},{3,2},{4,5},{5,4},{6,7},{7,6},{8,9},{9,8},{10,11... | collective-permute-start | bytes 1179656 | tf_op jit(solution)/shard_map/ppermute | solution.py:275
  43.5 22.2 %collective-permute-start.6 = (bf16[8,4,48,128]{3,2,1,0:T(8,128)(2,1)S(1)}, bf16[8,4,48,128]{3,2,1,0:T(8,128)(2,1)S(1)}, u32[]{:S(2)}, u32[]{:S(2)}) collective-permute-start(bf16[8,4,48,128]{3,2,1,0:T(8,128)(2,1)S(1)} %get-tuple-element.55), channel_id=1, source_target_pairs={{0,1},{1,0},{2,3},{3,2},{4,5},{5,4},{6,7},{7,6},{8,9},{9,8},{10,11... | collective-permute-start | bytes 1179656 | tf_op jit(solution)/shard_map/ppermute | solution.py:275
  44.1 8.4 %collective-permute-start.21 = (bf16[4,4,48,128]{3,2,1,0:T(8,128)(2,1)S(1)}, bf16[4,4,48,128]{3,2,1,0:T(8,128)(2,1)S(1)}, u32[]{:S(2)}, u32[]{:S(2)}) collective-permute-start(bf16[4,4,48,128]{3,2,1,0:T(8,128)(2,1)S(1)} %get-tuple-element.75), channel_id=1, source_target_pairs={{4,8},{8,4},{5,9},{9,5},{6,10},{10,6},{7,11},{11,7},{20,24},{24,20... | collective-permute-start | bytes 589832 | tf_op jit(solution)/shard_map/ppermute | solution.py:275
  44.8 12.9 %collective-permute-start.23 = (bf16[4,4,48,128]{3,2,1,0:T(8,128)(2,1)S(1)}, bf16[4,4,48,128]{3,2,1,0:T(8,128)(2,1)S(1)}, u32[]{:S(2)}, u32[]{:S(2)}) collective-permute-start(bf16[4,4,48,128]{3,2,1,0:T(8,128)(2,1)S(1)} %get-tuple-element.78), channel_id=1, source_target_pairs={{0,4},{4,0},{8,12},{12,8},{1,5},{5,1},{9,13},{13,9},{2,6},{6,2},{1... | collective-permute-start | bytes 589832 | tf_op jit(solution)/shard_map/ppermute | solution.py:275
  52.5 17.1 %collective-permute-start.10 = (bf16[4,4,48,128]{3,2,1,0:T(8,128)(2,1)S(1)}, bf16[4,4,48,128]{3,2,1,0:T(8,128)(2,1)S(1)}, u32[]{:S(2)}, u32[]{:S(2)}) collective-permute-start(bf16[4,4,48,128]{3,2,1,0:T(8,128)(2,1)S(1)} %get-tuple-element.60), channel_id=1, source_target_pairs={{0,4},{4,0},{8,12},{12,8},{1,5},{5,1},{9,13},{13,9},{2,6},{6,2},{1... | collective-permute-start | bytes 589832 | tf_op jit(solution)/shard_map/ppermute | solution.py:275
  57.7 12.5 %collective-permute-start.11 = (bf16[4,4,48,128]{3,2,1,0:T(8,128)(2,1)S(1)}, bf16[4,4,48,128]{3,2,1,0:T(8,128)(2,1)S(1)}, u32[]{:S(2)}, u32[]{:S(2)}) collective-permute-start(bf16[4,4,48,128]{3,2,1,0:T(8,128)(2,1)S(1)} %get-tuple-element.61), channel_id=1, source_target_pairs={{4,8},{8,4},{5,9},{9,5},{6,10},{10,6},{7,11},{11,7},{20,24},{24,20... | collective-permute-start | bytes 589832 | tf_op jit(solution)/shard_map/ppermute | solution.py:275
  58.4 14.0 %collective-permute-start.7 = (bf16[4,4,48,128]{3,2,1,0:T(8,128)(2,1)S(1)}, bf16[4,4,48,128]{3,2,1,0:T(8,128)(2,1)S(1)}, u32[]{:S(2)}, u32[]{:S(2)}) collective-permute-start(bf16[4,4,48,128]{3,2,1,0:T(8,128)(2,1)S(1)} %get-tuple-element.56), channel_id=1, source_target_pairs={{0,4},{4,0},{8,12},{12,8},{1,5},{5,1},{9,13},{13,9},{2,6},{6,2},{1... | collective-permute-start | bytes 589832 | tf_op jit(solution)/shard_map/ppermute | solution.py:275
  61.5 10.9 %collective-permute-start.8 = (bf16[4,4,48,128]{3,2,1,0:T(8,128)(2,1)S(1)}, bf16[4,4,48,128]{3,2,1,0:T(8,128)(2,1)S(1)}, u32[]{:S(2)}, u32[]{:S(2)}) collective-permute-start(bf16[4,4,48,128]{3,2,1,0:T(8,128)(2,1)S(1)} %get-tuple-element.57), channel_id=1, source_target_pairs={{4,8},{8,4},{5,9},{9,5},{6,10},{10,6},{7,11},{11,7},{20,24},{24,20... | collective-permute-start | bytes 589832 | tf_op jit(solution)/shard_map/ppermute | solution.py:275
  70.9 10.9 %collective-permute-start.12 = (bf16[4,4,48,128]{3,2,1,0:T(8,128)(2,1)S(1)}, bf16[4,4,48,128]{3,2,1,0:T(8,128)(2,1)S(1)}, u32[]{:S(2)}, u32[]{:S(2)}) collective-permute-start(bf16[4,4,48,128]{3,2,1,0:T(8,128)(2,1)S(1)} %get-tuple-element.63), channel_id=1, source_target_pairs={{0,2},{2,0},{1,3},{3,1},{4,6},{6,4},{5,7},{7,5},{8,10},{10,8},{9,1... | collective-permute-start | bytes 589832 | tf_op jit(solution)/shard_map/ppermute | solution.py:275
  73.1 11.6 %collective-permute-start.9 = (bf16[4,4,48,128]{3,2,1,0:T(8,128)(2,1)S(1)}, bf16[4,4,48,128]{3,2,1,0:T(8,128)(2,1)S(1)}, u32[]{:S(2)}, u32[]{:S(2)}) collective-permute-start(bf16[4,4,48,128]{3,2,1,0:T(8,128)(2,1)S(1)} %get-tuple-element.59), channel_id=1, source_target_pairs={{0,2},{2,0},{1,3},{3,1},{4,6},{6,4},{5,7},{7,5},{8,10},{10,8},{9,1... | collective-permute-start | bytes 589832 | tf_op jit(solution)/shard_map/ppermute | solution.py:275
  91.1 8.4 %collective-permute-start.28 = (bf16[144,256]{1,0:T(8,128)(2,1)S(1)}, bf16[144,256]{1,0:T(8,128)(2,1)S(1)}, u32[]{:S(2)}, u32[]{:S(2)}) collective-permute-start(bf16[144,256]{1,0:T(8,128)(2,1)S(1)} %get-tuple-element.86), channel_id=1, source_target_pairs={{0,8},{4,12},{8,0},{12,4},{1,9},{5,13},{9,1},{13,5},{2,10},{6,14},... | collective-permute-start | bytes 221192 | tf_op jit(solution)/shard_map/ppermute | solution.py:467
  (14 other events, 80.4 us)

commit v4 on v3

--- a/solution.py
+++ b/solution.py
@@ -529,11 +529,10 @@
                     else:
                         fields.append(out[0])
             else:
-                parts = 2 if paired and n == steps - 2 else 1
                 ((one, two),) = pairs
-                out = rim_step(base, one, two, courant, "middle", parts=parts)
+                out = rim_step(base, one, two, courant, "middle")
                 previous[c], now[c] = now[c], out[0]
-                halos[c] = exchange(out[1 : 1 + parts], out[1 + parts : 1 + 2 * parts], out[-1])
+                halos[c] = exchange([out[1]], [out[2]], out[3])
     if paired:
         cells = depth // 2 * across * along
         return coupled(tuple(pieces), fields, cells, cell_count)

time: 107 us -> 95.2 us (0.89)
  starting transfers between devices: 54.9 us -> 41.3 us
  waiting for transfers between devices: 23.8 us -> 26.3 us
    ppermute x27 -> x21, starting transfers between devices: 47.2 us -> 33.3 us  [swap(): lax.ppermute(x, axis, [p for a, b in pairs for p in ((a, b), (b, a))])]
    ppermute x27 -> x21, waiting for transfers between devices: 13.8 us -> 15.9 us  [swap(): lax.ppermute(x, axis, [p for a, b in pairs for p in ((a, b), (b, a))])]
    pallas_call x8 -> x6, Pallas kernels: 6.97 us -> 6.31 us  [rim_step(): pl.pallas_call(functools.partial(rim_body, first, kind, parts), in_specs=...]
  transfers between devices with their start and end apart: 33 -> 27, of which waited for: 9 -> 9; matrix products, arithmetic and copies ran while one was open for 0% -> 0% of each run, Pallas kernels for 20% -> 22%
where the time goes in v4:
time: 95.2 us; the launch traced here: 95 us
  starting transfers between devices  41.3 us (43%)
  waiting for transfers between devices  26.3 us (28%)
  Pallas kernels  24 us (25%)
  local copies, waits for them, and re-layouts  2.32 us (2%)
    ppermute x21, starting transfers between devices, swap(): lax.ppermute(x, axis, [p for a, b in pairs for p in ((a, b), (b, a))])  33.3 us
    ppermute x21, waiting for transfers between devices, swap(): lax.ppermute(x, axis, [p for a, b in pairs for p in ((a, b), (b, a))])  15.9 us
    pallas_call x6, Pallas kernels, local_step(): pl.pallas_call(functools.partial(local_body, chunk, moment, previous is n...  13.3 us
    ppermute x3, waiting for transfers between devices, coupled(): lax.ppermute(block, 'slab', [(i, i ^ d) for i in range(slabs)])  6.41 us
    pallas_call x6, Pallas kernels, rim_step(): pl.pallas_call(functools.partial(rim_body, first, kind, parts), in_specs=...  6.31 us
    ppermute x3, starting transfers between devices, coupled(): lax.ppermute(block, 'slab', [(i, i ^ d) for i in range(slabs)])  5.8 us
    ppermute x3, waiting for transfers between devices, coupled(): lax.ppermute(mine, both, [(i, i ^ flip) for i in range(4)])  4 us
    unnamed x10, local copies, waits for them, and re-layouts  2.32 us
  transfers between devices with their start and end apart: 27, of which 9 were waited for; matrix products, arithmetic and copies ran while one was open for 0% of the time, Pallas kernels for 22%

profile of v4, /device:TPU:0, one launch (start us, length us, event | category | flops | bytes accessed | tf_op | source)
XLA Modules:
  0.0 95.0 jit_solution(3085438366777048484)
XLA Ops:
  4.5 2.7 %collective-permute-start.11 = (bf16[4,8,48,128]{3,2,1,0:T(8,128)(2,1)S(1)}, bf16[4,8,48,128]{3,2,1,0:T(8,128)(2,1)S(1)}, u32[]{:S(2)}, u32[]{:S(2)}) collective-permute-start(bf16[4,8,48,128]{3,2,1,0:T(8,128)(2,1)S(1)} %get-tuple-element.54), channel_id=1, source_target_pairs={{0,4},{4,0},{8,12},{12,8},{1,5},{5,1},{9,13},{13,9},{2,6},{6,2},{1... | collective-permute-start | bytes 1179656 | tf_op jit(solution)/shard_map/ppermute | solution.py:275
  9.1 4.3 %collective-permute-start.1 = (bf16[4,8,48,128]{3,2,1,0:T(8,128)(2,1)S(1)}, bf16[4,8,48,128]{3,2,1,0:T(8,128)(2,1)S(1)}, u32[]{:S(2)}, u32[]{:S(2)}) collective-permute-start(bf16[4,8,48,128]{3,2,1,0:T(8,128)(2,1)S(1)} %get-tuple-element.40), channel_id=1, source_target_pairs={{0,4},{4,0},{8,12},{12,8},{1,5},{5,1},{9,13},{13,9},{2,6},{6,2},{1... | collective-permute-start | bytes 1179656 | tf_op jit(solution)/shard_map/ppermute | solution.py:275
  14.1 2.2 %shard_map.58.refs_0_ = f32[8,8,48,128]{3,2,1,0:T(8,128)S(1)} custom-call(f32[8,8,64,128]{3,2,1,0:T(8,128)S(1)} %get-tuple-element.52.refs_0_.refs_5_, bf16[8,4,48,128]{3,2,1,0:T(8,128)(2,1)S(1)} %collective-permute-done.10.refs_1_, bf16[8,8,48,256]{3,2,1,0:T(8,128)(2,1)S(1)} %copy-done, f32[64,48]{1,0:T(8,128)S(1)} %bitcast.11, f32[4,64,48]{2,1,0:T(8,128)S(1)} %bitcast.5), custom_call_target="tpu_custom_call" | custom-call | tf_op jit(solution)/shard_map/pallas_call | solution.py:186
  18.3 5.0 %collective-permute-start.14 = (bf16[4,8,48,128]{3,2,1,0:T(8,128)(2,1)S(1)}, bf16[4,8,48,128]{3,2,1,0:T(8,128)(2,1)S(1)}, u32[]{:S(2)}, u32[]{:S(2)}) collective-permute-start(bf16[4,8,48,128]{3,2,1,0:T(8,128)(2,1)S(1)} %get-tuple-element.58), channel_id=1, source_target_pairs={{0,4},{4,0},{8,12},{12,8},{1,5},{5,1},{9,13},{13,9},{2,6},{6,2},{1... | collective-permute-start | bytes 1179656 | tf_op jit(solution)/shard_map/ppermute | solution.py:275
  24.1 2.1 %shard_map.51.refs_0_ = f32[8,8,48,128]{3,2,1,0:T(8,128)S(1)} custom-call(f32[8,8,64,128]{3,2,1,0:T(8,128)S(1)} %get-tuple-element.38.refs_0_.refs_5_, bf16[8,4,48,128]{3,2,1,0:T(8,128)(2,1)S(1)} %collective-permute-done.refs_1_, bf16[8,8,48,256]{3,2,1,0:T(8,128)(2,1)S(1)} %copy-done.1, f32[64,48]{1,0:T(8,128)S(1)} %bitcast.13, f32[4,64,48]{2,1,0:T(8,128)S(1)} %bitcast.6), custom_call_target="tpu_custom_call" | custom-call | tf_op jit(solution)/shard_map/pallas_call | solution.py:186
  27.6 4.2 %collective-permute-start.4 = (bf16[4,8,48,128]{3,2,1,0:T(8,128)(2,1)S(1)}, bf16[4,8,48,128]{3,2,1,0:T(8,128)(2,1)S(1)}, u32[]{:S(2)}, u32[]{:S(2)}) collective-permute-start(bf16[4,8,48,128]{3,2,1,0:T(8,128)(2,1)S(1)} %get-tuple-element.44), channel_id=1, source_target_pairs={{0,4},{4,0},{8,12},{12,8},{1,5},{5,1},{9,13},{13,9},{2,6},{6,2},{1... | collective-permute-start | bytes 1179656 | tf_op jit(solution)/shard_map/ppermute | solution.py:275
  32.5 2.3 %shard_map.60.refs_0_ = f32[8,8,48,128]{3,2,1,0:T(8,128)S(1)} custom-call(f32[8,8,64,128]{3,2,1,0:T(8,128)S(1)} %get-tuple-element.56.refs_0_.refs_5_, bf16[8,4,48,128]{3,2,1,0:T(8,128)(2,1)S(1)} %collective-permute-done.13.refs_1_, bf16[8,8,48,256]{3,2,1,0:T(8,128)(2,1)S(1)} %copy-done.1, f32[64,48]{1,0:T(8,128)S(1)} %bitcast.15, f32[4,64,48]{2,1,0:T(8,128)S(1)} %bitcast.7, ...), custom_call_target="tpu_custom_call" | custom-call | tf_op jit(solution)/shard_map/pallas_call | solution.py:186
  36.1 4.1 %collective-permute-start.17 = (bf16[4,8,48,128]{3,2,1,0:T(8,128)(2,1)S(1)}, bf16[4,8,48,128]{3,2,1,0:T(8,128)(2,1)S(1)}, u32[]{:S(2)}, u32[]{:S(2)}) collective-permute-start(bf16[4,8,48,128]{3,2,1,0:T(8,128)(2,1)S(1)} %get-tuple-element.62), channel_id=1, source_target_pairs={{0,4},{4,0},{8,12},{12,8},{1,5},{5,1},{9,13},{13,9},{2,6},{6,2},{1... | collective-permute-start | bytes 1179656 | tf_op jit(solution)/shard_map/ppermute | solution.py:275
  40.9 2.3 %shard_map.53.refs_0_ = f32[8,8,48,128]{3,2,1,0:T(8,128)S(1)} custom-call(f32[8,8,64,128]{3,2,1,0:T(8,128)S(1)} %get-tuple-element.42.refs_0_.refs_5_, bf16[8,4,48,128]{3,2,1,0:T(8,128)(2,1)S(1)} %collective-permute-done.3.refs_1_, bf16[8,8,48,256]{3,2,1,0:T(8,128)(2,1)S(1)} %copy-done.1, f32[64,48]{1,0:T(8,128)S(1)} %bitcast.17, f32[4,64,48]{2,1,0:T(8,128)S(1)} %bitcast.8, ...), custom_call_target="tpu_custom_call" | custom-call | tf_op jit(solution)/shard_map/pallas_call | solution.py:186
  44.5 4.1 %collective-permute-start.7 = (bf16[4,8,48,128]{3,2,1,0:T(8,128)(2,1)S(1)}, bf16[4,8,48,128]{3,2,1,0:T(8,128)(2,1)S(1)}, u32[]{:S(2)}, u32[]{:S(2)}) collective-permute-start(bf16[4,8,48,128]{3,2,1,0:T(8,128)(2,1)S(1)} %get-tuple-element.48), channel_id=1, source_target_pairs={{0,4},{4,0},{8,12},{12,8},{1,5},{5,1},{9,13},{13,9},{2,6},{6,2},{1... | collective-permute-start | bytes 1179656 | tf_op jit(solution)/shard_map/ppermute | solution.py:275
  49.3 2.3 %shard_map.62.refs_0_ = f32[8,8,48,128]{3,2,1,0:T(8,128)S(1)} custom-call(f32[8,8,64,128]{3,2,1,0:T(8,128)S(1)} %get-tuple-element.60.refs_0_, bf16[8,4,48,128]{3,2,1,0:T(8,128)(2,1)S(1)} %collective-permute-done.16.refs_1_, bf16[8,8,48,256]{3,2,1,0:T(8,128)(2,1)S(1)} %copy-done.1, f32[64,48]{1,0:T(8,128)S(1)} %bitcast.19, f32[4,64,48]{2,1,0:T(8,128)S(1)} %bitcast.9, ...), custom_call_target="tpu_custom_call" | custom-call | tf_op jit(solution)/shard_map/pallas_call | solution.py:186
  52.6 1.6 %collective-permute-start.19 = (bf16[4,8,48,128]{3,2,1,0:T(8,128)(2,1)S(1)}, bf16[4,8,48,128]{3,2,1,0:T(8,128)(2,1)S(1)}, u32[]{:S(2)}, u32[]{:S(2)}) collective-permute-start(bf16[4,8,48,128]{3,2,1,0:T(8,128)(2,1)S(1)} %get-tuple-element.65), channel_id=1, source_target_pairs={{0,2},{2,0},{1,3},{3,1},{4,6},{6,4},{5,7},{7,5},{8,10},{10,8},{9,1... | collective-permute-start | bytes 1179656 | tf_op jit(solution)/shard_map/ppermute | solution.py:275
  54.1 2.2 %shard_map.55.refs_0_ = f32[8,8,48,128]{3,2,1,0:T(8,128)S(1)} custom-call(f32[8,8,64,128]{3,2,1,0:T(8,128)S(1)} %get-tuple-element.46.refs_0_, bf16[8,4,48,128]{3,2,1,0:T(8,128)(2,1)S(1)} %collective-permute-done.6.refs_1_, bf16[8,8,48,256]{3,2,1,0:T(8,128)(2,1)S(1)} %copy-done.1, f32[64,48]{1,0:T(8,128)S(1)} %bitcast.21, f32[4,64,48]{2,1,0:T(8,128)S(1)} %bitcast.10, ...), custom_call_target="tpu_custom_call" | custom-call | tf_op jit(solution)/shard_map/pallas_call | solution.py:186
  56.4 2.6 %collective-permute-done.7.refs_1_ = bf16[4,8,48,128]{3,2,1,0:T(8,128)(2,1)S(1)} collective-permute-done((bf16[4,8,48,128]{3,2,1,0:T(8,128)(2,1)S(1)}, bf16[4,8,48,128]{3,2,1,0:T(8,128)(2,1)S(1)}, u32[]{:S(2)}, u32[]{:S(2)}) %collective-permute-start.7) | collective-permute-done | bytes 393248 | tf_op jit(solution)/shard_map/ppermute | solution.py:275
  60.0 1.7 %collective-permute-start.9 = (bf16[4,8,48,128]{3,2,1,0:T(8,128)(2,1)S(1)}, bf16[4,8,48,128]{3,2,1,0:T(8,128)(2,1)S(1)}, u32[]{:S(2)}, u32[]{:S(2)}) collective-permute-start(bf16[4,8,48,128]{3,2,1,0:T(8,128)(2,1)S(1)} %get-tuple-element.51), channel_id=1, source_target_pairs={{0,2},{2,0},{1,3},{3,1},{4,6},{6,4},{5,7},{7,5},{8,10},{10,8},{9,1... | collective-permute-start | bytes 1179656 | tf_op jit(solution)/shard_map/ppermute | solution.py:275
  61.7 2.9 %collective-permute-done.19.refs_3_ = bf16[4,8,48,128]{3,2,1,0:T(8,128)(2,1)S(1)} collective-permute-done((bf16[4,8,48,128]{3,2,1,0:T(8,128)(2,1)S(1)}, bf16[4,8,48,128]{3,2,1,0:T(8,128)(2,1)S(1)}, u32[]{:S(2)}, u32[]{:S(2)}) %collective-permute-start.19) | collective-permute-done | bytes 393248 | tf_op jit(solution)/shard_map/ppermute | solution.py:275
  64.6 7.7 %collective-permute-done.9.refs_1_ = bf16[4,8,48,128]{3,2,1,0:T(8,128)(2,1)S(1)} collective-permute-done((bf16[4,8,48,128]{3,2,1,0:T(8,128)(2,1)S(1)}, bf16[4,8,48,128]{3,2,1,0:T(8,128)(2,1)S(1)}, u32[]{:S(2)}, u32[]{:S(2)}) %collective-permute-start.9) | collective-permute-done | bytes 393248 | tf_op jit(solution)/shard_map/ppermute | solution.py:275
  73.7 1.9 %collective-permute-done.20.got_ref = f32[520,256]{1,0:T(8,128)S(1)} collective-permute-done((f32[520,256]{1,0:T(8,128)S(1)}, f32[520,256]{1,0:T(8,128)S(1)}, u32[]{:S(2)}, u32[]{:S(2)}) %collective-permute-start.20) | collective-permute-done | bytes 532512 | tf_op jit(solution)/shard_map/ppermute | solution.py:275
  75.6 3.4 %collective-permute-start.21 = (bf16[144,256]{1,0:T(8,128)(2,1)S(1)}, bf16[144,256]{1,0:T(8,128)(2,1)S(1)}, u32[]{:S(2)}, u32[]{:S(2)}) collective-permute-start(bf16[144,256]{1,0:T(8,128)(2,1)S(1)} %get-tuple-element.69), channel_id=1, source_target_pairs={{0,4},{4,0},{8,12},{12,8},{1,5},{5,1},{9,13},{13,9},{2,6},{6,2},{1... | collective-permute-start | bytes 221192 | tf_op jit(solution)/shard_map/ppermute | solution.py:467
  79.9 1.6 %collective-permute-start.23 = (bf16[144,256]{1,0:T(8,128)(2,1)S(1)}, bf16[144,256]{1,0:T(8,128)(2,1)S(1)}, u32[]{:S(2)}, u32[]{:S(2)}) collective-permute-start(bf16[144,256]{1,0:T(8,128)(2,1)S(1)} %get-tuple-element.71), channel_id=1, source_target_pairs={{0,12},{4,8},{8,4},{12,0},{1,13},{5,9},{9,5},{13,1},{2,14},{6,10},... | collective-permute-start | bytes 221192 | tf_op jit(solution)/shard_map/ppermute | solution.py:467
  81.6 6.2 %collective-permute-done.22.refs_1_ = bf16[144,256]{1,0:T(8,128)(2,1)S(1)} collective-permute-done((bf16[144,256]{1,0:T(8,128)(2,1)S(1)}, bf16[144,256]{1,0:T(8,128)(2,1)S(1)}, u32[]{:S(2)}, u32[]{:S(2)}) %collective-permute-start.22) | collective-permute-done | bytes 73760 | tf_op jit(solution)/shard_map/ppermute | solution.py:467
  88.0 1.6 %collective-permute-start.25 = (bf16[144,256]{1,0:T(8,128)(2,1)S(1)}, bf16[144,256]{1,0:T(8,128)(2,1)S(1)}, u32[]{:S(2)}, u32[]{:S(2)}) collective-permute-start(bf16[144,256]{1,0:T(8,128)(2,1)S(1)} %shard_map.66.a_ref), channel_id=1, source_target_pairs={{0,1},{1,0},{2,3},{3,2},{4,5},{5,4},{6,7},{7,6},{8,9},{9,8},{10,11... | collective-permute-start | bytes 221192 | tf_op jit(solution)/shard_map/ppermute | solution.py:473
  90.1 2.4 %collective-permute-done.26.d_ref = bf16[144,256]{1,0:T(8,128)(2,1)S(1)} collective-permute-done((bf16[144,256]{1,0:T(8,128)(2,1)S(1)}, bf16[144,256]{1,0:T(8,128)(2,1)S(1)}, u32[]{:S(2)}, u32[]{:S(2)}) %collective-permute-start.26) | collective-permute-done | bytes 73760 | tf_op jit(solution)/shard_map/ppermute | solution.py:473
  92.5 1.6 %collective-permute-done.24.b_ref = bf16[144,256]{1,0:T(8,128)(2,1)S(1)} collective-permute-done((bf16[144,256]{1,0:T(8,128)(2,1)S(1)}, bf16[144,256]{1,0:T(8,128)(2,1)S(1)}, u32[]{:S(2)}, u32[]{:S(2)}) %collective-permute-start.24) | collective-permute-done | bytes 73760 | tf_op jit(solution)/shard_map/ppermute | solution.py:473
  (58 shorter events, 21.2 us)
Async XLA Ops:
  4.0 9.4 %collective-permute-start.10 = (bf16[8,4,48,128]{3,2,1,0:T(8,128)(2,1)S(1)}, bf16[8,4,48,128]{3,2,1,0:T(8,128)(2,1)S(1)}, u32[]{:S(2)}, u32[]{:S(2)}) collective-permute-start(bf16[8,4,48,128]{3,2,1,0:T(8,128)(2,1)S(1)} %get-tuple-element.53), channel_id=1, source_target_pairs={{0,1},{1,0},{2,3},{3,2},{4,5},{5,4},{6,7},{7,6},{8,9},{9,8},{10,11... | collective-permute-start | bytes 1179656 | tf_op jit(solution)/shard_map/ppermute | solution.py:275
  4.5 12.6 %collective-permute-start.11 = (bf16[4,8,48,128]{3,2,1,0:T(8,128)(2,1)S(1)}, bf16[4,8,48,128]{3,2,1,0:T(8,128)(2,1)S(1)}, u32[]{:S(2)}, u32[]{:S(2)}) collective-permute-start(bf16[4,8,48,128]{3,2,1,0:T(8,128)(2,1)S(1)} %get-tuple-element.54), channel_id=1, source_target_pairs={{0,4},{4,0},{8,12},{12,8},{1,5},{5,1},{9,13},{13,9},{2,6},{6,2},{1... | collective-permute-start | bytes 1179656 | tf_op jit(solution)/shard_map/ppermute | solution.py:275
  7.2 10.0 %collective-permute-start.12 = (bf16[4,8,48,128]{3,2,1,0:T(8,128)(2,1)S(1)}, bf16[4,8,48,128]{3,2,1,0:T(8,128)(2,1)S(1)}, u32[]{:S(2)}, u32[]{:S(2)}) collective-permute-start(bf16[4,8,48,128]{3,2,1,0:T(8,128)(2,1)S(1)} %get-tuple-element.55), channel_id=1, source_target_pairs={{4,8},{8,4},{5,9},{9,5},{6,10},{10,6},{7,11},{11,7},{20,24},{24,20... | collective-permute-start | bytes 1179656 | tf_op jit(solution)/shard_map/ppermute | solution.py:275
  8.9 14.4 %collective-permute-start = (bf16[8,4,48,128]{3,2,1,0:T(8,128)(2,1)S(1)}, bf16[8,4,48,128]{3,2,1,0:T(8,128)(2,1)S(1)}, u32[]{:S(2)}, u32[]{:S(2)}) collective-permute-start(bf16[8,4,48,128]{3,2,1,0:T(8,128)(2,1)S(1)} %get-tuple-element.39), channel_id=1, source_target_pairs={{0,1},{1,0},{2,3},{3,2},{4,5},{5,4},{6,7},{7,6},{8,9},{9,8},{10,11... | collective-permute-start | bytes 1179656 | tf_op jit(solution)/shard_map/ppermute | solution.py:275
  9.1 17.1 %collective-permute-start.1 = (bf16[4,8,48,128]{3,2,1,0:T(8,128)(2,1)S(1)}, bf16[4,8,48,128]{3,2,1,0:T(8,128)(2,1)S(1)}, u32[]{:S(2)}, u32[]{:S(2)}) collective-permute-start(bf16[4,8,48,128]{3,2,1,0:T(8,128)(2,1)S(1)} %get-tuple-element.40), channel_id=1, source_target_pairs={{0,4},{4,0},{8,12},{12,8},{1,5},{5,1},{9,13},{13,9},{2,6},{6,2},{1... | collective-permute-start | bytes 1179656 | tf_op jit(solution)/shard_map/ppermute | solution.py:275
  13.4 12.8 %collective-permute-start.2 = (bf16[4,8,48,128]{3,2,1,0:T(8,128)(2,1)S(1)}, bf16[4,8,48,128]{3,2,1,0:T(8,128)(2,1)S(1)}, u32[]{:S(2)}, u32[]{:S(2)}) collective-permute-start(bf16[4,8,48,128]{3,2,1,0:T(8,128)(2,1)S(1)} %get-tuple-element.41), channel_id=1, source_target_pairs={{4,8},{8,4},{5,9},{9,5},{6,10},{10,6},{7,11},{11,7},{20,24},{24,20... | collective-permute-start | bytes 1179656 | tf_op jit(solution)/shard_map/ppermute | solution.py:275
  18.2 13.5 %collective-permute-start.13 = (bf16[8,4,48,128]{3,2,1,0:T(8,128)(2,1)S(1)}, bf16[8,4,48,128]{3,2,1,0:T(8,128)(2,1)S(1)}, u32[]{:S(2)}, u32[]{:S(2)}) collective-permute-start(bf16[8,4,48,128]{3,2,1,0:T(8,128)(2,1)S(1)} %get-tuple-element.57), channel_id=1, source_target_pairs={{0,1},{1,0},{2,3},{3,2},{4,5},{5,4},{6,7},{7,6},{8,9},{9,8},{10,11... | collective-permute-start | bytes 1179656 | tf_op jit(solution)/shard_map/ppermute | solution.py:275
  18.3 16.4 %collective-permute-start.14 = (bf16[4,8,48,128]{3,2,1,0:T(8,128)(2,1)S(1)}, bf16[4,8,48,128]{3,2,1,0:T(8,128)(2,1)S(1)}, u32[]{:S(2)}, u32[]{:S(2)}) collective-permute-start(bf16[4,8,48,128]{3,2,1,0:T(8,128)(2,1)S(1)} %get-tuple-element.58), channel_id=1, source_target_pairs={{0,4},{4,0},{8,12},{12,8},{1,5},{5,1},{9,13},{13,9},{2,6},{6,2},{1... | collective-permute-start | bytes 1179656 | tf_op jit(solution)/shard_map/ppermute | solution.py:275
  23.4 11.4 %collective-permute-start.15 = (bf16[4,8,48,128]{3,2,1,0:T(8,128)(2,1)S(1)}, bf16[4,8,48,128]{3,2,1,0:T(8,128)(2,1)S(1)}, u32[]{:S(2)}, u32[]{:S(2)}) collective-permute-start(bf16[4,8,48,128]{3,2,1,0:T(8,128)(2,1)S(1)} %get-tuple-element.59), channel_id=1, source_target_pairs={{4,8},{8,4},{5,9},{9,5},{6,10},{10,6},{7,11},{11,7},{20,24},{24,20... | collective-permute-start | bytes 1179656 | tf_op jit(solution)/shard_map/ppermute | solution.py:275
  27.3 12.9 %collective-permute-start.3 = (bf16[8,4,48,128]{3,2,1,0:T(8,128)(2,1)S(1)}, bf16[8,4,48,128]{3,2,1,0:T(8,128)(2,1)S(1)}, u32[]{:S(2)}, u32[]{:S(2)}) collective-permute-start(bf16[8,4,48,128]{3,2,1,0:T(8,128)(2,1)S(1)} %get-tuple-element.43), channel_id=1, source_target_pairs={{0,1},{1,0},{2,3},{3,2},{4,5},{5,4},{6,7},{7,6},{8,9},{9,8},{10,11... | collective-permute-start | bytes 1179656 | tf_op jit(solution)/shard_map/ppermute | solution.py:275
  27.6 15.6 %collective-permute-start.4 = (bf16[4,8,48,128]{3,2,1,0:T(8,128)(2,1)S(1)}, bf16[4,8,48,128]{3,2,1,0:T(8,128)(2,1)S(1)}, u32[]{:S(2)}, u32[]{:S(2)}) collective-permute-start(bf16[4,8,48,128]{3,2,1,0:T(8,128)(2,1)S(1)} %get-tuple-element.44), channel_id=1, source_target_pairs={{0,4},{4,0},{8,12},{12,8},{1,5},{5,1},{9,13},{13,9},{2,6},{6,2},{1... | collective-permute-start | bytes 1179656 | tf_op jit(solution)/shard_map/ppermute | solution.py:275
  31.8 11.4 %collective-permute-start.5 = (bf16[4,8,48,128]{3,2,1,0:T(8,128)(2,1)S(1)}, bf16[4,8,48,128]{3,2,1,0:T(8,128)(2,1)S(1)}, u32[]{:S(2)}, u32[]{:S(2)}) collective-permute-start(bf16[4,8,48,128]{3,2,1,0:T(8,128)(2,1)S(1)} %get-tuple-element.45), channel_id=1, source_target_pairs={{4,8},{8,4},{5,9},{9,5},{6,10},{10,6},{7,11},{11,7},{20,24},{24,20... | collective-permute-start | bytes 1179656 | tf_op jit(solution)/shard_map/ppermute | solution.py:275
  35.9 12.8 %collective-permute-start.16 = (bf16[8,4,48,128]{3,2,1,0:T(8,128)(2,1)S(1)}, bf16[8,4,48,128]{3,2,1,0:T(8,128)(2,1)S(1)}, u32[]{:S(2)}, u32[]{:S(2)}) collective-permute-start(bf16[8,4,48,128]{3,2,1,0:T(8,128)(2,1)S(1)} %get-tuple-element.61), channel_id=1, source_target_pairs={{0,1},{1,0},{2,3},{3,2},{4,5},{5,4},{6,7},{7,6},{8,9},{9,8},{10,11... | collective-permute-start | bytes 1179656 | tf_op jit(solution)/shard_map/ppermute | solution.py:275
  36.1 15.5 %collective-permute-start.17 = (bf16[4,8,48,128]{3,2,1,0:T(8,128)(2,1)S(1)}, bf16[4,8,48,128]{3,2,1,0:T(8,128)(2,1)S(1)}, u32[]{:S(2)}, u32[]{:S(2)}) collective-permute-start(bf16[4,8,48,128]{3,2,1,0:T(8,128)(2,1)S(1)} %get-tuple-element.62), channel_id=1, source_target_pairs={{0,4},{4,0},{8,12},{12,8},{1,5},{5,1},{9,13},{13,9},{2,6},{6,2},{1... | collective-permute-start | bytes 1179656 | tf_op jit(solution)/shard_map/ppermute | solution.py:275
  40.2 11.4 %collective-permute-start.18 = (bf16[4,8,48,128]{3,2,1,0:T(8,128)(2,1)S(1)}, bf16[4,8,48,128]{3,2,1,0:T(8,128)(2,1)S(1)}, u32[]{:S(2)}, u32[]{:S(2)}) collective-permute-start(bf16[4,8,48,128]{3,2,1,0:T(8,128)(2,1)S(1)} %get-tuple-element.63), channel_id=1, source_target_pairs={{4,8},{8,4},{5,9},{9,5},{6,10},{10,6},{7,11},{11,7},{20,24},{24,20... | collective-permute-start | bytes 1179656 | tf_op jit(solution)/shard_map/ppermute | solution.py:275
  44.3 9.9 %collective-permute-start.6 = (bf16[8,4,48,128]{3,2,1,0:T(8,128)(2,1)S(1)}, bf16[8,4,48,128]{3,2,1,0:T(8,128)(2,1)S(1)}, u32[]{:S(2)}, u32[]{:S(2)}) collective-permute-start(bf16[8,4,48,128]{3,2,1,0:T(8,128)(2,1)S(1)} %get-tuple-element.47), channel_id=1, source_target_pairs={{0,1},{1,0},{2,3},{3,2},{4,5},{5,4},{6,7},{7,6},{8,9},{9,8},{10,11... | collective-permute-start | bytes 1179656 | tf_op jit(solution)/shard_map/ppermute | solution.py:275
  44.5 14.5 %collective-permute-start.7 = (bf16[4,8,48,128]{3,2,1,0:T(8,128)(2,1)S(1)}, bf16[4,8,48,128]{3,2,1,0:T(8,128)(2,1)S(1)}, u32[]{:S(2)}, u32[]{:S(2)}) collective-permute-start(bf16[4,8,48,128]{3,2,1,0:T(8,128)(2,1)S(1)} %get-tuple-element.48), channel_id=1, source_target_pairs={{0,4},{4,0},{8,12},{12,8},{1,5},{5,1},{9,13},{13,9},{2,6},{6,2},{1... | collective-permute-start | bytes 1179656 | tf_op jit(solution)/shard_map/ppermute | solution.py:275
  48.6 10.4 %collective-permute-start.8 = (bf16[4,8,48,128]{3,2,1,0:T(8,128)(2,1)S(1)}, bf16[4,8,48,128]{3,2,1,0:T(8,128)(2,1)S(1)}, u32[]{:S(2)}, u32[]{:S(2)}) collective-permute-start(bf16[4,8,48,128]{3,2,1,0:T(8,128)(2,1)S(1)} %get-tuple-element.49), channel_id=1, source_target_pairs={{4,8},{8,4},{5,9},{9,5},{6,10},{10,6},{7,11},{11,7},{20,24},{24,20... | collective-permute-start | bytes 1179656 | tf_op jit(solution)/shard_map/ppermute | solution.py:275
  52.6 12.0 %collective-permute-start.19 = (bf16[4,8,48,128]{3,2,1,0:T(8,128)(2,1)S(1)}, bf16[4,8,48,128]{3,2,1,0:T(8,128)(2,1)S(1)}, u32[]{:S(2)}, u32[]{:S(2)}) collective-permute-start(bf16[4,8,48,128]{3,2,1,0:T(8,128)(2,1)S(1)} %get-tuple-element.65), channel_id=1, source_target_pairs={{0,2},{2,0},{1,3},{3,1},{4,6},{6,4},{5,7},{7,5},{8,10},{10,8},{9,1... | collective-permute-start | bytes 1179656 | tf_op jit(solution)/shard_map/ppermute | solution.py:275
  60.0 12.3 %collective-permute-start.9 = (bf16[4,8,48,128]{3,2,1,0:T(8,128)(2,1)S(1)}, bf16[4,8,48,128]{3,2,1,0:T(8,128)(2,1)S(1)}, u32[]{:S(2)}, u32[]{:S(2)}) collective-permute-start(bf16[4,8,48,128]{3,2,1,0:T(8,128)(2,1)S(1)} %get-tuple-element.51), channel_id=1, source_target_pairs={{0,2},{2,0},{1,3},{3,1},{4,6},{6,4},{5,7},{7,5},{8,10},{10,8},{9,1... | collective-permute-start | bytes 1179656 | tf_op jit(solution)/shard_map/ppermute | solution.py:275
  75.6 6.0 %collective-permute-start.21 = (bf16[144,256]{1,0:T(8,128)(2,1)S(1)}, bf16[144,256]{1,0:T(8,128)(2,1)S(1)}, u32[]{:S(2)}, u32[]{:S(2)}) collective-permute-start(bf16[144,256]{1,0:T(8,128)(2,1)S(1)} %get-tuple-element.69), channel_id=1, source_target_pairs={{0,4},{4,0},{8,12},{12,8},{1,5},{5,1},{9,13},{13,9},{2,6},{6,2},{1... | collective-permute-start | bytes 221192 | tf_op jit(solution)/shard_map/ppermute | solution.py:467
  79.0 8.8 %collective-permute-start.22 = (bf16[144,256]{1,0:T(8,128)(2,1)S(1)}, bf16[144,256]{1,0:T(8,128)(2,1)S(1)}, u32[]{:S(2)}, u32[]{:S(2)}) collective-permute-start(bf16[144,256]{1,0:T(8,128)(2,1)S(1)} %get-tuple-element.70), channel_id=1, source_target_pairs={{0,8},{4,12},{8,0},{12,4},{1,9},{5,13},{9,1},{13,5},{2,10},{6,14},... | collective-permute-start | bytes 221192 | tf_op jit(solution)/shard_map/ppermute | solution.py:467
  79.9 8.0 %collective-permute-start.23 = (bf16[144,256]{1,0:T(8,128)(2,1)S(1)}, bf16[144,256]{1,0:T(8,128)(2,1)S(1)}, u32[]{:S(2)}, u32[]{:S(2)}) collective-permute-start(bf16[144,256]{1,0:T(8,128)(2,1)S(1)} %get-tuple-element.71), channel_id=1, source_target_pairs={{0,12},{4,8},{8,4},{12,0},{1,13},{5,9},{9,5},{13,1},{2,14},{6,10},... | collective-permute-start | bytes 221192 | tf_op jit(solution)/shard_map/ppermute | solution.py:467
  87.9 4.6 %collective-permute-start.26 = (bf16[144,256]{1,0:T(8,128)(2,1)S(1)}, bf16[144,256]{1,0:T(8,128)(2,1)S(1)}, u32[]{:S(2)}, u32[]{:S(2)}) collective-permute-start(bf16[144,256]{1,0:T(8,128)(2,1)S(1)} %shard_map.66.a_ref), channel_id=1, source_target_pairs={{0,3},{1,2},{2,1},{3,0},{4,7},{5,6},{6,5},{7,4},{8,11},{9,10},{10,... | collective-permute-start | bytes 221192 | tf_op jit(solution)/shard_map/ppermute | solution.py:473
  (8 other events, 40.0 us)

commit v5 on v4

--- a/solution.py
+++ b/solution.py
@@ -413,16 +413,13 @@
     )(own, *others)
 
 
-def finish_body(cell_count, a_ref, b_ref, c_ref, d_ref, out_ref, norms_ref):
+def normalise_body(cell_count, mine_ref, other_ref, out_ref, norms_ref):
     slab = lax.axis_index("slab")
     core = lax.axis_index("sub")
-    count = out_ref.shape[0]
-    near, tail = opened(a_ref)
-    far, _ = opened(c_ref)
-    more, more_tail = opened(b_ref)
-    near = near + more
-    far = far + opened(d_ref)[0]
-    norms = jnp.sqrt((tail + more_tail)[:2] / cell_count + EPSILON)
+    one, one_tail = opened(mine_ref)
+    two, two_tail = opened(other_ref)
+    total = one + two
+    norms = jnp.sqrt((one_tail + two_tail)[:2] / cell_count + EPSILON)
     blocks = [norms[n // 2 : n // 2 + 1, (n % 2) * LANES : (n % 2 + 1) * LANES] for n in range(4)]
     own = blocks[0]
     for n in range(1, 4):
@@ -435,27 +432,43 @@
         jnp.where(eye, jnp.broadcast_to(own, (LANES, LANES)), 0.0), axis=1, keepdims=True
     )
     for side in range(2):
-        for block, which in ((near, core), (far, 1 - core)):
-            index = 2 * side + which
-            others = jnp.where(which == 0, blocks[2 * side], blocks[2 * side + 1])
-            value = block[:count, side * LANES : (side + 1) * LANES]
-            value = value / math.sqrt(cell_count) / (own_column * others)
-            value = jnp.where(eye & (index == slab), 0.0, value)
-            out_ref[:, pl.ds(pl.multiple_of(index * LANES, LANES), LANES)] = value
-
-
-def finish(pieces, cell_count):
-    count = pieces[0].shape[0] - 16
-    return pl.pallas_call(
-        functools.partial(finish_body, cell_count),
-        in_specs=whole_vmem(4),
+        columns = slice(side * LANES, (side + 1) * LANES)
+        others = jnp.where(core == 0, blocks[2 * side], blocks[2 * side + 1])
+        value = total[:, columns] / math.sqrt(cell_count) / (own_column * others)
+        out_ref[:, columns] = jnp.where(eye & (2 * side + core == slab), 0.0, value)
+
+
+def normalise(mine, other, cell_count):
+    count = mine.shape[0] - 16
+    return pl.pallas_call(
+        functools.partial(normalise_body, cell_count),
+        in_specs=whole_vmem(2),
         out_specs=whole_vmem(2),
         out_shape=[
-            jax.ShapeDtypeStruct((count, 4 * LANES), F32),
+            jax.ShapeDtypeStruct((count, 2 * LANES), F32),
             jax.ShapeDtypeStruct((1, LANES), F32),
         ],
         compiler_params=params(),
-    )(*pieces)
+    )(mine, other)
+
+
+def assemble_body(near_ref, far_ref, out_ref):
+    core = lax.axis_index("sub")
+    for side in range(2):
+        columns = slice(side * LANES, (side + 1) * LANES)
+        for ref, which in ((near_ref, core), (far_ref, 1 - core)):
+            start = pl.multiple_of((2 * side + which) * LANES, LANES)
+            out_ref[:, pl.ds(start, LANES)] = ref[:, columns]
+
+
+def assemble(near, far):
+    return pl.pallas_call(
+        assemble_body,
+        in_specs=whole_vmem(2),
+        out_specs=whole_vmem(1)[0],
+        out_shape=jax.ShapeDtypeStruct((near.shape[0], 4 * LANES), F32),
+        compiler_params=params(),
+    )(near, far)
 
 
 def coupled(pieces, fields, cells, cell_count):
@@ -464,16 +477,13 @@
     got = swap(send, "sub", [(0, 1)])
     own, *sent = split_rows(keep, got, slabs)
     arrived = [
-        lax.ppermute(block, "slab", [(i, i ^ d) for i in range(slabs)])
-        for d, block in enumerate(sent, 1)
+        lax.ppermute(sent[d - 1], "slab", [(i, i ^ d) for i in range(slabs)]) for d in (2, 3, 1)
     ]
     mine = sum_all(own, arrived)
-    both = ("probe", "sub")
-    others = [
-        lax.ppermute(mine, both, [(i, i ^ flip) for i in range(4)]) for flip in (2, 1, 3)
-    ]
-    coupling, norms = finish([mine] + others, cell_count)
-    return coupling, norms.reshape(-1)
+    other = swap(mine, "probe", [(0, 1)])
+    near, norms = normalise(mine, other, cell_count)
+    far = swap(near, "sub", [(0, 1)])
+    return assemble(near, far), norms.reshape(-1)
 
 
 def coupled_general(fields, cell_count):

time: 95.2 us -> 94.4 us (level)
    ppermute x6 -> x3, waiting for transfers between devices: 10.4 us -> 5.67 us  [coupled(): lax.ppermute(sent[d - 1], 'slab', [(i, i ^ d) for i in range(slabs)])]
    ppermute x21 -> x23, waiting for transfers between devices: 15.9 us -> 20.1 us  [swap(): lax.ppermute(x, axis, [p for a, b in pairs for p in ((a, b), (b, a))])]
    ppermute x6 -> x3, starting transfers between devices: 8 us -> 5.72 us  [coupled(): lax.ppermute(sent[d - 1], 'slab', [(i, i ^ d) for i in range(slabs)])]
    ppermute x21 -> x23, starting transfers between devices: 33.3 us -> 34.9 us  [swap(): lax.ppermute(x, axis, [p for a, b in pairs for p in ((a, b), (b, a))])]
  transfers between devices with their start and end apart: 27 -> 26, of which waited for: 9 -> 10; matrix products, arithmetic and copies ran while one was open for 0% -> 0% of each run, Pallas kernels for 22% -> 22%
where the time goes in v5:
time: 94.4 us; the launch traced here: 94.1 us
  starting transfers between devices  40.6 us (43%)
  waiting for transfers between devices  25.8 us (27%)
  Pallas kernels  24.4 us (26%)
  local copies, waits for them, and re-layouts  2.32 us (2%)
    ppermute x23, starting transfers between devices, swap(): lax.ppermute(x, axis, [p for a, b in pairs for p in ((a, b), (b, a))])  34.9 us
    ppermute x23, waiting for transfers between devices, swap(): lax.ppermute(x, axis, [p for a, b in pairs for p in ((a, b), (b, a))])  20.1 us
    pallas_call x6, Pallas kernels, local_step(): pl.pallas_call(functools.partial(local_body, chunk, moment, previous is n...  13.3 us
    pallas_call x6, Pallas kernels, rim_step(): pl.pallas_call(functools.partial(rim_body, first, kind, parts), in_specs=...  6.31 us
    ppermute x3, starting transfers between devices, coupled(): lax.ppermute(sent[d - 1], 'slab', [(i, i ^ d) for i in range(slabs)])  5.72 us
    ppermute x3, waiting for transfers between devices, coupled(): lax.ppermute(sent[d - 1], 'slab', [(i, i ^ d) for i in range(slabs)])  5.67 us
    unnamed x10, local copies, waits for them, and re-layouts  2.32 us
    pallas_call x2, Pallas kernels, first_field(): pl.pallas_call(functools.partial(first_body, chunk), in_specs=whole_vmem(...  2.1 us
  transfers between devices with their start and end apart: 26, of which 10 were waited for; matrix products, arithmetic and copies ran while one was open for 0% of the time, Pallas kernels for 22%

profile of v5, /device:TPU:0, one launch (start us, length us, event | category | flops | bytes accessed | tf_op | source)
XLA Modules:
  0.0 94.1 jit_solution(1157263975733561203)
XLA Ops:
  0.6 1.4 %copy-done = bf16[8,8,48,256]{3,2,1,0:T(8,128)(2,1)S(1)} copy-done((bf16[8,8,48,256]{3,2,1,0:T(8,128)(2,1)S(1)}, bf16[8,8,48,256]{3,2,1,0:T(8,128)(2,1)}, u32[]{:S(2)}) %copy-start) | copy-done | bytes 1572888
  4.5 2.7 %collective-permute-start.11 = (bf16[4,8,48,128]{3,2,1,0:T(8,128)(2,1)S(1)}, bf16[4,8,48,128]{3,2,1,0:T(8,128)(2,1)S(1)}, u32[]{:S(2)}, u32[]{:S(2)}) collective-permute-start(bf16[4,8,48,128]{3,2,1,0:T(8,128)(2,1)S(1)} %get-tuple-element.54), channel_id=1, source_target_pairs={{0,4},{4,0},{8,12},{12,8},{1,5},{5,1},{9,13},{13,9},{2,6},{6,2},{1... | collective-permute-start | bytes 1179656 | tf_op jit(solution)/shard_map/ppermute | solution.py:275
  9.1 4.3 %collective-permute-start.1 = (bf16[4,8,48,128]{3,2,1,0:T(8,128)(2,1)S(1)}, bf16[4,8,48,128]{3,2,1,0:T(8,128)(2,1)S(1)}, u32[]{:S(2)}, u32[]{:S(2)}) collective-permute-start(bf16[4,8,48,128]{3,2,1,0:T(8,128)(2,1)S(1)} %get-tuple-element.40), channel_id=1, source_target_pairs={{0,4},{4,0},{8,12},{12,8},{1,5},{5,1},{9,13},{13,9},{2,6},{6,2},{1... | collective-permute-start | bytes 1179656 | tf_op jit(solution)/shard_map/ppermute | solution.py:275
  14.1 2.2 %shard_map.58.refs_0_ = f32[8,8,48,128]{3,2,1,0:T(8,128)S(1)} custom-call(f32[8,8,64,128]{3,2,1,0:T(8,128)S(1)} %get-tuple-element.52.refs_0_.refs_5_, bf16[8,4,48,128]{3,2,1,0:T(8,128)(2,1)S(1)} %collective-permute-done.10.refs_1_, bf16[8,8,48,256]{3,2,1,0:T(8,128)(2,1)S(1)} %copy-done, f32[64,48]{1,0:T(8,128)S(1)} %bitcast.11, f32[4,64,48]{2,1,0:T(8,128)S(1)} %bitcast.5), custom_call_target="tpu_custom_call" | custom-call | tf_op jit(solution)/shard_map/pallas_call | solution.py:186
  18.3 5.0 %collective-permute-start.14 = (bf16[4,8,48,128]{3,2,1,0:T(8,128)(2,1)S(1)}, bf16[4,8,48,128]{3,2,1,0:T(8,128)(2,1)S(1)}, u32[]{:S(2)}, u32[]{:S(2)}) collective-permute-start(bf16[4,8,48,128]{3,2,1,0:T(8,128)(2,1)S(1)} %get-tuple-element.58), channel_id=1, source_target_pairs={{0,4},{4,0},{8,12},{12,8},{1,5},{5,1},{9,13},{13,9},{2,6},{6,2},{1... | collective-permute-start | bytes 1179656 | tf_op jit(solution)/shard_map/ppermute | solution.py:275
  24.1 2.1 %shard_map.51.refs_0_ = f32[8,8,48,128]{3,2,1,0:T(8,128)S(1)} custom-call(f32[8,8,64,128]{3,2,1,0:T(8,128)S(1)} %get-tuple-element.38.refs_0_.refs_5_, bf16[8,4,48,128]{3,2,1,0:T(8,128)(2,1)S(1)} %collective-permute-done.refs_1_, bf16[8,8,48,256]{3,2,1,0:T(8,128)(2,1)S(1)} %copy-done.1, f32[64,48]{1,0:T(8,128)S(1)} %bitcast.13, f32[4,64,48]{2,1,0:T(8,128)S(1)} %bitcast.6), custom_call_target="tpu_custom_call" | custom-call | tf_op jit(solution)/shard_map/pallas_call | solution.py:186
  27.6 4.2 %collective-permute-start.4 = (bf16[4,8,48,128]{3,2,1,0:T(8,128)(2,1)S(1)}, bf16[4,8,48,128]{3,2,1,0:T(8,128)(2,1)S(1)}, u32[]{:S(2)}, u32[]{:S(2)}) collective-permute-start(bf16[4,8,48,128]{3,2,1,0:T(8,128)(2,1)S(1)} %get-tuple-element.44), channel_id=1, source_target_pairs={{0,4},{4,0},{8,12},{12,8},{1,5},{5,1},{9,13},{13,9},{2,6},{6,2},{1... | collective-permute-start | bytes 1179656 | tf_op jit(solution)/shard_map/ppermute | solution.py:275
  32.5 2.3 %shard_map.60.refs_0_ = f32[8,8,48,128]{3,2,1,0:T(8,128)S(1)} custom-call(f32[8,8,64,128]{3,2,1,0:T(8,128)S(1)} %get-tuple-element.56.refs_0_.refs_5_, bf16[8,4,48,128]{3,2,1,0:T(8,128)(2,1)S(1)} %collective-permute-done.13.refs_1_, bf16[8,8,48,256]{3,2,1,0:T(8,128)(2,1)S(1)} %copy-done.1, f32[64,48]{1,0:T(8,128)S(1)} %bitcast.15, f32[4,64,48]{2,1,0:T(8,128)S(1)} %bitcast.7, ...), custom_call_target="tpu_custom_call" | custom-call | tf_op jit(solution)/shard_map/pallas_call | solution.py:186
  36.1 4.1 %collective-permute-start.17 = (bf16[4,8,48,128]{3,2,1,0:T(8,128)(2,1)S(1)}, bf16[4,8,48,128]{3,2,1,0:T(8,128)(2,1)S(1)}, u32[]{:S(2)}, u32[]{:S(2)}) collective-permute-start(bf16[4,8,48,128]{3,2,1,0:T(8,128)(2,1)S(1)} %get-tuple-element.62), channel_id=1, source_target_pairs={{0,4},{4,0},{8,12},{12,8},{1,5},{5,1},{9,13},{13,9},{2,6},{6,2},{1... | collective-permute-start | bytes 1179656 | tf_op jit(solution)/shard_map/ppermute | solution.py:275
  40.9 2.3 %shard_map.53.refs_0_ = f32[8,8,48,128]{3,2,1,0:T(8,128)S(1)} custom-call(f32[8,8,64,128]{3,2,1,0:T(8,128)S(1)} %get-tuple-element.42.refs_0_.refs_5_, bf16[8,4,48,128]{3,2,1,0:T(8,128)(2,1)S(1)} %collective-permute-done.3.refs_1_, bf16[8,8,48,256]{3,2,1,0:T(8,128)(2,1)S(1)} %copy-done.1, f32[64,48]{1,0:T(8,128)S(1)} %bitcast.17, f32[4,64,48]{2,1,0:T(8,128)S(1)} %bitcast.8, ...), custom_call_target="tpu_custom_call" | custom-call | tf_op jit(solution)/shard_map/pallas_call | solution.py:186
  44.5 4.1 %collective-permute-start.7 = (bf16[4,8,48,128]{3,2,1,0:T(8,128)(2,1)S(1)}, bf16[4,8,48,128]{3,2,1,0:T(8,128)(2,1)S(1)}, u32[]{:S(2)}, u32[]{:S(2)}) collective-permute-start(bf16[4,8,48,128]{3,2,1,0:T(8,128)(2,1)S(1)} %get-tuple-element.48), channel_id=1, source_target_pairs={{0,4},{4,0},{8,12},{12,8},{1,5},{5,1},{9,13},{13,9},{2,6},{6,2},{1... | collective-permute-start | bytes 1179656 | tf_op jit(solution)/shard_map/ppermute | solution.py:275
  49.3 2.3 %shard_map.62.refs_0_ = f32[8,8,48,128]{3,2,1,0:T(8,128)S(1)} custom-call(f32[8,8,64,128]{3,2,1,0:T(8,128)S(1)} %get-tuple-element.60.refs_0_, bf16[8,4,48,128]{3,2,1,0:T(8,128)(2,1)S(1)} %collective-permute-done.16.refs_1_, bf16[8,8,48,256]{3,2,1,0:T(8,128)(2,1)S(1)} %copy-done.1, f32[64,48]{1,0:T(8,128)S(1)} %bitcast.19, f32[4,64,48]{2,1,0:T(8,128)S(1)} %bitcast.9, ...), custom_call_target="tpu_custom_call" | custom-call | tf_op jit(solution)/shard_map/pallas_call | solution.py:186
  52.6 1.6 %collective-permute-start.19 = (bf16[4,8,48,128]{3,2,1,0:T(8,128)(2,1)S(1)}, bf16[4,8,48,128]{3,2,1,0:T(8,128)(2,1)S(1)}, u32[]{:S(2)}, u32[]{:S(2)}) collective-permute-start(bf16[4,8,48,128]{3,2,1,0:T(8,128)(2,1)S(1)} %get-tuple-element.65), channel_id=1, source_target_pairs={{0,2},{2,0},{1,3},{3,1},{4,6},{6,4},{5,7},{7,5},{8,10},{10,8},{9,1... | collective-permute-start | bytes 1179656 | tf_op jit(solution)/shard_map/ppermute | solution.py:275
  54.1 2.2 %shard_map.55.refs_0_ = f32[8,8,48,128]{3,2,1,0:T(8,128)S(1)} custom-call(f32[8,8,64,128]{3,2,1,0:T(8,128)S(1)} %get-tuple-element.46.refs_0_, bf16[8,4,48,128]{3,2,1,0:T(8,128)(2,1)S(1)} %collective-permute-done.6.refs_1_, bf16[8,8,48,256]{3,2,1,0:T(8,128)(2,1)S(1)} %copy-done.1, f32[64,48]{1,0:T(8,128)S(1)} %bitcast.21, f32[4,64,48]{2,1,0:T(8,128)S(1)} %bitcast.10, ...), custom_call_target="tpu_custom_call" | custom-call | tf_op jit(solution)/shard_map/pallas_call | solution.py:186
  56.4 2.6 %collective-permute-done.7.refs_1_ = bf16[4,8,48,128]{3,2,1,0:T(8,128)(2,1)S(1)} collective-permute-done((bf16[4,8,48,128]{3,2,1,0:T(8,128)(2,1)S(1)}, bf16[4,8,48,128]{3,2,1,0:T(8,128)(2,1)S(1)}, u32[]{:S(2)}, u32[]{:S(2)}) %collective-permute-start.7) | collective-permute-done | bytes 393248 | tf_op jit(solution)/shard_map/ppermute | solution.py:275
  60.0 1.7 %collective-permute-start.9 = (bf16[4,8,48,128]{3,2,1,0:T(8,128)(2,1)S(1)}, bf16[4,8,48,128]{3,2,1,0:T(8,128)(2,1)S(1)}, u32[]{:S(2)}, u32[]{:S(2)}) collective-permute-start(bf16[4,8,48,128]{3,2,1,0:T(8,128)(2,1)S(1)} %get-tuple-element.51), channel_id=1, source_target_pairs={{0,2},{2,0},{1,3},{3,1},{4,6},{6,4},{5,7},{7,5},{8,10},{10,8},{9,1... | collective-permute-start | bytes 1179656 | tf_op jit(solution)/shard_map/ppermute | solution.py:275
  61.7 2.9 %collective-permute-done.19.refs_3_ = bf16[4,8,48,128]{3,2,1,0:T(8,128)(2,1)S(1)} collective-permute-done((bf16[4,8,48,128]{3,2,1,0:T(8,128)(2,1)S(1)}, bf16[4,8,48,128]{3,2,1,0:T(8,128)(2,1)S(1)}, u32[]{:S(2)}, u32[]{:S(2)}) %collective-permute-start.19) | collective-permute-done | bytes 393248 | tf_op jit(solution)/shard_map/ppermute | solution.py:275
  64.6 7.7 %collective-permute-done.9.refs_1_ = bf16[4,8,48,128]{3,2,1,0:T(8,128)(2,1)S(1)} collective-permute-done((bf16[4,8,48,128]{3,2,1,0:T(8,128)(2,1)S(1)}, bf16[4,8,48,128]{3,2,1,0:T(8,128)(2,1)S(1)}, u32[]{:S(2)}, u32[]{:S(2)}) %collective-permute-start.9) | collective-permute-done | bytes 393248 | tf_op jit(solution)/shard_map/ppermute | solution.py:275
  73.7 1.9 %collective-permute-done.20.got_ref = f32[520,256]{1,0:T(8,128)S(1)} collective-permute-done((f32[520,256]{1,0:T(8,128)S(1)}, f32[520,256]{1,0:T(8,128)S(1)}, u32[]{:S(2)}, u32[]{:S(2)}) %collective-permute-start.20) | collective-permute-done | bytes 532512 | tf_op jit(solution)/shard_map/ppermute | solution.py:275
  75.6 4.2 %collective-permute-start.21 = (bf16[144,256]{1,0:T(8,128)(2,1)S(1)}, bf16[144,256]{1,0:T(8,128)(2,1)S(1)}, u32[]{:S(2)}, u32[]{:S(2)}) collective-permute-start(bf16[144,256]{1,0:T(8,128)(2,1)S(1)} %get-tuple-element.69), channel_id=1, source_target_pairs={{0,8},{4,12},{8,0},{12,4},{1,9},{5,13},{9,1},{13,5},{2,10},{6,14},... | collective-permute-start | bytes 221192 | tf_op jit(solution)/shard_map/ppermute | solution.py:480
  79.8 1.6 %collective-permute-start.22 = (bf16[144,256]{1,0:T(8,128)(2,1)S(1)}, bf16[144,256]{1,0:T(8,128)(2,1)S(1)}, u32[]{:S(2)}, u32[]{:S(2)}) collective-permute-start(bf16[144,256]{1,0:T(8,128)(2,1)S(1)} %get-tuple-element.70), channel_id=1, source_target_pairs={{0,12},{4,8},{8,4},{12,0},{1,13},{5,9},{9,5},{13,1},{2,14},{6,10},... | collective-permute-start | bytes 221192 | tf_op jit(solution)/shard_map/ppermute | solution.py:480
  81.4 3.9 %collective-permute-done.21.refs_0_ = bf16[144,256]{1,0:T(8,128)(2,1)S(1)} collective-permute-done((bf16[144,256]{1,0:T(8,128)(2,1)S(1)}, bf16[144,256]{1,0:T(8,128)(2,1)S(1)}, u32[]{:S(2)}, u32[]{:S(2)}) %collective-permute-start.21) | collective-permute-done | bytes 73760 | tf_op jit(solution)/shard_map/ppermute | solution.py:480
  87.1 1.6 %collective-permute-start.24 = (bf16[144,256]{1,0:T(8,128)(2,1)S(1)}, bf16[144,256]{1,0:T(8,128)(2,1)S(1)}, u32[]{:S(2)}, u32[]{:S(2)}) collective-permute-start(bf16[144,256]{1,0:T(8,128)(2,1)S(1)} %shard_map.66.mine_ref), channel_id=1, source_target_pairs={{0,2},{2,0},{1,3},{3,1},{4,6},{6,4},{5,7},{7,5},{8,10},{10,8},{9,1... | collective-permute-start | bytes 221192 | tf_op jit(solution)/shard_map/ppermute | solution.py:275
  88.6 2.9 %collective-permute-done.24.other_ref = bf16[144,256]{1,0:T(8,128)(2,1)S(1)} collective-permute-done((bf16[144,256]{1,0:T(8,128)(2,1)S(1)}, bf16[144,256]{1,0:T(8,128)(2,1)S(1)}, u32[]{:S(2)}, u32[]{:S(2)}) %collective-permute-start.24) | collective-permute-done | bytes 73760 | tf_op jit(solution)/shard_map/ppermute | solution.py:275
  (57 shorter events, 21.6 us)
Async XLA Ops:
  4.0 9.4 %collective-permute-start.10 = (bf16[8,4,48,128]{3,2,1,0:T(8,128)(2,1)S(1)}, bf16[8,4,48,128]{3,2,1,0:T(8,128)(2,1)S(1)}, u32[]{:S(2)}, u32[]{:S(2)}) collective-permute-start(bf16[8,4,48,128]{3,2,1,0:T(8,128)(2,1)S(1)} %get-tuple-element.53), channel_id=1, source_target_pairs={{0,1},{1,0},{2,3},{3,2},{4,5},{5,4},{6,7},{7,6},{8,9},{9,8},{10,11... | collective-permute-start | bytes 1179656 | tf_op jit(solution)/shard_map/ppermute | solution.py:275
  4.5 12.6 %collective-permute-start.11 = (bf16[4,8,48,128]{3,2,1,0:T(8,128)(2,1)S(1)}, bf16[4,8,48,128]{3,2,1,0:T(8,128)(2,1)S(1)}, u32[]{:S(2)}, u32[]{:S(2)}) collective-permute-start(bf16[4,8,48,128]{3,2,1,0:T(8,128)(2,1)S(1)} %get-tuple-element.54), channel_id=1, source_target_pairs={{0,4},{4,0},{8,12},{12,8},{1,5},{5,1},{9,13},{13,9},{2,6},{6,2},{1... | collective-permute-start | bytes 1179656 | tf_op jit(solution)/shard_map/ppermute | solution.py:275
  7.2 10.0 %collective-permute-start.12 = (bf16[4,8,48,128]{3,2,1,0:T(8,128)(2,1)S(1)}, bf16[4,8,48,128]{3,2,1,0:T(8,128)(2,1)S(1)}, u32[]{:S(2)}, u32[]{:S(2)}) collective-permute-start(bf16[4,8,48,128]{3,2,1,0:T(8,128)(2,1)S(1)} %get-tuple-element.55), channel_id=1, source_target_pairs={{4,8},{8,4},{5,9},{9,5},{6,10},{10,6},{7,11},{11,7},{20,24},{24,20... | collective-permute-start | bytes 1179656 | tf_op jit(solution)/shard_map/ppermute | solution.py:275
  8.9 14.4 %collective-permute-start = (bf16[8,4,48,128]{3,2,1,0:T(8,128)(2,1)S(1)}, bf16[8,4,48,128]{3,2,1,0:T(8,128)(2,1)S(1)}, u32[]{:S(2)}, u32[]{:S(2)}) collective-permute-start(bf16[8,4,48,128]{3,2,1,0:T(8,128)(2,1)S(1)} %get-tuple-element.39), channel_id=1, source_target_pairs={{0,1},{1,0},{2,3},{3,2},{4,5},{5,4},{6,7},{7,6},{8,9},{9,8},{10,11... | collective-permute-start | bytes 1179656 | tf_op jit(solution)/shard_map/ppermute | solution.py:275
  9.1 17.1 %collective-permute-start.1 = (bf16[4,8,48,128]{3,2,1,0:T(8,128)(2,1)S(1)}, bf16[4,8,48,128]{3,2,1,0:T(8,128)(2,1)S(1)}, u32[]{:S(2)}, u32[]{:S(2)}) collective-permute-start(bf16[4,8,48,128]{3,2,1,0:T(8,128)(2,1)S(1)} %get-tuple-element.40), channel_id=1, source_target_pairs={{0,4},{4,0},{8,12},{12,8},{1,5},{5,1},{9,13},{13,9},{2,6},{6,2},{1... | collective-permute-start | bytes 1179656 | tf_op jit(solution)/shard_map/ppermute | solution.py:275
  13.4 12.8 %collective-permute-start.2 = (bf16[4,8,48,128]{3,2,1,0:T(8,128)(2,1)S(1)}, bf16[4,8,48,128]{3,2,1,0:T(8,128)(2,1)S(1)}, u32[]{:S(2)}, u32[]{:S(2)}) collective-permute-start(bf16[4,8,48,128]{3,2,1,0:T(8,128)(2,1)S(1)} %get-tuple-element.41), channel_id=1, source_target_pairs={{4,8},{8,4},{5,9},{9,5},{6,10},{10,6},{7,11},{11,7},{20,24},{24,20... | collective-permute-start | bytes 1179656 | tf_op jit(solution)/shard_map/ppermute | solution.py:275
  18.2 13.5 %collective-permute-start.13 = (bf16[8,4,48,128]{3,2,1,0:T(8,128)(2,1)S(1)}, bf16[8,4,48,128]{3,2,1,0:T(8,128)(2,1)S(1)}, u32[]{:S(2)}, u32[]{:S(2)}) collective-permute-start(bf16[8,4,48,128]{3,2,1,0:T(8,128)(2,1)S(1)} %get-tuple-element.57), channel_id=1, source_target_pairs={{0,1},{1,0},{2,3},{3,2},{4,5},{5,4},{6,7},{7,6},{8,9},{9,8},{10,11... | collective-permute-start | bytes 1179656 | tf_op jit(solution)/shard_map/ppermute | solution.py:275
  18.3 16.4 %collective-permute-start.14 = (bf16[4,8,48,128]{3,2,1,0:T(8,128)(2,1)S(1)}, bf16[4,8,48,128]{3,2,1,0:T(8,128)(2,1)S(1)}, u32[]{:S(2)}, u32[]{:S(2)}) collective-permute-start(bf16[4,8,48,128]{3,2,1,0:T(8,128)(2,1)S(1)} %get-tuple-element.58), channel_id=1, source_target_pairs={{0,4},{4,0},{8,12},{12,8},{1,5},{5,1},{9,13},{13,9},{2,6},{6,2},{1... | collective-permute-start | bytes 1179656 | tf_op jit(solution)/shard_map/ppermute | solution.py:275
  23.4 11.4 %collective-permute-start.15 = (bf16[4,8,48,128]{3,2,1,0:T(8,128)(2,1)S(1)}, bf16[4,8,48,128]{3,2,1,0:T(8,128)(2,1)S(1)}, u32[]{:S(2)}, u32[]{:S(2)}) collective-permute-start(bf16[4,8,48,128]{3,2,1,0:T(8,128)(2,1)S(1)} %get-tuple-element.59), channel_id=1, source_target_pairs={{4,8},{8,4},{5,9},{9,5},{6,10},{10,6},{7,11},{11,7},{20,24},{24,20... | collective-permute-start | bytes 1179656 | tf_op jit(solution)/shard_map/ppermute | solution.py:275
  27.3 12.9 %collective-permute-start.3 = (bf16[8,4,48,128]{3,2,1,0:T(8,128)(2,1)S(1)}, bf16[8,4,48,128]{3,2,1,0:T(8,128)(2,1)S(1)}, u32[]{:S(2)}, u32[]{:S(2)}) collective-permute-start(bf16[8,4,48,128]{3,2,1,0:T(8,128)(2,1)S(1)} %get-tuple-element.43), channel_id=1, source_target_pairs={{0,1},{1,0},{2,3},{3,2},{4,5},{5,4},{6,7},{7,6},{8,9},{9,8},{10,11... | collective-permute-start | bytes 1179656 | tf_op jit(solution)/shard_map/ppermute | solution.py:275
  27.6 15.6 %collective-permute-start.4 = (bf16[4,8,48,128]{3,2,1,0:T(8,128)(2,1)S(1)}, bf16[4,8,48,128]{3,2,1,0:T(8,128)(2,1)S(1)}, u32[]{:S(2)}, u32[]{:S(2)}) collective-permute-start(bf16[4,8,48,128]{3,2,1,0:T(8,128)(2,1)S(1)} %get-tuple-element.44), channel_id=1, source_target_pairs={{0,4},{4,0},{8,12},{12,8},{1,5},{5,1},{9,13},{13,9},{2,6},{6,2},{1... | collective-permute-start | bytes 1179656 | tf_op jit(solution)/shard_map/ppermute | solution.py:275
  31.8 11.4 %collective-permute-start.5 = (bf16[4,8,48,128]{3,2,1,0:T(8,128)(2,1)S(1)}, bf16[4,8,48,128]{3,2,1,0:T(8,128)(2,1)S(1)}, u32[]{:S(2)}, u32[]{:S(2)}) collective-permute-start(bf16[4,8,48,128]{3,2,1,0:T(8,128)(2,1)S(1)} %get-tuple-element.45), channel_id=1, source_target_pairs={{4,8},{8,4},{5,9},{9,5},{6,10},{10,6},{7,11},{11,7},{20,24},{24,20... | collective-permute-start | bytes 1179656 | tf_op jit(solution)/shard_map/ppermute | solution.py:275
  35.9 12.8 %collective-permute-start.16 = (bf16[8,4,48,128]{3,2,1,0:T(8,128)(2,1)S(1)}, bf16[8,4,48,128]{3,2,1,0:T(8,128)(2,1)S(1)}, u32[]{:S(2)}, u32[]{:S(2)}) collective-permute-start(bf16[8,4,48,128]{3,2,1,0:T(8,128)(2,1)S(1)} %get-tuple-element.61), channel_id=1, source_target_pairs={{0,1},{1,0},{2,3},{3,2},{4,5},{5,4},{6,7},{7,6},{8,9},{9,8},{10,11... | collective-permute-start | bytes 1179656 | tf_op jit(solution)/shard_map/ppermute | solution.py:275
  36.1 15.5 %collective-permute-start.17 = (bf16[4,8,48,128]{3,2,1,0:T(8,128)(2,1)S(1)}, bf16[4,8,48,128]{3,2,1,0:T(8,128)(2,1)S(1)}, u32[]{:S(2)}, u32[]{:S(2)}) collective-permute-start(bf16[4,8,48,128]{3,2,1,0:T(8,128)(2,1)S(1)} %get-tuple-element.62), channel_id=1, source_target_pairs={{0,4},{4,0},{8,12},{12,8},{1,5},{5,1},{9,13},{13,9},{2,6},{6,2},{1... | collective-permute-start | bytes 1179656 | tf_op jit(solution)/shard_map/ppermute | solution.py:275
  40.2 11.4 %collective-permute-start.18 = (bf16[4,8,48,128]{3,2,1,0:T(8,128)(2,1)S(1)}, bf16[4,8,48,128]{3,2,1,0:T(8,128)(2,1)S(1)}, u32[]{:S(2)}, u32[]{:S(2)}) collective-permute-start(bf16[4,8,48,128]{3,2,1,0:T(8,128)(2,1)S(1)} %get-tuple-element.63), channel_id=1, source_target_pairs={{4,8},{8,4},{5,9},{9,5},{6,10},{10,6},{7,11},{11,7},{20,24},{24,20... | collective-permute-start | bytes 1179656 | tf_op jit(solution)/shard_map/ppermute | solution.py:275
  44.3 9.9 %collective-permute-start.6 = (bf16[8,4,48,128]{3,2,1,0:T(8,128)(2,1)S(1)}, bf16[8,4,48,128]{3,2,1,0:T(8,128)(2,1)S(1)}, u32[]{:S(2)}, u32[]{:S(2)}) collective-permute-start(bf16[8,4,48,128]{3,2,1,0:T(8,128)(2,1)S(1)} %get-tuple-element.47), channel_id=1, source_target_pairs={{0,1},{1,0},{2,3},{3,2},{4,5},{5,4},{6,7},{7,6},{8,9},{9,8},{10,11... | collective-permute-start | bytes 1179656 | tf_op jit(solution)/shard_map/ppermute | solution.py:275
  44.5 14.5 %collective-permute-start.7 = (bf16[4,8,48,128]{3,2,1,0:T(8,128)(2,1)S(1)}, bf16[4,8,48,128]{3,2,1,0:T(8,128)(2,1)S(1)}, u32[]{:S(2)}, u32[]{:S(2)}) collective-permute-start(bf16[4,8,48,128]{3,2,1,0:T(8,128)(2,1)S(1)} %get-tuple-element.48), channel_id=1, source_target_pairs={{0,4},{4,0},{8,12},{12,8},{1,5},{5,1},{9,13},{13,9},{2,6},{6,2},{1... | collective-permute-start | bytes 1179656 | tf_op jit(solution)/shard_map/ppermute | solution.py:275
  48.6 10.4 %collective-permute-start.8 = (bf16[4,8,48,128]{3,2,1,0:T(8,128)(2,1)S(1)}, bf16[4,8,48,128]{3,2,1,0:T(8,128)(2,1)S(1)}, u32[]{:S(2)}, u32[]{:S(2)}) collective-permute-start(bf16[4,8,48,128]{3,2,1,0:T(8,128)(2,1)S(1)} %get-tuple-element.49), channel_id=1, source_target_pairs={{4,8},{8,4},{5,9},{9,5},{6,10},{10,6},{7,11},{11,7},{20,24},{24,20... | collective-permute-start | bytes 1179656 | tf_op jit(solution)/shard_map/ppermute | solution.py:275
  52.6 12.0 %collective-permute-start.19 = (bf16[4,8,48,128]{3,2,1,0:T(8,128)(2,1)S(1)}, bf16[4,8,48,128]{3,2,1,0:T(8,128)(2,1)S(1)}, u32[]{:S(2)}, u32[]{:S(2)}) collective-permute-start(bf16[4,8,48,128]{3,2,1,0:T(8,128)(2,1)S(1)} %get-tuple-element.65), channel_id=1, source_target_pairs={{0,2},{2,0},{1,3},{3,1},{4,6},{6,4},{5,7},{7,5},{8,10},{10,8},{9,1... | collective-permute-start | bytes 1179656 | tf_op jit(solution)/shard_map/ppermute | solution.py:275
  60.0 12.3 %collective-permute-start.9 = (bf16[4,8,48,128]{3,2,1,0:T(8,128)(2,1)S(1)}, bf16[4,8,48,128]{3,2,1,0:T(8,128)(2,1)S(1)}, u32[]{:S(2)}, u32[]{:S(2)}) collective-permute-start(bf16[4,8,48,128]{3,2,1,0:T(8,128)(2,1)S(1)} %get-tuple-element.51), channel_id=1, source_target_pairs={{0,2},{2,0},{1,3},{3,1},{4,6},{6,4},{5,7},{7,5},{8,10},{10,8},{9,1... | collective-permute-start | bytes 1179656 | tf_op jit(solution)/shard_map/ppermute | solution.py:275
  75.6 9.6 %collective-permute-start.21 = (bf16[144,256]{1,0:T(8,128)(2,1)S(1)}, bf16[144,256]{1,0:T(8,128)(2,1)S(1)}, u32[]{:S(2)}, u32[]{:S(2)}) collective-permute-start(bf16[144,256]{1,0:T(8,128)(2,1)S(1)} %get-tuple-element.69), channel_id=1, source_target_pairs={{0,8},{4,12},{8,0},{12,4},{1,9},{5,13},{9,1},{13,5},{2,10},{6,14},... | collective-permute-start | bytes 221192 | tf_op jit(solution)/shard_map/ppermute | solution.py:480
  79.8 6.7 %collective-permute-start.22 = (bf16[144,256]{1,0:T(8,128)(2,1)S(1)}, bf16[144,256]{1,0:T(8,128)(2,1)S(1)}, u32[]{:S(2)}, u32[]{:S(2)}) collective-permute-start(bf16[144,256]{1,0:T(8,128)(2,1)S(1)} %get-tuple-element.70), channel_id=1, source_target_pairs={{0,12},{4,8},{8,4},{12,0},{1,13},{5,9},{9,5},{13,1},{2,14},{6,10},... | collective-permute-start | bytes 221192 | tf_op jit(solution)/shard_map/ppermute | solution.py:480
  81.4 5.7 %collective-permute-start.23 = (bf16[144,256]{1,0:T(8,128)(2,1)S(1)}, bf16[144,256]{1,0:T(8,128)(2,1)S(1)}, u32[]{:S(2)}, u32[]{:S(2)}) collective-permute-start(bf16[144,256]{1,0:T(8,128)(2,1)S(1)} %get-tuple-element.71), channel_id=1, source_target_pairs={{0,4},{4,0},{8,12},{12,8},{1,5},{5,1},{9,13},{13,9},{2,6},{6,2},{1... | collective-permute-start | bytes 221192 | tf_op jit(solution)/shard_map/ppermute | solution.py:480
  87.1 4.4 %collective-permute-start.24 = (bf16[144,256]{1,0:T(8,128)(2,1)S(1)}, bf16[144,256]{1,0:T(8,128)(2,1)S(1)}, u32[]{:S(2)}, u32[]{:S(2)}) collective-permute-start(bf16[144,256]{1,0:T(8,128)(2,1)S(1)} %shard_map.66.mine_ref), channel_id=1, source_target_pairs={{0,2},{2,0},{1,3},{3,1},{4,6},{6,4},{5,7},{7,5},{8,10},{10,8},{9,1... | collective-permute-start | bytes 221192 | tf_op jit(solution)/shard_map/ppermute | solution.py:275
  (7 other events, 32.3 us)

commit v6 on v5

--- a/solution.py
+++ b/solution.py
@@ -23,6 +23,17 @@
     return pltpu.CompilerParams(
         dimension_semantics=semantics or None, vmem_limit_bytes=VMEM_LIMIT
     )
+
+
+def carried(operands, in_specs, out_specs, out_shape, carry):
+    aliases = {}
+    for array in carry:
+        aliases[len(operands)] = len(out_shape)
+        operands.append(array)
+        in_specs.append(pl.BlockSpec(memory_space=pl.ANY))
+        out_specs.append(pl.BlockSpec(memory_space=pl.ANY))
+        out_shape.append(jax.ShapeDtypeStruct(array.shape, array.dtype))
+    return aliases
 
 
 def whole_vmem(count):
@@ -132,11 +143,12 @@
     )(probes, source)
 
 
-def local_body(chunk, moment, has_previous, *refs):
+def local_body(chunk, moment, has_previous, carries, *refs):
     refs = list(refs)
     u_ref, beside_ref, p_ref, c_ref, s_ref = refs[:5]
     prev_ref = refs[5] if has_previous else None
-    base_ref, square, turned_c, turned_s = refs[-4:]
+    base_ref = refs[5 + has_previous + carries]
+    square, turned_c, turned_s = refs[-3:]
     depth, across, along, _ = base_ref.shape
     core = lax.axis_index("sub")
     left_on = (core == 1).astype(F32)
@@ -178,24 +190,28 @@
     tiles(along, tile)
 
 
-def local_step(u, beside, probes, chunk, courant, source, moment, previous):
+def local_step(u, beside, probes, chunk, courant, source, moment, previous, carry=()):
     depth, across, along, _ = probes.shape
     operands = [u, beside, probes, courant, source]
     if previous is not None:
         operands.append(previous)
-    return pl.pallas_call(
-        functools.partial(local_body, chunk, moment, previous is not None),
-        in_specs=whole_vmem(len(operands)),
-        out_specs=whole_vmem(1)[0],
-        out_shape=shape_of(depth, across, along, F32),
+    in_specs, out_specs = whole_vmem(len(operands)), whole_vmem(1)
+    out_shape = [shape_of(depth, across, along, F32)]
+    aliases = carried(operands, in_specs, out_specs, out_shape, carry)
+    return pl.pallas_call(
+        functools.partial(local_body, chunk, moment, previous is not None, len(carry)),
+        in_specs=in_specs,
+        out_specs=out_specs,
+        out_shape=out_shape,
+        input_output_aliases=aliases,
         scratch_shapes=square_scratch() + square_scratch()[:1],
         compiler_params=params(),
     )(*operands)
 
 
-def rim_body(first, kind, parts, *refs):
+def rim_body(first, kind, parts, after, *refs):
     base_ref, even_ref, odd_ref, c_ref = refs[:4]
-    outs, (square, turned_c) = refs[4:-2], refs[-2:]
+    outs, (square, turned_c) = refs[4 + after : -2], refs[-2:]
     depth, all_across, along, _ = base_ref.shape
     across = even_ref.shape[1]
     core = lax.axis_index("sub")
@@ -234,13 +250,6 @@
                     outs[0][z, place, rows] = new
                 edges = (outs[1 : 1 + parts], outs[1 + parts : 1 + 2 * parts])
                 store_edges(place, span, news, even, edges)
-            elif kind == "half":
-                keep_ref, send_ref = outs
-                lower = lax.axis_index("probe") == 0
-                for z in range(depth // 2):
-                    one, two = news[z].astype(BF16), news[z + depth // 2].astype(BF16)
-                    keep_ref[z, x, span] = jnp.where(lower, one, two)
-                    send_ref[z, x, span] = jnp.where(lower, two, one)
             else:
                 for z, new in enumerate(news):
                     outs[0][z, x, span] = new.astype(BF16)
@@ -250,59 +259,112 @@
     tiles(along, tile)
 
 
-def rim_step(base, evens, odds, courant, kind, first=0, parts=1):
+def rim_step(base, evens, odds, courant, kind, first=0, parts=1, after=()):
     depth, all_across, along, _ = base.shape
     across = evens.shape[1]
     if kind == "middle":
         edge = [shape_of(RADIUS, across // parts, along, BF16)] * parts
         out_shape = [shape_of(depth, across, along + 2 * EDGE, F32)]
         out_shape += edge + edge + [shape_of(depth, RADIUS, along, BF16)]
-    elif kind == "half":
-        out_shape = [shape_of(depth // 2, across, along, BF16)] * 2
     else:
         out_shape = [shape_of(depth, across, along, BF16)]
     return pl.pallas_call(
-        functools.partial(rim_body, first, kind, parts),
-        in_specs=whole_vmem(4),
+        functools.partial(rim_body, first, kind, parts, len(after)),
+        in_specs=whole_vmem(4) + [pl.BlockSpec(memory_space=pl.ANY)] * len(after),
         out_specs=whole_vmem(len(out_shape)),
         out_shape=out_shape,
         scratch_shapes=square_scratch(),
         compiler_params=params(),
-    )(base, evens, odds, courant)
+    )(base, evens, odds, courant, *after)
+
+
+def last_body(first, sent, carries, *refs):
+    base_ref, even_ref, odd_ref, c_ref = refs[:4]
+    out_ref = refs[4 + carries]
+    square, turned_c = refs[-2:]
+    depth, all_across, along, _ = base_ref.shape
+    across = even_ref.shape[1]
+    chip = lax.axis_index("probe")
+    low = (chip == 1) if sent else (chip == 0)
+    from_odd = low == slab_is_even()
+    turned_c[...] = turned(c_ref[...], square)
+
+    def tile(start):
+        span = pl.ds(start, TILE)
+        courant = turned_c[span]
+        for x in range(across):
+            place = first + x
+            near = []
+            for j in range(RADIUS):
+                at = jnp.where(low, RADIUS - 1 - j, j)
+                near.append(
+                    jnp.where(from_odd, odd_ref[at, x, span], even_ref[at, x, span]).astype(F32)
+                )
+            for m in range(RADIUS):
+                mirror = depth - 1 - m
+                added = COEFFICIENTS[m + 1] * near[0]
+                for r in range(m + 2, RADIUS + 1):
+                    added = added + COEFFICIENTS[r] * near[r - m - 1]
+                scale = jnp.where(
+                    low,
+                    lane(courant, m * all_across + place),
+                    lane(courant, mirror * all_across + place),
+                )
+                new = base_ref[jnp.where(low, m, mirror), place, span] + scale * added
+                out_ref[m, x, span] = new.astype(BF16)
+
+    tiles(along, tile)
+
+
+def last_step(base, evens, odds, courant, first, sent, carry=()):
+    _, _, along, _ = base.shape
+    across = evens.shape[1]
+    operands = [base, evens, odds, courant]
+    in_specs, out_specs = whole_vmem(4), whole_vmem(1)
+    out_shape = [shape_of(RADIUS, across, along, BF16)]
+    aliases = carried(operands, in_specs, out_specs, out_shape, carry)
+    return pl.pallas_call(
+        functools.partial(last_body, first, sent, len(carry)),
+        in_specs=in_specs,
+        out_specs=out_specs,
+        out_shape=out_shape,
+        input_output_aliases=aliases,
+        scratch_shapes=square_scratch(),
+        compiler_params=params(),
+    )(*operands)
 
 
 def swap(x, axis, pairs):
     return lax.ppermute(x, axis, [p for a, b in pairs for p in ((a, b), (b, a))])
 
 
-def exchange(evens, odds, edge):
-    slabs = lax.axis_size("slab")
-    pairs = []
-    for one, two in zip(evens, odds):
-        pairs.append(
-            (
-                swap(one, "slab", [(i, i + 1) for i in range(0, slabs - 1, 2)]),
-                swap(two, "slab", [(i, i + 1) for i in range(1, slabs - 1, 2)]),
-            )
-        )
-    return pairs, swap(edge, "sub", [(0, 1)])
-
-
-def gram_body(parts, pieces, *refs):
-    ins, (keep_ref, send_ref), panel = refs[: 2 * len(pieces)], refs[-3:-1], refs[-1]
+def even_swap(x):
+    return swap(x, "slab", [(i, i + 1) for i in range(0, lax.axis_size("slab") - 1, 2)])
+
+
+def odd_swap(x):
+    return swap(x, "slab", [(i, i + 1) for i in range(1, lax.axis_size("slab") - 1, 2)])
+
+
+def core_swap(x):
+    return swap(x, "sub", [(0, 1)])
+
+
+def chip_swap(x):
+    return swap(x, "probe", [(0, 1)])
+
+
+def gram_body(parts, first, last, *refs):
     half = parts // 2
+    ins, (keep_ref, send_ref), panel = refs[:parts], refs[-3:-1], refs[-1]
     chip = lax.axis_index("probe")
     core = lax.axis_index("sub")
-    depth, _, along, _ = ins[0].shape
-    across = panel.shape[0] // (depth * along)
-    for (chunk, first), keep, got in zip(pieces, ins[0::2], ins[1::2]):
-        mine = pl.multiple_of((chip * half + chunk) * LANES, LANES)
-        other = pl.multiple_of(((1 - chip) * half + chunk) * LANES, LANES)
-        width = keep.shape[1]
-        for z in range(depth):
-            rows = pl.ds((z * across + first) * along, width * along)
-            panel[rows, pl.ds(mine, LANES)] = keep[z].reshape(width * along, LANES)
-            panel[rows, pl.ds(other, LANES)] = got[z].reshape(width * along, LANES)
+    cells = panel.shape[0]
+    for n in range(half):
+        mine = pl.multiple_of((chip * half + n) * LANES, LANES)
+        other = pl.multiple_of(((1 - chip) * half + n) * LANES, LANES)
+        panel[:, pl.ds(mine, LANES)] = ins[2 * n][...].reshape(cells, LANES)
+        panel[:, pl.ds(other, LANES)] = ins[2 * n + 1][...].reshape(cells, LANES)
     size = parts * LANES
     everything = panel[...]
 
@@ -316,22 +378,28 @@
             preferred_element_type=F32,
         )
 
+    keep = columns(core)
+    send = columns(1 - core)
+    if not first:
+        keep = keep + refs[parts][...]
+        send = send + refs[parts + 1][...]
+    keep_ref[:size] = keep
+    send_ref[:size] = send
+    if not last:
+        return
+
     rows = lax.broadcasted_iota(jnp.int32, (LANES, LANES), 0)
     cols = lax.broadcasted_iota(jnp.int32, (LANES, LANES), 1)
     eye = rows == cols
-    keep = columns(core)
-    send = columns(1 - core)
-    keep_ref[:size] = keep
-    send_ref[:size] = send
-
-    def diagonal(which, first):
+
+    def diagonal(which):
         side = which // 2
         a = keep_ref[which * LANES : (which + 1) * LANES, side * LANES : (side + 1) * LANES]
         b = send_ref[which * LANES : (which + 1) * LANES, side * LANES : (side + 1) * LANES]
         block = jnp.where(core == which % 2, a, b)
         return jnp.sum(jnp.where(eye, block, 0.0), axis=0, keepdims=True)
 
-    diag = [diagonal(n, None) for n in range(parts)]
+    diag = [diagonal(n) for n in range(parts)]
     row0 = jnp.concatenate(diag[:2], axis=1)
     row1 = jnp.concatenate(diag[2:], axis=1)
     tail = jnp.concatenate([row0, row1, jnp.zeros((6, 2 * LANES), F32)], axis=0)
@@ -339,17 +407,19 @@
     send_ref[size:] = tail
 
 
-def gram(parts, pieces, fields, cells):
+def gram(parts, fields, before, last):
     size = parts * LANES
-    shape = jax.ShapeDtypeStruct((size + 8, 2 * LANES), F32)
-    return pl.pallas_call(
-        functools.partial(gram_body, parts, pieces),
-        in_specs=whole_vmem(len(fields)),
+    depth, across, along, _ = fields[0].shape
+    shape = jax.ShapeDtypeStruct((size + 8 * last, 2 * LANES), F32)
+    operands = list(fields) + list(before)
+    return pl.pallas_call(
+        functools.partial(gram_body, parts, not before, last),
+        in_specs=whole_vmem(len(operands)),
         out_specs=whole_vmem(2),
         out_shape=[shape, shape],
-        scratch_shapes=[pltpu.VMEM((cells, size), BF16)],
-        compiler_params=params(),
-    )(*fields)
+        scratch_shapes=[pltpu.VMEM((depth * across * along, size), BF16)],
+        compiler_params=params(),
+    )(*operands)
 
 
 def rounded(ref, block, tail):
@@ -471,18 +541,21 @@
     )(near, far)
 
 
-def coupled(pieces, fields, cells, cell_count):
+def coupled(groups, cell_count):
     slabs = 4
-    keep, send = gram(4, pieces, fields, cells)
-    got = swap(send, "sub", [(0, 1)])
+    sums = ()
+    for n, fields in enumerate(groups):
+        sums = gram(4, fields, sums, n == len(groups) - 1)
+    keep, send = sums
+    got = core_swap(send)
     own, *sent = split_rows(keep, got, slabs)
     arrived = [
         lax.ppermute(sent[d - 1], "slab", [(i, i ^ d) for i in range(slabs)]) for d in (2, 3, 1)
     ]
     mine = sum_all(own, arrived)
-    other = swap(mine, "probe", [(0, 1)])
+    other = chip_swap(mine)
     near, norms = normalise(mine, other, cell_count)
-    far = swap(near, "sub", [(0, 1)])
+    far = core_swap(near)
     return assemble(near, far), norms.reshape(-1)
 
 
@@ -513,40 +586,82 @@
     chunks = count // LANES
     slabs, chips = lax.axis_size("slab"), lax.axis_size("probe")
     cell_count = depth * across * along * slabs * lax.axis_size("sub")
-    paired = chips == 2 and slabs == 4 and chunks == 2
+    paired = chips == 2 and slabs == 4 and chunks == 2 and depth == 2 * RADIUS
     steps = source.shape[0]
     courant = courant.reshape(depth * across, along)
     source = source.reshape(steps, depth * across, along)
 
     now, previous, halos = [], [None] * chunks, []
     for c in range(chunks):
-        u, one, two, edge = first_field(probes, c, source)
+        u, even, odd, edge = first_field(probes, c, source)
         now.append(u)
-        halos.append(exchange([one], [two], edge))
-    pieces, fields = [], []
+        halos.append((even_swap(even), odd_swap(odd), core_swap(edge)))
+    parts = 2 if paired else 1
+    finals, order = [], ()
     for n in range(1, steps):
         for c in range(chunks):
-            pairs, beside = halos[c]
-            base = local_step(now[c], beside, probes, c, courant, source, n, previous[c])
+            even, odd, beside = halos[c]
+            if n == 1:
+                (base,) = local_step(
+                    now[c], beside, probes, c, courant, source, n, previous[c]
+                )
+            else:
+                base = beside
             if n == steps - 1:
-                width = across // len(pairs)
-                for h, (one, two) in enumerate(pairs):
-                    kind = "half" if paired else "all"
-                    out = rim_step(base, one, two, courant, kind, h * width)
-                    if paired:
-                        pieces.append((c, h * width))
-                        fields += [out[0], swap(out[1], "probe", [(0, 1)])]
-                    else:
-                        fields.append(out[0])
-            else:
-                ((one, two),) = pairs
-                out = rim_step(base, one, two, courant, "middle")
-                previous[c], now[c] = now[c], out[0]
-                halos[c] = exchange([out[1]], [out[2]], out[3])
-    if paired:
-        cells = depth // 2 * across * along
-        return coupled(tuple(pieces), fields, cells, cell_count)
-    return coupled_general(fields, cell_count)
+                finals.append((base, even, odd))
+                continue
+            ahead = n == steps - 2
+            pieces = parts if ahead else 1
+            out = rim_step(base, even, odd, courant, "middle", parts=pieces, after=order)
+            previous[c], now[c] = now[c], out[0]
+            evens, odds, edge = out[1 : 1 + pieces], out[1 + pieces : 1 + 2 * pieces], out[-1]
+            odd = odd_swap(odds[0])
+            base, *rest = local_step(
+                now[c],
+                core_swap(edge),
+                probes,
+                c,
+                courant,
+                source,
+                n + 1,
+                previous[c],
+                carry=list(evens) + list(odds[1:]),
+            )
+            order = (base,)
+            halos[c] = ([rest[:pieces], [odd], rest[pieces:]], None, base) if ahead else (
+                even_swap(rest[0]),
+                odd,
+                base,
+            )
+    if not paired:
+        fields = []
+        for base, ((even,), (odd,), _), _ in finals:
+            fields += rim_step(base, even_swap(even), odd, courant, "all")
+        return coupled_general(fields, cell_count)
+
+    width = across // parts
+    groups = [[] for _ in range(parts)]
+    waiting = None
+    for c, (base, (evens, (odd,), odds), _) in enumerate(finals):
+        if c == 0:
+            waiting = finals[1][1]
+        halves_even = [even_swap(evens[0])]
+        halves_odd = [odd]
+        for h in range(1, parts):
+            halves_even.append(even_swap(evens[h]))
+            halves_odd.append(odd_swap(odds[h - 1]))
+        for h in range(parts):
+            carry = ()
+            if c == 0 and h == 0:
+                carry = (waiting[0][1], waiting[2][0])
+            sent, *rest = last_step(
+                base, halves_even[h], halves_odd[h], courant, h * width, True, carry
+            )
+            if rest:
+                waiting[0][1], waiting[2][0] = rest
+            (kept,) = last_step(base, halves_even[h], halves_odd[h], courant, h * width, False)
+            groups[h] += [kept, chip_swap(sent)]
+    return coupled(groups, cell_count)
 
 
 def solution(mesh):

time: 94.4 us -> 124 us (1.31)
  waiting for transfers between devices: 25.8 us -> 45.1 us
  starting transfers between devices: 40.6 us -> 47.8 us
  Pallas kernels: 24.4 us -> 27.8 us
    ppermute x23 -> x29, waiting for transfers between devices: 20.1 us -> 39.2 us  [swap(): lax.ppermute(x, axis, [p for a, b in pairs for p in ((a, b), (b, a))])]
    ppermute x23 -> x29, starting transfers between devices: 34.9 us -> 42.4 us  [swap(): lax.ppermute(x, axis, [p for a, b in pairs for p in ((a, b), (b, a))])]
    pallas_call x7 -> x14, Pallas kernels: 7.64 us -> 11 us  [the longest x8 5.09 us: last_step(): pl.pallas_call(functools.partial(last_body, first, sent, len(carry)), in_...]
  transfers between devices with their start and end apart: 26 -> 32, of which waited for: 10 -> 15; matrix products, arithmetic and copies ran while one was open for 0% -> 0% of each run, Pallas kernels for 22% -> 17%
where the time goes in v6:
time: 124 us
  starting transfers between devices  47.8 us (39%)
  waiting for transfers between devices  45.1 us (36%)
  Pallas kernels  27.8 us (22%)
  local copies, waits for them, and re-layouts  2.32 us (2%)
    ppermute x29, starting transfers between devices, swap(): lax.ppermute(x, axis, [p for a, b in pairs for p in ((a, b), (b, a))])  42.4 us
    ppermute x29, waiting for transfers between devices, swap(): lax.ppermute(x, axis, [p for a, b in pairs for p in ((a, b), (b, a))])  39.2 us
    pallas_call x6, Pallas kernels, local_step(): pl.pallas_call(functools.partial(local_body, chunk, moment, previous is n...  13.3 us
    ppermute x3, waiting for transfers between devices, coupled(): lax.ppermute(sent[d - 1], 'slab', [(i, i ^ d) for i in range(slabs)])  5.9 us
    ppermute x3, starting transfers between devices, coupled(): lax.ppermute(sent[d - 1], 'slab', [(i, i ^ d) for i in range(slabs)])  5.4 us
    pallas_call x8, Pallas kernels, last_step(): pl.pallas_call(functools.partial(last_body, first, sent, len(carry)), in_...  5.09 us
    pallas_call x4, Pallas kernels, rim_step(): pl.pallas_call(functools.partial(rim_body, first, kind, parts, len(after)...  4.39 us
  transfers between devices with their start and end apart: 32, of which 15 were waited for; matrix products, arithmetic and copies ran while one was open for 0% of the time, Pallas kernels for 17%

profile of v6, /device:TPU:0, one launch (start us, length us, event | category | flops | bytes accessed | tf_op | source)
XLA Modules:
  0.0 124.0 jit_solution(9120597025218814593)
XLA Ops:
  4.5 2.7 %collective-permute-start.1 = (bf16[4,8,48,128]{3,2,1,0:T(8,128)(2,1)S(1)}, bf16[4,8,48,128]{3,2,1,0:T(8,128)(2,1)S(1)}, u32[]{:S(2)}, u32[]{:S(2)}) collective-permute-start(bf16[4,8,48,128]{3,2,1,0:T(8,128)(2,1)S(1)} %get-tuple-element.57), channel_id=1, source_target_pairs={{0,4},{4,0},{8,12},{12,8},{1,5},{5,1},{9,13},{13,9},{2,6},{6,2},{1... | collective-permute-start | bytes 1179656 | tf_op jit(solution)/shard_map/ppermute | solution.py:338
  9.2 2.1 %shard_map.51.refs_0_ = f32[8,8,48,128]{3,2,1,0:T(8,128)S(1)} custom-call(f32[8,8,64,128]{3,2,1,0:T(8,128)S(1)} %get-tuple-element.55.refs_0_.refs_5_, bf16[8,4,48,128]{3,2,1,0:T(8,128)(2,1)S(1)} %collective-permute-done.refs_1_, bf16[8,8,48,256]{3,2,1,0:T(8,128)(2,1)S(1)} %copy-done, f32[64,48]{1,0:T(8,128)S(1)} %bitcast.3, f32[4,64,48]{2,1,0:T(8,128)S(1)} %bitcast.23), custom_call_target="tpu_custom_call" | custom-call | tf_op jit(solution)/shard_map/pallas_call | solution.py:201
  11.3 5.6 %collective-permute-done.1.refs_1_ = bf16[4,8,48,128]{3,2,1,0:T(8,128)(2,1)S(1)} collective-permute-done((bf16[4,8,48,128]{3,2,1,0:T(8,128)(2,1)S(1)}, bf16[4,8,48,128]{3,2,1,0:T(8,128)(2,1)S(1)}, u32[]{:S(2)}, u32[]{:S(2)}) %collective-permute-start.1) | collective-permute-done | bytes 393248 | tf_op jit(solution)/shard_map/ppermute | solution.py:338
  18.1 4.8 %collective-permute-start.7 = (bf16[4,8,48,128]{3,2,1,0:T(8,128)(2,1)S(1)}, bf16[4,8,48,128]{3,2,1,0:T(8,128)(2,1)S(1)}, u32[]{:S(2)}, u32[]{:S(2)}) collective-permute-start(bf16[4,8,48,128]{3,2,1,0:T(8,128)(2,1)S(1)} %get-tuple-element.67), channel_id=1, source_target_pairs={{0,4},{4,0},{8,12},{12,8},{1,5},{5,1},{9,13},{13,9},{2,6},{6,2},{1... | collective-permute-start | bytes 1179656 | tf_op jit(solution)/shard_map/ppermute | solution.py:338
  23.6 2.2 %shard_map.55.refs_0_ = f32[8,8,48,128]{3,2,1,0:T(8,128)S(1)} custom-call(f32[8,8,64,128]{3,2,1,0:T(8,128)S(1)} %get-tuple-element.65.refs_0_.refs_5_, bf16[8,4,48,128]{3,2,1,0:T(8,128)(2,1)S(1)} %collective-permute-done.6.refs_1_, bf16[8,8,48,256]{3,2,1,0:T(8,128)(2,1)S(1)} %copy-done.1, f32[64,48]{1,0:T(8,128)S(1)} %bitcast.5, f32[4,64,48]{2,1,0:T(8,128)S(1)} %bitcast.24), custom_call_target="tpu_custom_call" | custom-call | tf_op jit(solution)/shard_map/pallas_call | solution.py:201
  25.8 2.3 %shard_map.53 = (f32[8,8,48,128]{3,2,1,0:T(8,128)S(1)}, bf16[4,8,48,128]{3,2,1,0:T(8,128)(2,1)S(1)}) custom-call(f32[8,8,64,128]{3,2,1,0:T(8,128)S(1)} %get-tuple-element.59.refs_0_.refs_5_, bf16[8,4,48,128]{3,2,1,0:T(8,128)(2,1)S(1)} %collective-permute-done.3.refs_1_, bf16[8,8,48,256]{3,2,1,0:T(8,128)(2,1)S(1)} %copy-done.1, ...), custom_call_target="tpu_custom_call", output_to_operand_aliasing={{1}: (6, {})} | custom-call | tf_op jit(solution)/shard_map/pallas_call | solution.py:201
  28.1 4.6 %collective-permute-done.7.refs_1_ = bf16[4,8,48,128]{3,2,1,0:T(8,128)(2,1)S(1)} collective-permute-done((bf16[4,8,48,128]{3,2,1,0:T(8,128)(2,1)S(1)}, bf16[4,8,48,128]{3,2,1,0:T(8,128)(2,1)S(1)}, u32[]{:S(2)}, u32[]{:S(2)}) %collective-permute-start.7) | collective-permute-done | bytes 393248 | tf_op jit(solution)/shard_map/ppermute | solution.py:338
  34.5 6.7 %collective-permute-start.4 = (bf16[4,8,48,128]{3,2,1,0:T(8,128)(2,1)S(1)}, bf16[4,8,48,128]{3,2,1,0:T(8,128)(2,1)S(1)}, u32[]{:S(2)}, u32[]{:S(2)}) collective-permute-start(bf16[4,8,48,128]{3,2,1,0:T(8,128)(2,1)S(1)} %get-tuple-element.63), channel_id=1, source_target_pairs={{0,4},{4,0},{8,12},{12,8},{1,5},{5,1},{9,13},{13,9},{2,6},{6,2},{1... | collective-permute-start | bytes 1179656 | tf_op jit(solution)/shard_map/ppermute | solution.py:338
  41.2 2.3 %shard_map.57 = (f32[8,8,48,128]{3,2,1,0:T(8,128)S(1)}, bf16[4,8,48,128]{3,2,1,0:T(8,128)(2,1)S(1)}) custom-call(f32[8,8,64,128]{3,2,1,0:T(8,128)S(1)} %get-tuple-element.69.refs_0_.refs_5_, bf16[8,4,48,128]{3,2,1,0:T(8,128)(2,1)S(1)} %collective-permute-done.9.refs_1_, bf16[8,8,48,256]{3,2,1,0:T(8,128)(2,1)S(1)} %copy-done.1, ...), custom_call_target="tpu_custom_call", output_to_operand_aliasing={{1}: (6, {})} | custom-call | tf_op jit(solution)/shard_map/pallas_call | solution.py:201
  43.4 7.2 %collective-permute-done.4.refs_1_ = bf16[4,8,48,128]{3,2,1,0:T(8,128)(2,1)S(1)} collective-permute-done((bf16[4,8,48,128]{3,2,1,0:T(8,128)(2,1)S(1)}, bf16[4,8,48,128]{3,2,1,0:T(8,128)(2,1)S(1)}, u32[]{:S(2)}, u32[]{:S(2)}) %collective-permute-start.4) | collective-permute-done | bytes 393248 | tf_op jit(solution)/shard_map/ppermute | solution.py:338
  52.5 3.3 %collective-permute-start.14 = (bf16[4,8,48,128]{3,2,1,0:T(8,128)(2,1)S(1)}, bf16[4,8,48,128]{3,2,1,0:T(8,128)(2,1)S(1)}, u32[]{:S(2)}, u32[]{:S(2)}) collective-permute-start(bf16[4,8,48,128]{3,2,1,0:T(8,128)(2,1)S(1)} %get-tuple-element.81), channel_id=1, source_target_pairs={{0,4},{4,0},{8,12},{12,8},{1,5},{5,1},{9,13},{13,9},{2,6},{6,2},{1... | collective-permute-start | bytes 1179656 | tf_op jit(solution)/shard_map/ppermute | solution.py:338
  55.9 2.2 %shard_map.59 = (f32[8,8,48,128]{3,2,1,0:T(8,128)S(1)}, bf16[4,4,48,128]{3,2,1,0:T(8,128)(2,1)S(1)}, bf16[4,4,48,128]{3,2,1,0:T(8,128)(2,1)S(1)}, bf16[4,4,48,128]{3,2,1,0:T(8,128)(2,1)S(1)}) custom-call(f32[8,8,64,128]{3,2,1,0:T(8,128)S(1)} %get-tuple-element.73.refs_0_, ...), custom_call_target="tpu_custom_call", output_to_operand_aliasing={{1}: (6, {}), {2}: (7, {}), {3}: (8, {})} | custom-call | tf_op jit(solution)/shard_map/pallas_call | solution.py:201
  58.1 7.2 %collective-permute-done.14.refs_1_ = bf16[4,8,48,128]{3,2,1,0:T(8,128)(2,1)S(1)} collective-permute-done((bf16[4,8,48,128]{3,2,1,0:T(8,128)(2,1)S(1)}, bf16[4,8,48,128]{3,2,1,0:T(8,128)(2,1)S(1)}, u32[]{:S(2)}, u32[]{:S(2)}) %collective-permute-start.14) | collective-permute-done | bytes 393248 | tf_op jit(solution)/shard_map/ppermute | solution.py:338
  67.2 4.8 %collective-permute-start.17 = (bf16[4,4,48,128]{3,2,1,0:T(8,128)(2,1)S(1)}, bf16[4,4,48,128]{3,2,1,0:T(8,128)(2,1)S(1)}, u32[]{:S(2)}, u32[]{:S(2)}) collective-permute-start(bf16[4,4,48,128]{3,2,1,0:T(8,128)(2,1)S(1)} %get-tuple-element.89), channel_id=1, source_target_pairs={{0,4},{4,0},{8,12},{12,8},{1,5},{5,1},{9,13},{13,9},{2,6},{6,2},{1... | collective-permute-start | bytes 589832 | tf_op jit(solution)/shard_map/ppermute | solution.py:338
  73.4 2.3 %shard_map.63 = (f32[8,8,48,128]{3,2,1,0:T(8,128)S(1)}, bf16[4,4,48,128]{3,2,1,0:T(8,128)(2,1)S(1)}, bf16[4,4,48,128]{3,2,1,0:T(8,128)(2,1)S(1)}, bf16[4,4,48,128]{3,2,1,0:T(8,128)(2,1)S(1)}) custom-call(f32[8,8,64,128]{3,2,1,0:T(8,128)S(1)} %get-tuple-element.83.refs_0_, ...), custom_call_target="tpu_custom_call", output_to_operand_aliasing={{1}: (6, {}), {2}: (7, {}), {3}: (8, {})} | custom-call | tf_op jit(solution)/shard_map/pallas_call | solution.py:201
  75.7 6.5 %collective-permute-start.23 = (bf16[4,4,48,128]{3,2,1,0:T(8,128)(2,1)S(1)}, bf16[4,4,48,128]{3,2,1,0:T(8,128)(2,1)S(1)}, u32[]{:S(2)}, u32[]{:S(2)}) collective-permute-start(bf16[4,4,48,128]{3,2,1,0:T(8,128)(2,1)S(1)} %get-tuple-element.96), channel_id=1, source_target_pairs={{0,4},{4,0},{8,12},{12,8},{1,5},{5,1},{9,13},{13,9},{2,6},{6,2},{1... | collective-permute-start | bytes 589832 | tf_op jit(solution)/shard_map/ppermute | solution.py:338
  84.5 1.6 %collective-permute-start.13 = (bf16[4,4,48,128]{3,2,1,0:T(8,128)(2,1)S(1)}, bf16[4,4,48,128]{3,2,1,0:T(8,128)(2,1)S(1)}, u32[]{:S(2)}, u32[]{:S(2)}) collective-permute-start(bf16[4,4,48,128]{3,2,1,0:T(8,128)(2,1)S(1)} %shard_map.61), channel_id=1, source_target_pairs={{0,2},{2,0},{1,3},{3,1},{4,6},{6,4},{5,7},{7,5},{8,10},{10,8},{9,1... | collective-permute-start | bytes 589832 | tf_op jit(solution)/shard_map/ppermute | solution.py:338
  88.7 1.6 %collective-permute-start.25 = (bf16[4,4,48,128]{3,2,1,0:T(8,128)(2,1)S(1)}, bf16[4,4,48,128]{3,2,1,0:T(8,128)(2,1)S(1)}, u32[]{:S(2)}, u32[]{:S(2)}) collective-permute-start(bf16[4,4,48,128]{3,2,1,0:T(8,128)(2,1)S(1)} %shard_map.69), channel_id=1, source_target_pairs={{0,2},{2,0},{1,3},{3,1},{4,6},{6,4},{5,7},{7,5},{8,10},{10,8},{9,1... | collective-permute-start | bytes 589832 | tf_op jit(solution)/shard_map/ppermute | solution.py:338
  96.6 4.1 %collective-permute-done.25.refs_3_ = bf16[4,4,48,128]{3,2,1,0:T(8,128)(2,1)S(1)} collective-permute-done((bf16[4,4,48,128]{3,2,1,0:T(8,128)(2,1)S(1)}, bf16[4,4,48,128]{3,2,1,0:T(8,128)(2,1)S(1)}, u32[]{:S(2)}, u32[]{:S(2)}) %collective-permute-start.25) | collective-permute-done | bytes 196640 | tf_op jit(solution)/shard_map/ppermute | solution.py:338
  103.6 1.9 %collective-permute-done.26.got_ref = f32[520,256]{1,0:T(8,128)S(1)} collective-permute-done((f32[520,256]{1,0:T(8,128)S(1)}, f32[520,256]{1,0:T(8,128)S(1)}, u32[]{:S(2)}, u32[]{:S(2)}) %collective-permute-start.26) | collective-permute-done | bytes 532512 | tf_op jit(solution)/shard_map/ppermute | solution.py:338
  105.6 4.2 %collective-permute-start.27 = (bf16[144,256]{1,0:T(8,128)(2,1)S(1)}, bf16[144,256]{1,0:T(8,128)(2,1)S(1)}, u32[]{:S(2)}, u32[]{:S(2)}) collective-permute-start(bf16[144,256]{1,0:T(8,128)(2,1)S(1)} %get-tuple-element.103), channel_id=1, source_target_pairs={{0,8},{4,12},{8,0},{12,4},{1,9},{5,13},{9,1},{13,5},{2,10},{6,14},... | collective-permute-start | bytes 221192 | tf_op jit(solution)/shard_map/ppermute | solution.py:553
  111.0 4.3 %collective-permute-done.27.refs_0_ = bf16[144,256]{1,0:T(8,128)(2,1)S(1)} collective-permute-done((bf16[144,256]{1,0:T(8,128)(2,1)S(1)}, bf16[144,256]{1,0:T(8,128)(2,1)S(1)}, u32[]{:S(2)}, u32[]{:S(2)}) %collective-permute-start.27) | collective-permute-done | bytes 73760 | tf_op jit(solution)/shard_map/ppermute | solution.py:553
  116.9 1.6 %collective-permute-start.30 = (bf16[144,256]{1,0:T(8,128)(2,1)S(1)}, bf16[144,256]{1,0:T(8,128)(2,1)S(1)}, u32[]{:S(2)}, u32[]{:S(2)}) collective-permute-start(bf16[144,256]{1,0:T(8,128)(2,1)S(1)} %shard_map.73.mine_ref), channel_id=1, source_target_pairs={{0,2},{2,0},{1,3},{3,1},{4,6},{6,4},{5,7},{7,5},{8,10},{10,8},{9,1... | collective-permute-start | bytes 221192 | tf_op jit(solution)/shard_map/ppermute | solution.py:338
  118.5 2.9 %collective-permute-done.30.other_ref = bf16[144,256]{1,0:T(8,128)(2,1)S(1)} collective-permute-done((bf16[144,256]{1,0:T(8,128)(2,1)S(1)}, bf16[144,256]{1,0:T(8,128)(2,1)S(1)}, u32[]{:S(2)}, u32[]{:S(2)}) %collective-permute-start.30) | collective-permute-done | bytes 73760 | tf_op jit(solution)/shard_map/ppermute | solution.py:338
  (76 shorter events, 34.4 us)
Async XLA Ops:
  4.5 12.4 %collective-permute-start.1 = (bf16[4,8,48,128]{3,2,1,0:T(8,128)(2,1)S(1)}, bf16[4,8,48,128]{3,2,1,0:T(8,128)(2,1)S(1)}, u32[]{:S(2)}, u32[]{:S(2)}) collective-permute-start(bf16[4,8,48,128]{3,2,1,0:T(8,128)(2,1)S(1)} %get-tuple-element.57), channel_id=1, source_target_pairs={{0,4},{4,0},{8,12},{12,8},{1,5},{5,1},{9,13},{13,9},{2,6},{6,2},{1... | collective-permute-start | bytes 1179656 | tf_op jit(solution)/shard_map/ppermute | solution.py:338
  7.2 9.7 %collective-permute-start.2 = (bf16[4,8,48,128]{3,2,1,0:T(8,128)(2,1)S(1)}, bf16[4,8,48,128]{3,2,1,0:T(8,128)(2,1)S(1)}, u32[]{:S(2)}, u32[]{:S(2)}) collective-permute-start(bf16[4,8,48,128]{3,2,1,0:T(8,128)(2,1)S(1)} %get-tuple-element.58), channel_id=1, source_target_pairs={{4,8},{8,4},{5,9},{9,5},{6,10},{10,6},{7,11},{11,7},{20,24},{24,20... | collective-permute-start | bytes 1179656 | tf_op jit(solution)/shard_map/ppermute | solution.py:338
  8.9 14.7 %collective-permute-start.6 = (bf16[8,4,48,128]{3,2,1,0:T(8,128)(2,1)S(1)}, bf16[8,4,48,128]{3,2,1,0:T(8,128)(2,1)S(1)}, u32[]{:S(2)}, u32[]{:S(2)}) collective-permute-start(bf16[8,4,48,128]{3,2,1,0:T(8,128)(2,1)S(1)} %get-tuple-element.66), channel_id=1, source_target_pairs={{0,1},{1,0},{2,3},{3,2},{4,5},{5,4},{6,7},{7,6},{8,9},{9,8},{10,11... | collective-permute-start | bytes 1179656 | tf_op jit(solution)/shard_map/ppermute | solution.py:338
  18.0 7.8 %collective-permute-start.3 = (bf16[8,4,48,128]{3,2,1,0:T(8,128)(2,1)S(1)}, bf16[8,4,48,128]{3,2,1,0:T(8,128)(2,1)S(1)}, u32[]{:S(2)}, u32[]{:S(2)}) collective-permute-start(bf16[8,4,48,128]{3,2,1,0:T(8,128)(2,1)S(1)} %get-tuple-element.60), channel_id=1, source_target_pairs={{0,1},{1,0},{2,3},{3,2},{4,5},{5,4},{6,7},{7,6},{8,9},{9,8},{10,11... | collective-permute-start | bytes 1179656 | tf_op jit(solution)/shard_map/ppermute | solution.py:338
  18.1 14.5 %collective-permute-start.7 = (bf16[4,8,48,128]{3,2,1,0:T(8,128)(2,1)S(1)}, bf16[4,8,48,128]{3,2,1,0:T(8,128)(2,1)S(1)}, u32[]{:S(2)}, u32[]{:S(2)}) collective-permute-start(bf16[4,8,48,128]{3,2,1,0:T(8,128)(2,1)S(1)} %get-tuple-element.67), channel_id=1, source_target_pairs={{0,4},{4,0},{8,12},{12,8},{1,5},{5,1},{9,13},{13,9},{2,6},{6,2},{1... | collective-permute-start | bytes 1179656 | tf_op jit(solution)/shard_map/ppermute | solution.py:338
  22.9 9.7 %collective-permute-start.8 = (bf16[4,8,48,128]{3,2,1,0:T(8,128)(2,1)S(1)}, bf16[4,8,48,128]{3,2,1,0:T(8,128)(2,1)S(1)}, u32[]{:S(2)}, u32[]{:S(2)}) collective-permute-start(bf16[4,8,48,128]{3,2,1,0:T(8,128)(2,1)S(1)} %get-tuple-element.68), channel_id=1, source_target_pairs={{4,8},{8,4},{5,9},{9,5},{6,10},{10,6},{7,11},{11,7},{20,24},{24,20... | collective-permute-start | bytes 1179656 | tf_op jit(solution)/shard_map/ppermute | solution.py:338
  33.7 7.4 %collective-permute-start.9 = (bf16[8,4,48,128]{3,2,1,0:T(8,128)(2,1)S(1)}, bf16[8,4,48,128]{3,2,1,0:T(8,128)(2,1)S(1)}, u32[]{:S(2)}, u32[]{:S(2)}) collective-permute-start(bf16[8,4,48,128]{3,2,1,0:T(8,128)(2,1)S(1)} %get-tuple-element.70), channel_id=1, source_target_pairs={{0,1},{1,0},{2,3},{3,2},{4,5},{5,4},{6,7},{7,6},{8,9},{9,8},{10,11... | collective-permute-start | bytes 1179656 | tf_op jit(solution)/shard_map/ppermute | solution.py:338
  33.8 9.6 %collective-permute-start.5 = (bf16[4,8,48,128]{3,2,1,0:T(8,128)(2,1)S(1)}, bf16[4,8,48,128]{3,2,1,0:T(8,128)(2,1)S(1)}, u32[]{:S(2)}, u32[]{:S(2)}) collective-permute-start(bf16[4,8,48,128]{3,2,1,0:T(8,128)(2,1)S(1)} %get-tuple-element.64), channel_id=1, source_target_pairs={{4,8},{8,4},{5,9},{9,5},{6,10},{10,6},{7,11},{11,7},{20,24},{24,20... | collective-permute-start | bytes 1179656 | tf_op jit(solution)/shard_map/ppermute | solution.py:338
  34.5 16.1 %collective-permute-start.4 = (bf16[4,8,48,128]{3,2,1,0:T(8,128)(2,1)S(1)}, bf16[4,8,48,128]{3,2,1,0:T(8,128)(2,1)S(1)}, u32[]{:S(2)}, u32[]{:S(2)}) collective-permute-start(bf16[4,8,48,128]{3,2,1,0:T(8,128)(2,1)S(1)} %get-tuple-element.63), channel_id=1, source_target_pairs={{0,4},{4,0},{8,12},{12,8},{1,5},{5,1},{9,13},{13,9},{2,6},{6,2},{1... | collective-permute-start | bytes 1179656 | tf_op jit(solution)/shard_map/ppermute | solution.py:338
  52.5 12.8 %collective-permute-start.14 = (bf16[4,8,48,128]{3,2,1,0:T(8,128)(2,1)S(1)}, bf16[4,8,48,128]{3,2,1,0:T(8,128)(2,1)S(1)}, u32[]{:S(2)}, u32[]{:S(2)}) collective-permute-start(bf16[4,8,48,128]{3,2,1,0:T(8,128)(2,1)S(1)} %get-tuple-element.81), channel_id=1, source_target_pairs={{0,4},{4,0},{8,12},{12,8},{1,5},{5,1},{9,13},{13,9},{2,6},{6,2},{1... | collective-permute-start | bytes 1179656 | tf_op jit(solution)/shard_map/ppermute | solution.py:338
  66.5 9.2 %collective-permute-start.18 = (bf16[4,4,48,128]{3,2,1,0:T(8,128)(2,1)S(1)}, bf16[4,4,48,128]{3,2,1,0:T(8,128)(2,1)S(1)}, u32[]{:S(2)}, u32[]{:S(2)}) collective-permute-start(bf16[4,4,48,128]{3,2,1,0:T(8,128)(2,1)S(1)} %get-tuple-element.90), channel_id=1, source_target_pairs={{4,8},{8,4},{5,9},{9,5},{6,10},{10,6},{7,11},{11,7},{20,24},{24,20... | collective-permute-start | bytes 589832 | tf_op jit(solution)/shard_map/ppermute | solution.py:338
  67.2 15.0 %collective-permute-start.17 = (bf16[4,4,48,128]{3,2,1,0:T(8,128)(2,1)S(1)}, bf16[4,4,48,128]{3,2,1,0:T(8,128)(2,1)S(1)}, u32[]{:S(2)}, u32[]{:S(2)}) collective-permute-start(bf16[4,4,48,128]{3,2,1,0:T(8,128)(2,1)S(1)} %get-tuple-element.89), channel_id=1, source_target_pairs={{0,4},{4,0},{8,12},{12,8},{1,5},{5,1},{9,13},{13,9},{2,6},{6,2},{1... | collective-permute-start | bytes 589832 | tf_op jit(solution)/shard_map/ppermute | solution.py:338
  72.0 11.0 %collective-permute-start.11 = (bf16[4,4,48,128]{3,2,1,0:T(8,128)(2,1)S(1)}, bf16[4,4,48,128]{3,2,1,0:T(8,128)(2,1)S(1)}, u32[]{:S(2)}, u32[]{:S(2)}) collective-permute-start(bf16[4,4,48,128]{3,2,1,0:T(8,128)(2,1)S(1)} %get-tuple-element.79), channel_id=1, source_target_pairs={{0,4},{4,0},{8,12},{12,8},{1,5},{5,1},{9,13},{13,9},{2,6},{6,2},{1... | collective-permute-start | bytes 589832 | tf_op jit(solution)/shard_map/ppermute | solution.py:338
  72.1 11.7 %collective-permute-start.12 = (bf16[4,4,48,128]{3,2,1,0:T(8,128)(2,1)S(1)}, bf16[4,4,48,128]{3,2,1,0:T(8,128)(2,1)S(1)}, u32[]{:S(2)}, u32[]{:S(2)}) collective-permute-start(bf16[4,4,48,128]{3,2,1,0:T(8,128)(2,1)S(1)} %get-tuple-element.80), channel_id=1, source_target_pairs={{4,8},{8,4},{5,9},{9,5},{6,10},{10,6},{7,11},{11,7},{20,24},{24,20... | collective-permute-start | bytes 589832 | tf_op jit(solution)/shard_map/ppermute | solution.py:338
  72.7 13.3 %collective-permute-start.24 = (bf16[4,4,48,128]{3,2,1,0:T(8,128)(2,1)S(1)}, bf16[4,4,48,128]{3,2,1,0:T(8,128)(2,1)S(1)}, u32[]{:S(2)}, u32[]{:S(2)}) collective-permute-start(bf16[4,4,48,128]{3,2,1,0:T(8,128)(2,1)S(1)} %get-tuple-element.97), channel_id=1, source_target_pairs={{4,8},{8,4},{5,9},{9,5},{6,10},{10,6},{7,11},{11,7},{20,24},{24,20... | collective-permute-start | bytes 589832 | tf_op jit(solution)/shard_map/ppermute | solution.py:338
  75.7 12.3 %collective-permute-start.23 = (bf16[4,4,48,128]{3,2,1,0:T(8,128)(2,1)S(1)}, bf16[4,4,48,128]{3,2,1,0:T(8,128)(2,1)S(1)}, u32[]{:S(2)}, u32[]{:S(2)}) collective-permute-start(bf16[4,4,48,128]{3,2,1,0:T(8,128)(2,1)S(1)} %get-tuple-element.96), channel_id=1, source_target_pairs={{0,4},{4,0},{8,12},{12,8},{1,5},{5,1},{9,13},{13,9},{2,6},{6,2},{1... | collective-permute-start | bytes 589832 | tf_op jit(solution)/shard_map/ppermute | solution.py:338
  82.8 7.7 %collective-permute-start.19 = (bf16[4,4,48,128]{3,2,1,0:T(8,128)(2,1)S(1)}, bf16[4,4,48,128]{3,2,1,0:T(8,128)(2,1)S(1)}, u32[]{:S(2)}, u32[]{:S(2)}) collective-permute-start(bf16[4,4,48,128]{3,2,1,0:T(8,128)(2,1)S(1)} %get-tuple-element.93), channel_id=1, source_target_pairs={{0,4},{4,0},{8,12},{12,8},{1,5},{5,1},{9,13},{13,9},{2,6},{6,2},{1... | collective-permute-start | bytes 589832 | tf_op jit(solution)/shard_map/ppermute | solution.py:338
  82.9 7.6 %collective-permute-start.20 = (bf16[4,4,48,128]{3,2,1,0:T(8,128)(2,1)S(1)}, bf16[4,4,48,128]{3,2,1,0:T(8,128)(2,1)S(1)}, u32[]{:S(2)}, u32[]{:S(2)}) collective-permute-start(bf16[4,4,48,128]{3,2,1,0:T(8,128)(2,1)S(1)} %get-tuple-element.94), channel_id=1, source_target_pairs={{4,8},{8,4},{5,9},{9,5},{6,10},{10,6},{7,11},{11,7},{20,24},{24,20... | collective-permute-start | bytes 589832 | tf_op jit(solution)/shard_map/ppermute | solution.py:338
  84.5 17.0 %collective-permute-start.13 = (bf16[4,4,48,128]{3,2,1,0:T(8,128)(2,1)S(1)}, bf16[4,4,48,128]{3,2,1,0:T(8,128)(2,1)S(1)}, u32[]{:S(2)}, u32[]{:S(2)}) collective-permute-start(bf16[4,4,48,128]{3,2,1,0:T(8,128)(2,1)S(1)} %shard_map.61), channel_id=1, source_target_pairs={{0,2},{2,0},{1,3},{3,1},{4,6},{6,4},{5,7},{7,5},{8,10},{10,8},{9,1... | collective-permute-start | bytes 589832 | tf_op jit(solution)/shard_map/ppermute | solution.py:338
  86.0 10.6 %collective-permute-start.22 = (bf16[4,4,48,128]{3,2,1,0:T(8,128)(2,1)S(1)}, bf16[4,4,48,128]{3,2,1,0:T(8,128)(2,1)S(1)}, u32[]{:S(2)}, u32[]{:S(2)}) collective-permute-start(bf16[4,4,48,128]{3,2,1,0:T(8,128)(2,1)S(1)} %get-tuple-element.95), channel_id=1, source_target_pairs={{0,2},{2,0},{1,3},{3,1},{4,6},{6,4},{5,7},{7,5},{8,10},{10,8},{9,1... | collective-permute-start | bytes 589832 | tf_op jit(solution)/shard_map/ppermute | solution.py:338
  88.7 12.0 %collective-permute-start.25 = (bf16[4,4,48,128]{3,2,1,0:T(8,128)(2,1)S(1)}, bf16[4,4,48,128]{3,2,1,0:T(8,128)(2,1)S(1)}, u32[]{:S(2)}, u32[]{:S(2)}) collective-permute-start(bf16[4,4,48,128]{3,2,1,0:T(8,128)(2,1)S(1)} %shard_map.69), channel_id=1, source_target_pairs={{0,2},{2,0},{1,3},{3,1},{4,6},{6,4},{5,7},{7,5},{8,10},{10,8},{9,1... | collective-permute-start | bytes 589832 | tf_op jit(solution)/shard_map/ppermute | solution.py:338
  91.2 11.6 %collective-permute-start.21 = (bf16[4,4,48,128]{3,2,1,0:T(8,128)(2,1)S(1)}, bf16[4,4,48,128]{3,2,1,0:T(8,128)(2,1)S(1)}, u32[]{:S(2)}, u32[]{:S(2)}) collective-permute-start(bf16[4,4,48,128]{3,2,1,0:T(8,128)(2,1)S(1)} %shard_map.66), channel_id=1, source_target_pairs={{0,2},{2,0},{1,3},{3,1},{4,6},{6,4},{5,7},{7,5},{8,10},{10,8},{9,1... | collective-permute-start | bytes 589832 | tf_op jit(solution)/shard_map/ppermute | solution.py:338
  105.6 9.7 %collective-permute-start.27 = (bf16[144,256]{1,0:T(8,128)(2,1)S(1)}, bf16[144,256]{1,0:T(8,128)(2,1)S(1)}, u32[]{:S(2)}, u32[]{:S(2)}) collective-permute-start(bf16[144,256]{1,0:T(8,128)(2,1)S(1)} %get-tuple-element.103), channel_id=1, source_target_pairs={{0,8},{4,12},{8,0},{12,4},{1,9},{5,13},{9,1},{13,5},{2,10},{6,14},... | collective-permute-start | bytes 221192 | tf_op jit(solution)/shard_map/ppermute | solution.py:553
  109.8 6.7 %collective-permute-start.28 = (bf16[144,256]{1,0:T(8,128)(2,1)S(1)}, bf16[144,256]{1,0:T(8,128)(2,1)S(1)}, u32[]{:S(2)}, u32[]{:S(2)}) collective-permute-start(bf16[144,256]{1,0:T(8,128)(2,1)S(1)} %get-tuple-element.104), channel_id=1, source_target_pairs={{0,12},{4,8},{8,4},{12,0},{1,13},{5,9},{9,5},{13,1},{2,14},{6,10},... | collective-permute-start | bytes 221192 | tf_op jit(solution)/shard_map/ppermute | solution.py:553
  (13 other events, 68.6 us)

commit v7 on v5

v7 whole, which is shorter than its diff:
```python
import functools
import math

import jax
import jax.numpy as jnp
from jax import lax
from jax.experimental import pallas as pl
from jax.experimental.pallas import tpu as pltpu
from jax.sharding import PartitionSpec as P

COEFFICIENTS = (-205.0 / 72.0, 8.0 / 5.0, -1.0 / 5.0, 8.0 / 315.0, -1.0 / 560.0)
EPSILON = 1e-06
LANES = 128
RADIUS = 4
EDGE = 8
TILE = 16
F32 = jnp.float32
BF16 = jnp.bfloat16
VMEM_LIMIT = 32 * 1024 * 1024


def params(*semantics):
    return pltpu.CompilerParams(
        dimension_semantics=semantics or None, vmem_limit_bytes=VMEM_LIMIT
    )


def whole_vmem(count):
    return [pl.BlockSpec(memory_space=pltpu.VMEM)] * count


def shape_of(depth, across, along, dtype):
    return jax.ShapeDtypeStruct((depth, across, along, LANES), dtype)


def turned(field, scratch):
    rows, along = field.shape
    scratch[:rows, :along] = field
    return jnp.transpose(scratch[...])


def lane(values, n):
    return jnp.broadcast_to(values[:, n : n + 1], (values.shape[0], LANES))


def store_edges(x, span, news, even, even_ref, odd_ref):
    for j in range(RADIUS):
        low = news[j].astype(BF16)
        high = news[len(news) - RADIUS + j].astype(BF16)
        even_ref[j, x, span] = jnp.where(even, high, low)
        odd_ref[j, x, span] = jnp.where(even, low, high)


def store_beside(span, rows, core, u_ref, edge_ref):
    depth, across, _, _ = u_ref.shape
    first = (across - RADIUS) * (1 - core)
    for z in range(depth):
        for j in range(RADIUS):
            edge_ref[z, j, span] = u_ref[z, first + j, rows].astype(BF16)


def slab_is_even():
    return lax.rem(lax.axis_index("slab"), 2) == 0


def clear_pads(u_ref):
    depth, across, padded, _ = u_ref.shape

    def plane(z, _):
        blank = jnp.zeros((across, EDGE, LANES), F32)
        u_ref[z, :, pl.ds(0, EDGE)] = blank
        u_ref[z, :, pl.ds(padded - EDGE, EDGE)] = blank
        return 0

    lax.fori_loop(0, depth, plane, 0)


def tiles(along, body):
    def one(t, _):
        body(pl.multiple_of(t * TILE, TILE))
        return 0

    lax.fori_loop(0, along // TILE, one, 0)


def first_body(chunk, p_ref, s_ref, u_ref, even_ref, odd_ref, edge_ref, square, turned_s):
    depth, across, padded, _ = u_ref.shape
    along = padded - 2 * EDGE
    core = lax.axis_index("sub")
    even = slab_is_even()
    turned_s[...] = turned(s_ref[0], square)
    clear_pads(u_ref)

    def tile(start):
        span = pl.ds(start, TILE)
        rows = pl.ds(start + EDGE, TILE)
        source = turned_s[span]
        for x in range(across):
            news = []
            for z in range(depth):
                p = p_ref[z, x, span, chunk * LANES : (chunk + 1) * LANES].astype(F32)
                new = lane(source, z * across + x) * p
                u_ref[z, x, rows] = new
                news.append(new)
            store_edges(x, span, news, even, even_ref, odd_ref)
        store_beside(span, rows, core, u_ref, edge_ref)

    tiles(along, tile)


def square_scratch():
    return [pltpu.VMEM((LANES, LANES), F32)] * 2


def first_field(probes, chunk, source):
    depth, across, along, _ = probes.shape
    return pl.pallas_call(
        functools.partial(first_body, chunk),
        in_specs=whole_vmem(2),
        out_specs=whole_vmem(4),
        out_shape=[
            shape_of(depth, across, along + 2 * EDGE, F32),
            shape_of(RADIUS, across, along, BF16),
            shape_of(RADIUS, across, along, BF16),
            shape_of(depth, RADIUS, along, BF16),
        ],
        scratch_shapes=square_scratch(),
        compiler_params=params(),
    )(probes, source)


def local_body(chunk, moment, has_previous, *refs):
    refs = list(refs)
    u_ref, beside_ref, p_ref, c_ref, s_ref = refs[:5]
    prev_ref = refs[5] if has_previous else None
    base_ref, square, turned_c, turned_s = refs[-4:]
    depth, across, along, _ = base_ref.shape
    core = lax.axis_index("sub")
    left_on = (core == 1).astype(F32)
    right_on = (core == 0).astype(F32)
    turned_c[...] = turned(c_ref[...], square)
    turned_s[...] = turned(s_ref[moment], square)

    def tile(start):
        span = pl.ds(start, TILE)
        rows = start + EDGE
        courant = turned_c[span]
        source = turned_s[span]
        for z in range(depth):
            beside = [beside_ref[z, j, span].astype(F32) for j in range(RADIUS)]
            row = [v * left_on for v in beside]
            row += [u_ref[z, x, pl.ds(rows, TILE)] for x in range(across)]
            row += [v * right_on for v in beside]
            for x in range(across):
                here = row[RADIUS + x]
                total = (3.0 * COEFFICIENTS[0]) * here
                for r in range(1, RADIUS + 1):
                    near = row[RADIUS + x + r] + row[RADIUS + x - r]
                    near = near + (
                        u_ref[z, x, pl.ds(rows + r, TILE)] + u_ref[z, x, pl.ds(rows - r, TILE)]
                    )
                    if z + r < depth:
                        near = near + u_ref[z + r, x, pl.ds(rows, TILE)]
                    if z - r >= 0:
                        near = near + u_ref[z - r, x, pl.ds(rows, TILE)]
                    total = total + COEFFICIENTS[r] * near
                cell = z * across + x
                p = p_ref[z, x, span, chunk * LANES : (chunk + 1) * LANES].astype(F32)
                new = 2.0 * here
                if has_previous:
                    new = new - prev_ref[z, x, pl.ds(rows, TILE)]
                new = new + lane(courant, cell) * total + lane(source, cell) * p
                base_ref[z, x, span] = new

    tiles(along, tile)


def local_step(u, beside, probes, chunk, courant, source, moment, previous):
    depth, across, along, _ = probes.shape
    operands = [u, beside, probes, courant, source]
    if previous is not None:
        operands.append(previous)
    return pl.pallas_call(
        functools.partial(local_body, chunk, moment, previous is not None),
        in_specs=whole_vmem(len(operands)),
        out_specs=whole_vmem(1)[0],
        out_shape=shape_of(depth, across, along, F32),
        scratch_shapes=square_scratch() + square_scratch()[:1],
        compiler_params=params(),
    )(*operands)


def rim_body(middle, *refs):
    base_ref, even_ref, odd_ref, c_ref = refs[:4]
    outs, (square, turned_c) = refs[4:-2], refs[-2:]
    depth, across, along, _ = base_ref.shape
    core = lax.axis_index("sub")
    even = slab_is_even()
    turned_c[...] = turned(c_ref[...], square)
    if middle:
        clear_pads(outs[0])

    def tile(start):
        span = pl.ds(start, TILE)
        rows = pl.ds(start + EDGE, TILE)
        courant = turned_c[span]
        for x in range(across):
            below, above = [], []
            for j in range(RADIUS):
                one, two = even_ref[j, x, span], odd_ref[j, x, span]
                below.append(jnp.where(even, two, one).astype(F32))
                above.append(jnp.where(even, one, two).astype(F32))
            news = []
            for z in range(depth):
                added = None
                for r in range(1, RADIUS + 1):
                    if z - r < 0:
                        term = COEFFICIENTS[r] * below[RADIUS + z - r]
                        added = term if added is None else added + term
                    if z + r >= depth:
                        term = COEFFICIENTS[r] * above[z + r - depth]
                        added = term if added is None else added + term
                new = base_ref[z, x, span]
                if added is not None:
                    new = new + lane(courant, z * across + x) * added
                news.append(new)
            if middle:
                for z, new in enumerate(news):
                    outs[0][z, x, rows] = new
                store_edges(x, span, news, even, outs[1], outs[2])
            else:
                for z, new in enumerate(news):
                    outs[0][z, x, span] = new.astype(BF16)
        if middle:
            store_beside(span, rows, core, outs[0], outs[3])

    tiles(along, tile)


def rim_step(base, evens, odds, courant, middle):
    depth, across, along, _ = base.shape
    if middle:
        out_shape = [
            shape_of(depth, across, along + 2 * EDGE, F32),
            shape_of(RADIUS, across, along, BF16),
            shape_of(RADIUS, across, along, BF16),
            shape_of(depth, RADIUS, along, BF16),
        ]
    else:
        out_shape = [shape_of(depth, across, along, BF16)]
    return pl.pallas_call(
        functools.partial(rim_body, middle),
        in_specs=whole_vmem(4),
        out_specs=whole_vmem(len(out_shape)),
        out_shape=out_shape,
        scratch_shapes=square_scratch(),
        compiler_params=params(),
    )(base, evens, odds, courant)


def last_body(sent, base_ref, even_ref, odd_ref, c_ref, out_ref, square, turned_c):
    depth, across, along, _ = base_ref.shape
    chip = lax.axis_index("probe")
    low = (chip == 1) if sent else (chip == 0)
    from_odd = low == slab_is_even()
    turned_c[...] = turned(c_ref[...], square)

    def tile(start):
        span = pl.ds(start, TILE)
        courant = turned_c[span]
        for x in range(across):
            near = []
            for j in range(RADIUS):
                at = jnp.where(low, RADIUS - 1 - j, j)
                near.append(
                    jnp.where(from_odd, odd_ref[at, x, span], even_ref[at, x, span]).astype(F32)
                )
            for m in range(RADIUS):
                mirror = depth - 1 - m
                added = COEFFICIENTS[m + 1] * near[0]
                for r in range(m + 2, RADIUS + 1):
                    added = added + COEFFICIENTS[r] * near[r - m - 1]
                scale = jnp.where(
                    low, lane(courant, m * across + x), lane(courant, mirror * across + x)
                )
                new = base_ref[jnp.where(low, m, mirror), x, span] + scale * added
                out_ref[m, x, span] = new.astype(BF16)

    tiles(along, tile)


def last_step(base, evens, odds, courant, sent):
    _, across, along, _ = base.shape
    return pl.pallas_call(
        functools.partial(last_body, sent),
        in_specs=whole_vmem(4),
        out_specs=whole_vmem(1)[0],
        out_shape=shape_of(RADIUS, across, along, BF16),
        scratch_shapes=square_scratch(),
        compiler_params=params(),
    )(base, evens, odds, courant)


def swap(x, axis, pairs):
    return lax.ppermute(x, axis, [p for a, b in pairs for p in ((a, b), (b, a))])


def even_swap(x):
    return swap(x, "slab", [(i, i + 1) for i in range(0, lax.axis_size("slab") - 1, 2)])


def odd_swap(x):
    return swap(x, "slab", [(i, i + 1) for i in range(1, lax.axis_size("slab") - 1, 2)])


def core_swap(x):
    return swap(x, "sub", [(0, 1)])


def chip_swap(x):
    return swap(x, "probe", [(0, 1)])


def product(a, b):
    return lax.dot_general(a, b, (((0,), (0,)), ((), ())), preferred_element_type=F32)


def block_of(array, i, j):
    return array[i * LANES : (i + 1) * LANES, j * LANES : (j + 1) * LANES]


def eye():
    rows = lax.broadcasted_iota(jnp.int32, (LANES, LANES), 0)
    cols = lax.broadcasted_iota(jnp.int32, (LANES, LANES), 1)
    return rows == cols


def inner_body(kept0, sent0, kept1, sent1, keep_ref, send_ref, diag_ref, panel):
    half = panel.shape[0] // 2
    for n, (kept, sent) in enumerate(((kept0, sent0), (kept1, sent1))):
        columns = slice(n * LANES, (n + 1) * LANES)
        panel[:half, columns] = kept[...].reshape(half, LANES)
        panel[half:, columns] = sent[...].reshape(half, LANES)
    core = lax.axis_index("sub")
    whole = product(panel[...], panel[...])
    first, second = whole[:, :LANES], whole[:, LANES:]
    keep_ref[...] = jnp.where(core == 0, first, second)
    send_ref[...] = jnp.where(core == 0, second, first)
    diag = [
        jnp.sum(jnp.where(eye(), block_of(whole, n, n), 0.0), axis=0, keepdims=True)
        for n in range(2)
    ]
    none = jnp.zeros_like(diag[0])
    chip = lax.axis_index("probe")
    rows = [jnp.where(chip == n // 2, diag[n % 2], none) for n in range(4)]
    diag_ref[...] = jnp.concatenate(rows + [none] * 4, axis=0)


def inner_gram(fields):
    size = 2 * LANES
    cells = 2 * math.prod(fields[0].shape[:3])
    half = jax.ShapeDtypeStruct((size, LANES), F32)
    return pl.pallas_call(
        inner_body,
        in_specs=whole_vmem(4),
        out_specs=whole_vmem(3),
        out_shape=[half, half, jax.ShapeDtypeStruct((8, LANES), F32)],
        scratch_shapes=[pltpu.VMEM((cells, size), BF16)],
        compiler_params=params(),
    )(*fields)


def inner_rows_body(keep_ref, got_ref, *outs):
    slab = lax.axis_index("slab")
    chip = lax.axis_index("probe")
    for d, out in enumerate(outs):
        row = jnp.clip((slab ^ d) - 2 * chip, 0, 1)
        span = pl.ds(pl.multiple_of(row * LANES, LANES), LANES)
        out[...] = keep_ref[span] + got_ref[span]


def inner_rows(keep, got, slabs):
    block = jax.ShapeDtypeStruct((LANES, LANES), F32)
    return pl.pallas_call(
        inner_rows_body,
        in_specs=whole_vmem(2),
        out_specs=whole_vmem(slabs),
        out_shape=[block] * slabs,
        compiler_params=params(),
    )(keep, got)


def cross_body(kept0, got0, kept1, got1, keep_ref, send_ref, panel):
    chip = lax.axis_index("probe")
    core = lax.axis_index("sub")
    cells = panel.shape[0]
    for n, (kept, got) in enumerate(((kept0, got0), (kept1, got1))):
        mine = pl.multiple_of((chip * 2 + n) * LANES, LANES)
        other = pl.multiple_of(((1 - chip) * 2 + n) * LANES, LANES)
        panel[:, pl.ds(mine, LANES)] = kept[...].reshape(cells, LANES)
        panel[:, pl.ds(other, LANES)] = got[...].reshape(cells, LANES)
    whole = product(panel[:, : 2 * LANES], panel[:, 2 * LANES :])
    for ref, which in ((keep_ref, core), (send_ref, 1 - core)):
        here = which == 0
        ref[:LANES] = jnp.where(here, block_of(whole, 0, 0), block_of(whole, 0, 1))
        ref[LANES : 2 * LANES] = jnp.where(here, block_of(whole, 1, 0), block_of(whole, 1, 1))
        mixed = jnp.where(here, block_of(whole, 0, 1), block_of(whole, 1, 0))
        ref[2 * LANES :] = mixed


def cross_gram(fields):
    cells = math.prod(fields[0].shape[:3])
    three = jax.ShapeDtypeStruct((3 * LANES, LANES), F32)
    return pl.pallas_call(
        cross_body,
        in_specs=whole_vmem(4),
        out_specs=whole_vmem(2),
        out_shape=[three, three],
        scratch_shapes=[pltpu.VMEM((cells, 4 * LANES), BF16)],
        compiler_params=params(),
    )(*fields)


def rounded(ref, block, tail):
    count = block.shape[0]
    high = tail.astype(BF16)
    low = tail - high.astype(F32)
    ref[:count] = block.astype(BF16)
    ref[count : count + 16] = jnp.concatenate([high.astype(F32), low], axis=0).astype(BF16)


def opened(ref, count):
    tail = ref[count : count + 16].astype(F32)
    return ref[:count].astype(F32), tail[:8] + tail[8:]


def cross_rows_body(keep_ref, got_ref, diag_ref, other_diag_ref, own_ref, *outs):
    slab = lax.axis_index("slab")
    core = lax.axis_index("sub")
    tail = diag_ref[...] + other_diag_ref[...]
    for d in range(len(outs) + 1):
        owner = slab ^ d
        late = jnp.where(core == 0, jnp.where(owner == 2, 0, 2), jnp.where(owner == 2, 2, 1))
        at = jnp.where(owner < 2, owner, late)
        span = pl.ds(pl.multiple_of(at * LANES, LANES), LANES)
        block = keep_ref[span] + got_ref[span]
        if d == 0:
            own_ref[:LANES] = block
            own_ref[LANES:] = tail
        else:
            rounded(outs[d - 1], block, tail)


def cross_rows(keep, got, diag, other_diag, slabs):
    own = jax.ShapeDtypeStruct((LANES + 8, LANES), F32)
    sent = jax.ShapeDtypeStruct((LANES + 16, LANES), BF16)
    return pl.pallas_call(
        cross_rows_body,
        in_specs=whole_vmem(4),
        out_specs=whole_vmem(slabs),
        out_shape=[own] + [sent] * (slabs - 1),
        compiler_params=params(),
    )(keep, got, diag, other_diag)


def sum_body(slabs, own_ref, *refs):
    block, tail = own_ref[:LANES], own_ref[LANES:]
    for ref in refs[: slabs - 1]:
        more, more_tail = opened(ref, LANES)
        block, tail = block + more, tail + more_tail
    inner = refs[slabs - 1][...]
    for ref in refs[slabs : 2 * slabs - 1]:
        inner = inner + ref[...]
    out_ref = refs[-1]
    rounded(out_ref, block, tail)
    out_ref[LANES + 16 :] = inner.astype(BF16)


def sum_all(own, others, inner, inner_others):
    slabs = 1 + len(others)
    return pl.pallas_call(
        functools.partial(sum_body, slabs),
        in_specs=whole_vmem(2 * slabs),
        out_specs=whole_vmem(1)[0],
        out_shape=jax.ShapeDtypeStruct((2 * LANES + 16, LANES), BF16),
        compiler_params=params(),
    )(own, *others, inner, *inner_others)


def normalise_body(cell_count, mine_ref, other_ref, out_ref, norms_ref):
    slab = lax.axis_index("slab")
    core = lax.axis_index("sub")
    chip = lax.axis_index("probe")
    one, one_tail = opened(mine_ref, LANES)
    two, two_tail = opened(other_ref, LANES)
    cross = one + two
    inner_span = pl.ds(LANES + 16, LANES)
    inner = jnp.where(slab // 2 == chip, mine_ref[inner_span], other_ref[inner_span]).astype(F32)
    upper = slab < 2
    values = [jnp.where(upper, inner, cross.T), jnp.where(upper, cross, inner)]
    norms = jnp.sqrt((one_tail + two_tail) / cell_count + EPSILON)
    blocks = [norms[n : n + 1] for n in range(4)]
    own = blocks[0]
    for n in range(1, 4):
        own = jnp.where(slab == n, blocks[n], own)
    norms_ref[...] = own
    own_column = jnp.sum(
        jnp.where(eye(), jnp.broadcast_to(own, (LANES, LANES)), 0.0), axis=1, keepdims=True
    )
    for side in range(2):
        others = jnp.where(core == 0, blocks[2 * side], blocks[2 * side + 1])
        value = values[side] / math.sqrt(cell_count) / (own_column * others)
        value = jnp.where(eye() & (2 * side + core == slab), 0.0, value)
        out_ref[:, side * LANES : (side + 1) * LANES] = value


def normalise(mine, other, cell_count):
    return pl.pallas_call(
        functools.partial(normalise_body, cell_count),
        in_specs=whole_vmem(2),
        out_specs=whole_vmem(2),
        out_shape=[
            jax.ShapeDtypeStruct((LANES, 2 * LANES), F32),
            jax.ShapeDtypeStruct((1, LANES), F32),
        ],
        compiler_params=params(),
    )(mine, other)


def assemble_body(near_ref, far_ref, out_ref):
    core = lax.axis_index("sub")
    for side in range(2):
        columns = slice(side * LANES, (side + 1) * LANES)
        for ref, which in ((near_ref, core), (far_ref, 1 - core)):
            start = pl.multiple_of((2 * side + which) * LANES, LANES)
            out_ref[:, pl.ds(start, LANES)] = ref[:, columns]


def assemble(near, far):
    return pl.pallas_call(
        assemble_body,
        in_specs=whole_vmem(2),
        out_specs=whole_vmem(1)[0],
        out_shape=jax.ShapeDtypeStruct((near.shape[0], 4 * LANES), F32),
        compiler_params=params(),
    )(near, far)


def coupled(finals, cell_count):
    slabs = 4
    own = [field for kept, sent, _ in finals for field in (kept, sent)]
    keep, send, diag = inner_gram(own)
    inner = inner_rows(keep, core_swap(send), slabs)
    other_diag = core_swap(diag)
    inner_arrived = []
    for d in (2, 3, 1):
        pairs = [
            (2 * (k ^ d) + chip, 2 * k + chip)
            for chip in range(2)
            for k in (2 * chip, 2 * chip + 1)
        ]
        inner_arrived.append(lax.ppermute(inner[d], ("slab", "probe"), pairs))

    keep, send = cross_gram([field for kept, _, got in finals for field in (kept, got)])
    mine, *blocks = cross_rows(keep, core_swap(send), diag, other_diag, slabs)
    arrived = [
        lax.ppermute(blocks[d - 1], "slab", [(i, i ^ d) for i in range(slabs)])
        for d in (2, 3, 1)
    ]
    total = sum_all(mine, arrived, inner[0], inner_arrived)
    near, norms = normalise(total, chip_swap(total), cell_count)
    return assemble(near, core_swap(near)), norms.reshape(-1)


def coupled_general(fields, cell_count):
    chips = lax.axis_size("probe")
    sketch = jnp.concatenate(fields, axis=-1)
    sketch = sketch.reshape(-1, sketch.shape[-1])
    if chips > 1:
        sketch = lax.all_to_all(sketch, "probe", split_axis=0, concat_axis=1, tiled=True)
    partial_gram = lax.dot_general(
        sketch, sketch, (((0,), (0,)), ((), ())), preferred_element_type=F32
    )
    rows = lax.psum_scatter(partial_gram, "slab", scatter_dimension=0, tiled=True)
    rows = lax.psum(rows, ("probe", "sub"))
    count = rows.shape[0]
    start = lax.axis_index("slab") * count
    own = jnp.diagonal(lax.dynamic_slice_in_dim(rows, start, count, 1))
    own_norms = jnp.sqrt(own / cell_count + EPSILON)
    norms = lax.all_gather(own_norms, "slab", axis=0, tiled=True)
    coupling = rows / math.sqrt(cell_count) / (own_norms[:, None] * norms[None, :])
    row_ids = start + lax.broadcasted_iota(jnp.int32, coupling.shape, 0)
    col_ids = lax.broadcasted_iota(jnp.int32, coupling.shape, 1)
    return jnp.where(row_ids == col_ids, 0.0, coupling), own_norms


def shards(probes, courant, source):
    depth, across, along, count = probes.shape
    chunks = count // LANES
    slabs, chips = lax.axis_size("slab"), lax.axis_size("probe")
    cell_count = depth * across * along * slabs * lax.axis_size("sub")
    paired = chips == 2 and slabs == 4 and chunks == 2 and depth == 2 * RADIUS
    steps = source.shape[0]
    courant = courant.reshape(depth * across, along)
    source = source.reshape(steps, depth * across, along)

    exchange = lambda even, odd, edge: (even_swap(even), odd_swap(odd), core_swap(edge))
    now, previous, halos = [], [None] * chunks, []
    for c in range(chunks):
        u, *edges = first_field(probes, c, source)
        now.append(u)
        halos.append(exchange(*edges))
    finals = []
    for n in range(1, steps):
        for c in range(chunks):
            even, odd, beside = halos[c]
            base = local_step(now[c], beside, probes, c, courant, source, n, previous[c])
            if n < steps - 1:
                u, *edges = rim_step(base, even, odd, courant, True)
                previous[c], now[c] = now[c], u
                halos[c] = exchange(*edges)
            elif paired:
                sent = last_step(base, even, odd, courant, True)
                kept = last_step(base, even, odd, courant, False)
                finals.append((kept, sent, chip_swap(sent)))
            else:
                finals += rim_step(base, even, odd, courant, False)
    return (coupled if paired else coupled_general)(finals, cell_count)


def solution(mesh):
    placed = (
        P(("groups", "slab"), "sub", None, "probe"),
        P("slab", "sub", None),
        P(None, ("groups", "slab"), "sub", None),
    )
    return jax.shard_map(
        shards,
        mesh=mesh,
        in_specs=placed,
        out_specs=(P(("groups", "slab"), None), P(("groups", "slab"))),
        check_vma=False,
    )
```

time: 94.4 us -> 98.8 us (1.047)
  starting transfers between devices: 40.6 us -> 47.4 us
  waiting for transfers between devices: 25.8 us -> 21.1 us
  Pallas kernels: 24.4 us -> 26.6 us
    ppermute x3 -> x6, starting transfers between devices: 5.72 us -> 11.4 us  [the longest x3 7.8 us: coupled(): inner_arrived.append(lax.ppermute(inner[d], ('slab', 'probe'), pairs))]
    ppermute x3 -> x6, waiting for transfers between devices: 5.67 us -> 3.24 us  [the longest x3 3.23 us: coupled(): lax.ppermute(blocks[d - 1], 'slab', [(i, i ^ d) for i in range(slabs)])]
    ppermute x23 -> x25, waiting for transfers between devices: 20.1 us -> 17.9 us  [swap(): lax.ppermute(x, axis, [p for a, b in pairs for p in ((a, b), (b, a))])]
    pallas_call x9 -> x13, Pallas kernels: 7.74 us -> 9.88 us  [the longest x4 4.4 us: rim_step(): pl.pallas_call(functools.partial(rim_body, middle), in_specs=whole_vmem(4...]
    ppermute x23 -> x25, starting transfers between devices: 34.9 us -> 36.1 us  [swap(): lax.ppermute(x, axis, [p for a, b in pairs for p in ((a, b), (b, a))])]
  transfers between devices with their start and end apart: 26 -> 31, of which waited for: 10 -> 10; matrix products, arithmetic and copies ran while one was open for 0% -> 0% of each run, Pallas kernels for 22% -> 24%
where the time goes in v7:
time: 98.8 us; the launch traced here: 98.4 us
  starting transfers between devices  47.4 us (48%)
  Pallas kernels  26.6 us (27%)
  waiting for transfers between devices  21.1 us (21%)
  local copies, waits for them, and re-layouts  2.32 us (2%)
  between operations  1 us (1%)
    ppermute x25, starting transfers between devices, swap(): lax.ppermute(x, axis, [p for a, b in pairs for p in ((a, b), (b, a))])  36.1 us
    ppermute x25, waiting for transfers between devices, swap(): lax.ppermute(x, axis, [p for a, b in pairs for p in ((a, b), (b, a))])  17.9 us
    pallas_call x6, Pallas kernels, local_step(): pl.pallas_call(functools.partial(local_body, chunk, moment, previous is n...  13.3 us
    ppermute x3, starting transfers between devices, coupled(): inner_arrived.append(lax.ppermute(inner[d], ('slab', 'probe'), pairs))  7.8 us
    pallas_call x4, Pallas kernels, rim_step(): pl.pallas_call(functools.partial(rim_body, middle), in_specs=whole_vmem(4...  4.4 us
    pallas_call x4, Pallas kernels, last_step(): pl.pallas_call(functools.partial(last_body, sent), in_specs=whole_vmem(4)...  3.82 us
    ppermute x3, starting transfers between devices, coupled(): lax.ppermute(blocks[d - 1], 'slab', [(i, i ^ d) for i in range(slabs)])  3.55 us
    ppermute x3, waiting for transfers between devices, coupled(): lax.ppermute(blocks[d - 1], 'slab', [(i, i ^ d) for i in range(slabs)])  3.23 us
  transfers between devices with their start and end apart: 31, of which 10 were waited for; matrix products, arithmetic and copies ran while one was open for 0% of the time, Pallas kernels for 24%

profile of v7, /device:TPU:0, one launch (start us, length us, event | category | flops | bytes accessed | tf_op | source)
XLA Modules:
  0.0 98.4 jit_solution(9655568483739638001)
XLA Ops:
  0.6 1.4 %copy-done = bf16[8,8,48,256]{3,2,1,0:T(8,128)(2,1)S(1)} copy-done((bf16[8,8,48,256]{3,2,1,0:T(8,128)(2,1)S(1)}, bf16[8,8,48,256]{3,2,1,0:T(8,128)(2,1)}, u32[]{:S(2)}) %copy-start) | copy-done | bytes 1572888
  4.5 2.7 %collective-permute-start.11 = (bf16[4,8,48,128]{3,2,1,0:T(8,128)(2,1)S(1)}, bf16[4,8,48,128]{3,2,1,0:T(8,128)(2,1)S(1)}, u32[]{:S(2)}, u32[]{:S(2)}) collective-permute-start(bf16[4,8,48,128]{3,2,1,0:T(8,128)(2,1)S(1)} %get-tuple-element.55), channel_id=1, source_target_pairs={{0,4},{4,0},{8,12},{12,8},{1,5},{5,1},{9,13},{13,9},{2,6},{6,2},{1... | collective-permute-start | bytes 1179656 | tf_op jit(solution)/shard_map/ppermute | solution.py:305
  9.1 4.3 %collective-permute-start.1 = (bf16[4,8,48,128]{3,2,1,0:T(8,128)(2,1)S(1)}, bf16[4,8,48,128]{3,2,1,0:T(8,128)(2,1)S(1)}, u32[]{:S(2)}, u32[]{:S(2)}) collective-permute-start(bf16[4,8,48,128]{3,2,1,0:T(8,128)(2,1)S(1)} %get-tuple-element.43), channel_id=1, source_target_pairs={{0,4},{4,0},{8,12},{12,8},{1,5},{5,1},{9,13},{13,9},{2,6},{6,2},{1... | collective-permute-start | bytes 1179656 | tf_op jit(solution)/shard_map/ppermute | solution.py:305
  14.1 2.2 %shard_map.59.refs_0_ = f32[8,8,48,128]{3,2,1,0:T(8,128)S(1)} custom-call(f32[8,8,64,128]{3,2,1,0:T(8,128)S(1)} %get-tuple-element.53.refs_0_.refs_5_, bf16[8,4,48,128]{3,2,1,0:T(8,128)(2,1)S(1)} %collective-permute-done.10.refs_1_, bf16[8,8,48,256]{3,2,1,0:T(8,128)(2,1)S(1)} %copy-done, f32[64,48]{1,0:T(8,128)S(1)} %bitcast.11, f32[4,64,48]{2,1,0:T(8,128)S(1)} %bitcast.5), custom_call_target="tpu_custom_call" | custom-call | tf_op jit(solution)/shard_map/pallas_call | solution.py:183
  18.3 5.0 %collective-permute-start.14 = (bf16[4,8,48,128]{3,2,1,0:T(8,128)(2,1)S(1)}, bf16[4,8,48,128]{3,2,1,0:T(8,128)(2,1)S(1)}, u32[]{:S(2)}, u32[]{:S(2)}) collective-permute-start(bf16[4,8,48,128]{3,2,1,0:T(8,128)(2,1)S(1)} %get-tuple-element.59), channel_id=1, source_target_pairs={{0,4},{4,0},{8,12},{12,8},{1,5},{5,1},{9,13},{13,9},{2,6},{6,2},{1... | collective-permute-start | bytes 1179656 | tf_op jit(solution)/shard_map/ppermute | solution.py:305
  24.1 2.1 %shard_map.51.refs_0_ = f32[8,8,48,128]{3,2,1,0:T(8,128)S(1)} custom-call(f32[8,8,64,128]{3,2,1,0:T(8,128)S(1)} %get-tuple-element.41.refs_0_.refs_5_, bf16[8,4,48,128]{3,2,1,0:T(8,128)(2,1)S(1)} %collective-permute-done.refs_1_, bf16[8,8,48,256]{3,2,1,0:T(8,128)(2,1)S(1)} %copy-done.1, f32[64,48]{1,0:T(8,128)S(1)} %bitcast.13, f32[4,64,48]{2,1,0:T(8,128)S(1)} %bitcast.6), custom_call_target="tpu_custom_call" | custom-call | tf_op jit(solution)/shard_map/pallas_call | solution.py:183
  27.6 4.2 %collective-permute-start.4 = (bf16[4,8,48,128]{3,2,1,0:T(8,128)(2,1)S(1)}, bf16[4,8,48,128]{3,2,1,0:T(8,128)(2,1)S(1)}, u32[]{:S(2)}, u32[]{:S(2)}) collective-permute-start(bf16[4,8,48,128]{3,2,1,0:T(8,128)(2,1)S(1)} %get-tuple-element.47), channel_id=1, source_target_pairs={{0,4},{4,0},{8,12},{12,8},{1,5},{5,1},{9,13},{13,9},{2,6},{6,2},{1... | collective-permute-start | bytes 1179656 | tf_op jit(solution)/shard_map/ppermute | solution.py:305
  32.5 2.3 %shard_map.61.refs_0_ = f32[8,8,48,128]{3,2,1,0:T(8,128)S(1)} custom-call(f32[8,8,64,128]{3,2,1,0:T(8,128)S(1)} %get-tuple-element.57.refs_0_.refs_5_, bf16[8,4,48,128]{3,2,1,0:T(8,128)(2,1)S(1)} %collective-permute-done.13.refs_1_, bf16[8,8,48,256]{3,2,1,0:T(8,128)(2,1)S(1)} %copy-done.1, f32[64,48]{1,0:T(8,128)S(1)} %bitcast.15, f32[4,64,48]{2,1,0:T(8,128)S(1)} %bitcast.7, ...), custom_call_target="tpu_custom_call" | custom-call | tf_op jit(solution)/shard_map/pallas_call | solution.py:183
  36.1 4.1 %collective-permute-start.17 = (bf16[4,8,48,128]{3,2,1,0:T(8,128)(2,1)S(1)}, bf16[4,8,48,128]{3,2,1,0:T(8,128)(2,1)S(1)}, u32[]{:S(2)}, u32[]{:S(2)}) collective-permute-start(bf16[4,8,48,128]{3,2,1,0:T(8,128)(2,1)S(1)} %get-tuple-element.63), channel_id=1, source_target_pairs={{0,4},{4,0},{8,12},{12,8},{1,5},{5,1},{9,13},{13,9},{2,6},{6,2},{1... | collective-permute-start | bytes 1179656 | tf_op jit(solution)/shard_map/ppermute | solution.py:305
  40.9 2.3 %shard_map.53.refs_0_ = f32[8,8,48,128]{3,2,1,0:T(8,128)S(1)} custom-call(f32[8,8,64,128]{3,2,1,0:T(8,128)S(1)} %get-tuple-element.45.refs_0_.refs_5_, bf16[8,4,48,128]{3,2,1,0:T(8,128)(2,1)S(1)} %collective-permute-done.3.refs_1_, bf16[8,8,48,256]{3,2,1,0:T(8,128)(2,1)S(1)} %copy-done.1, f32[64,48]{1,0:T(8,128)S(1)} %bitcast.17, f32[4,64,48]{2,1,0:T(8,128)S(1)} %bitcast.8, ...), custom_call_target="tpu_custom_call" | custom-call | tf_op jit(solution)/shard_map/pallas_call | solution.py:183
  44.5 4.1 %collective-permute-start.7 = (bf16[4,8,48,128]{3,2,1,0:T(8,128)(2,1)S(1)}, bf16[4,8,48,128]{3,2,1,0:T(8,128)(2,1)S(1)}, u32[]{:S(2)}, u32[]{:S(2)}) collective-permute-start(bf16[4,8,48,128]{3,2,1,0:T(8,128)(2,1)S(1)} %get-tuple-element.51), channel_id=1, source_target_pairs={{0,4},{4,0},{8,12},{12,8},{1,5},{5,1},{9,13},{13,9},{2,6},{6,2},{1... | collective-permute-start | bytes 1179656 | tf_op jit(solution)/shard_map/ppermute | solution.py:305
  49.3 2.3 %shard_map.63.base_ref = f32[8,8,48,128]{3,2,1,0:T(8,128)S(1)} custom-call(f32[8,8,64,128]{3,2,1,0:T(8,128)S(1)} %get-tuple-element.61.refs_0_, bf16[8,4,48,128]{3,2,1,0:T(8,128)(2,1)S(1)} %collective-permute-done.16.refs_1_, bf16[8,8,48,256]{3,2,1,0:T(8,128)(2,1)S(1)} %copy-done.1, f32[64,48]{1,0:T(8,128)S(1)} %bitcast.19, f32[4,64,48]{2,1,0:T(8,128)S(1)} %bitcast.9, ...), custom_call_target="tpu_custom_call" | custom-call | tf_op jit(solution)/shard_map/pallas_call | solution.py:183
  52.6 1.6 %collective-permute-start.19 = (bf16[4,8,48,128]{3,2,1,0:T(8,128)(2,1)S(1)}, bf16[4,8,48,128]{3,2,1,0:T(8,128)(2,1)S(1)}, u32[]{:S(2)}, u32[]{:S(2)}) collective-permute-start(bf16[4,8,48,128]{3,2,1,0:T(8,128)(2,1)S(1)} %shard_map.65.sent1), channel_id=1, source_target_pairs={{0,2},{2,0},{1,3},{3,1},{4,6},{6,4},{5,7},{7,5},{8,10},{10,8},{9,1... | collective-permute-start | bytes 1179656 | tf_op jit(solution)/shard_map/ppermute | solution.py:305
  54.1 2.2 %shard_map.55.base_ref = f32[8,8,48,128]{3,2,1,0:T(8,128)S(1)} custom-call(f32[8,8,64,128]{3,2,1,0:T(8,128)S(1)} %get-tuple-element.49.refs_0_, bf16[8,4,48,128]{3,2,1,0:T(8,128)(2,1)S(1)} %collective-permute-done.6.refs_1_, bf16[8,8,48,256]{3,2,1,0:T(8,128)(2,1)S(1)} %copy-done.1, f32[64,48]{1,0:T(8,128)S(1)} %bitcast.21, f32[4,64,48]{2,1,0:T(8,128)S(1)} %bitcast.10, ...), custom_call_target="tpu_custom_call" | custom-call | tf_op jit(solution)/shard_map/pallas_call | solution.py:183
  56.4 2.6 %collective-permute-done.7.even_ref = bf16[4,8,48,128]{3,2,1,0:T(8,128)(2,1)S(1)} collective-permute-done((bf16[4,8,48,128]{3,2,1,0:T(8,128)(2,1)S(1)}, bf16[4,8,48,128]{3,2,1,0:T(8,128)(2,1)S(1)}, u32[]{:S(2)}, u32[]{:S(2)}) %collective-permute-start.7) | collective-permute-done | bytes 393248 | tf_op jit(solution)/shard_map/ppermute | solution.py:305
  60.0 1.7 %collective-permute-start.9 = (bf16[4,8,48,128]{3,2,1,0:T(8,128)(2,1)S(1)}, bf16[4,8,48,128]{3,2,1,0:T(8,128)(2,1)S(1)}, u32[]{:S(2)}, u32[]{:S(2)}) collective-permute-start(bf16[4,8,48,128]{3,2,1,0:T(8,128)(2,1)S(1)} %shard_map.57.sent0), channel_id=1, source_target_pairs={{0,2},{2,0},{1,3},{3,1},{4,6},{6,4},{5,7},{7,5},{8,10},{10,8},{9,1... | collective-permute-start | bytes 1179656 | tf_op jit(solution)/shard_map/ppermute | solution.py:305
  64.6 7.7 %collective-permute-done.9.got0 = bf16[4,8,48,128]{3,2,1,0:T(8,128)(2,1)S(1)} collective-permute-done((bf16[4,8,48,128]{3,2,1,0:T(8,128)(2,1)S(1)}, bf16[4,8,48,128]{3,2,1,0:T(8,128)(2,1)S(1)}, u32[]{:S(2)}, u32[]{:S(2)}) %collective-permute-start.9) | collective-permute-done | bytes 393248 | tf_op jit(solution)/shard_map/ppermute | solution.py:305
  75.5 1.3 %collective-permute-start.26 = (f32[128,128]{1,0:T(8,128)S(1)}, f32[128,128]{1,0:T(8,128)S(1)}, u32[]{:S(2)}, u32[]{:S(2)}) collective-permute-start(f32[128,128]{1,0:T(8,128)S(1)} %get-tuple-element.75), channel_id=1, source_target_pairs={{8,0},{12,4},{2,10},{6,14},{9,1},{13,5},{3,11},{7,15},{24,16},{28,... | collective-permute-start | bytes 196616 | tf_op jit(solution)/shard_map/ppermute | solution.py:562
  78.1 5.2 %collective-permute-start.28 = (f32[128,128]{1,0:T(8,128)S(1)}, f32[128,128]{1,0:T(8,128)S(1)}, u32[]{:S(2)}, u32[]{:S(2)}) collective-permute-start(f32[128,128]{1,0:T(8,128)S(1)} %get-tuple-element.77), channel_id=1, source_target_pairs={{4,0},{0,4},{14,10},{10,14},{5,1},{1,5},{15,11},{11,15},{20,16},{1... | collective-permute-start | bytes 196616 | tf_op jit(solution)/shard_map/ppermute | solution.py:562
  85.5 1.5 %collective-permute-start.23 = (bf16[144,128]{1,0:T(8,128)(2,1)S(1)}, bf16[144,128]{1,0:T(8,128)(2,1)S(1)}, u32[]{:S(2)}, u32[]{:S(2)}) collective-permute-start(bf16[144,128]{1,0:T(8,128)(2,1)S(1)} %get-tuple-element.70), channel_id=1, source_target_pairs={{0,12},{4,8},{8,4},{12,0},{1,13},{5,9},{9,5},{13,1},{2,14},{6,10},... | collective-permute-start | bytes 110600 | tf_op jit(solution)/shard_map/ppermute | solution.py:567
  88.2 2.2 %collective-permute-done.22.refs_0_ = bf16[144,128]{1,0:T(8,128)(2,1)S(1)} collective-permute-done((bf16[144,128]{1,0:T(8,128)(2,1)S(1)}, bf16[144,128]{1,0:T(8,128)(2,1)S(1)}, u32[]{:S(2)}, u32[]{:S(2)}) %collective-permute-start.22) | collective-permute-done | bytes 36896 | tf_op jit(solution)/shard_map/ppermute | solution.py:567
  91.4 2.0 %collective-permute-start.29 = (bf16[272,128]{1,0:T(8,128)(2,1)S(1)}, bf16[272,128]{1,0:T(8,128)(2,1)S(1)}, u32[]{:S(2)}, u32[]{:S(2)}) collective-permute-start(bf16[272,128]{1,0:T(8,128)(2,1)S(1)} %shard_map.70.mine_ref), channel_id=1, source_target_pairs={{0,2},{2,0},{1,3},{3,1},{4,6},{6,4},{5,7},{7,5},{8,10},{10,8},{9,1... | collective-permute-start | bytes 208904 | tf_op jit(solution)/shard_map/ppermute | solution.py:305
  93.5 2.3 %collective-permute-done.29.other_ref = bf16[272,128]{1,0:T(8,128)(2,1)S(1)} collective-permute-done((bf16[272,128]{1,0:T(8,128)(2,1)S(1)}, bf16[272,128]{1,0:T(8,128)(2,1)S(1)}, u32[]{:S(2)}, u32[]{:S(2)}) %collective-permute-start.29) | collective-permute-done | bytes 69664 | tf_op jit(solution)/shard_map/ppermute | solution.py:305
  96.3 1.3 %collective-permute-done.30.far_ref = f32[128,256]{1,0:T(8,128)S(1)} collective-permute-done((f32[128,256]{1,0:T(8,128)S(1)}, f32[128,256]{1,0:T(8,128)S(1)}, u32[]{:S(2)}, u32[]{:S(2)}) %collective-permute-start.30) | collective-permute-done | bytes 131104 | tf_op jit(solution)/shard_map/ppermute | solution.py:305
  (71 shorter events, 28.7 us)
Async XLA Ops:
  4.0 9.4 %collective-permute-start.10 = (bf16[8,4,48,128]{3,2,1,0:T(8,128)(2,1)S(1)}, bf16[8,4,48,128]{3,2,1,0:T(8,128)(2,1)S(1)}, u32[]{:S(2)}, u32[]{:S(2)}) collective-permute-start(bf16[8,4,48,128]{3,2,1,0:T(8,128)(2,1)S(1)} %get-tuple-element.54), channel_id=1, source_target_pairs={{0,1},{1,0},{2,3},{3,2},{4,5},{5,4},{6,7},{7,6},{8,9},{9,8},{10,11... | collective-permute-start | bytes 1179656 | tf_op jit(solution)/shard_map/ppermute | solution.py:305
  4.5 12.6 %collective-permute-start.11 = (bf16[4,8,48,128]{3,2,1,0:T(8,128)(2,1)S(1)}, bf16[4,8,48,128]{3,2,1,0:T(8,128)(2,1)S(1)}, u32[]{:S(2)}, u32[]{:S(2)}) collective-permute-start(bf16[4,8,48,128]{3,2,1,0:T(8,128)(2,1)S(1)} %get-tuple-element.55), channel_id=1, source_target_pairs={{0,4},{4,0},{8,12},{12,8},{1,5},{5,1},{9,13},{13,9},{2,6},{6,2},{1... | collective-permute-start | bytes 1179656 | tf_op jit(solution)/shard_map/ppermute | solution.py:305
  7.2 10.0 %collective-permute-start.12 = (bf16[4,8,48,128]{3,2,1,0:T(8,128)(2,1)S(1)}, bf16[4,8,48,128]{3,2,1,0:T(8,128)(2,1)S(1)}, u32[]{:S(2)}, u32[]{:S(2)}) collective-permute-start(bf16[4,8,48,128]{3,2,1,0:T(8,128)(2,1)S(1)} %get-tuple-element.56), channel_id=1, source_target_pairs={{4,8},{8,4},{5,9},{9,5},{6,10},{10,6},{7,11},{11,7},{20,24},{24,20... | collective-permute-start | bytes 1179656 | tf_op jit(solution)/shard_map/ppermute | solution.py:305
  8.9 14.4 %collective-permute-start = (bf16[8,4,48,128]{3,2,1,0:T(8,128)(2,1)S(1)}, bf16[8,4,48,128]{3,2,1,0:T(8,128)(2,1)S(1)}, u32[]{:S(2)}, u32[]{:S(2)}) collective-permute-start(bf16[8,4,48,128]{3,2,1,0:T(8,128)(2,1)S(1)} %get-tuple-element.42), channel_id=1, source_target_pairs={{0,1},{1,0},{2,3},{3,2},{4,5},{5,4},{6,7},{7,6},{8,9},{9,8},{10,11... | collective-permute-start | bytes 1179656 | tf_op jit(solution)/shard_map/ppermute | solution.py:305
  9.1 17.1 %collective-permute-start.1 = (bf16[4,8,48,128]{3,2,1,0:T(8,128)(2,1)S(1)}, bf16[4,8,48,128]{3,2,1,0:T(8,128)(2,1)S(1)}, u32[]{:S(2)}, u32[]{:S(2)}) collective-permute-start(bf16[4,8,48,128]{3,2,1,0:T(8,128)(2,1)S(1)} %get-tuple-element.43), channel_id=1, source_target_pairs={{0,4},{4,0},{8,12},{12,8},{1,5},{5,1},{9,13},{13,9},{2,6},{6,2},{1... | collective-permute-start | bytes 1179656 | tf_op jit(solution)/shard_map/ppermute | solution.py:305
  13.4 12.8 %collective-permute-start.2 = (bf16[4,8,48,128]{3,2,1,0:T(8,128)(2,1)S(1)}, bf16[4,8,48,128]{3,2,1,0:T(8,128)(2,1)S(1)}, u32[]{:S(2)}, u32[]{:S(2)}) collective-permute-start(bf16[4,8,48,128]{3,2,1,0:T(8,128)(2,1)S(1)} %get-tuple-element.44), channel_id=1, source_target_pairs={{4,8},{8,4},{5,9},{9,5},{6,10},{10,6},{7,11},{11,7},{20,24},{24,20... | collective-permute-start | bytes 1179656 | tf_op jit(solution)/shard_map/ppermute | solution.py:305
  18.2 13.5 %collective-permute-start.13 = (bf16[8,4,48,128]{3,2,1,0:T(8,128)(2,1)S(1)}, bf16[8,4,48,128]{3,2,1,0:T(8,128)(2,1)S(1)}, u32[]{:S(2)}, u32[]{:S(2)}) collective-permute-start(bf16[8,4,48,128]{3,2,1,0:T(8,128)(2,1)S(1)} %get-tuple-element.58), channel_id=1, source_target_pairs={{0,1},{1,0},{2,3},{3,2},{4,5},{5,4},{6,7},{7,6},{8,9},{9,8},{10,11... | collective-permute-start | bytes 1179656 | tf_op jit(solution)/shard_map/ppermute | solution.py:305
  18.3 16.4 %collective-permute-start.14 = (bf16[4,8,48,128]{3,2,1,0:T(8,128)(2,1)S(1)}, bf16[4,8,48,128]{3,2,1,0:T(8,128)(2,1)S(1)}, u32[]{:S(2)}, u32[]{:S(2)}) collective-permute-start(bf16[4,8,48,128]{3,2,1,0:T(8,128)(2,1)S(1)} %get-tuple-element.59), channel_id=1, source_target_pairs={{0,4},{4,0},{8,12},{12,8},{1,5},{5,1},{9,13},{13,9},{2,6},{6,2},{1... | collective-permute-start | bytes 1179656 | tf_op jit(solution)/shard_map/ppermute | solution.py:305
  23.4 11.4 %collective-permute-start.15 = (bf16[4,8,48,128]{3,2,1,0:T(8,128)(2,1)S(1)}, bf16[4,8,48,128]{3,2,1,0:T(8,128)(2,1)S(1)}, u32[]{:S(2)}, u32[]{:S(2)}) collective-permute-start(bf16[4,8,48,128]{3,2,1,0:T(8,128)(2,1)S(1)} %get-tuple-element.60), channel_id=1, source_target_pairs={{4,8},{8,4},{5,9},{9,5},{6,10},{10,6},{7,11},{11,7},{20,24},{24,20... | collective-permute-start | bytes 1179656 | tf_op jit(solution)/shard_map/ppermute | solution.py:305
  27.3 12.9 %collective-permute-start.3 = (bf16[8,4,48,128]{3,2,1,0:T(8,128)(2,1)S(1)}, bf16[8,4,48,128]{3,2,1,0:T(8,128)(2,1)S(1)}, u32[]{:S(2)}, u32[]{:S(2)}) collective-permute-start(bf16[8,4,48,128]{3,2,1,0:T(8,128)(2,1)S(1)} %get-tuple-element.46), channel_id=1, source_target_pairs={{0,1},{1,0},{2,3},{3,2},{4,5},{5,4},{6,7},{7,6},{8,9},{9,8},{10,11... | collective-permute-start | bytes 1179656 | tf_op jit(solution)/shard_map/ppermute | solution.py:305
  27.6 15.6 %collective-permute-start.4 = (bf16[4,8,48,128]{3,2,1,0:T(8,128)(2,1)S(1)}, bf16[4,8,48,128]{3,2,1,0:T(8,128)(2,1)S(1)}, u32[]{:S(2)}, u32[]{:S(2)}) collective-permute-start(bf16[4,8,48,128]{3,2,1,0:T(8,128)(2,1)S(1)} %get-tuple-element.47), channel_id=1, source_target_pairs={{0,4},{4,0},{8,12},{12,8},{1,5},{5,1},{9,13},{13,9},{2,6},{6,2},{1... | collective-permute-start | bytes 1179656 | tf_op jit(solution)/shard_map/ppermute | solution.py:305
  31.8 11.4 %collective-permute-start.5 = (bf16[4,8,48,128]{3,2,1,0:T(8,128)(2,1)S(1)}, bf16[4,8,48,128]{3,2,1,0:T(8,128)(2,1)S(1)}, u32[]{:S(2)}, u32[]{:S(2)}) collective-permute-start(bf16[4,8,48,128]{3,2,1,0:T(8,128)(2,1)S(1)} %get-tuple-element.48), channel_id=1, source_target_pairs={{4,8},{8,4},{5,9},{9,5},{6,10},{10,6},{7,11},{11,7},{20,24},{24,20... | collective-permute-start | bytes 1179656 | tf_op jit(solution)/shard_map/ppermute | solution.py:305
  35.9 12.8 %collective-permute-start.16 = (bf16[8,4,48,128]{3,2,1,0:T(8,128)(2,1)S(1)}, bf16[8,4,48,128]{3,2,1,0:T(8,128)(2,1)S(1)}, u32[]{:S(2)}, u32[]{:S(2)}) collective-permute-start(bf16[8,4,48,128]{3,2,1,0:T(8,128)(2,1)S(1)} %get-tuple-element.62), channel_id=1, source_target_pairs={{0,1},{1,0},{2,3},{3,2},{4,5},{5,4},{6,7},{7,6},{8,9},{9,8},{10,11... | collective-permute-start | bytes 1179656 | tf_op jit(solution)/shard_map/ppermute | solution.py:305
  36.1 15.5 %collective-permute-start.17 = (bf16[4,8,48,128]{3,2,1,0:T(8,128)(2,1)S(1)}, bf16[4,8,48,128]{3,2,1,0:T(8,128)(2,1)S(1)}, u32[]{:S(2)}, u32[]{:S(2)}) collective-permute-start(bf16[4,8,48,128]{3,2,1,0:T(8,128)(2,1)S(1)} %get-tuple-element.63), channel_id=1, source_target_pairs={{0,4},{4,0},{8,12},{12,8},{1,5},{5,1},{9,13},{13,9},{2,6},{6,2},{1... | collective-permute-start | bytes 1179656 | tf_op jit(solution)/shard_map/ppermute | solution.py:305
  40.2 11.4 %collective-permute-start.18 = (bf16[4,8,48,128]{3,2,1,0:T(8,128)(2,1)S(1)}, bf16[4,8,48,128]{3,2,1,0:T(8,128)(2,1)S(1)}, u32[]{:S(2)}, u32[]{:S(2)}) collective-permute-start(bf16[4,8,48,128]{3,2,1,0:T(8,128)(2,1)S(1)} %get-tuple-element.64), channel_id=1, source_target_pairs={{4,8},{8,4},{5,9},{9,5},{6,10},{10,6},{7,11},{11,7},{20,24},{24,20... | collective-permute-start | bytes 1179656 | tf_op jit(solution)/shard_map/ppermute | solution.py:305
  44.3 9.8 %collective-permute-start.6 = (bf16[8,4,48,128]{3,2,1,0:T(8,128)(2,1)S(1)}, bf16[8,4,48,128]{3,2,1,0:T(8,128)(2,1)S(1)}, u32[]{:S(2)}, u32[]{:S(2)}) collective-permute-start(bf16[8,4,48,128]{3,2,1,0:T(8,128)(2,1)S(1)} %get-tuple-element.50), channel_id=1, source_target_pairs={{0,1},{1,0},{2,3},{3,2},{4,5},{5,4},{6,7},{7,6},{8,9},{9,8},{10,11... | collective-permute-start | bytes 1179656 | tf_op jit(solution)/shard_map/ppermute | solution.py:305
  44.5 14.5 %collective-permute-start.7 = (bf16[4,8,48,128]{3,2,1,0:T(8,128)(2,1)S(1)}, bf16[4,8,48,128]{3,2,1,0:T(8,128)(2,1)S(1)}, u32[]{:S(2)}, u32[]{:S(2)}) collective-permute-start(bf16[4,8,48,128]{3,2,1,0:T(8,128)(2,1)S(1)} %get-tuple-element.51), channel_id=1, source_target_pairs={{0,4},{4,0},{8,12},{12,8},{1,5},{5,1},{9,13},{13,9},{2,6},{6,2},{1... | collective-permute-start | bytes 1179656 | tf_op jit(solution)/shard_map/ppermute | solution.py:305
  48.6 10.4 %collective-permute-start.8 = (bf16[4,8,48,128]{3,2,1,0:T(8,128)(2,1)S(1)}, bf16[4,8,48,128]{3,2,1,0:T(8,128)(2,1)S(1)}, u32[]{:S(2)}, u32[]{:S(2)}) collective-permute-start(bf16[4,8,48,128]{3,2,1,0:T(8,128)(2,1)S(1)} %get-tuple-element.52), channel_id=1, source_target_pairs={{4,8},{8,4},{5,9},{9,5},{6,10},{10,6},{7,11},{11,7},{20,24},{24,20... | collective-permute-start | bytes 1179656 | tf_op jit(solution)/shard_map/ppermute | solution.py:305
  52.6 12.0 %collective-permute-start.19 = (bf16[4,8,48,128]{3,2,1,0:T(8,128)(2,1)S(1)}, bf16[4,8,48,128]{3,2,1,0:T(8,128)(2,1)S(1)}, u32[]{:S(2)}, u32[]{:S(2)}) collective-permute-start(bf16[4,8,48,128]{3,2,1,0:T(8,128)(2,1)S(1)} %shard_map.65.sent1), channel_id=1, source_target_pairs={{0,2},{2,0},{1,3},{3,1},{4,6},{6,4},{5,7},{7,5},{8,10},{10,8},{9,1... | collective-permute-start | bytes 1179656 | tf_op jit(solution)/shard_map/ppermute | solution.py:305
  60.0 12.3 %collective-permute-start.9 = (bf16[4,8,48,128]{3,2,1,0:T(8,128)(2,1)S(1)}, bf16[4,8,48,128]{3,2,1,0:T(8,128)(2,1)S(1)}, u32[]{:S(2)}, u32[]{:S(2)}) collective-permute-start(bf16[4,8,48,128]{3,2,1,0:T(8,128)(2,1)S(1)} %shard_map.57.sent0), channel_id=1, source_target_pairs={{0,2},{2,0},{1,3},{3,1},{4,6},{6,4},{5,7},{7,5},{8,10},{10,8},{9,1... | collective-permute-start | bytes 1179656 | tf_op jit(solution)/shard_map/ppermute | solution.py:305
  73.1 11.4 %collective-permute-start.20 = (f32[384,128]{1,0:T(8,128)S(1)}, f32[384,128]{1,0:T(8,128)S(1)}, u32[]{:S(2)}, u32[]{:S(2)}) collective-permute-start(f32[384,128]{1,0:T(8,128)S(1)} %get-tuple-element.66), channel_id=1, source_target_pairs={{0,1},{1,0},{2,3},{3,2},{4,5},{5,4},{6,7},{7,6},{8,9},{9,8},{10,11... | collective-permute-start | bytes 589832 | tf_op jit(solution)/shard_map/ppermute | solution.py:305
  75.5 11.5 %collective-permute-start.26 = (f32[128,128]{1,0:T(8,128)S(1)}, f32[128,128]{1,0:T(8,128)S(1)}, u32[]{:S(2)}, u32[]{:S(2)}) collective-permute-start(f32[128,128]{1,0:T(8,128)S(1)} %get-tuple-element.75), channel_id=1, source_target_pairs={{8,0},{12,4},{2,10},{6,14},{9,1},{13,5},{3,11},{7,15},{24,16},{28,... | collective-permute-start | bytes 196616 | tf_op jit(solution)/shard_map/ppermute | solution.py:562
  76.8 11.4 %collective-permute-start.27 = (f32[128,128]{1,0:T(8,128)S(1)}, f32[128,128]{1,0:T(8,128)S(1)}, u32[]{:S(2)}, u32[]{:S(2)}) collective-permute-start(f32[128,128]{1,0:T(8,128)S(1)} %get-tuple-element.76), channel_id=1, source_target_pairs={{12,0},{8,4},{6,10},{2,14},{13,1},{9,5},{7,11},{3,15},{28,16},{24,... | collective-permute-start | bytes 196616 | tf_op jit(solution)/shard_map/ppermute | solution.py:562
  78.1 10.1 %collective-permute-start.28 = (f32[128,128]{1,0:T(8,128)S(1)}, f32[128,128]{1,0:T(8,128)S(1)}, u32[]{:S(2)}, u32[]{:S(2)}) collective-permute-start(f32[128,128]{1,0:T(8,128)S(1)} %get-tuple-element.77), channel_id=1, source_target_pairs={{4,0},{0,4},{14,10},{10,14},{5,1},{1,5},{15,11},{11,15},{20,16},{1... | collective-permute-start | bytes 196616 | tf_op jit(solution)/shard_map/ppermute | solution.py:562
  (12 other events, 53.5 us)

commit v8 on v7

--- a/solution.py
+++ b/solution.py
@@ -190,14 +190,15 @@
     )(*operands)
 
 
-def rim_body(middle, *refs):
+def rim_body(kind, *refs):
     base_ref, even_ref, odd_ref, c_ref = refs[:4]
     outs, (square, turned_c) = refs[4:-2], refs[-2:]
     depth, across, along, _ = base_ref.shape
     core = lax.axis_index("sub")
     even = slab_is_even()
+    lower = lax.axis_index("probe") == 0
     turned_c[...] = turned(c_ref[...], square)
-    if middle:
+    if kind == "middle":
         clear_pads(outs[0])
 
     def tile(start):
@@ -224,32 +225,39 @@
                 if added is not None:
                     new = new + lane(courant, z * across + x) * added
                 news.append(new)
-            if middle:
+            if kind == "middle":
                 for z, new in enumerate(news):
                     outs[0][z, x, rows] = new
                 store_edges(x, span, news, even, outs[1], outs[2])
+            elif kind == "half":
+                for z in range(depth // 2):
+                    one, two = news[z].astype(BF16), news[z + depth // 2].astype(BF16)
+                    outs[0][z, x, span] = jnp.where(lower, one, two)
+                    outs[1][z, x, span] = jnp.where(lower, two, one)
             else:
                 for z, new in enumerate(news):
                     outs[0][z, x, span] = new.astype(BF16)
-        if middle:
+        if kind == "middle":
             store_beside(span, rows, core, outs[0], outs[3])
 
     tiles(along, tile)
 
 
-def rim_step(base, evens, odds, courant, middle):
+def rim_step(base, evens, odds, courant, kind):
     depth, across, along, _ = base.shape
-    if middle:
+    if kind == "middle":
         out_shape = [
             shape_of(depth, across, along + 2 * EDGE, F32),
             shape_of(RADIUS, across, along, BF16),
             shape_of(RADIUS, across, along, BF16),
             shape_of(depth, RADIUS, along, BF16),
         ]
+    elif kind == "half":
+        out_shape = [shape_of(depth // 2, across, along, BF16)] * 2
     else:
         out_shape = [shape_of(depth, across, along, BF16)]
     return pl.pallas_call(
-        functools.partial(rim_body, middle),
+        functools.partial(rim_body, kind),
         in_specs=whole_vmem(4),
         out_specs=whole_vmem(len(out_shape)),
         out_shape=out_shape,
@@ -258,49 +266,6 @@
     )(base, evens, odds, courant)
 
 
-def last_body(sent, base_ref, even_ref, odd_ref, c_ref, out_ref, square, turned_c):
-    depth, across, along, _ = base_ref.shape
-    chip = lax.axis_index("probe")
-    low = (chip == 1) if sent else (chip == 0)
-    from_odd = low == slab_is_even()
-    turned_c[...] = turned(c_ref[...], square)
-
-    def tile(start):
-        span = pl.ds(start, TILE)
-        courant = turned_c[span]
-        for x in range(across):
-            near = []
-            for j in range(RADIUS):
-                at = jnp.where(low, RADIUS - 1 - j, j)
-                near.append(
-                    jnp.where(from_odd, odd_ref[at, x, span], even_ref[at, x, span]).astype(F32)
-                )
-            for m in range(RADIUS):
-                mirror = depth - 1 - m
-                added = COEFFICIENTS[m + 1] * near[0]
-                for r in range(m + 2, RADIUS + 1):
-                    added = added + COEFFICIENTS[r] * near[r - m - 1]
-                scale = jnp.where(
-                    low, lane(courant, m * across + x), lane(courant, mirror * across + x)
-                )
-                new = base_ref[jnp.where(low, m, mirror), x, span] + scale * added
-                out_ref[m, x, span] = new.astype(BF16)
-
-    tiles(along, tile)
-
-
-def last_step(base, evens, odds, courant, sent):
-    _, across, along, _ = base.shape
-    return pl.pallas_call(
-        functools.partial(last_body, sent),
-        in_specs=whole_vmem(4),
-        out_specs=whole_vmem(1)[0],
-        out_shape=shape_of(RADIUS, across, along, BF16),
-        scratch_shapes=square_scratch(),
-        compiler_params=params(),
-    )(base, evens, odds, courant)
-
-
 def swap(x, axis, pairs):
     return lax.ppermute(x, axis, [p for a, b in pairs for p in ((a, b), (b, a))])
 
@@ -335,7 +300,7 @@
     return rows == cols
 
 
-def inner_body(kept0, sent0, kept1, sent1, keep_ref, send_ref, diag_ref, panel):
+def inner_body(kept0, sent0, kept1, sent1, keep_ref, send_ref, panel):
     half = panel.shape[0] // 2
     for n, (kept, sent) in enumerate(((kept0, sent0), (kept1, sent1))):
         columns = slice(n * LANES, (n + 1) * LANES)
@@ -344,8 +309,9 @@
     core = lax.axis_index("sub")
     whole = product(panel[...], panel[...])
     first, second = whole[:, :LANES], whole[:, LANES:]
-    keep_ref[...] = jnp.where(core == 0, first, second)
-    send_ref[...] = jnp.where(core == 0, second, first)
+    size = 2 * LANES
+    keep_ref[:size] = jnp.where(core == 0, first, second)
+    send_ref[:size] = jnp.where(core == 0, second, first)
     diag = [
         jnp.sum(jnp.where(eye(), block_of(whole, n, n), 0.0), axis=0, keepdims=True)
         for n in range(2)
@@ -353,44 +319,49 @@
     none = jnp.zeros_like(diag[0])
     chip = lax.axis_index("probe")
     rows = [jnp.where(chip == n // 2, diag[n % 2], none) for n in range(4)]
-    diag_ref[...] = jnp.concatenate(rows + [none] * 4, axis=0)
+    tail = jnp.concatenate(rows + [none] * 4, axis=0)
+    keep_ref[size:] = tail
+    send_ref[size:] = tail
 
 
 def inner_gram(fields):
     size = 2 * LANES
     cells = 2 * math.prod(fields[0].shape[:3])
-    half = jax.ShapeDtypeStruct((size, LANES), F32)
+    half = jax.ShapeDtypeStruct((size + 8, LANES), F32)
     return pl.pallas_call(
         inner_body,
         in_specs=whole_vmem(4),
-        out_specs=whole_vmem(3),
-        out_shape=[half, half, jax.ShapeDtypeStruct((8, LANES), F32)],
+        out_specs=whole_vmem(2),
+        out_shape=[half, half],
         scratch_shapes=[pltpu.VMEM((cells, size), BF16)],
         compiler_params=params(),
     )(*fields)
 
 
-def inner_rows_body(keep_ref, got_ref, *outs):
+def inner_rows_body(keep_ref, got_ref, tail_ref, *outs):
     slab = lax.axis_index("slab")
     chip = lax.axis_index("probe")
+    tail_ref[...] = keep_ref[2 * LANES :] + got_ref[2 * LANES :]
     for d, out in enumerate(outs):
         row = jnp.clip((slab ^ d) - 2 * chip, 0, 1)
         span = pl.ds(pl.multiple_of(row * LANES, LANES), LANES)
-        out[...] = keep_ref[span] + got_ref[span]
+        out[...] = (keep_ref[span] + got_ref[span]).astype(out.dtype)
 
 
 def inner_rows(keep, got, slabs):
-    block = jax.ShapeDtypeStruct((LANES, LANES), F32)
+    own = jax.ShapeDtypeStruct((LANES, LANES), F32)
+    sent = jax.ShapeDtypeStruct((LANES, LANES), BF16)
     return pl.pallas_call(
         inner_rows_body,
         in_specs=whole_vmem(2),
-        out_specs=whole_vmem(slabs),
-        out_shape=[block] * slabs,
+        out_specs=whole_vmem(1 + slabs),
+        out_shape=[jax.ShapeDtypeStruct((8, LANES), F32), own] + [sent] * (slabs - 1),
         compiler_params=params(),
     )(keep, got)
 
 
-def cross_body(kept0, got0, kept1, got1, keep_ref, send_ref, panel):
+def cross_body(kept0, got0, kept1, got1, *refs):
+    keep_ref, send_ref, panel = refs[-3:]
     chip = lax.axis_index("probe")
     core = lax.axis_index("sub")
     cells = panel.shape[0]
@@ -408,17 +379,17 @@
         ref[2 * LANES :] = mixed
 
 
-def cross_gram(fields):
+def cross_gram(fields, after):
     cells = math.prod(fields[0].shape[:3])
     three = jax.ShapeDtypeStruct((3 * LANES, LANES), F32)
     return pl.pallas_call(
         cross_body,
-        in_specs=whole_vmem(4),
+        in_specs=whole_vmem(4) + [pl.BlockSpec(memory_space=pl.ANY)] * len(after),
         out_specs=whole_vmem(2),
         out_shape=[three, three],
         scratch_shapes=[pltpu.VMEM((cells, 4 * LANES), BF16)],
         compiler_params=params(),
-    )(*fields)
+    )(*fields, *after)
 
 
 def rounded(ref, block, tail):
@@ -434,10 +405,10 @@
     return ref[:count].astype(F32), tail[:8] + tail[8:]
 
 
-def cross_rows_body(keep_ref, got_ref, diag_ref, other_diag_ref, own_ref, *outs):
+def cross_rows_body(keep_ref, got_ref, tail_ref, own_ref, *outs):
     slab = lax.axis_index("slab")
     core = lax.axis_index("sub")
-    tail = diag_ref[...] + other_diag_ref[...]
+    tail = tail_ref[...]
     for d in range(len(outs) + 1):
         owner = slab ^ d
         late = jnp.where(core == 0, jnp.where(owner == 2, 0, 2), jnp.where(owner == 2, 2, 1))
@@ -451,16 +422,16 @@
             rounded(outs[d - 1], block, tail)
 
 
-def cross_rows(keep, got, diag, other_diag, slabs):
+def cross_rows(keep, got, tail, slabs):
     own = jax.ShapeDtypeStruct((LANES + 8, LANES), F32)
     sent = jax.ShapeDtypeStruct((LANES + 16, LANES), BF16)
     return pl.pallas_call(
         cross_rows_body,
-        in_specs=whole_vmem(4),
+        in_specs=whole_vmem(3),
         out_specs=whole_vmem(slabs),
         out_shape=[own] + [sent] * (slabs - 1),
         compiler_params=params(),
-    )(keep, got, diag, other_diag)
+    )(keep, got, tail)
 
 
 def sum_body(slabs, own_ref, *refs):
@@ -470,7 +441,7 @@
         block, tail = block + more, tail + more_tail
     inner = refs[slabs - 1][...]
     for ref in refs[slabs : 2 * slabs - 1]:
-        inner = inner + ref[...]
+        inner = inner + ref[...].astype(F32)
     out_ref = refs[-1]
     rounded(out_ref, block, tail)
     out_ref[LANES + 16 :] = inner.astype(BF16)
@@ -549,9 +520,8 @@
 def coupled(finals, cell_count):
     slabs = 4
     own = [field for kept, sent, _ in finals for field in (kept, sent)]
-    keep, send, diag = inner_gram(own)
-    inner = inner_rows(keep, core_swap(send), slabs)
-    other_diag = core_swap(diag)
+    keep, send = inner_gram(own)
+    tail, *inner = inner_rows(keep, core_swap(send), slabs)
     inner_arrived = []
     for d in (2, 3, 1):
         pairs = [
@@ -561,8 +531,9 @@
         ]
         inner_arrived.append(lax.ppermute(inner[d], ("slab", "probe"), pairs))
 
-    keep, send = cross_gram([field for kept, _, got in finals for field in (kept, got)])
-    mine, *blocks = cross_rows(keep, core_swap(send), diag, other_diag, slabs)
+    pairs = [field for kept, _, got in finals for field in (kept, got)]
+    keep, send = cross_gram(pairs, inner_arrived)
+    mine, *blocks = cross_rows(keep, core_swap(send), tail, slabs)
     arrived = [
         lax.ppermute(blocks[d - 1], "slab", [(i, i ^ d) for i in range(slabs)])
         for d in (2, 3, 1)
@@ -616,15 +587,14 @@
             even, odd, beside = halos[c]
             base = local_step(now[c], beside, probes, c, courant, source, n, previous[c])
             if n < steps - 1:
-                u, *edges = rim_step(base, even, odd, courant, True)
+                u, *edges = rim_step(base, even, odd, courant, "middle")
                 previous[c], now[c] = now[c], u
                 halos[c] = exchange(*edges)
             elif paired:
-                sent = last_step(base, even, odd, courant, True)
-                kept = last_step(base, even, odd, courant, False)
+                kept, sent = rim_step(base, even, odd, courant, "half")
                 finals.append((kept, sent, chip_swap(sent)))
             else:
-                finals += rim_step(base, even, odd, courant, False)
+                finals += rim_step(base, even, odd, courant, "all")
     return (coupled if paired else coupled_general)(finals, cell_count)
 
 

time: 98.8 us -> 93.1 us (0.942)
  waiting for transfers between devices: 21.1 us -> 17.5 us
  Pallas kernels: 26.6 us -> 24.7 us
    ppermute x25 -> x24, waiting for transfers between devices: 17.9 us -> 10.8 us  [swap(): lax.ppermute(x, axis, [p for a, b in pairs for p in ((a, b), (b, a))])]
    ppermute x3, waiting for transfers between devices: 0.01 us -> 2.92 us  [coupled(): inner_arrived.append(lax.ppermute(inner[d], ('slab', 'probe'), pairs))]
    pallas_call x11 -> x9, Pallas kernels: 9.82 us -> 7.91 us  [the longest x6 6.32 us: rim_step(): pl.pallas_call(functools.partial(rim_body, kind), in_specs=whole_vmem(4),...]
    ppermute x25 -> x24, starting transfers between devices: 36.1 us -> 34.6 us  [swap(): lax.ppermute(x, axis, [p for a, b in pairs for p in ((a, b), (b, a))])]
    ppermute x3, starting transfers between devices: 7.8 us -> 9.09 us  [coupled(): inner_arrived.append(lax.ppermute(inner[d], ('slab', 'probe'), pairs))]
  transfers between devices with their start and end apart: 31 -> 30, of which waited for: 10 -> 9; matrix products, arithmetic and copies ran while one was open for 0% -> 0% of each run, Pallas kernels for 24% -> 23%
where the time goes in v8:
time: 93.1 us; the launch traced here: 92.7 us
  starting transfers between devices  47.3 us (51%)
  Pallas kernels  24.7 us (27%)
  waiting for transfers between devices  17.5 us (19%)
  local copies, waits for them, and re-layouts  2.32 us (2%)
  between operations  1 us (1%)
    ppermute x24, starting transfers between devices, swap(): lax.ppermute(x, axis, [p for a, b in pairs for p in ((a, b), (b, a))])  34.6 us
    pallas_call x6, Pallas kernels, local_step(): pl.pallas_call(functools.partial(local_body, chunk, moment, previous is n...  13.3 us
    ppermute x24, waiting for transfers between devices, swap(): lax.ppermute(x, axis, [p for a, b in pairs for p in ((a, b), (b, a))])  10.8 us
    ppermute x3, starting transfers between devices, coupled(): inner_arrived.append(lax.ppermute(inner[d], ('slab', 'probe'), pairs))  9.09 us
    pallas_call x6, Pallas kernels, rim_step(): pl.pallas_call(functools.partial(rim_body, kind), in_specs=whole_vmem(4),...  6.32 us
    ppermute x3, waiting for transfers between devices, coupled(): lax.ppermute(blocks[d - 1], 'slab', [(i, i ^ d) for i in range(slabs)])  3.79 us
    ppermute x3, starting transfers between devices, coupled(): lax.ppermute(blocks[d - 1], 'slab', [(i, i ^ d) for i in range(slabs)])  3.55 us
    ppermute x3, waiting for transfers between devices, coupled(): inner_arrived.append(lax.ppermute(inner[d], ('slab', 'probe'), pairs))  2.92 us
  transfers between devices with their start and end apart: 30, of which 9 were waited for; matrix products, arithmetic and copies ran while one was open for 0% of the time, Pallas kernels for 23%

profile of v8, /device:TPU:0, one launch (start us, length us, event | category | flops | bytes accessed | tf_op | source)
XLA Modules:
  0.0 92.7 jit_solution(11285749482395243452)
XLA Ops:
  0.6 1.4 %copy-done = bf16[8,8,48,256]{3,2,1,0:T(8,128)(2,1)S(1)} copy-done((bf16[8,8,48,256]{3,2,1,0:T(8,128)(2,1)S(1)}, bf16[8,8,48,256]{3,2,1,0:T(8,128)(2,1)}, u32[]{:S(2)}) %copy-start) | copy-done | bytes 1572888
  4.5 2.7 %collective-permute-start.11 = (bf16[4,8,48,128]{3,2,1,0:T(8,128)(2,1)S(1)}, bf16[4,8,48,128]{3,2,1,0:T(8,128)(2,1)S(1)}, u32[]{:S(2)}, u32[]{:S(2)}) collective-permute-start(bf16[4,8,48,128]{3,2,1,0:T(8,128)(2,1)S(1)} %get-tuple-element.61), channel_id=1, source_target_pairs={{0,4},{4,0},{8,12},{12,8},{1,5},{5,1},{9,13},{13,9},{2,6},{6,2},{1... | collective-permute-start | bytes 1179656 | tf_op jit(solution)/shard_map/ppermute | solution.py:270
  9.1 4.3 %collective-permute-start.1 = (bf16[4,8,48,128]{3,2,1,0:T(8,128)(2,1)S(1)}, bf16[4,8,48,128]{3,2,1,0:T(8,128)(2,1)S(1)}, u32[]{:S(2)}, u32[]{:S(2)}) collective-permute-start(bf16[4,8,48,128]{3,2,1,0:T(8,128)(2,1)S(1)} %get-tuple-element.47), channel_id=1, source_target_pairs={{0,4},{4,0},{8,12},{12,8},{1,5},{5,1},{9,13},{13,9},{2,6},{6,2},{1... | collective-permute-start | bytes 1179656 | tf_op jit(solution)/shard_map/ppermute | solution.py:270
  14.1 2.2 %shard_map.58.refs_0_ = f32[8,8,48,128]{3,2,1,0:T(8,128)S(1)} custom-call(f32[8,8,64,128]{3,2,1,0:T(8,128)S(1)} %get-tuple-element.59.refs_0_.refs_5_, bf16[8,4,48,128]{3,2,1,0:T(8,128)(2,1)S(1)} %collective-permute-done.10.refs_1_, bf16[8,8,48,256]{3,2,1,0:T(8,128)(2,1)S(1)} %copy-done, f32[64,48]{1,0:T(8,128)S(1)} %bitcast.11, f32[4,64,48]{2,1,0:T(8,128)S(1)} %bitcast.5), custom_call_target="tpu_custom_call" | custom-call | tf_op jit(solution)/shard_map/pallas_call | solution.py:183
  18.3 5.0 %collective-permute-start.14 = (bf16[4,8,48,128]{3,2,1,0:T(8,128)(2,1)S(1)}, bf16[4,8,48,128]{3,2,1,0:T(8,128)(2,1)S(1)}, u32[]{:S(2)}, u32[]{:S(2)}) collective-permute-start(bf16[4,8,48,128]{3,2,1,0:T(8,128)(2,1)S(1)} %get-tuple-element.65), channel_id=1, source_target_pairs={{0,4},{4,0},{8,12},{12,8},{1,5},{5,1},{9,13},{13,9},{2,6},{6,2},{1... | collective-permute-start | bytes 1179656 | tf_op jit(solution)/shard_map/ppermute | solution.py:270
  24.1 2.1 %shard_map.51.refs_0_ = f32[8,8,48,128]{3,2,1,0:T(8,128)S(1)} custom-call(f32[8,8,64,128]{3,2,1,0:T(8,128)S(1)} %get-tuple-element.45.refs_0_.refs_5_, bf16[8,4,48,128]{3,2,1,0:T(8,128)(2,1)S(1)} %collective-permute-done.refs_1_, bf16[8,8,48,256]{3,2,1,0:T(8,128)(2,1)S(1)} %copy-done.1, f32[64,48]{1,0:T(8,128)S(1)} %bitcast.13, f32[4,64,48]{2,1,0:T(8,128)S(1)} %bitcast.6), custom_call_target="tpu_custom_call" | custom-call | tf_op jit(solution)/shard_map/pallas_call | solution.py:183
  27.6 4.2 %collective-permute-start.4 = (bf16[4,8,48,128]{3,2,1,0:T(8,128)(2,1)S(1)}, bf16[4,8,48,128]{3,2,1,0:T(8,128)(2,1)S(1)}, u32[]{:S(2)}, u32[]{:S(2)}) collective-permute-start(bf16[4,8,48,128]{3,2,1,0:T(8,128)(2,1)S(1)} %get-tuple-element.51), channel_id=1, source_target_pairs={{0,4},{4,0},{8,12},{12,8},{1,5},{5,1},{9,13},{13,9},{2,6},{6,2},{1... | collective-permute-start | bytes 1179656 | tf_op jit(solution)/shard_map/ppermute | solution.py:270
  32.5 2.3 %shard_map.60.refs_0_ = f32[8,8,48,128]{3,2,1,0:T(8,128)S(1)} custom-call(f32[8,8,64,128]{3,2,1,0:T(8,128)S(1)} %get-tuple-element.63.refs_0_.refs_5_, bf16[8,4,48,128]{3,2,1,0:T(8,128)(2,1)S(1)} %collective-permute-done.13.refs_1_, bf16[8,8,48,256]{3,2,1,0:T(8,128)(2,1)S(1)} %copy-done.1, f32[64,48]{1,0:T(8,128)S(1)} %bitcast.15, f32[4,64,48]{2,1,0:T(8,128)S(1)} %bitcast.7, ...), custom_call_target="tpu_custom_call" | custom-call | tf_op jit(solution)/shard_map/pallas_call | solution.py:183
  36.1 4.1 %collective-permute-start.17 = (bf16[4,8,48,128]{3,2,1,0:T(8,128)(2,1)S(1)}, bf16[4,8,48,128]{3,2,1,0:T(8,128)(2,1)S(1)}, u32[]{:S(2)}, u32[]{:S(2)}) collective-permute-start(bf16[4,8,48,128]{3,2,1,0:T(8,128)(2,1)S(1)} %get-tuple-element.69), channel_id=1, source_target_pairs={{0,4},{4,0},{8,12},{12,8},{1,5},{5,1},{9,13},{13,9},{2,6},{6,2},{1... | collective-permute-start | bytes 1179656 | tf_op jit(solution)/shard_map/ppermute | solution.py:270
  40.9 2.3 %shard_map.53.refs_0_ = f32[8,8,48,128]{3,2,1,0:T(8,128)S(1)} custom-call(f32[8,8,64,128]{3,2,1,0:T(8,128)S(1)} %get-tuple-element.49.refs_0_.refs_5_, bf16[8,4,48,128]{3,2,1,0:T(8,128)(2,1)S(1)} %collective-permute-done.3.refs_1_, bf16[8,8,48,256]{3,2,1,0:T(8,128)(2,1)S(1)} %copy-done.1, f32[64,48]{1,0:T(8,128)S(1)} %bitcast.17, f32[4,64,48]{2,1,0:T(8,128)S(1)} %bitcast.8, ...), custom_call_target="tpu_custom_call" | custom-call | tf_op jit(solution)/shard_map/pallas_call | solution.py:183
  44.5 4.1 %collective-permute-start.7 = (bf16[4,8,48,128]{3,2,1,0:T(8,128)(2,1)S(1)}, bf16[4,8,48,128]{3,2,1,0:T(8,128)(2,1)S(1)}, u32[]{:S(2)}, u32[]{:S(2)}) collective-permute-start(bf16[4,8,48,128]{3,2,1,0:T(8,128)(2,1)S(1)} %get-tuple-element.55), channel_id=1, source_target_pairs={{0,4},{4,0},{8,12},{12,8},{1,5},{5,1},{9,13},{13,9},{2,6},{6,2},{1... | collective-permute-start | bytes 1179656 | tf_op jit(solution)/shard_map/ppermute | solution.py:270
  49.3 2.3 %shard_map.62.refs_0_ = f32[8,8,48,128]{3,2,1,0:T(8,128)S(1)} custom-call(f32[8,8,64,128]{3,2,1,0:T(8,128)S(1)} %get-tuple-element.67.refs_0_, bf16[8,4,48,128]{3,2,1,0:T(8,128)(2,1)S(1)} %collective-permute-done.16.refs_1_, bf16[8,8,48,256]{3,2,1,0:T(8,128)(2,1)S(1)} %copy-done.1, f32[64,48]{1,0:T(8,128)S(1)} %bitcast.19, f32[4,64,48]{2,1,0:T(8,128)S(1)} %bitcast.9, ...), custom_call_target="tpu_custom_call" | custom-call | tf_op jit(solution)/shard_map/pallas_call | solution.py:183
  52.6 1.6 %collective-permute-start.19 = (bf16[4,8,48,128]{3,2,1,0:T(8,128)(2,1)S(1)}, bf16[4,8,48,128]{3,2,1,0:T(8,128)(2,1)S(1)}, u32[]{:S(2)}, u32[]{:S(2)}) collective-permute-start(bf16[4,8,48,128]{3,2,1,0:T(8,128)(2,1)S(1)} %get-tuple-element.72.sent1), channel_id=1, source_target_pairs={{0,2},{2,0},{1,3},{3,1},{4,6},{6,4},{5,7},{7,5},{8,10},{10,8},{9,1... | collective-permute-start | bytes 1179656 | tf_op jit(solution)/shard_map/ppermute | solution.py:270
  54.1 2.2 %shard_map.55.refs_0_ = f32[8,8,48,128]{3,2,1,0:T(8,128)S(1)} custom-call(f32[8,8,64,128]{3,2,1,0:T(8,128)S(1)} %get-tuple-element.53.refs_0_, bf16[8,4,48,128]{3,2,1,0:T(8,128)(2,1)S(1)} %collective-permute-done.6.refs_1_, bf16[8,8,48,256]{3,2,1,0:T(8,128)(2,1)S(1)} %copy-done.1, f32[64,48]{1,0:T(8,128)S(1)} %bitcast.21, f32[4,64,48]{2,1,0:T(8,128)S(1)} %bitcast.10, ...), custom_call_target="tpu_custom_call" | custom-call | tf_op jit(solution)/shard_map/pallas_call | solution.py:183
  56.4 2.6 %collective-permute-done.7.refs_1_ = bf16[4,8,48,128]{3,2,1,0:T(8,128)(2,1)S(1)} collective-permute-done((bf16[4,8,48,128]{3,2,1,0:T(8,128)(2,1)S(1)}, bf16[4,8,48,128]{3,2,1,0:T(8,128)(2,1)S(1)}, u32[]{:S(2)}, u32[]{:S(2)}) %collective-permute-start.7) | collective-permute-done | bytes 393248 | tf_op jit(solution)/shard_map/ppermute | solution.py:270
  60.0 1.7 %collective-permute-start.9 = (bf16[4,8,48,128]{3,2,1,0:T(8,128)(2,1)S(1)}, bf16[4,8,48,128]{3,2,1,0:T(8,128)(2,1)S(1)}, u32[]{:S(2)}, u32[]{:S(2)}) collective-permute-start(bf16[4,8,48,128]{3,2,1,0:T(8,128)(2,1)S(1)} %get-tuple-element.58.sent0), channel_id=1, source_target_pairs={{0,2},{2,0},{1,3},{3,1},{4,6},{6,4},{5,7},{7,5},{8,10},{10,8},{9,1... | collective-permute-start | bytes 1179656 | tf_op jit(solution)/shard_map/ppermute | solution.py:270
  62.5 1.3 %collective-permute-done.20.got_ref = f32[264,128]{1,0:T(8,128)S(1)} collective-permute-done((f32[264,128]{1,0:T(8,128)S(1)}, f32[264,128]{1,0:T(8,128)S(1)}, u32[]{:S(2)}, u32[]{:S(2)}) %collective-permute-start.20) | collective-permute-done | bytes 135200 | tf_op jit(solution)/shard_map/ppermute | solution.py:270
  66.5 6.5 %collective-permute-start.23 = (bf16[128,128]{1,0:T(8,128)(2,1)S(1)}, bf16[128,128]{1,0:T(8,128)(2,1)S(1)}, u32[]{:S(2)}, u32[]{:S(2)}) collective-permute-start(bf16[128,128]{1,0:T(8,128)(2,1)S(1)} %get-tuple-element.77), channel_id=1, source_target_pairs={{4,0},{0,4},{14,10},{10,14},{5,1},{1,5},{15,11},{11,15},{20,16},{1... | collective-permute-start | bytes 98312 | tf_op jit(solution)/shard_map/ppermute | solution.py:532
  73.0 2.9 %collective-permute-done.22.refs_1_.refs_5_ = bf16[128,128]{1,0:T(8,128)(2,1)S(1)} collective-permute-done((bf16[128,128]{1,0:T(8,128)(2,1)S(1)}, bf16[128,128]{1,0:T(8,128)(2,1)S(1)}, u32[]{:S(2)}, u32[]{:S(2)}) %collective-permute-start.22) | collective-permute-done | bytes 32800 | tf_op jit(solution)/shard_map/ppermute | solution.py:532
  76.9 1.4 %collective-permute-done.24.got_ref = f32[384,128]{1,0:T(8,128)S(1)} collective-permute-done((f32[384,128]{1,0:T(8,128)S(1)}, f32[384,128]{1,0:T(8,128)S(1)}, u32[]{:S(2)}, u32[]{:S(2)}) %collective-permute-start.24) | collective-permute-done | bytes 196640 | tf_op jit(solution)/shard_map/ppermute | solution.py:270
  78.9 2.9 %collective-permute-start.26 = (bf16[144,128]{1,0:T(8,128)(2,1)S(1)}, bf16[144,128]{1,0:T(8,128)(2,1)S(1)}, u32[]{:S(2)}, u32[]{:S(2)}) collective-permute-start(bf16[144,128]{1,0:T(8,128)(2,1)S(1)} %get-tuple-element.83), channel_id=1, source_target_pairs={{0,12},{4,8},{8,4},{12,0},{1,13},{5,9},{9,5},{13,1},{2,14},{6,10},... | collective-permute-start | bytes 110600 | tf_op jit(solution)/shard_map/ppermute | solution.py:538
  81.9 3.0 %collective-permute-done.25.refs_0_ = bf16[144,128]{1,0:T(8,128)(2,1)S(1)} collective-permute-done((bf16[144,128]{1,0:T(8,128)(2,1)S(1)}, bf16[144,128]{1,0:T(8,128)(2,1)S(1)}, u32[]{:S(2)}, u32[]{:S(2)}) %collective-permute-start.25) | collective-permute-done | bytes 36896 | tf_op jit(solution)/shard_map/ppermute | solution.py:538
  87.0 3.2 %collective-permute-done.28.other_ref = bf16[272,128]{1,0:T(8,128)(2,1)S(1)} collective-permute-done((bf16[272,128]{1,0:T(8,128)(2,1)S(1)}, bf16[272,128]{1,0:T(8,128)(2,1)S(1)}, u32[]{:S(2)}, u32[]{:S(2)}) %collective-permute-start.28) | collective-permute-done | bytes 69664 | tf_op jit(solution)/shard_map/ppermute | solution.py:270
  90.6 1.3 %collective-permute-done.29.far_ref = f32[128,256]{1,0:T(8,128)S(1)} collective-permute-done((f32[128,256]{1,0:T(8,128)S(1)}, f32[128,256]{1,0:T(8,128)S(1)}, u32[]{:S(2)}, u32[]{:S(2)}) %collective-permute-start.29) | collective-permute-done | bytes 131104 | tf_op jit(solution)/shard_map/ppermute | solution.py:270
  (67 shorter events, 24.2 us)
Async XLA Ops:
  4.0 9.4 %collective-permute-start.10 = (bf16[8,4,48,128]{3,2,1,0:T(8,128)(2,1)S(1)}, bf16[8,4,48,128]{3,2,1,0:T(8,128)(2,1)S(1)}, u32[]{:S(2)}, u32[]{:S(2)}) collective-permute-start(bf16[8,4,48,128]{3,2,1,0:T(8,128)(2,1)S(1)} %get-tuple-element.60), channel_id=1, source_target_pairs={{0,1},{1,0},{2,3},{3,2},{4,5},{5,4},{6,7},{7,6},{8,9},{9,8},{10,11... | collective-permute-start | bytes 1179656 | tf_op jit(solution)/shard_map/ppermute | solution.py:270
  4.5 12.6 %collective-permute-start.11 = (bf16[4,8,48,128]{3,2,1,0:T(8,128)(2,1)S(1)}, bf16[4,8,48,128]{3,2,1,0:T(8,128)(2,1)S(1)}, u32[]{:S(2)}, u32[]{:S(2)}) collective-permute-start(bf16[4,8,48,128]{3,2,1,0:T(8,128)(2,1)S(1)} %get-tuple-element.61), channel_id=1, source_target_pairs={{0,4},{4,0},{8,12},{12,8},{1,5},{5,1},{9,13},{13,9},{2,6},{6,2},{1... | collective-permute-start | bytes 1179656 | tf_op jit(solution)/shard_map/ppermute | solution.py:270
  7.2 10.0 %collective-permute-start.12 = (bf16[4,8,48,128]{3,2,1,0:T(8,128)(2,1)S(1)}, bf16[4,8,48,128]{3,2,1,0:T(8,128)(2,1)S(1)}, u32[]{:S(2)}, u32[]{:S(2)}) collective-permute-start(bf16[4,8,48,128]{3,2,1,0:T(8,128)(2,1)S(1)} %get-tuple-element.62), channel_id=1, source_target_pairs={{4,8},{8,4},{5,9},{9,5},{6,10},{10,6},{7,11},{11,7},{20,24},{24,20... | collective-permute-start | bytes 1179656 | tf_op jit(solution)/shard_map/ppermute | solution.py:270
  8.9 14.4 %collective-permute-start = (bf16[8,4,48,128]{3,2,1,0:T(8,128)(2,1)S(1)}, bf16[8,4,48,128]{3,2,1,0:T(8,128)(2,1)S(1)}, u32[]{:S(2)}, u32[]{:S(2)}) collective-permute-start(bf16[8,4,48,128]{3,2,1,0:T(8,128)(2,1)S(1)} %get-tuple-element.46), channel_id=1, source_target_pairs={{0,1},{1,0},{2,3},{3,2},{4,5},{5,4},{6,7},{7,6},{8,9},{9,8},{10,11... | collective-permute-start | bytes 1179656 | tf_op jit(solution)/shard_map/ppermute | solution.py:270
  9.1 17.1 %collective-permute-start.1 = (bf16[4,8,48,128]{3,2,1,0:T(8,128)(2,1)S(1)}, bf16[4,8,48,128]{3,2,1,0:T(8,128)(2,1)S(1)}, u32[]{:S(2)}, u32[]{:S(2)}) collective-permute-start(bf16[4,8,48,128]{3,2,1,0:T(8,128)(2,1)S(1)} %get-tuple-element.47), channel_id=1, source_target_pairs={{0,4},{4,0},{8,12},{12,8},{1,5},{5,1},{9,13},{13,9},{2,6},{6,2},{1... | collective-permute-start | bytes 1179656 | tf_op jit(solution)/shard_map/ppermute | solution.py:270
  13.4 12.8 %collective-permute-start.2 = (bf16[4,8,48,128]{3,2,1,0:T(8,128)(2,1)S(1)}, bf16[4,8,48,128]{3,2,1,0:T(8,128)(2,1)S(1)}, u32[]{:S(2)}, u32[]{:S(2)}) collective-permute-start(bf16[4,8,48,128]{3,2,1,0:T(8,128)(2,1)S(1)} %get-tuple-element.48), channel_id=1, source_target_pairs={{4,8},{8,4},{5,9},{9,5},{6,10},{10,6},{7,11},{11,7},{20,24},{24,20... | collective-permute-start | bytes 1179656 | tf_op jit(solution)/shard_map/ppermute | solution.py:270
  18.2 13.5 %collective-permute-start.13 = (bf16[8,4,48,128]{3,2,1,0:T(8,128)(2,1)S(1)}, bf16[8,4,48,128]{3,2,1,0:T(8,128)(2,1)S(1)}, u32[]{:S(2)}, u32[]{:S(2)}) collective-permute-start(bf16[8,4,48,128]{3,2,1,0:T(8,128)(2,1)S(1)} %get-tuple-element.64), channel_id=1, source_target_pairs={{0,1},{1,0},{2,3},{3,2},{4,5},{5,4},{6,7},{7,6},{8,9},{9,8},{10,11... | collective-permute-start | bytes 1179656 | tf_op jit(solution)/shard_map/ppermute | solution.py:270
  18.3 16.4 %collective-permute-start.14 = (bf16[4,8,48,128]{3,2,1,0:T(8,128)(2,1)S(1)}, bf16[4,8,48,128]{3,2,1,0:T(8,128)(2,1)S(1)}, u32[]{:S(2)}, u32[]{:S(2)}) collective-permute-start(bf16[4,8,48,128]{3,2,1,0:T(8,128)(2,1)S(1)} %get-tuple-element.65), channel_id=1, source_target_pairs={{0,4},{4,0},{8,12},{12,8},{1,5},{5,1},{9,13},{13,9},{2,6},{6,2},{1... | collective-permute-start | bytes 1179656 | tf_op jit(solution)/shard_map/ppermute | solution.py:270
  23.4 11.4 %collective-permute-start.15 = (bf16[4,8,48,128]{3,2,1,0:T(8,128)(2,1)S(1)}, bf16[4,8,48,128]{3,2,1,0:T(8,128)(2,1)S(1)}, u32[]{:S(2)}, u32[]{:S(2)}) collective-permute-start(bf16[4,8,48,128]{3,2,1,0:T(8,128)(2,1)S(1)} %get-tuple-element.66), channel_id=1, source_target_pairs={{4,8},{8,4},{5,9},{9,5},{6,10},{10,6},{7,11},{11,7},{20,24},{24,20... | collective-permute-start | bytes 1179656 | tf_op jit(solution)/shard_map/ppermute | solution.py:270
  27.3 12.9 %collective-permute-start.3 = (bf16[8,4,48,128]{3,2,1,0:T(8,128)(2,1)S(1)}, bf16[8,4,48,128]{3,2,1,0:T(8,128)(2,1)S(1)}, u32[]{:S(2)}, u32[]{:S(2)}) collective-permute-start(bf16[8,4,48,128]{3,2,1,0:T(8,128)(2,1)S(1)} %get-tuple-element.50), channel_id=1, source_target_pairs={{0,1},{1,0},{2,3},{3,2},{4,5},{5,4},{6,7},{7,6},{8,9},{9,8},{10,11... | collective-permute-start | bytes 1179656 | tf_op jit(solution)/shard_map/ppermute | solution.py:270
  27.6 15.6 %collective-permute-start.4 = (bf16[4,8,48,128]{3,2,1,0:T(8,128)(2,1)S(1)}, bf16[4,8,48,128]{3,2,1,0:T(8,128)(2,1)S(1)}, u32[]{:S(2)}, u32[]{:S(2)}) collective-permute-start(bf16[4,8,48,128]{3,2,1,0:T(8,128)(2,1)S(1)} %get-tuple-element.51), channel_id=1, source_target_pairs={{0,4},{4,0},{8,12},{12,8},{1,5},{5,1},{9,13},{13,9},{2,6},{6,2},{1... | collective-permute-start | bytes 1179656 | tf_op jit(solution)/shard_map/ppermute | solution.py:270
  31.8 11.4 %collective-permute-start.5 = (bf16[4,8,48,128]{3,2,1,0:T(8,128)(2,1)S(1)}, bf16[4,8,48,128]{3,2,1,0:T(8,128)(2,1)S(1)}, u32[]{:S(2)}, u32[]{:S(2)}) collective-permute-start(bf16[4,8,48,128]{3,2,1,0:T(8,128)(2,1)S(1)} %get-tuple-element.52), channel_id=1, source_target_pairs={{4,8},{8,4},{5,9},{9,5},{6,10},{10,6},{7,11},{11,7},{20,24},{24,20... | collective-permute-start | bytes 1179656 | tf_op jit(solution)/shard_map/ppermute | solution.py:270
  35.9 12.8 %collective-permute-start.16 = (bf16[8,4,48,128]{3,2,1,0:T(8,128)(2,1)S(1)}, bf16[8,4,48,128]{3,2,1,0:T(8,128)(2,1)S(1)}, u32[]{:S(2)}, u32[]{:S(2)}) collective-permute-start(bf16[8,4,48,128]{3,2,1,0:T(8,128)(2,1)S(1)} %get-tuple-element.68), channel_id=1, source_target_pairs={{0,1},{1,0},{2,3},{3,2},{4,5},{5,4},{6,7},{7,6},{8,9},{9,8},{10,11... | collective-permute-start | bytes 1179656 | tf_op jit(solution)/shard_map/ppermute | solution.py:270
  36.1 15.5 %collective-permute-start.17 = (bf16[4,8,48,128]{3,2,1,0:T(8,128)(2,1)S(1)}, bf16[4,8,48,128]{3,2,1,0:T(8,128)(2,1)S(1)}, u32[]{:S(2)}, u32[]{:S(2)}) collective-permute-start(bf16[4,8,48,128]{3,2,1,0:T(8,128)(2,1)S(1)} %get-tuple-element.69), channel_id=1, source_target_pairs={{0,4},{4,0},{8,12},{12,8},{1,5},{5,1},{9,13},{13,9},{2,6},{6,2},{1... | collective-permute-start | bytes 1179656 | tf_op jit(solution)/shard_map/ppermute | solution.py:270
  40.2 11.4 %collective-permute-start.18 = (bf16[4,8,48,128]{3,2,1,0:T(8,128)(2,1)S(1)}, bf16[4,8,48,128]{3,2,1,0:T(8,128)(2,1)S(1)}, u32[]{:S(2)}, u32[]{:S(2)}) collective-permute-start(bf16[4,8,48,128]{3,2,1,0:T(8,128)(2,1)S(1)} %get-tuple-element.70), channel_id=1, source_target_pairs={{4,8},{8,4},{5,9},{9,5},{6,10},{10,6},{7,11},{11,7},{20,24},{24,20... | collective-permute-start | bytes 1179656 | tf_op jit(solution)/shard_map/ppermute | solution.py:270
  44.3 9.9 %collective-permute-start.6 = (bf16[8,4,48,128]{3,2,1,0:T(8,128)(2,1)S(1)}, bf16[8,4,48,128]{3,2,1,0:T(8,128)(2,1)S(1)}, u32[]{:S(2)}, u32[]{:S(2)}) collective-permute-start(bf16[8,4,48,128]{3,2,1,0:T(8,128)(2,1)S(1)} %get-tuple-element.54), channel_id=1, source_target_pairs={{0,1},{1,0},{2,3},{3,2},{4,5},{5,4},{6,7},{7,6},{8,9},{9,8},{10,11... | collective-permute-start | bytes 1179656 | tf_op jit(solution)/shard_map/ppermute | solution.py:270
  44.5 14.5 %collective-permute-start.7 = (bf16[4,8,48,128]{3,2,1,0:T(8,128)(2,1)S(1)}, bf16[4,8,48,128]{3,2,1,0:T(8,128)(2,1)S(1)}, u32[]{:S(2)}, u32[]{:S(2)}) collective-permute-start(bf16[4,8,48,128]{3,2,1,0:T(8,128)(2,1)S(1)} %get-tuple-element.55), channel_id=1, source_target_pairs={{0,4},{4,0},{8,12},{12,8},{1,5},{5,1},{9,13},{13,9},{2,6},{6,2},{1... | collective-permute-start | bytes 1179656 | tf_op jit(solution)/shard_map/ppermute | solution.py:270
  48.6 10.4 %collective-permute-start.8 = (bf16[4,8,48,128]{3,2,1,0:T(8,128)(2,1)S(1)}, bf16[4,8,48,128]{3,2,1,0:T(8,128)(2,1)S(1)}, u32[]{:S(2)}, u32[]{:S(2)}) collective-permute-start(bf16[4,8,48,128]{3,2,1,0:T(8,128)(2,1)S(1)} %get-tuple-element.56), channel_id=1, source_target_pairs={{4,8},{8,4},{5,9},{9,5},{6,10},{10,6},{7,11},{11,7},{20,24},{24,20... | collective-permute-start | bytes 1179656 | tf_op jit(solution)/shard_map/ppermute | solution.py:270
  52.6 23.3 %collective-permute-start.19 = (bf16[4,8,48,128]{3,2,1,0:T(8,128)(2,1)S(1)}, bf16[4,8,48,128]{3,2,1,0:T(8,128)(2,1)S(1)}, u32[]{:S(2)}, u32[]{:S(2)}) collective-permute-start(bf16[4,8,48,128]{3,2,1,0:T(8,128)(2,1)S(1)} %get-tuple-element.72.sent1), channel_id=1, source_target_pairs={{0,2},{2,0},{1,3},{3,1},{4,6},{6,4},{5,7},{7,5},{8,10},{10,8},{9,1... | collective-permute-start | bytes 1179656 | tf_op jit(solution)/shard_map/ppermute | solution.py:270
  60.0 15.9 %collective-permute-start.9 = (bf16[4,8,48,128]{3,2,1,0:T(8,128)(2,1)S(1)}, bf16[4,8,48,128]{3,2,1,0:T(8,128)(2,1)S(1)}, u32[]{:S(2)}, u32[]{:S(2)}) collective-permute-start(bf16[4,8,48,128]{3,2,1,0:T(8,128)(2,1)S(1)} %get-tuple-element.58.sent0), channel_id=1, source_target_pairs={{0,2},{2,0},{1,3},{3,1},{4,6},{6,4},{5,7},{7,5},{8,10},{10,8},{9,1... | collective-permute-start | bytes 1179656 | tf_op jit(solution)/shard_map/ppermute | solution.py:270
  63.9 9.1 %collective-permute-start.21 = (bf16[128,128]{1,0:T(8,128)(2,1)S(1)}, bf16[128,128]{1,0:T(8,128)(2,1)S(1)}, u32[]{:S(2)}, u32[]{:S(2)}) collective-permute-start(bf16[128,128]{1,0:T(8,128)(2,1)S(1)} %get-tuple-element.75), channel_id=1, source_target_pairs={{8,0},{12,4},{2,10},{6,14},{9,1},{13,5},{3,11},{7,15},{24,16},{28,... | collective-permute-start | bytes 98312 | tf_op jit(solution)/shard_map/ppermute | solution.py:532
  65.2 10.7 %collective-permute-start.22 = (bf16[128,128]{1,0:T(8,128)(2,1)S(1)}, bf16[128,128]{1,0:T(8,128)(2,1)S(1)}, u32[]{:S(2)}, u32[]{:S(2)}) collective-permute-start(bf16[128,128]{1,0:T(8,128)(2,1)S(1)} %get-tuple-element.76), channel_id=1, source_target_pairs={{12,0},{8,4},{6,10},{2,14},{13,1},{9,5},{7,11},{3,15},{28,16},{24,... | collective-permute-start | bytes 98312 | tf_op jit(solution)/shard_map/ppermute | solution.py:532
  66.5 9.4 %collective-permute-start.23 = (bf16[128,128]{1,0:T(8,128)(2,1)S(1)}, bf16[128,128]{1,0:T(8,128)(2,1)S(1)}, u32[]{:S(2)}, u32[]{:S(2)}) collective-permute-start(bf16[128,128]{1,0:T(8,128)(2,1)S(1)} %get-tuple-element.77), channel_id=1, source_target_pairs={{4,0},{0,4},{14,10},{10,14},{5,1},{1,5},{15,11},{11,15},{20,16},{1... | collective-permute-start | bytes 98312 | tf_op jit(solution)/shard_map/ppermute | solution.py:532
  78.3 6.5 %collective-permute-start.25 = (bf16[144,128]{1,0:T(8,128)(2,1)S(1)}, bf16[144,128]{1,0:T(8,128)(2,1)S(1)}, u32[]{:S(2)}, u32[]{:S(2)}) collective-permute-start(bf16[144,128]{1,0:T(8,128)(2,1)S(1)} %get-tuple-element.82), channel_id=1, source_target_pairs={{0,8},{4,12},{8,0},{12,4},{1,9},{5,13},{9,1},{13,5},{2,10},{6,14},... | collective-permute-start | bytes 110600 | tf_op jit(solution)/shard_map/ppermute | solution.py:538
  (11 other events, 47.6 us)

commit v9 on v8

--- a/solution.py
+++ b/solution.py
@@ -19,9 +19,12 @@
 VMEM_LIMIT = 32 * 1024 * 1024
 
 
-def params(*semantics):
-    return pltpu.CompilerParams(
-        dimension_semantics=semantics or None, vmem_limit_bytes=VMEM_LIMIT
+def call(body, **options):
+    return pl.pallas_call(
+        body,
+        compiler_params=pltpu.CompilerParams(vmem_limit_bytes=VMEM_LIMIT),
+        cost_estimate=pl.CostEstimate(flops=1, bytes_accessed=1, transcendentals=0),
+        **options,
     )
 
 
@@ -83,7 +86,7 @@
     lax.fori_loop(0, along // TILE, one, 0)
 
 
-def first_body(chunk, p_ref, s_ref, u_ref, even_ref, odd_ref, edge_ref, square, turned_s):
+def first_body(chunk, p_ref, s_ref, u_ref, odd_ref, even_ref, edge_ref, square, turned_s):
     depth, across, padded, _ = u_ref.shape
     along = padded - 2 * EDGE
     core = lax.axis_index("sub")
@@ -114,7 +117,7 @@
 
 def first_field(probes, chunk, source):
     depth, across, along, _ = probes.shape
-    return pl.pallas_call(
+    return call(
         functools.partial(first_body, chunk),
         in_specs=whole_vmem(2),
         out_specs=whole_vmem(4),
@@ -125,7 +128,6 @@
             shape_of(depth, RADIUS, along, BF16),
         ],
         scratch_shapes=square_scratch(),
-        compiler_params=params(),
     )(probes, source)
 
 
@@ -180,13 +182,12 @@
     operands = [u, beside, probes, courant, source]
     if previous is not None:
         operands.append(previous)
-    return pl.pallas_call(
+    return call(
         functools.partial(local_body, chunk, moment, previous is not None),
         in_specs=whole_vmem(len(operands)),
         out_specs=whole_vmem(1)[0],
         out_shape=shape_of(depth, across, along, F32),
         scratch_shapes=square_scratch() + square_scratch()[:1],
-        compiler_params=params(),
     )(*operands)
 
 
@@ -228,7 +229,7 @@
             if kind == "middle":
                 for z, new in enumerate(news):
                     outs[0][z, x, rows] = new
-                store_edges(x, span, news, even, outs[1], outs[2])
+                store_edges(x, span, news, even, outs[2], outs[1])
             elif kind == "half":
                 for z in range(depth // 2):
                     one, two = news[z].astype(BF16), news[z + depth // 2].astype(BF16)
@@ -256,13 +257,12 @@
         out_shape = [shape_of(depth // 2, across, along, BF16)] * 2
     else:
         out_shape = [shape_of(depth, across, along, BF16)]
-    return pl.pallas_call(
+    return call(
         functools.partial(rim_body, kind),
         in_specs=whole_vmem(4),
         out_specs=whole_vmem(len(out_shape)),
         out_shape=out_shape,
         scratch_shapes=square_scratch(),
-        compiler_params=params(),
     )(base, evens, odds, courant)
 
 
@@ -328,13 +328,12 @@
     size = 2 * LANES
     cells = 2 * math.prod(fields[0].shape[:3])
     half = jax.ShapeDtypeStruct((size + 8, LANES), F32)
-    return pl.pallas_call(
+    return call(
         inner_body,
         in_specs=whole_vmem(4),
         out_specs=whole_vmem(2),
         out_shape=[half, half],
         scratch_shapes=[pltpu.VMEM((cells, size), BF16)],
-        compiler_params=params(),
     )(*fields)
 
 
@@ -351,12 +350,11 @@
 def inner_rows(keep, got, slabs):
     own = jax.ShapeDtypeStruct((LANES, LANES), F32)
     sent = jax.ShapeDtypeStruct((LANES, LANES), BF16)
-    return pl.pallas_call(
+    return call(
         inner_rows_body,
         in_specs=whole_vmem(2),
         out_specs=whole_vmem(1 + slabs),
         out_shape=[jax.ShapeDtypeStruct((8, LANES), F32), own] + [sent] * (slabs - 1),
-        compiler_params=params(),
     )(keep, got)
 
 
@@ -382,13 +380,12 @@
 def cross_gram(fields, after):
     cells = math.prod(fields[0].shape[:3])
     three = jax.ShapeDtypeStruct((3 * LANES, LANES), F32)
-    return pl.pallas_call(
+    return call(
         cross_body,
         in_specs=whole_vmem(4) + [pl.BlockSpec(memory_space=pl.ANY)] * len(after),
         out_specs=whole_vmem(2),
         out_shape=[three, three],
         scratch_shapes=[pltpu.VMEM((cells, 4 * LANES), BF16)],
-        compiler_params=params(),
     )(*fields, *after)
 
 
@@ -425,12 +422,11 @@
 def cross_rows(keep, got, tail, slabs):
     own = jax.ShapeDtypeStruct((LANES + 8, LANES), F32)
     sent = jax.ShapeDtypeStruct((LANES + 16, LANES), BF16)
-    return pl.pallas_call(
+    return call(
         cross_rows_body,
         in_specs=whole_vmem(3),
         out_specs=whole_vmem(slabs),
         out_shape=[own] + [sent] * (slabs - 1),
-        compiler_params=params(),
     )(keep, got, tail)
 
 
@@ -449,12 +445,11 @@
 
 def sum_all(own, others, inner, inner_others):
     slabs = 1 + len(others)
-    return pl.pallas_call(
+    return call(
         functools.partial(sum_body, slabs),
         in_specs=whole_vmem(2 * slabs),
         out_specs=whole_vmem(1)[0],
         out_shape=jax.ShapeDtypeStruct((2 * LANES + 16, LANES), BF16),
-        compiler_params=params(),
     )(own, *others, inner, *inner_others)
 
 
@@ -486,7 +481,7 @@
 
 
 def normalise(mine, other, cell_count):
-    return pl.pallas_call(
+    return call(
         functools.partial(normalise_body, cell_count),
         in_specs=whole_vmem(2),
         out_specs=whole_vmem(2),
@@ -494,7 +489,6 @@
             jax.ShapeDtypeStruct((LANES, 2 * LANES), F32),
             jax.ShapeDtypeStruct((1, LANES), F32),
         ],
-        compiler_params=params(),
     )(mine, other)
 
 
@@ -508,12 +502,11 @@
 
 
 def assemble(near, far):
-    return pl.pallas_call(
+    return call(
         assemble_body,
         in_specs=whole_vmem(2),
         out_specs=whole_vmem(1)[0],
         out_shape=jax.ShapeDtypeStruct((near.shape[0], 4 * LANES), F32),
-        compiler_params=params(),
     )(near, far)
 
 
@@ -575,7 +568,7 @@
     courant = courant.reshape(depth * across, along)
     source = source.reshape(steps, depth * across, along)
 
-    exchange = lambda even, odd, edge: (even_swap(even), odd_swap(odd), core_swap(edge))
+    exchange = lambda odd, even, edge: (odd_swap(odd), even_swap(even), core_swap(edge))
     now, previous, halos = [], [None] * chunks, []
     for c in range(chunks):
         u, *edges = first_field(probes, c, source)
@@ -584,7 +577,7 @@
     finals = []
     for n in range(1, steps):
         for c in range(chunks):
-            even, odd, beside = halos[c]
+            odd, even, beside = halos[c]
             base = local_step(now[c], beside, probes, c, courant, source, n, previous[c])
             if n < steps - 1:
                 u, *edges = rim_step(base, even, odd, courant, "middle")

time: 93.1 us -> 93.1 us (level)
  no operation moved by 1% of the time
where the time goes in v9:
time: 93.1 us; the launch traced here: 92.7 us
  starting transfers between devices  47.3 us (51%)
  Pallas kernels  24.7 us (27%)
  waiting for transfers between devices  17.5 us (19%)
  local copies, waits for them, and re-layouts  2.32 us (2%)
  between operations  1 us (1%)
    ppermute x24, starting transfers between devices, swap(): lax.ppermute(x, axis, [p for a, b in pairs for p in ((a, b), (b, a))])  34.6 us
    pallas_call x6, Pallas kernels, local_step(): call(functools.partial(local_body, chunk, moment, previous is not None),...  13.3 us
    ppermute x24, waiting for transfers between devices, swap(): lax.ppermute(x, axis, [p for a, b in pairs for p in ((a, b), (b, a))])  10.8 us
    ppermute x3, starting transfers between devices, coupled(): inner_arrived.append(lax.ppermute(inner[d], ('slab', 'probe'), pairs))  9.09 us
    pallas_call x6, Pallas kernels, rim_step(): call(functools.partial(rim_body, kind), in_specs=whole_vmem(4), out_specs...  6.32 us
    ppermute x3, waiting for transfers between devices, coupled(): lax.ppermute(blocks[d - 1], 'slab', [(i, i ^ d) for i in range(slabs)])  3.79 us
    ppermute x3, starting transfers between devices, coupled(): lax.ppermute(blocks[d - 1], 'slab', [(i, i ^ d) for i in range(slabs)])  3.55 us
    ppermute x3, waiting for transfers between devices, coupled(): inner_arrived.append(lax.ppermute(inner[d], ('slab', 'probe'), pairs))  2.92 us
  transfers between devices with their start and end apart: 30, of which 9 were waited for; matrix products, arithmetic and copies ran while one was open for 0% of the time, Pallas kernels for 23%

profile of v9, /device:TPU:0, one launch (start us, length us, event | category | flops | bytes accessed | tf_op | source)
XLA Modules:
  0.0 92.7 jit_solution(9990513455959655013)
XLA Ops:
  0.6 1.4 %copy-done = bf16[8,8,48,256]{3,2,1,0:T(8,128)(2,1)S(1)} copy-done((bf16[8,8,48,256]{3,2,1,0:T(8,128)(2,1)S(1)}, bf16[8,8,48,256]{3,2,1,0:T(8,128)(2,1)}, u32[]{:S(2)}) %copy-start) | copy-done | bytes 1572888
  4.5 2.7 %collective-permute-start.11 = (bf16[4,8,48,128]{3,2,1,0:T(8,128)(2,1)S(1)}, bf16[4,8,48,128]{3,2,1,0:T(8,128)(2,1)S(1)}, u32[]{:S(2)}, u32[]{:S(2)}) collective-permute-start(bf16[4,8,48,128]{3,2,1,0:T(8,128)(2,1)S(1)} %get-tuple-element.61), channel_id=1, source_target_pairs={{0,4},{4,0},{8,12},{12,8},{1,5},{5,1},{9,13},{13,9},{2,6},{6,2},{1... | collective-permute-start | bytes 1179656 | tf_op jit(solution)/shard_map/ppermute | solution.py:270
  9.1 4.3 %collective-permute-start.1 = (bf16[4,8,48,128]{3,2,1,0:T(8,128)(2,1)S(1)}, bf16[4,8,48,128]{3,2,1,0:T(8,128)(2,1)S(1)}, u32[]{:S(2)}, u32[]{:S(2)}) collective-permute-start(bf16[4,8,48,128]{3,2,1,0:T(8,128)(2,1)S(1)} %get-tuple-element.47), channel_id=1, source_target_pairs={{0,4},{4,0},{8,12},{12,8},{1,5},{5,1},{9,13},{13,9},{2,6},{6,2},{1... | collective-permute-start | bytes 1179656 | tf_op jit(solution)/shard_map/ppermute | solution.py:270
  14.1 2.2 %shard_map.58.refs_0_ = f32[8,8,48,128]{3,2,1,0:T(8,128)S(1)} custom-call(f32[8,8,64,128]{3,2,1,0:T(8,128)S(1)} %get-tuple-element.59.refs_0_.refs_5_, bf16[8,4,48,128]{3,2,1,0:T(8,128)(2,1)S(1)} %collective-permute-done.10.refs_1_, bf16[8,8,48,256]{3,2,1,0:T(8,128)(2,1)S(1)} %copy-done, f32[64,48]{1,0:T(8,128)S(1)} %bitcast.11, f32[4,64,48]{2,1,0:T(8,128)S(1)} %bitcast.5), custom_call_target="tpu_custom_call" | custom-call | flops 1 | bytes 1 | tf_op jit(solution)/shard_map/pallas_call | solution.py:185
  18.3 5.0 %collective-permute-start.14 = (bf16[4,8,48,128]{3,2,1,0:T(8,128)(2,1)S(1)}, bf16[4,8,48,128]{3,2,1,0:T(8,128)(2,1)S(1)}, u32[]{:S(2)}, u32[]{:S(2)}) collective-permute-start(bf16[4,8,48,128]{3,2,1,0:T(8,128)(2,1)S(1)} %get-tuple-element.65), channel_id=1, source_target_pairs={{0,4},{4,0},{8,12},{12,8},{1,5},{5,1},{9,13},{13,9},{2,6},{6,2},{1... | collective-permute-start | bytes 1179656 | tf_op jit(solution)/shard_map/ppermute | solution.py:270
  24.1 2.1 %shard_map.51.refs_0_ = f32[8,8,48,128]{3,2,1,0:T(8,128)S(1)} custom-call(f32[8,8,64,128]{3,2,1,0:T(8,128)S(1)} %get-tuple-element.45.refs_0_.refs_5_, bf16[8,4,48,128]{3,2,1,0:T(8,128)(2,1)S(1)} %collective-permute-done.refs_1_, bf16[8,8,48,256]{3,2,1,0:T(8,128)(2,1)S(1)} %copy-done.1, f32[64,48]{1,0:T(8,128)S(1)} %bitcast.13, f32[4,64,48]{2,1,0:T(8,128)S(1)} %bitcast.6), custom_call_target="tpu_custom_call" | custom-call | flops 1 | bytes 1 | tf_op jit(solution)/shard_map/pallas_call | solution.py:185
  27.6 4.2 %collective-permute-start.4 = (bf16[4,8,48,128]{3,2,1,0:T(8,128)(2,1)S(1)}, bf16[4,8,48,128]{3,2,1,0:T(8,128)(2,1)S(1)}, u32[]{:S(2)}, u32[]{:S(2)}) collective-permute-start(bf16[4,8,48,128]{3,2,1,0:T(8,128)(2,1)S(1)} %get-tuple-element.51), channel_id=1, source_target_pairs={{0,4},{4,0},{8,12},{12,8},{1,5},{5,1},{9,13},{13,9},{2,6},{6,2},{1... | collective-permute-start | bytes 1179656 | tf_op jit(solution)/shard_map/ppermute | solution.py:270
  32.5 2.3 %shard_map.60.refs_0_ = f32[8,8,48,128]{3,2,1,0:T(8,128)S(1)} custom-call(f32[8,8,64,128]{3,2,1,0:T(8,128)S(1)} %get-tuple-element.63.refs_0_.refs_5_, bf16[8,4,48,128]{3,2,1,0:T(8,128)(2,1)S(1)} %collective-permute-done.13.refs_1_, bf16[8,8,48,256]{3,2,1,0:T(8,128)(2,1)S(1)} %copy-done.1, f32[64,48]{1,0:T(8,128)S(1)} %bitcast.15, f32[4,64,48]{2,1,0:T(8,128)S(1)} %bitcast.7, ...), custom_call_target="tpu_custom_call" | custom-call | flops 1 | bytes 1 | tf_op jit(solution)/shard_map/pallas_call | solution.py:185
  36.1 4.1 %collective-permute-start.17 = (bf16[4,8,48,128]{3,2,1,0:T(8,128)(2,1)S(1)}, bf16[4,8,48,128]{3,2,1,0:T(8,128)(2,1)S(1)}, u32[]{:S(2)}, u32[]{:S(2)}) collective-permute-start(bf16[4,8,48,128]{3,2,1,0:T(8,128)(2,1)S(1)} %get-tuple-element.69), channel_id=1, source_target_pairs={{0,4},{4,0},{8,12},{12,8},{1,5},{5,1},{9,13},{13,9},{2,6},{6,2},{1... | collective-permute-start | bytes 1179656 | tf_op jit(solution)/shard_map/ppermute | solution.py:270
  40.9 2.3 %shard_map.53.refs_0_ = f32[8,8,48,128]{3,2,1,0:T(8,128)S(1)} custom-call(f32[8,8,64,128]{3,2,1,0:T(8,128)S(1)} %get-tuple-element.49.refs_0_.refs_5_, bf16[8,4,48,128]{3,2,1,0:T(8,128)(2,1)S(1)} %collective-permute-done.3.refs_1_, bf16[8,8,48,256]{3,2,1,0:T(8,128)(2,1)S(1)} %copy-done.1, f32[64,48]{1,0:T(8,128)S(1)} %bitcast.17, f32[4,64,48]{2,1,0:T(8,128)S(1)} %bitcast.8, ...), custom_call_target="tpu_custom_call" | custom-call | flops 1 | bytes 1 | tf_op jit(solution)/shard_map/pallas_call | solution.py:185
  44.5 4.1 %collective-permute-start.7 = (bf16[4,8,48,128]{3,2,1,0:T(8,128)(2,1)S(1)}, bf16[4,8,48,128]{3,2,1,0:T(8,128)(2,1)S(1)}, u32[]{:S(2)}, u32[]{:S(2)}) collective-permute-start(bf16[4,8,48,128]{3,2,1,0:T(8,128)(2,1)S(1)} %get-tuple-element.55), channel_id=1, source_target_pairs={{0,4},{4,0},{8,12},{12,8},{1,5},{5,1},{9,13},{13,9},{2,6},{6,2},{1... | collective-permute-start | bytes 1179656 | tf_op jit(solution)/shard_map/ppermute | solution.py:270
  49.3 2.3 %shard_map.62.refs_0_ = f32[8,8,48,128]{3,2,1,0:T(8,128)S(1)} custom-call(f32[8,8,64,128]{3,2,1,0:T(8,128)S(1)} %get-tuple-element.67.refs_0_, bf16[8,4,48,128]{3,2,1,0:T(8,128)(2,1)S(1)} %collective-permute-done.16.refs_1_, bf16[8,8,48,256]{3,2,1,0:T(8,128)(2,1)S(1)} %copy-done.1, f32[64,48]{1,0:T(8,128)S(1)} %bitcast.19, f32[4,64,48]{2,1,0:T(8,128)S(1)} %bitcast.9, ...), custom_call_target="tpu_custom_call" | custom-call | flops 1 | bytes 1 | tf_op jit(solution)/shard_map/pallas_call | solution.py:185
  52.6 1.6 %collective-permute-start.19 = (bf16[4,8,48,128]{3,2,1,0:T(8,128)(2,1)S(1)}, bf16[4,8,48,128]{3,2,1,0:T(8,128)(2,1)S(1)}, u32[]{:S(2)}, u32[]{:S(2)}) collective-permute-start(bf16[4,8,48,128]{3,2,1,0:T(8,128)(2,1)S(1)} %get-tuple-element.72.sent1), channel_id=1, source_target_pairs={{0,2},{2,0},{1,3},{3,1},{4,6},{6,4},{5,7},{7,5},{8,10},{10,8},{9,1... | collective-permute-start | bytes 1179656 | tf_op jit(solution)/shard_map/ppermute | solution.py:270
  54.1 2.2 %shard_map.55.refs_0_ = f32[8,8,48,128]{3,2,1,0:T(8,128)S(1)} custom-call(f32[8,8,64,128]{3,2,1,0:T(8,128)S(1)} %get-tuple-element.53.refs_0_, bf16[8,4,48,128]{3,2,1,0:T(8,128)(2,1)S(1)} %collective-permute-done.6.refs_1_, bf16[8,8,48,256]{3,2,1,0:T(8,128)(2,1)S(1)} %copy-done.1, f32[64,48]{1,0:T(8,128)S(1)} %bitcast.21, f32[4,64,48]{2,1,0:T(8,128)S(1)} %bitcast.10, ...), custom_call_target="tpu_custom_call" | custom-call | flops 1 | bytes 1 | tf_op jit(solution)/shard_map/pallas_call | solution.py:185
  56.4 2.6 %collective-permute-done.7.refs_1_ = bf16[4,8,48,128]{3,2,1,0:T(8,128)(2,1)S(1)} collective-permute-done((bf16[4,8,48,128]{3,2,1,0:T(8,128)(2,1)S(1)}, bf16[4,8,48,128]{3,2,1,0:T(8,128)(2,1)S(1)}, u32[]{:S(2)}, u32[]{:S(2)}) %collective-permute-start.7) | collective-permute-done | bytes 393248 | tf_op jit(solution)/shard_map/ppermute | solution.py:270
  60.0 1.7 %collective-permute-start.9 = (bf16[4,8,48,128]{3,2,1,0:T(8,128)(2,1)S(1)}, bf16[4,8,48,128]{3,2,1,0:T(8,128)(2,1)S(1)}, u32[]{:S(2)}, u32[]{:S(2)}) collective-permute-start(bf16[4,8,48,128]{3,2,1,0:T(8,128)(2,1)S(1)} %get-tuple-element.58.sent0), channel_id=1, source_target_pairs={{0,2},{2,0},{1,3},{3,1},{4,6},{6,4},{5,7},{7,5},{8,10},{10,8},{9,1... | collective-permute-start | bytes 1179656 | tf_op jit(solution)/shard_map/ppermute | solution.py:270
  62.5 1.3 %collective-permute-done.20.got_ref = f32[264,128]{1,0:T(8,128)S(1)} collective-permute-done((f32[264,128]{1,0:T(8,128)S(1)}, f32[264,128]{1,0:T(8,128)S(1)}, u32[]{:S(2)}, u32[]{:S(2)}) %collective-permute-start.20) | collective-permute-done | bytes 135200 | tf_op jit(solution)/shard_map/ppermute | solution.py:270
  66.5 6.5 %collective-permute-start.23 = (bf16[128,128]{1,0:T(8,128)(2,1)S(1)}, bf16[128,128]{1,0:T(8,128)(2,1)S(1)}, u32[]{:S(2)}, u32[]{:S(2)}) collective-permute-start(bf16[128,128]{1,0:T(8,128)(2,1)S(1)} %get-tuple-element.77), channel_id=1, source_target_pairs={{4,0},{0,4},{14,10},{10,14},{5,1},{1,5},{15,11},{11,15},{20,16},{1... | collective-permute-start | bytes 98312 | tf_op jit(solution)/shard_map/ppermute | solution.py:525
  73.0 2.9 %collective-permute-done.22.refs_1_.refs_5_ = bf16[128,128]{1,0:T(8,128)(2,1)S(1)} collective-permute-done((bf16[128,128]{1,0:T(8,128)(2,1)S(1)}, bf16[128,128]{1,0:T(8,128)(2,1)S(1)}, u32[]{:S(2)}, u32[]{:S(2)}) %collective-permute-start.22) | collective-permute-done | bytes 32800 | tf_op jit(solution)/shard_map/ppermute | solution.py:525
  76.9 1.4 %collective-permute-done.24.got_ref = f32[384,128]{1,0:T(8,128)S(1)} collective-permute-done((f32[384,128]{1,0:T(8,128)S(1)}, f32[384,128]{1,0:T(8,128)S(1)}, u32[]{:S(2)}, u32[]{:S(2)}) %collective-permute-start.24) | collective-permute-done | bytes 196640 | tf_op jit(solution)/shard_map/ppermute | solution.py:270
  78.9 2.9 %collective-permute-start.26 = (bf16[144,128]{1,0:T(8,128)(2,1)S(1)}, bf16[144,128]{1,0:T(8,128)(2,1)S(1)}, u32[]{:S(2)}, u32[]{:S(2)}) collective-permute-start(bf16[144,128]{1,0:T(8,128)(2,1)S(1)} %get-tuple-element.83), channel_id=1, source_target_pairs={{0,12},{4,8},{8,4},{12,0},{1,13},{5,9},{9,5},{13,1},{2,14},{6,10},... | collective-permute-start | bytes 110600 | tf_op jit(solution)/shard_map/ppermute | solution.py:531
  81.9 3.0 %collective-permute-done.25.refs_0_ = bf16[144,128]{1,0:T(8,128)(2,1)S(1)} collective-permute-done((bf16[144,128]{1,0:T(8,128)(2,1)S(1)}, bf16[144,128]{1,0:T(8,128)(2,1)S(1)}, u32[]{:S(2)}, u32[]{:S(2)}) %collective-permute-start.25) | collective-permute-done | bytes 36896 | tf_op jit(solution)/shard_map/ppermute | solution.py:531
  87.0 3.2 %collective-permute-done.28.other_ref = bf16[272,128]{1,0:T(8,128)(2,1)S(1)} collective-permute-done((bf16[272,128]{1,0:T(8,128)(2,1)S(1)}, bf16[272,128]{1,0:T(8,128)(2,1)S(1)}, u32[]{:S(2)}, u32[]{:S(2)}) %collective-permute-start.28) | collective-permute-done | bytes 69664 | tf_op jit(solution)/shard_map/ppermute | solution.py:270
  90.6 1.3 %collective-permute-done.29.far_ref = f32[128,256]{1,0:T(8,128)S(1)} collective-permute-done((f32[128,256]{1,0:T(8,128)S(1)}, f32[128,256]{1,0:T(8,128)S(1)}, u32[]{:S(2)}, u32[]{:S(2)}) %collective-permute-start.29) | collective-permute-done | bytes 131104 | tf_op jit(solution)/shard_map/ppermute | solution.py:270
  (67 shorter events, 24.2 us)
Async XLA Ops:
  4.0 9.4 %collective-permute-start.10 = (bf16[8,4,48,128]{3,2,1,0:T(8,128)(2,1)S(1)}, bf16[8,4,48,128]{3,2,1,0:T(8,128)(2,1)S(1)}, u32[]{:S(2)}, u32[]{:S(2)}) collective-permute-start(bf16[8,4,48,128]{3,2,1,0:T(8,128)(2,1)S(1)} %get-tuple-element.60), channel_id=1, source_target_pairs={{0,1},{1,0},{2,3},{3,2},{4,5},{5,4},{6,7},{7,6},{8,9},{9,8},{10,11... | collective-permute-start | bytes 1179656 | tf_op jit(solution)/shard_map/ppermute | solution.py:270
  4.5 12.6 %collective-permute-start.11 = (bf16[4,8,48,128]{3,2,1,0:T(8,128)(2,1)S(1)}, bf16[4,8,48,128]{3,2,1,0:T(8,128)(2,1)S(1)}, u32[]{:S(2)}, u32[]{:S(2)}) collective-permute-start(bf16[4,8,48,128]{3,2,1,0:T(8,128)(2,1)S(1)} %get-tuple-element.61), channel_id=1, source_target_pairs={{0,4},{4,0},{8,12},{12,8},{1,5},{5,1},{9,13},{13,9},{2,6},{6,2},{1... | collective-permute-start | bytes 1179656 | tf_op jit(solution)/shard_map/ppermute | solution.py:270
  7.2 10.0 %collective-permute-start.12 = (bf16[4,8,48,128]{3,2,1,0:T(8,128)(2,1)S(1)}, bf16[4,8,48,128]{3,2,1,0:T(8,128)(2,1)S(1)}, u32[]{:S(2)}, u32[]{:S(2)}) collective-permute-start(bf16[4,8,48,128]{3,2,1,0:T(8,128)(2,1)S(1)} %get-tuple-element.62), channel_id=1, source_target_pairs={{4,8},{8,4},{5,9},{9,5},{6,10},{10,6},{7,11},{11,7},{20,24},{24,20... | collective-permute-start | bytes 1179656 | tf_op jit(solution)/shard_map/ppermute | solution.py:270
  8.9 14.4 %collective-permute-start = (bf16[8,4,48,128]{3,2,1,0:T(8,128)(2,1)S(1)}, bf16[8,4,48,128]{3,2,1,0:T(8,128)(2,1)S(1)}, u32[]{:S(2)}, u32[]{:S(2)}) collective-permute-start(bf16[8,4,48,128]{3,2,1,0:T(8,128)(2,1)S(1)} %get-tuple-element.46), channel_id=1, source_target_pairs={{0,1},{1,0},{2,3},{3,2},{4,5},{5,4},{6,7},{7,6},{8,9},{9,8},{10,11... | collective-permute-start | bytes 1179656 | tf_op jit(solution)/shard_map/ppermute | solution.py:270
  9.1 17.1 %collective-permute-start.1 = (bf16[4,8,48,128]{3,2,1,0:T(8,128)(2,1)S(1)}, bf16[4,8,48,128]{3,2,1,0:T(8,128)(2,1)S(1)}, u32[]{:S(2)}, u32[]{:S(2)}) collective-permute-start(bf16[4,8,48,128]{3,2,1,0:T(8,128)(2,1)S(1)} %get-tuple-element.47), channel_id=1, source_target_pairs={{0,4},{4,0},{8,12},{12,8},{1,5},{5,1},{9,13},{13,9},{2,6},{6,2},{1... | collective-permute-start | bytes 1179656 | tf_op jit(solution)/shard_map/ppermute | solution.py:270
  13.4 12.8 %collective-permute-start.2 = (bf16[4,8,48,128]{3,2,1,0:T(8,128)(2,1)S(1)}, bf16[4,8,48,128]{3,2,1,0:T(8,128)(2,1)S(1)}, u32[]{:S(2)}, u32[]{:S(2)}) collective-permute-start(bf16[4,8,48,128]{3,2,1,0:T(8,128)(2,1)S(1)} %get-tuple-element.48), channel_id=1, source_target_pairs={{4,8},{8,4},{5,9},{9,5},{6,10},{10,6},{7,11},{11,7},{20,24},{24,20... | collective-permute-start | bytes 1179656 | tf_op jit(solution)/shard_map/ppermute | solution.py:270
  18.2 13.5 %collective-permute-start.13 = (bf16[8,4,48,128]{3,2,1,0:T(8,128)(2,1)S(1)}, bf16[8,4,48,128]{3,2,1,0:T(8,128)(2,1)S(1)}, u32[]{:S(2)}, u32[]{:S(2)}) collective-permute-start(bf16[8,4,48,128]{3,2,1,0:T(8,128)(2,1)S(1)} %get-tuple-element.64), channel_id=1, source_target_pairs={{0,1},{1,0},{2,3},{3,2},{4,5},{5,4},{6,7},{7,6},{8,9},{9,8},{10,11... | collective-permute-start | bytes 1179656 | tf_op jit(solution)/shard_map/ppermute | solution.py:270
  18.3 16.4 %collective-permute-start.14 = (bf16[4,8,48,128]{3,2,1,0:T(8,128)(2,1)S(1)}, bf16[4,8,48,128]{3,2,1,0:T(8,128)(2,1)S(1)}, u32[]{:S(2)}, u32[]{:S(2)}) collective-permute-start(bf16[4,8,48,128]{3,2,1,0:T(8,128)(2,1)S(1)} %get-tuple-element.65), channel_id=1, source_target_pairs={{0,4},{4,0},{8,12},{12,8},{1,5},{5,1},{9,13},{13,9},{2,6},{6,2},{1... | collective-permute-start | bytes 1179656 | tf_op jit(solution)/shard_map/ppermute | solution.py:270
  23.4 11.4 %collective-permute-start.15 = (bf16[4,8,48,128]{3,2,1,0:T(8,128)(2,1)S(1)}, bf16[4,8,48,128]{3,2,1,0:T(8,128)(2,1)S(1)}, u32[]{:S(2)}, u32[]{:S(2)}) collective-permute-start(bf16[4,8,48,128]{3,2,1,0:T(8,128)(2,1)S(1)} %get-tuple-element.66), channel_id=1, source_target_pairs={{4,8},{8,4},{5,9},{9,5},{6,10},{10,6},{7,11},{11,7},{20,24},{24,20... | collective-permute-start | bytes 1179656 | tf_op jit(solution)/shard_map/ppermute | solution.py:270
  27.3 12.9 %collective-permute-start.3 = (bf16[8,4,48,128]{3,2,1,0:T(8,128)(2,1)S(1)}, bf16[8,4,48,128]{3,2,1,0:T(8,128)(2,1)S(1)}, u32[]{:S(2)}, u32[]{:S(2)}) collective-permute-start(bf16[8,4,48,128]{3,2,1,0:T(8,128)(2,1)S(1)} %get-tuple-element.50), channel_id=1, source_target_pairs={{0,1},{1,0},{2,3},{3,2},{4,5},{5,4},{6,7},{7,6},{8,9},{9,8},{10,11... | collective-permute-start | bytes 1179656 | tf_op jit(solution)/shard_map/ppermute | solution.py:270
  27.6 15.6 %collective-permute-start.4 = (bf16[4,8,48,128]{3,2,1,0:T(8,128)(2,1)S(1)}, bf16[4,8,48,128]{3,2,1,0:T(8,128)(2,1)S(1)}, u32[]{:S(2)}, u32[]{:S(2)}) collective-permute-start(bf16[4,8,48,128]{3,2,1,0:T(8,128)(2,1)S(1)} %get-tuple-element.51), channel_id=1, source_target_pairs={{0,4},{4,0},{8,12},{12,8},{1,5},{5,1},{9,13},{13,9},{2,6},{6,2},{1... | collective-permute-start | bytes 1179656 | tf_op jit(solution)/shard_map/ppermute | solution.py:270
  31.8 11.4 %collective-permute-start.5 = (bf16[4,8,48,128]{3,2,1,0:T(8,128)(2,1)S(1)}, bf16[4,8,48,128]{3,2,1,0:T(8,128)(2,1)S(1)}, u32[]{:S(2)}, u32[]{:S(2)}) collective-permute-start(bf16[4,8,48,128]{3,2,1,0:T(8,128)(2,1)S(1)} %get-tuple-element.52), channel_id=1, source_target_pairs={{4,8},{8,4},{5,9},{9,5},{6,10},{10,6},{7,11},{11,7},{20,24},{24,20... | collective-permute-start | bytes 1179656 | tf_op jit(solution)/shard_map/ppermute | solution.py:270
  35.9 12.8 %collective-permute-start.16 = (bf16[8,4,48,128]{3,2,1,0:T(8,128)(2,1)S(1)}, bf16[8,4,48,128]{3,2,1,0:T(8,128)(2,1)S(1)}, u32[]{:S(2)}, u32[]{:S(2)}) collective-permute-start(bf16[8,4,48,128]{3,2,1,0:T(8,128)(2,1)S(1)} %get-tuple-element.68), channel_id=1, source_target_pairs={{0,1},{1,0},{2,3},{3,2},{4,5},{5,4},{6,7},{7,6},{8,9},{9,8},{10,11... | collective-permute-start | bytes 1179656 | tf_op jit(solution)/shard_map/ppermute | solution.py:270
  36.1 15.5 %collective-permute-start.17 = (bf16[4,8,48,128]{3,2,1,0:T(8,128)(2,1)S(1)}, bf16[4,8,48,128]{3,2,1,0:T(8,128)(2,1)S(1)}, u32[]{:S(2)}, u32[]{:S(2)}) collective-permute-start(bf16[4,8,48,128]{3,2,1,0:T(8,128)(2,1)S(1)} %get-tuple-element.69), channel_id=1, source_target_pairs={{0,4},{4,0},{8,12},{12,8},{1,5},{5,1},{9,13},{13,9},{2,6},{6,2},{1... | collective-permute-start | bytes 1179656 | tf_op jit(solution)/shard_map/ppermute | solution.py:270
  40.2 11.4 %collective-permute-start.18 = (bf16[4,8,48,128]{3,2,1,0:T(8,128)(2,1)S(1)}, bf16[4,8,48,128]{3,2,1,0:T(8,128)(2,1)S(1)}, u32[]{:S(2)}, u32[]{:S(2)}) collective-permute-start(bf16[4,8,48,128]{3,2,1,0:T(8,128)(2,1)S(1)} %get-tuple-element.70), channel_id=1, source_target_pairs={{4,8},{8,4},{5,9},{9,5},{6,10},{10,6},{7,11},{11,7},{20,24},{24,20... | collective-permute-start | bytes 1179656 | tf_op jit(solution)/shard_map/ppermute | solution.py:270
  44.3 9.9 %collective-permute-start.6 = (bf16[8,4,48,128]{3,2,1,0:T(8,128)(2,1)S(1)}, bf16[8,4,48,128]{3,2,1,0:T(8,128)(2,1)S(1)}, u32[]{:S(2)}, u32[]{:S(2)}) collective-permute-start(bf16[8,4,48,128]{3,2,1,0:T(8,128)(2,1)S(1)} %get-tuple-element.54), channel_id=1, source_target_pairs={{0,1},{1,0},{2,3},{3,2},{4,5},{5,4},{6,7},{7,6},{8,9},{9,8},{10,11... | collective-permute-start | bytes 1179656 | tf_op jit(solution)/shard_map/ppermute | solution.py:270
  44.5 14.5 %collective-permute-start.7 = (bf16[4,8,48,128]{3,2,1,0:T(8,128)(2,1)S(1)}, bf16[4,8,48,128]{3,2,1,0:T(8,128)(2,1)S(1)}, u32[]{:S(2)}, u32[]{:S(2)}) collective-permute-start(bf16[4,8,48,128]{3,2,1,0:T(8,128)(2,1)S(1)} %get-tuple-element.55), channel_id=1, source_target_pairs={{0,4},{4,0},{8,12},{12,8},{1,5},{5,1},{9,13},{13,9},{2,6},{6,2},{1... | collective-permute-start | bytes 1179656 | tf_op jit(solution)/shard_map/ppermute | solution.py:270
  48.6 10.4 %collective-permute-start.8 = (bf16[4,8,48,128]{3,2,1,0:T(8,128)(2,1)S(1)}, bf16[4,8,48,128]{3,2,1,0:T(8,128)(2,1)S(1)}, u32[]{:S(2)}, u32[]{:S(2)}) collective-permute-start(bf16[4,8,48,128]{3,2,1,0:T(8,128)(2,1)S(1)} %get-tuple-element.56), channel_id=1, source_target_pairs={{4,8},{8,4},{5,9},{9,5},{6,10},{10,6},{7,11},{11,7},{20,24},{24,20... | collective-permute-start | bytes 1179656 | tf_op jit(solution)/shard_map/ppermute | solution.py:270
  52.6 23.3 %collective-permute-start.19 = (bf16[4,8,48,128]{3,2,1,0:T(8,128)(2,1)S(1)}, bf16[4,8,48,128]{3,2,1,0:T(8,128)(2,1)S(1)}, u32[]{:S(2)}, u32[]{:S(2)}) collective-permute-start(bf16[4,8,48,128]{3,2,1,0:T(8,128)(2,1)S(1)} %get-tuple-element.72.sent1), channel_id=1, source_target_pairs={{0,2},{2,0},{1,3},{3,1},{4,6},{6,4},{5,7},{7,5},{8,10},{10,8},{9,1... | collective-permute-start | bytes 1179656 | tf_op jit(solution)/shard_map/ppermute | solution.py:270
  60.0 15.9 %collective-permute-start.9 = (bf16[4,8,48,128]{3,2,1,0:T(8,128)(2,1)S(1)}, bf16[4,8,48,128]{3,2,1,0:T(8,128)(2,1)S(1)}, u32[]{:S(2)}, u32[]{:S(2)}) collective-permute-start(bf16[4,8,48,128]{3,2,1,0:T(8,128)(2,1)S(1)} %get-tuple-element.58.sent0), channel_id=1, source_target_pairs={{0,2},{2,0},{1,3},{3,1},{4,6},{6,4},{5,7},{7,5},{8,10},{10,8},{9,1... | collective-permute-start | bytes 1179656 | tf_op jit(solution)/shard_map/ppermute | solution.py:270
  63.9 9.1 %collective-permute-start.21 = (bf16[128,128]{1,0:T(8,128)(2,1)S(1)}, bf16[128,128]{1,0:T(8,128)(2,1)S(1)}, u32[]{:S(2)}, u32[]{:S(2)}) collective-permute-start(bf16[128,128]{1,0:T(8,128)(2,1)S(1)} %get-tuple-element.75), channel_id=1, source_target_pairs={{8,0},{12,4},{2,10},{6,14},{9,1},{13,5},{3,11},{7,15},{24,16},{28,... | collective-permute-start | bytes 98312 | tf_op jit(solution)/shard_map/ppermute | solution.py:525
  65.2 10.7 %collective-permute-start.22 = (bf16[128,128]{1,0:T(8,128)(2,1)S(1)}, bf16[128,128]{1,0:T(8,128)(2,1)S(1)}, u32[]{:S(2)}, u32[]{:S(2)}) collective-permute-start(bf16[128,128]{1,0:T(8,128)(2,1)S(1)} %get-tuple-element.76), channel_id=1, source_target_pairs={{12,0},{8,4},{6,10},{2,14},{13,1},{9,5},{7,11},{3,15},{28,16},{24,... | collective-permute-start | bytes 98312 | tf_op jit(solution)/shard_map/ppermute | solution.py:525
  66.5 9.4 %collective-permute-start.23 = (bf16[128,128]{1,0:T(8,128)(2,1)S(1)}, bf16[128,128]{1,0:T(8,128)(2,1)S(1)}, u32[]{:S(2)}, u32[]{:S(2)}) collective-permute-start(bf16[128,128]{1,0:T(8,128)(2,1)S(1)} %get-tuple-element.77), channel_id=1, source_target_pairs={{4,0},{0,4},{14,10},{10,14},{5,1},{1,5},{15,11},{11,15},{20,16},{1... | collective-permute-start | bytes 98312 | tf_op jit(solution)/shard_map/ppermute | solution.py:525
  78.3 6.5 %collective-permute-start.25 = (bf16[144,128]{1,0:T(8,128)(2,1)S(1)}, bf16[144,128]{1,0:T(8,128)(2,1)S(1)}, u32[]{:S(2)}, u32[]{:S(2)}) collective-permute-start(bf16[144,128]{1,0:T(8,128)(2,1)S(1)} %get-tuple-element.82), channel_id=1, source_target_pairs={{0,8},{4,12},{8,0},{12,4},{1,9},{5,13},{9,1},{13,5},{2,10},{6,14},... | collective-permute-start | bytes 110600 | tf_op jit(solution)/shard_map/ppermute | solution.py:531
  (11 other events, 47.6 us)

commit v10 on v9

--- a/solution.py
+++ b/solution.py
@@ -86,29 +86,55 @@
     lax.fori_loop(0, along // TILE, one, 0)
 
 
-def first_body(chunk, p_ref, s_ref, u_ref, odd_ref, even_ref, edge_ref, square, turned_s):
+def first_body(
+    chunk, p_hbm, s_hbm, u_ref, odd_ref, even_ref, edge_ref, p_ref, s_ref, square, turned_s, sems
+):
     depth, across, padded, _ = u_ref.shape
     along = padded - 2 * EDGE
     core = lax.axis_index("sub")
     even = slab_is_even()
-    turned_s[...] = turned(s_ref[0], square)
+    lanes = pl.ds(chunk * LANES, LANES)
+    pairs = [(j, depth - RADIUS + j) for j in range(RADIUS)]
+    order = [z for pair in pairs for z in pair] + list(range(RADIUS, depth - RADIUS))
+    source_copy = pltpu.make_async_copy(s_hbm.at[0], s_ref, sems.at[depth])
+    source_copy.start()
+    copies = {}
+    for z in order:
+        copies[z] = pltpu.make_async_copy(p_hbm.at[z, :, :, lanes], p_ref.at[z], sems.at[z])
+        copies[z].start()
     clear_pads(u_ref)
-
-    def tile(start):
-        span = pl.ds(start, TILE)
-        rows = pl.ds(start + EDGE, TILE)
-        source = turned_s[span]
-        for x in range(across):
-            news = []
-            for z in range(depth):
-                p = p_ref[z, x, span, chunk * LANES : (chunk + 1) * LANES].astype(F32)
-                new = lane(source, z * across + x) * p
-                u_ref[z, x, rows] = new
-                news.append(new)
-            store_edges(x, span, news, even, even_ref, odd_ref)
-        store_beside(span, rows, core, u_ref, edge_ref)
-
-    tiles(along, tile)
+    source_copy.wait()
+    turned_s[...] = turned(s_ref[...], square)
+
+    def planes(zs):
+        for z in zs:
+            copies[z].wait()
+
+        def tile(start):
+            span = pl.ds(start, TILE)
+            source = turned_s[span]
+            for x in range(across):
+                news = []
+                for z in zs:
+                    new = lane(source, z * across + x) * p_ref[z, x, span].astype(F32)
+                    u_ref[z, x, pl.ds(start + EDGE, TILE)] = new
+                    news.append(new.astype(BF16))
+                if len(zs) == 2:
+                    low, high = news
+                    even_ref[zs[0], x, span] = jnp.where(even, high, low)
+                    odd_ref[zs[0], x, span] = jnp.where(even, low, high)
+
+        tiles(along, tile)
+
+    for pair in pairs:
+        planes(pair)
+    for z in range(RADIUS, depth - RADIUS):
+        planes((z,))
+
+    def beside(start):
+        store_beside(pl.ds(start, TILE), pl.ds(start + EDGE, TILE), core, u_ref, edge_ref)
+
+    tiles(along, beside)
 
 
 def square_scratch():
@@ -119,7 +145,7 @@
     depth, across, along, _ = probes.shape
     return call(
         functools.partial(first_body, chunk),
-        in_specs=whole_vmem(2),
+        in_specs=[pl.BlockSpec(memory_space=pltpu.HBM)] * 2,
         out_specs=whole_vmem(4),
         out_shape=[
             shape_of(depth, across, along + 2 * EDGE, F32),
@@ -127,7 +153,12 @@
             shape_of(RADIUS, across, along, BF16),
             shape_of(depth, RADIUS, along, BF16),
         ],
-        scratch_shapes=square_scratch(),
+        scratch_shapes=[
+            pltpu.VMEM((depth, across, along, LANES), BF16),
+            pltpu.VMEM(source.shape[1:], F32),
+        ]
+        + square_scratch()
+        + [pltpu.SemaphoreType.DMA((depth + 1,))],
     )(probes, source)
 
 
@@ -192,7 +223,7 @@
 
 
 def rim_body(kind, *refs):
-    base_ref, even_ref, odd_ref, c_ref = refs[:4]
+    base_ref, odd_ref, even_ref, c_ref = refs[:4]
     outs, (square, turned_c) = refs[4:-2], refs[-2:]
     depth, across, along, _ = base_ref.shape
     core = lax.axis_index("sub")
@@ -244,7 +275,7 @@
     tiles(along, tile)
 
 
-def rim_step(base, evens, odds, courant, kind):
+def rim_step(base, odds, evens, courant, kind):
     depth, across, along, _ = base.shape
     if kind == "middle":
         out_shape = [
@@ -263,7 +294,7 @@
         out_specs=whole_vmem(len(out_shape)),
         out_shape=out_shape,
         scratch_shapes=square_scratch(),
-    )(base, evens, odds, courant)
+    )(base, odds, evens, courant)
 
 
 def swap(x, axis, pairs):
@@ -580,14 +611,14 @@
             odd, even, beside = halos[c]
             base = local_step(now[c], beside, probes, c, courant, source, n, previous[c])
             if n < steps - 1:
-                u, *edges = rim_step(base, even, odd, courant, "middle")
+                u, *edges = rim_step(base, odd, even, courant, "middle")
                 previous[c], now[c] = now[c], u
                 halos[c] = exchange(*edges)
             elif paired:
-                kept, sent = rim_step(base, even, odd, courant, "half")
+                kept, sent = rim_step(base, odd, even, courant, "half")
                 finals.append((kept, sent, chip_swap(sent)))
             else:
-                finals += rim_step(base, even, odd, courant, "all")
+                finals += rim_step(base, odd, even, courant, "all")
     return (coupled if paired else coupled_general)(finals, cell_count)
 
 

time: 93.1 us -> 94.2 us (1.012)
  starting transfers between devices: 47.3 us -> 39.6 us
  waiting for transfers between devices: 17.5 us -> 24.4 us
  Pallas kernels: 24.7 us -> 26.4 us
    ppermute x24, waiting for transfers between devices: 10.8 us -> 17.7 us  [swap(): lax.ppermute(x, axis, [p for a, b in pairs for p in ((a, b), (b, a))])]
    ppermute x24, starting transfers between devices: 34.6 us -> 29.9 us  [swap(): lax.ppermute(x, axis, [p for a, b in pairs for p in ((a, b), (b, a))])]
    ppermute x3, starting transfers between devices: 9.09 us -> 6.23 us  [coupled(): inner_arrived.append(lax.ppermute(inner[d], ('slab', 'probe'), pairs))]
    pallas_call x2, Pallas kernels: 2.1 us -> 3.82 us  [first_field(): call(functools.partial(first_body, chunk), in_specs=[pl.BlockSpec(memory_...]
  transfers between devices with their start and end apart: 30 -> 30, of which waited for: 9 -> 14; matrix products, arithmetic and copies ran while one was open for 0% -> 0% of each run, Pallas kernels for 23% -> 24%
where the time goes in v10:
time: 94.2 us; the launch traced here: 93.8 us
  starting transfers between devices  39.6 us (42%)
  Pallas kernels  26.4 us (28%)
  waiting for transfers between devices  24.4 us (26%)
  local copies, waits for them, and re-layouts  2.32 us (2%)
  between operations  1.03 us (1%)
    ppermute x24, starting transfers between devices, swap(): lax.ppermute(x, axis, [p for a, b in pairs for p in ((a, b), (b, a))])  29.9 us
    ppermute x24, waiting for transfers between devices, swap(): lax.ppermute(x, axis, [p for a, b in pairs for p in ((a, b), (b, a))])  17.7 us
    pallas_call x6, Pallas kernels, local_step(): call(functools.partial(local_body, chunk, moment, previous is not None),...  13.3 us
    pallas_call x6, Pallas kernels, rim_step(): call(functools.partial(rim_body, kind), in_specs=whole_vmem(4), out_specs...  6.31 us
    ppermute x3, starting transfers between devices, coupled(): inner_arrived.append(lax.ppermute(inner[d], ('slab', 'probe'), pairs))  6.23 us
    pallas_call x2, Pallas kernels, first_field(): call(functools.partial(first_body, chunk), in_specs=[pl.BlockSpec(memory_...  3.82 us
    ppermute x3, waiting for transfers between devices, coupled(): lax.ppermute(blocks[d - 1], 'slab', [(i, i ^ d) for i in range(slabs)])  3.78 us
    ppermute x3, starting transfers between devices, coupled(): lax.ppermute(blocks[d - 1], 'slab', [(i, i ^ d) for i in range(slabs)])  3.55 us
  transfers between devices with their start and end apart: 30, of which 14 were waited for; matrix products, arithmetic and copies ran while one was open for 0% of the time, Pallas kernels for 24%

profile of v10, /device:TPU:0, one launch (start us, length us, event | category | flops | bytes accessed | tf_op | source)
XLA Modules:
  0.0 93.8 jit_solution(14186978583579186507)
XLA Ops:
  2.9 1.9 %shard_map.57 = (f32[8,8,64,128]{3,2,1,0:T(8,128)S(1)}, bf16[4,8,48,128]{3,2,1,0:T(8,128)(2,1)S(1)}, bf16[4,8,48,128]{3,2,1,0:T(8,128)(2,1)S(1)}, bf16[8,4,48,128]{3,2,1,0:T(8,128)(2,1)S(1)}) custom-call(bf16[8,8,48,256]{3,2,1,0:T(8,128)(2,1)S(1)} %copy-done, f32[4,64,48]{2,1,0:T(8,128)S(1)} %bitcast.3), custom_call_target="tpu_custom_call" | custom-call | flops 1 | bytes 1 | tf_op jit(solution)/shard_map/pallas_call | solution.py:146
  6.1 5.5 %collective-permute-start.12 = (bf16[4,8,48,128]{3,2,1,0:T(8,128)(2,1)S(1)}, bf16[4,8,48,128]{3,2,1,0:T(8,128)(2,1)S(1)}, u32[]{:S(2)}, u32[]{:S(2)}) collective-permute-start(bf16[4,8,48,128]{3,2,1,0:T(8,128)(2,1)S(1)} %get-tuple-element.62), channel_id=1, source_target_pairs={{0,4},{4,0},{8,12},{12,8},{1,5},{5,1},{9,13},{13,9},{2,6},{6,2},{1... | collective-permute-start | bytes 1179656 | tf_op jit(solution)/shard_map/ppermute | solution.py:301
  11.5 1.9 %shard_map.50 = (f32[8,8,64,128]{3,2,1,0:T(8,128)S(1)}, bf16[4,8,48,128]{3,2,1,0:T(8,128)(2,1)S(1)}, bf16[4,8,48,128]{3,2,1,0:T(8,128)(2,1)S(1)}, bf16[8,4,48,128]{3,2,1,0:T(8,128)(2,1)S(1)}) custom-call(bf16[8,8,48,256]{3,2,1,0:T(8,128)(2,1)S(1)} %copy-done, f32[4,64,48]{2,1,0:T(8,128)S(1)} %bitcast.4), custom_call_target="tpu_custom_call" | custom-call | flops 1 | bytes 1 | tf_op jit(solution)/shard_map/pallas_call | solution.py:146
  14.2 2.0 %collective-permute-start.2 = (bf16[4,8,48,128]{3,2,1,0:T(8,128)(2,1)S(1)}, bf16[4,8,48,128]{3,2,1,0:T(8,128)(2,1)S(1)}, u32[]{:S(2)}, u32[]{:S(2)}) collective-permute-start(bf16[4,8,48,128]{3,2,1,0:T(8,128)(2,1)S(1)} %get-tuple-element.48), channel_id=1, source_target_pairs={{0,4},{4,0},{8,12},{12,8},{1,5},{5,1},{9,13},{13,9},{2,6},{6,2},{1... | collective-permute-start | bytes 1179656 | tf_op jit(solution)/shard_map/ppermute | solution.py:301
  16.2 2.1 %shard_map.58.refs_0_ = f32[8,8,48,128]{3,2,1,0:T(8,128)S(1)} custom-call(f32[8,8,64,128]{3,2,1,0:T(8,128)S(1)} %get-tuple-element.59.refs_0_.refs_5_, bf16[8,4,48,128]{3,2,1,0:T(8,128)(2,1)S(1)} %collective-permute-done.10.refs_1_, bf16[8,8,48,256]{3,2,1,0:T(8,128)(2,1)S(1)} %copy-done, f32[64,48]{1,0:T(8,128)S(1)} %bitcast.11, f32[4,64,48]{2,1,0:T(8,128)S(1)} %bitcast.5), custom_call_target="tpu_custom_call" | custom-call | flops 1 | bytes 1 | tf_op jit(solution)/shard_map/pallas_call | solution.py:216
  18.4 3.0 %collective-permute-done.12.refs_2_ = bf16[4,8,48,128]{3,2,1,0:T(8,128)(2,1)S(1)} collective-permute-done((bf16[4,8,48,128]{3,2,1,0:T(8,128)(2,1)S(1)}, bf16[4,8,48,128]{3,2,1,0:T(8,128)(2,1)S(1)}, u32[]{:S(2)}, u32[]{:S(2)}) %collective-permute-start.12) | collective-permute-done | bytes 393248 | tf_op jit(solution)/shard_map/ppermute | solution.py:301
  23.3 3.8 %collective-permute-start.15 = (bf16[4,8,48,128]{3,2,1,0:T(8,128)(2,1)S(1)}, bf16[4,8,48,128]{3,2,1,0:T(8,128)(2,1)S(1)}, u32[]{:S(2)}, u32[]{:S(2)}) collective-permute-start(bf16[4,8,48,128]{3,2,1,0:T(8,128)(2,1)S(1)} %get-tuple-element.66), channel_id=1, source_target_pairs={{0,4},{4,0},{8,12},{12,8},{1,5},{5,1},{9,13},{13,9},{2,6},{6,2},{1... | collective-permute-start | bytes 1179656 | tf_op jit(solution)/shard_map/ppermute | solution.py:301
  27.1 2.1 %shard_map.51.refs_0_ = f32[8,8,48,128]{3,2,1,0:T(8,128)S(1)} custom-call(f32[8,8,64,128]{3,2,1,0:T(8,128)S(1)} %get-tuple-element.45.refs_0_.refs_5_, bf16[8,4,48,128]{3,2,1,0:T(8,128)(2,1)S(1)} %collective-permute-done.refs_1_, bf16[8,8,48,256]{3,2,1,0:T(8,128)(2,1)S(1)} %copy-done.1, f32[64,48]{1,0:T(8,128)S(1)} %bitcast.13, f32[4,64,48]{2,1,0:T(8,128)S(1)} %bitcast.6), custom_call_target="tpu_custom_call" | custom-call | flops 1 | bytes 1 | tf_op jit(solution)/shard_map/pallas_call | solution.py:216
  31.7 3.4 %collective-permute-start.5 = (bf16[4,8,48,128]{3,2,1,0:T(8,128)(2,1)S(1)}, bf16[4,8,48,128]{3,2,1,0:T(8,128)(2,1)S(1)}, u32[]{:S(2)}, u32[]{:S(2)}) collective-permute-start(bf16[4,8,48,128]{3,2,1,0:T(8,128)(2,1)S(1)} %get-tuple-element.52), channel_id=1, source_target_pairs={{0,4},{4,0},{8,12},{12,8},{1,5},{5,1},{9,13},{13,9},{2,6},{6,2},{1... | collective-permute-start | bytes 1179656 | tf_op jit(solution)/shard_map/ppermute | solution.py:301
  35.1 2.3 %shard_map.60.refs_0_ = f32[8,8,48,128]{3,2,1,0:T(8,128)S(1)} custom-call(f32[8,8,64,128]{3,2,1,0:T(8,128)S(1)} %get-tuple-element.63.refs_0_.refs_5_, bf16[8,4,48,128]{3,2,1,0:T(8,128)(2,1)S(1)} %collective-permute-done.13.refs_1_, bf16[8,8,48,256]{3,2,1,0:T(8,128)(2,1)S(1)} %copy-done.1, f32[64,48]{1,0:T(8,128)S(1)} %bitcast.15, f32[4,64,48]{2,1,0:T(8,128)S(1)} %bitcast.7, ...), custom_call_target="tpu_custom_call" | custom-call | flops 1 | bytes 1 | tf_op jit(solution)/shard_map/pallas_call | solution.py:216
  40.2 3.4 %collective-permute-start.18 = (bf16[4,8,48,128]{3,2,1,0:T(8,128)(2,1)S(1)}, bf16[4,8,48,128]{3,2,1,0:T(8,128)(2,1)S(1)}, u32[]{:S(2)}, u32[]{:S(2)}) collective-permute-start(bf16[4,8,48,128]{3,2,1,0:T(8,128)(2,1)S(1)} %get-tuple-element.70), channel_id=1, source_target_pairs={{0,4},{4,0},{8,12},{12,8},{1,5},{5,1},{9,13},{13,9},{2,6},{6,2},{1... | collective-permute-start | bytes 1179656 | tf_op jit(solution)/shard_map/ppermute | solution.py:301
  43.5 2.2 %shard_map.53.refs_0_ = f32[8,8,48,128]{3,2,1,0:T(8,128)S(1)} custom-call(f32[8,8,64,128]{3,2,1,0:T(8,128)S(1)} %get-tuple-element.49.refs_0_.refs_5_, bf16[8,4,48,128]{3,2,1,0:T(8,128)(2,1)S(1)} %collective-permute-done.3.refs_1_, bf16[8,8,48,256]{3,2,1,0:T(8,128)(2,1)S(1)} %copy-done.1, f32[64,48]{1,0:T(8,128)S(1)} %bitcast.17, f32[4,64,48]{2,1,0:T(8,128)S(1)} %bitcast.8, ...), custom_call_target="tpu_custom_call" | custom-call | flops 1 | bytes 1 | tf_op jit(solution)/shard_map/pallas_call | solution.py:216
  48.6 3.4 %collective-permute-start.8 = (bf16[4,8,48,128]{3,2,1,0:T(8,128)(2,1)S(1)}, bf16[4,8,48,128]{3,2,1,0:T(8,128)(2,1)S(1)}, u32[]{:S(2)}, u32[]{:S(2)}) collective-permute-start(bf16[4,8,48,128]{3,2,1,0:T(8,128)(2,1)S(1)} %get-tuple-element.56), channel_id=1, source_target_pairs={{0,4},{4,0},{8,12},{12,8},{1,5},{5,1},{9,13},{13,9},{2,6},{6,2},{1... | collective-permute-start | bytes 1179656 | tf_op jit(solution)/shard_map/ppermute | solution.py:301
  52.0 2.3 %shard_map.62.refs_0_ = f32[8,8,48,128]{3,2,1,0:T(8,128)S(1)} custom-call(f32[8,8,64,128]{3,2,1,0:T(8,128)S(1)} %get-tuple-element.67.refs_0_, bf16[8,4,48,128]{3,2,1,0:T(8,128)(2,1)S(1)} %collective-permute-done.16.refs_1_, bf16[8,8,48,256]{3,2,1,0:T(8,128)(2,1)S(1)} %copy-done.1, f32[64,48]{1,0:T(8,128)S(1)} %bitcast.19, f32[4,64,48]{2,1,0:T(8,128)S(1)} %bitcast.9, ...), custom_call_target="tpu_custom_call" | custom-call | flops 1 | bytes 1 | tf_op jit(solution)/shard_map/pallas_call | solution.py:216
  56.1 1.6 %collective-permute-start.19 = (bf16[4,8,48,128]{3,2,1,0:T(8,128)(2,1)S(1)}, bf16[4,8,48,128]{3,2,1,0:T(8,128)(2,1)S(1)}, u32[]{:S(2)}, u32[]{:S(2)}) collective-permute-start(bf16[4,8,48,128]{3,2,1,0:T(8,128)(2,1)S(1)} %get-tuple-element.72.sent1), channel_id=1, source_target_pairs={{0,2},{2,0},{1,3},{3,1},{4,6},{6,4},{5,7},{7,5},{8,10},{10,8},{9,1... | collective-permute-start | bytes 1179656 | tf_op jit(solution)/shard_map/ppermute | solution.py:301
  57.6 2.2 %shard_map.55.refs_0_ = f32[8,8,48,128]{3,2,1,0:T(8,128)S(1)} custom-call(f32[8,8,64,128]{3,2,1,0:T(8,128)S(1)} %get-tuple-element.53.refs_0_, bf16[8,4,48,128]{3,2,1,0:T(8,128)(2,1)S(1)} %collective-permute-done.6.refs_1_, bf16[8,8,48,256]{3,2,1,0:T(8,128)(2,1)S(1)} %copy-done.1, f32[64,48]{1,0:T(8,128)S(1)} %bitcast.21, f32[4,64,48]{2,1,0:T(8,128)S(1)} %bitcast.10, ...), custom_call_target="tpu_custom_call" | custom-call | flops 1 | bytes 1 | tf_op jit(solution)/shard_map/pallas_call | solution.py:216
  59.9 3.2 %collective-permute-done.8.refs_2_ = bf16[4,8,48,128]{3,2,1,0:T(8,128)(2,1)S(1)} collective-permute-done((bf16[4,8,48,128]{3,2,1,0:T(8,128)(2,1)S(1)}, bf16[4,8,48,128]{3,2,1,0:T(8,128)(2,1)S(1)}, u32[]{:S(2)}, u32[]{:S(2)}) %collective-permute-start.8) | collective-permute-done | bytes 393248 | tf_op jit(solution)/shard_map/ppermute | solution.py:301
  64.1 1.6 %collective-permute-start.9 = (bf16[4,8,48,128]{3,2,1,0:T(8,128)(2,1)S(1)}, bf16[4,8,48,128]{3,2,1,0:T(8,128)(2,1)S(1)}, u32[]{:S(2)}, u32[]{:S(2)}) collective-permute-start(bf16[4,8,48,128]{3,2,1,0:T(8,128)(2,1)S(1)} %get-tuple-element.58.sent0), channel_id=1, source_target_pairs={{0,2},{2,0},{1,3},{3,1},{4,6},{6,4},{5,7},{7,5},{8,10},{10,8},{9,1... | collective-permute-start | bytes 1179656 | tf_op jit(solution)/shard_map/ppermute | solution.py:301
  70.4 3.6 %collective-permute-start.23 = (bf16[128,128]{1,0:T(8,128)(2,1)S(1)}, bf16[128,128]{1,0:T(8,128)(2,1)S(1)}, u32[]{:S(2)}, u32[]{:S(2)}) collective-permute-start(bf16[128,128]{1,0:T(8,128)(2,1)S(1)} %get-tuple-element.77), channel_id=1, source_target_pairs={{4,0},{0,4},{14,10},{10,14},{5,1},{1,5},{15,11},{11,15},{20,16},{1... | collective-permute-start | bytes 98312 | tf_op jit(solution)/shard_map/ppermute | solution.py:556
  74.5 2.5 %collective-permute-done.22.refs_1_.refs_5_ = bf16[128,128]{1,0:T(8,128)(2,1)S(1)} collective-permute-done((bf16[128,128]{1,0:T(8,128)(2,1)S(1)}, bf16[128,128]{1,0:T(8,128)(2,1)S(1)}, u32[]{:S(2)}, u32[]{:S(2)}) %collective-permute-start.22) | collective-permute-done | bytes 32800 | tf_op jit(solution)/shard_map/ppermute | solution.py:556
  78.0 1.4 %collective-permute-done.24.got_ref = f32[384,128]{1,0:T(8,128)S(1)} collective-permute-done((f32[384,128]{1,0:T(8,128)S(1)}, f32[384,128]{1,0:T(8,128)S(1)}, u32[]{:S(2)}, u32[]{:S(2)}) %collective-permute-start.24) | collective-permute-done | bytes 196640 | tf_op jit(solution)/shard_map/ppermute | solution.py:301
  79.5 3.3 %collective-permute-start.26 = (bf16[144,128]{1,0:T(8,128)(2,1)S(1)}, bf16[144,128]{1,0:T(8,128)(2,1)S(1)}, u32[]{:S(2)}, u32[]{:S(2)}) collective-permute-start(bf16[144,128]{1,0:T(8,128)(2,1)S(1)} %get-tuple-element.83), channel_id=1, source_target_pairs={{0,12},{4,8},{8,4},{12,0},{1,13},{5,9},{9,5},{13,1},{2,14},{6,10},... | collective-permute-start | bytes 110600 | tf_op jit(solution)/shard_map/ppermute | solution.py:562
  83.0 2.9 %collective-permute-done.25.refs_0_ = bf16[144,128]{1,0:T(8,128)(2,1)S(1)} collective-permute-done((bf16[144,128]{1,0:T(8,128)(2,1)S(1)}, bf16[144,128]{1,0:T(8,128)(2,1)S(1)}, u32[]{:S(2)}, u32[]{:S(2)}) %collective-permute-start.25) | collective-permute-done | bytes 36896 | tf_op jit(solution)/shard_map/ppermute | solution.py:562
  87.1 4.1 %collective-permute-done.28.other_ref = bf16[272,128]{1,0:T(8,128)(2,1)S(1)} collective-permute-done((bf16[272,128]{1,0:T(8,128)(2,1)S(1)}, bf16[272,128]{1,0:T(8,128)(2,1)S(1)}, u32[]{:S(2)}, u32[]{:S(2)}) %collective-permute-start.28) | collective-permute-done | bytes 69664 | tf_op jit(solution)/shard_map/ppermute | solution.py:301
  (67 shorter events, 27.2 us)
Async XLA Ops:
  4.9 9.3 %collective-permute-start.10 = (bf16[8,4,48,128]{3,2,1,0:T(8,128)(2,1)S(1)}, bf16[8,4,48,128]{3,2,1,0:T(8,128)(2,1)S(1)}, u32[]{:S(2)}, u32[]{:S(2)}) collective-permute-start(bf16[8,4,48,128]{3,2,1,0:T(8,128)(2,1)S(1)} %get-tuple-element.60), channel_id=1, source_target_pairs={{0,1},{1,0},{2,3},{3,2},{4,5},{5,4},{6,7},{7,6},{8,9},{9,8},{10,11... | collective-permute-start | bytes 1179656 | tf_op jit(solution)/shard_map/ppermute | solution.py:301
  5.4 13.0 %collective-permute-start.11 = (bf16[4,8,48,128]{3,2,1,0:T(8,128)(2,1)S(1)}, bf16[4,8,48,128]{3,2,1,0:T(8,128)(2,1)S(1)}, u32[]{:S(2)}, u32[]{:S(2)}) collective-permute-start(bf16[4,8,48,128]{3,2,1,0:T(8,128)(2,1)S(1)} %get-tuple-element.61), channel_id=1, source_target_pairs={{4,8},{8,4},{5,9},{9,5},{6,10},{10,6},{7,11},{11,7},{20,24},{24,20... | collective-permute-start | bytes 1179656 | tf_op jit(solution)/shard_map/ppermute | solution.py:301
  6.1 15.4 %collective-permute-start.12 = (bf16[4,8,48,128]{3,2,1,0:T(8,128)(2,1)S(1)}, bf16[4,8,48,128]{3,2,1,0:T(8,128)(2,1)S(1)}, u32[]{:S(2)}, u32[]{:S(2)}) collective-permute-start(bf16[4,8,48,128]{3,2,1,0:T(8,128)(2,1)S(1)} %get-tuple-element.62), channel_id=1, source_target_pairs={{0,4},{4,0},{8,12},{12,8},{1,5},{5,1},{9,13},{13,9},{2,6},{6,2},{1... | collective-permute-start | bytes 1179656 | tf_op jit(solution)/shard_map/ppermute | solution.py:301
  13.4 9.9 %collective-permute-start = (bf16[8,4,48,128]{3,2,1,0:T(8,128)(2,1)S(1)}, bf16[8,4,48,128]{3,2,1,0:T(8,128)(2,1)S(1)}, u32[]{:S(2)}, u32[]{:S(2)}) collective-permute-start(bf16[8,4,48,128]{3,2,1,0:T(8,128)(2,1)S(1)} %get-tuple-element.46), channel_id=1, source_target_pairs={{0,1},{1,0},{2,3},{3,2},{4,5},{5,4},{6,7},{7,6},{8,9},{9,8},{10,11... | collective-permute-start | bytes 1179656 | tf_op jit(solution)/shard_map/ppermute | solution.py:301
  13.5 15.7 %collective-permute-start.1 = (bf16[4,8,48,128]{3,2,1,0:T(8,128)(2,1)S(1)}, bf16[4,8,48,128]{3,2,1,0:T(8,128)(2,1)S(1)}, u32[]{:S(2)}, u32[]{:S(2)}) collective-permute-start(bf16[4,8,48,128]{3,2,1,0:T(8,128)(2,1)S(1)} %get-tuple-element.47), channel_id=1, source_target_pairs={{4,8},{8,4},{5,9},{9,5},{6,10},{10,6},{7,11},{11,7},{20,24},{24,20... | collective-permute-start | bytes 1179656 | tf_op jit(solution)/shard_map/ppermute | solution.py:301
  14.2 15.6 %collective-permute-start.2 = (bf16[4,8,48,128]{3,2,1,0:T(8,128)(2,1)S(1)}, bf16[4,8,48,128]{3,2,1,0:T(8,128)(2,1)S(1)}, u32[]{:S(2)}, u32[]{:S(2)}) collective-permute-start(bf16[4,8,48,128]{3,2,1,0:T(8,128)(2,1)S(1)} %get-tuple-element.48), channel_id=1, source_target_pairs={{0,4},{4,0},{8,12},{12,8},{1,5},{5,1},{9,13},{13,9},{2,6},{6,2},{1... | collective-permute-start | bytes 1179656 | tf_op jit(solution)/shard_map/ppermute | solution.py:301
  22.5 9.2 %collective-permute-start.13 = (bf16[8,4,48,128]{3,2,1,0:T(8,128)(2,1)S(1)}, bf16[8,4,48,128]{3,2,1,0:T(8,128)(2,1)S(1)}, u32[]{:S(2)}, u32[]{:S(2)}) collective-permute-start(bf16[8,4,48,128]{3,2,1,0:T(8,128)(2,1)S(1)} %get-tuple-element.64), channel_id=1, source_target_pairs={{0,1},{1,0},{2,3},{3,2},{4,5},{5,4},{6,7},{7,6},{8,9},{9,8},{10,11... | collective-permute-start | bytes 1179656 | tf_op jit(solution)/shard_map/ppermute | solution.py:301
  22.6 14.8 %collective-permute-start.14 = (bf16[4,8,48,128]{3,2,1,0:T(8,128)(2,1)S(1)}, bf16[4,8,48,128]{3,2,1,0:T(8,128)(2,1)S(1)}, u32[]{:S(2)}, u32[]{:S(2)}) collective-permute-start(bf16[4,8,48,128]{3,2,1,0:T(8,128)(2,1)S(1)} %get-tuple-element.65), channel_id=1, source_target_pairs={{4,8},{8,4},{5,9},{9,5},{6,10},{10,6},{7,11},{11,7},{20,24},{24,20... | collective-permute-start | bytes 1179656 | tf_op jit(solution)/shard_map/ppermute | solution.py:301
  23.3 15.0 %collective-permute-start.15 = (bf16[4,8,48,128]{3,2,1,0:T(8,128)(2,1)S(1)}, bf16[4,8,48,128]{3,2,1,0:T(8,128)(2,1)S(1)}, u32[]{:S(2)}, u32[]{:S(2)}) collective-permute-start(bf16[4,8,48,128]{3,2,1,0:T(8,128)(2,1)S(1)} %get-tuple-element.66), channel_id=1, source_target_pairs={{0,4},{4,0},{8,12},{12,8},{1,5},{5,1},{9,13},{13,9},{2,6},{6,2},{1... | collective-permute-start | bytes 1179656 | tf_op jit(solution)/shard_map/ppermute | solution.py:301
  30.9 9.2 %collective-permute-start.3 = (bf16[8,4,48,128]{3,2,1,0:T(8,128)(2,1)S(1)}, bf16[8,4,48,128]{3,2,1,0:T(8,128)(2,1)S(1)}, u32[]{:S(2)}, u32[]{:S(2)}) collective-permute-start(bf16[8,4,48,128]{3,2,1,0:T(8,128)(2,1)S(1)} %get-tuple-element.50), channel_id=1, source_target_pairs={{0,1},{1,0},{2,3},{3,2},{4,5},{5,4},{6,7},{7,6},{8,9},{9,8},{10,11... | collective-permute-start | bytes 1179656 | tf_op jit(solution)/shard_map/ppermute | solution.py:301
  31.0 14.8 %collective-permute-start.4 = (bf16[4,8,48,128]{3,2,1,0:T(8,128)(2,1)S(1)}, bf16[4,8,48,128]{3,2,1,0:T(8,128)(2,1)S(1)}, u32[]{:S(2)}, u32[]{:S(2)}) collective-permute-start(bf16[4,8,48,128]{3,2,1,0:T(8,128)(2,1)S(1)} %get-tuple-element.51), channel_id=1, source_target_pairs={{4,8},{8,4},{5,9},{9,5},{6,10},{10,6},{7,11},{11,7},{20,24},{24,20... | collective-permute-start | bytes 1179656 | tf_op jit(solution)/shard_map/ppermute | solution.py:301
  31.7 15.0 %collective-permute-start.5 = (bf16[4,8,48,128]{3,2,1,0:T(8,128)(2,1)S(1)}, bf16[4,8,48,128]{3,2,1,0:T(8,128)(2,1)S(1)}, u32[]{:S(2)}, u32[]{:S(2)}) collective-permute-start(bf16[4,8,48,128]{3,2,1,0:T(8,128)(2,1)S(1)} %get-tuple-element.52), channel_id=1, source_target_pairs={{0,4},{4,0},{8,12},{12,8},{1,5},{5,1},{9,13},{13,9},{2,6},{6,2},{1... | collective-permute-start | bytes 1179656 | tf_op jit(solution)/shard_map/ppermute | solution.py:301
  39.4 9.2 %collective-permute-start.16 = (bf16[8,4,48,128]{3,2,1,0:T(8,128)(2,1)S(1)}, bf16[8,4,48,128]{3,2,1,0:T(8,128)(2,1)S(1)}, u32[]{:S(2)}, u32[]{:S(2)}) collective-permute-start(bf16[8,4,48,128]{3,2,1,0:T(8,128)(2,1)S(1)} %get-tuple-element.68), channel_id=1, source_target_pairs={{0,1},{1,0},{2,3},{3,2},{4,5},{5,4},{6,7},{7,6},{8,9},{9,8},{10,11... | collective-permute-start | bytes 1179656 | tf_op jit(solution)/shard_map/ppermute | solution.py:301
  39.5 14.8 %collective-permute-start.17 = (bf16[4,8,48,128]{3,2,1,0:T(8,128)(2,1)S(1)}, bf16[4,8,48,128]{3,2,1,0:T(8,128)(2,1)S(1)}, u32[]{:S(2)}, u32[]{:S(2)}) collective-permute-start(bf16[4,8,48,128]{3,2,1,0:T(8,128)(2,1)S(1)} %get-tuple-element.69), channel_id=1, source_target_pairs={{4,8},{8,4},{5,9},{9,5},{6,10},{10,6},{7,11},{11,7},{20,24},{24,20... | collective-permute-start | bytes 1179656 | tf_op jit(solution)/shard_map/ppermute | solution.py:301
  40.2 15.0 %collective-permute-start.18 = (bf16[4,8,48,128]{3,2,1,0:T(8,128)(2,1)S(1)}, bf16[4,8,48,128]{3,2,1,0:T(8,128)(2,1)S(1)}, u32[]{:S(2)}, u32[]{:S(2)}) collective-permute-start(bf16[4,8,48,128]{3,2,1,0:T(8,128)(2,1)S(1)} %get-tuple-element.70), channel_id=1, source_target_pairs={{0,4},{4,0},{8,12},{12,8},{1,5},{5,1},{9,13},{13,9},{2,6},{6,2},{1... | collective-permute-start | bytes 1179656 | tf_op jit(solution)/shard_map/ppermute | solution.py:301
  47.8 9.8 %collective-permute-start.6 = (bf16[8,4,48,128]{3,2,1,0:T(8,128)(2,1)S(1)}, bf16[8,4,48,128]{3,2,1,0:T(8,128)(2,1)S(1)}, u32[]{:S(2)}, u32[]{:S(2)}) collective-permute-start(bf16[8,4,48,128]{3,2,1,0:T(8,128)(2,1)S(1)} %get-tuple-element.54), channel_id=1, source_target_pairs={{0,1},{1,0},{2,3},{3,2},{4,5},{5,4},{6,7},{7,6},{8,9},{9,8},{10,11... | collective-permute-start | bytes 1179656 | tf_op jit(solution)/shard_map/ppermute | solution.py:301
  47.9 12.0 %collective-permute-start.7 = (bf16[4,8,48,128]{3,2,1,0:T(8,128)(2,1)S(1)}, bf16[4,8,48,128]{3,2,1,0:T(8,128)(2,1)S(1)}, u32[]{:S(2)}, u32[]{:S(2)}) collective-permute-start(bf16[4,8,48,128]{3,2,1,0:T(8,128)(2,1)S(1)} %get-tuple-element.55), channel_id=1, source_target_pairs={{4,8},{8,4},{5,9},{9,5},{6,10},{10,6},{7,11},{11,7},{20,24},{24,20... | collective-permute-start | bytes 1179656 | tf_op jit(solution)/shard_map/ppermute | solution.py:301
  48.6 14.6 %collective-permute-start.8 = (bf16[4,8,48,128]{3,2,1,0:T(8,128)(2,1)S(1)}, bf16[4,8,48,128]{3,2,1,0:T(8,128)(2,1)S(1)}, u32[]{:S(2)}, u32[]{:S(2)}) collective-permute-start(bf16[4,8,48,128]{3,2,1,0:T(8,128)(2,1)S(1)} %get-tuple-element.56), channel_id=1, source_target_pairs={{0,4},{4,0},{8,12},{12,8},{1,5},{5,1},{9,13},{13,9},{2,6},{6,2},{1... | collective-permute-start | bytes 1179656 | tf_op jit(solution)/shard_map/ppermute | solution.py:301
  56.1 20.9 %collective-permute-start.19 = (bf16[4,8,48,128]{3,2,1,0:T(8,128)(2,1)S(1)}, bf16[4,8,48,128]{3,2,1,0:T(8,128)(2,1)S(1)}, u32[]{:S(2)}, u32[]{:S(2)}) collective-permute-start(bf16[4,8,48,128]{3,2,1,0:T(8,128)(2,1)S(1)} %get-tuple-element.72.sent1), channel_id=1, source_target_pairs={{0,2},{2,0},{1,3},{3,1},{4,6},{6,4},{5,7},{7,5},{8,10},{10,8},{9,1... | collective-permute-start | bytes 1179656 | tf_op jit(solution)/shard_map/ppermute | solution.py:301
  64.1 12.9 %collective-permute-start.9 = (bf16[4,8,48,128]{3,2,1,0:T(8,128)(2,1)S(1)}, bf16[4,8,48,128]{3,2,1,0:T(8,128)(2,1)S(1)}, u32[]{:S(2)}, u32[]{:S(2)}) collective-permute-start(bf16[4,8,48,128]{3,2,1,0:T(8,128)(2,1)S(1)} %get-tuple-element.58.sent0), channel_id=1, source_target_pairs={{0,2},{2,0},{1,3},{3,1},{4,6},{6,4},{5,7},{7,5},{8,10},{10,8},{9,1... | collective-permute-start | bytes 1179656 | tf_op jit(solution)/shard_map/ppermute | solution.py:301
  67.8 6.7 %collective-permute-start.21 = (bf16[128,128]{1,0:T(8,128)(2,1)S(1)}, bf16[128,128]{1,0:T(8,128)(2,1)S(1)}, u32[]{:S(2)}, u32[]{:S(2)}) collective-permute-start(bf16[128,128]{1,0:T(8,128)(2,1)S(1)} %get-tuple-element.75), channel_id=1, source_target_pairs={{8,0},{12,4},{2,10},{6,14},{9,1},{13,5},{3,11},{7,15},{24,16},{28,... | collective-permute-start | bytes 98312 | tf_op jit(solution)/shard_map/ppermute | solution.py:556
  69.1 7.9 %collective-permute-start.22 = (bf16[128,128]{1,0:T(8,128)(2,1)S(1)}, bf16[128,128]{1,0:T(8,128)(2,1)S(1)}, u32[]{:S(2)}, u32[]{:S(2)}) collective-permute-start(bf16[128,128]{1,0:T(8,128)(2,1)S(1)} %get-tuple-element.76), channel_id=1, source_target_pairs={{12,0},{8,4},{6,10},{2,14},{13,1},{9,5},{7,11},{3,15},{28,16},{24,... | collective-permute-start | bytes 98312 | tf_op jit(solution)/shard_map/ppermute | solution.py:556
  70.4 6.6 %collective-permute-start.23 = (bf16[128,128]{1,0:T(8,128)(2,1)S(1)}, bf16[128,128]{1,0:T(8,128)(2,1)S(1)}, u32[]{:S(2)}, u32[]{:S(2)}) collective-permute-start(bf16[128,128]{1,0:T(8,128)(2,1)S(1)} %get-tuple-element.77), channel_id=1, source_target_pairs={{4,0},{0,4},{14,10},{10,14},{5,1},{1,5},{15,11},{11,15},{20,16},{1... | collective-permute-start | bytes 98312 | tf_op jit(solution)/shard_map/ppermute | solution.py:556
  79.4 6.5 %collective-permute-start.25 = (bf16[144,128]{1,0:T(8,128)(2,1)S(1)}, bf16[144,128]{1,0:T(8,128)(2,1)S(1)}, u32[]{:S(2)}, u32[]{:S(2)}) collective-permute-start(bf16[144,128]{1,0:T(8,128)(2,1)S(1)} %get-tuple-element.82), channel_id=1, source_target_pairs={{0,8},{4,12},{8,0},{12,4},{1,9},{5,13},{9,1},{13,5},{2,10},{6,14},... | collective-permute-start | bytes 110600 | tf_op jit(solution)/shard_map/ppermute | solution.py:562
  (11 other events, 52.1 us)

commit v11 on v9

--- a/solution.py
+++ b/solution.py
@@ -192,7 +192,7 @@
 
 
 def rim_body(kind, *refs):
-    base_ref, even_ref, odd_ref, c_ref = refs[:4]
+    base_ref, odd_ref, even_ref, c_ref = refs[:4]
     outs, (square, turned_c) = refs[4:-2], refs[-2:]
     depth, across, along, _ = base_ref.shape
     core = lax.axis_index("sub")
@@ -244,7 +244,7 @@
     tiles(along, tile)
 
 
-def rim_step(base, evens, odds, courant, kind):
+def rim_step(base, odds, evens, courant, kind):
     depth, across, along, _ = base.shape
     if kind == "middle":
         out_shape = [
@@ -263,7 +263,7 @@
         out_specs=whole_vmem(len(out_shape)),
         out_shape=out_shape,
         scratch_shapes=square_scratch(),
-    )(base, evens, odds, courant)
+    )(base, odds, evens, courant)
 
 
 def swap(x, axis, pairs):
@@ -358,8 +358,7 @@
     )(keep, got)
 
 
-def cross_body(kept0, got0, kept1, got1, *refs):
-    keep_ref, send_ref, panel = refs[-3:]
+def cross_body(kept0, got0, kept1, got1, keep_ref, send_ref, panel):
     chip = lax.axis_index("probe")
     core = lax.axis_index("sub")
     cells = panel.shape[0]
@@ -377,16 +376,16 @@
         ref[2 * LANES :] = mixed
 
 
-def cross_gram(fields, after):
+def cross_gram(fields):
     cells = math.prod(fields[0].shape[:3])
     three = jax.ShapeDtypeStruct((3 * LANES, LANES), F32)
     return call(
         cross_body,
-        in_specs=whole_vmem(4) + [pl.BlockSpec(memory_space=pl.ANY)] * len(after),
+        in_specs=whole_vmem(4),
         out_specs=whole_vmem(2),
         out_shape=[three, three],
         scratch_shapes=[pltpu.VMEM((cells, 4 * LANES), BF16)],
-    )(*fields, *after)
+    )(*fields)
 
 
 def rounded(ref, block, tail):
@@ -402,7 +401,8 @@
     return ref[:count].astype(F32), tail[:8] + tail[8:]
 
 
-def cross_rows_body(keep_ref, got_ref, tail_ref, own_ref, *outs):
+def cross_rows_body(after, keep_ref, got_ref, tail_ref, *refs):
+    own_ref, *outs = refs[after:]
     slab = lax.axis_index("slab")
     core = lax.axis_index("sub")
     tail = tail_ref[...]
@@ -419,15 +419,15 @@
             rounded(outs[d - 1], block, tail)
 
 
-def cross_rows(keep, got, tail, slabs):
+def cross_rows(keep, got, tail, slabs, after):
     own = jax.ShapeDtypeStruct((LANES + 8, LANES), F32)
     sent = jax.ShapeDtypeStruct((LANES + 16, LANES), BF16)
     return call(
-        cross_rows_body,
-        in_specs=whole_vmem(3),
+        functools.partial(cross_rows_body, len(after)),
+        in_specs=whole_vmem(3) + [pl.BlockSpec(memory_space=pl.ANY)] * len(after),
         out_specs=whole_vmem(slabs),
         out_shape=[own] + [sent] * (slabs - 1),
-    )(keep, got, tail)
+    )(keep, got, tail, *after)
 
 
 def sum_body(slabs, own_ref, *refs):
@@ -525,8 +525,8 @@
         inner_arrived.append(lax.ppermute(inner[d], ("slab", "probe"), pairs))
 
     pairs = [field for kept, _, got in finals for field in (kept, got)]
-    keep, send = cross_gram(pairs, inner_arrived)
-    mine, *blocks = cross_rows(keep, core_swap(send), tail, slabs)
+    keep, send = cross_gram(pairs)
+    mine, *blocks = cross_rows(keep, core_swap(send), tail, slabs, inner_arrived)
     arrived = [
         lax.ppermute(blocks[d - 1], "slab", [(i, i ^ d) for i in range(slabs)])
         for d in (2, 3, 1)
@@ -571,7 +571,7 @@
     exchange = lambda odd, even, edge: (odd_swap(odd), even_swap(even), core_swap(edge))
     now, previous, halos = [], [None] * chunks, []
     for c in range(chunks):
-        u, *edges = first_field(probes, c, source)
+        u, *edges = first_field(probes, c, source[:1])
         now.append(u)
         halos.append(exchange(*edges))
     finals = []
@@ -580,14 +580,14 @@
             odd, even, beside = halos[c]
             base = local_step(now[c], beside, probes, c, courant, source, n, previous[c])
             if n < steps - 1:
-                u, *edges = rim_step(base, even, odd, courant, "middle")
+                u, *edges = rim_step(base, odd, even, courant, "middle")
                 previous[c], now[c] = now[c], u
                 halos[c] = exchange(*edges)
             elif paired:
-                kept, sent = rim_step(base, even, odd, courant, "half")
+                kept, sent = rim_step(base, odd, even, courant, "half")
                 finals.append((kept, sent, chip_swap(sent)))
             else:
-                finals += rim_step(base, even, odd, courant, "all")
+                finals += rim_step(base, odd, even, courant, "all")
     return (coupled if paired else coupled_general)(finals, cell_count)
 
 

time: 93.1 us -> 101 us (1.085)
  waiting for transfers between devices: 17.5 us -> 31.7 us
  starting transfers between devices: 47.3 us -> 40.9 us
    ppermute x24, waiting for transfers between devices: 10.8 us -> 25 us  [swap(): lax.ppermute(x, axis, [p for a, b in pairs for p in ((a, b), (b, a))])]
    ppermute x3, starting transfers between devices: 9.09 us -> 5.9 us  [coupled(): inner_arrived.append(lax.ppermute(inner[d], ('slab', 'probe'), pairs))]
    ppermute x24, starting transfers between devices: 34.6 us -> 31.5 us  [swap(): lax.ppermute(x, axis, [p for a, b in pairs for p in ((a, b), (b, a))])]
    unnamed x10 -> x8, local copies, waits for them, and re-layouts: 2.32 us -> 1.42 us
  transfers between devices with their start and end apart: 30 -> 30, of which waited for: 9 -> 17; matrix products, arithmetic and copies ran while one was open for 0% -> 0% of each run, Pallas kernels for 23% -> 21%
where the time goes in v11:
time: 101 us; the launch traced here: 100 us
  starting transfers between devices  40.9 us (40%)
  waiting for transfers between devices  31.7 us (31%)
  Pallas kernels  24.7 us (24%)
  local copies, waits for them, and re-layouts  2.18 us (2%)
  between operations  1.01 us (1%)
    ppermute x24, starting transfers between devices, swap(): lax.ppermute(x, axis, [p for a, b in pairs for p in ((a, b), (b, a))])  31.5 us
    ppermute x24, waiting for transfers between devices, swap(): lax.ppermute(x, axis, [p for a, b in pairs for p in ((a, b), (b, a))])  25 us
    pallas_call x6, Pallas kernels, local_step(): call(functools.partial(local_body, chunk, moment, previous is not None),...  13.3 us
    pallas_call x6, Pallas kernels, rim_step(): call(functools.partial(rim_body, kind), in_specs=whole_vmem(4), out_specs...  6.31 us
    ppermute x3, starting transfers between devices, coupled(): inner_arrived.append(lax.ppermute(inner[d], ('slab', 'probe'), pairs))  5.9 us
    ppermute x3, waiting for transfers between devices, coupled(): lax.ppermute(blocks[d - 1], 'slab', [(i, i ^ d) for i in range(slabs)])  3.63 us
    ppermute x3, starting transfers between devices, coupled(): lax.ppermute(blocks[d - 1], 'slab', [(i, i ^ d) for i in range(slabs)])  3.55 us
    ppermute x3, waiting for transfers between devices, coupled(): inner_arrived.append(lax.ppermute(inner[d], ('slab', 'probe'), pairs))  3.09 us
  transfers between devices with their start and end apart: 30, of which 17 were waited for; matrix products, arithmetic and copies ran while one was open for 0% of the time, Pallas kernels for 21%

profile of v11, /device:TPU:0, one launch (start us, length us, event | category | flops | bytes accessed | tf_op | source)
XLA Modules:
  0.0 100.4 jit_solution(6819874265055524536)
XLA Ops:
  1.4 1.4 %copy-done = bf16[8,8,48,256]{3,2,1,0:T(8,128)(2,1)S(1)} copy-done((bf16[8,8,48,256]{3,2,1,0:T(8,128)(2,1)S(1)}, bf16[8,8,48,256]{3,2,1,0:T(8,128)(2,1)}, u32[]{:S(2)}) %copy-start) | copy-done | bytes 1572888
  5.1 5.5 %collective-permute-start.12 = (bf16[4,8,48,128]{3,2,1,0:T(8,128)(2,1)S(1)}, bf16[4,8,48,128]{3,2,1,0:T(8,128)(2,1)S(1)}, u32[]{:S(2)}, u32[]{:S(2)}) collective-permute-start(bf16[4,8,48,128]{3,2,1,0:T(8,128)(2,1)S(1)} %get-tuple-element.62), channel_id=1, source_target_pairs={{0,4},{4,0},{8,12},{12,8},{1,5},{5,1},{9,13},{13,9},{2,6},{6,2},{1... | collective-permute-start | bytes 1179656 | tf_op jit(solution)/shard_map/ppermute | solution.py:270
  12.4 1.9 %collective-permute-start.2 = (bf16[4,8,48,128]{3,2,1,0:T(8,128)(2,1)S(1)}, bf16[4,8,48,128]{3,2,1,0:T(8,128)(2,1)S(1)}, u32[]{:S(2)}, u32[]{:S(2)}) collective-permute-start(bf16[4,8,48,128]{3,2,1,0:T(8,128)(2,1)S(1)} %get-tuple-element.48), channel_id=1, source_target_pairs={{0,4},{4,0},{8,12},{12,8},{1,5},{5,1},{9,13},{13,9},{2,6},{6,2},{1... | collective-permute-start | bytes 1179656 | tf_op jit(solution)/shard_map/ppermute | solution.py:270
  14.3 2.1 %shard_map.58.refs_0_ = f32[8,8,48,128]{3,2,1,0:T(8,128)S(1)} custom-call(f32[8,8,64,128]{3,2,1,0:T(8,128)S(1)} %get-tuple-element.59.refs_0_.refs_5_, bf16[8,4,48,128]{3,2,1,0:T(8,128)(2,1)S(1)} %collective-permute-done.10.refs_1_, bf16[8,8,48,256]{3,2,1,0:T(8,128)(2,1)S(1)} %copy-done, f32[64,48]{1,0:T(8,128)S(1)} %bitcast.11, f32[4,64,48]{2,1,0:T(8,128)S(1)} %bitcast.5), custom_call_target="tpu_custom_call" | custom-call | flops 1 | bytes 1 | tf_op jit(solution)/shard_map/pallas_call | solution.py:185
  16.5 3.9 %collective-permute-done.12.refs_2_ = bf16[4,8,48,128]{3,2,1,0:T(8,128)(2,1)S(1)} collective-permute-done((bf16[4,8,48,128]{3,2,1,0:T(8,128)(2,1)S(1)}, bf16[4,8,48,128]{3,2,1,0:T(8,128)(2,1)S(1)}, u32[]{:S(2)}, u32[]{:S(2)}) %collective-permute-start.12) | collective-permute-done | bytes 393248 | tf_op jit(solution)/shard_map/ppermute | solution.py:270
  22.3 3.8 %collective-permute-start.15 = (bf16[4,8,48,128]{3,2,1,0:T(8,128)(2,1)S(1)}, bf16[4,8,48,128]{3,2,1,0:T(8,128)(2,1)S(1)}, u32[]{:S(2)}, u32[]{:S(2)}) collective-permute-start(bf16[4,8,48,128]{3,2,1,0:T(8,128)(2,1)S(1)} %get-tuple-element.66), channel_id=1, source_target_pairs={{0,4},{4,0},{8,12},{12,8},{1,5},{5,1},{9,13},{13,9},{2,6},{6,2},{1... | collective-permute-start | bytes 1179656 | tf_op jit(solution)/shard_map/ppermute | solution.py:270
  26.1 2.1 %shard_map.51.refs_0_ = f32[8,8,48,128]{3,2,1,0:T(8,128)S(1)} custom-call(f32[8,8,64,128]{3,2,1,0:T(8,128)S(1)} %get-tuple-element.45.refs_0_.refs_5_, bf16[8,4,48,128]{3,2,1,0:T(8,128)(2,1)S(1)} %collective-permute-done.refs_1_, bf16[8,8,48,256]{3,2,1,0:T(8,128)(2,1)S(1)} %copy-done.1, f32[64,48]{1,0:T(8,128)S(1)} %bitcast.13, f32[4,64,48]{2,1,0:T(8,128)S(1)} %bitcast.6), custom_call_target="tpu_custom_call" | custom-call | flops 1 | bytes 1 | tf_op jit(solution)/shard_map/pallas_call | solution.py:185
  30.7 3.4 %collective-permute-start.5 = (bf16[4,8,48,128]{3,2,1,0:T(8,128)(2,1)S(1)}, bf16[4,8,48,128]{3,2,1,0:T(8,128)(2,1)S(1)}, u32[]{:S(2)}, u32[]{:S(2)}) collective-permute-start(bf16[4,8,48,128]{3,2,1,0:T(8,128)(2,1)S(1)} %get-tuple-element.52), channel_id=1, source_target_pairs={{0,4},{4,0},{8,12},{12,8},{1,5},{5,1},{9,13},{13,9},{2,6},{6,2},{1... | collective-permute-start | bytes 1179656 | tf_op jit(solution)/shard_map/ppermute | solution.py:270
  34.1 2.3 %shard_map.60.refs_0_ = f32[8,8,48,128]{3,2,1,0:T(8,128)S(1)} custom-call(f32[8,8,64,128]{3,2,1,0:T(8,128)S(1)} %get-tuple-element.63.refs_0_.refs_5_, bf16[8,4,48,128]{3,2,1,0:T(8,128)(2,1)S(1)} %collective-permute-done.13.refs_1_, bf16[8,8,48,256]{3,2,1,0:T(8,128)(2,1)S(1)} %copy-done.1, f32[64,48]{1,0:T(8,128)S(1)} %bitcast.15, f32[4,64,48]{2,1,0:T(8,128)S(1)} %bitcast.7, ...), custom_call_target="tpu_custom_call" | custom-call | flops 1 | bytes 1 | tf_op jit(solution)/shard_map/pallas_call | solution.py:185
  39.2 3.4 %collective-permute-start.18 = (bf16[4,8,48,128]{3,2,1,0:T(8,128)(2,1)S(1)}, bf16[4,8,48,128]{3,2,1,0:T(8,128)(2,1)S(1)}, u32[]{:S(2)}, u32[]{:S(2)}) collective-permute-start(bf16[4,8,48,128]{3,2,1,0:T(8,128)(2,1)S(1)} %get-tuple-element.70), channel_id=1, source_target_pairs={{0,4},{4,0},{8,12},{12,8},{1,5},{5,1},{9,13},{13,9},{2,6},{6,2},{1... | collective-permute-start | bytes 1179656 | tf_op jit(solution)/shard_map/ppermute | solution.py:270
  42.5 2.2 %shard_map.53.refs_0_ = f32[8,8,48,128]{3,2,1,0:T(8,128)S(1)} custom-call(f32[8,8,64,128]{3,2,1,0:T(8,128)S(1)} %get-tuple-element.49.refs_0_.refs_5_, bf16[8,4,48,128]{3,2,1,0:T(8,128)(2,1)S(1)} %collective-permute-done.3.refs_1_, bf16[8,8,48,256]{3,2,1,0:T(8,128)(2,1)S(1)} %copy-done.1, f32[64,48]{1,0:T(8,128)S(1)} %bitcast.17, f32[4,64,48]{2,1,0:T(8,128)S(1)} %bitcast.8, ...), custom_call_target="tpu_custom_call" | custom-call | flops 1 | bytes 1 | tf_op jit(solution)/shard_map/pallas_call | solution.py:185
  47.6 3.4 %collective-permute-start.8 = (bf16[4,8,48,128]{3,2,1,0:T(8,128)(2,1)S(1)}, bf16[4,8,48,128]{3,2,1,0:T(8,128)(2,1)S(1)}, u32[]{:S(2)}, u32[]{:S(2)}) collective-permute-start(bf16[4,8,48,128]{3,2,1,0:T(8,128)(2,1)S(1)} %get-tuple-element.56), channel_id=1, source_target_pairs={{0,4},{4,0},{8,12},{12,8},{1,5},{5,1},{9,13},{13,9},{2,6},{6,2},{1... | collective-permute-start | bytes 1179656 | tf_op jit(solution)/shard_map/ppermute | solution.py:270
  50.9 2.3 %shard_map.62.refs_0_ = f32[8,8,48,128]{3,2,1,0:T(8,128)S(1)} custom-call(f32[8,8,64,128]{3,2,1,0:T(8,128)S(1)} %get-tuple-element.67.refs_0_, bf16[8,4,48,128]{3,2,1,0:T(8,128)(2,1)S(1)} %collective-permute-done.16.refs_1_, bf16[8,8,48,256]{3,2,1,0:T(8,128)(2,1)S(1)} %copy-done.1, f32[64,48]{1,0:T(8,128)S(1)} %bitcast.19, f32[4,64,48]{2,1,0:T(8,128)S(1)} %bitcast.9, ...), custom_call_target="tpu_custom_call" | custom-call | flops 1 | bytes 1 | tf_op jit(solution)/shard_map/pallas_call | solution.py:185
  55.1 1.6 %collective-permute-start.19 = (bf16[4,8,48,128]{3,2,1,0:T(8,128)(2,1)S(1)}, bf16[4,8,48,128]{3,2,1,0:T(8,128)(2,1)S(1)}, u32[]{:S(2)}, u32[]{:S(2)}) collective-permute-start(bf16[4,8,48,128]{3,2,1,0:T(8,128)(2,1)S(1)} %get-tuple-element.72.sent1), channel_id=1, source_target_pairs={{0,2},{2,0},{1,3},{3,1},{4,6},{6,4},{5,7},{7,5},{8,10},{10,8},{9,1... | collective-permute-start | bytes 1179656 | tf_op jit(solution)/shard_map/ppermute | solution.py:270
  56.6 2.2 %shard_map.55.refs_0_ = f32[8,8,48,128]{3,2,1,0:T(8,128)S(1)} custom-call(f32[8,8,64,128]{3,2,1,0:T(8,128)S(1)} %get-tuple-element.53.refs_0_, bf16[8,4,48,128]{3,2,1,0:T(8,128)(2,1)S(1)} %collective-permute-done.6.refs_1_, bf16[8,8,48,256]{3,2,1,0:T(8,128)(2,1)S(1)} %copy-done.1, f32[64,48]{1,0:T(8,128)S(1)} %bitcast.21, f32[4,64,48]{2,1,0:T(8,128)S(1)} %bitcast.10, ...), custom_call_target="tpu_custom_call" | custom-call | flops 1 | bytes 1 | tf_op jit(solution)/shard_map/pallas_call | solution.py:185
  58.9 3.2 %collective-permute-done.8.refs_2_ = bf16[4,8,48,128]{3,2,1,0:T(8,128)(2,1)S(1)} collective-permute-done((bf16[4,8,48,128]{3,2,1,0:T(8,128)(2,1)S(1)}, bf16[4,8,48,128]{3,2,1,0:T(8,128)(2,1)S(1)}, u32[]{:S(2)}, u32[]{:S(2)}) %collective-permute-start.8) | collective-permute-done | bytes 393248 | tf_op jit(solution)/shard_map/ppermute | solution.py:270
  63.1 1.6 %collective-permute-start.9 = (bf16[4,8,48,128]{3,2,1,0:T(8,128)(2,1)S(1)}, bf16[4,8,48,128]{3,2,1,0:T(8,128)(2,1)S(1)}, u32[]{:S(2)}, u32[]{:S(2)}) collective-permute-start(bf16[4,8,48,128]{3,2,1,0:T(8,128)(2,1)S(1)} %get-tuple-element.58.sent0), channel_id=1, source_target_pairs={{0,2},{2,0},{1,3},{3,1},{4,6},{6,4},{5,7},{7,5},{8,10},{10,8},{9,1... | collective-permute-start | bytes 1179656 | tf_op jit(solution)/shard_map/ppermute | solution.py:270
  65.5 8.4 %collective-permute-done.9.got0 = bf16[4,8,48,128]{3,2,1,0:T(8,128)(2,1)S(1)} collective-permute-done((bf16[4,8,48,128]{3,2,1,0:T(8,128)(2,1)S(1)}, bf16[4,8,48,128]{3,2,1,0:T(8,128)(2,1)S(1)}, u32[]{:S(2)}, u32[]{:S(2)}) %collective-permute-start.9) | collective-permute-done | bytes 393248 | tf_op jit(solution)/shard_map/ppermute | solution.py:270
  79.8 3.3 %collective-permute-start.24 = (bf16[128,128]{1,0:T(8,128)(2,1)S(1)}, bf16[128,128]{1,0:T(8,128)(2,1)S(1)}, u32[]{:S(2)}, u32[]{:S(2)}) collective-permute-start(bf16[128,128]{1,0:T(8,128)(2,1)S(1)} %get-tuple-element.80), channel_id=1, source_target_pairs={{4,0},{0,4},{14,10},{10,14},{5,1},{1,5},{15,11},{11,15},{20,16},{1... | collective-permute-start | bytes 98312 | tf_op jit(solution)/shard_map/ppermute | solution.py:525
  84.3 1.9 %collective-permute-done.23.refs_1_.refs_5_ = bf16[128,128]{1,0:T(8,128)(2,1)S(1)} collective-permute-done((bf16[128,128]{1,0:T(8,128)(2,1)S(1)}, bf16[128,128]{1,0:T(8,128)(2,1)S(1)}, u32[]{:S(2)}, u32[]{:S(2)}) %collective-permute-start.23) | collective-permute-done | bytes 32800 | tf_op jit(solution)/shard_map/ppermute | solution.py:525
  86.3 3.1 %collective-permute-start.26 = (bf16[144,128]{1,0:T(8,128)(2,1)S(1)}, bf16[144,128]{1,0:T(8,128)(2,1)S(1)}, u32[]{:S(2)}, u32[]{:S(2)}) collective-permute-start(bf16[144,128]{1,0:T(8,128)(2,1)S(1)} %get-tuple-element.83), channel_id=1, source_target_pairs={{0,12},{4,8},{8,4},{12,0},{1,13},{5,9},{9,5},{13,1},{2,14},{6,10},... | collective-permute-start | bytes 110600 | tf_op jit(solution)/shard_map/ppermute | solution.py:531
  89.8 1.8 %collective-permute-done.25.refs_0_ = bf16[144,128]{1,0:T(8,128)(2,1)S(1)} collective-permute-done((bf16[144,128]{1,0:T(8,128)(2,1)S(1)}, bf16[144,128]{1,0:T(8,128)(2,1)S(1)}, u32[]{:S(2)}, u32[]{:S(2)}) %collective-permute-start.25) | collective-permute-done | bytes 36896 | tf_op jit(solution)/shard_map/ppermute | solution.py:531
  93.5 1.5 %collective-permute-start.28 = (bf16[272,128]{1,0:T(8,128)(2,1)S(1)}, bf16[272,128]{1,0:T(8,128)(2,1)S(1)}, u32[]{:S(2)}, u32[]{:S(2)}) collective-permute-start(bf16[272,128]{1,0:T(8,128)(2,1)S(1)} %shard_map.68.mine_ref), channel_id=1, source_target_pairs={{0,2},{2,0},{1,3},{3,1},{4,6},{6,4},{5,7},{7,5},{8,10},{10,8},{9,1... | collective-permute-start | bytes 208904 | tf_op jit(solution)/shard_map/ppermute | solution.py:270
  94.9 2.9 %collective-permute-done.28.other_ref = bf16[272,128]{1,0:T(8,128)(2,1)S(1)} collective-permute-done((bf16[272,128]{1,0:T(8,128)(2,1)S(1)}, bf16[272,128]{1,0:T(8,128)(2,1)S(1)}, u32[]{:S(2)}, u32[]{:S(2)}) %collective-permute-start.28) | collective-permute-done | bytes 69664 | tf_op jit(solution)/shard_map/ppermute | solution.py:270
  (66 shorter events, 30.3 us)
Async XLA Ops:
  3.9 8.5 %collective-permute-start.10 = (bf16[8,4,48,128]{3,2,1,0:T(8,128)(2,1)S(1)}, bf16[8,4,48,128]{3,2,1,0:T(8,128)(2,1)S(1)}, u32[]{:S(2)}, u32[]{:S(2)}) collective-permute-start(bf16[8,4,48,128]{3,2,1,0:T(8,128)(2,1)S(1)} %get-tuple-element.60), channel_id=1, source_target_pairs={{0,1},{1,0},{2,3},{3,2},{4,5},{5,4},{6,7},{7,6},{8,9},{9,8},{10,11... | collective-permute-start | bytes 1179656 | tf_op jit(solution)/shard_map/ppermute | solution.py:270
  4.4 12.1 %collective-permute-start.11 = (bf16[4,8,48,128]{3,2,1,0:T(8,128)(2,1)S(1)}, bf16[4,8,48,128]{3,2,1,0:T(8,128)(2,1)S(1)}, u32[]{:S(2)}, u32[]{:S(2)}) collective-permute-start(bf16[4,8,48,128]{3,2,1,0:T(8,128)(2,1)S(1)} %get-tuple-element.61), channel_id=1, source_target_pairs={{4,8},{8,4},{5,9},{9,5},{6,10},{10,6},{7,11},{11,7},{20,24},{24,20... | collective-permute-start | bytes 1179656 | tf_op jit(solution)/shard_map/ppermute | solution.py:270
  5.1 15.4 %collective-permute-start.12 = (bf16[4,8,48,128]{3,2,1,0:T(8,128)(2,1)S(1)}, bf16[4,8,48,128]{3,2,1,0:T(8,128)(2,1)S(1)}, u32[]{:S(2)}, u32[]{:S(2)}) collective-permute-start(bf16[4,8,48,128]{3,2,1,0:T(8,128)(2,1)S(1)} %get-tuple-element.62), channel_id=1, source_target_pairs={{0,4},{4,0},{8,12},{12,8},{1,5},{5,1},{9,13},{13,9},{2,6},{6,2},{1... | collective-permute-start | bytes 1179656 | tf_op jit(solution)/shard_map/ppermute | solution.py:270
  11.6 10.7 %collective-permute-start = (bf16[8,4,48,128]{3,2,1,0:T(8,128)(2,1)S(1)}, bf16[8,4,48,128]{3,2,1,0:T(8,128)(2,1)S(1)}, u32[]{:S(2)}, u32[]{:S(2)}) collective-permute-start(bf16[8,4,48,128]{3,2,1,0:T(8,128)(2,1)S(1)} %get-tuple-element.46), channel_id=1, source_target_pairs={{0,1},{1,0},{2,3},{3,2},{4,5},{5,4},{6,7},{7,6},{8,9},{9,8},{10,11... | collective-permute-start | bytes 1179656 | tf_op jit(solution)/shard_map/ppermute | solution.py:270
  11.7 16.6 %collective-permute-start.1 = (bf16[4,8,48,128]{3,2,1,0:T(8,128)(2,1)S(1)}, bf16[4,8,48,128]{3,2,1,0:T(8,128)(2,1)S(1)}, u32[]{:S(2)}, u32[]{:S(2)}) collective-permute-start(bf16[4,8,48,128]{3,2,1,0:T(8,128)(2,1)S(1)} %get-tuple-element.47), channel_id=1, source_target_pairs={{4,8},{8,4},{5,9},{9,5},{6,10},{10,6},{7,11},{11,7},{20,24},{24,20... | collective-permute-start | bytes 1179656 | tf_op jit(solution)/shard_map/ppermute | solution.py:270
  12.4 16.5 %collective-permute-start.2 = (bf16[4,8,48,128]{3,2,1,0:T(8,128)(2,1)S(1)}, bf16[4,8,48,128]{3,2,1,0:T(8,128)(2,1)S(1)}, u32[]{:S(2)}, u32[]{:S(2)}) collective-permute-start(bf16[4,8,48,128]{3,2,1,0:T(8,128)(2,1)S(1)} %get-tuple-element.48), channel_id=1, source_target_pairs={{0,4},{4,0},{8,12},{12,8},{1,5},{5,1},{9,13},{13,9},{2,6},{6,2},{1... | collective-permute-start | bytes 1179656 | tf_op jit(solution)/shard_map/ppermute | solution.py:270
  21.5 9.2 %collective-permute-start.13 = (bf16[8,4,48,128]{3,2,1,0:T(8,128)(2,1)S(1)}, bf16[8,4,48,128]{3,2,1,0:T(8,128)(2,1)S(1)}, u32[]{:S(2)}, u32[]{:S(2)}) collective-permute-start(bf16[8,4,48,128]{3,2,1,0:T(8,128)(2,1)S(1)} %get-tuple-element.64), channel_id=1, source_target_pairs={{0,1},{1,0},{2,3},{3,2},{4,5},{5,4},{6,7},{7,6},{8,9},{9,8},{10,11... | collective-permute-start | bytes 1179656 | tf_op jit(solution)/shard_map/ppermute | solution.py:270
  21.6 14.8 %collective-permute-start.14 = (bf16[4,8,48,128]{3,2,1,0:T(8,128)(2,1)S(1)}, bf16[4,8,48,128]{3,2,1,0:T(8,128)(2,1)S(1)}, u32[]{:S(2)}, u32[]{:S(2)}) collective-permute-start(bf16[4,8,48,128]{3,2,1,0:T(8,128)(2,1)S(1)} %get-tuple-element.65), channel_id=1, source_target_pairs={{4,8},{8,4},{5,9},{9,5},{6,10},{10,6},{7,11},{11,7},{20,24},{24,20... | collective-permute-start | bytes 1179656 | tf_op jit(solution)/shard_map/ppermute | solution.py:270
  22.3 15.0 %collective-permute-start.15 = (bf16[4,8,48,128]{3,2,1,0:T(8,128)(2,1)S(1)}, bf16[4,8,48,128]{3,2,1,0:T(8,128)(2,1)S(1)}, u32[]{:S(2)}, u32[]{:S(2)}) collective-permute-start(bf16[4,8,48,128]{3,2,1,0:T(8,128)(2,1)S(1)} %get-tuple-element.66), channel_id=1, source_target_pairs={{0,4},{4,0},{8,12},{12,8},{1,5},{5,1},{9,13},{13,9},{2,6},{6,2},{1... | collective-permute-start | bytes 1179656 | tf_op jit(solution)/shard_map/ppermute | solution.py:270
  29.9 9.2 %collective-permute-start.3 = (bf16[8,4,48,128]{3,2,1,0:T(8,128)(2,1)S(1)}, bf16[8,4,48,128]{3,2,1,0:T(8,128)(2,1)S(1)}, u32[]{:S(2)}, u32[]{:S(2)}) collective-permute-start(bf16[8,4,48,128]{3,2,1,0:T(8,128)(2,1)S(1)} %get-tuple-element.50), channel_id=1, source_target_pairs={{0,1},{1,0},{2,3},{3,2},{4,5},{5,4},{6,7},{7,6},{8,9},{9,8},{10,11... | collective-permute-start | bytes 1179656 | tf_op jit(solution)/shard_map/ppermute | solution.py:270
  30.0 14.8 %collective-permute-start.4 = (bf16[4,8,48,128]{3,2,1,0:T(8,128)(2,1)S(1)}, bf16[4,8,48,128]{3,2,1,0:T(8,128)(2,1)S(1)}, u32[]{:S(2)}, u32[]{:S(2)}) collective-permute-start(bf16[4,8,48,128]{3,2,1,0:T(8,128)(2,1)S(1)} %get-tuple-element.51), channel_id=1, source_target_pairs={{4,8},{8,4},{5,9},{9,5},{6,10},{10,6},{7,11},{11,7},{20,24},{24,20... | collective-permute-start | bytes 1179656 | tf_op jit(solution)/shard_map/ppermute | solution.py:270
  30.7 15.0 %collective-permute-start.5 = (bf16[4,8,48,128]{3,2,1,0:T(8,128)(2,1)S(1)}, bf16[4,8,48,128]{3,2,1,0:T(8,128)(2,1)S(1)}, u32[]{:S(2)}, u32[]{:S(2)}) collective-permute-start(bf16[4,8,48,128]{3,2,1,0:T(8,128)(2,1)S(1)} %get-tuple-element.52), channel_id=1, source_target_pairs={{0,4},{4,0},{8,12},{12,8},{1,5},{5,1},{9,13},{13,9},{2,6},{6,2},{1... | collective-permute-start | bytes 1179656 | tf_op jit(solution)/shard_map/ppermute | solution.py:270
  38.4 9.2 %collective-permute-start.16 = (bf16[8,4,48,128]{3,2,1,0:T(8,128)(2,1)S(1)}, bf16[8,4,48,128]{3,2,1,0:T(8,128)(2,1)S(1)}, u32[]{:S(2)}, u32[]{:S(2)}) collective-permute-start(bf16[8,4,48,128]{3,2,1,0:T(8,128)(2,1)S(1)} %get-tuple-element.68), channel_id=1, source_target_pairs={{0,1},{1,0},{2,3},{3,2},{4,5},{5,4},{6,7},{7,6},{8,9},{9,8},{10,11... | collective-permute-start | bytes 1179656 | tf_op jit(solution)/shard_map/ppermute | solution.py:270
  38.5 14.8 %collective-permute-start.17 = (bf16[4,8,48,128]{3,2,1,0:T(8,128)(2,1)S(1)}, bf16[4,8,48,128]{3,2,1,0:T(8,128)(2,1)S(1)}, u32[]{:S(2)}, u32[]{:S(2)}) collective-permute-start(bf16[4,8,48,128]{3,2,1,0:T(8,128)(2,1)S(1)} %get-tuple-element.69), channel_id=1, source_target_pairs={{4,8},{8,4},{5,9},{9,5},{6,10},{10,6},{7,11},{11,7},{20,24},{24,20... | collective-permute-start | bytes 1179656 | tf_op jit(solution)/shard_map/ppermute | solution.py:270
  39.2 15.0 %collective-permute-start.18 = (bf16[4,8,48,128]{3,2,1,0:T(8,128)(2,1)S(1)}, bf16[4,8,48,128]{3,2,1,0:T(8,128)(2,1)S(1)}, u32[]{:S(2)}, u32[]{:S(2)}) collective-permute-start(bf16[4,8,48,128]{3,2,1,0:T(8,128)(2,1)S(1)} %get-tuple-element.70), channel_id=1, source_target_pairs={{0,4},{4,0},{8,12},{12,8},{1,5},{5,1},{9,13},{13,9},{2,6},{6,2},{1... | collective-permute-start | bytes 1179656 | tf_op jit(solution)/shard_map/ppermute | solution.py:270
  46.8 9.8 %collective-permute-start.6 = (bf16[8,4,48,128]{3,2,1,0:T(8,128)(2,1)S(1)}, bf16[8,4,48,128]{3,2,1,0:T(8,128)(2,1)S(1)}, u32[]{:S(2)}, u32[]{:S(2)}) collective-permute-start(bf16[8,4,48,128]{3,2,1,0:T(8,128)(2,1)S(1)} %get-tuple-element.54), channel_id=1, source_target_pairs={{0,1},{1,0},{2,3},{3,2},{4,5},{5,4},{6,7},{7,6},{8,9},{9,8},{10,11... | collective-permute-start | bytes 1179656 | tf_op jit(solution)/shard_map/ppermute | solution.py:270
  46.9 12.0 %collective-permute-start.7 = (bf16[4,8,48,128]{3,2,1,0:T(8,128)(2,1)S(1)}, bf16[4,8,48,128]{3,2,1,0:T(8,128)(2,1)S(1)}, u32[]{:S(2)}, u32[]{:S(2)}) collective-permute-start(bf16[4,8,48,128]{3,2,1,0:T(8,128)(2,1)S(1)} %get-tuple-element.55), channel_id=1, source_target_pairs={{4,8},{8,4},{5,9},{9,5},{6,10},{10,6},{7,11},{11,7},{20,24},{24,20... | collective-permute-start | bytes 1179656 | tf_op jit(solution)/shard_map/ppermute | solution.py:270
  47.6 14.6 %collective-permute-start.8 = (bf16[4,8,48,128]{3,2,1,0:T(8,128)(2,1)S(1)}, bf16[4,8,48,128]{3,2,1,0:T(8,128)(2,1)S(1)}, u32[]{:S(2)}, u32[]{:S(2)}) collective-permute-start(bf16[4,8,48,128]{3,2,1,0:T(8,128)(2,1)S(1)} %get-tuple-element.56), channel_id=1, source_target_pairs={{0,4},{4,0},{8,12},{12,8},{1,5},{5,1},{9,13},{13,9},{2,6},{6,2},{1... | collective-permute-start | bytes 1179656 | tf_op jit(solution)/shard_map/ppermute | solution.py:270
  55.1 10.4 %collective-permute-start.19 = (bf16[4,8,48,128]{3,2,1,0:T(8,128)(2,1)S(1)}, bf16[4,8,48,128]{3,2,1,0:T(8,128)(2,1)S(1)}, u32[]{:S(2)}, u32[]{:S(2)}) collective-permute-start(bf16[4,8,48,128]{3,2,1,0:T(8,128)(2,1)S(1)} %get-tuple-element.72.sent1), channel_id=1, source_target_pairs={{0,2},{2,0},{1,3},{3,1},{4,6},{6,4},{5,7},{7,5},{8,10},{10,8},{9,1... | collective-permute-start | bytes 1179656 | tf_op jit(solution)/shard_map/ppermute | solution.py:270
  63.1 10.8 %collective-permute-start.9 = (bf16[4,8,48,128]{3,2,1,0:T(8,128)(2,1)S(1)}, bf16[4,8,48,128]{3,2,1,0:T(8,128)(2,1)S(1)}, u32[]{:S(2)}, u32[]{:S(2)}) collective-permute-start(bf16[4,8,48,128]{3,2,1,0:T(8,128)(2,1)S(1)} %get-tuple-element.58.sent0), channel_id=1, source_target_pairs={{0,2},{2,0},{1,3},{3,1},{4,6},{6,4},{5,7},{7,5},{8,10},{10,8},{9,1... | collective-permute-start | bytes 1179656 | tf_op jit(solution)/shard_map/ppermute | solution.py:270
  74.8 11.4 %collective-permute-start.20 = (f32[384,128]{1,0:T(8,128)S(1)}, f32[384,128]{1,0:T(8,128)S(1)}, u32[]{:S(2)}, u32[]{:S(2)}) collective-permute-start(f32[384,128]{1,0:T(8,128)S(1)} %get-tuple-element.74), channel_id=1, source_target_pairs={{0,1},{1,0},{2,3},{3,2},{4,5},{5,4},{6,7},{7,6},{8,9},{9,8},{10,11... | collective-permute-start | bytes 589832 | tf_op jit(solution)/shard_map/ppermute | solution.py:270
  77.2 7.1 %collective-permute-start.22 = (bf16[128,128]{1,0:T(8,128)(2,1)S(1)}, bf16[128,128]{1,0:T(8,128)(2,1)S(1)}, u32[]{:S(2)}, u32[]{:S(2)}) collective-permute-start(bf16[128,128]{1,0:T(8,128)(2,1)S(1)} %get-tuple-element.78), channel_id=1, source_target_pairs={{8,0},{12,4},{2,10},{6,14},{9,1},{13,5},{3,11},{7,15},{24,16},{28,... | collective-permute-start | bytes 98312 | tf_op jit(solution)/shard_map/ppermute | solution.py:525
  78.5 7.7 %collective-permute-start.23 = (bf16[128,128]{1,0:T(8,128)(2,1)S(1)}, bf16[128,128]{1,0:T(8,128)(2,1)S(1)}, u32[]{:S(2)}, u32[]{:S(2)}) collective-permute-start(bf16[128,128]{1,0:T(8,128)(2,1)S(1)} %get-tuple-element.79), channel_id=1, source_target_pairs={{12,0},{8,4},{6,10},{2,14},{13,1},{9,5},{7,11},{3,15},{28,16},{24,... | collective-permute-start | bytes 98312 | tf_op jit(solution)/shard_map/ppermute | solution.py:525
  79.8 6.4 %collective-permute-start.24 = (bf16[128,128]{1,0:T(8,128)(2,1)S(1)}, bf16[128,128]{1,0:T(8,128)(2,1)S(1)}, u32[]{:S(2)}, u32[]{:S(2)}) collective-permute-start(bf16[128,128]{1,0:T(8,128)(2,1)S(1)} %get-tuple-element.80), channel_id=1, source_target_pairs={{4,0},{0,4},{14,10},{10,14},{5,1},{1,5},{15,11},{11,15},{20,16},{1... | collective-permute-start | bytes 98312 | tf_op jit(solution)/shard_map/ppermute | solution.py:525
  (10 other events, 56.5 us)

commit v12 on v11

--- a/solution.py
+++ b/solution.py
@@ -337,28 +337,29 @@
     )(*fields)
 
 
-def inner_rows_body(keep_ref, got_ref, tail_ref, *outs):
-    slab = lax.axis_index("slab")
-    chip = lax.axis_index("probe")
-    tail_ref[...] = keep_ref[2 * LANES :] + got_ref[2 * LANES :]
-    for d, out in enumerate(outs):
-        row = jnp.clip((slab ^ d) - 2 * chip, 0, 1)
-        span = pl.ds(pl.multiple_of(row * LANES, LANES), LANES)
-        out[...] = (keep_ref[span] + got_ref[span]).astype(out.dtype)
-
-
-def inner_rows(keep, got, slabs):
-    own = jax.ShapeDtypeStruct((LANES, LANES), F32)
-    sent = jax.ShapeDtypeStruct((LANES, LANES), BF16)
-    return call(
-        inner_rows_body,
+def inner_sum_body(keep_ref, got_ref, tail_ref, own_ref, sent_ref):
+    size = sent_ref.shape[0]
+    total = keep_ref[:size] + got_ref[:size]
+    own_ref[...] = total
+    sent_ref[...] = total.astype(BF16)
+    tail_ref[...] = keep_ref[size:] + got_ref[size:]
+
+
+def inner_sum(keep, got):
+    size = keep.shape[0] - 8
+    return call(
+        inner_sum_body,
         in_specs=whole_vmem(2),
-        out_specs=whole_vmem(1 + slabs),
-        out_shape=[jax.ShapeDtypeStruct((8, LANES), F32), own] + [sent] * (slabs - 1),
+        out_specs=whole_vmem(3),
+        out_shape=[
+            jax.ShapeDtypeStruct((8, LANES), F32),
+            jax.ShapeDtypeStruct((size, LANES), F32),
+            jax.ShapeDtypeStruct((size, LANES), BF16),
+        ],
     )(keep, got)
 
 
-def cross_body(kept0, got0, kept1, got1, keep_ref, send_ref, panel):
+def cross_body(kept0, got0, kept1, got1, _, keep_ref, send_ref, panel):
     chip = lax.axis_index("probe")
     core = lax.axis_index("sub")
     cells = panel.shape[0]
@@ -376,16 +377,16 @@
         ref[2 * LANES :] = mixed
 
 
-def cross_gram(fields):
+def cross_gram(fields, after):
     cells = math.prod(fields[0].shape[:3])
     three = jax.ShapeDtypeStruct((3 * LANES, LANES), F32)
     return call(
         cross_body,
-        in_specs=whole_vmem(4),
+        in_specs=whole_vmem(4) + [pl.BlockSpec(memory_space=pl.ANY)],
         out_specs=whole_vmem(2),
         out_shape=[three, three],
         scratch_shapes=[pltpu.VMEM((cells, 4 * LANES), BF16)],
-    )(*fields)
+    )(*fields, after)
 
 
 def rounded(ref, block, tail):
@@ -401,10 +402,10 @@
     return ref[:count].astype(F32), tail[:8] + tail[8:]
 
 
-def cross_rows_body(after, keep_ref, got_ref, tail_ref, *refs):
-    own_ref, *outs = refs[after:]
+def cross_rows_body(keep_ref, got_ref, tail_ref, inner_ref, inner_got_ref, own_ref, *outs):
     slab = lax.axis_index("slab")
     core = lax.axis_index("sub")
+    chip = lax.axis_index("probe")
     tail = tail_ref[...]
     for d in range(len(outs) + 1):
         owner = slab ^ d
@@ -412,45 +413,48 @@
         at = jnp.where(owner < 2, owner, late)
         span = pl.ds(pl.multiple_of(at * LANES, LANES), LANES)
         block = keep_ref[span] + got_ref[span]
+        row = pl.multiple_of(jnp.clip(owner - 2 * chip, 0, 1) * LANES, LANES)
+        inner = inner_ref[pl.ds(row, LANES)] + inner_got_ref[pl.ds(row, LANES)].astype(F32)
         if d == 0:
             own_ref[:LANES] = block
-            own_ref[LANES:] = tail
+            own_ref[LANES : LANES + 8] = tail
+            own_ref[LANES + 8 :] = inner
         else:
             rounded(outs[d - 1], block, tail)
-
-
-def cross_rows(keep, got, tail, slabs, after):
-    own = jax.ShapeDtypeStruct((LANES + 8, LANES), F32)
-    sent = jax.ShapeDtypeStruct((LANES + 16, LANES), BF16)
-    return call(
-        functools.partial(cross_rows_body, len(after)),
-        in_specs=whole_vmem(3) + [pl.BlockSpec(memory_space=pl.ANY)] * len(after),
+            if d == 1:
+                outs[0][LANES + 16 :] = inner.astype(BF16)
+
+
+def cross_rows(keep, got, tail, inner, inner_got, slabs):
+    own = jax.ShapeDtypeStruct((2 * LANES + 8, LANES), F32)
+    near = jax.ShapeDtypeStruct((2 * LANES + 16, LANES), BF16)
+    far = jax.ShapeDtypeStruct((LANES + 16, LANES), BF16)
+    return call(
+        cross_rows_body,
+        in_specs=whole_vmem(5),
         out_specs=whole_vmem(slabs),
-        out_shape=[own] + [sent] * (slabs - 1),
-    )(keep, got, tail, *after)
-
-
-def sum_body(slabs, own_ref, *refs):
-    block, tail = own_ref[:LANES], own_ref[LANES:]
-    for ref in refs[: slabs - 1]:
+        out_shape=[own, near] + [far] * (slabs - 2),
+    )(keep, got, tail, inner, inner_got)
+
+
+def sum_body(own_ref, *refs):
+    block, tail = own_ref[:LANES], own_ref[LANES : LANES + 8]
+    *others, out_ref = refs
+    for ref in others:
         more, more_tail = opened(ref, LANES)
         block, tail = block + more, tail + more_tail
-    inner = refs[slabs - 1][...]
-    for ref in refs[slabs : 2 * slabs - 1]:
-        inner = inner + ref[...].astype(F32)
-    out_ref = refs[-1]
+    inner = own_ref[LANES + 8 :] + others[-1][LANES + 16 :].astype(F32)
     rounded(out_ref, block, tail)
     out_ref[LANES + 16 :] = inner.astype(BF16)
 
 
-def sum_all(own, others, inner, inner_others):
-    slabs = 1 + len(others)
-    return call(
-        functools.partial(sum_body, slabs),
-        in_specs=whole_vmem(2 * slabs),
+def sum_all(own, others):
+    return call(
+        sum_body,
+        in_specs=whole_vmem(1 + len(others)),
         out_specs=whole_vmem(1)[0],
-        out_shape=jax.ShapeDtypeStruct((2 * LANES + 16, LANES), BF16),
-    )(own, *others, inner, *inner_others)
+        out_shape=jax.ShapeDtypeStruct(others[-1].shape, BF16),
+    )(own, *others)
 
 
 def normalise_body(cell_count, mine_ref, other_ref, out_ref, norms_ref):
@@ -514,24 +518,20 @@
     slabs = 4
     own = [field for kept, sent, _ in finals for field in (kept, sent)]
     keep, send = inner_gram(own)
-    tail, *inner = inner_rows(keep, core_swap(send), slabs)
-    inner_arrived = []
-    for d in (2, 3, 1):
-        pairs = [
-            (2 * (k ^ d) + chip, 2 * k + chip)
-            for chip in range(2)
-            for k in (2 * chip, 2 * chip + 1)
-        ]
-        inner_arrived.append(lax.ppermute(inner[d], ("slab", "probe"), pairs))
+    tail, inner, sent = inner_sum(keep, core_swap(send))
+    pairs = [
+        (2 * (k ^ 2) + chip, 2 * k + chip) for chip in range(2) for k in (2 * chip, 2 * chip + 1)
+    ]
+    inner_got = lax.ppermute(sent, ("slab", "probe"), pairs)
 
     pairs = [field for kept, _, got in finals for field in (kept, got)]
-    keep, send = cross_gram(pairs)
-    mine, *blocks = cross_rows(keep, core_swap(send), tail, slabs, inner_arrived)
+    keep, send = cross_gram(pairs, inner_got)
+    mine, *blocks = cross_rows(keep, core_swap(send), tail, inner, inner_got, slabs)
     arrived = [
         lax.ppermute(blocks[d - 1], "slab", [(i, i ^ d) for i in range(slabs)])
         for d in (2, 3, 1)
     ]
-    total = sum_all(mine, arrived, inner[0], inner_arrived)
+    total = sum_all(mine, arrived)
     near, norms = normalise(total, chip_swap(total), cell_count)
     return assemble(near, core_swap(near)), norms.reshape(-1)
 

time: 101 us -> 92.8 us (0.919)
  starting transfers between devices: 40.9 us -> 36.8 us
  waiting for transfers between devices: 31.7 us -> 27.8 us
    ppermute x24, waiting for transfers between devices: 25 us -> 17.4 us  [swap(): lax.ppermute(x, axis, [p for a, b in pairs for p in ((a, b), (b, a))])]
    ppermute x3 -> x1, starting transfers between devices: 5.9 us -> 1.29 us  [coupled(): inner_got = lax.ppermute(sent, ('slab', 'probe'), pairs)]
    ppermute x3 -> x1, waiting for transfers between devices: 3.09 us -> 7.16 us  [coupled(): inner_got = lax.ppermute(sent, ('slab', 'probe'), pairs)]
  transfers between devices with their start and end apart: 30 -> 28, of which waited for: 17 -> 13; matrix products, arithmetic and copies ran while one was open for 0% -> 0% of each run, Pallas kernels for 21% -> 23%
where the time goes in v12:
time: 92.8 us; the launch traced here: 92.4 us
  starting transfers between devices  36.8 us (40%)
  waiting for transfers between devices  27.8 us (30%)
  Pallas kernels  24.7 us (27%)
  local copies, waits for them, and re-layouts  2.18 us (2%)
  between operations  0.99 us (1%)
    ppermute x24, starting transfers between devices, swap(): lax.ppermute(x, axis, [p for a, b in pairs for p in ((a, b), (b, a))])  31.1 us
    ppermute x24, waiting for transfers between devices, swap(): lax.ppermute(x, axis, [p for a, b in pairs for p in ((a, b), (b, a))])  17.4 us
    pallas_call x6, Pallas kernels, local_step(): call(functools.partial(local_body, chunk, moment, previous is not None),...  13.3 us
    ppermute x1, waiting for transfers between devices, coupled(): inner_got = lax.ppermute(sent, ('slab', 'probe'), pairs)  7.16 us
    pallas_call x6, Pallas kernels, rim_step(): call(functools.partial(rim_body, kind), in_specs=whole_vmem(4), out_specs...  6.31 us
    ppermute x3, starting transfers between devices, coupled(): lax.ppermute(blocks[d - 1], 'slab', [(i, i ^ d) for i in range(slabs)])  4.45 us
    ppermute x3, waiting for transfers between devices, coupled(): lax.ppermute(blocks[d - 1], 'slab', [(i, i ^ d) for i in range(slabs)])  3.21 us
    pallas_call x2, Pallas kernels, first_field(): call(functools.partial(first_body, chunk), in_specs=whole_vmem(2), out_sp...  2.1 us
  transfers between devices with their start and end apart: 28, of which 13 were waited for; matrix products, arithmetic and copies ran while one was open for 0% of the time, Pallas kernels for 23%

profile of v12, /device:TPU:0, one launch (start us, length us, event | category | flops | bytes accessed | tf_op | source)
XLA Modules:
  0.0 92.4 jit_solution(4406722037277124986)
XLA Ops:
  1.4 1.4 %copy-done = bf16[8,8,48,256]{3,2,1,0:T(8,128)(2,1)S(1)} copy-done((bf16[8,8,48,256]{3,2,1,0:T(8,128)(2,1)S(1)}, bf16[8,8,48,256]{3,2,1,0:T(8,128)(2,1)}, u32[]{:S(2)}) %copy-start) | copy-done | bytes 1572888
  5.1 5.5 %collective-permute-start.12 = (bf16[4,8,48,128]{3,2,1,0:T(8,128)(2,1)S(1)}, bf16[4,8,48,128]{3,2,1,0:T(8,128)(2,1)S(1)}, u32[]{:S(2)}, u32[]{:S(2)}) collective-permute-start(bf16[4,8,48,128]{3,2,1,0:T(8,128)(2,1)S(1)} %get-tuple-element.60), channel_id=1, source_target_pairs={{0,4},{4,0},{8,12},{12,8},{1,5},{5,1},{9,13},{13,9},{2,6},{6,2},{1... | collective-permute-start | bytes 1179656 | tf_op jit(solution)/shard_map/ppermute | solution.py:270
  12.4 1.9 %collective-permute-start.2 = (bf16[4,8,48,128]{3,2,1,0:T(8,128)(2,1)S(1)}, bf16[4,8,48,128]{3,2,1,0:T(8,128)(2,1)S(1)}, u32[]{:S(2)}, u32[]{:S(2)}) collective-permute-start(bf16[4,8,48,128]{3,2,1,0:T(8,128)(2,1)S(1)} %get-tuple-element.46), channel_id=1, source_target_pairs={{0,4},{4,0},{8,12},{12,8},{1,5},{5,1},{9,13},{13,9},{2,6},{6,2},{1... | collective-permute-start | bytes 1179656 | tf_op jit(solution)/shard_map/ppermute | solution.py:270
  14.3 2.1 %shard_map.58.refs_0_ = f32[8,8,48,128]{3,2,1,0:T(8,128)S(1)} custom-call(f32[8,8,64,128]{3,2,1,0:T(8,128)S(1)} %get-tuple-element.57.refs_0_.refs_5_, bf16[8,4,48,128]{3,2,1,0:T(8,128)(2,1)S(1)} %collective-permute-done.10.refs_1_, bf16[8,8,48,256]{3,2,1,0:T(8,128)(2,1)S(1)} %copy-done, f32[64,48]{1,0:T(8,128)S(1)} %bitcast.11, f32[4,64,48]{2,1,0:T(8,128)S(1)} %bitcast.5), custom_call_target="tpu_custom_call" | custom-call | flops 1 | bytes 1 | tf_op jit(solution)/shard_map/pallas_call | solution.py:185
  16.5 3.9 %collective-permute-done.12.refs_2_ = bf16[4,8,48,128]{3,2,1,0:T(8,128)(2,1)S(1)} collective-permute-done((bf16[4,8,48,128]{3,2,1,0:T(8,128)(2,1)S(1)}, bf16[4,8,48,128]{3,2,1,0:T(8,128)(2,1)S(1)}, u32[]{:S(2)}, u32[]{:S(2)}) %collective-permute-start.12) | collective-permute-done | bytes 393248 | tf_op jit(solution)/shard_map/ppermute | solution.py:270
  22.3 3.8 %collective-permute-start.15 = (bf16[4,8,48,128]{3,2,1,0:T(8,128)(2,1)S(1)}, bf16[4,8,48,128]{3,2,1,0:T(8,128)(2,1)S(1)}, u32[]{:S(2)}, u32[]{:S(2)}) collective-permute-start(bf16[4,8,48,128]{3,2,1,0:T(8,128)(2,1)S(1)} %get-tuple-element.64), channel_id=1, source_target_pairs={{0,4},{4,0},{8,12},{12,8},{1,5},{5,1},{9,13},{13,9},{2,6},{6,2},{1... | collective-permute-start | bytes 1179656 | tf_op jit(solution)/shard_map/ppermute | solution.py:270
  26.1 2.1 %shard_map.51.refs_0_ = f32[8,8,48,128]{3,2,1,0:T(8,128)S(1)} custom-call(f32[8,8,64,128]{3,2,1,0:T(8,128)S(1)} %get-tuple-element.43.refs_0_.refs_5_, bf16[8,4,48,128]{3,2,1,0:T(8,128)(2,1)S(1)} %collective-permute-done.refs_1_, bf16[8,8,48,256]{3,2,1,0:T(8,128)(2,1)S(1)} %copy-done.1, f32[64,48]{1,0:T(8,128)S(1)} %bitcast.13, f32[4,64,48]{2,1,0:T(8,128)S(1)} %bitcast.6), custom_call_target="tpu_custom_call" | custom-call | flops 1 | bytes 1 | tf_op jit(solution)/shard_map/pallas_call | solution.py:185
  30.7 3.4 %collective-permute-start.5 = (bf16[4,8,48,128]{3,2,1,0:T(8,128)(2,1)S(1)}, bf16[4,8,48,128]{3,2,1,0:T(8,128)(2,1)S(1)}, u32[]{:S(2)}, u32[]{:S(2)}) collective-permute-start(bf16[4,8,48,128]{3,2,1,0:T(8,128)(2,1)S(1)} %get-tuple-element.50), channel_id=1, source_target_pairs={{0,4},{4,0},{8,12},{12,8},{1,5},{5,1},{9,13},{13,9},{2,6},{6,2},{1... | collective-permute-start | bytes 1179656 | tf_op jit(solution)/shard_map/ppermute | solution.py:270
  34.1 2.3 %shard_map.60.refs_0_ = f32[8,8,48,128]{3,2,1,0:T(8,128)S(1)} custom-call(f32[8,8,64,128]{3,2,1,0:T(8,128)S(1)} %get-tuple-element.61.refs_0_.refs_5_, bf16[8,4,48,128]{3,2,1,0:T(8,128)(2,1)S(1)} %collective-permute-done.13.refs_1_, bf16[8,8,48,256]{3,2,1,0:T(8,128)(2,1)S(1)} %copy-done.1, f32[64,48]{1,0:T(8,128)S(1)} %bitcast.15, f32[4,64,48]{2,1,0:T(8,128)S(1)} %bitcast.7, ...), custom_call_target="tpu_custom_call" | custom-call | flops 1 | bytes 1 | tf_op jit(solution)/shard_map/pallas_call | solution.py:185
  39.2 3.4 %collective-permute-start.18 = (bf16[4,8,48,128]{3,2,1,0:T(8,128)(2,1)S(1)}, bf16[4,8,48,128]{3,2,1,0:T(8,128)(2,1)S(1)}, u32[]{:S(2)}, u32[]{:S(2)}) collective-permute-start(bf16[4,8,48,128]{3,2,1,0:T(8,128)(2,1)S(1)} %get-tuple-element.68), channel_id=1, source_target_pairs={{0,4},{4,0},{8,12},{12,8},{1,5},{5,1},{9,13},{13,9},{2,6},{6,2},{1... | collective-permute-start | bytes 1179656 | tf_op jit(solution)/shard_map/ppermute | solution.py:270
  42.5 2.2 %shard_map.53.refs_0_ = f32[8,8,48,128]{3,2,1,0:T(8,128)S(1)} custom-call(f32[8,8,64,128]{3,2,1,0:T(8,128)S(1)} %get-tuple-element.47.refs_0_.refs_5_, bf16[8,4,48,128]{3,2,1,0:T(8,128)(2,1)S(1)} %collective-permute-done.3.refs_1_, bf16[8,8,48,256]{3,2,1,0:T(8,128)(2,1)S(1)} %copy-done.1, f32[64,48]{1,0:T(8,128)S(1)} %bitcast.17, f32[4,64,48]{2,1,0:T(8,128)S(1)} %bitcast.8, ...), custom_call_target="tpu_custom_call" | custom-call | flops 1 | bytes 1 | tf_op jit(solution)/shard_map/pallas_call | solution.py:185
  47.6 3.4 %collective-permute-start.8 = (bf16[4,8,48,128]{3,2,1,0:T(8,128)(2,1)S(1)}, bf16[4,8,48,128]{3,2,1,0:T(8,128)(2,1)S(1)}, u32[]{:S(2)}, u32[]{:S(2)}) collective-permute-start(bf16[4,8,48,128]{3,2,1,0:T(8,128)(2,1)S(1)} %get-tuple-element.54), channel_id=1, source_target_pairs={{0,4},{4,0},{8,12},{12,8},{1,5},{5,1},{9,13},{13,9},{2,6},{6,2},{1... | collective-permute-start | bytes 1179656 | tf_op jit(solution)/shard_map/ppermute | solution.py:270
  50.9 2.3 %shard_map.62.refs_0_ = f32[8,8,48,128]{3,2,1,0:T(8,128)S(1)} custom-call(f32[8,8,64,128]{3,2,1,0:T(8,128)S(1)} %get-tuple-element.65.refs_0_, bf16[8,4,48,128]{3,2,1,0:T(8,128)(2,1)S(1)} %collective-permute-done.16.refs_1_, bf16[8,8,48,256]{3,2,1,0:T(8,128)(2,1)S(1)} %copy-done.1, f32[64,48]{1,0:T(8,128)S(1)} %bitcast.19, f32[4,64,48]{2,1,0:T(8,128)S(1)} %bitcast.9, ...), custom_call_target="tpu_custom_call" | custom-call | flops 1 | bytes 1 | tf_op jit(solution)/shard_map/pallas_call | solution.py:185
  55.1 1.6 %collective-permute-start.19 = (bf16[4,8,48,128]{3,2,1,0:T(8,128)(2,1)S(1)}, bf16[4,8,48,128]{3,2,1,0:T(8,128)(2,1)S(1)}, u32[]{:S(2)}, u32[]{:S(2)}) collective-permute-start(bf16[4,8,48,128]{3,2,1,0:T(8,128)(2,1)S(1)} %get-tuple-element.70.sent1), channel_id=1, source_target_pairs={{0,2},{2,0},{1,3},{3,1},{4,6},{6,4},{5,7},{7,5},{8,10},{10,8},{9,1... | collective-permute-start | bytes 1179656 | tf_op jit(solution)/shard_map/ppermute | solution.py:270
  56.6 2.2 %shard_map.55.refs_0_ = f32[8,8,48,128]{3,2,1,0:T(8,128)S(1)} custom-call(f32[8,8,64,128]{3,2,1,0:T(8,128)S(1)} %get-tuple-element.51.refs_0_, bf16[8,4,48,128]{3,2,1,0:T(8,128)(2,1)S(1)} %collective-permute-done.6.refs_1_, bf16[8,8,48,256]{3,2,1,0:T(8,128)(2,1)S(1)} %copy-done.1, f32[64,48]{1,0:T(8,128)S(1)} %bitcast.21, f32[4,64,48]{2,1,0:T(8,128)S(1)} %bitcast.10, ...), custom_call_target="tpu_custom_call" | custom-call | flops 1 | bytes 1 | tf_op jit(solution)/shard_map/pallas_call | solution.py:185
  58.9 3.2 %collective-permute-done.8.refs_2_ = bf16[4,8,48,128]{3,2,1,0:T(8,128)(2,1)S(1)} collective-permute-done((bf16[4,8,48,128]{3,2,1,0:T(8,128)(2,1)S(1)}, bf16[4,8,48,128]{3,2,1,0:T(8,128)(2,1)S(1)}, u32[]{:S(2)}, u32[]{:S(2)}) %collective-permute-start.8) | collective-permute-done | bytes 393248 | tf_op jit(solution)/shard_map/ppermute | solution.py:270
  63.1 1.6 %collective-permute-start.9 = (bf16[4,8,48,128]{3,2,1,0:T(8,128)(2,1)S(1)}, bf16[4,8,48,128]{3,2,1,0:T(8,128)(2,1)S(1)}, u32[]{:S(2)}, u32[]{:S(2)}) collective-permute-start(bf16[4,8,48,128]{3,2,1,0:T(8,128)(2,1)S(1)} %get-tuple-element.56.sent0), channel_id=1, source_target_pairs={{0,2},{2,0},{1,3},{3,1},{4,6},{6,4},{5,7},{7,5},{8,10},{10,8},{9,1... | collective-permute-start | bytes 1179656 | tf_op jit(solution)/shard_map/ppermute | solution.py:270
  68.1 7.2 %collective-permute-done.21._.inner_got_ref = bf16[256,128]{1,0:T(8,128)(2,1)S(1)} collective-permute-done((bf16[256,128]{1,0:T(8,128)(2,1)S(1)}, bf16[256,128]{1,0:T(8,128)(2,1)S(1)}, u32[]{:S(2)}, u32[]{:S(2)}) %collective-permute-start.21) | collective-permute-done | bytes 65568 | tf_op jit(solution)/shard_map/ppermute | solution.py:525
  76.2 1.4 %collective-permute-done.22.got_ref = f32[384,128]{1,0:T(8,128)S(1)} collective-permute-done((f32[384,128]{1,0:T(8,128)S(1)}, f32[384,128]{1,0:T(8,128)S(1)}, u32[]{:S(2)}, u32[]{:S(2)}) %collective-permute-start.22) | collective-permute-done | bytes 196640 | tf_op jit(solution)/shard_map/ppermute | solution.py:270
  78.1 1.5 %collective-permute-start.23 = (bf16[144,128]{1,0:T(8,128)(2,1)S(1)}, bf16[144,128]{1,0:T(8,128)(2,1)S(1)}, u32[]{:S(2)}, u32[]{:S(2)}) collective-permute-start(bf16[144,128]{1,0:T(8,128)(2,1)S(1)} %get-tuple-element.79), channel_id=1, source_target_pairs={{0,8},{4,12},{8,0},{12,4},{1,9},{5,13},{9,1},{13,5},{2,10},{6,14},... | collective-permute-start | bytes 110600 | tf_op jit(solution)/shard_map/ppermute | solution.py:531
  79.6 2.5 %collective-permute-start.24 = (bf16[144,128]{1,0:T(8,128)(2,1)S(1)}, bf16[144,128]{1,0:T(8,128)(2,1)S(1)}, u32[]{:S(2)}, u32[]{:S(2)}) collective-permute-start(bf16[144,128]{1,0:T(8,128)(2,1)S(1)} %get-tuple-element.80), channel_id=1, source_target_pairs={{0,12},{4,8},{8,4},{12,0},{1,13},{5,9},{9,5},{13,1},{2,14},{6,10},... | collective-permute-start | bytes 110600 | tf_op jit(solution)/shard_map/ppermute | solution.py:531
  83.4 2.0 %collective-permute-done.24.refs_1_ = bf16[144,128]{1,0:T(8,128)(2,1)S(1)} collective-permute-done((bf16[144,128]{1,0:T(8,128)(2,1)S(1)}, bf16[144,128]{1,0:T(8,128)(2,1)S(1)}, u32[]{:S(2)}, u32[]{:S(2)}) %collective-permute-start.24) | collective-permute-done | bytes 36896 | tf_op jit(solution)/shard_map/ppermute | solution.py:531
  85.4 1.6 %collective-permute-start.26 = (bf16[272,128]{1,0:T(8,128)(2,1)S(1)}, bf16[272,128]{1,0:T(8,128)(2,1)S(1)}, u32[]{:S(2)}, u32[]{:S(2)}) collective-permute-start(bf16[272,128]{1,0:T(8,128)(2,1)S(1)} %shard_map.68.mine_ref), channel_id=1, source_target_pairs={{0,2},{2,0},{1,3},{3,1},{4,6},{6,4},{5,7},{7,5},{8,10},{10,8},{9,1... | collective-permute-start | bytes 208904 | tf_op jit(solution)/shard_map/ppermute | solution.py:270
  87.0 2.8 %collective-permute-done.26.other_ref = bf16[272,128]{1,0:T(8,128)(2,1)S(1)} collective-permute-done((bf16[272,128]{1,0:T(8,128)(2,1)S(1)}, bf16[272,128]{1,0:T(8,128)(2,1)S(1)}, u32[]{:S(2)}, u32[]{:S(2)}) %collective-permute-start.26) | collective-permute-done | bytes 69664 | tf_op jit(solution)/shard_map/ppermute | solution.py:270
  (62 shorter events, 26.2 us)
Async XLA Ops:
  3.9 8.5 %collective-permute-start.10 = (bf16[8,4,48,128]{3,2,1,0:T(8,128)(2,1)S(1)}, bf16[8,4,48,128]{3,2,1,0:T(8,128)(2,1)S(1)}, u32[]{:S(2)}, u32[]{:S(2)}) collective-permute-start(bf16[8,4,48,128]{3,2,1,0:T(8,128)(2,1)S(1)} %get-tuple-element.58), channel_id=1, source_target_pairs={{0,1},{1,0},{2,3},{3,2},{4,5},{5,4},{6,7},{7,6},{8,9},{9,8},{10,11... | collective-permute-start | bytes 1179656 | tf_op jit(solution)/shard_map/ppermute | solution.py:270
  4.4 12.1 %collective-permute-start.11 = (bf16[4,8,48,128]{3,2,1,0:T(8,128)(2,1)S(1)}, bf16[4,8,48,128]{3,2,1,0:T(8,128)(2,1)S(1)}, u32[]{:S(2)}, u32[]{:S(2)}) collective-permute-start(bf16[4,8,48,128]{3,2,1,0:T(8,128)(2,1)S(1)} %get-tuple-element.59), channel_id=1, source_target_pairs={{4,8},{8,4},{5,9},{9,5},{6,10},{10,6},{7,11},{11,7},{20,24},{24,20... | collective-permute-start | bytes 1179656 | tf_op jit(solution)/shard_map/ppermute | solution.py:270
  5.1 15.4 %collective-permute-start.12 = (bf16[4,8,48,128]{3,2,1,0:T(8,128)(2,1)S(1)}, bf16[4,8,48,128]{3,2,1,0:T(8,128)(2,1)S(1)}, u32[]{:S(2)}, u32[]{:S(2)}) collective-permute-start(bf16[4,8,48,128]{3,2,1,0:T(8,128)(2,1)S(1)} %get-tuple-element.60), channel_id=1, source_target_pairs={{0,4},{4,0},{8,12},{12,8},{1,5},{5,1},{9,13},{13,9},{2,6},{6,2},{1... | collective-permute-start | bytes 1179656 | tf_op jit(solution)/shard_map/ppermute | solution.py:270
  11.6 10.7 %collective-permute-start = (bf16[8,4,48,128]{3,2,1,0:T(8,128)(2,1)S(1)}, bf16[8,4,48,128]{3,2,1,0:T(8,128)(2,1)S(1)}, u32[]{:S(2)}, u32[]{:S(2)}) collective-permute-start(bf16[8,4,48,128]{3,2,1,0:T(8,128)(2,1)S(1)} %get-tuple-element.44), channel_id=1, source_target_pairs={{0,1},{1,0},{2,3},{3,2},{4,5},{5,4},{6,7},{7,6},{8,9},{9,8},{10,11... | collective-permute-start | bytes 1179656 | tf_op jit(solution)/shard_map/ppermute | solution.py:270
  11.7 16.6 %collective-permute-start.1 = (bf16[4,8,48,128]{3,2,1,0:T(8,128)(2,1)S(1)}, bf16[4,8,48,128]{3,2,1,0:T(8,128)(2,1)S(1)}, u32[]{:S(2)}, u32[]{:S(2)}) collective-permute-start(bf16[4,8,48,128]{3,2,1,0:T(8,128)(2,1)S(1)} %get-tuple-element.45), channel_id=1, source_target_pairs={{4,8},{8,4},{5,9},{9,5},{6,10},{10,6},{7,11},{11,7},{20,24},{24,20... | collective-permute-start | bytes 1179656 | tf_op jit(solution)/shard_map/ppermute | solution.py:270
  12.4 16.5 %collective-permute-start.2 = (bf16[4,8,48,128]{3,2,1,0:T(8,128)(2,1)S(1)}, bf16[4,8,48,128]{3,2,1,0:T(8,128)(2,1)S(1)}, u32[]{:S(2)}, u32[]{:S(2)}) collective-permute-start(bf16[4,8,48,128]{3,2,1,0:T(8,128)(2,1)S(1)} %get-tuple-element.46), channel_id=1, source_target_pairs={{0,4},{4,0},{8,12},{12,8},{1,5},{5,1},{9,13},{13,9},{2,6},{6,2},{1... | collective-permute-start | bytes 1179656 | tf_op jit(solution)/shard_map/ppermute | solution.py:270
  21.5 9.2 %collective-permute-start.13 = (bf16[8,4,48,128]{3,2,1,0:T(8,128)(2,1)S(1)}, bf16[8,4,48,128]{3,2,1,0:T(8,128)(2,1)S(1)}, u32[]{:S(2)}, u32[]{:S(2)}) collective-permute-start(bf16[8,4,48,128]{3,2,1,0:T(8,128)(2,1)S(1)} %get-tuple-element.62), channel_id=1, source_target_pairs={{0,1},{1,0},{2,3},{3,2},{4,5},{5,4},{6,7},{7,6},{8,9},{9,8},{10,11... | collective-permute-start | bytes 1179656 | tf_op jit(solution)/shard_map/ppermute | solution.py:270
  21.6 14.8 %collective-permute-start.14 = (bf16[4,8,48,128]{3,2,1,0:T(8,128)(2,1)S(1)}, bf16[4,8,48,128]{3,2,1,0:T(8,128)(2,1)S(1)}, u32[]{:S(2)}, u32[]{:S(2)}) collective-permute-start(bf16[4,8,48,128]{3,2,1,0:T(8,128)(2,1)S(1)} %get-tuple-element.63), channel_id=1, source_target_pairs={{4,8},{8,4},{5,9},{9,5},{6,10},{10,6},{7,11},{11,7},{20,24},{24,20... | collective-permute-start | bytes 1179656 | tf_op jit(solution)/shard_map/ppermute | solution.py:270
  22.3 15.0 %collective-permute-start.15 = (bf16[4,8,48,128]{3,2,1,0:T(8,128)(2,1)S(1)}, bf16[4,8,48,128]{3,2,1,0:T(8,128)(2,1)S(1)}, u32[]{:S(2)}, u32[]{:S(2)}) collective-permute-start(bf16[4,8,48,128]{3,2,1,0:T(8,128)(2,1)S(1)} %get-tuple-element.64), channel_id=1, source_target_pairs={{0,4},{4,0},{8,12},{12,8},{1,5},{5,1},{9,13},{13,9},{2,6},{6,2},{1... | collective-permute-start | bytes 1179656 | tf_op jit(solution)/shard_map/ppermute | solution.py:270
  29.9 9.2 %collective-permute-start.3 = (bf16[8,4,48,128]{3,2,1,0:T(8,128)(2,1)S(1)}, bf16[8,4,48,128]{3,2,1,0:T(8,128)(2,1)S(1)}, u32[]{:S(2)}, u32[]{:S(2)}) collective-permute-start(bf16[8,4,48,128]{3,2,1,0:T(8,128)(2,1)S(1)} %get-tuple-element.48), channel_id=1, source_target_pairs={{0,1},{1,0},{2,3},{3,2},{4,5},{5,4},{6,7},{7,6},{8,9},{9,8},{10,11... | collective-permute-start | bytes 1179656 | tf_op jit(solution)/shard_map/ppermute | solution.py:270
  30.0 14.8 %collective-permute-start.4 = (bf16[4,8,48,128]{3,2,1,0:T(8,128)(2,1)S(1)}, bf16[4,8,48,128]{3,2,1,0:T(8,128)(2,1)S(1)}, u32[]{:S(2)}, u32[]{:S(2)}) collective-permute-start(bf16[4,8,48,128]{3,2,1,0:T(8,128)(2,1)S(1)} %get-tuple-element.49), channel_id=1, source_target_pairs={{4,8},{8,4},{5,9},{9,5},{6,10},{10,6},{7,11},{11,7},{20,24},{24,20... | collective-permute-start | bytes 1179656 | tf_op jit(solution)/shard_map/ppermute | solution.py:270
  30.7 15.0 %collective-permute-start.5 = (bf16[4,8,48,128]{3,2,1,0:T(8,128)(2,1)S(1)}, bf16[4,8,48,128]{3,2,1,0:T(8,128)(2,1)S(1)}, u32[]{:S(2)}, u32[]{:S(2)}) collective-permute-start(bf16[4,8,48,128]{3,2,1,0:T(8,128)(2,1)S(1)} %get-tuple-element.50), channel_id=1, source_target_pairs={{0,4},{4,0},{8,12},{12,8},{1,5},{5,1},{9,13},{13,9},{2,6},{6,2},{1... | collective-permute-start | bytes 1179656 | tf_op jit(solution)/shard_map/ppermute | solution.py:270
  38.4 9.2 %collective-permute-start.16 = (bf16[8,4,48,128]{3,2,1,0:T(8,128)(2,1)S(1)}, bf16[8,4,48,128]{3,2,1,0:T(8,128)(2,1)S(1)}, u32[]{:S(2)}, u32[]{:S(2)}) collective-permute-start(bf16[8,4,48,128]{3,2,1,0:T(8,128)(2,1)S(1)} %get-tuple-element.66), channel_id=1, source_target_pairs={{0,1},{1,0},{2,3},{3,2},{4,5},{5,4},{6,7},{7,6},{8,9},{9,8},{10,11... | collective-permute-start | bytes 1179656 | tf_op jit(solution)/shard_map/ppermute | solution.py:270
  38.5 14.8 %collective-permute-start.17 = (bf16[4,8,48,128]{3,2,1,0:T(8,128)(2,1)S(1)}, bf16[4,8,48,128]{3,2,1,0:T(8,128)(2,1)S(1)}, u32[]{:S(2)}, u32[]{:S(2)}) collective-permute-start(bf16[4,8,48,128]{3,2,1,0:T(8,128)(2,1)S(1)} %get-tuple-element.67), channel_id=1, source_target_pairs={{4,8},{8,4},{5,9},{9,5},{6,10},{10,6},{7,11},{11,7},{20,24},{24,20... | collective-permute-start | bytes 1179656 | tf_op jit(solution)/shard_map/ppermute | solution.py:270
  39.2 15.0 %collective-permute-start.18 = (bf16[4,8,48,128]{3,2,1,0:T(8,128)(2,1)S(1)}, bf16[4,8,48,128]{3,2,1,0:T(8,128)(2,1)S(1)}, u32[]{:S(2)}, u32[]{:S(2)}) collective-permute-start(bf16[4,8,48,128]{3,2,1,0:T(8,128)(2,1)S(1)} %get-tuple-element.68), channel_id=1, source_target_pairs={{0,4},{4,0},{8,12},{12,8},{1,5},{5,1},{9,13},{13,9},{2,6},{6,2},{1... | collective-permute-start | bytes 1179656 | tf_op jit(solution)/shard_map/ppermute | solution.py:270
  46.8 9.8 %collective-permute-start.6 = (bf16[8,4,48,128]{3,2,1,0:T(8,128)(2,1)S(1)}, bf16[8,4,48,128]{3,2,1,0:T(8,128)(2,1)S(1)}, u32[]{:S(2)}, u32[]{:S(2)}) collective-permute-start(bf16[8,4,48,128]{3,2,1,0:T(8,128)(2,1)S(1)} %get-tuple-element.52), channel_id=1, source_target_pairs={{0,1},{1,0},{2,3},{3,2},{4,5},{5,4},{6,7},{7,6},{8,9},{9,8},{10,11... | collective-permute-start | bytes 1179656 | tf_op jit(solution)/shard_map/ppermute | solution.py:270
  46.9 12.0 %collective-permute-start.7 = (bf16[4,8,48,128]{3,2,1,0:T(8,128)(2,1)S(1)}, bf16[4,8,48,128]{3,2,1,0:T(8,128)(2,1)S(1)}, u32[]{:S(2)}, u32[]{:S(2)}) collective-permute-start(bf16[4,8,48,128]{3,2,1,0:T(8,128)(2,1)S(1)} %get-tuple-element.53), channel_id=1, source_target_pairs={{4,8},{8,4},{5,9},{9,5},{6,10},{10,6},{7,11},{11,7},{20,24},{24,20... | collective-permute-start | bytes 1179656 | tf_op jit(solution)/shard_map/ppermute | solution.py:270
  47.6 14.6 %collective-permute-start.8 = (bf16[4,8,48,128]{3,2,1,0:T(8,128)(2,1)S(1)}, bf16[4,8,48,128]{3,2,1,0:T(8,128)(2,1)S(1)}, u32[]{:S(2)}, u32[]{:S(2)}) collective-permute-start(bf16[4,8,48,128]{3,2,1,0:T(8,128)(2,1)S(1)} %get-tuple-element.54), channel_id=1, source_target_pairs={{0,4},{4,0},{8,12},{12,8},{1,5},{5,1},{9,13},{13,9},{2,6},{6,2},{1... | collective-permute-start | bytes 1179656 | tf_op jit(solution)/shard_map/ppermute | solution.py:270
  55.1 20.2 %collective-permute-start.19 = (bf16[4,8,48,128]{3,2,1,0:T(8,128)(2,1)S(1)}, bf16[4,8,48,128]{3,2,1,0:T(8,128)(2,1)S(1)}, u32[]{:S(2)}, u32[]{:S(2)}) collective-permute-start(bf16[4,8,48,128]{3,2,1,0:T(8,128)(2,1)S(1)} %get-tuple-element.70.sent1), channel_id=1, source_target_pairs={{0,2},{2,0},{1,3},{3,1},{4,6},{6,4},{5,7},{7,5},{8,10},{10,8},{9,1... | collective-permute-start | bytes 1179656 | tf_op jit(solution)/shard_map/ppermute | solution.py:270
  63.1 12.2 %collective-permute-start.9 = (bf16[4,8,48,128]{3,2,1,0:T(8,128)(2,1)S(1)}, bf16[4,8,48,128]{3,2,1,0:T(8,128)(2,1)S(1)}, u32[]{:S(2)}, u32[]{:S(2)}) collective-permute-start(bf16[4,8,48,128]{3,2,1,0:T(8,128)(2,1)S(1)} %get-tuple-element.56.sent0), channel_id=1, source_target_pairs={{0,2},{2,0},{1,3},{3,1},{4,6},{6,4},{5,7},{7,5},{8,10},{10,8},{9,1... | collective-permute-start | bytes 1179656 | tf_op jit(solution)/shard_map/ppermute | solution.py:270
  66.8 8.5 %collective-permute-start.21 = (bf16[256,128]{1,0:T(8,128)(2,1)S(1)}, bf16[256,128]{1,0:T(8,128)(2,1)S(1)}, u32[]{:S(2)}, u32[]{:S(2)}) collective-permute-start(bf16[256,128]{1,0:T(8,128)(2,1)S(1)} %get-tuple-element.73), channel_id=1, source_target_pairs={{8,0},{12,4},{2,10},{6,14},{9,1},{13,5},{3,11},{7,15},{24,16},{28,... | collective-permute-start | bytes 196616 | tf_op jit(solution)/shard_map/ppermute | solution.py:525
  77.7 7.7 %collective-permute-start.25 = (bf16[272,128]{1,0:T(8,128)(2,1)S(1)}, bf16[272,128]{1,0:T(8,128)(2,1)S(1)}, u32[]{:S(2)}, u32[]{:S(2)}) collective-permute-start(bf16[272,128]{1,0:T(8,128)(2,1)S(1)} %get-tuple-element.81), channel_id=1, source_target_pairs={{0,4},{4,0},{8,12},{12,8},{1,5},{5,1},{9,13},{13,9},{2,6},{6,2},{1... | collective-permute-start | bytes 208904 | tf_op jit(solution)/shard_map/ppermute | solution.py:531
  78.1 5.3 %collective-permute-start.23 = (bf16[144,128]{1,0:T(8,128)(2,1)S(1)}, bf16[144,128]{1,0:T(8,128)(2,1)S(1)}, u32[]{:S(2)}, u32[]{:S(2)}) collective-permute-start(bf16[144,128]{1,0:T(8,128)(2,1)S(1)} %get-tuple-element.79), channel_id=1, source_target_pairs={{0,8},{4,12},{8,0},{12,4},{1,9},{5,13},{9,1},{13,5},{2,10},{6,14},... | collective-permute-start | bytes 110600 | tf_op jit(solution)/shard_map/ppermute | solution.py:531
  79.6 5.8 %collective-permute-start.24 = (bf16[144,128]{1,0:T(8,128)(2,1)S(1)}, bf16[144,128]{1,0:T(8,128)(2,1)S(1)}, u32[]{:S(2)}, u32[]{:S(2)}) collective-permute-start(bf16[144,128]{1,0:T(8,128)(2,1)S(1)} %get-tuple-element.80), channel_id=1, source_target_pairs={{0,12},{4,8},{8,4},{12,0},{1,13},{5,9},{9,5},{13,1},{2,14},{6,10},... | collective-permute-start | bytes 110600 | tf_op jit(solution)/shard_map/ppermute | solution.py:531
  (8 other events, 42.7 us)

commit v13 on v5

--- a/solution.py
+++ b/solution.py
@@ -19,9 +19,12 @@
 VMEM_LIMIT = 32 * 1024 * 1024
 
 
-def params(*semantics):
-    return pltpu.CompilerParams(
-        dimension_semantics=semantics or None, vmem_limit_bytes=VMEM_LIMIT
+def call(body, **options):
+    return pl.pallas_call(
+        body,
+        compiler_params=pltpu.CompilerParams(vmem_limit_bytes=VMEM_LIMIT),
+        cost_estimate=pl.CostEstimate(flops=1, bytes_accessed=1, transcendentals=0),
+        **options,
     )
 
 
@@ -43,15 +46,12 @@
     return jnp.broadcast_to(values[:, n : n + 1], (values.shape[0], LANES))
 
 
-def store_edges(x, span, news, even, refs):
-    even_refs, odd_refs = refs
-    width = even_refs[0].shape[1]
-    part, x = x // width, x % width
+def store_edges(x, span, news, even, even_ref, odd_ref):
     for j in range(RADIUS):
         low = news[j].astype(BF16)
         high = news[len(news) - RADIUS + j].astype(BF16)
-        even_refs[part][j, x, span] = jnp.where(even, high, low)
-        odd_refs[part][j, x, span] = jnp.where(even, low, high)
+        even_ref[j, x, span] = jnp.where(even, high, low)
+        odd_ref[j, x, span] = jnp.where(even, low, high)
 
 
 def store_beside(span, rows, core, u_ref, edge_ref):
@@ -86,7 +86,7 @@
     lax.fori_loop(0, along // TILE, one, 0)
 
 
-def first_body(chunk, p_ref, s_ref, u_ref, even_ref, odd_ref, edge_ref, square, turned_s):
+def first_body(chunk, p_ref, s_ref, u_ref, odd_ref, even_ref, edge_ref, square, turned_s):
     depth, across, padded, _ = u_ref.shape
     along = padded - 2 * EDGE
     core = lax.axis_index("sub")
@@ -105,7 +105,7 @@
                 new = lane(source, z * across + x) * p
                 u_ref[z, x, rows] = new
                 news.append(new)
-            store_edges(x, span, news, even, ([even_ref], [odd_ref]))
+            store_edges(x, span, news, even, even_ref, odd_ref)
         store_beside(span, rows, core, u_ref, edge_ref)
 
     tiles(along, tile)
@@ -117,7 +117,7 @@
 
 def first_field(probes, chunk, source):
     depth, across, along, _ = probes.shape
-    return pl.pallas_call(
+    return call(
         functools.partial(first_body, chunk),
         in_specs=whole_vmem(2),
         out_specs=whole_vmem(4),
@@ -128,7 +128,6 @@
             shape_of(depth, RADIUS, along, BF16),
         ],
         scratch_shapes=square_scratch(),
-        compiler_params=params(),
     )(probes, source)
 
 
@@ -183,23 +182,22 @@
     operands = [u, beside, probes, courant, source]
     if previous is not None:
         operands.append(previous)
-    return pl.pallas_call(
+    return call(
         functools.partial(local_body, chunk, moment, previous is not None),
         in_specs=whole_vmem(len(operands)),
         out_specs=whole_vmem(1)[0],
         out_shape=shape_of(depth, across, along, F32),
         scratch_shapes=square_scratch() + square_scratch()[:1],
-        compiler_params=params(),
     )(*operands)
 
 
-def rim_body(first, kind, parts, *refs):
-    base_ref, even_ref, odd_ref, c_ref = refs[:4]
+def rim_body(kind, *refs):
+    base_ref, odd_ref, even_ref, c_ref = refs[:4]
     outs, (square, turned_c) = refs[4:-2], refs[-2:]
-    depth, all_across, along, _ = base_ref.shape
-    across = even_ref.shape[1]
+    depth, across, along, _ = base_ref.shape
     core = lax.axis_index("sub")
     even = slab_is_even()
+    lower = lax.axis_index("probe") == 0
     turned_c[...] = turned(c_ref[...], square)
     if kind == "middle":
         clear_pads(outs[0])
@@ -209,7 +207,6 @@
         rows = pl.ds(start + EDGE, TILE)
         courant = turned_c[span]
         for x in range(across):
-            place = first + x
             below, above = [], []
             for j in range(RADIUS):
                 one, two = even_ref[j, x, span], odd_ref[j, x, span]
@@ -225,85 +222,401 @@
                     if z + r >= depth:
                         term = COEFFICIENTS[r] * above[z + r - depth]
                         added = term if added is None else added + term
-                new = base_ref[z, place, span]
+                new = base_ref[z, x, span]
                 if added is not None:
-                    new = new + lane(courant, z * all_across + place) * added
+                    new = new + lane(courant, z * across + x) * added
                 news.append(new)
             if kind == "middle":
                 for z, new in enumerate(news):
-                    outs[0][z, place, rows] = new
-                edges = (outs[1 : 1 + parts], outs[1 + parts : 1 + 2 * parts])
-                store_edges(place, span, news, even, edges)
+                    outs[0][z, x, rows] = new
+                store_edges(x, span, news, even, outs[2], outs[1])
             elif kind == "half":
-                keep_ref, send_ref = outs
-                lower = lax.axis_index("probe") == 0
                 for z in range(depth // 2):
                     one, two = news[z].astype(BF16), news[z + depth // 2].astype(BF16)
-                    keep_ref[z, x, span] = jnp.where(lower, one, two)
-                    send_ref[z, x, span] = jnp.where(lower, two, one)
+                    outs[0][z, x, span] = jnp.where(lower, one, two)
+                    outs[1][z, x, span] = jnp.where(lower, two, one)
             else:
                 for z, new in enumerate(news):
                     outs[0][z, x, span] = new.astype(BF16)
         if kind == "middle":
-            store_beside(span, rows, core, outs[0], outs[-1])
+            store_beside(span, rows, core, outs[0], outs[3])
 
     tiles(along, tile)
 
 
-def rim_step(base, evens, odds, courant, kind, first=0, parts=1):
-    depth, all_across, along, _ = base.shape
-    across = evens.shape[1]
+def rim_step(base, odds, evens, courant, kind):
+    depth, across, along, _ = base.shape
     if kind == "middle":
-        edge = [shape_of(RADIUS, across // parts, along, BF16)] * parts
-        out_shape = [shape_of(depth, across, along + 2 * EDGE, F32)]
-        out_shape += edge + edge + [shape_of(depth, RADIUS, along, BF16)]
+        out_shape = [
+            shape_of(depth, across, along + 2 * EDGE, F32),
+            shape_of(RADIUS, across, along, BF16),
+            shape_of(RADIUS, across, along, BF16),
+            shape_of(depth, RADIUS, along, BF16),
+        ]
     elif kind == "half":
         out_shape = [shape_of(depth // 2, across, along, BF16)] * 2
     else:
         out_shape = [shape_of(depth, across, along, BF16)]
-    return pl.pallas_call(
-        functools.partial(rim_body, first, kind, parts),
+    return call(
+        functools.partial(rim_body, kind),
         in_specs=whole_vmem(4),
         out_specs=whole_vmem(len(out_shape)),
         out_shape=out_shape,
         scratch_shapes=square_scratch(),
-        compiler_params=params(),
-    )(base, evens, odds, courant)
+    )(base, odds, evens, courant)
 
 
 def swap(x, axis, pairs):
     return lax.ppermute(x, axis, [p for a, b in pairs for p in ((a, b), (b, a))])
 
 
-def exchange(evens, odds, edge):
-    slabs = lax.axis_size("slab")
-    pairs = []
-    for one, two in zip(evens, odds):
-        pairs.append(
-            (
-                swap(one, "slab", [(i, i + 1) for i in range(0, slabs - 1, 2)]),
-                swap(two, "slab", [(i, i + 1) for i in range(1, slabs - 1, 2)]),
-            )
-        )
-    return pairs, swap(edge, "sub", [(0, 1)])
-
-
-def gram_body(parts, pieces, *refs):
-    ins, (keep_ref, send_ref), panel = refs[: 2 * len(pieces)], refs[-3:-1], refs[-1]
-    half = parts // 2
+def even_swap(x):
+    return swap(x, "slab", [(i, i + 1) for i in range(0, lax.axis_size("slab") - 1, 2)])
+
+
+def odd_swap(x):
+    return swap(x, "slab", [(i, i + 1) for i in range(1, lax.axis_size("slab") - 1, 2)])
+
+
+def core_swap(x):
+    return swap(x, "sub", [(0, 1)])
+
+
+def chip_swap(x):
+    return swap(x, "probe", [(0, 1)])
+
+
+def half_rows(square, field, half, chip):
+    square[...] = turned(field, square)
+    rows = square[pl.ds(pl.multiple_of(chip * half, 8), half)]
+    return jnp.concatenate([rows, rows], axis=0)
+
+
+def own_half(window, half, chip):
+    return jnp.where(chip == 0, window[:half], window[window.shape[0] - half :])
+
+
+def prepare_body(p_ref, s_ref, window_ref, odd_ref, even_ref, square):
+    depth, across, rows, _ = window_ref.shape
+    half = rows - EDGE
+    along = 2 * half
+    chip = lax.axis_index("probe")
+    even = slab_is_even()
+    lanes = slice(LANES, 2 * LANES)
+    skip = along - rows
+
+    def plane(z, _):
+        start = pl.multiple_of((1 - chip) * skip, TILE)
+        window_ref[z] = p_ref[z, :, pl.ds(start, rows), lanes]
+        return 0
+
+    lax.fori_loop(0, depth, plane, 0)
+    source = half_rows(square, s_ref[0], half, chip)[:half]
+    start = pl.multiple_of(chip * skip, TILE)
+
+    def value(z, x):
+        window = p_ref[z, x, pl.ds(start, rows), lanes].astype(F32)
+        return lane(source, z * across + x) * own_half(window, half, chip)
+
+    for j in range(RADIUS):
+        for i in range(across // 2):
+            low, high = [
+                jnp.concatenate([value(z, 2 * i), value(z, 2 * i + 1)], axis=0).astype(BF16)
+                for z in (j, depth - RADIUS + j)
+            ]
+            even_ref[j, i] = jnp.where(even, high, low)
+            odd_ref[j, i] = jnp.where(even, low, high)
+
+
+def prepare(probes, source):
+    depth, across, along, _ = probes.shape
+    edge = shape_of(RADIUS, across // 2, along, BF16)
+    return call(
+        prepare_body,
+        in_specs=whole_vmem(2),
+        out_specs=whole_vmem(3),
+        out_shape=[shape_of(depth, across, along // 2 + EDGE, BF16), edge, edge],
+        scratch_shapes=square_scratch()[:1],
+    )(probes, source)
+
+
+def store_sides(core, chip, u_ref, edge_ref, rows_ref):
+    depth, across, padded, _ = u_ref.shape
+    segment = padded // 2
+    half = segment - 2 * EDGE
+    first = (across - RADIUS) * (1 - core)
+    near = pl.multiple_of(jnp.where(chip == 0, half, EDGE), 8)
+
+    def plane(z, _):
+        for j in range(RADIUS):
+            parts = [
+                u_ref[z, first + j, g * segment + EDGE : g * segment + EDGE + half]
+                for g in range(2)
+            ]
+            edge_ref[z, j] = jnp.concatenate(parts, axis=0).astype(BF16)
+        if rows_ref is not None:
+            for x in range(across):
+                parts = [u_ref[z, x, pl.ds(near + g * segment, EDGE)] for g in range(2)]
+                rows_ref[z, x] = jnp.concatenate(parts, axis=0).astype(BF16)
+        return 0
+
+    lax.fori_loop(0, depth, plane, 0)
+
+
+def shared_first_body(
+    p_ref, got_ref, s_ref, u_ref, odd_ref, even_ref, edge_ref, both_ref, square
+):
+    depth, across, rows, _ = got_ref.shape
+    half = rows - EDGE
+    segment = half + 2 * EDGE
+    along = 2 * half
     chip = lax.axis_index("probe")
     core = lax.axis_index("sub")
-    depth, _, along, _ = ins[0].shape
-    across = panel.shape[0] // (depth * along)
-    for (chunk, first), keep, got in zip(pieces, ins[0::2], ins[1::2]):
-        mine = pl.multiple_of((chip * half + chunk) * LANES, LANES)
-        other = pl.multiple_of(((1 - chip) * half + chunk) * LANES, LANES)
-        width = keep.shape[1]
+    even = slab_is_even()
+    lanes = slice(LANES, 2 * LANES)
+    square[...] = turned(s_ref[0], square)
+    start = pl.multiple_of(chip * (along - rows), TILE)
+    source = square[pl.ds(start, rows)]
+    blank = jnp.zeros((EDGE, LANES), F32)
+    for i in range(across // 2):
+        theirs = []
         for z in range(depth):
-            rows = pl.ds((z * across + first) * along, width * along)
-            panel[rows, pl.ds(mine, LANES)] = keep[z].reshape(width * along, LANES)
-            panel[rows, pl.ds(other, LANES)] = got[z].reshape(width * along, LANES)
-    size = parts * LANES
+            pair = []
+            for x in (2 * i, 2 * i + 1):
+                mine = p_ref[z, x, pl.ds(start, rows), lanes].astype(F32)
+                got = got_ref[z, x].astype(F32)
+                scale = lane(source, z * across + x)
+                windows = [jnp.where(chip == 0, mine, got), jnp.where(chip == 0, got, mine)]
+                for g, window in enumerate(windows):
+                    at = pl.multiple_of(g * segment + EDGE * (1 - chip), 8)
+                    u_ref[z, x, pl.ds(at, rows)] = scale * window
+                    out = pl.multiple_of(g * segment + chip * (half + EDGE), 8)
+                    u_ref[z, x, pl.ds(out, EDGE)] = blank
+                both = [own_half(window, half, chip) for window in windows]
+                both_ref[z, x] = jnp.concatenate(both, axis=0).astype(BF16)
+                pair.append(own_half(scale * got, half, chip))
+            theirs.append(jnp.concatenate(pair, axis=0))
+        store_edges(i, pl.ds(0, along), theirs, even, even_ref, odd_ref)
+    store_sides(core, chip, u_ref, edge_ref, None)
+
+
+def shared_first(probes, got, source):
+    depth, across, along, _ = probes.shape
+    edge = shape_of(RADIUS, across // 2, along, BF16)
+    return call(
+        shared_first_body,
+        in_specs=whole_vmem(3),
+        out_specs=whole_vmem(5),
+        out_shape=[
+            shape_of(depth, across, along + 4 * EDGE, F32),
+            edge,
+            edge,
+            shape_of(depth, RADIUS, along, BF16),
+            shape_of(depth, across, along, BF16),
+        ],
+        scratch_shapes=square_scratch()[:1],
+    )(probes, got, source)
+
+
+def fill_rows(u_ref, rows_ref, chip):
+    depth, across, padded, _ = u_ref.shape
+    segment = padded // 2
+
+    def plane(z, _):
+        for x in range(across):
+            got = rows_ref[z, x].astype(F32)
+            for g in range(2):
+                part = got[g * EDGE : (g + 1) * EDGE]
+                blank = jnp.zeros_like(part)
+                before, after = g * segment, (g + 1) * segment - EDGE
+                u_ref[z, x, before : before + EDGE] = jnp.where(chip == 0, blank, part)
+                u_ref[z, x, after : after + EDGE] = jnp.where(chip == 0, part, blank)
+        return 0
+
+    lax.fori_loop(0, depth, plane, 0)
+
+
+def shared_local_body(moment, has_rows, has_previous, *refs):
+    refs = list(refs)
+    u_ref, beside_ref, p_ref, c_ref, s_ref = refs[:5]
+    rest = refs[5:]
+    rows_ref = rest.pop(0) if has_rows else None
+    prev_ref = rest.pop(0) if has_previous else None
+    base_ref = rest.pop(0)
+    if has_rows:
+        u_ref = rest.pop(0)
+    square, turned_c, turned_s = rest
+    depth, across, along, _ = base_ref.shape
+    half = along // 2
+    core = lax.axis_index("sub")
+    chip = lax.axis_index("probe")
+    left_on = (core == 1).astype(F32)
+    right_on = (core == 0).astype(F32)
+    turned_c[:along] = half_rows(square, c_ref[...], half, chip)
+    turned_s[:along] = half_rows(square, s_ref[moment], half, chip)
+    if has_rows:
+        fill_rows(u_ref, rows_ref, chip)
+
+    def tile(start):
+        span = pl.ds(start, TILE)
+        courant = turned_c[span]
+        source = turned_s[span]
+        firsts = []
+        for k in range(TILE // 8):
+            row = start + 8 * k
+            firsts.append(pl.multiple_of(row + EDGE + jnp.where(row >= half, 2 * EDGE, 0), 8))
+
+        def load(ref, z, x, shift=0):
+            parts = [ref[z, x, pl.ds(first + shift, 8)] for first in firsts]
+            return jnp.concatenate(parts, axis=0)
+
+        for z in range(depth):
+            beside = [beside_ref[z, j, span].astype(F32) for j in range(RADIUS)]
+            row = [v * left_on for v in beside]
+            row += [load(u_ref, z, x) for x in range(across)]
+            row += [v * right_on for v in beside]
+            for x in range(across):
+                here = row[RADIUS + x]
+                total = (3.0 * COEFFICIENTS[0]) * here
+                for r in range(1, RADIUS + 1):
+                    near = row[RADIUS + x + r] + row[RADIUS + x - r]
+                    near = near + (load(u_ref, z, x, r) + load(u_ref, z, x, -r))
+                    if z + r < depth:
+                        near = near + load(u_ref, z + r, x)
+                    if z - r >= 0:
+                        near = near + load(u_ref, z - r, x)
+                    total = total + COEFFICIENTS[r] * near
+                cell = z * across + x
+                new = 2.0 * here
+                if has_previous:
+                    new = new - load(prev_ref, z, x)
+                p = p_ref[z, x, span].astype(F32)
+                base_ref[z, x, span] = new + lane(courant, cell) * total + lane(source, cell) * p
+
+    tiles(along, tile)
+
+
+def shared_local(u, beside, both, courant, source, moment, rows, previous):
+    depth, across, along, _ = both.shape
+    operands = [u, beside, both, courant, source]
+    operands += [a for a in (rows, previous) if a is not None]
+    out_shape = [shape_of(depth, across, along, F32)]
+    aliases = {}
+    if rows is not None:
+        aliases = {0: 1}
+        out_shape.append(jax.ShapeDtypeStruct(u.shape, F32))
+    out = call(
+        functools.partial(shared_local_body, moment, rows is not None, previous is not None),
+        in_specs=whole_vmem(len(operands)),
+        out_specs=whole_vmem(len(out_shape)),
+        out_shape=out_shape,
+        input_output_aliases=aliases,
+        scratch_shapes=square_scratch() + square_scratch()[:1],
+    )(*operands)
+    return out[0], (u if rows is None else out[1])
+
+
+def planes_of(refs, x, half, chip):
+    if len(refs) == 1:
+        return [refs[0][j, x].astype(F32) for j in range(RADIUS)]
+    planes = []
+    for j in range(RADIUS):
+        at = (x % 2) * half
+        own, other = [ref[j, x // 2].astype(F32)[at : at + half] for ref in refs]
+        parts = [jnp.where(chip == 0, own, other), jnp.where(chip == 0, other, own)]
+        planes.append(jnp.concatenate(parts, axis=0))
+    return planes
+
+
+def wide_rim_body(kind, count, *refs):
+    base_ref, c_ref = refs[:2]
+    odd_refs, even_refs = refs[2 : 2 + count], refs[2 + count : 2 + 2 * count]
+    outs, square = refs[2 + 2 * count : -1], refs[-1]
+    depth, across, along, _ = base_ref.shape
+    half = along // 2
+    segment = half + 2 * EDGE
+    core = lax.axis_index("sub")
+    chip = lax.axis_index("probe")
+    even = slab_is_even()
+    if kind == "own":
+        courant = turned(c_ref[...], square)[:along]
+    else:
+        courant = half_rows(square, c_ref[...], half, chip)
+
+    def values(x):
+        ones, twos = planes_of(even_refs, x, half, chip), planes_of(odd_refs, x, half, chip)
+        below = [jnp.where(even, two, one) for one, two in zip(ones, twos)]
+        above = [jnp.where(even, one, two) for one, two in zip(ones, twos)]
+        news = []
+        for z in range(depth):
+            added = None
+            for r in range(1, RADIUS + 1):
+                if z - r < 0:
+                    term = COEFFICIENTS[r] * below[RADIUS + z - r]
+                    added = term if added is None else added + term
+                if z + r >= depth:
+                    term = COEFFICIENTS[r] * above[z + r - depth]
+                    added = term if added is None else added + term
+            new = base_ref[z, x]
+            if added is not None:
+                new = new + lane(courant, z * across + x) * added
+            news.append(new)
+        return news
+
+    if kind == "middle":
+        u_ref, odd_ref, even_ref, edge_ref, rows_ref = outs
+        for x in range(across):
+            news = values(x)
+            for z, new in enumerate(news):
+                for g in range(2):
+                    at = g * segment + EDGE
+                    u_ref[z, x, at : at + half] = new[g * half : (g + 1) * half]
+            store_edges(x, pl.ds(0, along), news, even, even_ref, odd_ref)
+        store_sides(core, chip, u_ref, edge_ref, rows_ref)
+        return
+    for i in range(across // 2):
+        for z, (one, two) in enumerate(zip(values(2 * i), values(2 * i + 1))):
+            first = jnp.concatenate([one[:half], two[:half]], axis=0).astype(BF16)
+            second = jnp.concatenate([one[half:], two[half:]], axis=0).astype(BF16)
+            if kind == "own":
+                first, second = (
+                    jnp.where(chip == 0, first, second),
+                    jnp.where(chip == 0, second, first),
+                )
+            outs[0][z, i] = first
+            outs[1][z, i] = second
+
+
+def wide_rim(base, courant, odds, evens, kind):
+    depth, across, along, _ = base.shape
+    if kind == "middle":
+        edge = shape_of(RADIUS, across, along, BF16)
+        out_shape = [
+            shape_of(depth, across, along + 4 * EDGE, F32),
+            edge,
+            edge,
+            shape_of(depth, RADIUS, along, BF16),
+            shape_of(depth, across, 2 * EDGE, BF16),
+        ]
+    else:
+        out_shape = [shape_of(depth, across // 2, along, BF16)] * 2
+    return call(
+        functools.partial(wide_rim_body, kind, len(odds)),
+        in_specs=whole_vmem(2 + 2 * len(odds)),
+        out_specs=whole_vmem(len(out_shape)),
+        out_shape=out_shape,
+        scratch_shapes=square_scratch()[:1],
+    )(base, courant, *odds, *evens)
+
+
+def gram_body(kept_ref, got_ref, one_ref, two_ref, keep_ref, send_ref, panel):
+    chip = lax.axis_index("probe")
+    core = lax.axis_index("sub")
+    cells, size = panel.shape
+    places = (2 * chip, 2 * (1 - chip), 1, 3)
+    for place, ref in zip(places, (kept_ref, got_ref, one_ref, two_ref)):
+        at = place * LANES if isinstance(place, int) else pl.multiple_of(place * LANES, LANES)
+        panel[:, pl.ds(at, LANES)] = ref[...].reshape(cells, LANES)
     everything = panel[...]
 
     def columns(which):
@@ -316,22 +629,19 @@
             preferred_element_type=F32,
         )
 
+    keep_ref[:size] = columns(core)
+    send_ref[:size] = columns(1 - core)
     rows = lax.broadcasted_iota(jnp.int32, (LANES, LANES), 0)
     cols = lax.broadcasted_iota(jnp.int32, (LANES, LANES), 1)
     eye = rows == cols
-    keep = columns(core)
-    send = columns(1 - core)
-    keep_ref[:size] = keep
-    send_ref[:size] = send
-
-    def diagonal(which, first):
-        side = which // 2
-        a = keep_ref[which * LANES : (which + 1) * LANES, side * LANES : (side + 1) * LANES]
-        b = send_ref[which * LANES : (which + 1) * LANES, side * LANES : (side + 1) * LANES]
-        block = jnp.where(core == which % 2, a, b)
+
+    def diagonal(which):
+        block = slice(which * LANES, (which + 1) * LANES)
+        lanes = slice(which // 2 * LANES, (which // 2 + 1) * LANES)
+        block = jnp.where(core == which % 2, keep_ref[block, lanes], send_ref[block, lanes])
         return jnp.sum(jnp.where(eye, block, 0.0), axis=0, keepdims=True)
 
-    diag = [diagonal(n, None) for n in range(parts)]
+    diag = [diagonal(n) for n in range(4)]
     row0 = jnp.concatenate(diag[:2], axis=1)
     row1 = jnp.concatenate(diag[2:], axis=1)
     tail = jnp.concatenate([row0, row1, jnp.zeros((6, 2 * LANES), F32)], axis=0)
@@ -339,16 +649,16 @@
     send_ref[size:] = tail
 
 
-def gram(parts, pieces, fields, cells):
-    size = parts * LANES
+def gram(fields):
+    cells = math.prod(fields[0].shape[:3])
+    size = 4 * LANES
     shape = jax.ShapeDtypeStruct((size + 8, 2 * LANES), F32)
-    return pl.pallas_call(
-        functools.partial(gram_body, parts, pieces),
-        in_specs=whole_vmem(len(fields)),
+    return call(
+        gram_body,
+        in_specs=whole_vmem(4),
         out_specs=whole_vmem(2),
         out_shape=[shape, shape],
         scratch_shapes=[pltpu.VMEM((cells, size), BF16)],
-        compiler_params=params(),
     )(*fields)
 
 
@@ -385,12 +695,11 @@
     count = (keep.shape[0] - 8) // slabs
     own = jax.ShapeDtypeStruct((count + 8, keep.shape[1]), F32)
     sent = jax.ShapeDtypeStruct((count + 16, keep.shape[1]), BF16)
-    return pl.pallas_call(
+    return call(
         functools.partial(rows_body, slabs, count),
         in_specs=whole_vmem(2),
         out_specs=whole_vmem(slabs),
         out_shape=[own] + [sent] * (slabs - 1),
-        compiler_params=params(),
     )(keep, got)
 
 
@@ -404,12 +713,11 @@
 
 
 def sum_all(own, others):
-    return pl.pallas_call(
+    return call(
         sum_body,
         in_specs=whole_vmem(1 + len(others)),
         out_specs=whole_vmem(1)[0],
         out_shape=jax.ShapeDtypeStruct(others[0].shape, BF16),
-        compiler_params=params(),
     )(own, *others)
 
 
@@ -440,7 +748,7 @@
 
 def normalise(mine, other, cell_count):
     count = mine.shape[0] - 16
-    return pl.pallas_call(
+    return call(
         functools.partial(normalise_body, cell_count),
         in_specs=whole_vmem(2),
         out_specs=whole_vmem(2),
@@ -448,7 +756,6 @@
             jax.ShapeDtypeStruct((count, 2 * LANES), F32),
             jax.ShapeDtypeStruct((1, LANES), F32),
         ],
-        compiler_params=params(),
     )(mine, other)
 
 
@@ -462,28 +769,25 @@
 
 
 def assemble(near, far):
-    return pl.pallas_call(
+    return call(
         assemble_body,
         in_specs=whole_vmem(2),
         out_specs=whole_vmem(1)[0],
         out_shape=jax.ShapeDtypeStruct((near.shape[0], 4 * LANES), F32),
-        compiler_params=params(),
     )(near, far)
 
 
-def coupled(pieces, fields, cells, cell_count):
+def coupled(fields, cell_count):
     slabs = 4
-    keep, send = gram(4, pieces, fields, cells)
-    got = swap(send, "sub", [(0, 1)])
-    own, *sent = split_rows(keep, got, slabs)
+    keep, send = gram(fields)
+    own, *blocks = split_rows(keep, core_swap(send), slabs)
     arrived = [
-        lax.ppermute(sent[d - 1], "slab", [(i, i ^ d) for i in range(slabs)]) for d in (2, 3, 1)
+        lax.ppermute(blocks[d - 1], "slab", [(i, i ^ d) for i in range(slabs)])
+        for d in (2, 3, 1)
     ]
     mine = sum_all(own, arrived)
-    other = swap(mine, "probe", [(0, 1)])
-    near, norms = normalise(mine, other, cell_count)
-    far = swap(near, "sub", [(0, 1)])
-    return assemble(near, far), norms.reshape(-1)
+    near, norms = normalise(mine, chip_swap(mine), cell_count)
+    return assemble(near, core_swap(near)), norms.reshape(-1)
 
 
 def coupled_general(fields, cell_count):
@@ -513,40 +817,70 @@
     chunks = count // LANES
     slabs, chips = lax.axis_size("slab"), lax.axis_size("probe")
     cell_count = depth * across * along * slabs * lax.axis_size("sub")
-    paired = chips == 2 and slabs == 4 and chunks == 2
+    half = along // 2
+    paired = chips == 2 and slabs == 4 and chunks == 2 and depth == 2 * RADIUS
+    paired = paired and half % 8 == 0 and (half - EDGE) % TILE == 0 and along % TILE == 0
     steps = source.shape[0]
     courant = courant.reshape(depth * across, along)
     source = source.reshape(steps, depth * across, along)
+    exchange = lambda odd, even, edge: (odd_swap(odd), even_swap(even), core_swap(edge))
+    if paired and across % 2 == 0:
+        return shared_shards(probes, courant, source, exchange, cell_count)
 
     now, previous, halos = [], [None] * chunks, []
     for c in range(chunks):
-        u, one, two, edge = first_field(probes, c, source)
+        u, *edges = first_field(probes, c, source[:1])
         now.append(u)
-        halos.append(exchange([one], [two], edge))
-    pieces, fields = [], []
+        halos.append(exchange(*edges))
+    fields = []
     for n in range(1, steps):
         for c in range(chunks):
-            pairs, beside = halos[c]
+            odd, even, beside = halos[c]
             base = local_step(now[c], beside, probes, c, courant, source, n, previous[c])
             if n == steps - 1:
-                width = across // len(pairs)
-                for h, (one, two) in enumerate(pairs):
-                    kind = "half" if paired else "all"
-                    out = rim_step(base, one, two, courant, kind, h * width)
-                    if paired:
-                        pieces.append((c, h * width))
-                        fields += [out[0], swap(out[1], "probe", [(0, 1)])]
-                    else:
-                        fields.append(out[0])
+                fields += rim_step(base, odd, even, courant, "all")
             else:
-                ((one, two),) = pairs
-                out = rim_step(base, one, two, courant, "middle")
-                previous[c], now[c] = now[c], out[0]
-                halos[c] = exchange([out[1]], [out[2]], out[3])
-    if paired:
-        cells = depth // 2 * across * along
-        return coupled(tuple(pieces), fields, cells, cell_count)
+                u, *edges = rim_step(base, odd, even, courant, "middle")
+                previous[c], now[c] = now[c], u
+                halos[c] = exchange(*edges)
     return coupled_general(fields, cell_count)
+
+
+def shared_shards(probes, courant, source, exchange, cell_count):
+    steps = source.shape[0]
+    first_source = source[:1]
+    u, *edges = first_field(probes, 0, first_source)
+    odd, even, beside = exchange(*edges)
+    window, one, two = prepare(probes, first_source)
+    got = chip_swap(window)
+    odds, evens = [odd_swap(one)], [even_swap(two)]
+    shared_u, one, two, edge, both = shared_first(probes, got, first_source)
+    odds.append(odd_swap(one))
+    evens.append(even_swap(two))
+    shared_beside, rows = core_swap(edge), None
+
+    previous = shared_previous = None
+    for n in range(1, steps):
+        last = n == steps - 1
+        base = local_step(u, beside, probes, 0, courant, source, n, previous)
+        if last:
+            kept, sent = wide_rim(base, courant, [odd], [even], "own")
+            fields = [kept, chip_swap(sent)]
+        else:
+            previous = u
+            u, *edges = rim_step(base, odd, even, courant, "middle")
+            odd, even, beside = exchange(*edges)
+        base, shared_u = shared_local(
+            shared_u, shared_beside, both, courant, source, n, rows, shared_previous
+        )
+        if last:
+            fields += wide_rim(base, courant, odds, evens, "both")
+        else:
+            shared_previous = shared_u
+            shared_u, one, two, edge, rows = wide_rim(base, courant, odds, evens, "middle")
+            odds, evens = [odd_swap(one)], [even_swap(two)]
+            shared_beside, rows = core_swap(edge), chip_swap(rows)
+    return coupled(fields, cell_count)
 
 
 def solution(mesh):

time: 94.4 us -> 111 us (1.18)
  waiting for transfers between devices: 25.8 us -> 43.3 us
    ppermute x23 -> x27, waiting for transfers between devices: 20.1 us -> 37.4 us  [swap(): lax.ppermute(x, axis, [p for a, b in pairs for p in ((a, b), (b, a))])]
    ppermute x3, starting transfers between devices: 5.72 us -> 3.85 us  [coupled(): lax.ppermute(blocks[d - 1], 'slab', [(i, i ^ d) for i in range(slabs)])]
    unnamed x10 -> x8, local copies, waits for them, and re-layouts: 2.32 us -> 1.42 us
    ppermute x23 -> x27, starting transfers between devices: 34.9 us -> 35.7 us  [swap(): lax.ppermute(x, axis, [p for a, b in pairs for p in ((a, b), (b, a))])]
    pallas_call x19 -> x20, Pallas kernels: 24.4 us -> 24.3 us  [the longest x3 7.48 us: shared_local(): call(functools.partial(shared_local_body, moment, rows is not None, previ...]
  transfers between devices with their start and end apart: 26 -> 30, of which waited for: 10 -> 10; matrix products, arithmetic and copies ran while one was open for 0% -> 0% of each run, Pallas kernels for 22% -> 19%
where the time goes in v13:
time: 111 us; the launch traced here: 110 us
  waiting for transfers between devices  43.3 us (39%)
  starting transfers between devices  39.6 us (36%)
  Pallas kernels  24.3 us (22%)
  local copies, waits for them, and re-layouts  2.19 us (2%)
    ppermute x27, waiting for transfers between devices, swap(): lax.ppermute(x, axis, [p for a, b in pairs for p in ((a, b), (b, a))])  37.4 us
    ppermute x27, starting transfers between devices, swap(): lax.ppermute(x, axis, [p for a, b in pairs for p in ((a, b), (b, a))])  35.7 us
    pallas_call x3, Pallas kernels, shared_local(): call(functools.partial(shared_local_body, moment, rows is not None, previ...  7.48 us
    pallas_call x3, Pallas kernels, local_step(): call(functools.partial(local_body, chunk, moment, previous is not None),...  6.64 us
    ppermute x3, waiting for transfers between devices, coupled(): lax.ppermute(blocks[d - 1], 'slab', [(i, i ^ d) for i in range(slabs)])  5.9 us
    ppermute x3, starting transfers between devices, coupled(): lax.ppermute(blocks[d - 1], 'slab', [(i, i ^ d) for i in range(slabs)])  3.85 us
    pallas_call x4, Pallas kernels, wide_rim(): call(functools.partial(wide_rim_body, kind, len(odds)), in_specs=whole_vm...  2.92 us
  transfers between devices with their start and end apart: 30, of which 10 were waited for; matrix products, arithmetic and copies ran while one was open for 0% of the time, Pallas kernels for 19%

profile of v13, /device:TPU:0, one launch (start us, length us, event | category | flops | bytes accessed | tf_op | source)
XLA Modules:
  0.0 110.5 jit_solution(18257480744398547233)
XLA Ops:
  3.4 3.0 %collective-permute-start.10 = (bf16[8,8,32,128]{3,2,1,0:T(8,128)(2,1)S(1)}, bf16[8,8,32,128]{3,2,1,0:T(8,128)(2,1)S(1)}, u32[]{:S(2)}, u32[]{:S(2)}) collective-permute-start(bf16[8,8,32,128]{3,2,1,0:T(8,128)(2,1)S(1)} %get-tuple-element.61), channel_id=1, source_target_pairs={{0,2},{2,0},{1,3},{3,1},{4,6},{6,4},{5,7},{7,5},{8,10},{10,8},{9,1... | collective-permute-start | bytes 1572872 | tf_op jit(solution)/shard_map/ppermute | solution.py:270
  8.3 4.4 %collective-permute-start.2 = (bf16[4,8,48,128]{3,2,1,0:T(8,128)(2,1)S(1)}, bf16[4,8,48,128]{3,2,1,0:T(8,128)(2,1)S(1)}, u32[]{:S(2)}, u32[]{:S(2)}) collective-permute-start(bf16[4,8,48,128]{3,2,1,0:T(8,128)(2,1)S(1)} %get-tuple-element.50), channel_id=1, source_target_pairs={{0,4},{4,0},{8,12},{12,8},{1,5},{5,1},{9,13},{13,9},{2,6},{6,2},{1... | collective-permute-start | bytes 1179656 | tf_op jit(solution)/shard_map/ppermute | solution.py:270
  12.7 2.1 %shard_map.51.refs_0_ = f32[8,8,48,128]{3,2,1,0:T(8,128)S(1)} custom-call(f32[8,8,64,128]{3,2,1,0:T(8,128)S(1)} %get-tuple-element.47.refs_0_.refs_5_, bf16[8,4,48,128]{3,2,1,0:T(8,128)(2,1)S(1)} %collective-permute-done.refs_1_, bf16[8,8,48,256]{3,2,1,0:T(8,128)(2,1)S(1)} %copy-done, f32[64,48]{1,0:T(8,128)S(1)} %bitcast.11, f32[4,64,48]{2,1,0:T(8,128)S(1)} %bitcast.5), custom_call_target="tpu_custom_call" | custom-call | flops 1 | bytes 1 | tf_op jit(solution)/shard_map/pallas_call | solution.py:185
  14.9 7.3 %collective-permute-done.2.refs_2_ = bf16[4,8,48,128]{3,2,1,0:T(8,128)(2,1)S(1)} collective-permute-done((bf16[4,8,48,128]{3,2,1,0:T(8,128)(2,1)S(1)}, bf16[4,8,48,128]{3,2,1,0:T(8,128)(2,1)S(1)}, u32[]{:S(2)}, u32[]{:S(2)}) %collective-permute-start.2) | collective-permute-done | bytes 393248 | tf_op jit(solution)/shard_map/ppermute | solution.py:270
  24.1 3.5 %collective-permute-start.5 = (bf16[4,8,48,128]{3,2,1,0:T(8,128)(2,1)S(1)}, bf16[4,8,48,128]{3,2,1,0:T(8,128)(2,1)S(1)}, u32[]{:S(2)}, u32[]{:S(2)}) collective-permute-start(bf16[4,8,48,128]{3,2,1,0:T(8,128)(2,1)S(1)} %get-tuple-element.54), channel_id=1, source_target_pairs={{0,4},{4,0},{8,12},{12,8},{1,5},{5,1},{9,13},{13,9},{2,6},{6,2},{1... | collective-permute-start | bytes 1179656 | tf_op jit(solution)/shard_map/ppermute | solution.py:270
  29.1 3.1 %collective-permute-start.14 = (bf16[4,4,48,128]{3,2,1,0:T(8,128)(2,1)S(1)}, bf16[4,4,48,128]{3,2,1,0:T(8,128)(2,1)S(1)}, u32[]{:S(2)}, u32[]{:S(2)}) collective-permute-start(bf16[4,4,48,128]{3,2,1,0:T(8,128)(2,1)S(1)} %get-tuple-element.67), channel_id=1, source_target_pairs={{0,4},{4,0},{8,12},{12,8},{1,5},{5,1},{9,13},{13,9},{2,6},{6,2},{1... | collective-permute-start | bytes 589832 | tf_op jit(solution)/shard_map/ppermute | solution.py:270
  32.9 4.6 %collective-permute-done.5.refs_2_ = bf16[4,8,48,128]{3,2,1,0:T(8,128)(2,1)S(1)} collective-permute-done((bf16[4,8,48,128]{3,2,1,0:T(8,128)(2,1)S(1)}, bf16[4,8,48,128]{3,2,1,0:T(8,128)(2,1)S(1)}, u32[]{:S(2)}, u32[]{:S(2)}) %collective-permute-start.5) | collective-permute-done | bytes 393248 | tf_op jit(solution)/shard_map/ppermute | solution.py:270
  37.5 3.9 %collective-permute-start.15 = (bf16[4,4,48,128]{3,2,1,0:T(8,128)(2,1)S(1)}, bf16[4,4,48,128]{3,2,1,0:T(8,128)(2,1)S(1)}, u32[]{:S(2)}, u32[]{:S(2)}) collective-permute-start(bf16[4,4,48,128]{3,2,1,0:T(8,128)(2,1)S(1)} %get-tuple-element.68), channel_id=1, source_target_pairs={{0,4},{4,0},{8,12},{12,8},{1,5},{5,1},{9,13},{13,9},{2,6},{6,2},{1... | collective-permute-start | bytes 589832 | tf_op jit(solution)/shard_map/ppermute | solution.py:270
  41.4 2.2 %shard_map.53.refs_0_ = f32[8,8,48,128]{3,2,1,0:T(8,128)S(1)} custom-call(f32[8,8,64,128]{3,2,1,0:T(8,128)S(1)} %get-tuple-element.51.refs_0_.refs_5_, bf16[8,4,48,128]{3,2,1,0:T(8,128)(2,1)S(1)} %collective-permute-done.3.refs_1_, bf16[8,8,48,256]{3,2,1,0:T(8,128)(2,1)S(1)} %copy-done.1, f32[64,48]{1,0:T(8,128)S(1)} %bitcast.13, f32[4,64,48]{2,1,0:T(8,128)S(1)} %bitcast.6, ...), custom_call_target="tpu_custom_call" | custom-call | flops 1 | bytes 1 | tf_op jit(solution)/shard_map/pallas_call | solution.py:185
  44.8 2.3 %shard_map.59.refs_0_ = f32[8,8,48,128]{3,2,1,0:T(8,128)S(1)} custom-call(f32[8,8,80,128]{3,2,1,0:T(8,128)S(1)} %get-tuple-element.62.refs_0_.refs_6_, bf16[8,4,48,128]{3,2,1,0:T(8,128)(2,1)S(1)} %collective-permute-done.11.refs_1_, bf16[8,8,48,128]{3,2,1,0:T(8,128)(2,1)S(1)} %get-tuple-element.64.refs_2_, f32[64,48]{1,0:T(8,128)S(1)} %bitcast.15, ...), custom_call_target="tpu_custom_call" | custom-call | flops 1 | bytes 1 | tf_op jit(solution)/shard_map/pallas_call | solution.py:508
  49.5 2.9 %collective-permute-start.19 = (bf16[4,8,48,128]{3,2,1,0:T(8,128)(2,1)S(1)}, bf16[4,8,48,128]{3,2,1,0:T(8,128)(2,1)S(1)}, u32[]{:S(2)}, u32[]{:S(2)}) collective-permute-start(bf16[4,8,48,128]{3,2,1,0:T(8,128)(2,1)S(1)} %get-tuple-element.74), channel_id=1, source_target_pairs={{0,4},{4,0},{8,12},{12,8},{1,5},{5,1},{9,13},{13,9},{2,6},{6,2},{1... | collective-permute-start | bytes 1179656 | tf_op jit(solution)/shard_map/ppermute | solution.py:270
  52.4 4.4 %collective-permute-done.17.refs_5_ = bf16[8,8,16,128]{3,2,1,0:T(8,128)(2,1)S(1)} collective-permute-done((bf16[8,8,16,128]{3,2,1,0:T(8,128)(2,1)S(1)}, bf16[8,8,16,128]{3,2,1,0:T(8,128)(2,1)S(1)}, u32[]{:S(2)}, u32[]{:S(2)}) %collective-permute-start.17) | collective-permute-done | bytes 262176 | tf_op jit(solution)/shard_map/ppermute | solution.py:270
  57.5 2.9 %collective-permute-start.8 = (bf16[4,8,48,128]{3,2,1,0:T(8,128)(2,1)S(1)}, bf16[4,8,48,128]{3,2,1,0:T(8,128)(2,1)S(1)}, u32[]{:S(2)}, u32[]{:S(2)}) collective-permute-start(bf16[4,8,48,128]{3,2,1,0:T(8,128)(2,1)S(1)} %get-tuple-element.58), channel_id=1, source_target_pairs={{0,4},{4,0},{8,12},{12,8},{1,5},{5,1},{9,13},{13,9},{2,6},{6,2},{1... | collective-permute-start | bytes 1179656 | tf_op jit(solution)/shard_map/ppermute | solution.py:270
  60.3 2.2 %shard_map.55.refs_0_ = f32[8,8,48,128]{3,2,1,0:T(8,128)S(1)} custom-call(f32[8,8,64,128]{3,2,1,0:T(8,128)S(1)} %get-tuple-element.55.refs_0_, bf16[8,4,48,128]{3,2,1,0:T(8,128)(2,1)S(1)} %collective-permute-done.6.refs_1_, bf16[8,8,48,256]{3,2,1,0:T(8,128)(2,1)S(1)} %copy-done.1, f32[64,48]{1,0:T(8,128)S(1)} %bitcast.17, f32[4,64,48]{2,1,0:T(8,128)S(1)} %bitcast.8, ...), custom_call_target="tpu_custom_call" | custom-call | flops 1 | bytes 1 | tf_op jit(solution)/shard_map/pallas_call | solution.py:185
  62.6 2.6 %shard_map.61 = (f32[8,8,48,128]{3,2,1,0:T(8,128)S(1)}, f32[8,8,80,128]{3,2,1,0:T(8,128)S(1)}) custom-call(f32[8,8,80,128]{3,2,1,0:T(8,128)S(1)} %get-tuple-element.69.refs_0_, bf16[8,4,48,128]{3,2,1,0:T(8,128)(2,1)S(1)} %collective-permute-done.16.refs_1_, bf16[8,8,48,128]{3,2,1,0:T(8,128)(2,1)S(1)} %get-tuple-element.64.refs_2_, ...), custom_call_target="tpu_custom_call", output_to_operand_aliasing={{1}: (0, {})} | custom-call | flops 1 | bytes 1 | tf_op jit(solution)/shard_map/pallas_call | solution.py:508
  66.9 2.1 %collective-permute-start.23 = (bf16[4,8,48,128]{3,2,1,0:T(8,128)(2,1)S(1)}, bf16[4,8,48,128]{3,2,1,0:T(8,128)(2,1)S(1)}, u32[]{:S(2)}, u32[]{:S(2)}) collective-permute-start(bf16[4,8,48,128]{3,2,1,0:T(8,128)(2,1)S(1)} %get-tuple-element.81), channel_id=1, source_target_pairs={{0,4},{4,0},{8,12},{12,8},{1,5},{5,1},{9,13},{13,9},{2,6},{6,2},{1... | collective-permute-start | bytes 1179656 | tf_op jit(solution)/shard_map/ppermute | solution.py:270
  70.9 2.2 %collective-permute-start.9 = (bf16[8,4,48,128]{3,2,1,0:T(8,128)(2,1)S(1)}, bf16[8,4,48,128]{3,2,1,0:T(8,128)(2,1)S(1)}, u32[]{:S(2)}, u32[]{:S(2)}) collective-permute-start(bf16[8,4,48,128]{3,2,1,0:T(8,128)(2,1)S(1)} %get-tuple-element.60), channel_id=1, source_target_pairs={{0,2},{2,0},{1,3},{3,1},{4,6},{6,4},{5,7},{7,5},{8,10},{10,8},{9,1... | collective-permute-start | bytes 1179656 | tf_op jit(solution)/shard_map/ppermute | solution.py:270
  73.1 13.9 %collective-permute-done.21.refs_5_ = bf16[8,8,16,128]{3,2,1,0:T(8,128)(2,1)S(1)} collective-permute-done((bf16[8,8,16,128]{3,2,1,0:T(8,128)(2,1)S(1)}, bf16[8,8,16,128]{3,2,1,0:T(8,128)(2,1)S(1)}, u32[]{:S(2)}, u32[]{:S(2)}) %collective-permute-start.21) | collective-permute-done | bytes 262176 | tf_op jit(solution)/shard_map/ppermute | solution.py:270
  87.1 2.6 %shard_map.63 = (f32[8,8,48,128]{3,2,1,0:T(8,128)S(1)}, f32[8,8,80,128]{3,2,1,0:T(8,128)S(1)}) custom-call(f32[8,8,80,128]{3,2,1,0:T(8,128)S(1)} %get-tuple-element.75.refs_0_, bf16[8,4,48,128]{3,2,1,0:T(8,128)(2,1)S(1)} %collective-permute-done.20.refs_1_, bf16[8,8,48,128]{3,2,1,0:T(8,128)(2,1)S(1)} %get-tuple-element.64.refs_2_, ...), custom_call_target="tpu_custom_call", output_to_operand_aliasing={{1}: (0, {})} | custom-call | flops 1 | bytes 1 | tf_op jit(solution)/shard_map/pallas_call | solution.py:508
  91.7 1.9 %collective-permute-done.24.got_ref = f32[520,256]{1,0:T(8,128)S(1)} collective-permute-done((f32[520,256]{1,0:T(8,128)S(1)}, f32[520,256]{1,0:T(8,128)S(1)}, u32[]{:S(2)}, u32[]{:S(2)}) %collective-permute-start.24) | collective-permute-done | bytes 532512 | tf_op jit(solution)/shard_map/ppermute | solution.py:270
  95.1 2.4 %collective-permute-start.26 = (bf16[144,256]{1,0:T(8,128)(2,1)S(1)}, bf16[144,256]{1,0:T(8,128)(2,1)S(1)}, u32[]{:S(2)}, u32[]{:S(2)}) collective-permute-start(bf16[144,256]{1,0:T(8,128)(2,1)S(1)} %get-tuple-element.88), channel_id=1, source_target_pairs={{0,12},{4,8},{8,4},{12,0},{1,13},{5,9},{9,5},{13,1},{2,14},{6,10},... | collective-permute-start | bytes 221192 | tf_op jit(solution)/shard_map/ppermute | solution.py:785
  97.5 5.4 %collective-permute-done.25.refs_0_ = bf16[144,256]{1,0:T(8,128)(2,1)S(1)} collective-permute-done((bf16[144,256]{1,0:T(8,128)(2,1)S(1)}, bf16[144,256]{1,0:T(8,128)(2,1)S(1)}, u32[]{:S(2)}, u32[]{:S(2)}) %collective-permute-start.25) | collective-permute-done | bytes 73760 | tf_op jit(solution)/shard_map/ppermute | solution.py:785
  103.4 1.6 %collective-permute-start.28 = (bf16[144,256]{1,0:T(8,128)(2,1)S(1)}, bf16[144,256]{1,0:T(8,128)(2,1)S(1)}, u32[]{:S(2)}, u32[]{:S(2)}) collective-permute-start(bf16[144,256]{1,0:T(8,128)(2,1)S(1)} %shard_map.67.mine_ref), channel_id=1, source_target_pairs={{0,2},{2,0},{1,3},{3,1},{4,6},{6,4},{5,7},{7,5},{8,10},{10,8},{9,1... | collective-permute-start | bytes 221192 | tf_op jit(solution)/shard_map/ppermute | solution.py:270
  105.0 2.9 %collective-permute-done.28.other_ref = bf16[144,256]{1,0:T(8,128)(2,1)S(1)} collective-permute-done((bf16[144,256]{1,0:T(8,128)(2,1)S(1)}, bf16[144,256]{1,0:T(8,128)(2,1)S(1)}, u32[]{:S(2)}, u32[]{:S(2)}) %collective-permute-start.28) | collective-permute-done | bytes 73760 | tf_op jit(solution)/shard_map/ppermute | solution.py:270
  (65 shorter events, 23.1 us)
Async XLA Ops:
  3.4 24.1 %collective-permute-start.10 = (bf16[8,8,32,128]{3,2,1,0:T(8,128)(2,1)S(1)}, bf16[8,8,32,128]{3,2,1,0:T(8,128)(2,1)S(1)}, u32[]{:S(2)}, u32[]{:S(2)}) collective-permute-start(bf16[8,8,32,128]{3,2,1,0:T(8,128)(2,1)S(1)} %get-tuple-element.61), channel_id=1, source_target_pairs={{0,2},{2,0},{1,3},{3,1},{4,6},{6,4},{5,7},{7,5},{8,10},{10,8},{9,1... | collective-permute-start | bytes 1572872 | tf_op jit(solution)/shard_map/ppermute | solution.py:270
  7.6 7.3 %collective-permute-start.1 = (bf16[4,8,48,128]{3,2,1,0:T(8,128)(2,1)S(1)}, bf16[4,8,48,128]{3,2,1,0:T(8,128)(2,1)S(1)}, u32[]{:S(2)}, u32[]{:S(2)}) collective-permute-start(bf16[4,8,48,128]{3,2,1,0:T(8,128)(2,1)S(1)} %get-tuple-element.49), channel_id=1, source_target_pairs={{4,8},{8,4},{5,9},{9,5},{6,10},{10,6},{7,11},{11,7},{20,24},{24,20... | collective-permute-start | bytes 1179656 | tf_op jit(solution)/shard_map/ppermute | solution.py:270
  8.3 13.9 %collective-permute-start.2 = (bf16[4,8,48,128]{3,2,1,0:T(8,128)(2,1)S(1)}, bf16[4,8,48,128]{3,2,1,0:T(8,128)(2,1)S(1)}, u32[]{:S(2)}, u32[]{:S(2)}) collective-permute-start(bf16[4,8,48,128]{3,2,1,0:T(8,128)(2,1)S(1)} %get-tuple-element.50), channel_id=1, source_target_pairs={{0,4},{4,0},{8,12},{12,8},{1,5},{5,1},{9,13},{13,9},{2,6},{6,2},{1... | collective-permute-start | bytes 1179656 | tf_op jit(solution)/shard_map/ppermute | solution.py:270
  23.4 8.8 %collective-permute-start.4 = (bf16[4,8,48,128]{3,2,1,0:T(8,128)(2,1)S(1)}, bf16[4,8,48,128]{3,2,1,0:T(8,128)(2,1)S(1)}, u32[]{:S(2)}, u32[]{:S(2)}) collective-permute-start(bf16[4,8,48,128]{3,2,1,0:T(8,128)(2,1)S(1)} %get-tuple-element.53), channel_id=1, source_target_pairs={{4,8},{8,4},{5,9},{9,5},{6,10},{10,6},{7,11},{11,7},{20,24},{24,20... | collective-permute-start | bytes 1179656 | tf_op jit(solution)/shard_map/ppermute | solution.py:270
  24.1 13.4 %collective-permute-start.5 = (bf16[4,8,48,128]{3,2,1,0:T(8,128)(2,1)S(1)}, bf16[4,8,48,128]{3,2,1,0:T(8,128)(2,1)S(1)}, u32[]{:S(2)}, u32[]{:S(2)}) collective-permute-start(bf16[4,8,48,128]{3,2,1,0:T(8,128)(2,1)S(1)} %get-tuple-element.54), channel_id=1, source_target_pairs={{0,4},{4,0},{8,12},{12,8},{1,5},{5,1},{9,13},{13,9},{2,6},{6,2},{1... | collective-permute-start | bytes 1179656 | tf_op jit(solution)/shard_map/ppermute | solution.py:270
  28.3 16.4 %collective-permute-start.11 = (bf16[8,4,48,128]{3,2,1,0:T(8,128)(2,1)S(1)}, bf16[8,4,48,128]{3,2,1,0:T(8,128)(2,1)S(1)}, u32[]{:S(2)}, u32[]{:S(2)}) collective-permute-start(bf16[8,4,48,128]{3,2,1,0:T(8,128)(2,1)S(1)} %get-tuple-element.63), channel_id=1, source_target_pairs={{0,1},{1,0},{2,3},{3,2},{4,5},{5,4},{6,7},{7,6},{8,9},{9,8},{10,11... | collective-permute-start | bytes 1179656 | tf_op jit(solution)/shard_map/ppermute | solution.py:270
  28.4 18.8 %collective-permute-start.12 = (bf16[4,4,48,128]{3,2,1,0:T(8,128)(2,1)S(1)}, bf16[4,4,48,128]{3,2,1,0:T(8,128)(2,1)S(1)}, u32[]{:S(2)}, u32[]{:S(2)}) collective-permute-start(bf16[4,4,48,128]{3,2,1,0:T(8,128)(2,1)S(1)} %get-tuple-element.65), channel_id=1, source_target_pairs={{4,8},{8,4},{5,9},{9,5},{6,10},{10,6},{7,11},{11,7},{20,24},{24,20... | collective-permute-start | bytes 589832 | tf_op jit(solution)/shard_map/ppermute | solution.py:270
  29.1 18.1 %collective-permute-start.14 = (bf16[4,4,48,128]{3,2,1,0:T(8,128)(2,1)S(1)}, bf16[4,4,48,128]{3,2,1,0:T(8,128)(2,1)S(1)}, u32[]{:S(2)}, u32[]{:S(2)}) collective-permute-start(bf16[4,4,48,128]{3,2,1,0:T(8,128)(2,1)S(1)} %get-tuple-element.67), channel_id=1, source_target_pairs={{0,4},{4,0},{8,12},{12,8},{1,5},{5,1},{9,13},{13,9},{2,6},{6,2},{1... | collective-permute-start | bytes 589832 | tf_op jit(solution)/shard_map/ppermute | solution.py:270
  32.2 15.0 %collective-permute-start.13 = (bf16[4,4,48,128]{3,2,1,0:T(8,128)(2,1)S(1)}, bf16[4,4,48,128]{3,2,1,0:T(8,128)(2,1)S(1)}, u32[]{:S(2)}, u32[]{:S(2)}) collective-permute-start(bf16[4,4,48,128]{3,2,1,0:T(8,128)(2,1)S(1)} %get-tuple-element.66), channel_id=1, source_target_pairs={{4,8},{8,4},{5,9},{9,5},{6,10},{10,6},{7,11},{11,7},{20,24},{24,20... | collective-permute-start | bytes 589832 | tf_op jit(solution)/shard_map/ppermute | solution.py:270
  37.5 9.7 %collective-permute-start.15 = (bf16[4,4,48,128]{3,2,1,0:T(8,128)(2,1)S(1)}, bf16[4,4,48,128]{3,2,1,0:T(8,128)(2,1)S(1)}, u32[]{:S(2)}, u32[]{:S(2)}) collective-permute-start(bf16[4,4,48,128]{3,2,1,0:T(8,128)(2,1)S(1)} %get-tuple-element.68), channel_id=1, source_target_pairs={{0,4},{4,0},{8,12},{12,8},{1,5},{5,1},{9,13},{13,9},{2,6},{6,2},{1... | collective-permute-start | bytes 589832 | tf_op jit(solution)/shard_map/ppermute | solution.py:270
  44.7 12.7 %collective-permute-start.6 = (bf16[8,4,48,128]{3,2,1,0:T(8,128)(2,1)S(1)}, bf16[8,4,48,128]{3,2,1,0:T(8,128)(2,1)S(1)}, u32[]{:S(2)}, u32[]{:S(2)}) collective-permute-start(bf16[8,4,48,128]{3,2,1,0:T(8,128)(2,1)S(1)} %get-tuple-element.56), channel_id=1, source_target_pairs={{0,1},{1,0},{2,3},{3,2},{4,5},{5,4},{6,7},{7,6},{8,9},{9,8},{10,11... | collective-permute-start | bytes 1179656 | tf_op jit(solution)/shard_map/ppermute | solution.py:270
  48.0 8.8 %collective-permute-start.17 = (bf16[8,8,16,128]{3,2,1,0:T(8,128)(2,1)S(1)}, bf16[8,8,16,128]{3,2,1,0:T(8,128)(2,1)S(1)}, u32[]{:S(2)}, u32[]{:S(2)}) collective-permute-start(bf16[8,8,16,128]{3,2,1,0:T(8,128)(2,1)S(1)} %get-tuple-element.71), channel_id=1, source_target_pairs={{0,2},{2,0},{1,3},{3,1},{4,6},{6,4},{5,7},{7,5},{8,10},{10,8},{9,1... | collective-permute-start | bytes 786440 | tf_op jit(solution)/shard_map/ppermute | solution.py:270
  48.6 14.0 %collective-permute-start.16 = (bf16[8,4,48,128]{3,2,1,0:T(8,128)(2,1)S(1)}, bf16[8,4,48,128]{3,2,1,0:T(8,128)(2,1)S(1)}, u32[]{:S(2)}, u32[]{:S(2)}) collective-permute-start(bf16[8,4,48,128]{3,2,1,0:T(8,128)(2,1)S(1)} %get-tuple-element.70), channel_id=1, source_target_pairs={{0,1},{1,0},{2,3},{3,2},{4,5},{5,4},{6,7},{7,6},{8,9},{9,8},{10,11... | collective-permute-start | bytes 1179656 | tf_op jit(solution)/shard_map/ppermute | solution.py:270
  48.8 16.4 %collective-permute-start.18 = (bf16[4,8,48,128]{3,2,1,0:T(8,128)(2,1)S(1)}, bf16[4,8,48,128]{3,2,1,0:T(8,128)(2,1)S(1)}, u32[]{:S(2)}, u32[]{:S(2)}) collective-permute-start(bf16[4,8,48,128]{3,2,1,0:T(8,128)(2,1)S(1)} %get-tuple-element.73), channel_id=1, source_target_pairs={{4,8},{8,4},{5,9},{9,5},{6,10},{10,6},{7,11},{11,7},{20,24},{24,20... | collective-permute-start | bytes 1179656 | tf_op jit(solution)/shard_map/ppermute | solution.py:270
  49.5 15.7 %collective-permute-start.19 = (bf16[4,8,48,128]{3,2,1,0:T(8,128)(2,1)S(1)}, bf16[4,8,48,128]{3,2,1,0:T(8,128)(2,1)S(1)}, u32[]{:S(2)}, u32[]{:S(2)}) collective-permute-start(bf16[4,8,48,128]{3,2,1,0:T(8,128)(2,1)S(1)} %get-tuple-element.74), channel_id=1, source_target_pairs={{0,4},{4,0},{8,12},{12,8},{1,5},{5,1},{9,13},{13,9},{2,6},{6,2},{1... | collective-permute-start | bytes 1179656 | tf_op jit(solution)/shard_map/ppermute | solution.py:270
  56.8 12.3 %collective-permute-start.7 = (bf16[4,8,48,128]{3,2,1,0:T(8,128)(2,1)S(1)}, bf16[4,8,48,128]{3,2,1,0:T(8,128)(2,1)S(1)}, u32[]{:S(2)}, u32[]{:S(2)}) collective-permute-start(bf16[4,8,48,128]{3,2,1,0:T(8,128)(2,1)S(1)} %get-tuple-element.57), channel_id=1, source_target_pairs={{4,8},{8,4},{5,9},{9,5},{6,10},{10,6},{7,11},{11,7},{20,24},{24,20... | collective-permute-start | bytes 1179656 | tf_op jit(solution)/shard_map/ppermute | solution.py:270
  57.5 12.6 %collective-permute-start.8 = (bf16[4,8,48,128]{3,2,1,0:T(8,128)(2,1)S(1)}, bf16[4,8,48,128]{3,2,1,0:T(8,128)(2,1)S(1)}, u32[]{:S(2)}, u32[]{:S(2)}) collective-permute-start(bf16[4,8,48,128]{3,2,1,0:T(8,128)(2,1)S(1)} %get-tuple-element.58), channel_id=1, source_target_pairs={{0,4},{4,0},{8,12},{12,8},{1,5},{5,1},{9,13},{13,9},{2,6},{6,2},{1... | collective-permute-start | bytes 1179656 | tf_op jit(solution)/shard_map/ppermute | solution.py:270
  66.0 21.1 %collective-permute-start.20 = (bf16[8,4,48,128]{3,2,1,0:T(8,128)(2,1)S(1)}, bf16[8,4,48,128]{3,2,1,0:T(8,128)(2,1)S(1)}, u32[]{:S(2)}, u32[]{:S(2)}) collective-permute-start(bf16[8,4,48,128]{3,2,1,0:T(8,128)(2,1)S(1)} %get-tuple-element.76), channel_id=1, source_target_pairs={{0,1},{1,0},{2,3},{3,2},{4,5},{5,4},{6,7},{7,6},{8,9},{9,8},{10,11... | collective-permute-start | bytes 1179656 | tf_op jit(solution)/shard_map/ppermute | solution.py:270
  66.1 23.6 %collective-permute-start.22 = (bf16[4,8,48,128]{3,2,1,0:T(8,128)(2,1)S(1)}, bf16[4,8,48,128]{3,2,1,0:T(8,128)(2,1)S(1)}, u32[]{:S(2)}, u32[]{:S(2)}) collective-permute-start(bf16[4,8,48,128]{3,2,1,0:T(8,128)(2,1)S(1)} %get-tuple-element.80), channel_id=1, source_target_pairs={{4,8},{8,4},{5,9},{9,5},{6,10},{10,6},{7,11},{11,7},{20,24},{24,20... | collective-permute-start | bytes 1179656 | tf_op jit(solution)/shard_map/ppermute | solution.py:270
  66.9 22.7 %collective-permute-start.23 = (bf16[4,8,48,128]{3,2,1,0:T(8,128)(2,1)S(1)}, bf16[4,8,48,128]{3,2,1,0:T(8,128)(2,1)S(1)}, u32[]{:S(2)}, u32[]{:S(2)}) collective-permute-start(bf16[4,8,48,128]{3,2,1,0:T(8,128)(2,1)S(1)} %get-tuple-element.81), channel_id=1, source_target_pairs={{0,4},{4,0},{8,12},{12,8},{1,5},{5,1},{9,13},{13,9},{2,6},{6,2},{1... | collective-permute-start | bytes 1179656 | tf_op jit(solution)/shard_map/ppermute | solution.py:270
  70.9 19.4 %collective-permute-start.9 = (bf16[8,4,48,128]{3,2,1,0:T(8,128)(2,1)S(1)}, bf16[8,4,48,128]{3,2,1,0:T(8,128)(2,1)S(1)}, u32[]{:S(2)}, u32[]{:S(2)}) collective-permute-start(bf16[8,4,48,128]{3,2,1,0:T(8,128)(2,1)S(1)} %get-tuple-element.60), channel_id=1, source_target_pairs={{0,2},{2,0},{1,3},{3,1},{4,6},{6,4},{5,7},{7,5},{8,10},{10,8},{9,1... | collective-permute-start | bytes 1179656 | tf_op jit(solution)/shard_map/ppermute | solution.py:270
  73.0 14.0 %collective-permute-start.21 = (bf16[8,8,16,128]{3,2,1,0:T(8,128)(2,1)S(1)}, bf16[8,8,16,128]{3,2,1,0:T(8,128)(2,1)S(1)}, u32[]{:S(2)}, u32[]{:S(2)}) collective-permute-start(bf16[8,8,16,128]{3,2,1,0:T(8,128)(2,1)S(1)} %get-tuple-element.77), channel_id=1, source_target_pairs={{0,2},{2,0},{1,3},{3,1},{4,6},{6,4},{5,7},{7,5},{8,10},{10,8},{9,1... | collective-permute-start | bytes 786440 | tf_op jit(solution)/shard_map/ppermute | solution.py:270
  93.6 9.2 %collective-permute-start.25 = (bf16[144,256]{1,0:T(8,128)(2,1)S(1)}, bf16[144,256]{1,0:T(8,128)(2,1)S(1)}, u32[]{:S(2)}, u32[]{:S(2)}) collective-permute-start(bf16[144,256]{1,0:T(8,128)(2,1)S(1)} %get-tuple-element.87), channel_id=1, source_target_pairs={{0,8},{4,12},{8,0},{12,4},{1,9},{5,13},{9,1},{13,5},{2,10},{6,14},... | collective-permute-start | bytes 221192 | tf_op jit(solution)/shard_map/ppermute | solution.py:785
  95.1 7.8 %collective-permute-start.26 = (bf16[144,256]{1,0:T(8,128)(2,1)S(1)}, bf16[144,256]{1,0:T(8,128)(2,1)S(1)}, u32[]{:S(2)}, u32[]{:S(2)}) collective-permute-start(bf16[144,256]{1,0:T(8,128)(2,1)S(1)} %get-tuple-element.88), channel_id=1, source_target_pairs={{0,12},{4,8},{8,4},{12,0},{1,13},{5,9},{9,5},{13,1},{2,14},{6,10},... | collective-permute-start | bytes 221192 | tf_op jit(solution)/shard_map/ppermute | solution.py:785
  (10 other events, 60.8 us)

commit v14 on v13

--- a/solution.py
+++ b/solution.py
@@ -296,48 +296,26 @@
     return jnp.where(chip == 0, window[:half], window[window.shape[0] - half :])
 
 
-def prepare_body(p_ref, s_ref, window_ref, odd_ref, even_ref, square):
-    depth, across, rows, _ = window_ref.shape
-    half = rows - EDGE
-    along = 2 * half
-    chip = lax.axis_index("probe")
-    even = slab_is_even()
-    lanes = slice(LANES, 2 * LANES)
-    skip = along - rows
+def window_body(p_ref, window_ref):
+    depth, _, rows, _ = window_ref.shape
+    skip = p_ref.shape[2] - rows
+    start = pl.multiple_of((1 - lax.axis_index("probe")) * skip, TILE)
 
     def plane(z, _):
-        start = pl.multiple_of((1 - chip) * skip, TILE)
-        window_ref[z] = p_ref[z, :, pl.ds(start, rows), lanes]
+        window_ref[z] = p_ref[z, :, pl.ds(start, rows), LANES : 2 * LANES]
         return 0
 
     lax.fori_loop(0, depth, plane, 0)
-    source = half_rows(square, s_ref[0], half, chip)[:half]
-    start = pl.multiple_of(chip * skip, TILE)
-
-    def value(z, x):
-        window = p_ref[z, x, pl.ds(start, rows), lanes].astype(F32)
-        return lane(source, z * across + x) * own_half(window, half, chip)
-
-    for j in range(RADIUS):
-        for i in range(across // 2):
-            low, high = [
-                jnp.concatenate([value(z, 2 * i), value(z, 2 * i + 1)], axis=0).astype(BF16)
-                for z in (j, depth - RADIUS + j)
-            ]
-            even_ref[j, i] = jnp.where(even, high, low)
-            odd_ref[j, i] = jnp.where(even, low, high)
-
-
-def prepare(probes, source):
+
+
+def window_of(probes):
     depth, across, along, _ = probes.shape
-    edge = shape_of(RADIUS, across // 2, along, BF16)
-    return call(
-        prepare_body,
-        in_specs=whole_vmem(2),
-        out_specs=whole_vmem(3),
-        out_shape=[shape_of(depth, across, along // 2 + EDGE, BF16), edge, edge],
-        scratch_shapes=square_scratch()[:1],
-    )(probes, source)
+    return call(
+        window_body,
+        in_specs=whole_vmem(1),
+        out_specs=whole_vmem(1)[0],
+        out_shape=shape_of(depth, across, along // 2 + EDGE, BF16),
+    )(probes)
 
 
 def store_sides(core, chip, u_ref, edge_ref, rows_ref):
@@ -378,31 +356,29 @@
     start = pl.multiple_of(chip * (along - rows), TILE)
     source = square[pl.ds(start, rows)]
     blank = jnp.zeros((EDGE, LANES), F32)
-    for i in range(across // 2):
-        theirs = []
+    for x in range(across):
+        news = []
         for z in range(depth):
-            pair = []
-            for x in (2 * i, 2 * i + 1):
-                mine = p_ref[z, x, pl.ds(start, rows), lanes].astype(F32)
-                got = got_ref[z, x].astype(F32)
-                scale = lane(source, z * across + x)
-                windows = [jnp.where(chip == 0, mine, got), jnp.where(chip == 0, got, mine)]
-                for g, window in enumerate(windows):
-                    at = pl.multiple_of(g * segment + EDGE * (1 - chip), 8)
-                    u_ref[z, x, pl.ds(at, rows)] = scale * window
-                    out = pl.multiple_of(g * segment + chip * (half + EDGE), 8)
-                    u_ref[z, x, pl.ds(out, EDGE)] = blank
-                both = [own_half(window, half, chip) for window in windows]
-                both_ref[z, x] = jnp.concatenate(both, axis=0).astype(BF16)
-                pair.append(own_half(scale * got, half, chip))
-            theirs.append(jnp.concatenate(pair, axis=0))
-        store_edges(i, pl.ds(0, along), theirs, even, even_ref, odd_ref)
+            mine = p_ref[z, x, pl.ds(start, rows), lanes].astype(F32)
+            got = got_ref[z, x].astype(F32)
+            scale = lane(source, z * across + x)
+            windows = [jnp.where(chip == 0, mine, got), jnp.where(chip == 0, got, mine)]
+            for g, window in enumerate(windows):
+                at = pl.multiple_of(g * segment + EDGE * (1 - chip), 8)
+                u_ref[z, x, pl.ds(at, rows)] = scale * window
+                out = pl.multiple_of(g * segment + chip * (half + EDGE), 8)
+                u_ref[z, x, pl.ds(out, EDGE)] = blank
+            both = [own_half(window, half, chip) for window in windows]
+            both_ref[z, x] = jnp.concatenate(both, axis=0).astype(BF16)
+            u = [own_half(scale * window, half, chip) for window in windows]
+            news.append(jnp.concatenate(u, axis=0))
+        store_edges(x, pl.ds(0, along), news, even, even_ref, odd_ref)
     store_sides(core, chip, u_ref, edge_ref, None)
 
 
 def shared_first(probes, got, source):
     depth, across, along, _ = probes.shape
-    edge = shape_of(RADIUS, across // 2, along, BF16)
+    edge = shape_of(RADIUS, across, along, BF16)
     return call(
         shared_first_body,
         in_specs=whole_vmem(3),
@@ -418,34 +394,11 @@
     )(probes, got, source)
 
 
-def fill_rows(u_ref, rows_ref, chip):
-    depth, across, padded, _ = u_ref.shape
-    segment = padded // 2
-
-    def plane(z, _):
-        for x in range(across):
-            got = rows_ref[z, x].astype(F32)
-            for g in range(2):
-                part = got[g * EDGE : (g + 1) * EDGE]
-                blank = jnp.zeros_like(part)
-                before, after = g * segment, (g + 1) * segment - EDGE
-                u_ref[z, x, before : before + EDGE] = jnp.where(chip == 0, blank, part)
-                u_ref[z, x, after : after + EDGE] = jnp.where(chip == 0, part, blank)
-        return 0
-
-    lax.fori_loop(0, depth, plane, 0)
-
-
-def shared_local_body(moment, has_rows, has_previous, *refs):
+def shared_local_body(moment, has_previous, *refs):
     refs = list(refs)
     u_ref, beside_ref, p_ref, c_ref, s_ref = refs[:5]
-    rest = refs[5:]
-    rows_ref = rest.pop(0) if has_rows else None
-    prev_ref = rest.pop(0) if has_previous else None
-    base_ref = rest.pop(0)
-    if has_rows:
-        u_ref = rest.pop(0)
-    square, turned_c, turned_s = rest
+    prev_ref = refs[5] if has_previous else None
+    base_ref, square, turned_c, turned_s = refs[-4:]
     depth, across, along, _ = base_ref.shape
     half = along // 2
     core = lax.axis_index("sub")
@@ -454,8 +407,6 @@
     right_on = (core == 0).astype(F32)
     turned_c[:along] = half_rows(square, c_ref[...], half, chip)
     turned_s[:along] = half_rows(square, s_ref[moment], half, chip)
-    if has_rows:
-        fill_rows(u_ref, rows_ref, chip)
 
     def tile(start):
         span = pl.ds(start, TILE)
@@ -496,60 +447,72 @@
     tiles(along, tile)
 
 
-def shared_local(u, beside, both, courant, source, moment, rows, previous):
+def shared_local(u, beside, both, courant, source, moment, previous):
     depth, across, along, _ = both.shape
     operands = [u, beside, both, courant, source]
-    operands += [a for a in (rows, previous) if a is not None]
-    out_shape = [shape_of(depth, across, along, F32)]
-    aliases = {}
-    if rows is not None:
-        aliases = {0: 1}
-        out_shape.append(jax.ShapeDtypeStruct(u.shape, F32))
-    out = call(
-        functools.partial(shared_local_body, moment, rows is not None, previous is not None),
+    if previous is not None:
+        operands.append(previous)
+    return call(
+        functools.partial(shared_local_body, moment, previous is not None),
         in_specs=whole_vmem(len(operands)),
-        out_specs=whole_vmem(len(out_shape)),
-        out_shape=out_shape,
-        input_output_aliases=aliases,
+        out_specs=whole_vmem(1)[0],
+        out_shape=shape_of(depth, across, along, F32),
         scratch_shapes=square_scratch() + square_scratch()[:1],
     )(*operands)
-    return out[0], (u if rows is None else out[1])
-
-
-def planes_of(refs, x, half, chip):
-    if len(refs) == 1:
-        return [refs[0][j, x].astype(F32) for j in range(RADIUS)]
-    planes = []
-    for j in range(RADIUS):
-        at = (x % 2) * half
-        own, other = [ref[j, x // 2].astype(F32)[at : at + half] for ref in refs]
-        parts = [jnp.where(chip == 0, own, other), jnp.where(chip == 0, other, own)]
-        planes.append(jnp.concatenate(parts, axis=0))
-    return planes
-
-
-def wide_rim_body(kind, count, *refs):
-    base_ref, c_ref = refs[:2]
-    odd_refs, even_refs = refs[2 : 2 + count], refs[2 + count : 2 + 2 * count]
-    outs, square = refs[2 + 2 * count : -1], refs[-1]
+
+
+def wide_rim_body(kind, has_rows, *refs):
+    base_ref, c_ref, odd_ref, even_ref = refs[:4]
+    rows_ref = refs[4] if has_rows else None
+    outs = refs[4 + has_rows : -2]
+    square, shifted = refs[-2:]
     depth, across, along, _ = base_ref.shape
     half = along // 2
     segment = half + 2 * EDGE
     core = lax.axis_index("sub")
     chip = lax.axis_index("probe")
     even = slab_is_even()
+    blank = jnp.zeros((EDGE, LANES), F32)
     if kind == "own":
         courant = turned(c_ref[...], square)[:along]
     else:
         courant = half_rows(square, c_ref[...], half, chip)
 
+    if has_rows:
+
+        def place(z, _):
+            for x in range(across):
+                got = rows_ref[z, x].astype(F32)
+                for g in range(2):
+                    shifted[z, x, g, :EDGE] = blank
+                    shifted[z, x, g, EDGE : 2 * EDGE] = got[g * EDGE : (g + 1) * EDGE]
+                    shifted[z, x, g, 2 * EDGE :] = blank
+            return 0
+
+        lax.fori_loop(0, depth, place, 0)
+
+    def rows_beyond(z, x):
+        parts = []
+        for g in range(2):
+            total = None
+            for r in range(1, RADIUS + 1):
+                after = shifted[z, x, g, r : r + EDGE]
+                before = shifted[z, x, g, 2 * EDGE - r : 3 * EDGE - r]
+                term = COEFFICIENTS[r] * jnp.where(chip == 0, after, before)
+                total = term if total is None else total + term
+            first = jnp.where(chip == 0, blank, total)
+            last = jnp.where(chip == 0, total, blank)
+            parts += [first] + [blank] * (half // EDGE - 2) + [last]
+        return jnp.concatenate(parts, axis=0)
+
     def values(x):
-        ones, twos = planes_of(even_refs, x, half, chip), planes_of(odd_refs, x, half, chip)
+        ones = [even_ref[j, x].astype(F32) for j in range(RADIUS)]
+        twos = [odd_ref[j, x].astype(F32) for j in range(RADIUS)]
         below = [jnp.where(even, two, one) for one, two in zip(ones, twos)]
         above = [jnp.where(even, one, two) for one, two in zip(ones, twos)]
         news = []
         for z in range(depth):
-            added = None
+            added = rows_beyond(z, x) if has_rows else None
             for r in range(1, RADIUS + 1):
                 if z - r < 0:
                     term = COEFFICIENTS[r] * below[RADIUS + z - r]
@@ -564,15 +527,17 @@
         return news
 
     if kind == "middle":
-        u_ref, odd_ref, even_ref, edge_ref, rows_ref = outs
+        u_ref, odd_out, even_out, edge_ref, rows_out = outs
         for x in range(across):
             news = values(x)
             for z, new in enumerate(news):
                 for g in range(2):
                     at = g * segment + EDGE
+                    u_ref[z, x, at - EDGE : at] = blank
                     u_ref[z, x, at : at + half] = new[g * half : (g + 1) * half]
-            store_edges(x, pl.ds(0, along), news, even, even_ref, odd_ref)
-        store_sides(core, chip, u_ref, edge_ref, rows_ref)
+                    u_ref[z, x, at + half : at + half + EDGE] = blank
+            store_edges(x, pl.ds(0, along), news, even, even_out, odd_out)
+        store_sides(core, chip, u_ref, edge_ref, rows_out)
         return
     for i in range(across // 2):
         for z, (one, two) in enumerate(zip(values(2 * i), values(2 * i + 1))):
@@ -587,7 +552,7 @@
             outs[1][z, i] = second
 
 
-def wide_rim(base, courant, odds, evens, kind):
+def wide_rim(base, courant, odd, even, kind, rows=None):
     depth, across, along, _ = base.shape
     if kind == "middle":
         edge = shape_of(RADIUS, across, along, BF16)
@@ -600,13 +565,17 @@
         ]
     else:
         out_shape = [shape_of(depth, across // 2, along, BF16)] * 2
-    return call(
-        functools.partial(wide_rim_body, kind, len(odds)),
-        in_specs=whole_vmem(2 + 2 * len(odds)),
+    operands = [base, courant, odd, even]
+    if rows is not None:
+        operands.append(rows)
+    return call(
+        functools.partial(wide_rim_body, kind, rows is not None),
+        in_specs=whole_vmem(len(operands)),
         out_specs=whole_vmem(len(out_shape)),
         out_shape=out_shape,
-        scratch_shapes=square_scratch()[:1],
-    )(base, courant, *odds, *evens)
+        scratch_shapes=square_scratch()[:1]
+        + [pltpu.VMEM((depth, across, 2, 3 * EDGE, LANES), F32)],
+    )(*operands)
 
 
 def gram_body(kept_ref, got_ref, one_ref, two_ref, keep_ref, send_ref, panel):
@@ -849,37 +818,35 @@
 def shared_shards(probes, courant, source, exchange, cell_count):
     steps = source.shape[0]
     first_source = source[:1]
+    got = chip_swap(window_of(probes))
     u, *edges = first_field(probes, 0, first_source)
     odd, even, beside = exchange(*edges)
-    window, one, two = prepare(probes, first_source)
-    got = chip_swap(window)
-    odds, evens = [odd_swap(one)], [even_swap(two)]
-    shared_u, one, two, edge, both = shared_first(probes, got, first_source)
-    odds.append(odd_swap(one))
-    evens.append(even_swap(two))
-    shared_beside, rows = core_swap(edge), None
-
-    previous = shared_previous = None
+    shared_u, *edges, both = shared_first(probes, got, first_source)
+    shared_odd, shared_even, shared_beside = exchange(*edges)
+
+    previous = shared_previous = rows = None
     for n in range(1, steps):
         last = n == steps - 1
         base = local_step(u, beside, probes, 0, courant, source, n, previous)
         if last:
-            kept, sent = wide_rim(base, courant, [odd], [even], "own")
+            kept, sent = wide_rim(base, courant, odd, even, "own")
             fields = [kept, chip_swap(sent)]
         else:
             previous = u
             u, *edges = rim_step(base, odd, even, courant, "middle")
             odd, even, beside = exchange(*edges)
-        base, shared_u = shared_local(
-            shared_u, shared_beside, both, courant, source, n, rows, shared_previous
+        base = shared_local(
+            shared_u, shared_beside, both, courant, source, n, shared_previous
         )
         if last:
-            fields += wide_rim(base, courant, odds, evens, "both")
+            fields += wide_rim(base, courant, shared_odd, shared_even, "both", rows)
         else:
             shared_previous = shared_u
-            shared_u, one, two, edge, rows = wide_rim(base, courant, odds, evens, "middle")
-            odds, evens = [odd_swap(one)], [even_swap(two)]
-            shared_beside, rows = core_swap(edge), chip_swap(rows)
+            shared_u, *edges, rows = wide_rim(
+                base, courant, shared_odd, shared_even, "middle", rows
+            )
+            shared_odd, shared_even, shared_beside = exchange(*edges)
+            rows = chip_swap(rows)
     return coupled(fields, cell_count)
 
 

time: 111 us -> 109 us (0.982)
  starting transfers between devices: 39.6 us -> 37.3 us
    ppermute x27 -> x25, starting transfers between devices: 35.7 us -> 33.7 us  [swap(): lax.ppermute(x, axis, [p for a, b in pairs for p in ((a, b), (b, a))])]
    ppermute x27 -> x25, waiting for transfers between devices: 37.4 us -> 38.2 us  [swap(): lax.ppermute(x, axis, [p for a, b in pairs for p in ((a, b), (b, a))])]
  transfers between devices with their start and end apart: 30 -> 28, of which waited for: 10 -> 11; matrix products, arithmetic and copies ran while one was open for 0% -> 0% of each run, Pallas kernels for 19% -> 19%
where the time goes in v14:
time: 109 us
  waiting for transfers between devices  44.2 us (41%)
  starting transfers between devices  37.3 us (34%)
  Pallas kernels  24.5 us (22%)
  local copies, waits for them, and re-layouts  2.18 us (2%)
    ppermute x25, waiting for transfers between devices, swap(): lax.ppermute(x, axis, [p for a, b in pairs for p in ((a, b), (b, a))])  38.2 us
    ppermute x25, starting transfers between devices, swap(): lax.ppermute(x, axis, [p for a, b in pairs for p in ((a, b), (b, a))])  33.7 us
    pallas_call x3, Pallas kernels, shared_local(): call(functools.partial(shared_local_body, moment, previous is not None),...  7.28 us
    pallas_call x3, Pallas kernels, local_step(): call(functools.partial(local_body, chunk, moment, previous is not None),...  6.64 us
    ppermute x3, waiting for transfers between devices, coupled(): lax.ppermute(blocks[d - 1], 'slab', [(i, i ^ d) for i in range(slabs)])  6.08 us
    pallas_call x4, Pallas kernels, wide_rim(): call(functools.partial(wide_rim_body, kind, rows is not None), in_specs=w...  3.81 us
    ppermute x3, starting transfers between devices, coupled(): lax.ppermute(blocks[d - 1], 'slab', [(i, i ^ d) for i in range(slabs)])  3.55 us
    pallas_call x2, Pallas kernels, rim_step(): call(functools.partial(rim_body, kind), in_specs=whole_vmem(4), out_specs...  2.19 us
  transfers between devices with their start and end apart: 28, of which 11 were waited for; matrix products, arithmetic and copies ran while one was open for 0% of the time, Pallas kernels for 19%

profile of v14, /device:TPU:0, one launch (start us, length us, event | category | flops | bytes accessed | tf_op | source)
XLA Modules:
  0.0 109.2 jit_solution(12532642119590928430)
XLA Ops:
  5.1 5.5 %collective-permute-start.2 = (bf16[4,8,48,128]{3,2,1,0:T(8,128)(2,1)S(1)}, bf16[4,8,48,128]{3,2,1,0:T(8,128)(2,1)S(1)}, u32[]{:S(2)}, u32[]{:S(2)}) collective-permute-start(bf16[4,8,48,128]{3,2,1,0:T(8,128)(2,1)S(1)} %get-tuple-element.44), channel_id=1, source_target_pairs={{0,4},{4,0},{8,12},{12,8},{1,5},{5,1},{9,13},{13,9},{2,6},{6,2},{1... | collective-permute-start | bytes 1179656 | tf_op jit(solution)/shard_map/ppermute | solution.py:270
  10.7 1.6 %collective-permute-start.10 = (bf16[8,8,32,128]{3,2,1,0:T(8,128)(2,1)S(1)}, bf16[8,8,32,128]{3,2,1,0:T(8,128)(2,1)S(1)}, u32[]{:S(2)}, u32[]{:S(2)}) collective-permute-start(bf16[8,8,32,128]{3,2,1,0:T(8,128)(2,1)S(1)} %shard_map.57), channel_id=1, source_target_pairs={{0,2},{2,0},{1,3},{3,1},{4,6},{6,4},{5,7},{7,5},{8,10},{10,8},{9,1... | collective-permute-start | bytes 1572872 | tf_op jit(solution)/shard_map/ppermute | solution.py:270
  12.2 2.1 %shard_map.51.refs_0_ = f32[8,8,48,128]{3,2,1,0:T(8,128)S(1)} custom-call(f32[8,8,64,128]{3,2,1,0:T(8,128)S(1)} %get-tuple-element.41.refs_0_.refs_5_, bf16[8,4,48,128]{3,2,1,0:T(8,128)(2,1)S(1)} %collective-permute-done.refs_1_, bf16[8,8,48,256]{3,2,1,0:T(8,128)(2,1)S(1)} %copy-done, f32[64,48]{1,0:T(8,128)S(1)} %bitcast.11, f32[4,64,48]{2,1,0:T(8,128)S(1)} %bitcast.5), custom_call_target="tpu_custom_call" | custom-call | flops 1 | bytes 1 | tf_op jit(solution)/shard_map/pallas_call | solution.py:185
  14.4 5.6 %collective-permute-done.2.refs_2_ = bf16[4,8,48,128]{3,2,1,0:T(8,128)(2,1)S(1)} collective-permute-done((bf16[4,8,48,128]{3,2,1,0:T(8,128)(2,1)S(1)}, bf16[4,8,48,128]{3,2,1,0:T(8,128)(2,1)S(1)}, u32[]{:S(2)}, u32[]{:S(2)}) %collective-permute-start.2) | collective-permute-done | bytes 393248 | tf_op jit(solution)/shard_map/ppermute | solution.py:270
  21.9 3.5 %collective-permute-start.5 = (bf16[4,8,48,128]{3,2,1,0:T(8,128)(2,1)S(1)}, bf16[4,8,48,128]{3,2,1,0:T(8,128)(2,1)S(1)}, u32[]{:S(2)}, u32[]{:S(2)}) collective-permute-start(bf16[4,8,48,128]{3,2,1,0:T(8,128)(2,1)S(1)} %get-tuple-element.48), channel_id=1, source_target_pairs={{0,4},{4,0},{8,12},{12,8},{1,5},{5,1},{9,13},{13,9},{2,6},{6,2},{1... | collective-permute-start | bytes 1179656 | tf_op jit(solution)/shard_map/ppermute | solution.py:270
  26.9 3.1 %collective-permute-start.13 = (bf16[4,8,48,128]{3,2,1,0:T(8,128)(2,1)S(1)}, bf16[4,8,48,128]{3,2,1,0:T(8,128)(2,1)S(1)}, u32[]{:S(2)}, u32[]{:S(2)}) collective-permute-start(bf16[4,8,48,128]{3,2,1,0:T(8,128)(2,1)S(1)} %get-tuple-element.59), channel_id=1, source_target_pairs={{0,4},{4,0},{8,12},{12,8},{1,5},{5,1},{9,13},{13,9},{2,6},{6,2},{1... | collective-permute-start | bytes 1179656 | tf_op jit(solution)/shard_map/ppermute | solution.py:270
  30.0 2.2 %shard_map.53.refs_0_ = f32[8,8,48,128]{3,2,1,0:T(8,128)S(1)} custom-call(f32[8,8,64,128]{3,2,1,0:T(8,128)S(1)} %get-tuple-element.45.refs_0_.refs_5_, bf16[8,4,48,128]{3,2,1,0:T(8,128)(2,1)S(1)} %collective-permute-done.3.refs_1_, bf16[8,8,48,256]{3,2,1,0:T(8,128)(2,1)S(1)} %copy-done.1, f32[64,48]{1,0:T(8,128)S(1)} %bitcast.13, f32[4,64,48]{2,1,0:T(8,128)S(1)} %bitcast.6, ...), custom_call_target="tpu_custom_call" | custom-call | flops 1 | bytes 1 | tf_op jit(solution)/shard_map/pallas_call | solution.py:185
  32.2 3.0 %collective-permute-done.5.refs_2_ = bf16[4,8,48,128]{3,2,1,0:T(8,128)(2,1)S(1)} collective-permute-done((bf16[4,8,48,128]{3,2,1,0:T(8,128)(2,1)S(1)}, bf16[4,8,48,128]{3,2,1,0:T(8,128)(2,1)S(1)}, u32[]{:S(2)}, u32[]{:S(2)}) %collective-permute-start.5) | collective-permute-done | bytes 393248 | tf_op jit(solution)/shard_map/ppermute | solution.py:270
  36.5 2.3 %shard_map.59.refs_0_ = f32[8,8,48,128]{3,2,1,0:T(8,128)S(1)} custom-call(f32[8,8,80,128]{3,2,1,0:T(8,128)S(1)} %get-tuple-element.55.refs_0_.refs_5_, bf16[8,4,48,128]{3,2,1,0:T(8,128)(2,1)S(1)} %collective-permute-done.11.refs_1_, bf16[8,8,48,128]{3,2,1,0:T(8,128)(2,1)S(1)} %get-tuple-element.57.refs_2_, f32[64,48]{1,0:T(8,128)S(1)} %bitcast.15, ...), custom_call_target="tpu_custom_call" | custom-call | flops 1 | bytes 1 | tf_op jit(solution)/shard_map/pallas_call | solution.py:455
  38.8 4.5 %collective-permute-done.13.refs_3_ = bf16[4,8,48,128]{3,2,1,0:T(8,128)(2,1)S(1)} collective-permute-done((bf16[4,8,48,128]{3,2,1,0:T(8,128)(2,1)S(1)}, bf16[4,8,48,128]{3,2,1,0:T(8,128)(2,1)S(1)}, u32[]{:S(2)}, u32[]{:S(2)}) %collective-permute-start.13) | collective-permute-done | bytes 393248 | tf_op jit(solution)/shard_map/ppermute | solution.py:270
  44.9 4.6 %collective-permute-start.16 = (bf16[4,8,48,128]{3,2,1,0:T(8,128)(2,1)S(1)}, bf16[4,8,48,128]{3,2,1,0:T(8,128)(2,1)S(1)}, u32[]{:S(2)}, u32[]{:S(2)}) collective-permute-start(bf16[4,8,48,128]{3,2,1,0:T(8,128)(2,1)S(1)} %get-tuple-element.63), channel_id=1, source_target_pairs={{0,4},{4,0},{8,12},{12,8},{1,5},{5,1},{9,13},{13,9},{2,6},{6,2},{1... | collective-permute-start | bytes 1179656 | tf_op jit(solution)/shard_map/ppermute | solution.py:270
  50.2 1.8 %collective-permute-start.8 = (bf16[4,8,48,128]{3,2,1,0:T(8,128)(2,1)S(1)}, bf16[4,8,48,128]{3,2,1,0:T(8,128)(2,1)S(1)}, u32[]{:S(2)}, u32[]{:S(2)}) collective-permute-start(bf16[4,8,48,128]{3,2,1,0:T(8,128)(2,1)S(1)} %get-tuple-element.52), channel_id=1, source_target_pairs={{0,4},{4,0},{8,12},{12,8},{1,5},{5,1},{9,13},{13,9},{2,6},{6,2},{1... | collective-permute-start | bytes 1179656 | tf_op jit(solution)/shard_map/ppermute | solution.py:270
  52.0 1.5 %collective-permute-start.17 = (bf16[8,8,16,128]{3,2,1,0:T(8,128)(2,1)S(1)}, bf16[8,8,16,128]{3,2,1,0:T(8,128)(2,1)S(1)}, u32[]{:S(2)}, u32[]{:S(2)}) collective-permute-start(bf16[8,8,16,128]{3,2,1,0:T(8,128)(2,1)S(1)} %get-tuple-element.64), channel_id=1, source_target_pairs={{0,2},{2,0},{1,3},{3,1},{4,6},{6,4},{5,7},{7,5},{8,10},{10,8},{9,1... | collective-permute-start | bytes 786440 | tf_op jit(solution)/shard_map/ppermute | solution.py:270
  53.5 2.2 %shard_map.55.refs_0_ = f32[8,8,48,128]{3,2,1,0:T(8,128)S(1)} custom-call(f32[8,8,64,128]{3,2,1,0:T(8,128)S(1)} %get-tuple-element.49.refs_0_, bf16[8,4,48,128]{3,2,1,0:T(8,128)(2,1)S(1)} %collective-permute-done.6.refs_1_, bf16[8,8,48,256]{3,2,1,0:T(8,128)(2,1)S(1)} %copy-done.1, f32[64,48]{1,0:T(8,128)S(1)} %bitcast.17, f32[4,64,48]{2,1,0:T(8,128)S(1)} %bitcast.8, ...), custom_call_target="tpu_custom_call" | custom-call | flops 1 | bytes 1 | tf_op jit(solution)/shard_map/pallas_call | solution.py:185
  55.7 2.5 %shard_map.61.refs_0_ = f32[8,8,48,128]{3,2,1,0:T(8,128)S(1)} custom-call(f32[8,8,80,128]{3,2,1,0:T(8,128)S(1)} %get-tuple-element.60.refs_0_.refs_5_, bf16[8,4,48,128]{3,2,1,0:T(8,128)(2,1)S(1)} %collective-permute-done.14.refs_1_, bf16[8,8,48,128]{3,2,1,0:T(8,128)(2,1)S(1)} %get-tuple-element.57.refs_2_, f32[64,48]{1,0:T(8,128)S(1)} %bitcast.18, ...), custom_call_target="tpu_custom_call" | custom-call | flops 1 | bytes 1 | tf_op jit(solution)/shard_map/pallas_call | solution.py:455
  58.2 1.6 %collective-permute-done.17.refs_4_ = bf16[8,8,16,128]{3,2,1,0:T(8,128)(2,1)S(1)} collective-permute-done((bf16[8,8,16,128]{3,2,1,0:T(8,128)(2,1)S(1)}, bf16[8,8,16,128]{3,2,1,0:T(8,128)(2,1)S(1)}, u32[]{:S(2)}, u32[]{:S(2)}) %collective-permute-start.17) | collective-permute-done | bytes 262176 | tf_op jit(solution)/shard_map/ppermute | solution.py:270
  61.1 6.3 %collective-permute-done.8.refs_3_ = bf16[4,8,48,128]{3,2,1,0:T(8,128)(2,1)S(1)} collective-permute-done((bf16[4,8,48,128]{3,2,1,0:T(8,128)(2,1)S(1)}, bf16[4,8,48,128]{3,2,1,0:T(8,128)(2,1)S(1)}, u32[]{:S(2)}, u32[]{:S(2)}) %collective-permute-start.8) | collective-permute-done | bytes 393248 | tf_op jit(solution)/shard_map/ppermute | solution.py:270
  69.1 3.5 %collective-permute-start.20 = (bf16[4,8,48,128]{3,2,1,0:T(8,128)(2,1)S(1)}, bf16[4,8,48,128]{3,2,1,0:T(8,128)(2,1)S(1)}, u32[]{:S(2)}, u32[]{:S(2)}) collective-permute-start(bf16[4,8,48,128]{3,2,1,0:T(8,128)(2,1)S(1)} %get-tuple-element.68), channel_id=1, source_target_pairs={{0,4},{4,0},{8,12},{12,8},{1,5},{5,1},{9,13},{13,9},{2,6},{6,2},{1... | collective-permute-start | bytes 1179656 | tf_op jit(solution)/shard_map/ppermute | solution.py:270
  74.6 2.5 %shard_map.63.refs_0_ = f32[8,8,48,128]{3,2,1,0:T(8,128)S(1)} custom-call(f32[8,8,80,128]{3,2,1,0:T(8,128)S(1)} %get-tuple-element.65.refs_0_, bf16[8,4,48,128]{3,2,1,0:T(8,128)(2,1)S(1)} %collective-permute-done.18.refs_1_, bf16[8,8,48,128]{3,2,1,0:T(8,128)(2,1)S(1)} %get-tuple-element.57.refs_2_, f32[64,48]{1,0:T(8,128)S(1)} %bitcast.21, ...), custom_call_target="tpu_custom_call" | custom-call | flops 1 | bytes 1 | tf_op jit(solution)/shard_map/pallas_call | solution.py:455
  77.0 11.0 %collective-permute-done.21.refs_4_ = bf16[8,8,16,128]{3,2,1,0:T(8,128)(2,1)S(1)} collective-permute-done((bf16[8,8,16,128]{3,2,1,0:T(8,128)(2,1)S(1)}, bf16[8,8,16,128]{3,2,1,0:T(8,128)(2,1)S(1)}, u32[]{:S(2)}, u32[]{:S(2)}) %collective-permute-start.21) | collective-permute-done | bytes 262176 | tf_op jit(solution)/shard_map/ppermute | solution.py:270
  90.5 1.9 %collective-permute-done.22.got_ref = f32[520,256]{1,0:T(8,128)S(1)} collective-permute-done((f32[520,256]{1,0:T(8,128)S(1)}, f32[520,256]{1,0:T(8,128)S(1)}, u32[]{:S(2)}, u32[]{:S(2)}) %collective-permute-start.22) | collective-permute-done | bytes 532512 | tf_op jit(solution)/shard_map/ppermute | solution.py:270
  96.0 4.8 %collective-permute-done.23.refs_0_ = bf16[144,256]{1,0:T(8,128)(2,1)S(1)} collective-permute-done((bf16[144,256]{1,0:T(8,128)(2,1)S(1)}, bf16[144,256]{1,0:T(8,128)(2,1)S(1)}, u32[]{:S(2)}, u32[]{:S(2)}) %collective-permute-start.23) | collective-permute-done | bytes 73760 | tf_op jit(solution)/shard_map/ppermute | solution.py:754
  102.1 1.6 %collective-permute-start.26 = (bf16[144,256]{1,0:T(8,128)(2,1)S(1)}, bf16[144,256]{1,0:T(8,128)(2,1)S(1)}, u32[]{:S(2)}, u32[]{:S(2)}) collective-permute-start(bf16[144,256]{1,0:T(8,128)(2,1)S(1)} %shard_map.67.mine_ref), channel_id=1, source_target_pairs={{0,2},{2,0},{1,3},{3,1},{4,6},{6,4},{5,7},{7,5},{8,10},{10,8},{9,1... | collective-permute-start | bytes 221192 | tf_op jit(solution)/shard_map/ppermute | solution.py:270
  103.7 2.9 %collective-permute-done.26.other_ref = bf16[144,256]{1,0:T(8,128)(2,1)S(1)} collective-permute-done((bf16[144,256]{1,0:T(8,128)(2,1)S(1)}, bf16[144,256]{1,0:T(8,128)(2,1)S(1)}, u32[]{:S(2)}, u32[]{:S(2)}) %collective-permute-start.26) | collective-permute-done | bytes 73760 | tf_op jit(solution)/shard_map/ppermute | solution.py:270
  (61 shorter events, 26.3 us)
Async XLA Ops:
  3.9 8.4 %collective-permute-start = (bf16[8,4,48,128]{3,2,1,0:T(8,128)(2,1)S(1)}, bf16[8,4,48,128]{3,2,1,0:T(8,128)(2,1)S(1)}, u32[]{:S(2)}, u32[]{:S(2)}) collective-permute-start(bf16[8,4,48,128]{3,2,1,0:T(8,128)(2,1)S(1)} %get-tuple-element.42), channel_id=1, source_target_pairs={{0,1},{1,0},{2,3},{3,2},{4,5},{5,4},{6,7},{7,6},{8,9},{9,8},{10,11... | collective-permute-start | bytes 1179656 | tf_op jit(solution)/shard_map/ppermute | solution.py:270
  4.4 10.0 %collective-permute-start.1 = (bf16[4,8,48,128]{3,2,1,0:T(8,128)(2,1)S(1)}, bf16[4,8,48,128]{3,2,1,0:T(8,128)(2,1)S(1)}, u32[]{:S(2)}, u32[]{:S(2)}) collective-permute-start(bf16[4,8,48,128]{3,2,1,0:T(8,128)(2,1)S(1)} %get-tuple-element.43), channel_id=1, source_target_pairs={{4,8},{8,4},{5,9},{9,5},{6,10},{10,6},{7,11},{11,7},{20,24},{24,20... | collective-permute-start | bytes 1179656 | tf_op jit(solution)/shard_map/ppermute | solution.py:270
  5.1 14.9 %collective-permute-start.2 = (bf16[4,8,48,128]{3,2,1,0:T(8,128)(2,1)S(1)}, bf16[4,8,48,128]{3,2,1,0:T(8,128)(2,1)S(1)}, u32[]{:S(2)}, u32[]{:S(2)}) collective-permute-start(bf16[4,8,48,128]{3,2,1,0:T(8,128)(2,1)S(1)} %get-tuple-element.44), channel_id=1, source_target_pairs={{0,4},{4,0},{8,12},{12,8},{1,5},{5,1},{9,13},{13,9},{2,6},{6,2},{1... | collective-permute-start | bytes 1179656 | tf_op jit(solution)/shard_map/ppermute | solution.py:270
  10.7 14.7 %collective-permute-start.10 = (bf16[8,8,32,128]{3,2,1,0:T(8,128)(2,1)S(1)}, bf16[8,8,32,128]{3,2,1,0:T(8,128)(2,1)S(1)}, u32[]{:S(2)}, u32[]{:S(2)}) collective-permute-start(bf16[8,8,32,128]{3,2,1,0:T(8,128)(2,1)S(1)} %shard_map.57), channel_id=1, source_target_pairs={{0,2},{2,0},{1,3},{3,1},{4,6},{6,4},{5,7},{7,5},{8,10},{10,8},{9,1... | collective-permute-start | bytes 1572872 | tf_op jit(solution)/shard_map/ppermute | solution.py:270
  21.2 11.0 %collective-permute-start.4 = (bf16[4,8,48,128]{3,2,1,0:T(8,128)(2,1)S(1)}, bf16[4,8,48,128]{3,2,1,0:T(8,128)(2,1)S(1)}, u32[]{:S(2)}, u32[]{:S(2)}) collective-permute-start(bf16[4,8,48,128]{3,2,1,0:T(8,128)(2,1)S(1)} %get-tuple-element.47), channel_id=1, source_target_pairs={{4,8},{8,4},{5,9},{9,5},{6,10},{10,6},{7,11},{11,7},{20,24},{24,20... | collective-permute-start | bytes 1179656 | tf_op jit(solution)/shard_map/ppermute | solution.py:270
  21.9 13.4 %collective-permute-start.5 = (bf16[4,8,48,128]{3,2,1,0:T(8,128)(2,1)S(1)}, bf16[4,8,48,128]{3,2,1,0:T(8,128)(2,1)S(1)}, u32[]{:S(2)}, u32[]{:S(2)}) collective-permute-start(bf16[4,8,48,128]{3,2,1,0:T(8,128)(2,1)S(1)} %get-tuple-element.48), channel_id=1, source_target_pairs={{0,4},{4,0},{8,12},{12,8},{1,5},{5,1},{9,13},{13,9},{2,6},{6,2},{1... | collective-permute-start | bytes 1179656 | tf_op jit(solution)/shard_map/ppermute | solution.py:270
  26.1 10.3 %collective-permute-start.11 = (bf16[8,4,48,128]{3,2,1,0:T(8,128)(2,1)S(1)}, bf16[8,4,48,128]{3,2,1,0:T(8,128)(2,1)S(1)}, u32[]{:S(2)}, u32[]{:S(2)}) collective-permute-start(bf16[8,4,48,128]{3,2,1,0:T(8,128)(2,1)S(1)} %get-tuple-element.56), channel_id=1, source_target_pairs={{0,1},{1,0},{2,3},{3,2},{4,5},{5,4},{6,7},{7,6},{8,9},{9,8},{10,11... | collective-permute-start | bytes 1179656 | tf_op jit(solution)/shard_map/ppermute | solution.py:270
  26.2 12.6 %collective-permute-start.12 = (bf16[4,8,48,128]{3,2,1,0:T(8,128)(2,1)S(1)}, bf16[4,8,48,128]{3,2,1,0:T(8,128)(2,1)S(1)}, u32[]{:S(2)}, u32[]{:S(2)}) collective-permute-start(bf16[4,8,48,128]{3,2,1,0:T(8,128)(2,1)S(1)} %get-tuple-element.58), channel_id=1, source_target_pairs={{4,8},{8,4},{5,9},{9,5},{6,10},{10,6},{7,11},{11,7},{20,24},{24,20... | collective-permute-start | bytes 1179656 | tf_op jit(solution)/shard_map/ppermute | solution.py:270
  26.9 16.4 %collective-permute-start.13 = (bf16[4,8,48,128]{3,2,1,0:T(8,128)(2,1)S(1)}, bf16[4,8,48,128]{3,2,1,0:T(8,128)(2,1)S(1)}, u32[]{:S(2)}, u32[]{:S(2)}) collective-permute-start(bf16[4,8,48,128]{3,2,1,0:T(8,128)(2,1)S(1)} %get-tuple-element.59), channel_id=1, source_target_pairs={{0,4},{4,0},{8,12},{12,8},{1,5},{5,1},{9,13},{13,9},{2,6},{6,2},{1... | collective-permute-start | bytes 1179656 | tf_op jit(solution)/shard_map/ppermute | solution.py:270
  36.4 13.8 %collective-permute-start.6 = (bf16[8,4,48,128]{3,2,1,0:T(8,128)(2,1)S(1)}, bf16[8,4,48,128]{3,2,1,0:T(8,128)(2,1)S(1)}, u32[]{:S(2)}, u32[]{:S(2)}) collective-permute-start(bf16[8,4,48,128]{3,2,1,0:T(8,128)(2,1)S(1)} %get-tuple-element.50), channel_id=1, source_target_pairs={{0,1},{1,0},{2,3},{3,2},{4,5},{5,4},{6,7},{7,6},{8,9},{9,8},{10,11... | collective-permute-start | bytes 1179656 | tf_op jit(solution)/shard_map/ppermute | solution.py:270
  44.1 7.8 %collective-permute-start.14 = (bf16[8,4,48,128]{3,2,1,0:T(8,128)(2,1)S(1)}, bf16[8,4,48,128]{3,2,1,0:T(8,128)(2,1)S(1)}, u32[]{:S(2)}, u32[]{:S(2)}) collective-permute-start(bf16[8,4,48,128]{3,2,1,0:T(8,128)(2,1)S(1)} %get-tuple-element.61), channel_id=1, source_target_pairs={{0,1},{1,0},{2,3},{3,2},{4,5},{5,4},{6,7},{7,6},{8,9},{9,8},{10,11... | collective-permute-start | bytes 1179656 | tf_op jit(solution)/shard_map/ppermute | solution.py:270
  44.2 15.6 %collective-permute-start.15 = (bf16[4,8,48,128]{3,2,1,0:T(8,128)(2,1)S(1)}, bf16[4,8,48,128]{3,2,1,0:T(8,128)(2,1)S(1)}, u32[]{:S(2)}, u32[]{:S(2)}) collective-permute-start(bf16[4,8,48,128]{3,2,1,0:T(8,128)(2,1)S(1)} %get-tuple-element.62), channel_id=1, source_target_pairs={{4,8},{8,4},{5,9},{9,5},{6,10},{10,6},{7,11},{11,7},{20,24},{24,20... | collective-permute-start | bytes 1179656 | tf_op jit(solution)/shard_map/ppermute | solution.py:270
  44.9 14.9 %collective-permute-start.16 = (bf16[4,8,48,128]{3,2,1,0:T(8,128)(2,1)S(1)}, bf16[4,8,48,128]{3,2,1,0:T(8,128)(2,1)S(1)}, u32[]{:S(2)}, u32[]{:S(2)}) collective-permute-start(bf16[4,8,48,128]{3,2,1,0:T(8,128)(2,1)S(1)} %get-tuple-element.63), channel_id=1, source_target_pairs={{0,4},{4,0},{8,12},{12,8},{1,5},{5,1},{9,13},{13,9},{2,6},{6,2},{1... | collective-permute-start | bytes 1179656 | tf_op jit(solution)/shard_map/ppermute | solution.py:270
  49.5 11.6 %collective-permute-start.7 = (bf16[4,8,48,128]{3,2,1,0:T(8,128)(2,1)S(1)}, bf16[4,8,48,128]{3,2,1,0:T(8,128)(2,1)S(1)}, u32[]{:S(2)}, u32[]{:S(2)}) collective-permute-start(bf16[4,8,48,128]{3,2,1,0:T(8,128)(2,1)S(1)} %get-tuple-element.51), channel_id=1, source_target_pairs={{4,8},{8,4},{5,9},{9,5},{6,10},{10,6},{7,11},{11,7},{20,24},{24,20... | collective-permute-start | bytes 1179656 | tf_op jit(solution)/shard_map/ppermute | solution.py:270
  50.2 17.2 %collective-permute-start.8 = (bf16[4,8,48,128]{3,2,1,0:T(8,128)(2,1)S(1)}, bf16[4,8,48,128]{3,2,1,0:T(8,128)(2,1)S(1)}, u32[]{:S(2)}, u32[]{:S(2)}) collective-permute-start(bf16[4,8,48,128]{3,2,1,0:T(8,128)(2,1)S(1)} %get-tuple-element.52), channel_id=1, source_target_pairs={{0,4},{4,0},{8,12},{12,8},{1,5},{5,1},{9,13},{13,9},{2,6},{6,2},{1... | collective-permute-start | bytes 1179656 | tf_op jit(solution)/shard_map/ppermute | solution.py:270
  52.0 7.9 %collective-permute-start.17 = (bf16[8,8,16,128]{3,2,1,0:T(8,128)(2,1)S(1)}, bf16[8,8,16,128]{3,2,1,0:T(8,128)(2,1)S(1)}, u32[]{:S(2)}, u32[]{:S(2)}) collective-permute-start(bf16[8,8,16,128]{3,2,1,0:T(8,128)(2,1)S(1)} %get-tuple-element.64), channel_id=1, source_target_pairs={{0,2},{2,0},{1,3},{3,1},{4,6},{6,4},{5,7},{7,5},{8,10},{10,8},{9,1... | collective-permute-start | bytes 786440 | tf_op jit(solution)/shard_map/ppermute | solution.py:270
  61.1 13.5 %collective-permute-start.18 = (bf16[8,4,48,128]{3,2,1,0:T(8,128)(2,1)S(1)}, bf16[8,4,48,128]{3,2,1,0:T(8,128)(2,1)S(1)}, u32[]{:S(2)}, u32[]{:S(2)}) collective-permute-start(bf16[8,4,48,128]{3,2,1,0:T(8,128)(2,1)S(1)} %get-tuple-element.66), channel_id=1, source_target_pairs={{0,1},{1,0},{2,3},{3,2},{4,5},{5,4},{6,7},{7,6},{8,9},{9,8},{10,11... | collective-permute-start | bytes 1179656 | tf_op jit(solution)/shard_map/ppermute | solution.py:270
  68.2 19.9 %collective-permute-start.19 = (bf16[4,8,48,128]{3,2,1,0:T(8,128)(2,1)S(1)}, bf16[4,8,48,128]{3,2,1,0:T(8,128)(2,1)S(1)}, u32[]{:S(2)}, u32[]{:S(2)}) collective-permute-start(bf16[4,8,48,128]{3,2,1,0:T(8,128)(2,1)S(1)} %get-tuple-element.67), channel_id=1, source_target_pairs={{4,8},{8,4},{5,9},{9,5},{6,10},{10,6},{7,11},{11,7},{20,24},{24,20... | collective-permute-start | bytes 1179656 | tf_op jit(solution)/shard_map/ppermute | solution.py:270
  69.1 19.0 %collective-permute-start.20 = (bf16[4,8,48,128]{3,2,1,0:T(8,128)(2,1)S(1)}, bf16[4,8,48,128]{3,2,1,0:T(8,128)(2,1)S(1)}, u32[]{:S(2)}, u32[]{:S(2)}) collective-permute-start(bf16[4,8,48,128]{3,2,1,0:T(8,128)(2,1)S(1)} %get-tuple-element.68), channel_id=1, source_target_pairs={{0,4},{4,0},{8,12},{12,8},{1,5},{5,1},{9,13},{13,9},{2,6},{6,2},{1... | collective-permute-start | bytes 1179656 | tf_op jit(solution)/shard_map/ppermute | solution.py:270
  72.5 16.5 %collective-permute-start.9 = (bf16[8,4,48,128]{3,2,1,0:T(8,128)(2,1)S(1)}, bf16[8,4,48,128]{3,2,1,0:T(8,128)(2,1)S(1)}, u32[]{:S(2)}, u32[]{:S(2)}) collective-permute-start(bf16[8,4,48,128]{3,2,1,0:T(8,128)(2,1)S(1)} %get-tuple-element.54), channel_id=1, source_target_pairs={{0,2},{2,0},{1,3},{3,1},{4,6},{6,4},{5,7},{7,5},{8,10},{10,8},{9,1... | collective-permute-start | bytes 1179656 | tf_op jit(solution)/shard_map/ppermute | solution.py:270
  74.0 14.0 %collective-permute-start.21 = (bf16[8,8,16,128]{3,2,1,0:T(8,128)(2,1)S(1)}, bf16[8,8,16,128]{3,2,1,0:T(8,128)(2,1)S(1)}, u32[]{:S(2)}, u32[]{:S(2)}) collective-permute-start(bf16[8,8,16,128]{3,2,1,0:T(8,128)(2,1)S(1)} %get-tuple-element.69), channel_id=1, source_target_pairs={{0,2},{2,0},{1,3},{3,1},{4,6},{6,4},{5,7},{7,5},{8,10},{10,8},{9,1... | collective-permute-start | bytes 786440 | tf_op jit(solution)/shard_map/ppermute | solution.py:270
  92.4 8.4 %collective-permute-start.23 = (bf16[144,256]{1,0:T(8,128)(2,1)S(1)}, bf16[144,256]{1,0:T(8,128)(2,1)S(1)}, u32[]{:S(2)}, u32[]{:S(2)}) collective-permute-start(bf16[144,256]{1,0:T(8,128)(2,1)S(1)} %get-tuple-element.75), channel_id=1, source_target_pairs={{0,8},{4,12},{8,0},{12,4},{1,9},{5,13},{9,1},{13,5},{2,10},{6,14},... | collective-permute-start | bytes 221192 | tf_op jit(solution)/shard_map/ppermute | solution.py:754
  93.8 7.0 %collective-permute-start.24 = (bf16[144,256]{1,0:T(8,128)(2,1)S(1)}, bf16[144,256]{1,0:T(8,128)(2,1)S(1)}, u32[]{:S(2)}, u32[]{:S(2)}) collective-permute-start(bf16[144,256]{1,0:T(8,128)(2,1)S(1)} %get-tuple-element.76), channel_id=1, source_target_pairs={{0,12},{4,8},{8,4},{12,0},{1,13},{5,9},{9,5},{13,1},{2,14},{6,10},... | collective-permute-start | bytes 221192 | tf_op jit(solution)/shard_map/ppermute | solution.py:754
  95.2 6.9 %collective-permute-start.25 = (bf16[144,256]{1,0:T(8,128)(2,1)S(1)}, bf16[144,256]{1,0:T(8,128)(2,1)S(1)}, u32[]{:S(2)}, u32[]{:S(2)}) collective-permute-start(bf16[144,256]{1,0:T(8,128)(2,1)S(1)} %get-tuple-element.77), channel_id=1, source_target_pairs={{0,4},{4,0},{8,12},{12,8},{1,5},{5,1},{9,13},{13,9},{2,6},{6,2},{1... | collective-permute-start | bytes 221192 | tf_op jit(solution)/shard_map/ppermute | solution.py:754
  (8 other events, 44.8 us)

commit v15 on v14

--- a/solution.py
+++ b/solution.py
@@ -28,6 +28,10 @@
     )
 
 
+def unread(arrays):
+    return [pl.BlockSpec(memory_space=pl.ANY)] * len(arrays)
+
+
 def whole_vmem(count):
     return [pl.BlockSpec(memory_space=pltpu.VMEM)] * count
 
@@ -86,7 +90,8 @@
     lax.fori_loop(0, along // TILE, one, 0)
 
 
-def first_body(chunk, p_ref, s_ref, u_ref, odd_ref, even_ref, edge_ref, square, turned_s):
+def first_body(chunk, after, p_ref, s_ref, *refs):
+    u_ref, odd_ref, even_ref, edge_ref, square, turned_s = refs[after:]
     depth, across, padded, _ = u_ref.shape
     along = padded - 2 * EDGE
     core = lax.axis_index("sub")
@@ -115,11 +120,11 @@
     return [pltpu.VMEM((LANES, LANES), F32)] * 2
 
 
-def first_field(probes, chunk, source):
+def first_field(probes, chunk, source, after=()):
     depth, across, along, _ = probes.shape
     return call(
-        functools.partial(first_body, chunk),
-        in_specs=whole_vmem(2),
+        functools.partial(first_body, chunk, len(after)),
+        in_specs=whole_vmem(2) + unread(after),
         out_specs=whole_vmem(4),
         out_shape=[
             shape_of(depth, across, along + 2 * EDGE, F32),
@@ -128,7 +133,7 @@
             shape_of(depth, RADIUS, along, BF16),
         ],
         scratch_shapes=square_scratch(),
-    )(probes, source)
+    )(probes, source, *after)
 
 
 def local_body(chunk, moment, has_previous, *refs):
@@ -191,9 +196,9 @@
     )(*operands)
 
 
-def rim_body(kind, *refs):
+def rim_body(kind, after, *refs):
     base_ref, odd_ref, even_ref, c_ref = refs[:4]
-    outs, (square, turned_c) = refs[4:-2], refs[-2:]
+    outs, (square, turned_c) = refs[4 + after : -2], refs[-2:]
     depth, across, along, _ = base_ref.shape
     core = lax.axis_index("sub")
     even = slab_is_even()
@@ -244,7 +249,7 @@
     tiles(along, tile)
 
 
-def rim_step(base, odds, evens, courant, kind):
+def rim_step(base, odds, evens, courant, kind, after=()):
     depth, across, along, _ = base.shape
     if kind == "middle":
         out_shape = [
@@ -258,12 +263,12 @@
     else:
         out_shape = [shape_of(depth, across, along, BF16)]
     return call(
-        functools.partial(rim_body, kind),
-        in_specs=whole_vmem(4),
+        functools.partial(rim_body, kind, len(after)),
+        in_specs=whole_vmem(4) + unread(after),
         out_specs=whole_vmem(len(out_shape)),
         out_shape=out_shape,
         scratch_shapes=square_scratch(),
-    )(base, odds, evens, courant)
+    )(base, odds, evens, courant, *after)
 
 
 def swap(x, axis, pairs):
@@ -461,10 +466,10 @@
     )(*operands)
 
 
-def wide_rim_body(kind, has_rows, *refs):
+def wide_rim_body(kind, has_rows, after, *refs):
     base_ref, c_ref, odd_ref, even_ref = refs[:4]
     rows_ref = refs[4] if has_rows else None
-    outs = refs[4 + has_rows : -2]
+    outs = refs[4 + has_rows + after : -2]
     square, shifted = refs[-2:]
     depth, across, along, _ = base_ref.shape
     half = along // 2
@@ -552,7 +557,7 @@
             outs[1][z, i] = second
 
 
-def wide_rim(base, courant, odd, even, kind, rows=None):
+def wide_rim(base, courant, odd, even, kind, rows=None, after=()):
     depth, across, along, _ = base.shape
     if kind == "middle":
         edge = shape_of(RADIUS, across, along, BF16)
@@ -569,13 +574,13 @@
     if rows is not None:
         operands.append(rows)
     return call(
-        functools.partial(wide_rim_body, kind, rows is not None),
-        in_specs=whole_vmem(len(operands)),
+        functools.partial(wide_rim_body, kind, rows is not None, len(after)),
+        in_specs=whole_vmem(len(operands)) + unread(after),
         out_specs=whole_vmem(len(out_shape)),
         out_shape=out_shape,
         scratch_shapes=square_scratch()[:1]
         + [pltpu.VMEM((depth, across, 2, 3 * EDGE, LANES), F32)],
-    )(*operands)
+    )(*operands, *after)
 
 
 def gram_body(kept_ref, got_ref, one_ref, two_ref, keep_ref, send_ref, panel):
@@ -818,33 +823,38 @@
 def shared_shards(probes, courant, source, exchange, cell_count):
     steps = source.shape[0]
     first_source = source[:1]
-    got = chip_swap(window_of(probes))
-    u, *edges = first_field(probes, 0, first_source)
+    window = window_of(probes)
+    got = chip_swap(window)
+    u, *edges = first_field(probes, 0, first_source, (window,))
     odd, even, beside = exchange(*edges)
     shared_u, *edges, both = shared_first(probes, got, first_source)
     shared_odd, shared_even, shared_beside = exchange(*edges)
 
     previous = shared_previous = rows = None
+    before = (both,)
     for n in range(1, steps):
         last = n == steps - 1
         base = local_step(u, beside, probes, 0, courant, source, n, previous)
         if last:
-            kept, sent = wide_rim(base, courant, odd, even, "own")
+            kept, sent = wide_rim(base, courant, odd, even, "own", after=before)
             fields = [kept, chip_swap(sent)]
+            before = (kept,)
         else:
             previous = u
-            u, *edges = rim_step(base, odd, even, courant, "middle")
+            u, *edges = rim_step(base, odd, even, courant, "middle", before)
             odd, even, beside = exchange(*edges)
+            before = (edges[-1],)
         base = shared_local(
             shared_u, shared_beside, both, courant, source, n, shared_previous
         )
         if last:
-            fields += wide_rim(base, courant, shared_odd, shared_even, "both", rows)
+            fields += wide_rim(base, courant, shared_odd, shared_even, "both", rows, before)
         else:
             shared_previous = shared_u
             shared_u, *edges, rows = wide_rim(
-                base, courant, shared_odd, shared_even, "middle", rows
+                base, courant, shared_odd, shared_even, "middle", rows, before
             )
+            before = (edges[-1],)
             shared_odd, shared_even, shared_beside = exchange(*edges)
             rows = chip_swap(rows)
     return coupled(fields, cell_count)

time: 109 us -> 102 us (0.936)
  waiting for transfers between devices: 44.2 us -> 33.7 us
  starting transfers between devices: 37.3 us -> 41.3 us
    ppermute x25, waiting for transfers between devices: 38.2 us -> 27.3 us  [swap(): lax.ppermute(x, axis, [p for a, b in pairs for p in ((a, b), (b, a))])]
    ppermute x25, starting transfers between devices: 33.7 us -> 37.7 us  [swap(): lax.ppermute(x, axis, [p for a, b in pairs for p in ((a, b), (b, a))])]
  transfers between devices with their start and end apart: 28 -> 28, of which waited for: 11 -> 9; matrix products, arithmetic and copies ran while one was open for 0% -> 0% of each run, Pallas kernels for 19% -> 21%
where the time goes in v15:
time: 102 us
  starting transfers between devices  41.3 us (40%)
  waiting for transfers between devices  33.7 us (33%)
  Pallas kernels  24.5 us (24%)
  local copies, waits for them, and re-layouts  1.42 us (1%)
    ppermute x25, starting transfers between devices, swap(): lax.ppermute(x, axis, [p for a, b in pairs for p in ((a, b), (b, a))])  37.7 us
    ppermute x25, waiting for transfers between devices, swap(): lax.ppermute(x, axis, [p for a, b in pairs for p in ((a, b), (b, a))])  27.3 us
    pallas_call x3, Pallas kernels, shared_local(): call(functools.partial(shared_local_body, moment, previous is not None),...  7.27 us
    pallas_call x3, Pallas kernels, local_step(): call(functools.partial(local_body, chunk, moment, previous is not None),...  6.64 us
    ppermute x3, waiting for transfers between devices, coupled(): lax.ppermute(blocks[d - 1], 'slab', [(i, i ^ d) for i in range(slabs)])  6.32 us
    pallas_call x4, Pallas kernels, wide_rim(): call(functools.partial(wide_rim_body, kind, rows is not None, len(after))...  3.81 us
    ppermute x3, starting transfers between devices, coupled(): lax.ppermute(blocks[d - 1], 'slab', [(i, i ^ d) for i in range(slabs)])  3.55 us
    pallas_call x2, Pallas kernels, rim_step(): call(functools.partial(rim_body, kind, len(after)), in_specs=whole_vmem(4...  2.2 us
  transfers between devices with their start and end apart: 28, of which 9 were waited for; matrix products, arithmetic and copies ran while one was open for 0% of the time, Pallas kernels for 21%

profile of v15, /device:TPU:0, one launch (start us, length us, event | category | flops | bytes accessed | tf_op | source)
XLA Modules:
  0.0 101.9 jit_solution(6319601570433501827)
XLA Ops:
  2.2 3.0 %collective-permute-start.3 = (bf16[8,8,32,128]{3,2,1,0:T(8,128)(2,1)S(1)}, bf16[8,8,32,128]{3,2,1,0:T(8,128)(2,1)S(1)}, u32[]{:S(2)}, u32[]{:S(2)}) collective-permute-start(bf16[8,8,32,128]{3,2,1,0:T(8,128)(2,1)S(1)} %shard_map.50.refs_0_), channel_id=1, source_target_pairs={{0,2},{2,0},{1,3},{3,1},{4,6},{6,4},{5,7},{7,5},{8,10},{10,8},{9,1... | collective-permute-start | bytes 1572872 | tf_op jit(solution)/shard_map/ppermute | solution.py:275
  7.0 4.4 %collective-permute-start.2 = (bf16[4,8,48,128]{3,2,1,0:T(8,128)(2,1)S(1)}, bf16[4,8,48,128]{3,2,1,0:T(8,128)(2,1)S(1)}, u32[]{:S(2)}, u32[]{:S(2)}) collective-permute-start(bf16[4,8,48,128]{3,2,1,0:T(8,128)(2,1)S(1)} %get-tuple-element.44), channel_id=1, source_target_pairs={{0,4},{4,0},{8,12},{12,8},{1,5},{5,1},{9,13},{13,9},{2,6},{6,2},{1... | collective-permute-start | bytes 1179656 | tf_op jit(solution)/shard_map/ppermute | solution.py:275
  11.5 5.6 %collective-permute-done.3.got_ref = bf16[8,8,32,128]{3,2,1,0:T(8,128)(2,1)S(1)} collective-permute-done((bf16[8,8,32,128]{3,2,1,0:T(8,128)(2,1)S(1)}, bf16[8,8,32,128]{3,2,1,0:T(8,128)(2,1)S(1)}, u32[]{:S(2)}, u32[]{:S(2)}) %collective-permute-start.3) | collective-permute-done | bytes 524320 | tf_op jit(solution)/shard_map/ppermute | solution.py:275
  18.6 4.7 %collective-permute-start.9 = (bf16[4,8,48,128]{3,2,1,0:T(8,128)(2,1)S(1)}, bf16[4,8,48,128]{3,2,1,0:T(8,128)(2,1)S(1)}, u32[]{:S(2)}, u32[]{:S(2)}) collective-permute-start(bf16[4,8,48,128]{3,2,1,0:T(8,128)(2,1)S(1)} %get-tuple-element.53), channel_id=1, source_target_pairs={{0,4},{4,0},{8,12},{12,8},{1,5},{5,1},{9,13},{13,9},{2,6},{6,2},{1... | collective-permute-start | bytes 1179656 | tf_op jit(solution)/shard_map/ppermute | solution.py:275
  23.3 2.1 %shard_map.52.refs_0_ = f32[8,8,48,128]{3,2,1,0:T(8,128)S(1)} custom-call(f32[8,8,64,128]{3,2,1,0:T(8,128)S(1)} %get-tuple-element.41.refs_0_.refs_5_, bf16[8,4,48,128]{3,2,1,0:T(8,128)(2,1)S(1)} %collective-permute-done.refs_1_, bf16[8,8,48,256]{3,2,1,0:T(8,128)(2,1)S(1)} %copy-done, f32[64,48]{1,0:T(8,128)S(1)} %bitcast.11, f32[4,64,48]{2,1,0:T(8,128)S(1)} %bitcast.5), custom_call_target="tpu_custom_call" | custom-call | flops 1 | bytes 1 | tf_op jit(solution)/shard_map/pallas_call | solution.py:190
  27.4 1.8 %collective-permute-start.6 = (bf16[4,8,48,128]{3,2,1,0:T(8,128)(2,1)S(1)}, bf16[4,8,48,128]{3,2,1,0:T(8,128)(2,1)S(1)}, u32[]{:S(2)}, u32[]{:S(2)}) collective-permute-start(bf16[4,8,48,128]{3,2,1,0:T(8,128)(2,1)S(1)} %get-tuple-element.49), channel_id=1, source_target_pairs={{0,4},{4,0},{8,12},{12,8},{1,5},{5,1},{9,13},{13,9},{2,6},{6,2},{1... | collective-permute-start | bytes 1179656 | tf_op jit(solution)/shard_map/ppermute | solution.py:275
  29.2 2.3 %shard_map.56.refs_0_ = f32[8,8,48,128]{3,2,1,0:T(8,128)S(1)} custom-call(f32[8,8,80,128]{3,2,1,0:T(8,128)S(1)} %get-tuple-element.50.refs_0_.refs_5_, bf16[8,4,48,128]{3,2,1,0:T(8,128)(2,1)S(1)} %collective-permute-done.7.refs_1_, bf16[8,8,48,128]{3,2,1,0:T(8,128)(2,1)S(1)} %get-tuple-element.45.refs_4_.refs_2_, f32[64,48]{1,0:T(8,128)S(1)} %bitcast.13, ...), custom_call_target="tpu_custom_call" | custom-call | flops 1 | bytes 1 | tf_op jit(solution)/shard_map/pallas_call | solution.py:460
  31.5 1.7 %collective-permute-done.9.refs_3_ = bf16[4,8,48,128]{3,2,1,0:T(8,128)(2,1)S(1)} collective-permute-done((bf16[4,8,48,128]{3,2,1,0:T(8,128)(2,1)S(1)}, bf16[4,8,48,128]{3,2,1,0:T(8,128)(2,1)S(1)}, u32[]{:S(2)}, u32[]{:S(2)}) %collective-permute-start.9) | collective-permute-done | bytes 393248 | tf_op jit(solution)/shard_map/ppermute | solution.py:275
  34.2 1.6 %collective-permute-start.16 = (bf16[8,8,16,128]{3,2,1,0:T(8,128)(2,1)S(1)}, bf16[8,8,16,128]{3,2,1,0:T(8,128)(2,1)S(1)}, u32[]{:S(2)}, u32[]{:S(2)}) collective-permute-start(bf16[8,8,16,128]{3,2,1,0:T(8,128)(2,1)S(1)} %get-tuple-element.62), channel_id=1, source_target_pairs={{0,2},{2,0},{1,3},{3,1},{4,6},{6,4},{5,7},{7,5},{8,10},{10,8},{9,1... | collective-permute-start | bytes 786440 | tf_op jit(solution)/shard_map/ppermute | solution.py:275
  36.4 8.7 %collective-permute-start.15 = (bf16[4,8,48,128]{3,2,1,0:T(8,128)(2,1)S(1)}, bf16[4,8,48,128]{3,2,1,0:T(8,128)(2,1)S(1)}, u32[]{:S(2)}, u32[]{:S(2)}) collective-permute-start(bf16[4,8,48,128]{3,2,1,0:T(8,128)(2,1)S(1)} %get-tuple-element.61), channel_id=1, source_target_pairs={{0,4},{4,0},{8,12},{12,8},{1,5},{5,1},{9,13},{13,9},{2,6},{6,2},{1... | collective-permute-start | bytes 1179656 | tf_op jit(solution)/shard_map/ppermute | solution.py:275
  45.1 2.2 %shard_map.55.refs_0_ = f32[8,8,48,128]{3,2,1,0:T(8,128)S(1)} custom-call(f32[8,8,64,128]{3,2,1,0:T(8,128)S(1)} %get-tuple-element.46.refs_0_.refs_5_, bf16[8,4,48,128]{3,2,1,0:T(8,128)(2,1)S(1)} %collective-permute-done.4.refs_1_, bf16[8,8,48,256]{3,2,1,0:T(8,128)(2,1)S(1)} %copy-done.1, f32[64,48]{1,0:T(8,128)S(1)} %bitcast.15, f32[4,64,48]{2,1,0:T(8,128)S(1)} %bitcast.7, ...), custom_call_target="tpu_custom_call" | custom-call | flops 1 | bytes 1 | tf_op jit(solution)/shard_map/pallas_call | solution.py:190
  49.3 1.8 %collective-permute-start.12 = (bf16[4,8,48,128]{3,2,1,0:T(8,128)(2,1)S(1)}, bf16[4,8,48,128]{3,2,1,0:T(8,128)(2,1)S(1)}, u32[]{:S(2)}, u32[]{:S(2)}) collective-permute-start(bf16[4,8,48,128]{3,2,1,0:T(8,128)(2,1)S(1)} %get-tuple-element.58), channel_id=1, source_target_pairs={{0,4},{4,0},{8,12},{12,8},{1,5},{5,1},{9,13},{13,9},{2,6},{6,2},{1... | collective-permute-start | bytes 1179656 | tf_op jit(solution)/shard_map/ppermute | solution.py:275
  51.1 2.5 %shard_map.60.refs_0_ = f32[8,8,48,128]{3,2,1,0:T(8,128)S(1)} custom-call(f32[8,8,80,128]{3,2,1,0:T(8,128)S(1)} %get-tuple-element.59.refs_0_.refs_5_, bf16[8,4,48,128]{3,2,1,0:T(8,128)(2,1)S(1)} %collective-permute-done.13.refs_1_, bf16[8,8,48,128]{3,2,1,0:T(8,128)(2,1)S(1)} %get-tuple-element.45.refs_4_.refs_2_, f32[64,48]{1,0:T(8,128)S(1)} %bitcast.17, ...), custom_call_target="tpu_custom_call" | custom-call | flops 1 | bytes 1 | tf_op jit(solution)/shard_map/pallas_call | solution.py:460
  53.6 1.6 %collective-permute-done.15.refs_3_ = bf16[4,8,48,128]{3,2,1,0:T(8,128)(2,1)S(1)} collective-permute-done((bf16[4,8,48,128]{3,2,1,0:T(8,128)(2,1)S(1)}, bf16[4,8,48,128]{3,2,1,0:T(8,128)(2,1)S(1)}, u32[]{:S(2)}, u32[]{:S(2)}) %collective-permute-start.15) | collective-permute-done | bytes 393248 | tf_op jit(solution)/shard_map/ppermute | solution.py:275
  57.3 3.4 %collective-permute-start.20 = (bf16[4,8,48,128]{3,2,1,0:T(8,128)(2,1)S(1)}, bf16[4,8,48,128]{3,2,1,0:T(8,128)(2,1)S(1)}, u32[]{:S(2)}, u32[]{:S(2)}) collective-permute-start(bf16[4,8,48,128]{3,2,1,0:T(8,128)(2,1)S(1)} %get-tuple-element.68), channel_id=1, source_target_pairs={{0,4},{4,0},{8,12},{12,8},{1,5},{5,1},{9,13},{13,9},{2,6},{6,2},{1... | collective-permute-start | bytes 1179656 | tf_op jit(solution)/shard_map/ppermute | solution.py:275
  60.7 2.2 %shard_map.59.refs_0_ = f32[8,8,48,128]{3,2,1,0:T(8,128)S(1)} custom-call(f32[8,8,64,128]{3,2,1,0:T(8,128)S(1)} %get-tuple-element.55.refs_0_, bf16[8,4,48,128]{3,2,1,0:T(8,128)(2,1)S(1)} %collective-permute-done.10.refs_1_, bf16[8,8,48,256]{3,2,1,0:T(8,128)(2,1)S(1)} %copy-done.1, f32[64,48]{1,0:T(8,128)S(1)} %bitcast.19, f32[4,64,48]{2,1,0:T(8,128)S(1)} %bitcast.9, ...), custom_call_target="tpu_custom_call" | custom-call | flops 1 | bytes 1 | tf_op jit(solution)/shard_map/pallas_call | solution.py:190
  63.7 1.6 %collective-permute-start.17 = (bf16[8,4,48,128]{3,2,1,0:T(8,128)(2,1)S(1)}, bf16[8,4,48,128]{3,2,1,0:T(8,128)(2,1)S(1)}, u32[]{:S(2)}, u32[]{:S(2)}) collective-permute-start(bf16[8,4,48,128]{3,2,1,0:T(8,128)(2,1)S(1)} %get-tuple-element.65), channel_id=1, source_target_pairs={{0,2},{2,0},{1,3},{3,1},{4,6},{6,4},{5,7},{7,5},{8,10},{10,8},{9,1... | collective-permute-start | bytes 1179656 | tf_op jit(solution)/shard_map/ppermute | solution.py:275
  65.8 2.5 %shard_map.63.refs_0_ = f32[8,8,48,128]{3,2,1,0:T(8,128)S(1)} custom-call(f32[8,8,80,128]{3,2,1,0:T(8,128)S(1)} %get-tuple-element.66.refs_0_, bf16[8,4,48,128]{3,2,1,0:T(8,128)(2,1)S(1)} %collective-permute-done.18.refs_1_, bf16[8,8,48,128]{3,2,1,0:T(8,128)(2,1)S(1)} %get-tuple-element.45.refs_4_.refs_2_, f32[64,48]{1,0:T(8,128)S(1)} %bitcast.21, ...), custom_call_target="tpu_custom_call" | custom-call | flops 1 | bytes 1 | tf_op jit(solution)/shard_map/pallas_call | solution.py:460
  68.3 12.3 %collective-permute-done.21.refs_4_ = bf16[8,8,16,128]{3,2,1,0:T(8,128)(2,1)S(1)} collective-permute-done((bf16[8,8,16,128]{3,2,1,0:T(8,128)(2,1)S(1)}, bf16[8,8,16,128]{3,2,1,0:T(8,128)(2,1)S(1)}, u32[]{:S(2)}, u32[]{:S(2)}) %collective-permute-start.21) | collective-permute-done | bytes 262176 | tf_op jit(solution)/shard_map/ppermute | solution.py:275
  83.0 1.9 %collective-permute-done.22.got_ref = f32[520,256]{1,0:T(8,128)S(1)} collective-permute-done((f32[520,256]{1,0:T(8,128)S(1)}, f32[520,256]{1,0:T(8,128)S(1)}, u32[]{:S(2)}, u32[]{:S(2)}) %collective-permute-start.22) | collective-permute-done | bytes 532512 | tf_op jit(solution)/shard_map/ppermute | solution.py:275
  85.0 1.8 %collective-permute-start.23 = (bf16[144,256]{1,0:T(8,128)(2,1)S(1)}, bf16[144,256]{1,0:T(8,128)(2,1)S(1)}, u32[]{:S(2)}, u32[]{:S(2)}) collective-permute-start(bf16[144,256]{1,0:T(8,128)(2,1)S(1)} %get-tuple-element.75), channel_id=1, source_target_pairs={{0,8},{4,12},{8,0},{12,4},{1,9},{5,13},{9,1},{13,5},{2,10},{6,14},... | collective-permute-start | bytes 221192 | tf_op jit(solution)/shard_map/ppermute | solution.py:759
  88.5 5.3 %collective-permute-done.23.refs_0_ = bf16[144,256]{1,0:T(8,128)(2,1)S(1)} collective-permute-done((bf16[144,256]{1,0:T(8,128)(2,1)S(1)}, bf16[144,256]{1,0:T(8,128)(2,1)S(1)}, u32[]{:S(2)}, u32[]{:S(2)}) %collective-permute-start.23) | collective-permute-done | bytes 73760 | tf_op jit(solution)/shard_map/ppermute | solution.py:759
  94.9 1.6 %collective-permute-start.26 = (bf16[144,256]{1,0:T(8,128)(2,1)S(1)}, bf16[144,256]{1,0:T(8,128)(2,1)S(1)}, u32[]{:S(2)}, u32[]{:S(2)}) collective-permute-start(bf16[144,256]{1,0:T(8,128)(2,1)S(1)} %shard_map.67.mine_ref), channel_id=1, source_target_pairs={{0,2},{2,0},{1,3},{3,1},{4,6},{6,4},{5,7},{7,5},{8,10},{10,8},{9,1... | collective-permute-start | bytes 221192 | tf_op jit(solution)/shard_map/ppermute | solution.py:275
  96.5 2.8 %collective-permute-done.26.other_ref = bf16[144,256]{1,0:T(8,128)(2,1)S(1)} collective-permute-done((bf16[144,256]{1,0:T(8,128)(2,1)S(1)}, bf16[144,256]{1,0:T(8,128)(2,1)S(1)}, u32[]{:S(2)}, u32[]{:S(2)}) %collective-permute-start.26) | collective-permute-done | bytes 73760 | tf_op jit(solution)/shard_map/ppermute | solution.py:275
  (61 shorter events, 21.6 us)
Async XLA Ops:
  2.2 14.9 %collective-permute-start.3 = (bf16[8,8,32,128]{3,2,1,0:T(8,128)(2,1)S(1)}, bf16[8,8,32,128]{3,2,1,0:T(8,128)(2,1)S(1)}, u32[]{:S(2)}, u32[]{:S(2)}) collective-permute-start(bf16[8,8,32,128]{3,2,1,0:T(8,128)(2,1)S(1)} %shard_map.50.refs_0_), channel_id=1, source_target_pairs={{0,2},{2,0},{1,3},{3,1},{4,6},{6,4},{5,7},{7,5},{8,10},{10,8},{9,1... | collective-permute-start | bytes 1572872 | tf_op jit(solution)/shard_map/ppermute | solution.py:275
  6.3 12.4 %collective-permute-start = (bf16[8,4,48,128]{3,2,1,0:T(8,128)(2,1)S(1)}, bf16[8,4,48,128]{3,2,1,0:T(8,128)(2,1)S(1)}, u32[]{:S(2)}, u32[]{:S(2)}) collective-permute-start(bf16[8,4,48,128]{3,2,1,0:T(8,128)(2,1)S(1)} %get-tuple-element.42), channel_id=1, source_target_pairs={{0,1},{1,0},{2,3},{3,2},{4,5},{5,4},{6,7},{7,6},{8,9},{9,8},{10,11... | collective-permute-start | bytes 1179656 | tf_op jit(solution)/shard_map/ppermute | solution.py:275
  6.3 19.1 %collective-permute-start.1 = (bf16[4,8,48,128]{3,2,1,0:T(8,128)(2,1)S(1)}, bf16[4,8,48,128]{3,2,1,0:T(8,128)(2,1)S(1)}, u32[]{:S(2)}, u32[]{:S(2)}) collective-permute-start(bf16[4,8,48,128]{3,2,1,0:T(8,128)(2,1)S(1)} %get-tuple-element.43), channel_id=1, source_target_pairs={{4,8},{8,4},{5,9},{9,5},{6,10},{10,6},{7,11},{11,7},{20,24},{24,20... | collective-permute-start | bytes 1179656 | tf_op jit(solution)/shard_map/ppermute | solution.py:275
  7.0 18.5 %collective-permute-start.2 = (bf16[4,8,48,128]{3,2,1,0:T(8,128)(2,1)S(1)}, bf16[4,8,48,128]{3,2,1,0:T(8,128)(2,1)S(1)}, u32[]{:S(2)}, u32[]{:S(2)}) collective-permute-start(bf16[4,8,48,128]{3,2,1,0:T(8,128)(2,1)S(1)} %get-tuple-element.44), channel_id=1, source_target_pairs={{0,4},{4,0},{8,12},{12,8},{1,5},{5,1},{9,13},{13,9},{2,6},{6,2},{1... | collective-permute-start | bytes 1179656 | tf_op jit(solution)/shard_map/ppermute | solution.py:275
  17.9 9.5 %collective-permute-start.7 = (bf16[8,4,48,128]{3,2,1,0:T(8,128)(2,1)S(1)}, bf16[8,4,48,128]{3,2,1,0:T(8,128)(2,1)S(1)}, u32[]{:S(2)}, u32[]{:S(2)}) collective-permute-start(bf16[8,4,48,128]{3,2,1,0:T(8,128)(2,1)S(1)} %get-tuple-element.51), channel_id=1, source_target_pairs={{0,1},{1,0},{2,3},{3,2},{4,5},{5,4},{6,7},{7,6},{8,9},{9,8},{10,11... | collective-permute-start | bytes 1179656 | tf_op jit(solution)/shard_map/ppermute | solution.py:275
  17.9 13.6 %collective-permute-start.8 = (bf16[4,8,48,128]{3,2,1,0:T(8,128)(2,1)S(1)}, bf16[4,8,48,128]{3,2,1,0:T(8,128)(2,1)S(1)}, u32[]{:S(2)}, u32[]{:S(2)}) collective-permute-start(bf16[4,8,48,128]{3,2,1,0:T(8,128)(2,1)S(1)} %get-tuple-element.52), channel_id=1, source_target_pairs={{4,8},{8,4},{5,9},{9,5},{6,10},{10,6},{7,11},{11,7},{20,24},{24,20... | collective-permute-start | bytes 1179656 | tf_op jit(solution)/shard_map/ppermute | solution.py:275
  18.6 14.6 %collective-permute-start.9 = (bf16[4,8,48,128]{3,2,1,0:T(8,128)(2,1)S(1)}, bf16[4,8,48,128]{3,2,1,0:T(8,128)(2,1)S(1)}, u32[]{:S(2)}, u32[]{:S(2)}) collective-permute-start(bf16[4,8,48,128]{3,2,1,0:T(8,128)(2,1)S(1)} %get-tuple-element.53), channel_id=1, source_target_pairs={{0,4},{4,0},{8,12},{12,8},{1,5},{5,1},{9,13},{13,9},{2,6},{6,2},{1... | collective-permute-start | bytes 1179656 | tf_op jit(solution)/shard_map/ppermute | solution.py:275
  26.6 9.1 %collective-permute-start.5 = (bf16[4,8,48,128]{3,2,1,0:T(8,128)(2,1)S(1)}, bf16[4,8,48,128]{3,2,1,0:T(8,128)(2,1)S(1)}, u32[]{:S(2)}, u32[]{:S(2)}) collective-permute-start(bf16[4,8,48,128]{3,2,1,0:T(8,128)(2,1)S(1)} %get-tuple-element.48), channel_id=1, source_target_pairs={{4,8},{8,4},{5,9},{9,5},{6,10},{10,6},{7,11},{11,7},{20,24},{24,20... | collective-permute-start | bytes 1179656 | tf_op jit(solution)/shard_map/ppermute | solution.py:275
  27.3 9.1 %collective-permute-start.4 = (bf16[8,4,48,128]{3,2,1,0:T(8,128)(2,1)S(1)}, bf16[8,4,48,128]{3,2,1,0:T(8,128)(2,1)S(1)}, u32[]{:S(2)}, u32[]{:S(2)}) collective-permute-start(bf16[8,4,48,128]{3,2,1,0:T(8,128)(2,1)S(1)} %get-tuple-element.47.refs_4_), channel_id=1, source_target_pairs={{0,1},{1,0},{2,3},{3,2},{4,5},{5,4},{6,7},{7,6},{8,9},{9,8},{10,11... | collective-permute-start | bytes 1179656 | tf_op jit(solution)/shard_map/ppermute | solution.py:275
  27.4 20.0 %collective-permute-start.6 = (bf16[4,8,48,128]{3,2,1,0:T(8,128)(2,1)S(1)}, bf16[4,8,48,128]{3,2,1,0:T(8,128)(2,1)S(1)}, u32[]{:S(2)}, u32[]{:S(2)}) collective-permute-start(bf16[4,8,48,128]{3,2,1,0:T(8,128)(2,1)S(1)} %get-tuple-element.49), channel_id=1, source_target_pairs={{0,4},{4,0},{8,12},{12,8},{1,5},{5,1},{9,13},{13,9},{2,6},{6,2},{1... | collective-permute-start | bytes 1179656 | tf_op jit(solution)/shard_map/ppermute | solution.py:275
  34.1 15.2 %collective-permute-start.13 = (bf16[8,4,48,128]{3,2,1,0:T(8,128)(2,1)S(1)}, bf16[8,4,48,128]{3,2,1,0:T(8,128)(2,1)S(1)}, u32[]{:S(2)}, u32[]{:S(2)}) collective-permute-start(bf16[8,4,48,128]{3,2,1,0:T(8,128)(2,1)S(1)} %get-tuple-element.54.refs_4_), channel_id=1, source_target_pairs={{0,1},{1,0},{2,3},{3,2},{4,5},{5,4},{6,7},{7,6},{8,9},{9,8},{10,11... | collective-permute-start | bytes 1179656 | tf_op jit(solution)/shard_map/ppermute | solution.py:275
  34.2 14.5 %collective-permute-start.16 = (bf16[8,8,16,128]{3,2,1,0:T(8,128)(2,1)S(1)}, bf16[8,8,16,128]{3,2,1,0:T(8,128)(2,1)S(1)}, u32[]{:S(2)}, u32[]{:S(2)}) collective-permute-start(bf16[8,8,16,128]{3,2,1,0:T(8,128)(2,1)S(1)} %get-tuple-element.62), channel_id=1, source_target_pairs={{0,2},{2,0},{1,3},{3,1},{4,6},{6,4},{5,7},{7,5},{8,10},{10,8},{9,1... | collective-permute-start | bytes 786440 | tf_op jit(solution)/shard_map/ppermute | solution.py:275
  35.7 17.8 %collective-permute-start.14 = (bf16[4,8,48,128]{3,2,1,0:T(8,128)(2,1)S(1)}, bf16[4,8,48,128]{3,2,1,0:T(8,128)(2,1)S(1)}, u32[]{:S(2)}, u32[]{:S(2)}) collective-permute-start(bf16[4,8,48,128]{3,2,1,0:T(8,128)(2,1)S(1)} %get-tuple-element.60), channel_id=1, source_target_pairs={{4,8},{8,4},{5,9},{9,5},{6,10},{10,6},{7,11},{11,7},{20,24},{24,20... | collective-permute-start | bytes 1179656 | tf_op jit(solution)/shard_map/ppermute | solution.py:275
  36.4 18.7 %collective-permute-start.15 = (bf16[4,8,48,128]{3,2,1,0:T(8,128)(2,1)S(1)}, bf16[4,8,48,128]{3,2,1,0:T(8,128)(2,1)S(1)}, u32[]{:S(2)}, u32[]{:S(2)}) collective-permute-start(bf16[4,8,48,128]{3,2,1,0:T(8,128)(2,1)S(1)} %get-tuple-element.61), channel_id=1, source_target_pairs={{0,4},{4,0},{8,12},{12,8},{1,5},{5,1},{9,13},{13,9},{2,6},{6,2},{1... | collective-permute-start | bytes 1179656 | tf_op jit(solution)/shard_map/ppermute | solution.py:275
  48.5 8.8 %collective-permute-start.10 = (bf16[8,4,48,128]{3,2,1,0:T(8,128)(2,1)S(1)}, bf16[8,4,48,128]{3,2,1,0:T(8,128)(2,1)S(1)}, u32[]{:S(2)}, u32[]{:S(2)}) collective-permute-start(bf16[8,4,48,128]{3,2,1,0:T(8,128)(2,1)S(1)} %get-tuple-element.56.refs_5_), channel_id=1, source_target_pairs={{0,1},{1,0},{2,3},{3,2},{4,5},{5,4},{6,7},{7,6},{8,9},{9,8},{10,11... | collective-permute-start | bytes 1179656 | tf_op jit(solution)/shard_map/ppermute | solution.py:275
  48.6 14.3 %collective-permute-start.11 = (bf16[4,8,48,128]{3,2,1,0:T(8,128)(2,1)S(1)}, bf16[4,8,48,128]{3,2,1,0:T(8,128)(2,1)S(1)}, u32[]{:S(2)}, u32[]{:S(2)}) collective-permute-start(bf16[4,8,48,128]{3,2,1,0:T(8,128)(2,1)S(1)} %get-tuple-element.57), channel_id=1, source_target_pairs={{4,8},{8,4},{5,9},{9,5},{6,10},{10,6},{7,11},{11,7},{20,24},{24,20... | collective-permute-start | bytes 1179656 | tf_op jit(solution)/shard_map/ppermute | solution.py:275
  49.3 13.6 %collective-permute-start.12 = (bf16[4,8,48,128]{3,2,1,0:T(8,128)(2,1)S(1)}, bf16[4,8,48,128]{3,2,1,0:T(8,128)(2,1)S(1)}, u32[]{:S(2)}, u32[]{:S(2)}) collective-permute-start(bf16[4,8,48,128]{3,2,1,0:T(8,128)(2,1)S(1)} %get-tuple-element.58), channel_id=1, source_target_pairs={{0,4},{4,0},{8,12},{12,8},{1,5},{5,1},{9,13},{13,9},{2,6},{6,2},{1... | collective-permute-start | bytes 1179656 | tf_op jit(solution)/shard_map/ppermute | solution.py:275
  56.4 24.2 %collective-permute-start.19 = (bf16[4,8,48,128]{3,2,1,0:T(8,128)(2,1)S(1)}, bf16[4,8,48,128]{3,2,1,0:T(8,128)(2,1)S(1)}, u32[]{:S(2)}, u32[]{:S(2)}) collective-permute-start(bf16[4,8,48,128]{3,2,1,0:T(8,128)(2,1)S(1)} %get-tuple-element.67), channel_id=1, source_target_pairs={{4,8},{8,4},{5,9},{9,5},{6,10},{10,6},{7,11},{11,7},{20,24},{24,20... | collective-permute-start | bytes 1179656 | tf_op jit(solution)/shard_map/ppermute | solution.py:275
  57.2 8.6 %collective-permute-start.18 = (bf16[8,4,48,128]{3,2,1,0:T(8,128)(2,1)S(1)}, bf16[8,4,48,128]{3,2,1,0:T(8,128)(2,1)S(1)}, u32[]{:S(2)}, u32[]{:S(2)}) collective-permute-start(bf16[8,4,48,128]{3,2,1,0:T(8,128)(2,1)S(1)} %get-tuple-element.63.refs_4_), channel_id=1, source_target_pairs={{0,1},{1,0},{2,3},{3,2},{4,5},{5,4},{6,7},{7,6},{8,9},{9,8},{10,11... | collective-permute-start | bytes 1179656 | tf_op jit(solution)/shard_map/ppermute | solution.py:275
  57.3 23.3 %collective-permute-start.20 = (bf16[4,8,48,128]{3,2,1,0:T(8,128)(2,1)S(1)}, bf16[4,8,48,128]{3,2,1,0:T(8,128)(2,1)S(1)}, u32[]{:S(2)}, u32[]{:S(2)}) collective-permute-start(bf16[4,8,48,128]{3,2,1,0:T(8,128)(2,1)S(1)} %get-tuple-element.68), channel_id=1, source_target_pairs={{0,4},{4,0},{8,12},{12,8},{1,5},{5,1},{9,13},{13,9},{2,6},{6,2},{1... | collective-permute-start | bytes 1179656 | tf_op jit(solution)/shard_map/ppermute | solution.py:275
  63.7 17.9 %collective-permute-start.17 = (bf16[8,4,48,128]{3,2,1,0:T(8,128)(2,1)S(1)}, bf16[8,4,48,128]{3,2,1,0:T(8,128)(2,1)S(1)}, u32[]{:S(2)}, u32[]{:S(2)}) collective-permute-start(bf16[8,4,48,128]{3,2,1,0:T(8,128)(2,1)S(1)} %get-tuple-element.65), channel_id=1, source_target_pairs={{0,2},{2,0},{1,3},{3,1},{4,6},{6,4},{5,7},{7,5},{8,10},{10,8},{9,1... | collective-permute-start | bytes 1179656 | tf_op jit(solution)/shard_map/ppermute | solution.py:275
  65.3 15.3 %collective-permute-start.21 = (bf16[8,8,16,128]{3,2,1,0:T(8,128)(2,1)S(1)}, bf16[8,8,16,128]{3,2,1,0:T(8,128)(2,1)S(1)}, u32[]{:S(2)}, u32[]{:S(2)}) collective-permute-start(bf16[8,8,16,128]{3,2,1,0:T(8,128)(2,1)S(1)} %get-tuple-element.69), channel_id=1, source_target_pairs={{0,2},{2,0},{1,3},{3,1},{4,6},{6,4},{5,7},{7,5},{8,10},{10,8},{9,1... | collective-permute-start | bytes 786440 | tf_op jit(solution)/shard_map/ppermute | solution.py:275
  85.0 8.8 %collective-permute-start.23 = (bf16[144,256]{1,0:T(8,128)(2,1)S(1)}, bf16[144,256]{1,0:T(8,128)(2,1)S(1)}, u32[]{:S(2)}, u32[]{:S(2)}) collective-permute-start(bf16[144,256]{1,0:T(8,128)(2,1)S(1)} %get-tuple-element.75), channel_id=1, source_target_pairs={{0,8},{4,12},{8,0},{12,4},{1,9},{5,13},{9,1},{13,5},{2,10},{6,14},... | collective-permute-start | bytes 221192 | tf_op jit(solution)/shard_map/ppermute | solution.py:759
  86.8 7.0 %collective-permute-start.24 = (bf16[144,256]{1,0:T(8,128)(2,1)S(1)}, bf16[144,256]{1,0:T(8,128)(2,1)S(1)}, u32[]{:S(2)}, u32[]{:S(2)}) collective-permute-start(bf16[144,256]{1,0:T(8,128)(2,1)S(1)} %get-tuple-element.76), channel_id=1, source_target_pairs={{0,12},{4,8},{8,4},{12,0},{1,13},{5,9},{9,5},{13,1},{2,14},{6,10},... | collective-permute-start | bytes 221192 | tf_op jit(solution)/shard_map/ppermute | solution.py:759
  (8 other events, 49.9 us)

commit v16 on v15

--- a/solution.py
+++ b/solution.py
@@ -347,7 +347,7 @@
 
 
 def shared_first_body(
-    p_ref, got_ref, s_ref, u_ref, odd_ref, even_ref, edge_ref, both_ref, square
+    p_ref, got_ref, s_ref, _, u_ref, odd_ref, even_ref, edge_ref, both_ref, square
 ):
     depth, across, rows, _ = got_ref.shape
     half = rows - EDGE
@@ -381,12 +381,12 @@
     store_sides(core, chip, u_ref, edge_ref, None)
 
 
-def shared_first(probes, got, source):
+def shared_first(probes, got, source, after):
     depth, across, along, _ = probes.shape
     edge = shape_of(RADIUS, across, along, BF16)
     return call(
         shared_first_body,
-        in_specs=whole_vmem(3),
+        in_specs=whole_vmem(3) + unread([after]),
         out_specs=whole_vmem(5),
         out_shape=[
             shape_of(depth, across, along + 4 * EDGE, F32),
@@ -396,7 +396,7 @@
             shape_of(depth, across, along, BF16),
         ],
         scratch_shapes=square_scratch()[:1],
-    )(probes, got, source)
+    )(probes, got, source, after)
 
 
 def shared_local_body(moment, has_previous, *refs):
@@ -827,36 +827,35 @@
     got = chip_swap(window)
     u, *edges = first_field(probes, 0, first_source, (window,))
     odd, even, beside = exchange(*edges)
-    shared_u, *edges, both = shared_first(probes, got, first_source)
+    base = local_step(u, beside, probes, 0, courant, source, 1, None)
+    shared_u, *edges, both = shared_first(probes, got, first_source, base)
     shared_odd, shared_even, shared_beside = exchange(*edges)
 
     previous = shared_previous = rows = None
-    before = (both,)
+    before = both
     for n in range(1, steps):
         last = n == steps - 1
-        base = local_step(u, beside, probes, 0, courant, source, n, previous)
         if last:
-            kept, sent = wide_rim(base, courant, odd, even, "own", after=before)
+            kept, sent = wide_rim(base, courant, odd, even, "own", after=(before,))
             fields = [kept, chip_swap(sent)]
-            before = (kept,)
+            before = kept
         else:
-            previous = u
-            u, *edges = rim_step(base, odd, even, courant, "middle", before)
+            previous, (u, *edges) = u, rim_step(base, odd, even, courant, "middle", (before,))
             odd, even, beside = exchange(*edges)
-            before = (edges[-1],)
-        base = shared_local(
+            base = local_step(u, beside, probes, 0, courant, source, n + 1, previous)
+            before = base
+        shared_base = shared_local(
             shared_u, shared_beside, both, courant, source, n, shared_previous
         )
+        shared = (shared_base, courant, shared_odd, shared_even)
         if last:
-            fields += wide_rim(base, courant, shared_odd, shared_even, "both", rows, before)
+            fields += wide_rim(*shared, "both", rows, (before,))
         else:
             shared_previous = shared_u
-            shared_u, *edges, rows = wide_rim(
-                base, courant, shared_odd, shared_even, "middle", rows, before
-            )
-            before = (edges[-1],)
+            shared_u, *edges, rows = wide_rim(*shared, "middle", rows, (before,))
+            rows = chip_swap(rows)
+            before = rows if n == steps - 2 else edges[-1]
             shared_odd, shared_even, shared_beside = exchange(*edges)
-            rows = chip_swap(rows)
     return coupled(fields, cell_count)
 
 

time: 102 us -> 101 us (level)
  starting transfers between devices: 41.3 us -> 37.6 us
  waiting for transfers between devices: 33.7 us -> 36.1 us
    ppermute x25, starting transfers between devices: 37.7 us -> 33.8 us  [swap(): lax.ppermute(x, axis, [p for a, b in pairs for p in ((a, b), (b, a))])]
    ppermute x25, waiting for transfers between devices: 27.3 us -> 30.1 us  [swap(): lax.ppermute(x, axis, [p for a, b in pairs for p in ((a, b), (b, a))])]
  transfers between devices with their start and end apart: 28 -> 28, of which waited for: 9 -> 14; matrix products, arithmetic and copies ran while one was open for 0% -> 0% of each run, Pallas kernels for 21% -> 21%
where the time goes in v16:
time: 101 us
  starting transfers between devices  37.6 us (37%)
  waiting for transfers between devices  36.1 us (36%)
  Pallas kernels  24.5 us (24%)
  local copies, waits for them, and re-layouts  1.42 us (1%)
    ppermute x25, starting transfers between devices, swap(): lax.ppermute(x, axis, [p for a, b in pairs for p in ((a, b), (b, a))])  33.8 us
    ppermute x25, waiting for transfers between devices, swap(): lax.ppermute(x, axis, [p for a, b in pairs for p in ((a, b), (b, a))])  30.1 us
    pallas_call x3, Pallas kernels, shared_local(): call(functools.partial(shared_local_body, moment, previous is not None),...  7.27 us
    pallas_call x3, Pallas kernels, local_step(): call(functools.partial(local_body, chunk, moment, previous is not None),...  6.64 us
    ppermute x3, waiting for transfers between devices, coupled(): lax.ppermute(blocks[d - 1], 'slab', [(i, i ^ d) for i in range(slabs)])  5.95 us
    pallas_call x4, Pallas kernels, wide_rim(): call(functools.partial(wide_rim_body, kind, rows is not None, len(after))...  3.8 us
    ppermute x3, starting transfers between devices, coupled(): lax.ppermute(blocks[d - 1], 'slab', [(i, i ^ d) for i in range(slabs)])  3.77 us
    pallas_call x2, Pallas kernels, rim_step(): call(functools.partial(rim_body, kind, len(after)), in_specs=whole_vmem(4...  2.19 us
  transfers between devices with their start and end apart: 28, of which 14 were waited for; matrix products, arithmetic and copies ran while one was open for 0% of the time, Pallas kernels for 21%

profile of v16, /device:TPU:0, one launch (start us, length us, event | category | flops | bytes accessed | tf_op | source)
XLA Modules:
  0.0 100.5 jit_solution(15917539137359375533)
XLA Ops:
  2.2 3.0 %collective-permute-start.3 = (bf16[8,8,32,128]{3,2,1,0:T(8,128)(2,1)S(1)}, bf16[8,8,32,128]{3,2,1,0:T(8,128)(2,1)S(1)}, u32[]{:S(2)}, u32[]{:S(2)}) collective-permute-start(bf16[8,8,32,128]{3,2,1,0:T(8,128)(2,1)S(1)} %shard_map.50.refs_0_), channel_id=1, source_target_pairs={{0,2},{2,0},{1,3},{3,1},{4,6},{6,4},{5,7},{7,5},{8,10},{10,8},{9,1... | collective-permute-start | bytes 1572872 | tf_op jit(solution)/shard_map/ppermute | solution.py:275
  7.0 4.4 %collective-permute-start.2 = (bf16[4,8,48,128]{3,2,1,0:T(8,128)(2,1)S(1)}, bf16[4,8,48,128]{3,2,1,0:T(8,128)(2,1)S(1)}, u32[]{:S(2)}, u32[]{:S(2)}) collective-permute-start(bf16[4,8,48,128]{3,2,1,0:T(8,128)(2,1)S(1)} %get-tuple-element.44), channel_id=1, source_target_pairs={{0,4},{4,0},{8,12},{12,8},{1,5},{5,1},{9,13},{13,9},{2,6},{6,2},{1... | collective-permute-start | bytes 1179656 | tf_op jit(solution)/shard_map/ppermute | solution.py:275
  11.5 2.1 %shard_map.52._.refs_0_ = f32[8,8,48,128]{3,2,1,0:T(8,128)S(1)} custom-call(f32[8,8,64,128]{3,2,1,0:T(8,128)S(1)} %get-tuple-element.41.refs_0_.refs_5_, bf16[8,4,48,128]{3,2,1,0:T(8,128)(2,1)S(1)} %collective-permute-done.refs_1_, bf16[8,8,48,256]{3,2,1,0:T(8,128)(2,1)S(1)} %copy-done, f32[64,48]{1,0:T(8,128)S(1)} %bitcast.11, f32[4,64,48]{2,1,0:T(8,128)S(1)} %bitcast.5), custom_call_target="tpu_custom_call" | custom-call | flops 1 | bytes 1 | tf_op jit(solution)/shard_map/pallas_call | solution.py:190
  13.6 3.5 %collective-permute-done.3.got_ref = bf16[8,8,32,128]{3,2,1,0:T(8,128)(2,1)S(1)} collective-permute-done((bf16[8,8,32,128]{3,2,1,0:T(8,128)(2,1)S(1)}, bf16[8,8,32,128]{3,2,1,0:T(8,128)(2,1)S(1)}, u32[]{:S(2)}, u32[]{:S(2)}) %collective-permute-start.3) | collective-permute-done | bytes 524320 | tf_op jit(solution)/shard_map/ppermute | solution.py:275
  17.9 3.1 %collective-permute-done.2.refs_2_ = bf16[4,8,48,128]{3,2,1,0:T(8,128)(2,1)S(1)} collective-permute-done((bf16[4,8,48,128]{3,2,1,0:T(8,128)(2,1)S(1)}, bf16[4,8,48,128]{3,2,1,0:T(8,128)(2,1)S(1)}, u32[]{:S(2)}, u32[]{:S(2)}) %collective-permute-start.2) | collective-permute-done | bytes 393248 | tf_op jit(solution)/shard_map/ppermute | solution.py:275
  23.3 3.5 %collective-permute-start.9 = (bf16[4,8,48,128]{3,2,1,0:T(8,128)(2,1)S(1)}, bf16[4,8,48,128]{3,2,1,0:T(8,128)(2,1)S(1)}, u32[]{:S(2)}, u32[]{:S(2)}) collective-permute-start(bf16[4,8,48,128]{3,2,1,0:T(8,128)(2,1)S(1)} %get-tuple-element.53), channel_id=1, source_target_pairs={{0,4},{4,0},{8,12},{12,8},{1,5},{5,1},{9,13},{13,9},{2,6},{6,2},{1... | collective-permute-start | bytes 1179656 | tf_op jit(solution)/shard_map/ppermute | solution.py:275
  27.5 2.9 %collective-permute-start.6 = (bf16[4,8,48,128]{3,2,1,0:T(8,128)(2,1)S(1)}, bf16[4,8,48,128]{3,2,1,0:T(8,128)(2,1)S(1)}, u32[]{:S(2)}, u32[]{:S(2)}) collective-permute-start(bf16[4,8,48,128]{3,2,1,0:T(8,128)(2,1)S(1)} %get-tuple-element.49), channel_id=1, source_target_pairs={{0,4},{4,0},{8,12},{12,8},{1,5},{5,1},{9,13},{13,9},{2,6},{6,2},{1... | collective-permute-start | bytes 1179656 | tf_op jit(solution)/shard_map/ppermute | solution.py:275
  30.4 2.2 %shard_map.55.refs_4_.refs_0_ = f32[8,8,48,128]{3,2,1,0:T(8,128)S(1)} custom-call(f32[8,8,64,128]{3,2,1,0:T(8,128)S(1)} %get-tuple-element.46.refs_0_.refs_5_, bf16[8,4,48,128]{3,2,1,0:T(8,128)(2,1)S(1)} %collective-permute-done.4.refs_1_, bf16[8,8,48,256]{3,2,1,0:T(8,128)(2,1)S(1)} %copy-done.1, f32[64,48]{1,0:T(8,128)S(1)} %bitcast.13, ...), custom_call_target="tpu_custom_call" | custom-call | flops 1 | bytes 1 | tf_op jit(solution)/shard_map/pallas_call | solution.py:190
  32.7 2.3 %shard_map.56.refs_0_ = f32[8,8,48,128]{3,2,1,0:T(8,128)S(1)} custom-call(f32[8,8,80,128]{3,2,1,0:T(8,128)S(1)} %get-tuple-element.50.refs_0_.refs_5_, bf16[8,4,48,128]{3,2,1,0:T(8,128)(2,1)S(1)} %collective-permute-done.7.refs_1_, bf16[8,8,48,128]{3,2,1,0:T(8,128)(2,1)S(1)} %get-tuple-element.45.refs_4_.refs_2_, f32[64,48]{1,0:T(8,128)S(1)} %bitcast.14, ...), custom_call_target="tpu_custom_call" | custom-call | flops 1 | bytes 1 | tf_op jit(solution)/shard_map/pallas_call | solution.py:460
  35.0 1.7 %collective-permute-done.9.refs_3_ = bf16[4,8,48,128]{3,2,1,0:T(8,128)(2,1)S(1)} collective-permute-done((bf16[4,8,48,128]{3,2,1,0:T(8,128)(2,1)S(1)}, bf16[4,8,48,128]{3,2,1,0:T(8,128)(2,1)S(1)}, u32[]{:S(2)}, u32[]{:S(2)}) %collective-permute-start.9) | collective-permute-done | bytes 393248 | tf_op jit(solution)/shard_map/ppermute | solution.py:275
  37.7 6.6 %collective-permute-done.6.refs_2_ = bf16[4,8,48,128]{3,2,1,0:T(8,128)(2,1)S(1)} collective-permute-done((bf16[4,8,48,128]{3,2,1,0:T(8,128)(2,1)S(1)}, bf16[4,8,48,128]{3,2,1,0:T(8,128)(2,1)S(1)}, u32[]{:S(2)}, u32[]{:S(2)}) %collective-permute-start.6) | collective-permute-done | bytes 393248 | tf_op jit(solution)/shard_map/ppermute | solution.py:275
  46.2 4.6 %collective-permute-start.15 = (bf16[4,8,48,128]{3,2,1,0:T(8,128)(2,1)S(1)}, bf16[4,8,48,128]{3,2,1,0:T(8,128)(2,1)S(1)}, u32[]{:S(2)}, u32[]{:S(2)}) collective-permute-start(bf16[4,8,48,128]{3,2,1,0:T(8,128)(2,1)S(1)} %get-tuple-element.61), channel_id=1, source_target_pairs={{0,4},{4,0},{8,12},{12,8},{1,5},{5,1},{9,13},{13,9},{2,6},{6,2},{1... | collective-permute-start | bytes 1179656 | tf_op jit(solution)/shard_map/ppermute | solution.py:275
  52.2 1.8 %collective-permute-start.12 = (bf16[4,8,48,128]{3,2,1,0:T(8,128)(2,1)S(1)}, bf16[4,8,48,128]{3,2,1,0:T(8,128)(2,1)S(1)}, u32[]{:S(2)}, u32[]{:S(2)}) collective-permute-start(bf16[4,8,48,128]{3,2,1,0:T(8,128)(2,1)S(1)} %get-tuple-element.58), channel_id=1, source_target_pairs={{0,4},{4,0},{8,12},{12,8},{1,5},{5,1},{9,13},{13,9},{2,6},{6,2},{1... | collective-permute-start | bytes 1179656 | tf_op jit(solution)/shard_map/ppermute | solution.py:275
  54.0 2.5 %shard_map.60.refs_0_ = f32[8,8,48,128]{3,2,1,0:T(8,128)S(1)} custom-call(f32[8,8,80,128]{3,2,1,0:T(8,128)S(1)} %get-tuple-element.59.refs_0_.refs_5_, bf16[8,4,48,128]{3,2,1,0:T(8,128)(2,1)S(1)} %collective-permute-done.13.refs_1_, bf16[8,8,48,128]{3,2,1,0:T(8,128)(2,1)S(1)} %get-tuple-element.45.refs_4_.refs_2_, f32[64,48]{1,0:T(8,128)S(1)} %bitcast.17, ...), custom_call_target="tpu_custom_call" | custom-call | flops 1 | bytes 1 | tf_op jit(solution)/shard_map/pallas_call | solution.py:460
  56.5 2.3 %shard_map.59.refs_5_.refs_0_ = f32[8,8,48,128]{3,2,1,0:T(8,128)S(1)} custom-call(f32[8,8,64,128]{3,2,1,0:T(8,128)S(1)} %get-tuple-element.55.refs_0_, bf16[8,4,48,128]{3,2,1,0:T(8,128)(2,1)S(1)} %collective-permute-done.10.refs_1_, bf16[8,8,48,256]{3,2,1,0:T(8,128)(2,1)S(1)} %copy-done.1, f32[64,48]{1,0:T(8,128)S(1)} %bitcast.18, f32[4,64,48]{2,1,0:T(8,128)S(1)} %bitcast.9, ...), custom_call_target="tpu_custom_call" | custom-call | flops 1 | bytes 1 | tf_op jit(solution)/shard_map/pallas_call | solution.py:190
  58.9 1.8 %collective-permute-done.15.refs_3_ = bf16[4,8,48,128]{3,2,1,0:T(8,128)(2,1)S(1)} collective-permute-done((bf16[4,8,48,128]{3,2,1,0:T(8,128)(2,1)S(1)}, bf16[4,8,48,128]{3,2,1,0:T(8,128)(2,1)S(1)}, u32[]{:S(2)}, u32[]{:S(2)}) %collective-permute-start.15) | collective-permute-done | bytes 393248 | tf_op jit(solution)/shard_map/ppermute | solution.py:275
  63.5 5.5 %collective-permute-start.21 = (bf16[4,8,48,128]{3,2,1,0:T(8,128)(2,1)S(1)}, bf16[4,8,48,128]{3,2,1,0:T(8,128)(2,1)S(1)}, u32[]{:S(2)}, u32[]{:S(2)}) collective-permute-start(bf16[4,8,48,128]{3,2,1,0:T(8,128)(2,1)S(1)} %get-tuple-element.69), channel_id=1, source_target_pairs={{0,4},{4,0},{8,12},{12,8},{1,5},{5,1},{9,13},{13,9},{2,6},{6,2},{1... | collective-permute-start | bytes 1179656 | tf_op jit(solution)/shard_map/ppermute | solution.py:275
  71.0 2.5 %shard_map.63.refs_0_ = f32[8,8,48,128]{3,2,1,0:T(8,128)S(1)} custom-call(f32[8,8,80,128]{3,2,1,0:T(8,128)S(1)} %get-tuple-element.66.refs_0_, bf16[8,4,48,128]{3,2,1,0:T(8,128)(2,1)S(1)} %collective-permute-done.19.refs_1_, bf16[8,8,48,128]{3,2,1,0:T(8,128)(2,1)S(1)} %get-tuple-element.45.refs_4_.refs_2_, f32[64,48]{1,0:T(8,128)S(1)} %bitcast.21, ...), custom_call_target="tpu_custom_call" | custom-call | flops 1 | bytes 1 | tf_op jit(solution)/shard_map/pallas_call | solution.py:460
  73.5 4.5 %collective-permute-done.21.refs_3_ = bf16[4,8,48,128]{3,2,1,0:T(8,128)(2,1)S(1)} collective-permute-done((bf16[4,8,48,128]{3,2,1,0:T(8,128)(2,1)S(1)}, bf16[4,8,48,128]{3,2,1,0:T(8,128)(2,1)S(1)}, u32[]{:S(2)}, u32[]{:S(2)}) %collective-permute-start.21) | collective-permute-done | bytes 393248 | tf_op jit(solution)/shard_map/ppermute | solution.py:275
  81.7 1.9 %collective-permute-done.22.got_ref = f32[520,256]{1,0:T(8,128)S(1)} collective-permute-done((f32[520,256]{1,0:T(8,128)S(1)}, f32[520,256]{1,0:T(8,128)S(1)}, u32[]{:S(2)}, u32[]{:S(2)}) %collective-permute-start.22) | collective-permute-done | bytes 532512 | tf_op jit(solution)/shard_map/ppermute | solution.py:275
  83.7 1.5 %collective-permute-start.23 = (bf16[144,256]{1,0:T(8,128)(2,1)S(1)}, bf16[144,256]{1,0:T(8,128)(2,1)S(1)}, u32[]{:S(2)}, u32[]{:S(2)}) collective-permute-start(bf16[144,256]{1,0:T(8,128)(2,1)S(1)} %get-tuple-element.75), channel_id=1, source_target_pairs={{0,8},{4,12},{8,0},{12,4},{1,9},{5,13},{9,1},{13,5},{2,10},{6,14},... | collective-permute-start | bytes 221192 | tf_op jit(solution)/shard_map/ppermute | solution.py:759
  85.2 2.3 %collective-permute-start.24 = (bf16[144,256]{1,0:T(8,128)(2,1)S(1)}, bf16[144,256]{1,0:T(8,128)(2,1)S(1)}, u32[]{:S(2)}, u32[]{:S(2)}) collective-permute-start(bf16[144,256]{1,0:T(8,128)(2,1)S(1)} %get-tuple-element.76), channel_id=1, source_target_pairs={{0,12},{4,8},{8,4},{12,0},{1,13},{5,9},{9,5},{13,1},{2,14},{6,10},... | collective-permute-start | bytes 221192 | tf_op jit(solution)/shard_map/ppermute | solution.py:759
  87.5 5.4 %collective-permute-done.23.refs_0_ = bf16[144,256]{1,0:T(8,128)(2,1)S(1)} collective-permute-done((bf16[144,256]{1,0:T(8,128)(2,1)S(1)}, bf16[144,256]{1,0:T(8,128)(2,1)S(1)}, u32[]{:S(2)}, u32[]{:S(2)}) %collective-permute-start.23) | collective-permute-done | bytes 73760 | tf_op jit(solution)/shard_map/ppermute | solution.py:759
  94.2 3.7 %collective-permute-done.26.other_ref = bf16[144,256]{1,0:T(8,128)(2,1)S(1)} collective-permute-done((bf16[144,256]{1,0:T(8,128)(2,1)S(1)}, bf16[144,256]{1,0:T(8,128)(2,1)S(1)}, u32[]{:S(2)}, u32[]{:S(2)}) %collective-permute-start.26) | collective-permute-done | bytes 73760 | tf_op jit(solution)/shard_map/ppermute | solution.py:275
  (61 shorter events, 23.9 us)
Async XLA Ops:
  2.2 14.9 %collective-permute-start.3 = (bf16[8,8,32,128]{3,2,1,0:T(8,128)(2,1)S(1)}, bf16[8,8,32,128]{3,2,1,0:T(8,128)(2,1)S(1)}, u32[]{:S(2)}, u32[]{:S(2)}) collective-permute-start(bf16[8,8,32,128]{3,2,1,0:T(8,128)(2,1)S(1)} %shard_map.50.refs_0_), channel_id=1, source_target_pairs={{0,2},{2,0},{1,3},{3,1},{4,6},{6,4},{5,7},{7,5},{8,10},{10,8},{9,1... | collective-permute-start | bytes 1572872 | tf_op jit(solution)/shard_map/ppermute | solution.py:275
  6.3 11.5 %collective-permute-start.1 = (bf16[4,8,48,128]{3,2,1,0:T(8,128)(2,1)S(1)}, bf16[4,8,48,128]{3,2,1,0:T(8,128)(2,1)S(1)}, u32[]{:S(2)}, u32[]{:S(2)}) collective-permute-start(bf16[4,8,48,128]{3,2,1,0:T(8,128)(2,1)S(1)} %get-tuple-element.43), channel_id=1, source_target_pairs={{4,8},{8,4},{5,9},{9,5},{6,10},{10,6},{7,11},{11,7},{20,24},{24,20... | collective-permute-start | bytes 1179656 | tf_op jit(solution)/shard_map/ppermute | solution.py:275
  7.0 13.9 %collective-permute-start.2 = (bf16[4,8,48,128]{3,2,1,0:T(8,128)(2,1)S(1)}, bf16[4,8,48,128]{3,2,1,0:T(8,128)(2,1)S(1)}, u32[]{:S(2)}, u32[]{:S(2)}) collective-permute-start(bf16[4,8,48,128]{3,2,1,0:T(8,128)(2,1)S(1)} %get-tuple-element.44), channel_id=1, source_target_pairs={{0,4},{4,0},{8,12},{12,8},{1,5},{5,1},{9,13},{13,9},{2,6},{6,2},{1... | collective-permute-start | bytes 1179656 | tf_op jit(solution)/shard_map/ppermute | solution.py:275
  22.1 5.4 %collective-permute-start.4 = (bf16[8,4,48,128]{3,2,1,0:T(8,128)(2,1)S(1)}, bf16[8,4,48,128]{3,2,1,0:T(8,128)(2,1)S(1)}, u32[]{:S(2)}, u32[]{:S(2)}) collective-permute-start(bf16[8,4,48,128]{3,2,1,0:T(8,128)(2,1)S(1)} %get-tuple-element.47), channel_id=1, source_target_pairs={{0,1},{1,0},{2,3},{3,2},{4,5},{5,4},{6,7},{7,6},{8,9},{9,8},{10,11... | collective-permute-start | bytes 1179656 | tf_op jit(solution)/shard_map/ppermute | solution.py:275
  22.2 10.5 %collective-permute-start.7 = (bf16[8,4,48,128]{3,2,1,0:T(8,128)(2,1)S(1)}, bf16[8,4,48,128]{3,2,1,0:T(8,128)(2,1)S(1)}, u32[]{:S(2)}, u32[]{:S(2)}) collective-permute-start(bf16[8,4,48,128]{3,2,1,0:T(8,128)(2,1)S(1)} %get-tuple-element.51), channel_id=1, source_target_pairs={{0,1},{1,0},{2,3},{3,2},{4,5},{5,4},{6,7},{7,6},{8,9},{9,8},{10,11... | collective-permute-start | bytes 1179656 | tf_op jit(solution)/shard_map/ppermute | solution.py:275
  22.6 12.4 %collective-permute-start.8 = (bf16[4,8,48,128]{3,2,1,0:T(8,128)(2,1)S(1)}, bf16[4,8,48,128]{3,2,1,0:T(8,128)(2,1)S(1)}, u32[]{:S(2)}, u32[]{:S(2)}) collective-permute-start(bf16[4,8,48,128]{3,2,1,0:T(8,128)(2,1)S(1)} %get-tuple-element.52), channel_id=1, source_target_pairs={{4,8},{8,4},{5,9},{9,5},{6,10},{10,6},{7,11},{11,7},{20,24},{24,20... | collective-permute-start | bytes 1179656 | tf_op jit(solution)/shard_map/ppermute | solution.py:275
  23.3 13.4 %collective-permute-start.9 = (bf16[4,8,48,128]{3,2,1,0:T(8,128)(2,1)S(1)}, bf16[4,8,48,128]{3,2,1,0:T(8,128)(2,1)S(1)}, u32[]{:S(2)}, u32[]{:S(2)}) collective-permute-start(bf16[4,8,48,128]{3,2,1,0:T(8,128)(2,1)S(1)} %get-tuple-element.53), channel_id=1, source_target_pairs={{0,4},{4,0},{8,12},{12,8},{1,5},{5,1},{9,13},{13,9},{2,6},{6,2},{1... | collective-permute-start | bytes 1179656 | tf_op jit(solution)/shard_map/ppermute | solution.py:275
  26.8 10.9 %collective-permute-start.5 = (bf16[4,8,48,128]{3,2,1,0:T(8,128)(2,1)S(1)}, bf16[4,8,48,128]{3,2,1,0:T(8,128)(2,1)S(1)}, u32[]{:S(2)}, u32[]{:S(2)}) collective-permute-start(bf16[4,8,48,128]{3,2,1,0:T(8,128)(2,1)S(1)} %get-tuple-element.48), channel_id=1, source_target_pairs={{4,8},{8,4},{5,9},{9,5},{6,10},{10,6},{7,11},{11,7},{20,24},{24,20... | collective-permute-start | bytes 1179656 | tf_op jit(solution)/shard_map/ppermute | solution.py:275
  27.5 16.8 %collective-permute-start.6 = (bf16[4,8,48,128]{3,2,1,0:T(8,128)(2,1)S(1)}, bf16[4,8,48,128]{3,2,1,0:T(8,128)(2,1)S(1)}, u32[]{:S(2)}, u32[]{:S(2)}) collective-permute-start(bf16[4,8,48,128]{3,2,1,0:T(8,128)(2,1)S(1)} %get-tuple-element.49), channel_id=1, source_target_pairs={{0,4},{4,0},{8,12},{12,8},{1,5},{5,1},{9,13},{13,9},{2,6},{6,2},{1... | collective-permute-start | bytes 1179656 | tf_op jit(solution)/shard_map/ppermute | solution.py:275
  37.6 13.9 %collective-permute-start.13 = (bf16[8,4,48,128]{3,2,1,0:T(8,128)(2,1)S(1)}, bf16[8,4,48,128]{3,2,1,0:T(8,128)(2,1)S(1)}, u32[]{:S(2)}, u32[]{:S(2)}) collective-permute-start(bf16[8,4,48,128]{3,2,1,0:T(8,128)(2,1)S(1)} %get-tuple-element.54.refs_4_), channel_id=1, source_target_pairs={{0,1},{1,0},{2,3},{3,2},{4,5},{5,4},{6,7},{7,6},{8,9},{9,8},{10,11... | collective-permute-start | bytes 1179656 | tf_op jit(solution)/shard_map/ppermute | solution.py:275
  45.4 6.7 %collective-permute-start.10 = (bf16[8,4,48,128]{3,2,1,0:T(8,128)(2,1)S(1)}, bf16[8,4,48,128]{3,2,1,0:T(8,128)(2,1)S(1)}, u32[]{:S(2)}, u32[]{:S(2)}) collective-permute-start(bf16[8,4,48,128]{3,2,1,0:T(8,128)(2,1)S(1)} %get-tuple-element.56), channel_id=1, source_target_pairs={{0,1},{1,0},{2,3},{3,2},{4,5},{5,4},{6,7},{7,6},{8,9},{9,8},{10,11... | collective-permute-start | bytes 1179656 | tf_op jit(solution)/shard_map/ppermute | solution.py:275
  45.5 13.4 %collective-permute-start.14 = (bf16[4,8,48,128]{3,2,1,0:T(8,128)(2,1)S(1)}, bf16[4,8,48,128]{3,2,1,0:T(8,128)(2,1)S(1)}, u32[]{:S(2)}, u32[]{:S(2)}) collective-permute-start(bf16[4,8,48,128]{3,2,1,0:T(8,128)(2,1)S(1)} %get-tuple-element.60), channel_id=1, source_target_pairs={{4,8},{8,4},{5,9},{9,5},{6,10},{10,6},{7,11},{11,7},{20,24},{24,20... | collective-permute-start | bytes 1179656 | tf_op jit(solution)/shard_map/ppermute | solution.py:275
  46.2 14.5 %collective-permute-start.15 = (bf16[4,8,48,128]{3,2,1,0:T(8,128)(2,1)S(1)}, bf16[4,8,48,128]{3,2,1,0:T(8,128)(2,1)S(1)}, u32[]{:S(2)}, u32[]{:S(2)}) collective-permute-start(bf16[4,8,48,128]{3,2,1,0:T(8,128)(2,1)S(1)} %get-tuple-element.61), channel_id=1, source_target_pairs={{0,4},{4,0},{8,12},{12,8},{1,5},{5,1},{9,13},{13,9},{2,6},{6,2},{1... | collective-permute-start | bytes 1179656 | tf_op jit(solution)/shard_map/ppermute | solution.py:275
  50.8 8.1 %collective-permute-start.16 = (bf16[8,8,16,128]{3,2,1,0:T(8,128)(2,1)S(1)}, bf16[8,8,16,128]{3,2,1,0:T(8,128)(2,1)S(1)}, u32[]{:S(2)}, u32[]{:S(2)}) collective-permute-start(bf16[8,8,16,128]{3,2,1,0:T(8,128)(2,1)S(1)} %get-tuple-element.62), channel_id=1, source_target_pairs={{0,2},{2,0},{1,3},{3,1},{4,6},{6,4},{5,7},{7,5},{8,10},{10,8},{9,1... | collective-permute-start | bytes 786440 | tf_op jit(solution)/shard_map/ppermute | solution.py:275
  51.5 12.1 %collective-permute-start.11 = (bf16[4,8,48,128]{3,2,1,0:T(8,128)(2,1)S(1)}, bf16[4,8,48,128]{3,2,1,0:T(8,128)(2,1)S(1)}, u32[]{:S(2)}, u32[]{:S(2)}) collective-permute-start(bf16[4,8,48,128]{3,2,1,0:T(8,128)(2,1)S(1)} %get-tuple-element.57), channel_id=1, source_target_pairs={{4,8},{8,4},{5,9},{9,5},{6,10},{10,6},{7,11},{11,7},{20,24},{24,20... | collective-permute-start | bytes 1179656 | tf_op jit(solution)/shard_map/ppermute | solution.py:275
  52.2 16.9 %collective-permute-start.12 = (bf16[4,8,48,128]{3,2,1,0:T(8,128)(2,1)S(1)}, bf16[4,8,48,128]{3,2,1,0:T(8,128)(2,1)S(1)}, u32[]{:S(2)}, u32[]{:S(2)}) collective-permute-start(bf16[4,8,48,128]{3,2,1,0:T(8,128)(2,1)S(1)} %get-tuple-element.58), channel_id=1, source_target_pairs={{0,4},{4,0},{8,12},{12,8},{1,5},{5,1},{9,13},{13,9},{2,6},{6,2},{1... | collective-permute-start | bytes 1179656 | tf_op jit(solution)/shard_map/ppermute | solution.py:275
  61.9 7.6 %collective-permute-start.17 = (bf16[8,8,16,128]{3,2,1,0:T(8,128)(2,1)S(1)}, bf16[8,8,16,128]{3,2,1,0:T(8,128)(2,1)S(1)}, u32[]{:S(2)}, u32[]{:S(2)}) collective-permute-start(bf16[8,8,16,128]{3,2,1,0:T(8,128)(2,1)S(1)} %get-tuple-element.63), channel_id=1, source_target_pairs={{0,2},{2,0},{1,3},{3,1},{4,6},{6,4},{5,7},{7,5},{8,10},{10,8},{9,1... | collective-permute-start | bytes 786440 | tf_op jit(solution)/shard_map/ppermute | solution.py:275
  62.7 8.3 %collective-permute-start.19 = (bf16[8,4,48,128]{3,2,1,0:T(8,128)(2,1)S(1)}, bf16[8,4,48,128]{3,2,1,0:T(8,128)(2,1)S(1)}, u32[]{:S(2)}, u32[]{:S(2)}) collective-permute-start(bf16[8,4,48,128]{3,2,1,0:T(8,128)(2,1)S(1)} %get-tuple-element.67), channel_id=1, source_target_pairs={{0,1},{1,0},{2,3},{3,2},{4,5},{5,4},{6,7},{7,6},{8,9},{9,8},{10,11... | collective-permute-start | bytes 1179656 | tf_op jit(solution)/shard_map/ppermute | solution.py:275
  62.7 10.8 %collective-permute-start.20 = (bf16[4,8,48,128]{3,2,1,0:T(8,128)(2,1)S(1)}, bf16[4,8,48,128]{3,2,1,0:T(8,128)(2,1)S(1)}, u32[]{:S(2)}, u32[]{:S(2)}) collective-permute-start(bf16[4,8,48,128]{3,2,1,0:T(8,128)(2,1)S(1)} %get-tuple-element.68), channel_id=1, source_target_pairs={{4,8},{8,4},{5,9},{9,5},{6,10},{10,6},{7,11},{11,7},{20,24},{24,20... | collective-permute-start | bytes 1179656 | tf_op jit(solution)/shard_map/ppermute | solution.py:275
  63.5 14.5 %collective-permute-start.21 = (bf16[4,8,48,128]{3,2,1,0:T(8,128)(2,1)S(1)}, bf16[4,8,48,128]{3,2,1,0:T(8,128)(2,1)S(1)}, u32[]{:S(2)}, u32[]{:S(2)}) collective-permute-start(bf16[4,8,48,128]{3,2,1,0:T(8,128)(2,1)S(1)} %get-tuple-element.69), channel_id=1, source_target_pairs={{0,4},{4,0},{8,12},{12,8},{1,5},{5,1},{9,13},{13,9},{2,6},{6,2},{1... | collective-permute-start | bytes 1179656 | tf_op jit(solution)/shard_map/ppermute | solution.py:275
  70.3 10.1 %collective-permute-start.18 = (bf16[8,4,48,128]{3,2,1,0:T(8,128)(2,1)S(1)}, bf16[8,4,48,128]{3,2,1,0:T(8,128)(2,1)S(1)}, u32[]{:S(2)}, u32[]{:S(2)}) collective-permute-start(bf16[8,4,48,128]{3,2,1,0:T(8,128)(2,1)S(1)} %get-tuple-element.65), channel_id=1, source_target_pairs={{0,2},{2,0},{1,3},{3,1},{4,6},{6,4},{5,7},{7,5},{8,10},{10,8},{9,1... | collective-permute-start | bytes 1179656 | tf_op jit(solution)/shard_map/ppermute | solution.py:275
  83.7 9.2 %collective-permute-start.23 = (bf16[144,256]{1,0:T(8,128)(2,1)S(1)}, bf16[144,256]{1,0:T(8,128)(2,1)S(1)}, u32[]{:S(2)}, u32[]{:S(2)}) collective-permute-start(bf16[144,256]{1,0:T(8,128)(2,1)S(1)} %get-tuple-element.75), channel_id=1, source_target_pairs={{0,8},{4,12},{8,0},{12,4},{1,9},{5,13},{9,1},{13,5},{2,10},{6,14},... | collective-permute-start | bytes 221192 | tf_op jit(solution)/shard_map/ppermute | solution.py:759
  85.2 7.7 %collective-permute-start.24 = (bf16[144,256]{1,0:T(8,128)(2,1)S(1)}, bf16[144,256]{1,0:T(8,128)(2,1)S(1)}, u32[]{:S(2)}, u32[]{:S(2)}) collective-permute-start(bf16[144,256]{1,0:T(8,128)(2,1)S(1)} %get-tuple-element.76), channel_id=1, source_target_pairs={{0,12},{4,8},{8,4},{12,0},{1,13},{5,9},{9,5},{13,1},{2,14},{6,10},... | collective-permute-start | bytes 221192 | tf_op jit(solution)/shard_map/ppermute | solution.py:759
  87.5 6.0 %collective-permute-start.25 = (bf16[144,256]{1,0:T(8,128)(2,1)S(1)}, bf16[144,256]{1,0:T(8,128)(2,1)S(1)}, u32[]{:S(2)}, u32[]{:S(2)}) collective-permute-start(bf16[144,256]{1,0:T(8,128)(2,1)S(1)} %get-tuple-element.77), channel_id=1, source_target_pairs={{0,4},{4,0},{8,12},{12,8},{1,5},{5,1},{9,13},{13,9},{2,6},{6,2},{1... | collective-permute-start | bytes 221192 | tf_op jit(solution)/shard_map/ppermute | solution.py:759
  (8 other events, 36.3 us)

commit v17 on v16

--- a/solution.py
+++ b/solution.py
@@ -323,12 +323,11 @@
     )(probes)
 
 
-def store_sides(core, chip, u_ref, edge_ref, rows_ref):
+def store_sides(core, u_ref, edge_ref):
     depth, across, padded, _ = u_ref.shape
     segment = padded // 2
     half = segment - 2 * EDGE
     first = (across - RADIUS) * (1 - core)
-    near = pl.multiple_of(jnp.where(chip == 0, half, EDGE), 8)
 
     def plane(z, _):
         for j in range(RADIUS):
@@ -337,17 +336,38 @@
                 for g in range(2)
             ]
             edge_ref[z, j] = jnp.concatenate(parts, axis=0).astype(BF16)
-        if rows_ref is not None:
-            for x in range(across):
-                parts = [u_ref[z, x, pl.ds(near + g * segment, EDGE)] for g in range(2)]
-                rows_ref[z, x] = jnp.concatenate(parts, axis=0).astype(BF16)
         return 0
 
     lax.fori_loop(0, depth, plane, 0)
 
 
+def rows_body(u_ref, _, rows_ref):
+    depth, across, padded, _ = u_ref.shape
+    segment = padded // 2
+    half = segment - 2 * EDGE
+    near = pl.multiple_of(jnp.where(lax.axis_index("probe") == 0, half, EDGE), 8)
+
+    def plane(z, _):
+        for x in range(across):
+            parts = [u_ref[z, x, pl.ds(near + g * segment, EDGE)] for g in range(2)]
+            rows_ref[z, x] = jnp.concatenate(parts, axis=0).astype(BF16)
+        return 0
+
+    lax.fori_loop(0, depth, plane, 0)
+
+
+def rows_of(u, after):
+    depth, across, _, _ = u.shape
+    return call(
+        rows_body,
+        in_specs=whole_vmem(1) + unread([after]),
+        out_specs=whole_vmem(1)[0],
+        out_shape=shape_of(depth, across, 2 * EDGE, BF16),
+    )(u, after)
+
+
 def shared_first_body(
-    p_ref, got_ref, s_ref, _, u_ref, odd_ref, even_ref, edge_ref, both_ref, square
+    p_ref, got_ref, s_ref, u_ref, odd_ref, even_ref, edge_ref, both_ref, square
 ):
     depth, across, rows, _ = got_ref.shape
     half = rows - EDGE
@@ -378,15 +398,15 @@
             u = [own_half(scale * window, half, chip) for window in windows]
             news.append(jnp.concatenate(u, axis=0))
         store_edges(x, pl.ds(0, along), news, even, even_ref, odd_ref)
-    store_sides(core, chip, u_ref, edge_ref, None)
-
-
-def shared_first(probes, got, source, after):
+    store_sides(core, u_ref, edge_ref)
+
+
+def shared_first(probes, got, source):
     depth, across, along, _ = probes.shape
     edge = shape_of(RADIUS, across, along, BF16)
     return call(
         shared_first_body,
-        in_specs=whole_vmem(3) + unread([after]),
+        in_specs=whole_vmem(3),
         out_specs=whole_vmem(5),
         out_shape=[
             shape_of(depth, across, along + 4 * EDGE, F32),
@@ -396,7 +416,7 @@
             shape_of(depth, across, along, BF16),
         ],
         scratch_shapes=square_scratch()[:1],
-    )(probes, got, source, after)
+    )(probes, got, source)
 
 
 def shared_local_body(moment, has_previous, *refs):
@@ -532,7 +552,7 @@
         return news
 
     if kind == "middle":
-        u_ref, odd_out, even_out, edge_ref, rows_out = outs
+        u_ref, odd_out, even_out, edge_ref = outs
         for x in range(across):
             news = values(x)
             for z, new in enumerate(news):
@@ -542,7 +562,7 @@
                     u_ref[z, x, at : at + half] = new[g * half : (g + 1) * half]
                     u_ref[z, x, at + half : at + half + EDGE] = blank
             store_edges(x, pl.ds(0, along), news, even, even_out, odd_out)
-        store_sides(core, chip, u_ref, edge_ref, rows_out)
+        store_sides(core, u_ref, edge_ref)
         return
     for i in range(across // 2):
         for z, (one, two) in enumerate(zip(values(2 * i), values(2 * i + 1))):
@@ -566,7 +586,6 @@
             edge,
             edge,
             shape_of(depth, RADIUS, along, BF16),
-            shape_of(depth, across, 2 * EDGE, BF16),
         ]
     else:
         out_shape = [shape_of(depth, across // 2, along, BF16)] * 2
@@ -650,7 +669,7 @@
     return ref[:count].astype(F32), tail[:8] + tail[8:]
 
 
-def rows_body(slabs, count, keep_ref, got_ref, own_ref, *outs):
+def split_rows_body(slabs, count, keep_ref, got_ref, own_ref, *outs):
     slab = lax.axis_index("slab")
     size = slabs * count
     tail = keep_ref[pl.ds(size, 8)] + got_ref[pl.ds(size, 8)]
@@ -670,7 +689,7 @@
     own = jax.ShapeDtypeStruct((count + 8, keep.shape[1]), F32)
     sent = jax.ShapeDtypeStruct((count + 16, keep.shape[1]), BF16)
     return call(
-        functools.partial(rows_body, slabs, count),
+        functools.partial(split_rows_body, slabs, count),
         in_specs=whole_vmem(2),
         out_specs=whole_vmem(slabs),
         out_shape=[own] + [sent] * (slabs - 1),
@@ -827,12 +846,12 @@
     got = chip_swap(window)
     u, *edges = first_field(probes, 0, first_source, (window,))
     odd, even, beside = exchange(*edges)
-    base = local_step(u, beside, probes, 0, courant, source, 1, None)
-    shared_u, *edges, both = shared_first(probes, got, first_source, base)
+    shared_u, *edges, both = shared_first(probes, got, first_source)
     shared_odd, shared_even, shared_beside = exchange(*edges)
 
     previous = shared_previous = rows = None
     before = both
+    base = local_step(u, beside, probes, 0, courant, source, 1, None)
     for n in range(1, steps):
         last = n == steps - 1
         if last:
@@ -842,8 +861,8 @@
         else:
             previous, (u, *edges) = u, rim_step(base, odd, even, courant, "middle", (before,))
             odd, even, beside = exchange(*edges)
+            before = edges[-1]
             base = local_step(u, beside, probes, 0, courant, source, n + 1, previous)
-            before = base
         shared_base = shared_local(
             shared_u, shared_beside, both, courant, source, n, shared_previous
         )
@@ -852,10 +871,10 @@
             fields += wide_rim(*shared, "both", rows, (before,))
         else:
             shared_previous = shared_u
-            shared_u, *edges, rows = wide_rim(*shared, "middle", rows, (before,))
-            rows = chip_swap(rows)
-            before = rows if n == steps - 2 else edges[-1]
+            shared_u, *edges = wide_rim(*shared, "middle", rows, (before,))
             shared_odd, shared_even, shared_beside = exchange(*edges)
+            before = rows_of(shared_u, base)
+            rows = chip_swap(before)
     return coupled(fields, cell_count)
 
 

time: 101 us -> 101 us (level)
  waiting for transfers between devices: 36.1 us -> 34.1 us
  starting transfers between devices: 37.6 us -> 39.1 us
    ppermute x25, waiting for transfers between devices: 30.1 us -> 28.2 us  [swap(): lax.ppermute(x, axis, [p for a, b in pairs for p in ((a, b), (b, a))])]
    ppermute x25, starting transfers between devices: 33.8 us -> 35.5 us  [swap(): lax.ppermute(x, axis, [p for a, b in pairs for p in ((a, b), (b, a))])]
  transfers between devices with their start and end apart: 28 -> 28, of which waited for: 14 -> 10; matrix products, arithmetic and copies ran while one was open for 0% -> 0% of each run, Pallas kernels for 21% -> 22%
where the time goes in v17:
time: 101 us; the launch traced here: 100 us
  starting transfers between devices  39.1 us (39%)
  waiting for transfers between devices  34.1 us (34%)
  Pallas kernels  24.6 us (24%)
  local copies, waits for them, and re-layouts  1.42 us (1%)
  between operations  1.03 us (1%)
    ppermute x25, starting transfers between devices, swap(): lax.ppermute(x, axis, [p for a, b in pairs for p in ((a, b), (b, a))])  35.5 us
    ppermute x25, waiting for transfers between devices, swap(): lax.ppermute(x, axis, [p for a, b in pairs for p in ((a, b), (b, a))])  28.2 us
    pallas_call x3, Pallas kernels, shared_local(): call(functools.partial(shared_local_body, moment, previous is not None),...  7.27 us
    pallas_call x3, Pallas kernels, local_step(): call(functools.partial(local_body, chunk, moment, previous is not None),...  6.64 us
    ppermute x3, waiting for transfers between devices, coupled(): lax.ppermute(blocks[d - 1], 'slab', [(i, i ^ d) for i in range(slabs)])  5.85 us
    pallas_call x4, Pallas kernels, wide_rim(): call(functools.partial(wide_rim_body, kind, rows is not None, len(after))...  3.76 us
    ppermute x3, starting transfers between devices, coupled(): lax.ppermute(blocks[d - 1], 'slab', [(i, i ^ d) for i in range(slabs)])  3.55 us
    pallas_call x2, Pallas kernels, rim_step(): call(functools.partial(rim_body, kind, len(after)), in_specs=whole_vmem(4...  2.2 us
  transfers between devices with their start and end apart: 28, of which 10 were waited for; matrix products, arithmetic and copies ran while one was open for 0% of the time, Pallas kernels for 22%

profile of v17, /device:TPU:0, one launch (start us, length us, event | category | flops | bytes accessed | tf_op | source)
XLA Modules:
  0.0 100.2 jit_solution(10720373518989821359)
XLA Ops:
  0.6 1.4 %copy-done = bf16[8,8,48,256]{3,2,1,0:T(8,128)(2,1)S(1)} copy-done((bf16[8,8,48,256]{3,2,1,0:T(8,128)(2,1)S(1)}, bf16[8,8,48,256]{3,2,1,0:T(8,128)(2,1)}, u32[]{:S(2)}) %copy-start) | copy-done | bytes 1572888
  2.2 3.0 %collective-permute-start.3 = (bf16[8,8,32,128]{3,2,1,0:T(8,128)(2,1)S(1)}, bf16[8,8,32,128]{3,2,1,0:T(8,128)(2,1)S(1)}, u32[]{:S(2)}, u32[]{:S(2)}) collective-permute-start(bf16[8,8,32,128]{3,2,1,0:T(8,128)(2,1)S(1)} %shard_map.50.refs_0_), channel_id=1, source_target_pairs={{0,2},{2,0},{1,3},{3,1},{4,6},{6,4},{5,7},{7,5},{8,10},{10,8},{9,1... | collective-permute-start | bytes 1572872 | tf_op jit(solution)/shard_map/ppermute | solution.py:275
  7.0 4.4 %collective-permute-start.2 = (bf16[4,8,48,128]{3,2,1,0:T(8,128)(2,1)S(1)}, bf16[4,8,48,128]{3,2,1,0:T(8,128)(2,1)S(1)}, u32[]{:S(2)}, u32[]{:S(2)}) collective-permute-start(bf16[4,8,48,128]{3,2,1,0:T(8,128)(2,1)S(1)} %get-tuple-element.42), channel_id=1, source_target_pairs={{0,4},{4,0},{8,12},{12,8},{1,5},{5,1},{9,13},{13,9},{2,6},{6,2},{1... | collective-permute-start | bytes 1179656 | tf_op jit(solution)/shard_map/ppermute | solution.py:275
  11.5 5.6 %collective-permute-done.3.got_ref = bf16[8,8,32,128]{3,2,1,0:T(8,128)(2,1)S(1)} collective-permute-done((bf16[8,8,32,128]{3,2,1,0:T(8,128)(2,1)S(1)}, bf16[8,8,32,128]{3,2,1,0:T(8,128)(2,1)S(1)}, u32[]{:S(2)}, u32[]{:S(2)}) %collective-permute-start.3) | collective-permute-done | bytes 524320 | tf_op jit(solution)/shard_map/ppermute | solution.py:275
  18.6 4.7 %collective-permute-start.9 = (bf16[4,8,48,128]{3,2,1,0:T(8,128)(2,1)S(1)}, bf16[4,8,48,128]{3,2,1,0:T(8,128)(2,1)S(1)}, u32[]{:S(2)}, u32[]{:S(2)}) collective-permute-start(bf16[4,8,48,128]{3,2,1,0:T(8,128)(2,1)S(1)} %get-tuple-element.51), channel_id=1, source_target_pairs={{0,4},{4,0},{8,12},{12,8},{1,5},{5,1},{9,13},{13,9},{2,6},{6,2},{1... | collective-permute-start | bytes 1179656 | tf_op jit(solution)/shard_map/ppermute | solution.py:275
  23.3 2.1 %shard_map.52.refs_0_ = f32[8,8,48,128]{3,2,1,0:T(8,128)S(1)} custom-call(f32[8,8,64,128]{3,2,1,0:T(8,128)S(1)} %get-tuple-element.39.refs_0_.refs_5_, bf16[8,4,48,128]{3,2,1,0:T(8,128)(2,1)S(1)} %collective-permute-done.refs_1_, bf16[8,8,48,256]{3,2,1,0:T(8,128)(2,1)S(1)} %copy-done, f32[64,48]{1,0:T(8,128)S(1)} %bitcast.11, f32[4,64,48]{2,1,0:T(8,128)S(1)} %bitcast.5), custom_call_target="tpu_custom_call" | custom-call | flops 1 | bytes 1 | tf_op jit(solution)/shard_map/pallas_call | solution.py:190
  27.4 1.9 %collective-permute-start.6 = (bf16[4,8,48,128]{3,2,1,0:T(8,128)(2,1)S(1)}, bf16[4,8,48,128]{3,2,1,0:T(8,128)(2,1)S(1)}, u32[]{:S(2)}, u32[]{:S(2)}) collective-permute-start(bf16[4,8,48,128]{3,2,1,0:T(8,128)(2,1)S(1)} %get-tuple-element.47), channel_id=1, source_target_pairs={{0,4},{4,0},{8,12},{12,8},{1,5},{5,1},{9,13},{13,9},{2,6},{6,2},{1... | collective-permute-start | bytes 1179656 | tf_op jit(solution)/shard_map/ppermute | solution.py:275
  29.3 2.3 %shard_map.56.refs_0_ = f32[8,8,48,128]{3,2,1,0:T(8,128)S(1)} custom-call(f32[8,8,80,128]{3,2,1,0:T(8,128)S(1)} %get-tuple-element.48.refs_0_.refs_5_, bf16[8,4,48,128]{3,2,1,0:T(8,128)(2,1)S(1)} %collective-permute-done.7.refs_1_, bf16[8,8,48,128]{3,2,1,0:T(8,128)(2,1)S(1)} %get-tuple-element.43.refs_4_.refs_2_, f32[64,48]{1,0:T(8,128)S(1)} %bitcast.13, ...), custom_call_target="tpu_custom_call" | custom-call | flops 1 | bytes 1 | tf_op jit(solution)/shard_map/pallas_call | solution.py:480
  31.7 1.5 %collective-permute-done.9.refs_3_ = bf16[4,8,48,128]{3,2,1,0:T(8,128)(2,1)S(1)} collective-permute-done((bf16[4,8,48,128]{3,2,1,0:T(8,128)(2,1)S(1)}, bf16[4,8,48,128]{3,2,1,0:T(8,128)(2,1)S(1)}, u32[]{:S(2)}, u32[]{:S(2)}) %collective-permute-start.9) | collective-permute-done | bytes 393248 | tf_op jit(solution)/shard_map/ppermute | solution.py:275
  34.1 2.3 %shard_map.55._.refs_0_ = f32[8,8,48,128]{3,2,1,0:T(8,128)S(1)} custom-call(f32[8,8,64,128]{3,2,1,0:T(8,128)S(1)} %get-tuple-element.44.refs_0_.refs_5_, bf16[8,4,48,128]{3,2,1,0:T(8,128)(2,1)S(1)} %collective-permute-done.4.refs_1_, bf16[8,8,48,256]{3,2,1,0:T(8,128)(2,1)S(1)} %copy-done.1, f32[64,48]{1,0:T(8,128)S(1)} %bitcast.15, ...), custom_call_target="tpu_custom_call" | custom-call | flops 1 | bytes 1 | tf_op jit(solution)/shard_map/pallas_call | solution.py:190
  36.5 1.6 %collective-permute-start.16 = (bf16[8,8,16,128]{3,2,1,0:T(8,128)(2,1)S(1)}, bf16[8,8,16,128]{3,2,1,0:T(8,128)(2,1)S(1)}, u32[]{:S(2)}, u32[]{:S(2)}) collective-permute-start(bf16[8,8,16,128]{3,2,1,0:T(8,128)(2,1)S(1)} %shard_map.58.refs_4_), channel_id=1, source_target_pairs={{0,2},{2,0},{1,3},{3,1},{4,6},{6,4},{5,7},{7,5},{8,10},{10,8},{9,1... | collective-permute-start | bytes 786440 | tf_op jit(solution)/shard_map/ppermute | solution.py:275
  38.8 3.8 %collective-permute-start.15 = (bf16[4,8,48,128]{3,2,1,0:T(8,128)(2,1)S(1)}, bf16[4,8,48,128]{3,2,1,0:T(8,128)(2,1)S(1)}, u32[]{:S(2)}, u32[]{:S(2)}) collective-permute-start(bf16[4,8,48,128]{3,2,1,0:T(8,128)(2,1)S(1)} %get-tuple-element.59), channel_id=1, source_target_pairs={{0,4},{4,0},{8,12},{12,8},{1,5},{5,1},{9,13},{13,9},{2,6},{6,2},{1... | collective-permute-start | bytes 1179656 | tf_op jit(solution)/shard_map/ppermute | solution.py:275
  43.7 1.5 %collective-permute-done.16.refs_4_ = bf16[8,8,16,128]{3,2,1,0:T(8,128)(2,1)S(1)} collective-permute-done((bf16[8,8,16,128]{3,2,1,0:T(8,128)(2,1)S(1)}, bf16[8,8,16,128]{3,2,1,0:T(8,128)(2,1)S(1)}, u32[]{:S(2)}, u32[]{:S(2)}) %collective-permute-start.16) | collective-permute-done | bytes 262176 | tf_op jit(solution)/shard_map/ppermute | solution.py:275
  45.9 3.8 %collective-permute-start.12 = (bf16[4,8,48,128]{3,2,1,0:T(8,128)(2,1)S(1)}, bf16[4,8,48,128]{3,2,1,0:T(8,128)(2,1)S(1)}, u32[]{:S(2)}, u32[]{:S(2)}) collective-permute-start(bf16[4,8,48,128]{3,2,1,0:T(8,128)(2,1)S(1)} %get-tuple-element.56), channel_id=1, source_target_pairs={{0,4},{4,0},{8,12},{12,8},{1,5},{5,1},{9,13},{13,9},{2,6},{6,2},{1... | collective-permute-start | bytes 1179656 | tf_op jit(solution)/shard_map/ppermute | solution.py:275
  49.7 2.5 %shard_map.61.refs_0_ = f32[8,8,48,128]{3,2,1,0:T(8,128)S(1)} custom-call(f32[8,8,80,128]{3,2,1,0:T(8,128)S(1)} %get-tuple-element.52.u_ref.refs_0_.refs_5_, bf16[8,4,48,128]{3,2,1,0:T(8,128)(2,1)S(1)} %collective-permute-done.13.refs_1_, bf16[8,8,48,128]{3,2,1,0:T(8,128)(2,1)S(1)} %get-tuple-element.43.refs_4_.refs_2_, f32[64,48]{1,0:T(8,128)S(1)} %bitcast.17, ...), custom_call_target="tpu_custom_call" | custom-call | flops 1 | bytes 1 | tf_op jit(solution)/shard_map/pallas_call | solution.py:480
  54.7 4.9 %collective-permute-start.20 = (bf16[4,8,48,128]{3,2,1,0:T(8,128)(2,1)S(1)}, bf16[4,8,48,128]{3,2,1,0:T(8,128)(2,1)S(1)}, u32[]{:S(2)}, u32[]{:S(2)}) collective-permute-start(bf16[4,8,48,128]{3,2,1,0:T(8,128)(2,1)S(1)} %get-tuple-element.65), channel_id=1, source_target_pairs={{0,4},{4,0},{8,12},{12,8},{1,5},{5,1},{9,13},{13,9},{2,6},{6,2},{1... | collective-permute-start | bytes 1179656 | tf_op jit(solution)/shard_map/ppermute | solution.py:275
  59.6 2.2 %shard_map.60._.refs_0_ = f32[8,8,48,128]{3,2,1,0:T(8,128)S(1)} custom-call(f32[8,8,64,128]{3,2,1,0:T(8,128)S(1)} %get-tuple-element.53.refs_0_, bf16[8,4,48,128]{3,2,1,0:T(8,128)(2,1)S(1)} %collective-permute-done.10.refs_1_, bf16[8,8,48,256]{3,2,1,0:T(8,128)(2,1)S(1)} %copy-done.1, f32[64,48]{1,0:T(8,128)S(1)} %bitcast.19, f32[4,64,48]{2,1,0:T(8,128)S(1)} %bitcast.9, ...), custom_call_target="tpu_custom_call" | custom-call | flops 1 | bytes 1 | tf_op jit(solution)/shard_map/pallas_call | solution.py:190
  62.9 1.9 %collective-permute-start.21 = (bf16[8,8,16,128]{3,2,1,0:T(8,128)(2,1)S(1)}, bf16[8,8,16,128]{3,2,1,0:T(8,128)(2,1)S(1)}, u32[]{:S(2)}, u32[]{:S(2)}) collective-permute-start(bf16[8,8,16,128]{3,2,1,0:T(8,128)(2,1)S(1)} %shard_map.63.refs_4_), channel_id=1, source_target_pairs={{0,2},{2,0},{1,3},{3,1},{4,6},{6,4},{5,7},{7,5},{8,10},{10,8},{9,1... | collective-permute-start | bytes 786440 | tf_op jit(solution)/shard_map/ppermute | solution.py:275
  64.8 2.5 %shard_map.65.refs_0_ = f32[8,8,48,128]{3,2,1,0:T(8,128)S(1)} custom-call(f32[8,8,80,128]{3,2,1,0:T(8,128)S(1)} %get-tuple-element.60.u_ref.refs_0_, bf16[8,4,48,128]{3,2,1,0:T(8,128)(2,1)S(1)} %collective-permute-done.18.refs_1_, bf16[8,8,48,128]{3,2,1,0:T(8,128)(2,1)S(1)} %get-tuple-element.43.refs_4_.refs_2_, f32[64,48]{1,0:T(8,128)S(1)} %bitcast.21, ...), custom_call_target="tpu_custom_call" | custom-call | flops 1 | bytes 1 | tf_op jit(solution)/shard_map/pallas_call | solution.py:480
  67.3 12.1 %collective-permute-done.21.refs_4_ = bf16[8,8,16,128]{3,2,1,0:T(8,128)(2,1)S(1)} collective-permute-done((bf16[8,8,16,128]{3,2,1,0:T(8,128)(2,1)S(1)}, bf16[8,8,16,128]{3,2,1,0:T(8,128)(2,1)S(1)}, u32[]{:S(2)}, u32[]{:S(2)}) %collective-permute-start.21) | collective-permute-done | bytes 262176 | tf_op jit(solution)/shard_map/ppermute | solution.py:275
  81.7 1.9 %collective-permute-done.22.got_ref = f32[520,256]{1,0:T(8,128)S(1)} collective-permute-done((f32[520,256]{1,0:T(8,128)S(1)}, f32[520,256]{1,0:T(8,128)S(1)}, u32[]{:S(2)}, u32[]{:S(2)}) %collective-permute-start.22) | collective-permute-done | bytes 532512 | tf_op jit(solution)/shard_map/ppermute | solution.py:275
  84.0 2.5 %collective-permute-start.24 = (bf16[144,256]{1,0:T(8,128)(2,1)S(1)}, bf16[144,256]{1,0:T(8,128)(2,1)S(1)}, u32[]{:S(2)}, u32[]{:S(2)}) collective-permute-start(bf16[144,256]{1,0:T(8,128)(2,1)S(1)} %get-tuple-element.72), channel_id=1, source_target_pairs={{0,12},{4,8},{8,4},{12,0},{1,13},{5,9},{9,5},{13,1},{2,14},{6,10},... | collective-permute-start | bytes 221192 | tf_op jit(solution)/shard_map/ppermute | solution.py:778
  87.3 4.7 %collective-permute-done.23.refs_0_ = bf16[144,256]{1,0:T(8,128)(2,1)S(1)} collective-permute-done((bf16[144,256]{1,0:T(8,128)(2,1)S(1)}, bf16[144,256]{1,0:T(8,128)(2,1)S(1)}, u32[]{:S(2)}, u32[]{:S(2)}) %collective-permute-start.23) | collective-permute-done | bytes 73760 | tf_op jit(solution)/shard_map/ppermute | solution.py:778
  93.6 3.9 %collective-permute-done.26.other_ref = bf16[144,256]{1,0:T(8,128)(2,1)S(1)} collective-permute-done((bf16[144,256]{1,0:T(8,128)(2,1)S(1)}, bf16[144,256]{1,0:T(8,128)(2,1)S(1)}, u32[]{:S(2)}, u32[]{:S(2)}) %collective-permute-start.26) | collective-permute-done | bytes 73760 | tf_op jit(solution)/shard_map/ppermute | solution.py:275
  (63 shorter events, 20.0 us)
Async XLA Ops:
  2.2 14.9 %collective-permute-start.3 = (bf16[8,8,32,128]{3,2,1,0:T(8,128)(2,1)S(1)}, bf16[8,8,32,128]{3,2,1,0:T(8,128)(2,1)S(1)}, u32[]{:S(2)}, u32[]{:S(2)}) collective-permute-start(bf16[8,8,32,128]{3,2,1,0:T(8,128)(2,1)S(1)} %shard_map.50.refs_0_), channel_id=1, source_target_pairs={{0,2},{2,0},{1,3},{3,1},{4,6},{6,4},{5,7},{7,5},{8,10},{10,8},{9,1... | collective-permute-start | bytes 1572872 | tf_op jit(solution)/shard_map/ppermute | solution.py:275
  6.3 12.4 %collective-permute-start = (bf16[8,4,48,128]{3,2,1,0:T(8,128)(2,1)S(1)}, bf16[8,4,48,128]{3,2,1,0:T(8,128)(2,1)S(1)}, u32[]{:S(2)}, u32[]{:S(2)}) collective-permute-start(bf16[8,4,48,128]{3,2,1,0:T(8,128)(2,1)S(1)} %get-tuple-element.40), channel_id=1, source_target_pairs={{0,1},{1,0},{2,3},{3,2},{4,5},{5,4},{6,7},{7,6},{8,9},{9,8},{10,11... | collective-permute-start | bytes 1179656 | tf_op jit(solution)/shard_map/ppermute | solution.py:275
  6.3 19.1 %collective-permute-start.1 = (bf16[4,8,48,128]{3,2,1,0:T(8,128)(2,1)S(1)}, bf16[4,8,48,128]{3,2,1,0:T(8,128)(2,1)S(1)}, u32[]{:S(2)}, u32[]{:S(2)}) collective-permute-start(bf16[4,8,48,128]{3,2,1,0:T(8,128)(2,1)S(1)} %get-tuple-element.41), channel_id=1, source_target_pairs={{4,8},{8,4},{5,9},{9,5},{6,10},{10,6},{7,11},{11,7},{20,24},{24,20... | collective-permute-start | bytes 1179656 | tf_op jit(solution)/shard_map/ppermute | solution.py:275
  7.0 18.5 %collective-permute-start.2 = (bf16[4,8,48,128]{3,2,1,0:T(8,128)(2,1)S(1)}, bf16[4,8,48,128]{3,2,1,0:T(8,128)(2,1)S(1)}, u32[]{:S(2)}, u32[]{:S(2)}) collective-permute-start(bf16[4,8,48,128]{3,2,1,0:T(8,128)(2,1)S(1)} %get-tuple-element.42), channel_id=1, source_target_pairs={{0,4},{4,0},{8,12},{12,8},{1,5},{5,1},{9,13},{13,9},{2,6},{6,2},{1... | collective-permute-start | bytes 1179656 | tf_op jit(solution)/shard_map/ppermute | solution.py:275
  17.9 9.5 %collective-permute-start.7 = (bf16[8,4,48,128]{3,2,1,0:T(8,128)(2,1)S(1)}, bf16[8,4,48,128]{3,2,1,0:T(8,128)(2,1)S(1)}, u32[]{:S(2)}, u32[]{:S(2)}) collective-permute-start(bf16[8,4,48,128]{3,2,1,0:T(8,128)(2,1)S(1)} %get-tuple-element.49), channel_id=1, source_target_pairs={{0,1},{1,0},{2,3},{3,2},{4,5},{5,4},{6,7},{7,6},{8,9},{9,8},{10,11... | collective-permute-start | bytes 1179656 | tf_op jit(solution)/shard_map/ppermute | solution.py:275
  17.9 13.8 %collective-permute-start.8 = (bf16[4,8,48,128]{3,2,1,0:T(8,128)(2,1)S(1)}, bf16[4,8,48,128]{3,2,1,0:T(8,128)(2,1)S(1)}, u32[]{:S(2)}, u32[]{:S(2)}) collective-permute-start(bf16[4,8,48,128]{3,2,1,0:T(8,128)(2,1)S(1)} %get-tuple-element.50), channel_id=1, source_target_pairs={{4,8},{8,4},{5,9},{9,5},{6,10},{10,6},{7,11},{11,7},{20,24},{24,20... | collective-permute-start | bytes 1179656 | tf_op jit(solution)/shard_map/ppermute | solution.py:275
  18.6 14.6 %collective-permute-start.9 = (bf16[4,8,48,128]{3,2,1,0:T(8,128)(2,1)S(1)}, bf16[4,8,48,128]{3,2,1,0:T(8,128)(2,1)S(1)}, u32[]{:S(2)}, u32[]{:S(2)}) collective-permute-start(bf16[4,8,48,128]{3,2,1,0:T(8,128)(2,1)S(1)} %get-tuple-element.51), channel_id=1, source_target_pairs={{0,4},{4,0},{8,12},{12,8},{1,5},{5,1},{9,13},{13,9},{2,6},{6,2},{1... | collective-permute-start | bytes 1179656 | tf_op jit(solution)/shard_map/ppermute | solution.py:275
  26.6 7.5 %collective-permute-start.4 = (bf16[8,4,48,128]{3,2,1,0:T(8,128)(2,1)S(1)}, bf16[8,4,48,128]{3,2,1,0:T(8,128)(2,1)S(1)}, u32[]{:S(2)}, u32[]{:S(2)}) collective-permute-start(bf16[8,4,48,128]{3,2,1,0:T(8,128)(2,1)S(1)} %get-tuple-element.45.refs_4_), channel_id=1, source_target_pairs={{0,1},{1,0},{2,3},{3,2},{4,5},{5,4},{6,7},{7,6},{8,9},{9,8},{10,11... | collective-permute-start | bytes 1179656 | tf_op jit(solution)/shard_map/ppermute | solution.py:275
  26.7 12.1 %collective-permute-start.5 = (bf16[4,8,48,128]{3,2,1,0:T(8,128)(2,1)S(1)}, bf16[4,8,48,128]{3,2,1,0:T(8,128)(2,1)S(1)}, u32[]{:S(2)}, u32[]{:S(2)}) collective-permute-start(bf16[4,8,48,128]{3,2,1,0:T(8,128)(2,1)S(1)} %get-tuple-element.46), channel_id=1, source_target_pairs={{4,8},{8,4},{5,9},{9,5},{6,10},{10,6},{7,11},{11,7},{20,24},{24,20... | collective-permute-start | bytes 1179656 | tf_op jit(solution)/shard_map/ppermute | solution.py:275
  27.4 15.2 %collective-permute-start.6 = (bf16[4,8,48,128]{3,2,1,0:T(8,128)(2,1)S(1)}, bf16[4,8,48,128]{3,2,1,0:T(8,128)(2,1)S(1)}, u32[]{:S(2)}, u32[]{:S(2)}) collective-permute-start(bf16[4,8,48,128]{3,2,1,0:T(8,128)(2,1)S(1)} %get-tuple-element.47), channel_id=1, source_target_pairs={{0,4},{4,0},{8,12},{12,8},{1,5},{5,1},{9,13},{13,9},{2,6},{6,2},{1... | collective-permute-start | bytes 1179656 | tf_op jit(solution)/shard_map/ppermute | solution.py:275
  34.0 11.9 %collective-permute-start.13 = (bf16[8,4,48,128]{3,2,1,0:T(8,128)(2,1)S(1)}, bf16[8,4,48,128]{3,2,1,0:T(8,128)(2,1)S(1)}, u32[]{:S(2)}, u32[]{:S(2)}) collective-permute-start(bf16[8,4,48,128]{3,2,1,0:T(8,128)(2,1)S(1)} %get-tuple-element.57), channel_id=1, source_target_pairs={{0,1},{1,0},{2,3},{3,2},{4,5},{5,4},{6,7},{7,6},{8,9},{9,8},{10,11... | collective-permute-start | bytes 1179656 | tf_op jit(solution)/shard_map/ppermute | solution.py:275
  36.5 8.8 %collective-permute-start.16 = (bf16[8,8,16,128]{3,2,1,0:T(8,128)(2,1)S(1)}, bf16[8,8,16,128]{3,2,1,0:T(8,128)(2,1)S(1)}, u32[]{:S(2)}, u32[]{:S(2)}) collective-permute-start(bf16[8,8,16,128]{3,2,1,0:T(8,128)(2,1)S(1)} %shard_map.58.refs_4_), channel_id=1, source_target_pairs={{0,2},{2,0},{1,3},{3,1},{4,6},{6,4},{5,7},{7,5},{8,10},{10,8},{9,1... | collective-permute-start | bytes 786440 | tf_op jit(solution)/shard_map/ppermute | solution.py:275
  38.1 14.2 %collective-permute-start.14 = (bf16[4,8,48,128]{3,2,1,0:T(8,128)(2,1)S(1)}, bf16[4,8,48,128]{3,2,1,0:T(8,128)(2,1)S(1)}, u32[]{:S(2)}, u32[]{:S(2)}) collective-permute-start(bf16[4,8,48,128]{3,2,1,0:T(8,128)(2,1)S(1)} %get-tuple-element.58), channel_id=1, source_target_pairs={{4,8},{8,4},{5,9},{9,5},{6,10},{10,6},{7,11},{11,7},{20,24},{24,20... | collective-permute-start | bytes 1179656 | tf_op jit(solution)/shard_map/ppermute | solution.py:275
  38.8 13.7 %collective-permute-start.15 = (bf16[4,8,48,128]{3,2,1,0:T(8,128)(2,1)S(1)}, bf16[4,8,48,128]{3,2,1,0:T(8,128)(2,1)S(1)}, u32[]{:S(2)}, u32[]{:S(2)}) collective-permute-start(bf16[4,8,48,128]{3,2,1,0:T(8,128)(2,1)S(1)} %get-tuple-element.59), channel_id=1, source_target_pairs={{0,4},{4,0},{8,12},{12,8},{1,5},{5,1},{9,13},{13,9},{2,6},{6,2},{1... | collective-permute-start | bytes 1179656 | tf_op jit(solution)/shard_map/ppermute | solution.py:275
  43.7 11.0 %collective-permute-start.10 = (bf16[8,4,48,128]{3,2,1,0:T(8,128)(2,1)S(1)}, bf16[8,4,48,128]{3,2,1,0:T(8,128)(2,1)S(1)}, u32[]{:S(2)}, u32[]{:S(2)}) collective-permute-start(bf16[8,4,48,128]{3,2,1,0:T(8,128)(2,1)S(1)} %get-tuple-element.54.refs_5_), channel_id=1, source_target_pairs={{0,1},{1,0},{2,3},{3,2},{4,5},{5,4},{6,7},{7,6},{8,9},{9,8},{10,11... | collective-permute-start | bytes 1179656 | tf_op jit(solution)/shard_map/ppermute | solution.py:275
  45.2 16.7 %collective-permute-start.11 = (bf16[4,8,48,128]{3,2,1,0:T(8,128)(2,1)S(1)}, bf16[4,8,48,128]{3,2,1,0:T(8,128)(2,1)S(1)}, u32[]{:S(2)}, u32[]{:S(2)}) collective-permute-start(bf16[4,8,48,128]{3,2,1,0:T(8,128)(2,1)S(1)} %get-tuple-element.55), channel_id=1, source_target_pairs={{4,8},{8,4},{5,9},{9,5},{6,10},{10,6},{7,11},{11,7},{20,24},{24,20... | collective-permute-start | bytes 1179656 | tf_op jit(solution)/shard_map/ppermute | solution.py:275
  45.9 16.0 %collective-permute-start.12 = (bf16[4,8,48,128]{3,2,1,0:T(8,128)(2,1)S(1)}, bf16[4,8,48,128]{3,2,1,0:T(8,128)(2,1)S(1)}, u32[]{:S(2)}, u32[]{:S(2)}) collective-permute-start(bf16[4,8,48,128]{3,2,1,0:T(8,128)(2,1)S(1)} %get-tuple-element.56), channel_id=1, source_target_pairs={{0,4},{4,0},{8,12},{12,8},{1,5},{5,1},{9,13},{13,9},{2,6},{6,2},{1... | collective-permute-start | bytes 1179656 | tf_op jit(solution)/shard_map/ppermute | solution.py:275
  53.7 11.1 %collective-permute-start.18 = (bf16[8,4,48,128]{3,2,1,0:T(8,128)(2,1)S(1)}, bf16[8,4,48,128]{3,2,1,0:T(8,128)(2,1)S(1)}, u32[]{:S(2)}, u32[]{:S(2)}) collective-permute-start(bf16[8,4,48,128]{3,2,1,0:T(8,128)(2,1)S(1)} %get-tuple-element.63), channel_id=1, source_target_pairs={{0,1},{1,0},{2,3},{3,2},{4,5},{5,4},{6,7},{7,6},{8,9},{9,8},{10,11... | collective-permute-start | bytes 1179656 | tf_op jit(solution)/shard_map/ppermute | solution.py:275
  53.8 25.6 %collective-permute-start.19 = (bf16[4,8,48,128]{3,2,1,0:T(8,128)(2,1)S(1)}, bf16[4,8,48,128]{3,2,1,0:T(8,128)(2,1)S(1)}, u32[]{:S(2)}, u32[]{:S(2)}) collective-permute-start(bf16[4,8,48,128]{3,2,1,0:T(8,128)(2,1)S(1)} %get-tuple-element.64), channel_id=1, source_target_pairs={{4,8},{8,4},{5,9},{9,5},{6,10},{10,6},{7,11},{11,7},{20,24},{24,20... | collective-permute-start | bytes 1179656 | tf_op jit(solution)/shard_map/ppermute | solution.py:275
  54.7 24.7 %collective-permute-start.20 = (bf16[4,8,48,128]{3,2,1,0:T(8,128)(2,1)S(1)}, bf16[4,8,48,128]{3,2,1,0:T(8,128)(2,1)S(1)}, u32[]{:S(2)}, u32[]{:S(2)}) collective-permute-start(bf16[4,8,48,128]{3,2,1,0:T(8,128)(2,1)S(1)} %get-tuple-element.65), channel_id=1, source_target_pairs={{0,4},{4,0},{8,12},{12,8},{1,5},{5,1},{9,13},{13,9},{2,6},{6,2},{1... | collective-permute-start | bytes 1179656 | tf_op jit(solution)/shard_map/ppermute | solution.py:275
  62.7 17.6 %collective-permute-start.17 = (bf16[8,4,48,128]{3,2,1,0:T(8,128)(2,1)S(1)}, bf16[8,4,48,128]{3,2,1,0:T(8,128)(2,1)S(1)}, u32[]{:S(2)}, u32[]{:S(2)}) collective-permute-start(bf16[8,4,48,128]{3,2,1,0:T(8,128)(2,1)S(1)} %get-tuple-element.62), channel_id=1, source_target_pairs={{0,2},{2,0},{1,3},{3,1},{4,6},{6,4},{5,7},{7,5},{8,10},{10,8},{9,1... | collective-permute-start | bytes 1179656 | tf_op jit(solution)/shard_map/ppermute | solution.py:275
  62.9 16.4 %collective-permute-start.21 = (bf16[8,8,16,128]{3,2,1,0:T(8,128)(2,1)S(1)}, bf16[8,8,16,128]{3,2,1,0:T(8,128)(2,1)S(1)}, u32[]{:S(2)}, u32[]{:S(2)}) collective-permute-start(bf16[8,8,16,128]{3,2,1,0:T(8,128)(2,1)S(1)} %shard_map.63.refs_4_), channel_id=1, source_target_pairs={{0,2},{2,0},{1,3},{3,1},{4,6},{6,4},{5,7},{7,5},{8,10},{10,8},{9,1... | collective-permute-start | bytes 786440 | tf_op jit(solution)/shard_map/ppermute | solution.py:275
  83.7 8.3 %collective-permute-start.23 = (bf16[144,256]{1,0:T(8,128)(2,1)S(1)}, bf16[144,256]{1,0:T(8,128)(2,1)S(1)}, u32[]{:S(2)}, u32[]{:S(2)}) collective-permute-start(bf16[144,256]{1,0:T(8,128)(2,1)S(1)} %get-tuple-element.71), channel_id=1, source_target_pairs={{0,8},{4,12},{8,0},{12,4},{1,9},{5,13},{9,1},{13,5},{2,10},{6,14},... | collective-permute-start | bytes 221192 | tf_op jit(solution)/shard_map/ppermute | solution.py:778
  84.0 8.0 %collective-permute-start.24 = (bf16[144,256]{1,0:T(8,128)(2,1)S(1)}, bf16[144,256]{1,0:T(8,128)(2,1)S(1)}, u32[]{:S(2)}, u32[]{:S(2)}) collective-permute-start(bf16[144,256]{1,0:T(8,128)(2,1)S(1)} %get-tuple-element.72), channel_id=1, source_target_pairs={{0,12},{4,8},{8,4},{12,0},{1,13},{5,9},{9,5},{13,1},{2,14},{6,10},... | collective-permute-start | bytes 221192 | tf_op jit(solution)/shard_map/ppermute | solution.py:778
  (8 other events, 38.5 us)

commit v18 on v12

--- a/solution.py
+++ b/solution.py
@@ -189,6 +189,50 @@
         out_shape=shape_of(depth, across, along, F32),
         scratch_shapes=square_scratch() + square_scratch()[:1],
     )(*operands)
+
+
+def part_body(sent, base_ref, odd_ref, even_ref, c_ref, out_ref, square, turned_c):
+    depth, across, along, _ = base_ref.shape
+    even = slab_is_even()
+    turned_c[...] = turned(c_ref[...], square)
+
+    def planes(low):
+        def tile(start):
+            span = pl.ds(start, TILE)
+            courant = turned_c[span]
+            for x in range(across):
+                near = []
+                for j in range(RADIUS):
+                    one, two = even_ref[j, x, span], odd_ref[j, x, span]
+                    pair = (two, one) if low else (one, two)
+                    near.append(jnp.where(even, *pair).astype(F32))
+                for m in range(RADIUS):
+                    z = m if low else depth - RADIUS + m
+                    added = None
+                    for r in range(1, RADIUS + 1):
+                        at = RADIUS + m - r if low else m + r - RADIUS
+                        if 0 <= at < RADIUS:
+                            term = COEFFICIENTS[r] * near[at]
+                            added = term if added is None else added + term
+                    new = base_ref[z, x, span] + lane(courant, z * across + x) * added
+                    out_ref[m, x, span] = new.astype(BF16)
+
+        tiles(along, tile)
+
+    low = lax.axis_index("probe") == (1 if sent else 0)
+    pl.when(low)(lambda: planes(True))
+    pl.when(jnp.logical_not(low))(lambda: planes(False))
+
+
+def part_step(base, odds, evens, courant, sent):
+    _, across, along, _ = base.shape
+    return call(
+        functools.partial(part_body, sent),
+        in_specs=whole_vmem(4),
+        out_specs=whole_vmem(1)[0],
+        out_shape=shape_of(RADIUS, across, along, BF16),
+        scratch_shapes=square_scratch(),
+    )(base, odds, evens, courant)
 
 
 def rim_body(kind, *refs):
@@ -338,23 +382,23 @@
 
 
 def inner_sum_body(keep_ref, got_ref, tail_ref, own_ref, sent_ref):
-    size = sent_ref.shape[0]
-    total = keep_ref[:size] + got_ref[:size]
-    own_ref[...] = total
-    sent_ref[...] = total.astype(BF16)
+    size = 2 * LANES
+    row = pl.multiple_of(lax.rem(lax.axis_index("slab"), 2) * LANES, LANES)
+    own, other = pl.ds(row, LANES), pl.ds(LANES - row, LANES)
+    own_ref[...] = keep_ref[own] + got_ref[own]
+    sent_ref[...] = (keep_ref[other] + got_ref[other]).astype(BF16)
     tail_ref[...] = keep_ref[size:] + got_ref[size:]
 
 
 def inner_sum(keep, got):
-    size = keep.shape[0] - 8
     return call(
         inner_sum_body,
         in_specs=whole_vmem(2),
         out_specs=whole_vmem(3),
         out_shape=[
             jax.ShapeDtypeStruct((8, LANES), F32),
-            jax.ShapeDtypeStruct((size, LANES), F32),
-            jax.ShapeDtypeStruct((size, LANES), BF16),
+            jax.ShapeDtypeStruct((LANES, LANES), F32),
+            jax.ShapeDtypeStruct((LANES, LANES), BF16),
         ],
     )(keep, got)
 
@@ -405,35 +449,33 @@
 def cross_rows_body(keep_ref, got_ref, tail_ref, inner_ref, inner_got_ref, own_ref, *outs):
     slab = lax.axis_index("slab")
     core = lax.axis_index("sub")
-    chip = lax.axis_index("probe")
     tail = tail_ref[...]
+    inner = inner_ref[...] + inner_got_ref[...].astype(F32)
     for d in range(len(outs) + 1):
         owner = slab ^ d
         late = jnp.where(core == 0, jnp.where(owner == 2, 0, 2), jnp.where(owner == 2, 2, 1))
         at = jnp.where(owner < 2, owner, late)
         span = pl.ds(pl.multiple_of(at * LANES, LANES), LANES)
         block = keep_ref[span] + got_ref[span]
-        row = pl.multiple_of(jnp.clip(owner - 2 * chip, 0, 1) * LANES, LANES)
-        inner = inner_ref[pl.ds(row, LANES)] + inner_got_ref[pl.ds(row, LANES)].astype(F32)
         if d == 0:
             own_ref[:LANES] = block
             own_ref[LANES : LANES + 8] = tail
             own_ref[LANES + 8 :] = inner
         else:
             rounded(outs[d - 1], block, tail)
-            if d == 1:
-                outs[0][LANES + 16 :] = inner.astype(BF16)
+            if d == 2:
+                outs[1][LANES + 16 :] = inner.astype(BF16)
 
 
 def cross_rows(keep, got, tail, inner, inner_got, slabs):
     own = jax.ShapeDtypeStruct((2 * LANES + 8, LANES), F32)
-    near = jax.ShapeDtypeStruct((2 * LANES + 16, LANES), BF16)
-    far = jax.ShapeDtypeStruct((LANES + 16, LANES), BF16)
+    long = jax.ShapeDtypeStruct((2 * LANES + 16, LANES), BF16)
+    short = jax.ShapeDtypeStruct((LANES + 16, LANES), BF16)
     return call(
         cross_rows_body,
         in_specs=whole_vmem(5),
         out_specs=whole_vmem(slabs),
-        out_shape=[own, near] + [far] * (slabs - 2),
+        out_shape=[own, short, long, short],
     )(keep, got, tail, inner, inner_got)
 
 
@@ -443,7 +485,7 @@
     for ref in others:
         more, more_tail = opened(ref, LANES)
         block, tail = block + more, tail + more_tail
-    inner = own_ref[LANES + 8 :] + others[-1][LANES + 16 :].astype(F32)
+    inner = own_ref[LANES + 8 :] + others[0][LANES + 16 :].astype(F32)
     rounded(out_ref, block, tail)
     out_ref[LANES + 16 :] = inner.astype(BF16)
 
@@ -453,7 +495,7 @@
         sum_body,
         in_specs=whole_vmem(1 + len(others)),
         out_specs=whole_vmem(1)[0],
-        out_shape=jax.ShapeDtypeStruct(others[-1].shape, BF16),
+        out_shape=jax.ShapeDtypeStruct(others[0].shape, BF16),
     )(own, *others)
 
 
@@ -519,11 +561,7 @@
     own = [field for kept, sent, _ in finals for field in (kept, sent)]
     keep, send = inner_gram(own)
     tail, inner, sent = inner_sum(keep, core_swap(send))
-    pairs = [
-        (2 * (k ^ 2) + chip, 2 * k + chip) for chip in range(2) for k in (2 * chip, 2 * chip + 1)
-    ]
-    inner_got = lax.ppermute(sent, ("slab", "probe"), pairs)
-
+    inner_got = lax.ppermute(sent, "slab", [(i, i ^ 1) for i in range(slabs)])
     pairs = [field for kept, _, got in finals for field in (kept, got)]
     keep, send = cross_gram(pairs, inner_got)
     mine, *blocks = cross_rows(keep, core_swap(send), tail, inner, inner_got, slabs)
@@ -584,7 +622,11 @@
                 previous[c], now[c] = now[c], u
                 halos[c] = exchange(*edges)
             elif paired:
-                kept, sent = rim_step(base, odd, even, courant, "half")
+                if c < chunks - 1:
+                    kept, sent = rim_step(base, odd, even, courant, "half")
+                else:
+                    sent = part_step(base, odd, even, courant, True)
+                    kept = part_step(base, odd, even, courant, False)
                 finals.append((kept, sent, chip_swap(sent)))
             else:
                 finals += rim_step(base, odd, even, courant, "all")

time: 92.8 us -> 91.9 us (level)
  waiting for transfers between devices: 27.8 us -> 26.7 us
    ppermute x1, waiting for transfers between devices: 7.16 us -> 2.17 us  [coupled(): inner_got = lax.ppermute(sent, 'slab', [(i, i ^ 1) for i in range(slabs)])]
    ppermute x24, waiting for transfers between devices: 17.4 us -> 20.2 us  [swap(): lax.ppermute(x, axis, [p for a, b in pairs for p in ((a, b), (b, a))])]
    pallas_call x0 -> x2, Pallas kernels: none -> 1.28 us  [part_step(): call(functools.partial(part_body, sent), in_specs=whole_vmem(4), out_spec...]
    ppermute x3, waiting for transfers between devices: 3.21 us -> 4.34 us  [coupled(): lax.ppermute(blocks[d - 1], 'slab', [(i, i ^ d) for i in range(slabs)])]
    pallas_call x6 -> x5, Pallas kernels: 6.31 us -> 5.35 us  [rim_step(): call(functools.partial(rim_body, kind), in_specs=whole_vmem(4), out_specs...]
  transfers between devices with their start and end apart: 28 -> 28, of which waited for: 13 -> 14; matrix products, arithmetic and copies ran while one was open for 0% -> 0% of each run, Pallas kernels for 23% -> 24%
where the time goes in v18:
time: 91.9 us; the launch traced here: 91.6 us
  starting transfers between devices  36.7 us (40%)
  waiting for transfers between devices  26.7 us (29%)
  Pallas kernels  25 us (27%)
  local copies, waits for them, and re-layouts  2.18 us (2%)
  between operations  0.99 us (1%)
    ppermute x24, starting transfers between devices, swap(): lax.ppermute(x, axis, [p for a, b in pairs for p in ((a, b), (b, a))])  31.1 us
    ppermute x24, waiting for transfers between devices, swap(): lax.ppermute(x, axis, [p for a, b in pairs for p in ((a, b), (b, a))])  20.2 us
    pallas_call x6, Pallas kernels, local_step(): call(functools.partial(local_body, chunk, moment, previous is not None),...  13.3 us
    pallas_call x5, Pallas kernels, rim_step(): call(functools.partial(rim_body, kind), in_specs=whole_vmem(4), out_specs...  5.35 us
    ppermute x3, waiting for transfers between devices, coupled(): lax.ppermute(blocks[d - 1], 'slab', [(i, i ^ d) for i in range(slabs)])  4.34 us
    ppermute x3, starting transfers between devices, coupled(): lax.ppermute(blocks[d - 1], 'slab', [(i, i ^ d) for i in range(slabs)])  3.85 us
    ppermute x1, waiting for transfers between devices, coupled(): inner_got = lax.ppermute(sent, 'slab', [(i, i ^ 1) for i in range(slabs)])  2.17 us
    pallas_call x2, Pallas kernels, first_field(): call(functools.partial(first_body, chunk), in_specs=whole_vmem(2), out_sp...  2.1 us
  transfers between devices with their start and end apart: 28, of which 14 were waited for; matrix products, arithmetic and copies ran while one was open for 0% of the time, Pallas kernels for 24%

profile of v18, /device:TPU:0, one launch (start us, length us, event | category | flops | bytes accessed | tf_op | source)
XLA Modules:
  0.0 91.6 jit_solution(2800956966434946689)
XLA Ops:
  5.1 5.5 %collective-permute-start.12 = (bf16[4,8,48,128]{3,2,1,0:T(8,128)(2,1)S(1)}, bf16[4,8,48,128]{3,2,1,0:T(8,128)(2,1)S(1)}, u32[]{:S(2)}, u32[]{:S(2)}) collective-permute-start(bf16[4,8,48,128]{3,2,1,0:T(8,128)(2,1)S(1)} %get-tuple-element.58), channel_id=1, source_target_pairs={{0,4},{4,0},{8,12},{12,8},{1,5},{5,1},{9,13},{13,9},{2,6},{6,2},{1... | collective-permute-start | bytes 1179656 | tf_op jit(solution)/shard_map/ppermute | solution.py:314
  12.4 1.9 %collective-permute-start.2 = (bf16[4,8,48,128]{3,2,1,0:T(8,128)(2,1)S(1)}, bf16[4,8,48,128]{3,2,1,0:T(8,128)(2,1)S(1)}, u32[]{:S(2)}, u32[]{:S(2)}) collective-permute-start(bf16[4,8,48,128]{3,2,1,0:T(8,128)(2,1)S(1)} %get-tuple-element.44), channel_id=1, source_target_pairs={{0,4},{4,0},{8,12},{12,8},{1,5},{5,1},{9,13},{13,9},{2,6},{6,2},{1... | collective-permute-start | bytes 1179656 | tf_op jit(solution)/shard_map/ppermute | solution.py:314
  14.3 2.1 %shard_map.58.refs_0_ = f32[8,8,48,128]{3,2,1,0:T(8,128)S(1)} custom-call(f32[8,8,64,128]{3,2,1,0:T(8,128)S(1)} %get-tuple-element.55.refs_0_.refs_5_, bf16[8,4,48,128]{3,2,1,0:T(8,128)(2,1)S(1)} %collective-permute-done.10.refs_1_, bf16[8,8,48,256]{3,2,1,0:T(8,128)(2,1)S(1)} %copy-done, f32[64,48]{1,0:T(8,128)S(1)} %bitcast.5, f32[4,64,48]{2,1,0:T(8,128)S(1)} %bitcast.18), custom_call_target="tpu_custom_call" | custom-call | flops 1 | bytes 1 | tf_op jit(solution)/shard_map/pallas_call | solution.py:185
  16.5 3.9 %collective-permute-done.12.refs_2_ = bf16[4,8,48,128]{3,2,1,0:T(8,128)(2,1)S(1)} collective-permute-done((bf16[4,8,48,128]{3,2,1,0:T(8,128)(2,1)S(1)}, bf16[4,8,48,128]{3,2,1,0:T(8,128)(2,1)S(1)}, u32[]{:S(2)}, u32[]{:S(2)}) %collective-permute-start.12) | collective-permute-done | bytes 393248 | tf_op jit(solution)/shard_map/ppermute | solution.py:314
  22.3 3.8 %collective-permute-start.15 = (bf16[4,8,48,128]{3,2,1,0:T(8,128)(2,1)S(1)}, bf16[4,8,48,128]{3,2,1,0:T(8,128)(2,1)S(1)}, u32[]{:S(2)}, u32[]{:S(2)}) collective-permute-start(bf16[4,8,48,128]{3,2,1,0:T(8,128)(2,1)S(1)} %get-tuple-element.62), channel_id=1, source_target_pairs={{0,4},{4,0},{8,12},{12,8},{1,5},{5,1},{9,13},{13,9},{2,6},{6,2},{1... | collective-permute-start | bytes 1179656 | tf_op jit(solution)/shard_map/ppermute | solution.py:314
  26.1 2.1 %shard_map.51.refs_0_ = f32[8,8,48,128]{3,2,1,0:T(8,128)S(1)} custom-call(f32[8,8,64,128]{3,2,1,0:T(8,128)S(1)} %get-tuple-element.41.refs_0_.refs_5_, bf16[8,4,48,128]{3,2,1,0:T(8,128)(2,1)S(1)} %collective-permute-done.refs_1_, bf16[8,8,48,256]{3,2,1,0:T(8,128)(2,1)S(1)} %copy-done.1, f32[64,48]{1,0:T(8,128)S(1)} %bitcast.7, f32[4,64,48]{2,1,0:T(8,128)S(1)} %bitcast.19), custom_call_target="tpu_custom_call" | custom-call | flops 1 | bytes 1 | tf_op jit(solution)/shard_map/pallas_call | solution.py:185
  30.7 3.4 %collective-permute-start.5 = (bf16[4,8,48,128]{3,2,1,0:T(8,128)(2,1)S(1)}, bf16[4,8,48,128]{3,2,1,0:T(8,128)(2,1)S(1)}, u32[]{:S(2)}, u32[]{:S(2)}) collective-permute-start(bf16[4,8,48,128]{3,2,1,0:T(8,128)(2,1)S(1)} %get-tuple-element.48), channel_id=1, source_target_pairs={{0,4},{4,0},{8,12},{12,8},{1,5},{5,1},{9,13},{13,9},{2,6},{6,2},{1... | collective-permute-start | bytes 1179656 | tf_op jit(solution)/shard_map/ppermute | solution.py:314
  34.1 2.3 %shard_map.60.refs_0_ = f32[8,8,48,128]{3,2,1,0:T(8,128)S(1)} custom-call(f32[8,8,64,128]{3,2,1,0:T(8,128)S(1)} %get-tuple-element.59.refs_0_.refs_5_, bf16[8,4,48,128]{3,2,1,0:T(8,128)(2,1)S(1)} %collective-permute-done.13.refs_1_, bf16[8,8,48,256]{3,2,1,0:T(8,128)(2,1)S(1)} %copy-done.1, f32[64,48]{1,0:T(8,128)S(1)} %bitcast.9, f32[4,64,48]{2,1,0:T(8,128)S(1)} %bitcast.20, ...), custom_call_target="tpu_custom_call" | custom-call | flops 1 | bytes 1 | tf_op jit(solution)/shard_map/pallas_call | solution.py:185
  39.2 3.4 %collective-permute-start.18 = (bf16[4,8,48,128]{3,2,1,0:T(8,128)(2,1)S(1)}, bf16[4,8,48,128]{3,2,1,0:T(8,128)(2,1)S(1)}, u32[]{:S(2)}, u32[]{:S(2)}) collective-permute-start(bf16[4,8,48,128]{3,2,1,0:T(8,128)(2,1)S(1)} %get-tuple-element.66), channel_id=1, source_target_pairs={{0,4},{4,0},{8,12},{12,8},{1,5},{5,1},{9,13},{13,9},{2,6},{6,2},{1... | collective-permute-start | bytes 1179656 | tf_op jit(solution)/shard_map/ppermute | solution.py:314
  42.5 2.2 %shard_map.53.refs_0_ = f32[8,8,48,128]{3,2,1,0:T(8,128)S(1)} custom-call(f32[8,8,64,128]{3,2,1,0:T(8,128)S(1)} %get-tuple-element.45.refs_0_.refs_5_, bf16[8,4,48,128]{3,2,1,0:T(8,128)(2,1)S(1)} %collective-permute-done.3.refs_1_, bf16[8,8,48,256]{3,2,1,0:T(8,128)(2,1)S(1)} %copy-done.1, f32[64,48]{1,0:T(8,128)S(1)} %bitcast.11, f32[4,64,48]{2,1,0:T(8,128)S(1)} %bitcast.21, ...), custom_call_target="tpu_custom_call" | custom-call | flops 1 | bytes 1 | tf_op jit(solution)/shard_map/pallas_call | solution.py:185
  47.6 3.4 %collective-permute-start.8 = (bf16[4,8,48,128]{3,2,1,0:T(8,128)(2,1)S(1)}, bf16[4,8,48,128]{3,2,1,0:T(8,128)(2,1)S(1)}, u32[]{:S(2)}, u32[]{:S(2)}) collective-permute-start(bf16[4,8,48,128]{3,2,1,0:T(8,128)(2,1)S(1)} %get-tuple-element.52), channel_id=1, source_target_pairs={{0,4},{4,0},{8,12},{12,8},{1,5},{5,1},{9,13},{13,9},{2,6},{6,2},{1... | collective-permute-start | bytes 1179656 | tf_op jit(solution)/shard_map/ppermute | solution.py:314
  50.9 2.3 %shard_map.62.base_ref = f32[8,8,48,128]{3,2,1,0:T(8,128)S(1)} custom-call(f32[8,8,64,128]{3,2,1,0:T(8,128)S(1)} %get-tuple-element.63.refs_0_, bf16[8,4,48,128]{3,2,1,0:T(8,128)(2,1)S(1)} %collective-permute-done.16.refs_1_, bf16[8,8,48,256]{3,2,1,0:T(8,128)(2,1)S(1)} %copy-done.1, f32[64,48]{1,0:T(8,128)S(1)} %bitcast.13, f32[4,64,48]{2,1,0:T(8,128)S(1)} %bitcast.22, ...), custom_call_target="tpu_custom_call" | custom-call | flops 1 | bytes 1 | tf_op jit(solution)/shard_map/pallas_call | solution.py:185
  54.8 1.6 %collective-permute-start.19 = (bf16[4,8,48,128]{3,2,1,0:T(8,128)(2,1)S(1)}, bf16[4,8,48,128]{3,2,1,0:T(8,128)(2,1)S(1)}, u32[]{:S(2)}, u32[]{:S(2)}) collective-permute-start(bf16[4,8,48,128]{3,2,1,0:T(8,128)(2,1)S(1)} %shard_map.64.sent1), channel_id=1, source_target_pairs={{0,2},{2,0},{1,3},{3,1},{4,6},{6,4},{5,7},{7,5},{8,10},{10,8},{9,1... | collective-permute-start | bytes 1179656 | tf_op jit(solution)/shard_map/ppermute | solution.py:314
  56.3 2.2 %shard_map.55.refs_0_ = f32[8,8,48,128]{3,2,1,0:T(8,128)S(1)} custom-call(f32[8,8,64,128]{3,2,1,0:T(8,128)S(1)} %get-tuple-element.49.refs_0_, bf16[8,4,48,128]{3,2,1,0:T(8,128)(2,1)S(1)} %collective-permute-done.6.refs_1_, bf16[8,8,48,256]{3,2,1,0:T(8,128)(2,1)S(1)} %copy-done.1, f32[64,48]{1,0:T(8,128)S(1)} %bitcast.15, f32[4,64,48]{2,1,0:T(8,128)S(1)} %bitcast.23, ...), custom_call_target="tpu_custom_call" | custom-call | flops 1 | bytes 1 | tf_op jit(solution)/shard_map/pallas_call | solution.py:185
  58.6 3.5 %collective-permute-done.8.refs_2_ = bf16[4,8,48,128]{3,2,1,0:T(8,128)(2,1)S(1)} collective-permute-done((bf16[4,8,48,128]{3,2,1,0:T(8,128)(2,1)S(1)}, bf16[4,8,48,128]{3,2,1,0:T(8,128)(2,1)S(1)}, u32[]{:S(2)}, u32[]{:S(2)}) %collective-permute-start.8) | collective-permute-done | bytes 393248 | tf_op jit(solution)/shard_map/ppermute | solution.py:314
  63.1 1.6 %collective-permute-start.9 = (bf16[4,8,48,128]{3,2,1,0:T(8,128)(2,1)S(1)}, bf16[4,8,48,128]{3,2,1,0:T(8,128)(2,1)S(1)}, u32[]{:S(2)}, u32[]{:S(2)}) collective-permute-start(bf16[4,8,48,128]{3,2,1,0:T(8,128)(2,1)S(1)} %get-tuple-element.54.sent0), channel_id=1, source_target_pairs={{0,2},{2,0},{1,3},{3,1},{4,6},{6,4},{5,7},{7,5},{8,10},{10,8},{9,1... | collective-permute-start | bytes 1179656 | tf_op jit(solution)/shard_map/ppermute | solution.py:314
  67.4 1.8 %collective-permute-start.21 = (bf16[128,128]{1,0:T(8,128)(2,1)S(1)}, bf16[128,128]{1,0:T(8,128)(2,1)S(1)}, u32[]{:S(2)}, u32[]{:S(2)}) collective-permute-start(bf16[128,128]{1,0:T(8,128)(2,1)S(1)} %get-tuple-element.69), channel_id=1, source_target_pairs={{0,4},{4,0},{8,12},{12,8},{1,5},{5,1},{9,13},{13,9},{2,6},{6,2},{1... | collective-permute-start | bytes 98312 | tf_op jit(solution)/shard_map/ppermute | solution.py:564
  69.2 2.2 %collective-permute-done.21._.inner_got_ref = bf16[128,128]{1,0:T(8,128)(2,1)S(1)} collective-permute-done((bf16[128,128]{1,0:T(8,128)(2,1)S(1)}, bf16[128,128]{1,0:T(8,128)(2,1)S(1)}, u32[]{:S(2)}, u32[]{:S(2)}) %collective-permute-start.21) | collective-permute-done | bytes 32800 | tf_op jit(solution)/shard_map/ppermute | solution.py:564
  71.4 2.5 %collective-permute-done.9.got0 = bf16[4,8,48,128]{3,2,1,0:T(8,128)(2,1)S(1)} collective-permute-done((bf16[4,8,48,128]{3,2,1,0:T(8,128)(2,1)S(1)}, bf16[4,8,48,128]{3,2,1,0:T(8,128)(2,1)S(1)}, u32[]{:S(2)}, u32[]{:S(2)}) %collective-permute-start.9) | collective-permute-done | bytes 393248 | tf_op jit(solution)/shard_map/ppermute | solution.py:314
  76.3 1.5 %collective-permute-start.23 = (bf16[272,128]{1,0:T(8,128)(2,1)S(1)}, bf16[272,128]{1,0:T(8,128)(2,1)S(1)}, u32[]{:S(2)}, u32[]{:S(2)}) collective-permute-start(bf16[272,128]{1,0:T(8,128)(2,1)S(1)} %get-tuple-element.75), channel_id=1, source_target_pairs={{0,8},{4,12},{8,0},{12,4},{1,9},{5,13},{9,1},{13,5},{2,10},{6,14},... | collective-permute-start | bytes 208904 | tf_op jit(solution)/shard_map/ppermute | solution.py:569
  77.9 2.3 %collective-permute-start.24 = (bf16[144,128]{1,0:T(8,128)(2,1)S(1)}, bf16[144,128]{1,0:T(8,128)(2,1)S(1)}, u32[]{:S(2)}, u32[]{:S(2)}) collective-permute-start(bf16[144,128]{1,0:T(8,128)(2,1)S(1)} %get-tuple-element.76), channel_id=1, source_target_pairs={{0,12},{4,8},{8,4},{12,0},{1,13},{5,9},{9,5},{13,1},{2,14},{6,10},... | collective-permute-start | bytes 110600 | tf_op jit(solution)/shard_map/ppermute | solution.py:569
  80.2 3.5 %collective-permute-done.24.refs_1_ = bf16[144,128]{1,0:T(8,128)(2,1)S(1)} collective-permute-done((bf16[144,128]{1,0:T(8,128)(2,1)S(1)}, bf16[144,128]{1,0:T(8,128)(2,1)S(1)}, u32[]{:S(2)}, u32[]{:S(2)}) %collective-permute-start.24) | collective-permute-done | bytes 36896 | tf_op jit(solution)/shard_map/ppermute | solution.py:569
  84.6 1.6 %collective-permute-start.26 = (bf16[272,128]{1,0:T(8,128)(2,1)S(1)}, bf16[272,128]{1,0:T(8,128)(2,1)S(1)}, u32[]{:S(2)}, u32[]{:S(2)}) collective-permute-start(bf16[272,128]{1,0:T(8,128)(2,1)S(1)} %shard_map.69.mine_ref), channel_id=1, source_target_pairs={{0,2},{2,0},{1,3},{3,1},{4,6},{6,4},{5,7},{7,5},{8,10},{10,8},{9,1... | collective-permute-start | bytes 208904 | tf_op jit(solution)/shard_map/ppermute | solution.py:314
  86.1 2.8 %collective-permute-done.26.other_ref = bf16[272,128]{1,0:T(8,128)(2,1)S(1)} collective-permute-done((bf16[272,128]{1,0:T(8,128)(2,1)S(1)}, bf16[272,128]{1,0:T(8,128)(2,1)S(1)}, u32[]{:S(2)}, u32[]{:S(2)}) %collective-permute-start.26) | collective-permute-done | bytes 69664 | tf_op jit(solution)/shard_map/ppermute | solution.py:314
  (63 shorter events, 27.3 us)
Async XLA Ops:
  3.9 8.5 %collective-permute-start.10 = (bf16[8,4,48,128]{3,2,1,0:T(8,128)(2,1)S(1)}, bf16[8,4,48,128]{3,2,1,0:T(8,128)(2,1)S(1)}, u32[]{:S(2)}, u32[]{:S(2)}) collective-permute-start(bf16[8,4,48,128]{3,2,1,0:T(8,128)(2,1)S(1)} %get-tuple-element.56), channel_id=1, source_target_pairs={{0,1},{1,0},{2,3},{3,2},{4,5},{5,4},{6,7},{7,6},{8,9},{9,8},{10,11... | collective-permute-start | bytes 1179656 | tf_op jit(solution)/shard_map/ppermute | solution.py:314
  4.4 12.1 %collective-permute-start.11 = (bf16[4,8,48,128]{3,2,1,0:T(8,128)(2,1)S(1)}, bf16[4,8,48,128]{3,2,1,0:T(8,128)(2,1)S(1)}, u32[]{:S(2)}, u32[]{:S(2)}) collective-permute-start(bf16[4,8,48,128]{3,2,1,0:T(8,128)(2,1)S(1)} %get-tuple-element.57), channel_id=1, source_target_pairs={{4,8},{8,4},{5,9},{9,5},{6,10},{10,6},{7,11},{11,7},{20,24},{24,20... | collective-permute-start | bytes 1179656 | tf_op jit(solution)/shard_map/ppermute | solution.py:314
  5.1 15.4 %collective-permute-start.12 = (bf16[4,8,48,128]{3,2,1,0:T(8,128)(2,1)S(1)}, bf16[4,8,48,128]{3,2,1,0:T(8,128)(2,1)S(1)}, u32[]{:S(2)}, u32[]{:S(2)}) collective-permute-start(bf16[4,8,48,128]{3,2,1,0:T(8,128)(2,1)S(1)} %get-tuple-element.58), channel_id=1, source_target_pairs={{0,4},{4,0},{8,12},{12,8},{1,5},{5,1},{9,13},{13,9},{2,6},{6,2},{1... | collective-permute-start | bytes 1179656 | tf_op jit(solution)/shard_map/ppermute | solution.py:314
  11.6 10.7 %collective-permute-start = (bf16[8,4,48,128]{3,2,1,0:T(8,128)(2,1)S(1)}, bf16[8,4,48,128]{3,2,1,0:T(8,128)(2,1)S(1)}, u32[]{:S(2)}, u32[]{:S(2)}) collective-permute-start(bf16[8,4,48,128]{3,2,1,0:T(8,128)(2,1)S(1)} %get-tuple-element.42), channel_id=1, source_target_pairs={{0,1},{1,0},{2,3},{3,2},{4,5},{5,4},{6,7},{7,6},{8,9},{9,8},{10,11... | collective-permute-start | bytes 1179656 | tf_op jit(solution)/shard_map/ppermute | solution.py:314
  11.7 16.6 %collective-permute-start.1 = (bf16[4,8,48,128]{3,2,1,0:T(8,128)(2,1)S(1)}, bf16[4,8,48,128]{3,2,1,0:T(8,128)(2,1)S(1)}, u32[]{:S(2)}, u32[]{:S(2)}) collective-permute-start(bf16[4,8,48,128]{3,2,1,0:T(8,128)(2,1)S(1)} %get-tuple-element.43), channel_id=1, source_target_pairs={{4,8},{8,4},{5,9},{9,5},{6,10},{10,6},{7,11},{11,7},{20,24},{24,20... | collective-permute-start | bytes 1179656 | tf_op jit(solution)/shard_map/ppermute | solution.py:314
  12.4 16.5 %collective-permute-start.2 = (bf16[4,8,48,128]{3,2,1,0:T(8,128)(2,1)S(1)}, bf16[4,8,48,128]{3,2,1,0:T(8,128)(2,1)S(1)}, u32[]{:S(2)}, u32[]{:S(2)}) collective-permute-start(bf16[4,8,48,128]{3,2,1,0:T(8,128)(2,1)S(1)} %get-tuple-element.44), channel_id=1, source_target_pairs={{0,4},{4,0},{8,12},{12,8},{1,5},{5,1},{9,13},{13,9},{2,6},{6,2},{1... | collective-permute-start | bytes 1179656 | tf_op jit(solution)/shard_map/ppermute | solution.py:314
  21.5 9.2 %collective-permute-start.13 = (bf16[8,4,48,128]{3,2,1,0:T(8,128)(2,1)S(1)}, bf16[8,4,48,128]{3,2,1,0:T(8,128)(2,1)S(1)}, u32[]{:S(2)}, u32[]{:S(2)}) collective-permute-start(bf16[8,4,48,128]{3,2,1,0:T(8,128)(2,1)S(1)} %get-tuple-element.60), channel_id=1, source_target_pairs={{0,1},{1,0},{2,3},{3,2},{4,5},{5,4},{6,7},{7,6},{8,9},{9,8},{10,11... | collective-permute-start | bytes 1179656 | tf_op jit(solution)/shard_map/ppermute | solution.py:314
  21.6 14.8 %collective-permute-start.14 = (bf16[4,8,48,128]{3,2,1,0:T(8,128)(2,1)S(1)}, bf16[4,8,48,128]{3,2,1,0:T(8,128)(2,1)S(1)}, u32[]{:S(2)}, u32[]{:S(2)}) collective-permute-start(bf16[4,8,48,128]{3,2,1,0:T(8,128)(2,1)S(1)} %get-tuple-element.61), channel_id=1, source_target_pairs={{4,8},{8,4},{5,9},{9,5},{6,10},{10,6},{7,11},{11,7},{20,24},{24,20... | collective-permute-start | bytes 1179656 | tf_op jit(solution)/shard_map/ppermute | solution.py:314
  22.3 15.0 %collective-permute-start.15 = (bf16[4,8,48,128]{3,2,1,0:T(8,128)(2,1)S(1)}, bf16[4,8,48,128]{3,2,1,0:T(8,128)(2,1)S(1)}, u32[]{:S(2)}, u32[]{:S(2)}) collective-permute-start(bf16[4,8,48,128]{3,2,1,0:T(8,128)(2,1)S(1)} %get-tuple-element.62), channel_id=1, source_target_pairs={{0,4},{4,0},{8,12},{12,8},{1,5},{5,1},{9,13},{13,9},{2,6},{6,2},{1... | collective-permute-start | bytes 1179656 | tf_op jit(solution)/shard_map/ppermute | solution.py:314
  29.9 9.2 %collective-permute-start.3 = (bf16[8,4,48,128]{3,2,1,0:T(8,128)(2,1)S(1)}, bf16[8,4,48,128]{3,2,1,0:T(8,128)(2,1)S(1)}, u32[]{:S(2)}, u32[]{:S(2)}) collective-permute-start(bf16[8,4,48,128]{3,2,1,0:T(8,128)(2,1)S(1)} %get-tuple-element.46), channel_id=1, source_target_pairs={{0,1},{1,0},{2,3},{3,2},{4,5},{5,4},{6,7},{7,6},{8,9},{9,8},{10,11... | collective-permute-start | bytes 1179656 | tf_op jit(solution)/shard_map/ppermute | solution.py:314
  30.0 14.8 %collective-permute-start.4 = (bf16[4,8,48,128]{3,2,1,0:T(8,128)(2,1)S(1)}, bf16[4,8,48,128]{3,2,1,0:T(8,128)(2,1)S(1)}, u32[]{:S(2)}, u32[]{:S(2)}) collective-permute-start(bf16[4,8,48,128]{3,2,1,0:T(8,128)(2,1)S(1)} %get-tuple-element.47), channel_id=1, source_target_pairs={{4,8},{8,4},{5,9},{9,5},{6,10},{10,6},{7,11},{11,7},{20,24},{24,20... | collective-permute-start | bytes 1179656 | tf_op jit(solution)/shard_map/ppermute | solution.py:314
  30.7 15.0 %collective-permute-start.5 = (bf16[4,8,48,128]{3,2,1,0:T(8,128)(2,1)S(1)}, bf16[4,8,48,128]{3,2,1,0:T(8,128)(2,1)S(1)}, u32[]{:S(2)}, u32[]{:S(2)}) collective-permute-start(bf16[4,8,48,128]{3,2,1,0:T(8,128)(2,1)S(1)} %get-tuple-element.48), channel_id=1, source_target_pairs={{0,4},{4,0},{8,12},{12,8},{1,5},{5,1},{9,13},{13,9},{2,6},{6,2},{1... | collective-permute-start | bytes 1179656 | tf_op jit(solution)/shard_map/ppermute | solution.py:314
  38.4 9.2 %collective-permute-start.16 = (bf16[8,4,48,128]{3,2,1,0:T(8,128)(2,1)S(1)}, bf16[8,4,48,128]{3,2,1,0:T(8,128)(2,1)S(1)}, u32[]{:S(2)}, u32[]{:S(2)}) collective-permute-start(bf16[8,4,48,128]{3,2,1,0:T(8,128)(2,1)S(1)} %get-tuple-element.64), channel_id=1, source_target_pairs={{0,1},{1,0},{2,3},{3,2},{4,5},{5,4},{6,7},{7,6},{8,9},{9,8},{10,11... | collective-permute-start | bytes 1179656 | tf_op jit(solution)/shard_map/ppermute | solution.py:314
  38.5 14.8 %collective-permute-start.17 = (bf16[4,8,48,128]{3,2,1,0:T(8,128)(2,1)S(1)}, bf16[4,8,48,128]{3,2,1,0:T(8,128)(2,1)S(1)}, u32[]{:S(2)}, u32[]{:S(2)}) collective-permute-start(bf16[4,8,48,128]{3,2,1,0:T(8,128)(2,1)S(1)} %get-tuple-element.65), channel_id=1, source_target_pairs={{4,8},{8,4},{5,9},{9,5},{6,10},{10,6},{7,11},{11,7},{20,24},{24,20... | collective-permute-start | bytes 1179656 | tf_op jit(solution)/shard_map/ppermute | solution.py:314
  39.2 15.0 %collective-permute-start.18 = (bf16[4,8,48,128]{3,2,1,0:T(8,128)(2,1)S(1)}, bf16[4,8,48,128]{3,2,1,0:T(8,128)(2,1)S(1)}, u32[]{:S(2)}, u32[]{:S(2)}) collective-permute-start(bf16[4,8,48,128]{3,2,1,0:T(8,128)(2,1)S(1)} %get-tuple-element.66), channel_id=1, source_target_pairs={{0,4},{4,0},{8,12},{12,8},{1,5},{5,1},{9,13},{13,9},{2,6},{6,2},{1... | collective-permute-start | bytes 1179656 | tf_op jit(solution)/shard_map/ppermute | solution.py:314
  46.8 9.5 %collective-permute-start.6 = (bf16[8,4,48,128]{3,2,1,0:T(8,128)(2,1)S(1)}, bf16[8,4,48,128]{3,2,1,0:T(8,128)(2,1)S(1)}, u32[]{:S(2)}, u32[]{:S(2)}) collective-permute-start(bf16[8,4,48,128]{3,2,1,0:T(8,128)(2,1)S(1)} %get-tuple-element.50), channel_id=1, source_target_pairs={{0,1},{1,0},{2,3},{3,2},{4,5},{5,4},{6,7},{7,6},{8,9},{9,8},{10,11... | collective-permute-start | bytes 1179656 | tf_op jit(solution)/shard_map/ppermute | solution.py:314
  46.9 11.7 %collective-permute-start.7 = (bf16[4,8,48,128]{3,2,1,0:T(8,128)(2,1)S(1)}, bf16[4,8,48,128]{3,2,1,0:T(8,128)(2,1)S(1)}, u32[]{:S(2)}, u32[]{:S(2)}) collective-permute-start(bf16[4,8,48,128]{3,2,1,0:T(8,128)(2,1)S(1)} %get-tuple-element.51), channel_id=1, source_target_pairs={{4,8},{8,4},{5,9},{9,5},{6,10},{10,6},{7,11},{11,7},{20,24},{24,20... | collective-permute-start | bytes 1179656 | tf_op jit(solution)/shard_map/ppermute | solution.py:314
  47.6 14.6 %collective-permute-start.8 = (bf16[4,8,48,128]{3,2,1,0:T(8,128)(2,1)S(1)}, bf16[4,8,48,128]{3,2,1,0:T(8,128)(2,1)S(1)}, u32[]{:S(2)}, u32[]{:S(2)}) collective-permute-start(bf16[4,8,48,128]{3,2,1,0:T(8,128)(2,1)S(1)} %get-tuple-element.52), channel_id=1, source_target_pairs={{0,4},{4,0},{8,12},{12,8},{1,5},{5,1},{9,13},{13,9},{2,6},{6,2},{1... | collective-permute-start | bytes 1179656 | tf_op jit(solution)/shard_map/ppermute | solution.py:314
  54.8 16.7 %collective-permute-start.19 = (bf16[4,8,48,128]{3,2,1,0:T(8,128)(2,1)S(1)}, bf16[4,8,48,128]{3,2,1,0:T(8,128)(2,1)S(1)}, u32[]{:S(2)}, u32[]{:S(2)}) collective-permute-start(bf16[4,8,48,128]{3,2,1,0:T(8,128)(2,1)S(1)} %shard_map.64.sent1), channel_id=1, source_target_pairs={{0,2},{2,0},{1,3},{3,1},{4,6},{6,4},{5,7},{7,5},{8,10},{10,8},{9,1... | collective-permute-start | bytes 1179656 | tf_op jit(solution)/shard_map/ppermute | solution.py:314
  63.1 10.8 %collective-permute-start.9 = (bf16[4,8,48,128]{3,2,1,0:T(8,128)(2,1)S(1)}, bf16[4,8,48,128]{3,2,1,0:T(8,128)(2,1)S(1)}, u32[]{:S(2)}, u32[]{:S(2)}) collective-permute-start(bf16[4,8,48,128]{3,2,1,0:T(8,128)(2,1)S(1)} %get-tuple-element.54.sent0), channel_id=1, source_target_pairs={{0,2},{2,0},{1,3},{3,1},{4,6},{6,4},{5,7},{7,5},{8,10},{10,8},{9,1... | collective-permute-start | bytes 1179656 | tf_op jit(solution)/shard_map/ppermute | solution.py:314
  76.3 8.2 %collective-permute-start.23 = (bf16[272,128]{1,0:T(8,128)(2,1)S(1)}, bf16[272,128]{1,0:T(8,128)(2,1)S(1)}, u32[]{:S(2)}, u32[]{:S(2)}) collective-permute-start(bf16[272,128]{1,0:T(8,128)(2,1)S(1)} %get-tuple-element.75), channel_id=1, source_target_pairs={{0,8},{4,12},{8,0},{12,4},{1,9},{5,13},{9,1},{13,5},{2,10},{6,14},... | collective-permute-start | bytes 208904 | tf_op jit(solution)/shard_map/ppermute | solution.py:569
  77.9 5.8 %collective-permute-start.24 = (bf16[144,128]{1,0:T(8,128)(2,1)S(1)}, bf16[144,128]{1,0:T(8,128)(2,1)S(1)}, u32[]{:S(2)}, u32[]{:S(2)}) collective-permute-start(bf16[144,128]{1,0:T(8,128)(2,1)S(1)} %get-tuple-element.76), channel_id=1, source_target_pairs={{0,12},{4,8},{8,4},{12,0},{1,13},{5,9},{9,5},{13,1},{2,14},{6,10},... | collective-permute-start | bytes 110600 | tf_op jit(solution)/shard_map/ppermute | solution.py:569
  80.2 4.3 %collective-permute-start.25 = (bf16[144,128]{1,0:T(8,128)(2,1)S(1)}, bf16[144,128]{1,0:T(8,128)(2,1)S(1)}, u32[]{:S(2)}, u32[]{:S(2)}) collective-permute-start(bf16[144,128]{1,0:T(8,128)(2,1)S(1)} %get-tuple-element.77), channel_id=1, source_target_pairs={{0,4},{4,0},{8,12},{12,8},{1,5},{5,1},{9,13},{13,9},{2,6},{6,2},{1... | collective-permute-start | bytes 110600 | tf_op jit(solution)/shard_map/ppermute | solution.py:569
  84.6 4.4 %collective-permute-start.26 = (bf16[272,128]{1,0:T(8,128)(2,1)S(1)}, bf16[272,128]{1,0:T(8,128)(2,1)S(1)}, u32[]{:S(2)}, u32[]{:S(2)}) collective-permute-start(bf16[272,128]{1,0:T(8,128)(2,1)S(1)} %shard_map.69.mine_ref), channel_id=1, source_target_pairs={{0,2},{2,0},{1,3},{3,1},{4,6},{6,4},{5,7},{7,5},{8,10},{10,8},{9,1... | collective-permute-start | bytes 208904 | tf_op jit(solution)/shard_map/ppermute | solution.py:314
  (8 other events, 42.3 us)

commit v19 on v18

--- a/solution.py
+++ b/solution.py
@@ -191,7 +191,7 @@
     )(*operands)
 
 
-def part_body(sent, base_ref, odd_ref, even_ref, c_ref, out_ref, square, turned_c):
+def part_body(sent, begin, base_ref, odd_ref, even_ref, c_ref, out_ref, square, turned_c):
     depth, across, along, _ = base_ref.shape
     even = slab_is_even()
     turned_c[...] = turned(c_ref[...], square)
@@ -206,7 +206,7 @@
                     one, two = even_ref[j, x, span], odd_ref[j, x, span]
                     pair = (two, one) if low else (one, two)
                     near.append(jnp.where(even, *pair).astype(F32))
-                for m in range(RADIUS):
+                for m in range(begin, begin + out_ref.shape[0]):
                     z = m if low else depth - RADIUS + m
                     added = None
                     for r in range(1, RADIUS + 1):
@@ -215,7 +215,7 @@
                             term = COEFFICIENTS[r] * near[at]
                             added = term if added is None else added + term
                     new = base_ref[z, x, span] + lane(courant, z * across + x) * added
-                    out_ref[m, x, span] = new.astype(BF16)
+                    out_ref[m - begin, x, span] = new.astype(BF16)
 
         tiles(along, tile)
 
@@ -224,13 +224,13 @@
     pl.when(jnp.logical_not(low))(lambda: planes(False))
 
 
-def part_step(base, odds, evens, courant, sent):
+def part_step(base, odds, evens, courant, sent, begin=0, count=RADIUS):
     _, across, along, _ = base.shape
     return call(
-        functools.partial(part_body, sent),
+        functools.partial(part_body, sent, begin),
         in_specs=whole_vmem(4),
         out_specs=whole_vmem(1)[0],
-        out_shape=shape_of(RADIUS, across, along, BF16),
+        out_shape=shape_of(count, across, along, BF16),
         scratch_shapes=square_scratch(),
     )(base, odds, evens, courant)
 
@@ -344,12 +344,30 @@
     return rows == cols
 
 
-def inner_body(kept0, sent0, kept1, sent1, keep_ref, send_ref, panel):
-    half = panel.shape[0] // 2
-    for n, (kept, sent) in enumerate(((kept0, sent0), (kept1, sent1))):
-        columns = slice(n * LANES, (n + 1) * LANES)
-        panel[:half, columns] = kept[...].reshape(half, LANES)
-        panel[half:, columns] = sent[...].reshape(half, LANES)
+def lay(panel, columns, refs):
+    row = 0
+    for ref in refs:
+        cells = math.prod(ref.shape[:3])
+        panel[row : row + cells, columns] = ref[...].reshape(cells, LANES)
+        row += cells
+
+
+def flat(groups):
+    return [field for group in groups for field in group]
+
+
+def regroup(sizes, refs):
+    groups, refs = [], list(refs)
+    for size in sizes:
+        groups.append(refs[:size])
+        refs = refs[size:]
+    return groups, refs
+
+
+def inner_body(sizes, *refs):
+    groups, (keep_ref, send_ref, panel) = regroup(sizes, refs)
+    for n, group in enumerate(groups):
+        lay(panel, slice(n * LANES, (n + 1) * LANES), group)
     core = lax.axis_index("sub")
     whole = product(panel[...], panel[...])
     first, second = whole[:, :LANES], whole[:, LANES:]
@@ -368,17 +386,17 @@
     send_ref[size:] = tail
 
 
-def inner_gram(fields):
+def inner_gram(groups):
     size = 2 * LANES
-    cells = 2 * math.prod(fields[0].shape[:3])
+    cells = sum(math.prod(field.shape[:3]) for field in groups[0])
     half = jax.ShapeDtypeStruct((size + 8, LANES), F32)
     return call(
-        inner_body,
-        in_specs=whole_vmem(4),
+        functools.partial(inner_body, [len(group) for group in groups]),
+        in_specs=whole_vmem(len(flat(groups))),
         out_specs=whole_vmem(2),
         out_shape=[half, half],
         scratch_shapes=[pltpu.VMEM((cells, size), BF16)],
-    )(*fields)
+    )(*flat(groups))
 
 
 def inner_sum_body(keep_ref, got_ref, tail_ref, own_ref, sent_ref):
@@ -403,15 +421,15 @@
     )(keep, got)
 
 
-def cross_body(kept0, got0, kept1, got1, _, keep_ref, send_ref, panel):
+def cross_body(sizes, *refs):
+    groups, (_, keep_ref, send_ref, panel) = regroup(sizes, refs)
     chip = lax.axis_index("probe")
     core = lax.axis_index("sub")
-    cells = panel.shape[0]
-    for n, (kept, got) in enumerate(((kept0, got0), (kept1, got1))):
+    for n in range(2):
         mine = pl.multiple_of((chip * 2 + n) * LANES, LANES)
         other = pl.multiple_of(((1 - chip) * 2 + n) * LANES, LANES)
-        panel[:, pl.ds(mine, LANES)] = kept[...].reshape(cells, LANES)
-        panel[:, pl.ds(other, LANES)] = got[...].reshape(cells, LANES)
+        lay(panel, pl.ds(mine, LANES), groups[2 * n])
+        lay(panel, pl.ds(other, LANES), groups[2 * n + 1])
     whole = product(panel[:, : 2 * LANES], panel[:, 2 * LANES :])
     for ref, which in ((keep_ref, core), (send_ref, 1 - core)):
         here = which == 0
@@ -421,16 +439,16 @@
         ref[2 * LANES :] = mixed
 
 
-def cross_gram(fields, after):
-    cells = math.prod(fields[0].shape[:3])
+def cross_gram(groups, after):
+    cells = sum(math.prod(field.shape[:3]) for field in groups[0])
     three = jax.ShapeDtypeStruct((3 * LANES, LANES), F32)
     return call(
-        cross_body,
-        in_specs=whole_vmem(4) + [pl.BlockSpec(memory_space=pl.ANY)],
+        functools.partial(cross_body, [len(group) for group in groups]),
+        in_specs=whole_vmem(len(flat(groups))) + [pl.BlockSpec(memory_space=pl.ANY)],
         out_specs=whole_vmem(2),
         out_shape=[three, three],
         scratch_shapes=[pltpu.VMEM((cells, 4 * LANES), BF16)],
-    )(*fields, after)
+    )(*flat(groups), after)
 
 
 def rounded(ref, block, tail):
@@ -558,12 +576,10 @@
 
 def coupled(finals, cell_count):
     slabs = 4
-    own = [field for kept, sent, _ in finals for field in (kept, sent)]
-    keep, send = inner_gram(own)
+    keep, send = inner_gram([kept + sent for kept, sent, _ in finals])
     tail, inner, sent = inner_sum(keep, core_swap(send))
     inner_got = lax.ppermute(sent, "slab", [(i, i ^ 1) for i in range(slabs)])
-    pairs = [field for kept, _, got in finals for field in (kept, got)]
-    keep, send = cross_gram(pairs, inner_got)
+    keep, send = cross_gram([g for kept, _, got in finals for g in (kept, got)], inner_got)
     mine, *blocks = cross_rows(keep, core_swap(send), tail, inner, inner_got, slabs)
     arrived = [
         lax.ppermute(blocks[d - 1], "slab", [(i, i ^ d) for i in range(slabs)])
@@ -622,12 +638,15 @@
                 previous[c], now[c] = now[c], u
                 halos[c] = exchange(*edges)
             elif paired:
-                if c < chunks - 1:
-                    kept, sent = rim_step(base, odd, even, courant, "half")
+                if c > 0:
+                    kept, *sent = rim_step(base, odd, even, courant, "half")
                 else:
-                    sent = part_step(base, odd, even, courant, True)
+                    sent = [
+                        part_step(base, odd, even, courant, True, begin, RADIUS // 2)
+                        for begin in (0, RADIUS // 2)
+                    ]
                     kept = part_step(base, odd, even, courant, False)
-                finals.append((kept, sent, chip_swap(sent)))
+                finals.append(([kept], sent, [chip_swap(a) for a in sent]))
             else:
                 finals += rim_step(base, odd, even, courant, "all")
     return (coupled if paired else coupled_general)(finals, cell_count)

time: 91.9 us -> 91.9 us (level)
    ppermute x24 -> x25, waiting for transfers between devices: 20.2 us -> 19.3 us  [swap(): lax.ppermute(x, axis, [p for a, b in pairs for p in ((a, b), (b, a))])]
    ppermute x24 -> x25, starting transfers between devices: 31.1 us -> 31.7 us  [swap(): lax.ppermute(x, axis, [p for a, b in pairs for p in ((a, b), (b, a))])]
    pallas_call x4 -> x5, Pallas kernels: 2.84 us -> 3.14 us  [the longest x3 1.57 us: part_step(): call(functools.partial(part_body, sent, begin), in_specs=whole_vmem(4), o...]
  transfers between devices with their start and end apart: 28 -> 29, of which waited for: 14 -> 14; matrix products, arithmetic and copies ran while one was open for 0% -> 0% of each run, Pallas kernels for 24% -> 24%
where the time goes in v19:
time: 91.9 us; the launch traced here: 91.6 us
  starting transfers between devices  37.3 us (41%)
  waiting for transfers between devices  25.8 us (28%)
  Pallas kernels  25.2 us (27%)
  local copies, waits for them, and re-layouts  2.18 us (2%)
  between operations  1 us (1%)
    ppermute x25, starting transfers between devices, swap(): lax.ppermute(x, axis, [p for a, b in pairs for p in ((a, b), (b, a))])  31.7 us
    ppermute x25, waiting for transfers between devices, swap(): lax.ppermute(x, axis, [p for a, b in pairs for p in ((a, b), (b, a))])  19.3 us
    pallas_call x6, Pallas kernels, local_step(): call(functools.partial(local_body, chunk, moment, previous is not None),...  13.3 us
    pallas_call x5, Pallas kernels, rim_step(): call(functools.partial(rim_body, kind), in_specs=whole_vmem(4), out_specs...  5.35 us
    ppermute x3, waiting for transfers between devices, coupled(): lax.ppermute(blocks[d - 1], 'slab', [(i, i ^ d) for i in range(slabs)])  4.36 us
    ppermute x3, starting transfers between devices, coupled(): lax.ppermute(blocks[d - 1], 'slab', [(i, i ^ d) for i in range(slabs)])  3.83 us
    ppermute x1, waiting for transfers between devices, coupled(): inner_got = lax.ppermute(sent, 'slab', [(i, i ^ 1) for i in range(slabs)])  2.17 us
    pallas_call x2, Pallas kernels, first_field(): call(functools.partial(first_body, chunk), in_specs=whole_vmem(2), out_sp...  2.1 us
  transfers between devices with their start and end apart: 29, of which 14 were waited for; matrix products, arithmetic and copies ran while one was open for 0% of the time, Pallas kernels for 24%

profile of v19, /device:TPU:0, one launch (start us, length us, event | category | flops | bytes accessed | tf_op | source)
XLA Modules:
  0.0 91.6 jit_solution(16725985520967948541)
XLA Ops:
  5.1 5.5 %collective-permute-start.13 = (bf16[4,8,48,128]{3,2,1,0:T(8,128)(2,1)S(1)}, bf16[4,8,48,128]{3,2,1,0:T(8,128)(2,1)S(1)}, u32[]{:S(2)}, u32[]{:S(2)}) collective-permute-start(bf16[4,8,48,128]{3,2,1,0:T(8,128)(2,1)S(1)} %get-tuple-element.56), channel_id=1, source_target_pairs={{0,4},{4,0},{8,12},{12,8},{1,5},{5,1},{9,13},{13,9},{2,6},{6,2},{1... | collective-permute-start | bytes 1179656 | tf_op jit(solution)/shard_map/ppermute | solution.py:314
  12.4 1.9 %collective-permute-start.2 = (bf16[4,8,48,128]{3,2,1,0:T(8,128)(2,1)S(1)}, bf16[4,8,48,128]{3,2,1,0:T(8,128)(2,1)S(1)}, u32[]{:S(2)}, u32[]{:S(2)}) collective-permute-start(bf16[4,8,48,128]{3,2,1,0:T(8,128)(2,1)S(1)} %get-tuple-element.44), channel_id=1, source_target_pairs={{0,4},{4,0},{8,12},{12,8},{1,5},{5,1},{9,13},{13,9},{2,6},{6,2},{1... | collective-permute-start | bytes 1179656 | tf_op jit(solution)/shard_map/ppermute | solution.py:314
  14.3 2.1 %shard_map.60.refs_0_ = f32[8,8,48,128]{3,2,1,0:T(8,128)S(1)} custom-call(f32[8,8,64,128]{3,2,1,0:T(8,128)S(1)} %get-tuple-element.53.refs_0_.refs_5_, bf16[8,4,48,128]{3,2,1,0:T(8,128)(2,1)S(1)} %collective-permute-done.11.refs_1_, bf16[8,8,48,256]{3,2,1,0:T(8,128)(2,1)S(1)} %copy-done, f32[64,48]{1,0:T(8,128)S(1)} %bitcast.5, f32[4,64,48]{2,1,0:T(8,128)S(1)} %bitcast.19), custom_call_target="tpu_custom_call" | custom-call | flops 1 | bytes 1 | tf_op jit(solution)/shard_map/pallas_call | solution.py:185
  16.5 3.9 %collective-permute-done.13.refs_2_ = bf16[4,8,48,128]{3,2,1,0:T(8,128)(2,1)S(1)} collective-permute-done((bf16[4,8,48,128]{3,2,1,0:T(8,128)(2,1)S(1)}, bf16[4,8,48,128]{3,2,1,0:T(8,128)(2,1)S(1)}, u32[]{:S(2)}, u32[]{:S(2)}) %collective-permute-start.13) | collective-permute-done | bytes 393248 | tf_op jit(solution)/shard_map/ppermute | solution.py:314
  22.3 3.8 %collective-permute-start.16 = (bf16[4,8,48,128]{3,2,1,0:T(8,128)(2,1)S(1)}, bf16[4,8,48,128]{3,2,1,0:T(8,128)(2,1)S(1)}, u32[]{:S(2)}, u32[]{:S(2)}) collective-permute-start(bf16[4,8,48,128]{3,2,1,0:T(8,128)(2,1)S(1)} %get-tuple-element.60), channel_id=1, source_target_pairs={{0,4},{4,0},{8,12},{12,8},{1,5},{5,1},{9,13},{13,9},{2,6},{6,2},{1... | collective-permute-start | bytes 1179656 | tf_op jit(solution)/shard_map/ppermute | solution.py:314
  26.1 2.1 %shard_map.51.refs_0_ = f32[8,8,48,128]{3,2,1,0:T(8,128)S(1)} custom-call(f32[8,8,64,128]{3,2,1,0:T(8,128)S(1)} %get-tuple-element.41.refs_0_.refs_5_, bf16[8,4,48,128]{3,2,1,0:T(8,128)(2,1)S(1)} %collective-permute-done.refs_1_, bf16[8,8,48,256]{3,2,1,0:T(8,128)(2,1)S(1)} %copy-done.1, f32[64,48]{1,0:T(8,128)S(1)} %bitcast.7, f32[4,64,48]{2,1,0:T(8,128)S(1)} %bitcast.20), custom_call_target="tpu_custom_call" | custom-call | flops 1 | bytes 1 | tf_op jit(solution)/shard_map/pallas_call | solution.py:185
  30.7 3.4 %collective-permute-start.5 = (bf16[4,8,48,128]{3,2,1,0:T(8,128)(2,1)S(1)}, bf16[4,8,48,128]{3,2,1,0:T(8,128)(2,1)S(1)}, u32[]{:S(2)}, u32[]{:S(2)}) collective-permute-start(bf16[4,8,48,128]{3,2,1,0:T(8,128)(2,1)S(1)} %get-tuple-element.48), channel_id=1, source_target_pairs={{0,4},{4,0},{8,12},{12,8},{1,5},{5,1},{9,13},{13,9},{2,6},{6,2},{1... | collective-permute-start | bytes 1179656 | tf_op jit(solution)/shard_map/ppermute | solution.py:314
  34.1 2.3 %shard_map.62.refs_0_ = f32[8,8,48,128]{3,2,1,0:T(8,128)S(1)} custom-call(f32[8,8,64,128]{3,2,1,0:T(8,128)S(1)} %get-tuple-element.57.refs_0_.refs_5_, bf16[8,4,48,128]{3,2,1,0:T(8,128)(2,1)S(1)} %collective-permute-done.14.refs_1_, bf16[8,8,48,256]{3,2,1,0:T(8,128)(2,1)S(1)} %copy-done.1, f32[64,48]{1,0:T(8,128)S(1)} %bitcast.9, f32[4,64,48]{2,1,0:T(8,128)S(1)} %bitcast.21, ...), custom_call_target="tpu_custom_call" | custom-call | flops 1 | bytes 1 | tf_op jit(solution)/shard_map/pallas_call | solution.py:185
  39.2 3.4 %collective-permute-start.19 = (bf16[4,8,48,128]{3,2,1,0:T(8,128)(2,1)S(1)}, bf16[4,8,48,128]{3,2,1,0:T(8,128)(2,1)S(1)}, u32[]{:S(2)}, u32[]{:S(2)}) collective-permute-start(bf16[4,8,48,128]{3,2,1,0:T(8,128)(2,1)S(1)} %get-tuple-element.64), channel_id=1, source_target_pairs={{0,4},{4,0},{8,12},{12,8},{1,5},{5,1},{9,13},{13,9},{2,6},{6,2},{1... | collective-permute-start | bytes 1179656 | tf_op jit(solution)/shard_map/ppermute | solution.py:314
  42.5 2.2 %shard_map.53.refs_0_ = f32[8,8,48,128]{3,2,1,0:T(8,128)S(1)} custom-call(f32[8,8,64,128]{3,2,1,0:T(8,128)S(1)} %get-tuple-element.45.refs_0_.refs_5_, bf16[8,4,48,128]{3,2,1,0:T(8,128)(2,1)S(1)} %collective-permute-done.3.refs_1_, bf16[8,8,48,256]{3,2,1,0:T(8,128)(2,1)S(1)} %copy-done.1, f32[64,48]{1,0:T(8,128)S(1)} %bitcast.11, f32[4,64,48]{2,1,0:T(8,128)S(1)} %bitcast.22, ...), custom_call_target="tpu_custom_call" | custom-call | flops 1 | bytes 1 | tf_op jit(solution)/shard_map/pallas_call | solution.py:185
  47.6 3.4 %collective-permute-start.8 = (bf16[4,8,48,128]{3,2,1,0:T(8,128)(2,1)S(1)}, bf16[4,8,48,128]{3,2,1,0:T(8,128)(2,1)S(1)}, u32[]{:S(2)}, u32[]{:S(2)}) collective-permute-start(bf16[4,8,48,128]{3,2,1,0:T(8,128)(2,1)S(1)} %get-tuple-element.52), channel_id=1, source_target_pairs={{0,4},{4,0},{8,12},{12,8},{1,5},{5,1},{9,13},{13,9},{2,6},{6,2},{1... | collective-permute-start | bytes 1179656 | tf_op jit(solution)/shard_map/ppermute | solution.py:314
  50.9 2.3 %shard_map.64.refs_0_ = f32[8,8,48,128]{3,2,1,0:T(8,128)S(1)} custom-call(f32[8,8,64,128]{3,2,1,0:T(8,128)S(1)} %get-tuple-element.61.refs_0_, bf16[8,4,48,128]{3,2,1,0:T(8,128)(2,1)S(1)} %collective-permute-done.17.refs_1_, bf16[8,8,48,256]{3,2,1,0:T(8,128)(2,1)S(1)} %copy-done.1, f32[64,48]{1,0:T(8,128)S(1)} %bitcast.13, f32[4,64,48]{2,1,0:T(8,128)S(1)} %bitcast.23, ...), custom_call_target="tpu_custom_call" | custom-call | flops 1 | bytes 1 | tf_op jit(solution)/shard_map/pallas_call | solution.py:185
  55.1 1.6 %collective-permute-start.20 = (bf16[4,8,48,128]{3,2,1,0:T(8,128)(2,1)S(1)}, bf16[4,8,48,128]{3,2,1,0:T(8,128)(2,1)S(1)}, u32[]{:S(2)}, u32[]{:S(2)}) collective-permute-start(bf16[4,8,48,128]{3,2,1,0:T(8,128)(2,1)S(1)} %get-tuple-element.66.refs_4_), channel_id=1, source_target_pairs={{0,2},{2,0},{1,3},{3,1},{4,6},{6,4},{5,7},{7,5},{8,10},{10,8},{9,1... | collective-permute-start | bytes 1179656 | tf_op jit(solution)/shard_map/ppermute | solution.py:314
  56.6 2.2 %shard_map.55.base_ref = f32[8,8,48,128]{3,2,1,0:T(8,128)S(1)} custom-call(f32[8,8,64,128]{3,2,1,0:T(8,128)S(1)} %get-tuple-element.49.refs_0_, bf16[8,4,48,128]{3,2,1,0:T(8,128)(2,1)S(1)} %collective-permute-done.6.refs_1_, bf16[8,8,48,256]{3,2,1,0:T(8,128)(2,1)S(1)} %copy-done.1, f32[64,48]{1,0:T(8,128)S(1)} %bitcast.15, f32[4,64,48]{2,1,0:T(8,128)S(1)} %bitcast.24, ...), custom_call_target="tpu_custom_call" | custom-call | flops 1 | bytes 1 | tf_op jit(solution)/shard_map/pallas_call | solution.py:185
  58.9 3.2 %collective-permute-done.8.even_ref = bf16[4,8,48,128]{3,2,1,0:T(8,128)(2,1)S(1)} collective-permute-done((bf16[4,8,48,128]{3,2,1,0:T(8,128)(2,1)S(1)}, bf16[4,8,48,128]{3,2,1,0:T(8,128)(2,1)S(1)}, u32[]{:S(2)}, u32[]{:S(2)}) %collective-permute-start.8) | collective-permute-done | bytes 393248 | tf_op jit(solution)/shard_map/ppermute | solution.py:314
  62.6 1.6 %collective-permute-start.10 = (bf16[2,8,48,128]{3,2,1,0:T(8,128)(2,1)S(1)}, bf16[2,8,48,128]{3,2,1,0:T(8,128)(2,1)S(1)}, u32[]{:S(2)}, u32[]{:S(2)}) collective-permute-start(bf16[2,8,48,128]{3,2,1,0:T(8,128)(2,1)S(1)} %shard_map.58.refs_2_), channel_id=1, source_target_pairs={{0,2},{2,0},{1,3},{3,1},{4,6},{6,4},{5,7},{7,5},{8,10},{10,8},{9,1... | collective-permute-start | bytes 589832 | tf_op jit(solution)/shard_map/ppermute | solution.py:314
  68.0 1.8 %collective-permute-start.22 = (bf16[128,128]{1,0:T(8,128)(2,1)S(1)}, bf16[128,128]{1,0:T(8,128)(2,1)S(1)}, u32[]{:S(2)}, u32[]{:S(2)}) collective-permute-start(bf16[128,128]{1,0:T(8,128)(2,1)S(1)} %get-tuple-element.69), channel_id=1, source_target_pairs={{0,4},{4,0},{8,12},{12,8},{1,5},{5,1},{9,13},{13,9},{2,6},{6,2},{1... | collective-permute-start | bytes 98312 | tf_op jit(solution)/shard_map/ppermute | solution.py:581
  69.8 2.2 %collective-permute-done.22.refs_5_.inner_got_ref = bf16[128,128]{1,0:T(8,128)(2,1)S(1)} collective-permute-done((bf16[128,128]{1,0:T(8,128)(2,1)S(1)}, bf16[128,128]{1,0:T(8,128)(2,1)S(1)}, u32[]{:S(2)}, u32[]{:S(2)}) %collective-permute-start.22) | collective-permute-done | bytes 32800 | tf_op jit(solution)/shard_map/ppermute | solution.py:581
  72.0 1.9 %collective-permute-done.9.refs_1_ = bf16[2,8,48,128]{3,2,1,0:T(8,128)(2,1)S(1)} collective-permute-done((bf16[2,8,48,128]{3,2,1,0:T(8,128)(2,1)S(1)}, bf16[2,8,48,128]{3,2,1,0:T(8,128)(2,1)S(1)}, u32[]{:S(2)}, u32[]{:S(2)}) %collective-permute-start.9) | collective-permute-done | bytes 196640 | tf_op jit(solution)/shard_map/ppermute | solution.py:314
  76.4 1.5 %collective-permute-start.24 = (bf16[272,128]{1,0:T(8,128)(2,1)S(1)}, bf16[272,128]{1,0:T(8,128)(2,1)S(1)}, u32[]{:S(2)}, u32[]{:S(2)}) collective-permute-start(bf16[272,128]{1,0:T(8,128)(2,1)S(1)} %get-tuple-element.75), channel_id=1, source_target_pairs={{0,8},{4,12},{8,0},{12,4},{1,9},{5,13},{9,1},{13,5},{2,10},{6,14},... | collective-permute-start | bytes 208904 | tf_op jit(solution)/shard_map/ppermute | solution.py:585
  77.9 2.3 %collective-permute-start.25 = (bf16[144,128]{1,0:T(8,128)(2,1)S(1)}, bf16[144,128]{1,0:T(8,128)(2,1)S(1)}, u32[]{:S(2)}, u32[]{:S(2)}) collective-permute-start(bf16[144,128]{1,0:T(8,128)(2,1)S(1)} %get-tuple-element.76), channel_id=1, source_target_pairs={{0,12},{4,8},{8,4},{12,0},{1,13},{5,9},{9,5},{13,1},{2,14},{6,10},... | collective-permute-start | bytes 110600 | tf_op jit(solution)/shard_map/ppermute | solution.py:585
  80.2 3.5 %collective-permute-done.25.refs_1_ = bf16[144,128]{1,0:T(8,128)(2,1)S(1)} collective-permute-done((bf16[144,128]{1,0:T(8,128)(2,1)S(1)}, bf16[144,128]{1,0:T(8,128)(2,1)S(1)}, u32[]{:S(2)}, u32[]{:S(2)}) %collective-permute-start.25) | collective-permute-done | bytes 36896 | tf_op jit(solution)/shard_map/ppermute | solution.py:585
  84.6 1.6 %collective-permute-start.27 = (bf16[272,128]{1,0:T(8,128)(2,1)S(1)}, bf16[272,128]{1,0:T(8,128)(2,1)S(1)}, u32[]{:S(2)}, u32[]{:S(2)}) collective-permute-start(bf16[272,128]{1,0:T(8,128)(2,1)S(1)} %shard_map.70.mine_ref), channel_id=1, source_target_pairs={{0,2},{2,0},{1,3},{3,1},{4,6},{6,4},{5,7},{7,5},{8,10},{10,8},{9,1... | collective-permute-start | bytes 208904 | tf_op jit(solution)/shard_map/ppermute | solution.py:314
  86.2 2.8 %collective-permute-done.27.other_ref = bf16[272,128]{1,0:T(8,128)(2,1)S(1)} collective-permute-done((bf16[272,128]{1,0:T(8,128)(2,1)S(1)}, bf16[272,128]{1,0:T(8,128)(2,1)S(1)}, u32[]{:S(2)}, u32[]{:S(2)}) %collective-permute-start.27) | collective-permute-done | bytes 69664 | tf_op jit(solution)/shard_map/ppermute | solution.py:314
  (66 shorter events, 28.2 us)
Async XLA Ops:
  3.9 8.5 %collective-permute-start.11 = (bf16[8,4,48,128]{3,2,1,0:T(8,128)(2,1)S(1)}, bf16[8,4,48,128]{3,2,1,0:T(8,128)(2,1)S(1)}, u32[]{:S(2)}, u32[]{:S(2)}) collective-permute-start(bf16[8,4,48,128]{3,2,1,0:T(8,128)(2,1)S(1)} %get-tuple-element.54), channel_id=1, source_target_pairs={{0,1},{1,0},{2,3},{3,2},{4,5},{5,4},{6,7},{7,6},{8,9},{9,8},{10,11... | collective-permute-start | bytes 1179656 | tf_op jit(solution)/shard_map/ppermute | solution.py:314
  4.4 12.1 %collective-permute-start.12 = (bf16[4,8,48,128]{3,2,1,0:T(8,128)(2,1)S(1)}, bf16[4,8,48,128]{3,2,1,0:T(8,128)(2,1)S(1)}, u32[]{:S(2)}, u32[]{:S(2)}) collective-permute-start(bf16[4,8,48,128]{3,2,1,0:T(8,128)(2,1)S(1)} %get-tuple-element.55), channel_id=1, source_target_pairs={{4,8},{8,4},{5,9},{9,5},{6,10},{10,6},{7,11},{11,7},{20,24},{24,20... | collective-permute-start | bytes 1179656 | tf_op jit(solution)/shard_map/ppermute | solution.py:314
  5.1 15.4 %collective-permute-start.13 = (bf16[4,8,48,128]{3,2,1,0:T(8,128)(2,1)S(1)}, bf16[4,8,48,128]{3,2,1,0:T(8,128)(2,1)S(1)}, u32[]{:S(2)}, u32[]{:S(2)}) collective-permute-start(bf16[4,8,48,128]{3,2,1,0:T(8,128)(2,1)S(1)} %get-tuple-element.56), channel_id=1, source_target_pairs={{0,4},{4,0},{8,12},{12,8},{1,5},{5,1},{9,13},{13,9},{2,6},{6,2},{1... | collective-permute-start | bytes 1179656 | tf_op jit(solution)/shard_map/ppermute | solution.py:314
  11.6 10.7 %collective-permute-start = (bf16[8,4,48,128]{3,2,1,0:T(8,128)(2,1)S(1)}, bf16[8,4,48,128]{3,2,1,0:T(8,128)(2,1)S(1)}, u32[]{:S(2)}, u32[]{:S(2)}) collective-permute-start(bf16[8,4,48,128]{3,2,1,0:T(8,128)(2,1)S(1)} %get-tuple-element.42), channel_id=1, source_target_pairs={{0,1},{1,0},{2,3},{3,2},{4,5},{5,4},{6,7},{7,6},{8,9},{9,8},{10,11... | collective-permute-start | bytes 1179656 | tf_op jit(solution)/shard_map/ppermute | solution.py:314
  11.7 16.6 %collective-permute-start.1 = (bf16[4,8,48,128]{3,2,1,0:T(8,128)(2,1)S(1)}, bf16[4,8,48,128]{3,2,1,0:T(8,128)(2,1)S(1)}, u32[]{:S(2)}, u32[]{:S(2)}) collective-permute-start(bf16[4,8,48,128]{3,2,1,0:T(8,128)(2,1)S(1)} %get-tuple-element.43), channel_id=1, source_target_pairs={{4,8},{8,4},{5,9},{9,5},{6,10},{10,6},{7,11},{11,7},{20,24},{24,20... | collective-permute-start | bytes 1179656 | tf_op jit(solution)/shard_map/ppermute | solution.py:314
  12.4 16.5 %collective-permute-start.2 = (bf16[4,8,48,128]{3,2,1,0:T(8,128)(2,1)S(1)}, bf16[4,8,48,128]{3,2,1,0:T(8,128)(2,1)S(1)}, u32[]{:S(2)}, u32[]{:S(2)}) collective-permute-start(bf16[4,8,48,128]{3,2,1,0:T(8,128)(2,1)S(1)} %get-tuple-element.44), channel_id=1, source_target_pairs={{0,4},{4,0},{8,12},{12,8},{1,5},{5,1},{9,13},{13,9},{2,6},{6,2},{1... | collective-permute-start | bytes 1179656 | tf_op jit(solution)/shard_map/ppermute | solution.py:314
  21.5 9.2 %collective-permute-start.14 = (bf16[8,4,48,128]{3,2,1,0:T(8,128)(2,1)S(1)}, bf16[8,4,48,128]{3,2,1,0:T(8,128)(2,1)S(1)}, u32[]{:S(2)}, u32[]{:S(2)}) collective-permute-start(bf16[8,4,48,128]{3,2,1,0:T(8,128)(2,1)S(1)} %get-tuple-element.58), channel_id=1, source_target_pairs={{0,1},{1,0},{2,3},{3,2},{4,5},{5,4},{6,7},{7,6},{8,9},{9,8},{10,11... | collective-permute-start | bytes 1179656 | tf_op jit(solution)/shard_map/ppermute | solution.py:314
  21.6 14.8 %collective-permute-start.15 = (bf16[4,8,48,128]{3,2,1,0:T(8,128)(2,1)S(1)}, bf16[4,8,48,128]{3,2,1,0:T(8,128)(2,1)S(1)}, u32[]{:S(2)}, u32[]{:S(2)}) collective-permute-start(bf16[4,8,48,128]{3,2,1,0:T(8,128)(2,1)S(1)} %get-tuple-element.59), channel_id=1, source_target_pairs={{4,8},{8,4},{5,9},{9,5},{6,10},{10,6},{7,11},{11,7},{20,24},{24,20... | collective-permute-start | bytes 1179656 | tf_op jit(solution)/shard_map/ppermute | solution.py:314
  22.3 15.0 %collective-permute-start.16 = (bf16[4,8,48,128]{3,2,1,0:T(8,128)(2,1)S(1)}, bf16[4,8,48,128]{3,2,1,0:T(8,128)(2,1)S(1)}, u32[]{:S(2)}, u32[]{:S(2)}) collective-permute-start(bf16[4,8,48,128]{3,2,1,0:T(8,128)(2,1)S(1)} %get-tuple-element.60), channel_id=1, source_target_pairs={{0,4},{4,0},{8,12},{12,8},{1,5},{5,1},{9,13},{13,9},{2,6},{6,2},{1... | collective-permute-start | bytes 1179656 | tf_op jit(solution)/shard_map/ppermute | solution.py:314
  29.9 9.2 %collective-permute-start.3 = (bf16[8,4,48,128]{3,2,1,0:T(8,128)(2,1)S(1)}, bf16[8,4,48,128]{3,2,1,0:T(8,128)(2,1)S(1)}, u32[]{:S(2)}, u32[]{:S(2)}) collective-permute-start(bf16[8,4,48,128]{3,2,1,0:T(8,128)(2,1)S(1)} %get-tuple-element.46), channel_id=1, source_target_pairs={{0,1},{1,0},{2,3},{3,2},{4,5},{5,4},{6,7},{7,6},{8,9},{9,8},{10,11... | collective-permute-start | bytes 1179656 | tf_op jit(solution)/shard_map/ppermute | solution.py:314
  30.0 14.8 %collective-permute-start.4 = (bf16[4,8,48,128]{3,2,1,0:T(8,128)(2,1)S(1)}, bf16[4,8,48,128]{3,2,1,0:T(8,128)(2,1)S(1)}, u32[]{:S(2)}, u32[]{:S(2)}) collective-permute-start(bf16[4,8,48,128]{3,2,1,0:T(8,128)(2,1)S(1)} %get-tuple-element.47), channel_id=1, source_target_pairs={{4,8},{8,4},{5,9},{9,5},{6,10},{10,6},{7,11},{11,7},{20,24},{24,20... | collective-permute-start | bytes 1179656 | tf_op jit(solution)/shard_map/ppermute | solution.py:314
  30.7 15.0 %collective-permute-start.5 = (bf16[4,8,48,128]{3,2,1,0:T(8,128)(2,1)S(1)}, bf16[4,8,48,128]{3,2,1,0:T(8,128)(2,1)S(1)}, u32[]{:S(2)}, u32[]{:S(2)}) collective-permute-start(bf16[4,8,48,128]{3,2,1,0:T(8,128)(2,1)S(1)} %get-tuple-element.48), channel_id=1, source_target_pairs={{0,4},{4,0},{8,12},{12,8},{1,5},{5,1},{9,13},{13,9},{2,6},{6,2},{1... | collective-permute-start | bytes 1179656 | tf_op jit(solution)/shard_map/ppermute | solution.py:314
  38.4 9.2 %collective-permute-start.17 = (bf16[8,4,48,128]{3,2,1,0:T(8,128)(2,1)S(1)}, bf16[8,4,48,128]{3,2,1,0:T(8,128)(2,1)S(1)}, u32[]{:S(2)}, u32[]{:S(2)}) collective-permute-start(bf16[8,4,48,128]{3,2,1,0:T(8,128)(2,1)S(1)} %get-tuple-element.62), channel_id=1, source_target_pairs={{0,1},{1,0},{2,3},{3,2},{4,5},{5,4},{6,7},{7,6},{8,9},{9,8},{10,11... | collective-permute-start | bytes 1179656 | tf_op jit(solution)/shard_map/ppermute | solution.py:314
  38.5 14.8 %collective-permute-start.18 = (bf16[4,8,48,128]{3,2,1,0:T(8,128)(2,1)S(1)}, bf16[4,8,48,128]{3,2,1,0:T(8,128)(2,1)S(1)}, u32[]{:S(2)}, u32[]{:S(2)}) collective-permute-start(bf16[4,8,48,128]{3,2,1,0:T(8,128)(2,1)S(1)} %get-tuple-element.63), channel_id=1, source_target_pairs={{4,8},{8,4},{5,9},{9,5},{6,10},{10,6},{7,11},{11,7},{20,24},{24,20... | collective-permute-start | bytes 1179656 | tf_op jit(solution)/shard_map/ppermute | solution.py:314
  39.2 15.0 %collective-permute-start.19 = (bf16[4,8,48,128]{3,2,1,0:T(8,128)(2,1)S(1)}, bf16[4,8,48,128]{3,2,1,0:T(8,128)(2,1)S(1)}, u32[]{:S(2)}, u32[]{:S(2)}) collective-permute-start(bf16[4,8,48,128]{3,2,1,0:T(8,128)(2,1)S(1)} %get-tuple-element.64), channel_id=1, source_target_pairs={{0,4},{4,0},{8,12},{12,8},{1,5},{5,1},{9,13},{13,9},{2,6},{6,2},{1... | collective-permute-start | bytes 1179656 | tf_op jit(solution)/shard_map/ppermute | solution.py:314
  46.8 9.8 %collective-permute-start.6 = (bf16[8,4,48,128]{3,2,1,0:T(8,128)(2,1)S(1)}, bf16[8,4,48,128]{3,2,1,0:T(8,128)(2,1)S(1)}, u32[]{:S(2)}, u32[]{:S(2)}) collective-permute-start(bf16[8,4,48,128]{3,2,1,0:T(8,128)(2,1)S(1)} %get-tuple-element.50), channel_id=1, source_target_pairs={{0,1},{1,0},{2,3},{3,2},{4,5},{5,4},{6,7},{7,6},{8,9},{9,8},{10,11... | collective-permute-start | bytes 1179656 | tf_op jit(solution)/shard_map/ppermute | solution.py:314
  46.9 12.0 %collective-permute-start.7 = (bf16[4,8,48,128]{3,2,1,0:T(8,128)(2,1)S(1)}, bf16[4,8,48,128]{3,2,1,0:T(8,128)(2,1)S(1)}, u32[]{:S(2)}, u32[]{:S(2)}) collective-permute-start(bf16[4,8,48,128]{3,2,1,0:T(8,128)(2,1)S(1)} %get-tuple-element.51), channel_id=1, source_target_pairs={{4,8},{8,4},{5,9},{9,5},{6,10},{10,6},{7,11},{11,7},{20,24},{24,20... | collective-permute-start | bytes 1179656 | tf_op jit(solution)/shard_map/ppermute | solution.py:314
  47.6 14.6 %collective-permute-start.8 = (bf16[4,8,48,128]{3,2,1,0:T(8,128)(2,1)S(1)}, bf16[4,8,48,128]{3,2,1,0:T(8,128)(2,1)S(1)}, u32[]{:S(2)}, u32[]{:S(2)}) collective-permute-start(bf16[4,8,48,128]{3,2,1,0:T(8,128)(2,1)S(1)} %get-tuple-element.52), channel_id=1, source_target_pairs={{0,4},{4,0},{8,12},{12,8},{1,5},{5,1},{9,13},{13,9},{2,6},{6,2},{1... | collective-permute-start | bytes 1179656 | tf_op jit(solution)/shard_map/ppermute | solution.py:314
  55.1 18.8 %collective-permute-start.20 = (bf16[4,8,48,128]{3,2,1,0:T(8,128)(2,1)S(1)}, bf16[4,8,48,128]{3,2,1,0:T(8,128)(2,1)S(1)}, u32[]{:S(2)}, u32[]{:S(2)}) collective-permute-start(bf16[4,8,48,128]{3,2,1,0:T(8,128)(2,1)S(1)} %get-tuple-element.66.refs_4_), channel_id=1, source_target_pairs={{0,2},{2,0},{1,3},{3,1},{4,6},{6,4},{5,7},{7,5},{8,10},{10,8},{9,1... | collective-permute-start | bytes 1179656 | tf_op jit(solution)/shard_map/ppermute | solution.py:314
  62.6 9.4 %collective-permute-start.10 = (bf16[2,8,48,128]{3,2,1,0:T(8,128)(2,1)S(1)}, bf16[2,8,48,128]{3,2,1,0:T(8,128)(2,1)S(1)}, u32[]{:S(2)}, u32[]{:S(2)}) collective-permute-start(bf16[2,8,48,128]{3,2,1,0:T(8,128)(2,1)S(1)} %shard_map.58.refs_2_), channel_id=1, source_target_pairs={{0,2},{2,0},{1,3},{3,1},{4,6},{6,4},{5,7},{7,5},{8,10},{10,8},{9,1... | collective-permute-start | bytes 589832 | tf_op jit(solution)/shard_map/ppermute | solution.py:314
  64.7 9.3 %collective-permute-start.9 = (bf16[2,8,48,128]{3,2,1,0:T(8,128)(2,1)S(1)}, bf16[2,8,48,128]{3,2,1,0:T(8,128)(2,1)S(1)}, u32[]{:S(2)}, u32[]{:S(2)}) collective-permute-start(bf16[2,8,48,128]{3,2,1,0:T(8,128)(2,1)S(1)} %shard_map.57.refs_1_), channel_id=1, source_target_pairs={{0,2},{2,0},{1,3},{3,1},{4,6},{6,4},{5,7},{7,5},{8,10},{10,8},{9,1... | collective-permute-start | bytes 589832 | tf_op jit(solution)/shard_map/ppermute | solution.py:314
  76.4 8.2 %collective-permute-start.24 = (bf16[272,128]{1,0:T(8,128)(2,1)S(1)}, bf16[272,128]{1,0:T(8,128)(2,1)S(1)}, u32[]{:S(2)}, u32[]{:S(2)}) collective-permute-start(bf16[272,128]{1,0:T(8,128)(2,1)S(1)} %get-tuple-element.75), channel_id=1, source_target_pairs={{0,8},{4,12},{8,0},{12,4},{1,9},{5,13},{9,1},{13,5},{2,10},{6,14},... | collective-permute-start | bytes 208904 | tf_op jit(solution)/shard_map/ppermute | solution.py:585
  77.9 5.8 %collective-permute-start.25 = (bf16[144,128]{1,0:T(8,128)(2,1)S(1)}, bf16[144,128]{1,0:T(8,128)(2,1)S(1)}, u32[]{:S(2)}, u32[]{:S(2)}) collective-permute-start(bf16[144,128]{1,0:T(8,128)(2,1)S(1)} %get-tuple-element.76), channel_id=1, source_target_pairs={{0,12},{4,8},{8,4},{12,0},{1,13},{5,9},{9,5},{13,1},{2,14},{6,10},... | collective-permute-start | bytes 110600 | tf_op jit(solution)/shard_map/ppermute | solution.py:585
  84.6 4.4 %collective-permute-start.27 = (bf16[272,128]{1,0:T(8,128)(2,1)S(1)}, bf16[272,128]{1,0:T(8,128)(2,1)S(1)}, u32[]{:S(2)}, u32[]{:S(2)}) collective-permute-start(bf16[272,128]{1,0:T(8,128)(2,1)S(1)} %shard_map.70.mine_ref), channel_id=1, source_target_pairs={{0,2},{2,0},{1,3},{3,1},{4,6},{6,4},{5,7},{7,5},{8,10},{10,8},{9,1... | collective-permute-start | bytes 208904 | tf_op jit(solution)/shard_map/ppermute | solution.py:314
  (9 other events, 46.7 us)

commit v20 on v19

--- a/solution.py
+++ b/solution.py
@@ -399,30 +399,45 @@
     )(*flat(groups))
 
 
-def inner_sum_body(keep_ref, got_ref, tail_ref, own_ref, sent_ref):
-    size = 2 * LANES
-    row = pl.multiple_of(lax.rem(lax.axis_index("slab"), 2) * LANES, LANES)
-    own, other = pl.ds(row, LANES), pl.ds(LANES - row, LANES)
-    own_ref[...] = keep_ref[own] + got_ref[own]
-    sent_ref[...] = (keep_ref[other] + got_ref[other]).astype(BF16)
-    tail_ref[...] = keep_ref[size:] + got_ref[size:]
-
-
-def inner_sum(keep, got):
-    return call(
-        inner_sum_body,
+def inner_rows_body(keep_ref, got_ref, tail_ref, *outs):
+    slab = lax.axis_index("slab")
+    chip = lax.axis_index("probe")
+    tail_ref[...] = keep_ref[2 * LANES :] + got_ref[2 * LANES :]
+    for d, out in enumerate(outs):
+        row = jnp.clip((slab ^ d) - 2 * chip, 0, 1)
+        span = pl.ds(pl.multiple_of(row * LANES, LANES), LANES)
+        out[...] = (keep_ref[span] + got_ref[span]).astype(out.dtype)
+
+
+def inner_rows(keep, got, slabs):
+    own = jax.ShapeDtypeStruct((LANES, LANES), F32)
+    sent = jax.ShapeDtypeStruct((LANES, LANES), BF16)
+    return call(
+        inner_rows_body,
         in_specs=whole_vmem(2),
-        out_specs=whole_vmem(3),
-        out_shape=[
-            jax.ShapeDtypeStruct((8, LANES), F32),
-            jax.ShapeDtypeStruct((LANES, LANES), F32),
-            jax.ShapeDtypeStruct((LANES, LANES), BF16),
-        ],
+        out_specs=whole_vmem(1 + slabs),
+        out_shape=[jax.ShapeDtypeStruct((8, LANES), F32), own] + [sent] * (slabs - 1),
     )(keep, got)
 
 
+def inner_total_body(own_ref, *refs):
+    total = own_ref[...]
+    for ref in refs[:-1]:
+        total = total + ref[...].astype(F32)
+    refs[-1][...] = total.astype(BF16)
+
+
+def inner_total(own, others):
+    return call(
+        inner_total_body,
+        in_specs=whole_vmem(1 + len(others)),
+        out_specs=whole_vmem(1)[0],
+        out_shape=jax.ShapeDtypeStruct(own.shape, BF16),
+    )(own, *others)
+
+
 def cross_body(sizes, *refs):
-    groups, (_, keep_ref, send_ref, panel) = regroup(sizes, refs)
+    groups, (*_, keep_ref, send_ref, panel) = regroup(sizes, refs)
     chip = lax.axis_index("probe")
     core = lax.axis_index("sub")
     for n in range(2):
@@ -444,11 +459,11 @@
     three = jax.ShapeDtypeStruct((3 * LANES, LANES), F32)
     return call(
         functools.partial(cross_body, [len(group) for group in groups]),
-        in_specs=whole_vmem(len(flat(groups))) + [pl.BlockSpec(memory_space=pl.ANY)],
+        in_specs=whole_vmem(len(flat(groups))) + [pl.BlockSpec(memory_space=pl.ANY)] * len(after),
         out_specs=whole_vmem(2),
         out_shape=[three, three],
         scratch_shapes=[pltpu.VMEM((cells, 4 * LANES), BF16)],
-    )(*flat(groups), after)
+    )(*flat(groups), *after)
 
 
 def rounded(ref, block, tail):
@@ -464,11 +479,10 @@
     return ref[:count].astype(F32), tail[:8] + tail[8:]
 
 
-def cross_rows_body(keep_ref, got_ref, tail_ref, inner_ref, inner_got_ref, own_ref, *outs):
+def cross_rows_body(keep_ref, got_ref, tail_ref, own_ref, *outs):
     slab = lax.axis_index("slab")
     core = lax.axis_index("sub")
     tail = tail_ref[...]
-    inner = inner_ref[...] + inner_got_ref[...].astype(F32)
     for d in range(len(outs) + 1):
         owner = slab ^ d
         late = jnp.where(core == 0, jnp.where(owner == 2, 0, 2), jnp.where(owner == 2, 2, 1))
@@ -477,35 +491,29 @@
         block = keep_ref[span] + got_ref[span]
         if d == 0:
             own_ref[:LANES] = block
-            own_ref[LANES : LANES + 8] = tail
-            own_ref[LANES + 8 :] = inner
+            own_ref[LANES:] = tail
         else:
             rounded(outs[d - 1], block, tail)
-            if d == 2:
-                outs[1][LANES + 16 :] = inner.astype(BF16)
-
-
-def cross_rows(keep, got, tail, inner, inner_got, slabs):
-    own = jax.ShapeDtypeStruct((2 * LANES + 8, LANES), F32)
-    long = jax.ShapeDtypeStruct((2 * LANES + 16, LANES), BF16)
-    short = jax.ShapeDtypeStruct((LANES + 16, LANES), BF16)
+
+
+def cross_rows(keep, got, tail, slabs):
+    own = jax.ShapeDtypeStruct((LANES + 8, LANES), F32)
+    sent = jax.ShapeDtypeStruct((LANES + 16, LANES), BF16)
     return call(
         cross_rows_body,
-        in_specs=whole_vmem(5),
+        in_specs=whole_vmem(3),
         out_specs=whole_vmem(slabs),
-        out_shape=[own, short, long, short],
-    )(keep, got, tail, inner, inner_got)
+        out_shape=[own] + [sent] * (slabs - 1),
+    )(keep, got, tail)
 
 
 def sum_body(own_ref, *refs):
-    block, tail = own_ref[:LANES], own_ref[LANES : LANES + 8]
+    block, tail = own_ref[:LANES], own_ref[LANES:]
     *others, out_ref = refs
     for ref in others:
         more, more_tail = opened(ref, LANES)
         block, tail = block + more, tail + more_tail
-    inner = own_ref[LANES + 8 :] + others[0][LANES + 16 :].astype(F32)
     rounded(out_ref, block, tail)
-    out_ref[LANES + 16 :] = inner.astype(BF16)
 
 
 def sum_all(own, others):
@@ -517,15 +525,14 @@
     )(own, *others)
 
 
-def normalise_body(cell_count, mine_ref, other_ref, out_ref, norms_ref):
+def normalise_body(cell_count, mine_ref, other_ref, inner_ref, other_inner_ref, out_ref, norms_ref):
     slab = lax.axis_index("slab")
     core = lax.axis_index("sub")
     chip = lax.axis_index("probe")
     one, one_tail = opened(mine_ref, LANES)
     two, two_tail = opened(other_ref, LANES)
     cross = one + two
-    inner_span = pl.ds(LANES + 16, LANES)
-    inner = jnp.where(slab // 2 == chip, mine_ref[inner_span], other_ref[inner_span]).astype(F32)
+    inner = jnp.where(slab // 2 == chip, inner_ref[...], other_inner_ref[...]).astype(F32)
     upper = slab < 2
     values = [jnp.where(upper, inner, cross.T), jnp.where(upper, cross, inner)]
     norms = jnp.sqrt((one_tail + two_tail) / cell_count + EPSILON)
@@ -544,16 +551,16 @@
         out_ref[:, side * LANES : (side + 1) * LANES] = value
 
 
-def normalise(mine, other, cell_count):
+def normalise(mine, other, inner, other_inner, cell_count):
     return call(
         functools.partial(normalise_body, cell_count),
-        in_specs=whole_vmem(2),
+        in_specs=whole_vmem(4),
         out_specs=whole_vmem(2),
         out_shape=[
             jax.ShapeDtypeStruct((LANES, 2 * LANES), F32),
             jax.ShapeDtypeStruct((1, LANES), F32),
         ],
-    )(mine, other)
+    )(mine, other, inner, other_inner)
 
 
 def assemble_body(near_ref, far_ref, out_ref):
@@ -577,16 +584,26 @@
 def coupled(finals, cell_count):
     slabs = 4
     keep, send = inner_gram([kept + sent for kept, sent, _ in finals])
-    tail, inner, sent = inner_sum(keep, core_swap(send))
-    inner_got = lax.ppermute(sent, "slab", [(i, i ^ 1) for i in range(slabs)])
-    keep, send = cross_gram([g for kept, _, got in finals for g in (kept, got)], inner_got)
-    mine, *blocks = cross_rows(keep, core_swap(send), tail, inner, inner_got, slabs)
+    tail, own, *sent = inner_rows(keep, core_swap(send), slabs)
+    inner_arrived = []
+    for d in (2, 3, 1):
+        pairs = [
+            (2 * (k ^ d) + chip, 2 * k + chip)
+            for chip in range(2)
+            for k in (2 * chip, 2 * chip + 1)
+        ]
+        inner_arrived.append(lax.ppermute(sent[d - 1], ("slab", "probe"), pairs))
+    inner = inner_total(own, inner_arrived)
+
+    groups = [group for kept, _, got in finals for group in (kept, got)]
+    keep, send = cross_gram(groups, inner_arrived)
+    mine, *blocks = cross_rows(keep, core_swap(send), tail, slabs)
     arrived = [
         lax.ppermute(blocks[d - 1], "slab", [(i, i ^ d) for i in range(slabs)])
         for d in (2, 3, 1)
     ]
     total = sum_all(mine, arrived)
-    near, norms = normalise(total, chip_swap(total), cell_count)
+    near, norms = normalise(total, chip_swap(total), inner, chip_swap(inner), cell_count)
     return assemble(near, core_swap(near)), norms.reshape(-1)
 
 

time: 91.9 us -> 97.8 us (1.064)
  starting transfers between devices: 37.3 us -> 41.8 us
  waiting for transfers between devices: 25.8 us -> 27.1 us
    ppermute x1 -> x3, waiting for transfers between devices: 2.17 us -> 7.13 us  [coupled(): inner_arrived.append(lax.ppermute(sent[d - 1], ('slab', 'probe'), pairs))]
    ppermute x1 -> x3, starting transfers between devices: 1.81 us -> 5.85 us  [coupled(): inner_arrived.append(lax.ppermute(sent[d - 1], ('slab', 'probe'), pairs))]
    ppermute x25 -> x26, waiting for transfers between devices: 19.3 us -> 16 us  [swap(): lax.ppermute(x, axis, [p for a, b in pairs for p in ((a, b), (b, a))])]
    ppermute x25 -> x26, starting transfers between devices: 31.7 us -> 32.2 us  [swap(): lax.ppermute(x, axis, [p for a, b in pairs for p in ((a, b), (b, a))])]
  transfers between devices with their start and end apart: 29 -> 32, of which waited for: 14 -> 14; matrix products, arithmetic and copies ran while one was open for 0% -> 0% of each run, Pallas kernels for 24% -> 23%
where the time goes in v20:
time: 97.8 us; the launch traced here: 97.4 us
  starting transfers between devices  41.8 us (43%)
  waiting for transfers between devices  27.1 us (28%)
  Pallas kernels  25.3 us (26%)
  local copies, waits for them, and re-layouts  2.18 us (2%)
  between operations  1.04 us (1%)
    ppermute x26, starting transfers between devices, swap(): lax.ppermute(x, axis, [p for a, b in pairs for p in ((a, b), (b, a))])  32.2 us
    ppermute x26, waiting for transfers between devices, swap(): lax.ppermute(x, axis, [p for a, b in pairs for p in ((a, b), (b, a))])  16 us
    pallas_call x6, Pallas kernels, local_step(): call(functools.partial(local_body, chunk, moment, previous is not None),...  13.3 us
    ppermute x3, waiting for transfers between devices, coupled(): inner_arrived.append(lax.ppermute(sent[d - 1], ('slab', 'probe'), pairs))  7.13 us
    ppermute x3, starting transfers between devices, coupled(): inner_arrived.append(lax.ppermute(sent[d - 1], ('slab', 'probe'), pairs))  5.85 us
    pallas_call x5, Pallas kernels, rim_step(): call(functools.partial(rim_body, kind), in_specs=whole_vmem(4), out_specs...  5.35 us
    ppermute x3, waiting for transfers between devices, coupled(): lax.ppermute(blocks[d - 1], 'slab', [(i, i ^ d) for i in range(slabs)])  3.95 us
    ppermute x3, starting transfers between devices, coupled(): lax.ppermute(blocks[d - 1], 'slab', [(i, i ^ d) for i in range(slabs)])  3.79 us
  transfers between devices with their start and end apart: 32, of which 14 were waited for; matrix products, arithmetic and copies ran while one was open for 0% of the time, Pallas kernels for 23%

profile of v20, /device:TPU:0, one launch (start us, length us, event | category | flops | bytes accessed | tf_op | source)
XLA Modules:
  0.0 97.4 jit_solution(317025500809574870)
XLA Ops:
  1.4 1.4 %copy-done = bf16[8,8,48,256]{3,2,1,0:T(8,128)(2,1)S(1)} copy-done((bf16[8,8,48,256]{3,2,1,0:T(8,128)(2,1)S(1)}, bf16[8,8,48,256]{3,2,1,0:T(8,128)(2,1)}, u32[]{:S(2)}) %copy-start) | copy-done | bytes 1572888
  5.1 5.5 %collective-permute-start.13 = (bf16[4,8,48,128]{3,2,1,0:T(8,128)(2,1)S(1)}, bf16[4,8,48,128]{3,2,1,0:T(8,128)(2,1)S(1)}, u32[]{:S(2)}, u32[]{:S(2)}) collective-permute-start(bf16[4,8,48,128]{3,2,1,0:T(8,128)(2,1)S(1)} %get-tuple-element.58), channel_id=1, source_target_pairs={{0,4},{4,0},{8,12},{12,8},{1,5},{5,1},{9,13},{13,9},{2,6},{6,2},{1... | collective-permute-start | bytes 1179656 | tf_op jit(solution)/shard_map/ppermute | solution.py:314
  12.4 1.9 %collective-permute-start.2 = (bf16[4,8,48,128]{3,2,1,0:T(8,128)(2,1)S(1)}, bf16[4,8,48,128]{3,2,1,0:T(8,128)(2,1)S(1)}, u32[]{:S(2)}, u32[]{:S(2)}) collective-permute-start(bf16[4,8,48,128]{3,2,1,0:T(8,128)(2,1)S(1)} %get-tuple-element.46), channel_id=1, source_target_pairs={{0,4},{4,0},{8,12},{12,8},{1,5},{5,1},{9,13},{13,9},{2,6},{6,2},{1... | collective-permute-start | bytes 1179656 | tf_op jit(solution)/shard_map/ppermute | solution.py:314
  14.3 2.1 %shard_map.60.refs_0_ = f32[8,8,48,128]{3,2,1,0:T(8,128)S(1)} custom-call(f32[8,8,64,128]{3,2,1,0:T(8,128)S(1)} %get-tuple-element.55.refs_0_.refs_5_, bf16[8,4,48,128]{3,2,1,0:T(8,128)(2,1)S(1)} %collective-permute-done.11.refs_1_, bf16[8,8,48,256]{3,2,1,0:T(8,128)(2,1)S(1)} %copy-done, f32[64,48]{1,0:T(8,128)S(1)} %bitcast.5, f32[4,64,48]{2,1,0:T(8,128)S(1)} %bitcast.19), custom_call_target="tpu_custom_call" | custom-call | flops 1 | bytes 1 | tf_op jit(solution)/shard_map/pallas_call | solution.py:185
  16.5 3.9 %collective-permute-done.13.refs_2_ = bf16[4,8,48,128]{3,2,1,0:T(8,128)(2,1)S(1)} collective-permute-done((bf16[4,8,48,128]{3,2,1,0:T(8,128)(2,1)S(1)}, bf16[4,8,48,128]{3,2,1,0:T(8,128)(2,1)S(1)}, u32[]{:S(2)}, u32[]{:S(2)}) %collective-permute-start.13) | collective-permute-done | bytes 393248 | tf_op jit(solution)/shard_map/ppermute | solution.py:314
  22.3 3.8 %collective-permute-start.16 = (bf16[4,8,48,128]{3,2,1,0:T(8,128)(2,1)S(1)}, bf16[4,8,48,128]{3,2,1,0:T(8,128)(2,1)S(1)}, u32[]{:S(2)}, u32[]{:S(2)}) collective-permute-start(bf16[4,8,48,128]{3,2,1,0:T(8,128)(2,1)S(1)} %get-tuple-element.62), channel_id=1, source_target_pairs={{0,4},{4,0},{8,12},{12,8},{1,5},{5,1},{9,13},{13,9},{2,6},{6,2},{1... | collective-permute-start | bytes 1179656 | tf_op jit(solution)/shard_map/ppermute | solution.py:314
  26.1 2.1 %shard_map.51.refs_0_ = f32[8,8,48,128]{3,2,1,0:T(8,128)S(1)} custom-call(f32[8,8,64,128]{3,2,1,0:T(8,128)S(1)} %get-tuple-element.43.refs_0_.refs_5_, bf16[8,4,48,128]{3,2,1,0:T(8,128)(2,1)S(1)} %collective-permute-done.refs_1_, bf16[8,8,48,256]{3,2,1,0:T(8,128)(2,1)S(1)} %copy-done.1, f32[64,48]{1,0:T(8,128)S(1)} %bitcast.7, f32[4,64,48]{2,1,0:T(8,128)S(1)} %bitcast.20), custom_call_target="tpu_custom_call" | custom-call | flops 1 | bytes 1 | tf_op jit(solution)/shard_map/pallas_call | solution.py:185
  30.7 3.4 %collective-permute-start.5 = (bf16[4,8,48,128]{3,2,1,0:T(8,128)(2,1)S(1)}, bf16[4,8,48,128]{3,2,1,0:T(8,128)(2,1)S(1)}, u32[]{:S(2)}, u32[]{:S(2)}) collective-permute-start(bf16[4,8,48,128]{3,2,1,0:T(8,128)(2,1)S(1)} %get-tuple-element.50), channel_id=1, source_target_pairs={{0,4},{4,0},{8,12},{12,8},{1,5},{5,1},{9,13},{13,9},{2,6},{6,2},{1... | collective-permute-start | bytes 1179656 | tf_op jit(solution)/shard_map/ppermute | solution.py:314
  34.1 2.3 %shard_map.62.refs_0_ = f32[8,8,48,128]{3,2,1,0:T(8,128)S(1)} custom-call(f32[8,8,64,128]{3,2,1,0:T(8,128)S(1)} %get-tuple-element.59.refs_0_.refs_5_, bf16[8,4,48,128]{3,2,1,0:T(8,128)(2,1)S(1)} %collective-permute-done.14.refs_1_, bf16[8,8,48,256]{3,2,1,0:T(8,128)(2,1)S(1)} %copy-done.1, f32[64,48]{1,0:T(8,128)S(1)} %bitcast.9, f32[4,64,48]{2,1,0:T(8,128)S(1)} %bitcast.21, ...), custom_call_target="tpu_custom_call" | custom-call | flops 1 | bytes 1 | tf_op jit(solution)/shard_map/pallas_call | solution.py:185
  39.2 3.4 %collective-permute-start.19 = (bf16[4,8,48,128]{3,2,1,0:T(8,128)(2,1)S(1)}, bf16[4,8,48,128]{3,2,1,0:T(8,128)(2,1)S(1)}, u32[]{:S(2)}, u32[]{:S(2)}) collective-permute-start(bf16[4,8,48,128]{3,2,1,0:T(8,128)(2,1)S(1)} %get-tuple-element.66), channel_id=1, source_target_pairs={{0,4},{4,0},{8,12},{12,8},{1,5},{5,1},{9,13},{13,9},{2,6},{6,2},{1... | collective-permute-start | bytes 1179656 | tf_op jit(solution)/shard_map/ppermute | solution.py:314
  42.5 2.2 %shard_map.53.refs_0_ = f32[8,8,48,128]{3,2,1,0:T(8,128)S(1)} custom-call(f32[8,8,64,128]{3,2,1,0:T(8,128)S(1)} %get-tuple-element.47.refs_0_.refs_5_, bf16[8,4,48,128]{3,2,1,0:T(8,128)(2,1)S(1)} %collective-permute-done.3.refs_1_, bf16[8,8,48,256]{3,2,1,0:T(8,128)(2,1)S(1)} %copy-done.1, f32[64,48]{1,0:T(8,128)S(1)} %bitcast.11, f32[4,64,48]{2,1,0:T(8,128)S(1)} %bitcast.22, ...), custom_call_target="tpu_custom_call" | custom-call | flops 1 | bytes 1 | tf_op jit(solution)/shard_map/pallas_call | solution.py:185
  47.6 3.4 %collective-permute-start.8 = (bf16[4,8,48,128]{3,2,1,0:T(8,128)(2,1)S(1)}, bf16[4,8,48,128]{3,2,1,0:T(8,128)(2,1)S(1)}, u32[]{:S(2)}, u32[]{:S(2)}) collective-permute-start(bf16[4,8,48,128]{3,2,1,0:T(8,128)(2,1)S(1)} %get-tuple-element.54), channel_id=1, source_target_pairs={{0,4},{4,0},{8,12},{12,8},{1,5},{5,1},{9,13},{13,9},{2,6},{6,2},{1... | collective-permute-start | bytes 1179656 | tf_op jit(solution)/shard_map/ppermute | solution.py:314
  50.9 2.3 %shard_map.64.refs_0_ = f32[8,8,48,128]{3,2,1,0:T(8,128)S(1)} custom-call(f32[8,8,64,128]{3,2,1,0:T(8,128)S(1)} %get-tuple-element.63.refs_0_, bf16[8,4,48,128]{3,2,1,0:T(8,128)(2,1)S(1)} %collective-permute-done.17.refs_1_, bf16[8,8,48,256]{3,2,1,0:T(8,128)(2,1)S(1)} %copy-done.1, f32[64,48]{1,0:T(8,128)S(1)} %bitcast.13, f32[4,64,48]{2,1,0:T(8,128)S(1)} %bitcast.23, ...), custom_call_target="tpu_custom_call" | custom-call | flops 1 | bytes 1 | tf_op jit(solution)/shard_map/pallas_call | solution.py:185
  55.1 1.6 %collective-permute-start.20 = (bf16[4,8,48,128]{3,2,1,0:T(8,128)(2,1)S(1)}, bf16[4,8,48,128]{3,2,1,0:T(8,128)(2,1)S(1)}, u32[]{:S(2)}, u32[]{:S(2)}) collective-permute-start(bf16[4,8,48,128]{3,2,1,0:T(8,128)(2,1)S(1)} %get-tuple-element.68.refs_4_), channel_id=1, source_target_pairs={{0,2},{2,0},{1,3},{3,1},{4,6},{6,4},{5,7},{7,5},{8,10},{10,8},{9,1... | collective-permute-start | bytes 1179656 | tf_op jit(solution)/shard_map/ppermute | solution.py:314
  56.6 2.2 %shard_map.55.base_ref = f32[8,8,48,128]{3,2,1,0:T(8,128)S(1)} custom-call(f32[8,8,64,128]{3,2,1,0:T(8,128)S(1)} %get-tuple-element.51.refs_0_, bf16[8,4,48,128]{3,2,1,0:T(8,128)(2,1)S(1)} %collective-permute-done.6.refs_1_, bf16[8,8,48,256]{3,2,1,0:T(8,128)(2,1)S(1)} %copy-done.1, f32[64,48]{1,0:T(8,128)S(1)} %bitcast.15, f32[4,64,48]{2,1,0:T(8,128)S(1)} %bitcast.24, ...), custom_call_target="tpu_custom_call" | custom-call | flops 1 | bytes 1 | tf_op jit(solution)/shard_map/pallas_call | solution.py:185
  58.9 3.2 %collective-permute-done.8.even_ref = bf16[4,8,48,128]{3,2,1,0:T(8,128)(2,1)S(1)} collective-permute-done((bf16[4,8,48,128]{3,2,1,0:T(8,128)(2,1)S(1)}, bf16[4,8,48,128]{3,2,1,0:T(8,128)(2,1)S(1)}, u32[]{:S(2)}, u32[]{:S(2)}) %collective-permute-start.8) | collective-permute-done | bytes 393248 | tf_op jit(solution)/shard_map/ppermute | solution.py:314
  64.5 1.6 %collective-permute-start.10 = (bf16[2,8,48,128]{3,2,1,0:T(8,128)(2,1)S(1)}, bf16[2,8,48,128]{3,2,1,0:T(8,128)(2,1)S(1)}, u32[]{:S(2)}, u32[]{:S(2)}) collective-permute-start(bf16[2,8,48,128]{3,2,1,0:T(8,128)(2,1)S(1)} %shard_map.58.refs_2_), channel_id=1, source_target_pairs={{0,2},{2,0},{1,3},{3,1},{4,6},{6,4},{5,7},{7,5},{8,10},{10,8},{9,1... | collective-permute-start | bytes 589832 | tf_op jit(solution)/shard_map/ppermute | solution.py:314
  69.2 4.6 %collective-permute-done.22.refs_5_.refs_0_ = bf16[128,128]{1,0:T(8,128)(2,1)S(1)} collective-permute-done((bf16[128,128]{1,0:T(8,128)(2,1)S(1)}, bf16[128,128]{1,0:T(8,128)(2,1)S(1)}, u32[]{:S(2)}, u32[]{:S(2)}) %collective-permute-start.22) | collective-permute-done | bytes 32800 | tf_op jit(solution)/shard_map/ppermute | solution.py:595
  73.9 3.3 %collective-permute-start.24 = (bf16[128,128]{1,0:T(8,128)(2,1)S(1)}, bf16[128,128]{1,0:T(8,128)(2,1)S(1)}, u32[]{:S(2)}, u32[]{:S(2)}) collective-permute-start(bf16[128,128]{1,0:T(8,128)(2,1)S(1)} %get-tuple-element.73), channel_id=1, source_target_pairs={{4,0},{0,4},{14,10},{10,14},{5,1},{1,5},{15,11},{11,15},{20,16},{1... | collective-permute-start | bytes 98312 | tf_op jit(solution)/shard_map/ppermute | solution.py:595
  77.1 2.5 %collective-permute-done.24.refs_7_.refs_2_ = bf16[128,128]{1,0:T(8,128)(2,1)S(1)} collective-permute-done((bf16[128,128]{1,0:T(8,128)(2,1)S(1)}, bf16[128,128]{1,0:T(8,128)(2,1)S(1)}, u32[]{:S(2)}, u32[]{:S(2)}) %collective-permute-start.24) | collective-permute-done | bytes 32800 | tf_op jit(solution)/shard_map/ppermute | solution.py:595
  80.6 1.4 %collective-permute-done.25.got_ref = f32[384,128]{1,0:T(8,128)S(1)} collective-permute-done((f32[384,128]{1,0:T(8,128)S(1)}, f32[384,128]{1,0:T(8,128)S(1)}, u32[]{:S(2)}, u32[]{:S(2)}) %collective-permute-start.25) | collective-permute-done | bytes 196640 | tf_op jit(solution)/shard_map/ppermute | solution.py:314
  82.2 3.7 %collective-permute-start.27 = (bf16[144,128]{1,0:T(8,128)(2,1)S(1)}, bf16[144,128]{1,0:T(8,128)(2,1)S(1)}, u32[]{:S(2)}, u32[]{:S(2)}) collective-permute-start(bf16[144,128]{1,0:T(8,128)(2,1)S(1)} %get-tuple-element.79), channel_id=1, source_target_pairs={{0,12},{4,8},{8,4},{12,0},{1,13},{5,9},{9,5},{13,1},{2,14},{6,10},... | collective-permute-start | bytes 110600 | tf_op jit(solution)/shard_map/ppermute | solution.py:602
  85.9 2.3 %collective-permute-done.26.refs_0_ = bf16[144,128]{1,0:T(8,128)(2,1)S(1)} collective-permute-done((bf16[144,128]{1,0:T(8,128)(2,1)S(1)}, bf16[144,128]{1,0:T(8,128)(2,1)S(1)}, u32[]{:S(2)}, u32[]{:S(2)}) %collective-permute-start.26) | collective-permute-done | bytes 36896 | tf_op jit(solution)/shard_map/ppermute | solution.py:602
  92.1 2.7 %collective-permute-done.30.other_inner_ref = bf16[128,128]{1,0:T(8,128)(2,1)S(1)} collective-permute-done((bf16[128,128]{1,0:T(8,128)(2,1)S(1)}, bf16[128,128]{1,0:T(8,128)(2,1)S(1)}, u32[]{:S(2)}, u32[]{:S(2)}) %collective-permute-start.30) | collective-permute-done | bytes 32800 | tf_op jit(solution)/shard_map/ppermute | solution.py:314
  (73 shorter events, 29.6 us)
Async XLA Ops:
  3.9 8.5 %collective-permute-start.11 = (bf16[8,4,48,128]{3,2,1,0:T(8,128)(2,1)S(1)}, bf16[8,4,48,128]{3,2,1,0:T(8,128)(2,1)S(1)}, u32[]{:S(2)}, u32[]{:S(2)}) collective-permute-start(bf16[8,4,48,128]{3,2,1,0:T(8,128)(2,1)S(1)} %get-tuple-element.56), channel_id=1, source_target_pairs={{0,1},{1,0},{2,3},{3,2},{4,5},{5,4},{6,7},{7,6},{8,9},{9,8},{10,11... | collective-permute-start | bytes 1179656 | tf_op jit(solution)/shard_map/ppermute | solution.py:314
  4.4 12.1 %collective-permute-start.12 = (bf16[4,8,48,128]{3,2,1,0:T(8,128)(2,1)S(1)}, bf16[4,8,48,128]{3,2,1,0:T(8,128)(2,1)S(1)}, u32[]{:S(2)}, u32[]{:S(2)}) collective-permute-start(bf16[4,8,48,128]{3,2,1,0:T(8,128)(2,1)S(1)} %get-tuple-element.57), channel_id=1, source_target_pairs={{4,8},{8,4},{5,9},{9,5},{6,10},{10,6},{7,11},{11,7},{20,24},{24,20... | collective-permute-start | bytes 1179656 | tf_op jit(solution)/shard_map/ppermute | solution.py:314
  5.1 15.4 %collective-permute-start.13 = (bf16[4,8,48,128]{3,2,1,0:T(8,128)(2,1)S(1)}, bf16[4,8,48,128]{3,2,1,0:T(8,128)(2,1)S(1)}, u32[]{:S(2)}, u32[]{:S(2)}) collective-permute-start(bf16[4,8,48,128]{3,2,1,0:T(8,128)(2,1)S(1)} %get-tuple-element.58), channel_id=1, source_target_pairs={{0,4},{4,0},{8,12},{12,8},{1,5},{5,1},{9,13},{13,9},{2,6},{6,2},{1... | collective-permute-start | bytes 1179656 | tf_op jit(solution)/shard_map/ppermute | solution.py:314
  11.6 10.7 %collective-permute-start = (bf16[8,4,48,128]{3,2,1,0:T(8,128)(2,1)S(1)}, bf16[8,4,48,128]{3,2,1,0:T(8,128)(2,1)S(1)}, u32[]{:S(2)}, u32[]{:S(2)}) collective-permute-start(bf16[8,4,48,128]{3,2,1,0:T(8,128)(2,1)S(1)} %get-tuple-element.44), channel_id=1, source_target_pairs={{0,1},{1,0},{2,3},{3,2},{4,5},{5,4},{6,7},{7,6},{8,9},{9,8},{10,11... | collective-permute-start | bytes 1179656 | tf_op jit(solution)/shard_map/ppermute | solution.py:314
  11.7 16.6 %collective-permute-start.1 = (bf16[4,8,48,128]{3,2,1,0:T(8,128)(2,1)S(1)}, bf16[4,8,48,128]{3,2,1,0:T(8,128)(2,1)S(1)}, u32[]{:S(2)}, u32[]{:S(2)}) collective-permute-start(bf16[4,8,48,128]{3,2,1,0:T(8,128)(2,1)S(1)} %get-tuple-element.45), channel_id=1, source_target_pairs={{4,8},{8,4},{5,9},{9,5},{6,10},{10,6},{7,11},{11,7},{20,24},{24,20... | collective-permute-start | bytes 1179656 | tf_op jit(solution)/shard_map/ppermute | solution.py:314
  12.4 16.5 %collective-permute-start.2 = (bf16[4,8,48,128]{3,2,1,0:T(8,128)(2,1)S(1)}, bf16[4,8,48,128]{3,2,1,0:T(8,128)(2,1)S(1)}, u32[]{:S(2)}, u32[]{:S(2)}) collective-permute-start(bf16[4,8,48,128]{3,2,1,0:T(8,128)(2,1)S(1)} %get-tuple-element.46), channel_id=1, source_target_pairs={{0,4},{4,0},{8,12},{12,8},{1,5},{5,1},{9,13},{13,9},{2,6},{6,2},{1... | collective-permute-start | bytes 1179656 | tf_op jit(solution)/shard_map/ppermute | solution.py:314
  21.5 9.2 %collective-permute-start.14 = (bf16[8,4,48,128]{3,2,1,0:T(8,128)(2,1)S(1)}, bf16[8,4,48,128]{3,2,1,0:T(8,128)(2,1)S(1)}, u32[]{:S(2)}, u32[]{:S(2)}) collective-permute-start(bf16[8,4,48,128]{3,2,1,0:T(8,128)(2,1)S(1)} %get-tuple-element.60), channel_id=1, source_target_pairs={{0,1},{1,0},{2,3},{3,2},{4,5},{5,4},{6,7},{7,6},{8,9},{9,8},{10,11... | collective-permute-start | bytes 1179656 | tf_op jit(solution)/shard_map/ppermute | solution.py:314
  21.6 14.8 %collective-permute-start.15 = (bf16[4,8,48,128]{3,2,1,0:T(8,128)(2,1)S(1)}, bf16[4,8,48,128]{3,2,1,0:T(8,128)(2,1)S(1)}, u32[]{:S(2)}, u32[]{:S(2)}) collective-permute-start(bf16[4,8,48,128]{3,2,1,0:T(8,128)(2,1)S(1)} %get-tuple-element.61), channel_id=1, source_target_pairs={{4,8},{8,4},{5,9},{9,5},{6,10},{10,6},{7,11},{11,7},{20,24},{24,20... | collective-permute-start | bytes 1179656 | tf_op jit(solution)/shard_map/ppermute | solution.py:314
  22.3 15.0 %collective-permute-start.16 = (bf16[4,8,48,128]{3,2,1,0:T(8,128)(2,1)S(1)}, bf16[4,8,48,128]{3,2,1,0:T(8,128)(2,1)S(1)}, u32[]{:S(2)}, u32[]{:S(2)}) collective-permute-start(bf16[4,8,48,128]{3,2,1,0:T(8,128)(2,1)S(1)} %get-tuple-element.62), channel_id=1, source_target_pairs={{0,4},{4,0},{8,12},{12,8},{1,5},{5,1},{9,13},{13,9},{2,6},{6,2},{1... | collective-permute-start | bytes 1179656 | tf_op jit(solution)/shard_map/ppermute | solution.py:314
  29.9 9.2 %collective-permute-start.3 = (bf16[8,4,48,128]{3,2,1,0:T(8,128)(2,1)S(1)}, bf16[8,4,48,128]{3,2,1,0:T(8,128)(2,1)S(1)}, u32[]{:S(2)}, u32[]{:S(2)}) collective-permute-start(bf16[8,4,48,128]{3,2,1,0:T(8,128)(2,1)S(1)} %get-tuple-element.48), channel_id=1, source_target_pairs={{0,1},{1,0},{2,3},{3,2},{4,5},{5,4},{6,7},{7,6},{8,9},{9,8},{10,11... | collective-permute-start | bytes 1179656 | tf_op jit(solution)/shard_map/ppermute | solution.py:314
  30.0 14.8 %collective-permute-start.4 = (bf16[4,8,48,128]{3,2,1,0:T(8,128)(2,1)S(1)}, bf16[4,8,48,128]{3,2,1,0:T(8,128)(2,1)S(1)}, u32[]{:S(2)}, u32[]{:S(2)}) collective-permute-start(bf16[4,8,48,128]{3,2,1,0:T(8,128)(2,1)S(1)} %get-tuple-element.49), channel_id=1, source_target_pairs={{4,8},{8,4},{5,9},{9,5},{6,10},{10,6},{7,11},{11,7},{20,24},{24,20... | collective-permute-start | bytes 1179656 | tf_op jit(solution)/shard_map/ppermute | solution.py:314
  30.7 15.0 %collective-permute-start.5 = (bf16[4,8,48,128]{3,2,1,0:T(8,128)(2,1)S(1)}, bf16[4,8,48,128]{3,2,1,0:T(8,128)(2,1)S(1)}, u32[]{:S(2)}, u32[]{:S(2)}) collective-permute-start(bf16[4,8,48,128]{3,2,1,0:T(8,128)(2,1)S(1)} %get-tuple-element.50), channel_id=1, source_target_pairs={{0,4},{4,0},{8,12},{12,8},{1,5},{5,1},{9,13},{13,9},{2,6},{6,2},{1... | collective-permute-start | bytes 1179656 | tf_op jit(solution)/shard_map/ppermute | solution.py:314
  38.4 9.2 %collective-permute-start.17 = (bf16[8,4,48,128]{3,2,1,0:T(8,128)(2,1)S(1)}, bf16[8,4,48,128]{3,2,1,0:T(8,128)(2,1)S(1)}, u32[]{:S(2)}, u32[]{:S(2)}) collective-permute-start(bf16[8,4,48,128]{3,2,1,0:T(8,128)(2,1)S(1)} %get-tuple-element.64), channel_id=1, source_target_pairs={{0,1},{1,0},{2,3},{3,2},{4,5},{5,4},{6,7},{7,6},{8,9},{9,8},{10,11... | collective-permute-start | bytes 1179656 | tf_op jit(solution)/shard_map/ppermute | solution.py:314
  38.5 14.8 %collective-permute-start.18 = (bf16[4,8,48,128]{3,2,1,0:T(8,128)(2,1)S(1)}, bf16[4,8,48,128]{3,2,1,0:T(8,128)(2,1)S(1)}, u32[]{:S(2)}, u32[]{:S(2)}) collective-permute-start(bf16[4,8,48,128]{3,2,1,0:T(8,128)(2,1)S(1)} %get-tuple-element.65), channel_id=1, source_target_pairs={{4,8},{8,4},{5,9},{9,5},{6,10},{10,6},{7,11},{11,7},{20,24},{24,20... | collective-permute-start | bytes 1179656 | tf_op jit(solution)/shard_map/ppermute | solution.py:314
  39.2 15.0 %collective-permute-start.19 = (bf16[4,8,48,128]{3,2,1,0:T(8,128)(2,1)S(1)}, bf16[4,8,48,128]{3,2,1,0:T(8,128)(2,1)S(1)}, u32[]{:S(2)}, u32[]{:S(2)}) collective-permute-start(bf16[4,8,48,128]{3,2,1,0:T(8,128)(2,1)S(1)} %get-tuple-element.66), channel_id=1, source_target_pairs={{0,4},{4,0},{8,12},{12,8},{1,5},{5,1},{9,13},{13,9},{2,6},{6,2},{1... | collective-permute-start | bytes 1179656 | tf_op jit(solution)/shard_map/ppermute | solution.py:314
  46.8 9.8 %collective-permute-start.6 = (bf16[8,4,48,128]{3,2,1,0:T(8,128)(2,1)S(1)}, bf16[8,4,48,128]{3,2,1,0:T(8,128)(2,1)S(1)}, u32[]{:S(2)}, u32[]{:S(2)}) collective-permute-start(bf16[8,4,48,128]{3,2,1,0:T(8,128)(2,1)S(1)} %get-tuple-element.52), channel_id=1, source_target_pairs={{0,1},{1,0},{2,3},{3,2},{4,5},{5,4},{6,7},{7,6},{8,9},{9,8},{10,11... | collective-permute-start | bytes 1179656 | tf_op jit(solution)/shard_map/ppermute | solution.py:314
  46.9 12.0 %collective-permute-start.7 = (bf16[4,8,48,128]{3,2,1,0:T(8,128)(2,1)S(1)}, bf16[4,8,48,128]{3,2,1,0:T(8,128)(2,1)S(1)}, u32[]{:S(2)}, u32[]{:S(2)}) collective-permute-start(bf16[4,8,48,128]{3,2,1,0:T(8,128)(2,1)S(1)} %get-tuple-element.53), channel_id=1, source_target_pairs={{4,8},{8,4},{5,9},{9,5},{6,10},{10,6},{7,11},{11,7},{20,24},{24,20... | collective-permute-start | bytes 1179656 | tf_op jit(solution)/shard_map/ppermute | solution.py:314
  47.6 14.6 %collective-permute-start.8 = (bf16[4,8,48,128]{3,2,1,0:T(8,128)(2,1)S(1)}, bf16[4,8,48,128]{3,2,1,0:T(8,128)(2,1)S(1)}, u32[]{:S(2)}, u32[]{:S(2)}) collective-permute-start(bf16[4,8,48,128]{3,2,1,0:T(8,128)(2,1)S(1)} %get-tuple-element.54), channel_id=1, source_target_pairs={{0,4},{4,0},{8,12},{12,8},{1,5},{5,1},{9,13},{13,9},{2,6},{6,2},{1... | collective-permute-start | bytes 1179656 | tf_op jit(solution)/shard_map/ppermute | solution.py:314
  55.1 24.6 %collective-permute-start.20 = (bf16[4,8,48,128]{3,2,1,0:T(8,128)(2,1)S(1)}, bf16[4,8,48,128]{3,2,1,0:T(8,128)(2,1)S(1)}, u32[]{:S(2)}, u32[]{:S(2)}) collective-permute-start(bf16[4,8,48,128]{3,2,1,0:T(8,128)(2,1)S(1)} %get-tuple-element.68.refs_4_), channel_id=1, source_target_pairs={{0,2},{2,0},{1,3},{3,1},{4,6},{6,4},{5,7},{7,5},{8,10},{10,8},{9,1... | collective-permute-start | bytes 1179656 | tf_op jit(solution)/shard_map/ppermute | solution.py:314
  64.5 15.1 %collective-permute-start.10 = (bf16[2,8,48,128]{3,2,1,0:T(8,128)(2,1)S(1)}, bf16[2,8,48,128]{3,2,1,0:T(8,128)(2,1)S(1)}, u32[]{:S(2)}, u32[]{:S(2)}) collective-permute-start(bf16[2,8,48,128]{3,2,1,0:T(8,128)(2,1)S(1)} %shard_map.58.refs_2_), channel_id=1, source_target_pairs={{0,2},{2,0},{1,3},{3,1},{4,6},{6,4},{5,7},{7,5},{8,10},{10,8},{9,1... | collective-permute-start | bytes 589832 | tf_op jit(solution)/shard_map/ppermute | solution.py:314
  66.1 13.6 %collective-permute-start.9 = (bf16[2,8,48,128]{3,2,1,0:T(8,128)(2,1)S(1)}, bf16[2,8,48,128]{3,2,1,0:T(8,128)(2,1)S(1)}, u32[]{:S(2)}, u32[]{:S(2)}) collective-permute-start(bf16[2,8,48,128]{3,2,1,0:T(8,128)(2,1)S(1)} %shard_map.57.refs_1_), channel_id=1, source_target_pairs={{0,2},{2,0},{1,3},{3,1},{4,6},{6,4},{5,7},{7,5},{8,10},{10,8},{9,1... | collective-permute-start | bytes 589832 | tf_op jit(solution)/shard_map/ppermute | solution.py:314
  66.6 7.2 %collective-permute-start.22 = (bf16[128,128]{1,0:T(8,128)(2,1)S(1)}, bf16[128,128]{1,0:T(8,128)(2,1)S(1)}, u32[]{:S(2)}, u32[]{:S(2)}) collective-permute-start(bf16[128,128]{1,0:T(8,128)(2,1)S(1)} %get-tuple-element.71), channel_id=1, source_target_pairs={{8,0},{12,4},{2,10},{6,14},{9,1},{13,5},{3,11},{7,15},{24,16},{28,... | collective-permute-start | bytes 98312 | tf_op jit(solution)/shard_map/ppermute | solution.py:595
  67.9 9.2 %collective-permute-start.23 = (bf16[128,128]{1,0:T(8,128)(2,1)S(1)}, bf16[128,128]{1,0:T(8,128)(2,1)S(1)}, u32[]{:S(2)}, u32[]{:S(2)}) collective-permute-start(bf16[128,128]{1,0:T(8,128)(2,1)S(1)} %get-tuple-element.72), channel_id=1, source_target_pairs={{12,0},{8,4},{6,10},{2,14},{13,1},{9,5},{7,11},{3,15},{28,16},{24,... | collective-permute-start | bytes 98312 | tf_op jit(solution)/shard_map/ppermute | solution.py:595
  82.2 6.5 %collective-permute-start.27 = (bf16[144,128]{1,0:T(8,128)(2,1)S(1)}, bf16[144,128]{1,0:T(8,128)(2,1)S(1)}, u32[]{:S(2)}, u32[]{:S(2)}) collective-permute-start(bf16[144,128]{1,0:T(8,128)(2,1)S(1)} %get-tuple-element.79), channel_id=1, source_target_pairs={{0,12},{4,8},{8,4},{12,0},{1,13},{5,9},{9,5},{13,1},{2,14},{6,10},... | collective-permute-start | bytes 110600 | tf_op jit(solution)/shard_map/ppermute | solution.py:602
  (12 other events, 63.8 us)

commit v21 on v19

--- a/solution.py
+++ b/solution.py
@@ -421,34 +421,61 @@
     )(keep, got)
 
 
-def cross_body(sizes, *refs):
-    groups, (_, keep_ref, send_ref, panel) = regroup(sizes, refs)
+def pair_blocks(got_refs, panel, chip):
+    got = [ref[...].reshape(-1, LANES) for ref in got_refs]
+    both = product(got[0] if len(got) == 1 else jnp.concatenate(got, axis=0), panel[...])
+    blocks = [both[:, n * LANES : (n + 1) * LANES] for n in range(2)]
+    return [jnp.where(chip == 0, block.T, block) for block in blocks]
+
+
+def first_cross_body(sizes, *refs):
+    (got, *kept), (panel, out_ref) = regroup(sizes, refs)
     chip = lax.axis_index("probe")
-    core = lax.axis_index("sub")
-    for n in range(2):
-        mine = pl.multiple_of((chip * 2 + n) * LANES, LANES)
-        other = pl.multiple_of(((1 - chip) * 2 + n) * LANES, LANES)
-        lay(panel, pl.ds(mine, LANES), groups[2 * n])
-        lay(panel, pl.ds(other, LANES), groups[2 * n + 1])
-    whole = product(panel[:, : 2 * LANES], panel[:, 2 * LANES :])
+    for n, group in enumerate(kept):
+        lay(panel, slice(n * LANES, (n + 1) * LANES), group)
+    one, two = pair_blocks(got, panel, chip)
+    out_ref[:LANES] = one
+    out_ref[LANES:] = two
+
+
+def first_cross(got, kept):
+    groups = [got] + kept
+    cells = sum(math.prod(field.shape[:3]) for field in got)
+    return call(
+        functools.partial(first_cross_body, [len(group) for group in groups]),
+        in_specs=whole_vmem(len(flat(groups))),
+        out_specs=whole_vmem(2),
+        out_shape=[
+            jax.ShapeDtypeStruct((cells, 2 * LANES), BF16),
+            jax.ShapeDtypeStruct((2 * LANES, LANES), F32),
+        ],
+    )(*flat(groups))
+
+
+def cross_body(count, *refs):
+    got, (panel, first_ref, _, keep_ref, send_ref) = refs[:count], refs[count:]
+    chip = lax.axis_index("probe")
+    core = lax.axis_index("sub")
+    zero, one = pair_blocks(got, panel, chip)
+    mixed = first_ref[:LANES]
+    corner = first_ref[LANES:]
+    upper = jnp.where(chip == 0, mixed, one)
+    lower = jnp.where(chip == 0, one, mixed)
     for ref, which in ((keep_ref, core), (send_ref, 1 - core)):
         here = which == 0
-        ref[:LANES] = jnp.where(here, block_of(whole, 0, 0), block_of(whole, 0, 1))
-        ref[LANES : 2 * LANES] = jnp.where(here, block_of(whole, 1, 0), block_of(whole, 1, 1))
-        mixed = jnp.where(here, block_of(whole, 0, 1), block_of(whole, 1, 0))
-        ref[2 * LANES :] = mixed
-
-
-def cross_gram(groups, after):
-    cells = sum(math.prod(field.shape[:3]) for field in groups[0])
+        ref[:LANES] = jnp.where(here, zero, upper)
+        ref[LANES : 2 * LANES] = jnp.where(here, lower, corner)
+        ref[2 * LANES :] = jnp.where(here, upper, lower)
+
+
+def cross_gram(got, panel, first, after):
     three = jax.ShapeDtypeStruct((3 * LANES, LANES), F32)
     return call(
-        functools.partial(cross_body, [len(group) for group in groups]),
-        in_specs=whole_vmem(len(flat(groups))) + [pl.BlockSpec(memory_space=pl.ANY)],
+        functools.partial(cross_body, len(got)),
+        in_specs=whole_vmem(len(got) + 2) + [pl.BlockSpec(memory_space=pl.ANY)],
         out_specs=whole_vmem(2),
         out_shape=[three, three],
-        scratch_shapes=[pltpu.VMEM((cells, 4 * LANES), BF16)],
-    )(*flat(groups), after)
+    )(*got, panel, first, after)
 
 
 def rounded(ref, block, tail):
@@ -579,7 +606,8 @@
     keep, send = inner_gram([kept + sent for kept, sent, _ in finals])
     tail, inner, sent = inner_sum(keep, core_swap(send))
     inner_got = lax.ppermute(sent, "slab", [(i, i ^ 1) for i in range(slabs)])
-    keep, send = cross_gram([g for kept, _, got in finals for g in (kept, got)], inner_got)
+    panel, first = first_cross(finals[1][2], [kept for kept, _, _ in finals])
+    keep, send = cross_gram(finals[0][2], panel, first, inner_got)
     mine, *blocks = cross_rows(keep, core_swap(send), tail, inner, inner_got, slabs)
     arrived = [
         lax.ppermute(blocks[d - 1], "slab", [(i, i ^ d) for i in range(slabs)])

time: 91.9 us -> 91.4 us (level)
  transfers between devices with their start and end apart: 29 -> 29, of which waited for: 14 -> 14; matrix products, arithmetic and copies ran while one was open for 0% -> 0% of each run, Pallas kernels for 24% -> 25%
where the time goes in v21:
time: 91.4 us; the launch traced here: 91.1 us
  starting transfers between devices  37.3 us (41%)
  waiting for transfers between devices  25.4 us (28%)
  Pallas kernels  25.2 us (28%)
  local copies, waits for them, and re-layouts  2.18 us (2%)
  between operations  1.01 us (1%)
    ppermute x25, starting transfers between devices, swap(): lax.ppermute(x, axis, [p for a, b in pairs for p in ((a, b), (b, a))])  31.7 us
    ppermute x25, waiting for transfers between devices, swap(): lax.ppermute(x, axis, [p for a, b in pairs for p in ((a, b), (b, a))])  19.3 us
    pallas_call x6, Pallas kernels, local_step(): call(functools.partial(local_body, chunk, moment, previous is not None),...  13.3 us
    pallas_call x5, Pallas kernels, rim_step(): call(functools.partial(rim_body, kind), in_specs=whole_vmem(4), out_specs...  5.35 us
    ppermute x3, waiting for transfers between devices, coupled(): lax.ppermute(blocks[d - 1], 'slab', [(i, i ^ d) for i in range(slabs)])  4.39 us
    ppermute x3, starting transfers between devices, coupled(): lax.ppermute(blocks[d - 1], 'slab', [(i, i ^ d) for i in range(slabs)])  3.82 us
    pallas_call x2, Pallas kernels, first_field(): call(functools.partial(first_body, chunk), in_specs=whole_vmem(2), out_sp...  2.1 us
  transfers between devices with their start and end apart: 29, of which 14 were waited for; matrix products, arithmetic and copies ran while one was open for 0% of the time, Pallas kernels for 25%

profile of v21, /device:TPU:0, one launch (start us, length us, event | category | flops | bytes accessed | tf_op | source)
XLA Modules:
  0.0 91.1 jit_solution(18057290799922092196)
XLA Ops:
  5.1 5.5 %collective-permute-start.13 = (bf16[4,8,48,128]{3,2,1,0:T(8,128)(2,1)S(1)}, bf16[4,8,48,128]{3,2,1,0:T(8,128)(2,1)S(1)}, u32[]{:S(2)}, u32[]{:S(2)}) collective-permute-start(bf16[4,8,48,128]{3,2,1,0:T(8,128)(2,1)S(1)} %get-tuple-element.58), channel_id=1, source_target_pairs={{0,4},{4,0},{8,12},{12,8},{1,5},{5,1},{9,13},{13,9},{2,6},{6,2},{1... | collective-permute-start | bytes 1179656 | tf_op jit(solution)/shard_map/ppermute | solution.py:314
  12.4 1.9 %collective-permute-start.2 = (bf16[4,8,48,128]{3,2,1,0:T(8,128)(2,1)S(1)}, bf16[4,8,48,128]{3,2,1,0:T(8,128)(2,1)S(1)}, u32[]{:S(2)}, u32[]{:S(2)}) collective-permute-start(bf16[4,8,48,128]{3,2,1,0:T(8,128)(2,1)S(1)} %get-tuple-element.46), channel_id=1, source_target_pairs={{0,4},{4,0},{8,12},{12,8},{1,5},{5,1},{9,13},{13,9},{2,6},{6,2},{1... | collective-permute-start | bytes 1179656 | tf_op jit(solution)/shard_map/ppermute | solution.py:314
  14.3 2.1 %shard_map.59.refs_0_ = f32[8,8,48,128]{3,2,1,0:T(8,128)S(1)} custom-call(f32[8,8,64,128]{3,2,1,0:T(8,128)S(1)} %get-tuple-element.55.refs_0_.refs_5_, bf16[8,4,48,128]{3,2,1,0:T(8,128)(2,1)S(1)} %collective-permute-done.11.refs_1_, bf16[8,8,48,256]{3,2,1,0:T(8,128)(2,1)S(1)} %copy-done, f32[64,48]{1,0:T(8,128)S(1)} %bitcast.5, f32[4,64,48]{2,1,0:T(8,128)S(1)} %bitcast.19), custom_call_target="tpu_custom_call" | custom-call | flops 1 | bytes 1 | tf_op jit(solution)/shard_map/pallas_call | solution.py:185
  16.5 3.9 %collective-permute-done.13.refs_2_ = bf16[4,8,48,128]{3,2,1,0:T(8,128)(2,1)S(1)} collective-permute-done((bf16[4,8,48,128]{3,2,1,0:T(8,128)(2,1)S(1)}, bf16[4,8,48,128]{3,2,1,0:T(8,128)(2,1)S(1)}, u32[]{:S(2)}, u32[]{:S(2)}) %collective-permute-start.13) | collective-permute-done | bytes 393248 | tf_op jit(solution)/shard_map/ppermute | solution.py:314
  22.3 3.8 %collective-permute-start.16 = (bf16[4,8,48,128]{3,2,1,0:T(8,128)(2,1)S(1)}, bf16[4,8,48,128]{3,2,1,0:T(8,128)(2,1)S(1)}, u32[]{:S(2)}, u32[]{:S(2)}) collective-permute-start(bf16[4,8,48,128]{3,2,1,0:T(8,128)(2,1)S(1)} %get-tuple-element.62), channel_id=1, source_target_pairs={{0,4},{4,0},{8,12},{12,8},{1,5},{5,1},{9,13},{13,9},{2,6},{6,2},{1... | collective-permute-start | bytes 1179656 | tf_op jit(solution)/shard_map/ppermute | solution.py:314
  26.1 2.1 %shard_map.51.refs_0_ = f32[8,8,48,128]{3,2,1,0:T(8,128)S(1)} custom-call(f32[8,8,64,128]{3,2,1,0:T(8,128)S(1)} %get-tuple-element.43.refs_0_.refs_5_, bf16[8,4,48,128]{3,2,1,0:T(8,128)(2,1)S(1)} %collective-permute-done.refs_1_, bf16[8,8,48,256]{3,2,1,0:T(8,128)(2,1)S(1)} %copy-done.1, f32[64,48]{1,0:T(8,128)S(1)} %bitcast.7, f32[4,64,48]{2,1,0:T(8,128)S(1)} %bitcast.20), custom_call_target="tpu_custom_call" | custom-call | flops 1 | bytes 1 | tf_op jit(solution)/shard_map/pallas_call | solution.py:185
  30.7 3.4 %collective-permute-start.5 = (bf16[4,8,48,128]{3,2,1,0:T(8,128)(2,1)S(1)}, bf16[4,8,48,128]{3,2,1,0:T(8,128)(2,1)S(1)}, u32[]{:S(2)}, u32[]{:S(2)}) collective-permute-start(bf16[4,8,48,128]{3,2,1,0:T(8,128)(2,1)S(1)} %get-tuple-element.50), channel_id=1, source_target_pairs={{0,4},{4,0},{8,12},{12,8},{1,5},{5,1},{9,13},{13,9},{2,6},{6,2},{1... | collective-permute-start | bytes 1179656 | tf_op jit(solution)/shard_map/ppermute | solution.py:314
  34.1 2.3 %shard_map.61.refs_0_ = f32[8,8,48,128]{3,2,1,0:T(8,128)S(1)} custom-call(f32[8,8,64,128]{3,2,1,0:T(8,128)S(1)} %get-tuple-element.59.refs_0_.refs_5_, bf16[8,4,48,128]{3,2,1,0:T(8,128)(2,1)S(1)} %collective-permute-done.14.refs_1_, bf16[8,8,48,256]{3,2,1,0:T(8,128)(2,1)S(1)} %copy-done.1, f32[64,48]{1,0:T(8,128)S(1)} %bitcast.9, f32[4,64,48]{2,1,0:T(8,128)S(1)} %bitcast.21, ...), custom_call_target="tpu_custom_call" | custom-call | flops 1 | bytes 1 | tf_op jit(solution)/shard_map/pallas_call | solution.py:185
  39.2 3.4 %collective-permute-start.19 = (bf16[4,8,48,128]{3,2,1,0:T(8,128)(2,1)S(1)}, bf16[4,8,48,128]{3,2,1,0:T(8,128)(2,1)S(1)}, u32[]{:S(2)}, u32[]{:S(2)}) collective-permute-start(bf16[4,8,48,128]{3,2,1,0:T(8,128)(2,1)S(1)} %get-tuple-element.66), channel_id=1, source_target_pairs={{0,4},{4,0},{8,12},{12,8},{1,5},{5,1},{9,13},{13,9},{2,6},{6,2},{1... | collective-permute-start | bytes 1179656 | tf_op jit(solution)/shard_map/ppermute | solution.py:314
  42.5 2.2 %shard_map.53.refs_0_ = f32[8,8,48,128]{3,2,1,0:T(8,128)S(1)} custom-call(f32[8,8,64,128]{3,2,1,0:T(8,128)S(1)} %get-tuple-element.47.refs_0_.refs_5_, bf16[8,4,48,128]{3,2,1,0:T(8,128)(2,1)S(1)} %collective-permute-done.3.refs_1_, bf16[8,8,48,256]{3,2,1,0:T(8,128)(2,1)S(1)} %copy-done.1, f32[64,48]{1,0:T(8,128)S(1)} %bitcast.11, f32[4,64,48]{2,1,0:T(8,128)S(1)} %bitcast.22, ...), custom_call_target="tpu_custom_call" | custom-call | flops 1 | bytes 1 | tf_op jit(solution)/shard_map/pallas_call | solution.py:185
  47.6 3.4 %collective-permute-start.8 = (bf16[4,8,48,128]{3,2,1,0:T(8,128)(2,1)S(1)}, bf16[4,8,48,128]{3,2,1,0:T(8,128)(2,1)S(1)}, u32[]{:S(2)}, u32[]{:S(2)}) collective-permute-start(bf16[4,8,48,128]{3,2,1,0:T(8,128)(2,1)S(1)} %get-tuple-element.54), channel_id=1, source_target_pairs={{0,4},{4,0},{8,12},{12,8},{1,5},{5,1},{9,13},{13,9},{2,6},{6,2},{1... | collective-permute-start | bytes 1179656 | tf_op jit(solution)/shard_map/ppermute | solution.py:314
  50.9 2.3 %shard_map.63.refs_0_ = f32[8,8,48,128]{3,2,1,0:T(8,128)S(1)} custom-call(f32[8,8,64,128]{3,2,1,0:T(8,128)S(1)} %get-tuple-element.63.refs_0_, bf16[8,4,48,128]{3,2,1,0:T(8,128)(2,1)S(1)} %collective-permute-done.17.refs_1_, bf16[8,8,48,256]{3,2,1,0:T(8,128)(2,1)S(1)} %copy-done.1, f32[64,48]{1,0:T(8,128)S(1)} %bitcast.13, f32[4,64,48]{2,1,0:T(8,128)S(1)} %bitcast.23, ...), custom_call_target="tpu_custom_call" | custom-call | flops 1 | bytes 1 | tf_op jit(solution)/shard_map/pallas_call | solution.py:185
  55.1 1.6 %collective-permute-start.20 = (bf16[4,8,48,128]{3,2,1,0:T(8,128)(2,1)S(1)}, bf16[4,8,48,128]{3,2,1,0:T(8,128)(2,1)S(1)}, u32[]{:S(2)}, u32[]{:S(2)}) collective-permute-start(bf16[4,8,48,128]{3,2,1,0:T(8,128)(2,1)S(1)} %get-tuple-element.67.refs_4_), channel_id=1, source_target_pairs={{0,2},{2,0},{1,3},{3,1},{4,6},{6,4},{5,7},{7,5},{8,10},{10,8},{9,1... | collective-permute-start | bytes 1179656 | tf_op jit(solution)/shard_map/ppermute | solution.py:314
  56.6 2.2 %shard_map.55.base_ref = f32[8,8,48,128]{3,2,1,0:T(8,128)S(1)} custom-call(f32[8,8,64,128]{3,2,1,0:T(8,128)S(1)} %get-tuple-element.51.refs_0_, bf16[8,4,48,128]{3,2,1,0:T(8,128)(2,1)S(1)} %collective-permute-done.6.refs_1_, bf16[8,8,48,256]{3,2,1,0:T(8,128)(2,1)S(1)} %copy-done.1, f32[64,48]{1,0:T(8,128)S(1)} %bitcast.15, f32[4,64,48]{2,1,0:T(8,128)S(1)} %bitcast.24, ...), custom_call_target="tpu_custom_call" | custom-call | flops 1 | bytes 1 | tf_op jit(solution)/shard_map/pallas_call | solution.py:185
  58.9 3.2 %collective-permute-done.8.even_ref = bf16[4,8,48,128]{3,2,1,0:T(8,128)(2,1)S(1)} collective-permute-done((bf16[4,8,48,128]{3,2,1,0:T(8,128)(2,1)S(1)}, bf16[4,8,48,128]{3,2,1,0:T(8,128)(2,1)S(1)}, u32[]{:S(2)}, u32[]{:S(2)}) %collective-permute-start.8) | collective-permute-done | bytes 393248 | tf_op jit(solution)/shard_map/ppermute | solution.py:314
  62.6 1.6 %collective-permute-start.9 = (bf16[2,8,48,128]{3,2,1,0:T(8,128)(2,1)S(1)}, bf16[2,8,48,128]{3,2,1,0:T(8,128)(2,1)S(1)}, u32[]{:S(2)}, u32[]{:S(2)}) collective-permute-start(bf16[2,8,48,128]{3,2,1,0:T(8,128)(2,1)S(1)} %shard_map.56.refs_1_), channel_id=1, source_target_pairs={{0,2},{2,0},{1,3},{3,1},{4,6},{6,4},{5,7},{7,5},{8,10},{10,8},{9,1... | collective-permute-start | bytes 589832 | tf_op jit(solution)/shard_map/ppermute | solution.py:314
  68.0 1.8 %collective-permute-start.22 = (bf16[128,128]{1,0:T(8,128)(2,1)S(1)}, bf16[128,128]{1,0:T(8,128)(2,1)S(1)}, u32[]{:S(2)}, u32[]{:S(2)}) collective-permute-start(bf16[128,128]{1,0:T(8,128)(2,1)S(1)} %get-tuple-element.73), channel_id=1, source_target_pairs={{0,4},{4,0},{8,12},{12,8},{1,5},{5,1},{9,13},{13,9},{2,6},{6,2},{1... | collective-permute-start | bytes 98312 | tf_op jit(solution)/shard_map/ppermute | solution.py:608
  70.3 1.7 %collective-permute-done.22.refs_4_.inner_got_ref = bf16[128,128]{1,0:T(8,128)(2,1)S(1)} collective-permute-done((bf16[128,128]{1,0:T(8,128)(2,1)S(1)}, bf16[128,128]{1,0:T(8,128)(2,1)S(1)}, u32[]{:S(2)}, u32[]{:S(2)}) %collective-permute-start.22) | collective-permute-done | bytes 32800 | tf_op jit(solution)/shard_map/ppermute | solution.py:608
  72.0 1.9 %collective-permute-done.10.refs_1_ = bf16[2,8,48,128]{3,2,1,0:T(8,128)(2,1)S(1)} collective-permute-done((bf16[2,8,48,128]{3,2,1,0:T(8,128)(2,1)S(1)}, bf16[2,8,48,128]{3,2,1,0:T(8,128)(2,1)S(1)}, u32[]{:S(2)}, u32[]{:S(2)}) %collective-permute-start.10) | collective-permute-done | bytes 196640 | tf_op jit(solution)/shard_map/ppermute | solution.py:314
  75.9 1.5 %collective-permute-start.24 = (bf16[272,128]{1,0:T(8,128)(2,1)S(1)}, bf16[272,128]{1,0:T(8,128)(2,1)S(1)}, u32[]{:S(2)}, u32[]{:S(2)}) collective-permute-start(bf16[272,128]{1,0:T(8,128)(2,1)S(1)} %get-tuple-element.79), channel_id=1, source_target_pairs={{0,8},{4,12},{8,0},{12,4},{1,9},{5,13},{9,1},{13,5},{2,10},{6,14},... | collective-permute-start | bytes 208904 | tf_op jit(solution)/shard_map/ppermute | solution.py:613
  77.4 2.3 %collective-permute-start.25 = (bf16[144,128]{1,0:T(8,128)(2,1)S(1)}, bf16[144,128]{1,0:T(8,128)(2,1)S(1)}, u32[]{:S(2)}, u32[]{:S(2)}) collective-permute-start(bf16[144,128]{1,0:T(8,128)(2,1)S(1)} %get-tuple-element.80), channel_id=1, source_target_pairs={{0,12},{4,8},{8,4},{12,0},{1,13},{5,9},{9,5},{13,1},{2,14},{6,10},... | collective-permute-start | bytes 110600 | tf_op jit(solution)/shard_map/ppermute | solution.py:613
  79.7 3.5 %collective-permute-done.25.refs_1_ = bf16[144,128]{1,0:T(8,128)(2,1)S(1)} collective-permute-done((bf16[144,128]{1,0:T(8,128)(2,1)S(1)}, bf16[144,128]{1,0:T(8,128)(2,1)S(1)}, u32[]{:S(2)}, u32[]{:S(2)}) %collective-permute-start.25) | collective-permute-done | bytes 36896 | tf_op jit(solution)/shard_map/ppermute | solution.py:613
  84.1 1.5 %collective-permute-start.27 = (bf16[272,128]{1,0:T(8,128)(2,1)S(1)}, bf16[272,128]{1,0:T(8,128)(2,1)S(1)}, u32[]{:S(2)}, u32[]{:S(2)}) collective-permute-start(bf16[272,128]{1,0:T(8,128)(2,1)S(1)} %shard_map.71.mine_ref), channel_id=1, source_target_pairs={{0,2},{2,0},{1,3},{3,1},{4,6},{6,4},{5,7},{7,5},{8,10},{10,8},{9,1... | collective-permute-start | bytes 208904 | tf_op jit(solution)/shard_map/ppermute | solution.py:314
  85.6 2.8 %collective-permute-done.27.other_ref = bf16[272,128]{1,0:T(8,128)(2,1)S(1)} collective-permute-done((bf16[272,128]{1,0:T(8,128)(2,1)S(1)}, bf16[272,128]{1,0:T(8,128)(2,1)S(1)}, u32[]{:S(2)}, u32[]{:S(2)}) %collective-permute-start.27) | collective-permute-done | bytes 69664 | tf_op jit(solution)/shard_map/ppermute | solution.py:314
  (67 shorter events, 28.2 us)
Async XLA Ops:
  3.9 8.5 %collective-permute-start.11 = (bf16[8,4,48,128]{3,2,1,0:T(8,128)(2,1)S(1)}, bf16[8,4,48,128]{3,2,1,0:T(8,128)(2,1)S(1)}, u32[]{:S(2)}, u32[]{:S(2)}) collective-permute-start(bf16[8,4,48,128]{3,2,1,0:T(8,128)(2,1)S(1)} %get-tuple-element.56), channel_id=1, source_target_pairs={{0,1},{1,0},{2,3},{3,2},{4,5},{5,4},{6,7},{7,6},{8,9},{9,8},{10,11... | collective-permute-start | bytes 1179656 | tf_op jit(solution)/shard_map/ppermute | solution.py:314
  4.4 12.1 %collective-permute-start.12 = (bf16[4,8,48,128]{3,2,1,0:T(8,128)(2,1)S(1)}, bf16[4,8,48,128]{3,2,1,0:T(8,128)(2,1)S(1)}, u32[]{:S(2)}, u32[]{:S(2)}) collective-permute-start(bf16[4,8,48,128]{3,2,1,0:T(8,128)(2,1)S(1)} %get-tuple-element.57), channel_id=1, source_target_pairs={{4,8},{8,4},{5,9},{9,5},{6,10},{10,6},{7,11},{11,7},{20,24},{24,20... | collective-permute-start | bytes 1179656 | tf_op jit(solution)/shard_map/ppermute | solution.py:314
  5.1 15.4 %collective-permute-start.13 = (bf16[4,8,48,128]{3,2,1,0:T(8,128)(2,1)S(1)}, bf16[4,8,48,128]{3,2,1,0:T(8,128)(2,1)S(1)}, u32[]{:S(2)}, u32[]{:S(2)}) collective-permute-start(bf16[4,8,48,128]{3,2,1,0:T(8,128)(2,1)S(1)} %get-tuple-element.58), channel_id=1, source_target_pairs={{0,4},{4,0},{8,12},{12,8},{1,5},{5,1},{9,13},{13,9},{2,6},{6,2},{1... | collective-permute-start | bytes 1179656 | tf_op jit(solution)/shard_map/ppermute | solution.py:314
  11.6 10.7 %collective-permute-start = (bf16[8,4,48,128]{3,2,1,0:T(8,128)(2,1)S(1)}, bf16[8,4,48,128]{3,2,1,0:T(8,128)(2,1)S(1)}, u32[]{:S(2)}, u32[]{:S(2)}) collective-permute-start(bf16[8,4,48,128]{3,2,1,0:T(8,128)(2,1)S(1)} %get-tuple-element.44), channel_id=1, source_target_pairs={{0,1},{1,0},{2,3},{3,2},{4,5},{5,4},{6,7},{7,6},{8,9},{9,8},{10,11... | collective-permute-start | bytes 1179656 | tf_op jit(solution)/shard_map/ppermute | solution.py:314
  11.7 16.6 %collective-permute-start.1 = (bf16[4,8,48,128]{3,2,1,0:T(8,128)(2,1)S(1)}, bf16[4,8,48,128]{3,2,1,0:T(8,128)(2,1)S(1)}, u32[]{:S(2)}, u32[]{:S(2)}) collective-permute-start(bf16[4,8,48,128]{3,2,1,0:T(8,128)(2,1)S(1)} %get-tuple-element.45), channel_id=1, source_target_pairs={{4,8},{8,4},{5,9},{9,5},{6,10},{10,6},{7,11},{11,7},{20,24},{24,20... | collective-permute-start | bytes 1179656 | tf_op jit(solution)/shard_map/ppermute | solution.py:314
  12.4 16.5 %collective-permute-start.2 = (bf16[4,8,48,128]{3,2,1,0:T(8,128)(2,1)S(1)}, bf16[4,8,48,128]{3,2,1,0:T(8,128)(2,1)S(1)}, u32[]{:S(2)}, u32[]{:S(2)}) collective-permute-start(bf16[4,8,48,128]{3,2,1,0:T(8,128)(2,1)S(1)} %get-tuple-element.46), channel_id=1, source_target_pairs={{0,4},{4,0},{8,12},{12,8},{1,5},{5,1},{9,13},{13,9},{2,6},{6,2},{1... | collective-permute-start | bytes 1179656 | tf_op jit(solution)/shard_map/ppermute | solution.py:314
  21.5 9.2 %collective-permute-start.14 = (bf16[8,4,48,128]{3,2,1,0:T(8,128)(2,1)S(1)}, bf16[8,4,48,128]{3,2,1,0:T(8,128)(2,1)S(1)}, u32[]{:S(2)}, u32[]{:S(2)}) collective-permute-start(bf16[8,4,48,128]{3,2,1,0:T(8,128)(2,1)S(1)} %get-tuple-element.60), channel_id=1, source_target_pairs={{0,1},{1,0},{2,3},{3,2},{4,5},{5,4},{6,7},{7,6},{8,9},{9,8},{10,11... | collective-permute-start | bytes 1179656 | tf_op jit(solution)/shard_map/ppermute | solution.py:314
  21.6 14.8 %collective-permute-start.15 = (bf16[4,8,48,128]{3,2,1,0:T(8,128)(2,1)S(1)}, bf16[4,8,48,128]{3,2,1,0:T(8,128)(2,1)S(1)}, u32[]{:S(2)}, u32[]{:S(2)}) collective-permute-start(bf16[4,8,48,128]{3,2,1,0:T(8,128)(2,1)S(1)} %get-tuple-element.61), channel_id=1, source_target_pairs={{4,8},{8,4},{5,9},{9,5},{6,10},{10,6},{7,11},{11,7},{20,24},{24,20... | collective-permute-start | bytes 1179656 | tf_op jit(solution)/shard_map/ppermute | solution.py:314
  22.3 15.0 %collective-permute-start.16 = (bf16[4,8,48,128]{3,2,1,0:T(8,128)(2,1)S(1)}, bf16[4,8,48,128]{3,2,1,0:T(8,128)(2,1)S(1)}, u32[]{:S(2)}, u32[]{:S(2)}) collective-permute-start(bf16[4,8,48,128]{3,2,1,0:T(8,128)(2,1)S(1)} %get-tuple-element.62), channel_id=1, source_target_pairs={{0,4},{4,0},{8,12},{12,8},{1,5},{5,1},{9,13},{13,9},{2,6},{6,2},{1... | collective-permute-start | bytes 1179656 | tf_op jit(solution)/shard_map/ppermute | solution.py:314
  29.9 9.2 %collective-permute-start.3 = (bf16[8,4,48,128]{3,2,1,0:T(8,128)(2,1)S(1)}, bf16[8,4,48,128]{3,2,1,0:T(8,128)(2,1)S(1)}, u32[]{:S(2)}, u32[]{:S(2)}) collective-permute-start(bf16[8,4,48,128]{3,2,1,0:T(8,128)(2,1)S(1)} %get-tuple-element.48), channel_id=1, source_target_pairs={{0,1},{1,0},{2,3},{3,2},{4,5},{5,4},{6,7},{7,6},{8,9},{9,8},{10,11... | collective-permute-start | bytes 1179656 | tf_op jit(solution)/shard_map/ppermute | solution.py:314
  30.0 14.8 %collective-permute-start.4 = (bf16[4,8,48,128]{3,2,1,0:T(8,128)(2,1)S(1)}, bf16[4,8,48,128]{3,2,1,0:T(8,128)(2,1)S(1)}, u32[]{:S(2)}, u32[]{:S(2)}) collective-permute-start(bf16[4,8,48,128]{3,2,1,0:T(8,128)(2,1)S(1)} %get-tuple-element.49), channel_id=1, source_target_pairs={{4,8},{8,4},{5,9},{9,5},{6,10},{10,6},{7,11},{11,7},{20,24},{24,20... | collective-permute-start | bytes 1179656 | tf_op jit(solution)/shard_map/ppermute | solution.py:314
  30.7 15.0 %collective-permute-start.5 = (bf16[4,8,48,128]{3,2,1,0:T(8,128)(2,1)S(1)}, bf16[4,8,48,128]{3,2,1,0:T(8,128)(2,1)S(1)}, u32[]{:S(2)}, u32[]{:S(2)}) collective-permute-start(bf16[4,8,48,128]{3,2,1,0:T(8,128)(2,1)S(1)} %get-tuple-element.50), channel_id=1, source_target_pairs={{0,4},{4,0},{8,12},{12,8},{1,5},{5,1},{9,13},{13,9},{2,6},{6,2},{1... | collective-permute-start | bytes 1179656 | tf_op jit(solution)/shard_map/ppermute | solution.py:314
  38.4 9.2 %collective-permute-start.17 = (bf16[8,4,48,128]{3,2,1,0:T(8,128)(2,1)S(1)}, bf16[8,4,48,128]{3,2,1,0:T(8,128)(2,1)S(1)}, u32[]{:S(2)}, u32[]{:S(2)}) collective-permute-start(bf16[8,4,48,128]{3,2,1,0:T(8,128)(2,1)S(1)} %get-tuple-element.64), channel_id=1, source_target_pairs={{0,1},{1,0},{2,3},{3,2},{4,5},{5,4},{6,7},{7,6},{8,9},{9,8},{10,11... | collective-permute-start | bytes 1179656 | tf_op jit(solution)/shard_map/ppermute | solution.py:314
  38.5 14.8 %collective-permute-start.18 = (bf16[4,8,48,128]{3,2,1,0:T(8,128)(2,1)S(1)}, bf16[4,8,48,128]{3,2,1,0:T(8,128)(2,1)S(1)}, u32[]{:S(2)}, u32[]{:S(2)}) collective-permute-start(bf16[4,8,48,128]{3,2,1,0:T(8,128)(2,1)S(1)} %get-tuple-element.65), channel_id=1, source_target_pairs={{4,8},{8,4},{5,9},{9,5},{6,10},{10,6},{7,11},{11,7},{20,24},{24,20... | collective-permute-start | bytes 1179656 | tf_op jit(solution)/shard_map/ppermute | solution.py:314
  39.2 15.0 %collective-permute-start.19 = (bf16[4,8,48,128]{3,2,1,0:T(8,128)(2,1)S(1)}, bf16[4,8,48,128]{3,2,1,0:T(8,128)(2,1)S(1)}, u32[]{:S(2)}, u32[]{:S(2)}) collective-permute-start(bf16[4,8,48,128]{3,2,1,0:T(8,128)(2,1)S(1)} %get-tuple-element.66), channel_id=1, source_target_pairs={{0,4},{4,0},{8,12},{12,8},{1,5},{5,1},{9,13},{13,9},{2,6},{6,2},{1... | collective-permute-start | bytes 1179656 | tf_op jit(solution)/shard_map/ppermute | solution.py:314
  46.8 9.8 %collective-permute-start.6 = (bf16[8,4,48,128]{3,2,1,0:T(8,128)(2,1)S(1)}, bf16[8,4,48,128]{3,2,1,0:T(8,128)(2,1)S(1)}, u32[]{:S(2)}, u32[]{:S(2)}) collective-permute-start(bf16[8,4,48,128]{3,2,1,0:T(8,128)(2,1)S(1)} %get-tuple-element.52), channel_id=1, source_target_pairs={{0,1},{1,0},{2,3},{3,2},{4,5},{5,4},{6,7},{7,6},{8,9},{9,8},{10,11... | collective-permute-start | bytes 1179656 | tf_op jit(solution)/shard_map/ppermute | solution.py:314
  46.9 12.0 %collective-permute-start.7 = (bf16[4,8,48,128]{3,2,1,0:T(8,128)(2,1)S(1)}, bf16[4,8,48,128]{3,2,1,0:T(8,128)(2,1)S(1)}, u32[]{:S(2)}, u32[]{:S(2)}) collective-permute-start(bf16[4,8,48,128]{3,2,1,0:T(8,128)(2,1)S(1)} %get-tuple-element.53), channel_id=1, source_target_pairs={{4,8},{8,4},{5,9},{9,5},{6,10},{10,6},{7,11},{11,7},{20,24},{24,20... | collective-permute-start | bytes 1179656 | tf_op jit(solution)/shard_map/ppermute | solution.py:314
  47.6 14.6 %collective-permute-start.8 = (bf16[4,8,48,128]{3,2,1,0:T(8,128)(2,1)S(1)}, bf16[4,8,48,128]{3,2,1,0:T(8,128)(2,1)S(1)}, u32[]{:S(2)}, u32[]{:S(2)}) collective-permute-start(bf16[4,8,48,128]{3,2,1,0:T(8,128)(2,1)S(1)} %get-tuple-element.54), channel_id=1, source_target_pairs={{0,4},{4,0},{8,12},{12,8},{1,5},{5,1},{9,13},{13,9},{2,6},{6,2},{1... | collective-permute-start | bytes 1179656 | tf_op jit(solution)/shard_map/ppermute | solution.py:314
  55.1 14.8 %collective-permute-start.20 = (bf16[4,8,48,128]{3,2,1,0:T(8,128)(2,1)S(1)}, bf16[4,8,48,128]{3,2,1,0:T(8,128)(2,1)S(1)}, u32[]{:S(2)}, u32[]{:S(2)}) collective-permute-start(bf16[4,8,48,128]{3,2,1,0:T(8,128)(2,1)S(1)} %get-tuple-element.67.refs_4_), channel_id=1, source_target_pairs={{0,2},{2,0},{1,3},{3,1},{4,6},{6,4},{5,7},{7,5},{8,10},{10,8},{9,1... | collective-permute-start | bytes 1179656 | tf_op jit(solution)/shard_map/ppermute | solution.py:314
  62.6 9.4 %collective-permute-start.9 = (bf16[2,8,48,128]{3,2,1,0:T(8,128)(2,1)S(1)}, bf16[2,8,48,128]{3,2,1,0:T(8,128)(2,1)S(1)}, u32[]{:S(2)}, u32[]{:S(2)}) collective-permute-start(bf16[2,8,48,128]{3,2,1,0:T(8,128)(2,1)S(1)} %shard_map.56.refs_1_), channel_id=1, source_target_pairs={{0,2},{2,0},{1,3},{3,1},{4,6},{6,4},{5,7},{7,5},{8,10},{10,8},{9,1... | collective-permute-start | bytes 589832 | tf_op jit(solution)/shard_map/ppermute | solution.py:314
  64.7 9.3 %collective-permute-start.10 = (bf16[2,8,48,128]{3,2,1,0:T(8,128)(2,1)S(1)}, bf16[2,8,48,128]{3,2,1,0:T(8,128)(2,1)S(1)}, u32[]{:S(2)}, u32[]{:S(2)}) collective-permute-start(bf16[2,8,48,128]{3,2,1,0:T(8,128)(2,1)S(1)} %shard_map.57.refs_2_), channel_id=1, source_target_pairs={{0,2},{2,0},{1,3},{3,1},{4,6},{6,4},{5,7},{7,5},{8,10},{10,8},{9,1... | collective-permute-start | bytes 589832 | tf_op jit(solution)/shard_map/ppermute | solution.py:314
  75.9 8.2 %collective-permute-start.24 = (bf16[272,128]{1,0:T(8,128)(2,1)S(1)}, bf16[272,128]{1,0:T(8,128)(2,1)S(1)}, u32[]{:S(2)}, u32[]{:S(2)}) collective-permute-start(bf16[272,128]{1,0:T(8,128)(2,1)S(1)} %get-tuple-element.79), channel_id=1, source_target_pairs={{0,8},{4,12},{8,0},{12,4},{1,9},{5,13},{9,1},{13,5},{2,10},{6,14},... | collective-permute-start | bytes 208904 | tf_op jit(solution)/shard_map/ppermute | solution.py:613
  77.4 5.8 %collective-permute-start.25 = (bf16[144,128]{1,0:T(8,128)(2,1)S(1)}, bf16[144,128]{1,0:T(8,128)(2,1)S(1)}, u32[]{:S(2)}, u32[]{:S(2)}) collective-permute-start(bf16[144,128]{1,0:T(8,128)(2,1)S(1)} %get-tuple-element.80), channel_id=1, source_target_pairs={{0,12},{4,8},{8,4},{12,0},{1,13},{5,9},{9,5},{13,1},{2,14},{6,10},... | collective-permute-start | bytes 110600 | tf_op jit(solution)/shard_map/ppermute | solution.py:613
  79.7 4.4 %collective-permute-start.26 = (bf16[144,128]{1,0:T(8,128)(2,1)S(1)}, bf16[144,128]{1,0:T(8,128)(2,1)S(1)}, u32[]{:S(2)}, u32[]{:S(2)}) collective-permute-start(bf16[144,128]{1,0:T(8,128)(2,1)S(1)} %get-tuple-element.81), channel_id=1, source_target_pairs={{0,4},{4,0},{8,12},{12,8},{1,5},{5,1},{9,13},{13,9},{2,6},{6,2},{1... | collective-permute-start | bytes 110600 | tf_op jit(solution)/shard_map/ppermute | solution.py:613
  (9 other events, 46.7 us)

commit v22 on v21

--- a/solution.py
+++ b/solution.py
@@ -131,23 +131,40 @@
     )(probes, source)
 
 
+def turn_body(c_ref, s_ref, _, c_out, s_out, square):
+    c_out[...] = turned(c_ref[...], square)
+    for n in range(s_ref.shape[0]):
+        s_out[n] = turned(s_ref[n], square)
+
+
+def turn(courant, source, after):
+    return call(
+        turn_body,
+        in_specs=whole_vmem(2) + [pl.BlockSpec(memory_space=pl.ANY)],
+        out_specs=whole_vmem(2),
+        out_shape=[
+            jax.ShapeDtypeStruct((LANES, LANES), F32),
+            jax.ShapeDtypeStruct((source.shape[0], LANES, LANES), F32),
+        ],
+        scratch_shapes=square_scratch()[:1],
+    )(courant, source, after)
+
+
 def local_body(chunk, moment, has_previous, *refs):
     refs = list(refs)
     u_ref, beside_ref, p_ref, c_ref, s_ref = refs[:5]
     prev_ref = refs[5] if has_previous else None
-    base_ref, square, turned_c, turned_s = refs[-4:]
+    base_ref = refs[-1]
     depth, across, along, _ = base_ref.shape
     core = lax.axis_index("sub")
     left_on = (core == 1).astype(F32)
     right_on = (core == 0).astype(F32)
-    turned_c[...] = turned(c_ref[...], square)
-    turned_s[...] = turned(s_ref[moment], square)
 
     def tile(start):
         span = pl.ds(start, TILE)
         rows = start + EDGE
-        courant = turned_c[span]
-        source = turned_s[span]
+        courant = c_ref[span]
+        source = s_ref[moment, span]
         for z in range(depth):
             beside = [beside_ref[z, j, span].astype(F32) for j in range(RADIUS)]
             row = [v * left_on for v in beside]
@@ -187,19 +204,17 @@
         in_specs=whole_vmem(len(operands)),
         out_specs=whole_vmem(1)[0],
         out_shape=shape_of(depth, across, along, F32),
-        scratch_shapes=square_scratch() + square_scratch()[:1],
     )(*operands)
 
 
-def part_body(sent, begin, base_ref, odd_ref, even_ref, c_ref, out_ref, square, turned_c):
+def part_body(sent, begin, base_ref, odd_ref, even_ref, c_ref, out_ref):
     depth, across, along, _ = base_ref.shape
     even = slab_is_even()
-    turned_c[...] = turned(c_ref[...], square)
 
     def planes(low):
         def tile(start):
             span = pl.ds(start, TILE)
-            courant = turned_c[span]
+            courant = c_ref[span]
             for x in range(across):
                 near = []
                 for j in range(RADIUS):
@@ -231,25 +246,23 @@
         in_specs=whole_vmem(4),
         out_specs=whole_vmem(1)[0],
         out_shape=shape_of(count, across, along, BF16),
-        scratch_shapes=square_scratch(),
     )(base, odds, evens, courant)
 
 
 def rim_body(kind, *refs):
     base_ref, odd_ref, even_ref, c_ref = refs[:4]
-    outs, (square, turned_c) = refs[4:-2], refs[-2:]
+    outs = refs[4:]
     depth, across, along, _ = base_ref.shape
     core = lax.axis_index("sub")
     even = slab_is_even()
     lower = lax.axis_index("probe") == 0
-    turned_c[...] = turned(c_ref[...], square)
     if kind == "middle":
         clear_pads(outs[0])
 
     def tile(start):
         span = pl.ds(start, TILE)
         rows = pl.ds(start + EDGE, TILE)
-        courant = turned_c[span]
+        courant = c_ref[span]
         for x in range(across):
             below, above = [], []
             for j in range(RADIUS):
@@ -306,7 +319,6 @@
         in_specs=whole_vmem(4),
         out_specs=whole_vmem(len(out_shape)),
         out_shape=out_shape,
-        scratch_shapes=square_scratch(),
     )(base, odds, evens, courant)
 
 
@@ -656,6 +668,7 @@
         u, *edges = first_field(probes, c, source[:1])
         now.append(u)
         halos.append(exchange(*edges))
+    courant, source = turn(courant, source, now[-1])
     finals = []
     for n in range(1, steps):
         for c in range(chunks):

time: 91.4 us -> 91.3 us (level)
  Pallas kernels: 25.2 us -> 23.9 us
  waiting for transfers between devices: 25.4 us -> 26.6 us
    ppermute x25, waiting for transfers between devices: 19.3 us -> 20.5 us  [swap(): lax.ppermute(x, axis, [p for a, b in pairs for p in ((a, b), (b, a))])]
  transfers between devices with their start and end apart: 29 -> 29, of which waited for: 14 -> 14; matrix products, arithmetic and copies ran while one was open for 0% -> 0% of each run, Pallas kernels for 25% -> 23%
where the time goes in v22:
time: 91.3 us; the launch traced here: 91 us
  starting transfers between devices  37.3 us (41%)
  waiting for transfers between devices  26.6 us (29%)
  Pallas kernels  23.9 us (26%)
  local copies, waits for them, and re-layouts  2.18 us (2%)
  between operations  1 us (1%)
    ppermute x25, starting transfers between devices, swap(): lax.ppermute(x, axis, [p for a, b in pairs for p in ((a, b), (b, a))])  31.7 us
    ppermute x25, waiting for transfers between devices, swap(): lax.ppermute(x, axis, [p for a, b in pairs for p in ((a, b), (b, a))])  20.5 us
    pallas_call x6, Pallas kernels, local_step(): call(functools.partial(local_body, chunk, moment, previous is not None),...  12.7 us
    pallas_call x5, Pallas kernels, rim_step(): call(functools.partial(rim_body, kind), in_specs=whole_vmem(4), out_specs...  4.81 us
    ppermute x3, waiting for transfers between devices, coupled(): lax.ppermute(blocks[d - 1], 'slab', [(i, i ^ d) for i in range(slabs)])  4.38 us
    ppermute x3, starting transfers between devices, coupled(): lax.ppermute(blocks[d - 1], 'slab', [(i, i ^ d) for i in range(slabs)])  3.85 us
    pallas_call x2, Pallas kernels, first_field(): call(functools.partial(first_body, chunk), in_specs=whole_vmem(2), out_sp...  2.1 us
  transfers between devices with their start and end apart: 29, of which 14 were waited for; matrix products, arithmetic and copies ran while one was open for 0% of the time, Pallas kernels for 23%

profile of v22, /device:TPU:0, one launch (start us, length us, event | category | flops | bytes accessed | tf_op | source)
XLA Modules:
  0.0 91.0 jit_solution(9288567683376110288)
XLA Ops:
  5.1 5.5 %collective-permute-start.13 = (bf16[4,8,48,128]{3,2,1,0:T(8,128)(2,1)S(1)}, bf16[4,8,48,128]{3,2,1,0:T(8,128)(2,1)S(1)}, u32[]{:S(2)}, u32[]{:S(2)}) collective-permute-start(bf16[4,8,48,128]{3,2,1,0:T(8,128)(2,1)S(1)} %get-tuple-element.62), channel_id=1, source_target_pairs={{0,4},{4,0},{8,12},{12,8},{1,5},{5,1},{9,13},{13,9},{2,6},{6,2},{1... | collective-permute-start | bytes 1179656 | tf_op jit(solution)/shard_map/ppermute | solution.py:326
  12.4 1.9 %collective-permute-start.2 = (bf16[4,8,48,128]{3,2,1,0:T(8,128)(2,1)S(1)}, bf16[4,8,48,128]{3,2,1,0:T(8,128)(2,1)S(1)}, u32[]{:S(2)}, u32[]{:S(2)}) collective-permute-start(bf16[4,8,48,128]{3,2,1,0:T(8,128)(2,1)S(1)} %get-tuple-element.51), channel_id=1, source_target_pairs={{0,4},{4,0},{8,12},{12,8},{1,5},{5,1},{9,13},{13,9},{2,6},{6,2},{1... | collective-permute-start | bytes 1179656 | tf_op jit(solution)/shard_map/ppermute | solution.py:326
  14.5 2.1 %shard_map.60.refs_0_ = f32[8,8,48,128]{3,2,1,0:T(8,128)S(1)} custom-call(f32[8,8,64,128]{3,2,1,0:T(8,128)S(1)} %get-tuple-element.47._.refs_0_.refs_5_, bf16[8,4,48,128]{3,2,1,0:T(8,128)(2,1)S(1)} %collective-permute-done.11.refs_1_, bf16[8,8,48,256]{3,2,1,0:T(8,128)(2,1)S(1)} %copy-done.1, f32[128,128]{1,0:T(8,128)S(1)} %get-tuple-element.48.refs_3_.c_ref, ...), custom_call_target="tpu_custom_call" | custom-call | flops 1 | bytes 1 | tf_op jit(solution)/shard_map/pallas_call | solution.py:202
  16.6 3.9 %collective-permute-done.13.refs_2_ = bf16[4,8,48,128]{3,2,1,0:T(8,128)(2,1)S(1)} collective-permute-done((bf16[4,8,48,128]{3,2,1,0:T(8,128)(2,1)S(1)}, bf16[4,8,48,128]{3,2,1,0:T(8,128)(2,1)S(1)}, u32[]{:S(2)}, u32[]{:S(2)}) %collective-permute-start.13) | collective-permute-done | bytes 393248 | tf_op jit(solution)/shard_map/ppermute | solution.py:326
  22.2 3.8 %collective-permute-start.16 = (bf16[4,8,48,128]{3,2,1,0:T(8,128)(2,1)S(1)}, bf16[4,8,48,128]{3,2,1,0:T(8,128)(2,1)S(1)}, u32[]{:S(2)}, u32[]{:S(2)}) collective-permute-start(bf16[4,8,48,128]{3,2,1,0:T(8,128)(2,1)S(1)} %get-tuple-element.66), channel_id=1, source_target_pairs={{0,4},{4,0},{8,12},{12,8},{1,5},{5,1},{9,13},{13,9},{2,6},{6,2},{1... | collective-permute-start | bytes 1179656 | tf_op jit(solution)/shard_map/ppermute | solution.py:326
  26.0 2.0 %shard_map.53.refs_0_ = f32[8,8,48,128]{3,2,1,0:T(8,128)S(1)} custom-call(f32[8,8,64,128]{3,2,1,0:T(8,128)S(1)} %get-tuple-element.45.refs_0_.refs_5_, bf16[8,4,48,128]{3,2,1,0:T(8,128)(2,1)S(1)} %collective-permute-done.refs_1_, bf16[8,8,48,256]{3,2,1,0:T(8,128)(2,1)S(1)} %copy-done.1, f32[128,128]{1,0:T(8,128)S(1)} %get-tuple-element.48.refs_3_.c_ref, ...), custom_call_target="tpu_custom_call" | custom-call | flops 1 | bytes 1 | tf_op jit(solution)/shard_map/pallas_call | solution.py:202
  30.6 3.4 %collective-permute-start.5 = (bf16[4,8,48,128]{3,2,1,0:T(8,128)(2,1)S(1)}, bf16[4,8,48,128]{3,2,1,0:T(8,128)(2,1)S(1)}, u32[]{:S(2)}, u32[]{:S(2)}) collective-permute-start(bf16[4,8,48,128]{3,2,1,0:T(8,128)(2,1)S(1)} %get-tuple-element.55), channel_id=1, source_target_pairs={{0,4},{4,0},{8,12},{12,8},{1,5},{5,1},{9,13},{13,9},{2,6},{6,2},{1... | collective-permute-start | bytes 1179656 | tf_op jit(solution)/shard_map/ppermute | solution.py:326
  34.0 2.1 %shard_map.62.refs_0_ = f32[8,8,48,128]{3,2,1,0:T(8,128)S(1)} custom-call(f32[8,8,64,128]{3,2,1,0:T(8,128)S(1)} %get-tuple-element.63.refs_0_.refs_5_, bf16[8,4,48,128]{3,2,1,0:T(8,128)(2,1)S(1)} %collective-permute-done.14.refs_1_, bf16[8,8,48,256]{3,2,1,0:T(8,128)(2,1)S(1)} %copy-done.1, f32[128,128]{1,0:T(8,128)S(1)} %get-tuple-element.48.refs_3_.c_ref, ...), custom_call_target="tpu_custom_call" | custom-call | flops 1 | bytes 1 | tf_op jit(solution)/shard_map/pallas_call | solution.py:202
  39.1 3.4 %collective-permute-start.19 = (bf16[4,8,48,128]{3,2,1,0:T(8,128)(2,1)S(1)}, bf16[4,8,48,128]{3,2,1,0:T(8,128)(2,1)S(1)}, u32[]{:S(2)}, u32[]{:S(2)}) collective-permute-start(bf16[4,8,48,128]{3,2,1,0:T(8,128)(2,1)S(1)} %get-tuple-element.70), channel_id=1, source_target_pairs={{0,4},{4,0},{8,12},{12,8},{1,5},{5,1},{9,13},{13,9},{2,6},{6,2},{1... | collective-permute-start | bytes 1179656 | tf_op jit(solution)/shard_map/ppermute | solution.py:326
  42.4 2.1 %shard_map.55.refs_0_ = f32[8,8,48,128]{3,2,1,0:T(8,128)S(1)} custom-call(f32[8,8,64,128]{3,2,1,0:T(8,128)S(1)} %get-tuple-element.52.refs_0_.refs_5_, bf16[8,4,48,128]{3,2,1,0:T(8,128)(2,1)S(1)} %collective-permute-done.3.refs_1_, bf16[8,8,48,256]{3,2,1,0:T(8,128)(2,1)S(1)} %copy-done.1, f32[128,128]{1,0:T(8,128)S(1)} %get-tuple-element.48.refs_3_.c_ref, ...), custom_call_target="tpu_custom_call" | custom-call | flops 1 | bytes 1 | tf_op jit(solution)/shard_map/pallas_call | solution.py:202
  47.5 3.4 %collective-permute-start.8 = (bf16[4,8,48,128]{3,2,1,0:T(8,128)(2,1)S(1)}, bf16[4,8,48,128]{3,2,1,0:T(8,128)(2,1)S(1)}, u32[]{:S(2)}, u32[]{:S(2)}) collective-permute-start(bf16[4,8,48,128]{3,2,1,0:T(8,128)(2,1)S(1)} %get-tuple-element.59), channel_id=1, source_target_pairs={{0,4},{4,0},{8,12},{12,8},{1,5},{5,1},{9,13},{13,9},{2,6},{6,2},{1... | collective-permute-start | bytes 1179656 | tf_op jit(solution)/shard_map/ppermute | solution.py:326
  50.9 2.1 %shard_map.64.refs_0_ = f32[8,8,48,128]{3,2,1,0:T(8,128)S(1)} custom-call(f32[8,8,64,128]{3,2,1,0:T(8,128)S(1)} %get-tuple-element.67.refs_0_, bf16[8,4,48,128]{3,2,1,0:T(8,128)(2,1)S(1)} %collective-permute-done.17.refs_1_, bf16[8,8,48,256]{3,2,1,0:T(8,128)(2,1)S(1)} %copy-done.1, f32[128,128]{1,0:T(8,128)S(1)} %get-tuple-element.48.refs_3_.c_ref, ...), custom_call_target="tpu_custom_call" | custom-call | flops 1 | bytes 1 | tf_op jit(solution)/shard_map/pallas_call | solution.py:202
  55.0 1.6 %collective-permute-start.20 = (bf16[4,8,48,128]{3,2,1,0:T(8,128)(2,1)S(1)}, bf16[4,8,48,128]{3,2,1,0:T(8,128)(2,1)S(1)}, u32[]{:S(2)}, u32[]{:S(2)}) collective-permute-start(bf16[4,8,48,128]{3,2,1,0:T(8,128)(2,1)S(1)} %get-tuple-element.71.refs_4_), channel_id=1, source_target_pairs={{0,2},{2,0},{1,3},{3,1},{4,6},{6,4},{5,7},{7,5},{8,10},{10,8},{9,1... | collective-permute-start | bytes 1179656 | tf_op jit(solution)/shard_map/ppermute | solution.py:326
  56.5 2.1 %shard_map.57.base_ref = f32[8,8,48,128]{3,2,1,0:T(8,128)S(1)} custom-call(f32[8,8,64,128]{3,2,1,0:T(8,128)S(1)} %get-tuple-element.56.refs_0_, bf16[8,4,48,128]{3,2,1,0:T(8,128)(2,1)S(1)} %collective-permute-done.6.refs_1_, bf16[8,8,48,256]{3,2,1,0:T(8,128)(2,1)S(1)} %copy-done.1, f32[128,128]{1,0:T(8,128)S(1)} %get-tuple-element.48.refs_3_.c_ref, ...), custom_call_target="tpu_custom_call" | custom-call | flops 1 | bytes 1 | tf_op jit(solution)/shard_map/pallas_call | solution.py:202
  58.7 3.5 %collective-permute-done.8.even_ref = bf16[4,8,48,128]{3,2,1,0:T(8,128)(2,1)S(1)} collective-permute-done((bf16[4,8,48,128]{3,2,1,0:T(8,128)(2,1)S(1)}, bf16[4,8,48,128]{3,2,1,0:T(8,128)(2,1)S(1)}, u32[]{:S(2)}, u32[]{:S(2)}) %collective-permute-start.8) | collective-permute-done | bytes 393248 | tf_op jit(solution)/shard_map/ppermute | solution.py:326
  62.5 1.6 %collective-permute-start.9 = (bf16[2,8,48,128]{3,2,1,0:T(8,128)(2,1)S(1)}, bf16[2,8,48,128]{3,2,1,0:T(8,128)(2,1)S(1)}, u32[]{:S(2)}, u32[]{:S(2)}) collective-permute-start(bf16[2,8,48,128]{3,2,1,0:T(8,128)(2,1)S(1)} %shard_map.58.refs_1_), channel_id=1, source_target_pairs={{0,2},{2,0},{1,3},{3,1},{4,6},{6,4},{5,7},{7,5},{8,10},{10,8},{9,1... | collective-permute-start | bytes 589832 | tf_op jit(solution)/shard_map/ppermute | solution.py:326
  67.7 1.8 %collective-permute-start.22 = (bf16[128,128]{1,0:T(8,128)(2,1)S(1)}, bf16[128,128]{1,0:T(8,128)(2,1)S(1)}, u32[]{:S(2)}, u32[]{:S(2)}) collective-permute-start(bf16[128,128]{1,0:T(8,128)(2,1)S(1)} %get-tuple-element.77), channel_id=1, source_target_pairs={{0,4},{4,0},{8,12},{12,8},{1,5},{5,1},{9,13},{13,9},{2,6},{6,2},{1... | collective-permute-start | bytes 98312 | tf_op jit(solution)/shard_map/ppermute | solution.py:620
  70.0 1.7 %collective-permute-done.22.refs_4_.inner_got_ref = bf16[128,128]{1,0:T(8,128)(2,1)S(1)} collective-permute-done((bf16[128,128]{1,0:T(8,128)(2,1)S(1)}, bf16[128,128]{1,0:T(8,128)(2,1)S(1)}, u32[]{:S(2)}, u32[]{:S(2)}) %collective-permute-start.22) | collective-permute-done | bytes 32800 | tf_op jit(solution)/shard_map/ppermute | solution.py:620
  71.7 2.1 %collective-permute-done.10.refs_1_ = bf16[2,8,48,128]{3,2,1,0:T(8,128)(2,1)S(1)} collective-permute-done((bf16[2,8,48,128]{3,2,1,0:T(8,128)(2,1)S(1)}, bf16[2,8,48,128]{3,2,1,0:T(8,128)(2,1)S(1)}, u32[]{:S(2)}, u32[]{:S(2)}) %collective-permute-start.10) | collective-permute-done | bytes 196640 | tf_op jit(solution)/shard_map/ppermute | solution.py:326
  75.7 1.6 %collective-permute-start.24 = (bf16[272,128]{1,0:T(8,128)(2,1)S(1)}, bf16[272,128]{1,0:T(8,128)(2,1)S(1)}, u32[]{:S(2)}, u32[]{:S(2)}) collective-permute-start(bf16[272,128]{1,0:T(8,128)(2,1)S(1)} %get-tuple-element.83), channel_id=1, source_target_pairs={{0,8},{4,12},{8,0},{12,4},{1,9},{5,13},{9,1},{13,5},{2,10},{6,14},... | collective-permute-start | bytes 208904 | tf_op jit(solution)/shard_map/ppermute | solution.py:625
  77.4 2.2 %collective-permute-start.25 = (bf16[144,128]{1,0:T(8,128)(2,1)S(1)}, bf16[144,128]{1,0:T(8,128)(2,1)S(1)}, u32[]{:S(2)}, u32[]{:S(2)}) collective-permute-start(bf16[144,128]{1,0:T(8,128)(2,1)S(1)} %get-tuple-element.84), channel_id=1, source_target_pairs={{0,12},{4,8},{8,4},{12,0},{1,13},{5,9},{9,5},{13,1},{2,14},{6,10},... | collective-permute-start | bytes 110600 | tf_op jit(solution)/shard_map/ppermute | solution.py:625
  79.6 3.6 %collective-permute-done.25.refs_1_ = bf16[144,128]{1,0:T(8,128)(2,1)S(1)} collective-permute-done((bf16[144,128]{1,0:T(8,128)(2,1)S(1)}, bf16[144,128]{1,0:T(8,128)(2,1)S(1)}, u32[]{:S(2)}, u32[]{:S(2)}) %collective-permute-start.25) | collective-permute-done | bytes 36896 | tf_op jit(solution)/shard_map/ppermute | solution.py:625
  84.0 1.6 %collective-permute-start.27 = (bf16[272,128]{1,0:T(8,128)(2,1)S(1)}, bf16[272,128]{1,0:T(8,128)(2,1)S(1)}, u32[]{:S(2)}, u32[]{:S(2)}) collective-permute-start(bf16[272,128]{1,0:T(8,128)(2,1)S(1)} %shard_map.72.mine_ref), channel_id=1, source_target_pairs={{0,2},{2,0},{1,3},{3,1},{4,6},{6,4},{5,7},{7,5},{8,10},{10,8},{9,1... | collective-permute-start | bytes 208904 | tf_op jit(solution)/shard_map/ppermute | solution.py:326
  85.6 2.8 %collective-permute-done.27.other_ref = bf16[272,128]{1,0:T(8,128)(2,1)S(1)} collective-permute-done((bf16[272,128]{1,0:T(8,128)(2,1)S(1)}, bf16[272,128]{1,0:T(8,128)(2,1)S(1)}, u32[]{:S(2)}, u32[]{:S(2)}) %collective-permute-start.27) | collective-permute-done | bytes 69664 | tf_op jit(solution)/shard_map/ppermute | solution.py:326
  (68 shorter events, 28.2 us)
Async XLA Ops:
  3.9 8.5 %collective-permute-start.11 = (bf16[8,4,48,128]{3,2,1,0:T(8,128)(2,1)S(1)}, bf16[8,4,48,128]{3,2,1,0:T(8,128)(2,1)S(1)}, u32[]{:S(2)}, u32[]{:S(2)}) collective-permute-start(bf16[8,4,48,128]{3,2,1,0:T(8,128)(2,1)S(1)} %get-tuple-element.60), channel_id=1, source_target_pairs={{0,1},{1,0},{2,3},{3,2},{4,5},{5,4},{6,7},{7,6},{8,9},{9,8},{10,11... | collective-permute-start | bytes 1179656 | tf_op jit(solution)/shard_map/ppermute | solution.py:326
  4.4 12.2 %collective-permute-start.12 = (bf16[4,8,48,128]{3,2,1,0:T(8,128)(2,1)S(1)}, bf16[4,8,48,128]{3,2,1,0:T(8,128)(2,1)S(1)}, u32[]{:S(2)}, u32[]{:S(2)}) collective-permute-start(bf16[4,8,48,128]{3,2,1,0:T(8,128)(2,1)S(1)} %get-tuple-element.61), channel_id=1, source_target_pairs={{4,8},{8,4},{5,9},{9,5},{6,10},{10,6},{7,11},{11,7},{20,24},{24,20... | collective-permute-start | bytes 1179656 | tf_op jit(solution)/shard_map/ppermute | solution.py:326
  5.1 15.4 %collective-permute-start.13 = (bf16[4,8,48,128]{3,2,1,0:T(8,128)(2,1)S(1)}, bf16[4,8,48,128]{3,2,1,0:T(8,128)(2,1)S(1)}, u32[]{:S(2)}, u32[]{:S(2)}) collective-permute-start(bf16[4,8,48,128]{3,2,1,0:T(8,128)(2,1)S(1)} %get-tuple-element.62), channel_id=1, source_target_pairs={{0,4},{4,0},{8,12},{12,8},{1,5},{5,1},{9,13},{13,9},{2,6},{6,2},{1... | collective-permute-start | bytes 1179656 | tf_op jit(solution)/shard_map/ppermute | solution.py:326
  11.6 10.6 %collective-permute-start = (bf16[8,4,48,128]{3,2,1,0:T(8,128)(2,1)S(1)}, bf16[8,4,48,128]{3,2,1,0:T(8,128)(2,1)S(1)}, u32[]{:S(2)}, u32[]{:S(2)}) collective-permute-start(bf16[8,4,48,128]{3,2,1,0:T(8,128)(2,1)S(1)} %get-tuple-element.46), channel_id=1, source_target_pairs={{0,1},{1,0},{2,3},{3,2},{4,5},{5,4},{6,7},{7,6},{8,9},{9,8},{10,11... | collective-permute-start | bytes 1179656 | tf_op jit(solution)/shard_map/ppermute | solution.py:326
  11.7 16.4 %collective-permute-start.1 = (bf16[4,8,48,128]{3,2,1,0:T(8,128)(2,1)S(1)}, bf16[4,8,48,128]{3,2,1,0:T(8,128)(2,1)S(1)}, u32[]{:S(2)}, u32[]{:S(2)}) collective-permute-start(bf16[4,8,48,128]{3,2,1,0:T(8,128)(2,1)S(1)} %get-tuple-element.50), channel_id=1, source_target_pairs={{4,8},{8,4},{5,9},{9,5},{6,10},{10,6},{7,11},{11,7},{20,24},{24,20... | collective-permute-start | bytes 1179656 | tf_op jit(solution)/shard_map/ppermute | solution.py:326
  12.4 16.5 %collective-permute-start.2 = (bf16[4,8,48,128]{3,2,1,0:T(8,128)(2,1)S(1)}, bf16[4,8,48,128]{3,2,1,0:T(8,128)(2,1)S(1)}, u32[]{:S(2)}, u32[]{:S(2)}) collective-permute-start(bf16[4,8,48,128]{3,2,1,0:T(8,128)(2,1)S(1)} %get-tuple-element.51), channel_id=1, source_target_pairs={{0,4},{4,0},{8,12},{12,8},{1,5},{5,1},{9,13},{13,9},{2,6},{6,2},{1... | collective-permute-start | bytes 1179656 | tf_op jit(solution)/shard_map/ppermute | solution.py:326
  21.4 9.2 %collective-permute-start.14 = (bf16[8,4,48,128]{3,2,1,0:T(8,128)(2,1)S(1)}, bf16[8,4,48,128]{3,2,1,0:T(8,128)(2,1)S(1)}, u32[]{:S(2)}, u32[]{:S(2)}) collective-permute-start(bf16[8,4,48,128]{3,2,1,0:T(8,128)(2,1)S(1)} %get-tuple-element.64), channel_id=1, source_target_pairs={{0,1},{1,0},{2,3},{3,2},{4,5},{5,4},{6,7},{7,6},{8,9},{9,8},{10,11... | collective-permute-start | bytes 1179656 | tf_op jit(solution)/shard_map/ppermute | solution.py:326
  21.5 14.7 %collective-permute-start.15 = (bf16[4,8,48,128]{3,2,1,0:T(8,128)(2,1)S(1)}, bf16[4,8,48,128]{3,2,1,0:T(8,128)(2,1)S(1)}, u32[]{:S(2)}, u32[]{:S(2)}) collective-permute-start(bf16[4,8,48,128]{3,2,1,0:T(8,128)(2,1)S(1)} %get-tuple-element.65), channel_id=1, source_target_pairs={{4,8},{8,4},{5,9},{9,5},{6,10},{10,6},{7,11},{11,7},{20,24},{24,20... | collective-permute-start | bytes 1179656 | tf_op jit(solution)/shard_map/ppermute | solution.py:326
  22.2 15.1 %collective-permute-start.16 = (bf16[4,8,48,128]{3,2,1,0:T(8,128)(2,1)S(1)}, bf16[4,8,48,128]{3,2,1,0:T(8,128)(2,1)S(1)}, u32[]{:S(2)}, u32[]{:S(2)}) collective-permute-start(bf16[4,8,48,128]{3,2,1,0:T(8,128)(2,1)S(1)} %get-tuple-element.66), channel_id=1, source_target_pairs={{0,4},{4,0},{8,12},{12,8},{1,5},{5,1},{9,13},{13,9},{2,6},{6,2},{1... | collective-permute-start | bytes 1179656 | tf_op jit(solution)/shard_map/ppermute | solution.py:326
  29.9 9.2 %collective-permute-start.3 = (bf16[8,4,48,128]{3,2,1,0:T(8,128)(2,1)S(1)}, bf16[8,4,48,128]{3,2,1,0:T(8,128)(2,1)S(1)}, u32[]{:S(2)}, u32[]{:S(2)}) collective-permute-start(bf16[8,4,48,128]{3,2,1,0:T(8,128)(2,1)S(1)} %get-tuple-element.53), channel_id=1, source_target_pairs={{0,1},{1,0},{2,3},{3,2},{4,5},{5,4},{6,7},{7,6},{8,9},{9,8},{10,11... | collective-permute-start | bytes 1179656 | tf_op jit(solution)/shard_map/ppermute | solution.py:326
  29.9 14.6 %collective-permute-start.4 = (bf16[4,8,48,128]{3,2,1,0:T(8,128)(2,1)S(1)}, bf16[4,8,48,128]{3,2,1,0:T(8,128)(2,1)S(1)}, u32[]{:S(2)}, u32[]{:S(2)}) collective-permute-start(bf16[4,8,48,128]{3,2,1,0:T(8,128)(2,1)S(1)} %get-tuple-element.54), channel_id=1, source_target_pairs={{4,8},{8,4},{5,9},{9,5},{6,10},{10,6},{7,11},{11,7},{20,24},{24,20... | collective-permute-start | bytes 1179656 | tf_op jit(solution)/shard_map/ppermute | solution.py:326
  30.6 15.1 %collective-permute-start.5 = (bf16[4,8,48,128]{3,2,1,0:T(8,128)(2,1)S(1)}, bf16[4,8,48,128]{3,2,1,0:T(8,128)(2,1)S(1)}, u32[]{:S(2)}, u32[]{:S(2)}) collective-permute-start(bf16[4,8,48,128]{3,2,1,0:T(8,128)(2,1)S(1)} %get-tuple-element.55), channel_id=1, source_target_pairs={{0,4},{4,0},{8,12},{12,8},{1,5},{5,1},{9,13},{13,9},{2,6},{6,2},{1... | collective-permute-start | bytes 1179656 | tf_op jit(solution)/shard_map/ppermute | solution.py:326
  38.3 9.2 %collective-permute-start.17 = (bf16[8,4,48,128]{3,2,1,0:T(8,128)(2,1)S(1)}, bf16[8,4,48,128]{3,2,1,0:T(8,128)(2,1)S(1)}, u32[]{:S(2)}, u32[]{:S(2)}) collective-permute-start(bf16[8,4,48,128]{3,2,1,0:T(8,128)(2,1)S(1)} %get-tuple-element.68), channel_id=1, source_target_pairs={{0,1},{1,0},{2,3},{3,2},{4,5},{5,4},{6,7},{7,6},{8,9},{9,8},{10,11... | collective-permute-start | bytes 1179656 | tf_op jit(solution)/shard_map/ppermute | solution.py:326
  38.4 14.7 %collective-permute-start.18 = (bf16[4,8,48,128]{3,2,1,0:T(8,128)(2,1)S(1)}, bf16[4,8,48,128]{3,2,1,0:T(8,128)(2,1)S(1)}, u32[]{:S(2)}, u32[]{:S(2)}) collective-permute-start(bf16[4,8,48,128]{3,2,1,0:T(8,128)(2,1)S(1)} %get-tuple-element.69), channel_id=1, source_target_pairs={{4,8},{8,4},{5,9},{9,5},{6,10},{10,6},{7,11},{11,7},{20,24},{24,20... | collective-permute-start | bytes 1179656 | tf_op jit(solution)/shard_map/ppermute | solution.py:326
  39.1 15.1 %collective-permute-start.19 = (bf16[4,8,48,128]{3,2,1,0:T(8,128)(2,1)S(1)}, bf16[4,8,48,128]{3,2,1,0:T(8,128)(2,1)S(1)}, u32[]{:S(2)}, u32[]{:S(2)}) collective-permute-start(bf16[4,8,48,128]{3,2,1,0:T(8,128)(2,1)S(1)} %get-tuple-element.70), channel_id=1, source_target_pairs={{0,4},{4,0},{8,12},{12,8},{1,5},{5,1},{9,13},{13,9},{2,6},{6,2},{1... | collective-permute-start | bytes 1179656 | tf_op jit(solution)/shard_map/ppermute | solution.py:326
  46.7 9.8 %collective-permute-start.6 = (bf16[8,4,48,128]{3,2,1,0:T(8,128)(2,1)S(1)}, bf16[8,4,48,128]{3,2,1,0:T(8,128)(2,1)S(1)}, u32[]{:S(2)}, u32[]{:S(2)}) collective-permute-start(bf16[8,4,48,128]{3,2,1,0:T(8,128)(2,1)S(1)} %get-tuple-element.57), channel_id=1, source_target_pairs={{0,1},{1,0},{2,3},{3,2},{4,5},{5,4},{6,7},{7,6},{8,9},{9,8},{10,11... | collective-permute-start | bytes 1179656 | tf_op jit(solution)/shard_map/ppermute | solution.py:326
  46.8 11.9 %collective-permute-start.7 = (bf16[4,8,48,128]{3,2,1,0:T(8,128)(2,1)S(1)}, bf16[4,8,48,128]{3,2,1,0:T(8,128)(2,1)S(1)}, u32[]{:S(2)}, u32[]{:S(2)}) collective-permute-start(bf16[4,8,48,128]{3,2,1,0:T(8,128)(2,1)S(1)} %get-tuple-element.58), channel_id=1, source_target_pairs={{4,8},{8,4},{5,9},{9,5},{6,10},{10,6},{7,11},{11,7},{20,24},{24,20... | collective-permute-start | bytes 1179656 | tf_op jit(solution)/shard_map/ppermute | solution.py:326
  47.5 14.7 %collective-permute-start.8 = (bf16[4,8,48,128]{3,2,1,0:T(8,128)(2,1)S(1)}, bf16[4,8,48,128]{3,2,1,0:T(8,128)(2,1)S(1)}, u32[]{:S(2)}, u32[]{:S(2)}) collective-permute-start(bf16[4,8,48,128]{3,2,1,0:T(8,128)(2,1)S(1)} %get-tuple-element.59), channel_id=1, source_target_pairs={{0,4},{4,0},{8,12},{12,8},{1,5},{5,1},{9,13},{13,9},{2,6},{6,2},{1... | collective-permute-start | bytes 1179656 | tf_op jit(solution)/shard_map/ppermute | solution.py:326
  55.0 14.5 %collective-permute-start.20 = (bf16[4,8,48,128]{3,2,1,0:T(8,128)(2,1)S(1)}, bf16[4,8,48,128]{3,2,1,0:T(8,128)(2,1)S(1)}, u32[]{:S(2)}, u32[]{:S(2)}) collective-permute-start(bf16[4,8,48,128]{3,2,1,0:T(8,128)(2,1)S(1)} %get-tuple-element.71.refs_4_), channel_id=1, source_target_pairs={{0,2},{2,0},{1,3},{3,1},{4,6},{6,4},{5,7},{7,5},{8,10},{10,8},{9,1... | collective-permute-start | bytes 1179656 | tf_op jit(solution)/shard_map/ppermute | solution.py:326
  62.5 9.2 %collective-permute-start.9 = (bf16[2,8,48,128]{3,2,1,0:T(8,128)(2,1)S(1)}, bf16[2,8,48,128]{3,2,1,0:T(8,128)(2,1)S(1)}, u32[]{:S(2)}, u32[]{:S(2)}) collective-permute-start(bf16[2,8,48,128]{3,2,1,0:T(8,128)(2,1)S(1)} %shard_map.58.refs_1_), channel_id=1, source_target_pairs={{0,2},{2,0},{1,3},{3,1},{4,6},{6,4},{5,7},{7,5},{8,10},{10,8},{9,1... | collective-permute-start | bytes 589832 | tf_op jit(solution)/shard_map/ppermute | solution.py:326
  64.5 9.3 %collective-permute-start.10 = (bf16[2,8,48,128]{3,2,1,0:T(8,128)(2,1)S(1)}, bf16[2,8,48,128]{3,2,1,0:T(8,128)(2,1)S(1)}, u32[]{:S(2)}, u32[]{:S(2)}) collective-permute-start(bf16[2,8,48,128]{3,2,1,0:T(8,128)(2,1)S(1)} %shard_map.59.refs_2_), channel_id=1, source_target_pairs={{0,2},{2,0},{1,3},{3,1},{4,6},{6,4},{5,7},{7,5},{8,10},{10,8},{9,1... | collective-permute-start | bytes 589832 | tf_op jit(solution)/shard_map/ppermute | solution.py:326
  75.7 8.2 %collective-permute-start.24 = (bf16[272,128]{1,0:T(8,128)(2,1)S(1)}, bf16[272,128]{1,0:T(8,128)(2,1)S(1)}, u32[]{:S(2)}, u32[]{:S(2)}) collective-permute-start(bf16[272,128]{1,0:T(8,128)(2,1)S(1)} %get-tuple-element.83), channel_id=1, source_target_pairs={{0,8},{4,12},{8,0},{12,4},{1,9},{5,13},{9,1},{13,5},{2,10},{6,14},... | collective-permute-start | bytes 208904 | tf_op jit(solution)/shard_map/ppermute | solution.py:625
  77.4 5.9 %collective-permute-start.25 = (bf16[144,128]{1,0:T(8,128)(2,1)S(1)}, bf16[144,128]{1,0:T(8,128)(2,1)S(1)}, u32[]{:S(2)}, u32[]{:S(2)}) collective-permute-start(bf16[144,128]{1,0:T(8,128)(2,1)S(1)} %get-tuple-element.84), channel_id=1, source_target_pairs={{0,12},{4,8},{8,4},{12,0},{1,13},{5,9},{9,5},{13,1},{2,14},{6,10},... | collective-permute-start | bytes 110600 | tf_op jit(solution)/shard_map/ppermute | solution.py:625
  79.6 4.4 %collective-permute-start.26 = (bf16[144,128]{1,0:T(8,128)(2,1)S(1)}, bf16[144,128]{1,0:T(8,128)(2,1)S(1)}, u32[]{:S(2)}, u32[]{:S(2)}) collective-permute-start(bf16[144,128]{1,0:T(8,128)(2,1)S(1)} %get-tuple-element.85), channel_id=1, source_target_pairs={{0,4},{4,0},{8,12},{12,8},{1,5},{5,1},{9,13},{13,9},{2,6},{6,2},{1... | collective-permute-start | bytes 110600 | tf_op jit(solution)/shard_map/ppermute | solution.py:625
  (9 other events, 46.5 us)

commit v23 on v22

--- a/solution.py
+++ b/solution.py
@@ -119,7 +119,8 @@
     depth, across, along, _ = probes.shape
     return call(
         functools.partial(first_body, chunk),
-        in_specs=whole_vmem(2),
+        grid=(1,),
+        in_specs=whole_vmem(1) + [pl.BlockSpec((1,) + source.shape[1:], lambda i: (0, 0, 0))],
         out_specs=whole_vmem(4),
         out_shape=[
             shape_of(depth, across, along + 2 * EDGE, F32),
@@ -665,7 +666,7 @@
     exchange = lambda odd, even, edge: (odd_swap(odd), even_swap(even), core_swap(edge))
     now, previous, halos = [], [None] * chunks, []
     for c in range(chunks):
-        u, *edges = first_field(probes, c, source[:1])
+        u, *edges = first_field(probes, c, source)
         now.append(u)
         halos.append(exchange(*edges))
     courant, source = turn(courant, source, now[-1])

time: 91.3 us -> 91.4 us (level)
  no operation moved by 1% of the time
where the time goes in v23:
time: 91.4 us; the launch traced here: 91.1 us
  starting transfers between devices  37.3 us (41%)
  waiting for transfers between devices  26.6 us (29%)
  Pallas kernels  23.9 us (26%)
  local copies, waits for them, and re-layouts  2.32 us (3%)
  between operations  1 us (1%)
    ppermute x25, starting transfers between devices, swap(): lax.ppermute(x, axis, [p for a, b in pairs for p in ((a, b), (b, a))])  31.7 us
    ppermute x25, waiting for transfers between devices, swap(): lax.ppermute(x, axis, [p for a, b in pairs for p in ((a, b), (b, a))])  20.5 us
    pallas_call x6, Pallas kernels, local_step(): call(functools.partial(local_body, chunk, moment, previous is not None),...  12.7 us
    pallas_call x5, Pallas kernels, rim_step(): call(functools.partial(rim_body, kind), in_specs=whole_vmem(4), out_specs...  4.81 us
    ppermute x3, waiting for transfers between devices, coupled(): lax.ppermute(blocks[d - 1], 'slab', [(i, i ^ d) for i in range(slabs)])  4.38 us
    ppermute x3, starting transfers between devices, coupled(): lax.ppermute(blocks[d - 1], 'slab', [(i, i ^ d) for i in range(slabs)])  3.85 us
    unnamed x8, local copies, waits for them, and re-layouts  2.32 us
    pallas_call x2, Pallas kernels, first_field(): call(functools.partial(first_body, chunk), grid=(1,), in_specs=whole_vmem...  2.1 us
  transfers between devices with their start and end apart: 29, of which 14 were waited for; matrix products, arithmetic and copies ran while one was open for 0% of the time, Pallas kernels for 23%

profile of v23, /device:TPU:0, one launch (start us, length us, event | category | flops | bytes accessed | tf_op | source)
XLA Modules:
  0.0 91.1 jit_solution(8787756203951622294)
XLA Ops:
  5.2 5.5 %collective-permute-start.13 = (bf16[4,8,48,128]{3,2,1,0:T(8,128)(2,1)S(1)}, bf16[4,8,48,128]{3,2,1,0:T(8,128)(2,1)S(1)}, u32[]{:S(2)}, u32[]{:S(2)}) collective-permute-start(bf16[4,8,48,128]{3,2,1,0:T(8,128)(2,1)S(1)} %get-tuple-element.62), channel_id=1, source_target_pairs={{0,4},{4,0},{8,12},{12,8},{1,5},{5,1},{9,13},{13,9},{2,6},{6,2},{1... | collective-permute-start | bytes 1179656 | tf_op jit(solution)/shard_map/ppermute | solution.py:327
  12.5 1.9 %collective-permute-start.2 = (bf16[4,8,48,128]{3,2,1,0:T(8,128)(2,1)S(1)}, bf16[4,8,48,128]{3,2,1,0:T(8,128)(2,1)S(1)}, u32[]{:S(2)}, u32[]{:S(2)}) collective-permute-start(bf16[4,8,48,128]{3,2,1,0:T(8,128)(2,1)S(1)} %get-tuple-element.51), channel_id=1, source_target_pairs={{0,4},{4,0},{8,12},{12,8},{1,5},{5,1},{9,13},{13,9},{2,6},{6,2},{1... | collective-permute-start | bytes 1179656 | tf_op jit(solution)/shard_map/ppermute | solution.py:327
  14.6 2.1 %shard_map.60.refs_0_ = f32[8,8,48,128]{3,2,1,0:T(8,128)S(1)} custom-call(f32[8,8,64,128]{3,2,1,0:T(8,128)S(1)} %get-tuple-element.47._.refs_0_.refs_5_, bf16[8,4,48,128]{3,2,1,0:T(8,128)(2,1)S(1)} %collective-permute-done.11.refs_1_, bf16[8,8,48,256]{3,2,1,0:T(8,128)(2,1)S(1)} %copy-done.1, f32[128,128]{1,0:T(8,128)S(1)} %get-tuple-element.48.refs_3_.c_ref, ...), custom_call_target="tpu_custom_call" | custom-call | flops 1 | bytes 1 | tf_op jit(solution)/shard_map/pallas_call | solution.py:203
  16.7 3.9 %collective-permute-done.13.refs_2_ = bf16[4,8,48,128]{3,2,1,0:T(8,128)(2,1)S(1)} collective-permute-done((bf16[4,8,48,128]{3,2,1,0:T(8,128)(2,1)S(1)}, bf16[4,8,48,128]{3,2,1,0:T(8,128)(2,1)S(1)}, u32[]{:S(2)}, u32[]{:S(2)}) %collective-permute-start.13) | collective-permute-done | bytes 393248 | tf_op jit(solution)/shard_map/ppermute | solution.py:327
  22.4 3.8 %collective-permute-start.16 = (bf16[4,8,48,128]{3,2,1,0:T(8,128)(2,1)S(1)}, bf16[4,8,48,128]{3,2,1,0:T(8,128)(2,1)S(1)}, u32[]{:S(2)}, u32[]{:S(2)}) collective-permute-start(bf16[4,8,48,128]{3,2,1,0:T(8,128)(2,1)S(1)} %get-tuple-element.66), channel_id=1, source_target_pairs={{0,4},{4,0},{8,12},{12,8},{1,5},{5,1},{9,13},{13,9},{2,6},{6,2},{1... | collective-permute-start | bytes 1179656 | tf_op jit(solution)/shard_map/ppermute | solution.py:327
  26.2 2.0 %shard_map.53.refs_0_ = f32[8,8,48,128]{3,2,1,0:T(8,128)S(1)} custom-call(f32[8,8,64,128]{3,2,1,0:T(8,128)S(1)} %get-tuple-element.45.refs_0_.refs_5_, bf16[8,4,48,128]{3,2,1,0:T(8,128)(2,1)S(1)} %collective-permute-done.refs_1_, bf16[8,8,48,256]{3,2,1,0:T(8,128)(2,1)S(1)} %copy-done.1, f32[128,128]{1,0:T(8,128)S(1)} %get-tuple-element.48.refs_3_.c_ref, ...), custom_call_target="tpu_custom_call" | custom-call | flops 1 | bytes 1 | tf_op jit(solution)/shard_map/pallas_call | solution.py:203
  30.8 3.4 %collective-permute-start.5 = (bf16[4,8,48,128]{3,2,1,0:T(8,128)(2,1)S(1)}, bf16[4,8,48,128]{3,2,1,0:T(8,128)(2,1)S(1)}, u32[]{:S(2)}, u32[]{:S(2)}) collective-permute-start(bf16[4,8,48,128]{3,2,1,0:T(8,128)(2,1)S(1)} %get-tuple-element.55), channel_id=1, source_target_pairs={{0,4},{4,0},{8,12},{12,8},{1,5},{5,1},{9,13},{13,9},{2,6},{6,2},{1... | collective-permute-start | bytes 1179656 | tf_op jit(solution)/shard_map/ppermute | solution.py:327
  34.1 2.1 %shard_map.62.refs_0_ = f32[8,8,48,128]{3,2,1,0:T(8,128)S(1)} custom-call(f32[8,8,64,128]{3,2,1,0:T(8,128)S(1)} %get-tuple-element.63.refs_0_.refs_5_, bf16[8,4,48,128]{3,2,1,0:T(8,128)(2,1)S(1)} %collective-permute-done.14.refs_1_, bf16[8,8,48,256]{3,2,1,0:T(8,128)(2,1)S(1)} %copy-done.1, f32[128,128]{1,0:T(8,128)S(1)} %get-tuple-element.48.refs_3_.c_ref, ...), custom_call_target="tpu_custom_call" | custom-call | flops 1 | bytes 1 | tf_op jit(solution)/shard_map/pallas_call | solution.py:203
  39.2 3.4 %collective-permute-start.19 = (bf16[4,8,48,128]{3,2,1,0:T(8,128)(2,1)S(1)}, bf16[4,8,48,128]{3,2,1,0:T(8,128)(2,1)S(1)}, u32[]{:S(2)}, u32[]{:S(2)}) collective-permute-start(bf16[4,8,48,128]{3,2,1,0:T(8,128)(2,1)S(1)} %get-tuple-element.70), channel_id=1, source_target_pairs={{0,4},{4,0},{8,12},{12,8},{1,5},{5,1},{9,13},{13,9},{2,6},{6,2},{1... | collective-permute-start | bytes 1179656 | tf_op jit(solution)/shard_map/ppermute | solution.py:327
  42.6 2.1 %shard_map.55.refs_0_ = f32[8,8,48,128]{3,2,1,0:T(8,128)S(1)} custom-call(f32[8,8,64,128]{3,2,1,0:T(8,128)S(1)} %get-tuple-element.52.refs_0_.refs_5_, bf16[8,4,48,128]{3,2,1,0:T(8,128)(2,1)S(1)} %collective-permute-done.3.refs_1_, bf16[8,8,48,256]{3,2,1,0:T(8,128)(2,1)S(1)} %copy-done.1, f32[128,128]{1,0:T(8,128)S(1)} %get-tuple-element.48.refs_3_.c_ref, ...), custom_call_target="tpu_custom_call" | custom-call | flops 1 | bytes 1 | tf_op jit(solution)/shard_map/pallas_call | solution.py:203
  47.6 3.4 %collective-permute-start.8 = (bf16[4,8,48,128]{3,2,1,0:T(8,128)(2,1)S(1)}, bf16[4,8,48,128]{3,2,1,0:T(8,128)(2,1)S(1)}, u32[]{:S(2)}, u32[]{:S(2)}) collective-permute-start(bf16[4,8,48,128]{3,2,1,0:T(8,128)(2,1)S(1)} %get-tuple-element.59), channel_id=1, source_target_pairs={{0,4},{4,0},{8,12},{12,8},{1,5},{5,1},{9,13},{13,9},{2,6},{6,2},{1... | collective-permute-start | bytes 1179656 | tf_op jit(solution)/shard_map/ppermute | solution.py:327
  51.0 2.1 %shard_map.64.refs_0_ = f32[8,8,48,128]{3,2,1,0:T(8,128)S(1)} custom-call(f32[8,8,64,128]{3,2,1,0:T(8,128)S(1)} %get-tuple-element.67.refs_0_, bf16[8,4,48,128]{3,2,1,0:T(8,128)(2,1)S(1)} %collective-permute-done.17.refs_1_, bf16[8,8,48,256]{3,2,1,0:T(8,128)(2,1)S(1)} %copy-done.1, f32[128,128]{1,0:T(8,128)S(1)} %get-tuple-element.48.refs_3_.c_ref, ...), custom_call_target="tpu_custom_call" | custom-call | flops 1 | bytes 1 | tf_op jit(solution)/shard_map/pallas_call | solution.py:203
  55.1 1.6 %collective-permute-start.20 = (bf16[4,8,48,128]{3,2,1,0:T(8,128)(2,1)S(1)}, bf16[4,8,48,128]{3,2,1,0:T(8,128)(2,1)S(1)}, u32[]{:S(2)}, u32[]{:S(2)}) collective-permute-start(bf16[4,8,48,128]{3,2,1,0:T(8,128)(2,1)S(1)} %get-tuple-element.71.refs_4_), channel_id=1, source_target_pairs={{0,2},{2,0},{1,3},{3,1},{4,6},{6,4},{5,7},{7,5},{8,10},{10,8},{9,1... | collective-permute-start | bytes 1179656 | tf_op jit(solution)/shard_map/ppermute | solution.py:327
  56.7 2.1 %shard_map.57.base_ref = f32[8,8,48,128]{3,2,1,0:T(8,128)S(1)} custom-call(f32[8,8,64,128]{3,2,1,0:T(8,128)S(1)} %get-tuple-element.56.refs_0_, bf16[8,4,48,128]{3,2,1,0:T(8,128)(2,1)S(1)} %collective-permute-done.6.refs_1_, bf16[8,8,48,256]{3,2,1,0:T(8,128)(2,1)S(1)} %copy-done.1, f32[128,128]{1,0:T(8,128)S(1)} %get-tuple-element.48.refs_3_.c_ref, ...), custom_call_target="tpu_custom_call" | custom-call | flops 1 | bytes 1 | tf_op jit(solution)/shard_map/pallas_call | solution.py:203
  58.8 3.5 %collective-permute-done.8.even_ref = bf16[4,8,48,128]{3,2,1,0:T(8,128)(2,1)S(1)} collective-permute-done((bf16[4,8,48,128]{3,2,1,0:T(8,128)(2,1)S(1)}, bf16[4,8,48,128]{3,2,1,0:T(8,128)(2,1)S(1)}, u32[]{:S(2)}, u32[]{:S(2)}) %collective-permute-start.8) | collective-permute-done | bytes 393248 | tf_op jit(solution)/shard_map/ppermute | solution.py:327
  62.7 1.6 %collective-permute-start.9 = (bf16[2,8,48,128]{3,2,1,0:T(8,128)(2,1)S(1)}, bf16[2,8,48,128]{3,2,1,0:T(8,128)(2,1)S(1)}, u32[]{:S(2)}, u32[]{:S(2)}) collective-permute-start(bf16[2,8,48,128]{3,2,1,0:T(8,128)(2,1)S(1)} %shard_map.58.refs_1_), channel_id=1, source_target_pairs={{0,2},{2,0},{1,3},{3,1},{4,6},{6,4},{5,7},{7,5},{8,10},{10,8},{9,1... | collective-permute-start | bytes 589832 | tf_op jit(solution)/shard_map/ppermute | solution.py:327
  67.9 1.8 %collective-permute-start.22 = (bf16[128,128]{1,0:T(8,128)(2,1)S(1)}, bf16[128,128]{1,0:T(8,128)(2,1)S(1)}, u32[]{:S(2)}, u32[]{:S(2)}) collective-permute-start(bf16[128,128]{1,0:T(8,128)(2,1)S(1)} %get-tuple-element.77), channel_id=1, source_target_pairs={{0,4},{4,0},{8,12},{12,8},{1,5},{5,1},{9,13},{13,9},{2,6},{6,2},{1... | collective-permute-start | bytes 98312 | tf_op jit(solution)/shard_map/ppermute | solution.py:621
  70.2 1.7 %collective-permute-done.22.refs_4_.inner_got_ref = bf16[128,128]{1,0:T(8,128)(2,1)S(1)} collective-permute-done((bf16[128,128]{1,0:T(8,128)(2,1)S(1)}, bf16[128,128]{1,0:T(8,128)(2,1)S(1)}, u32[]{:S(2)}, u32[]{:S(2)}) %collective-permute-start.22) | collective-permute-done | bytes 32800 | tf_op jit(solution)/shard_map/ppermute | solution.py:621
  71.8 2.1 %collective-permute-done.10.refs_1_ = bf16[2,8,48,128]{3,2,1,0:T(8,128)(2,1)S(1)} collective-permute-done((bf16[2,8,48,128]{3,2,1,0:T(8,128)(2,1)S(1)}, bf16[2,8,48,128]{3,2,1,0:T(8,128)(2,1)S(1)}, u32[]{:S(2)}, u32[]{:S(2)}) %collective-permute-start.10) | collective-permute-done | bytes 196640 | tf_op jit(solution)/shard_map/ppermute | solution.py:327
  75.9 1.6 %collective-permute-start.24 = (bf16[272,128]{1,0:T(8,128)(2,1)S(1)}, bf16[272,128]{1,0:T(8,128)(2,1)S(1)}, u32[]{:S(2)}, u32[]{:S(2)}) collective-permute-start(bf16[272,128]{1,0:T(8,128)(2,1)S(1)} %get-tuple-element.83), channel_id=1, source_target_pairs={{0,8},{4,12},{8,0},{12,4},{1,9},{5,13},{9,1},{13,5},{2,10},{6,14},... | collective-permute-start | bytes 208904 | tf_op jit(solution)/shard_map/ppermute | solution.py:626
  77.5 2.2 %collective-permute-start.25 = (bf16[144,128]{1,0:T(8,128)(2,1)S(1)}, bf16[144,128]{1,0:T(8,128)(2,1)S(1)}, u32[]{:S(2)}, u32[]{:S(2)}) collective-permute-start(bf16[144,128]{1,0:T(8,128)(2,1)S(1)} %get-tuple-element.84), channel_id=1, source_target_pairs={{0,12},{4,8},{8,4},{12,0},{1,13},{5,9},{9,5},{13,1},{2,14},{6,10},... | collective-permute-start | bytes 110600 | tf_op jit(solution)/shard_map/ppermute | solution.py:626
  79.7 3.6 %collective-permute-done.25.refs_1_ = bf16[144,128]{1,0:T(8,128)(2,1)S(1)} collective-permute-done((bf16[144,128]{1,0:T(8,128)(2,1)S(1)}, bf16[144,128]{1,0:T(8,128)(2,1)S(1)}, u32[]{:S(2)}, u32[]{:S(2)}) %collective-permute-start.25) | collective-permute-done | bytes 36896 | tf_op jit(solution)/shard_map/ppermute | solution.py:626
  84.1 1.6 %collective-permute-start.27 = (bf16[272,128]{1,0:T(8,128)(2,1)S(1)}, bf16[272,128]{1,0:T(8,128)(2,1)S(1)}, u32[]{:S(2)}, u32[]{:S(2)}) collective-permute-start(bf16[272,128]{1,0:T(8,128)(2,1)S(1)} %shard_map.72.mine_ref), channel_id=1, source_target_pairs={{0,2},{2,0},{1,3},{3,1},{4,6},{6,4},{5,7},{7,5},{8,10},{10,8},{9,1... | collective-permute-start | bytes 208904 | tf_op jit(solution)/shard_map/ppermute | solution.py:327
  85.7 2.8 %collective-permute-done.27.other_ref = bf16[272,128]{1,0:T(8,128)(2,1)S(1)} collective-permute-done((bf16[272,128]{1,0:T(8,128)(2,1)S(1)}, bf16[272,128]{1,0:T(8,128)(2,1)S(1)}, u32[]{:S(2)}, u32[]{:S(2)}) %collective-permute-start.27) | collective-permute-done | bytes 69664 | tf_op jit(solution)/shard_map/ppermute | solution.py:327
  (67 shorter events, 28.3 us)
Async XLA Ops:
  4.0 8.5 %collective-permute-start.11 = (bf16[8,4,48,128]{3,2,1,0:T(8,128)(2,1)S(1)}, bf16[8,4,48,128]{3,2,1,0:T(8,128)(2,1)S(1)}, u32[]{:S(2)}, u32[]{:S(2)}) collective-permute-start(bf16[8,4,48,128]{3,2,1,0:T(8,128)(2,1)S(1)} %get-tuple-element.60), channel_id=1, source_target_pairs={{0,1},{1,0},{2,3},{3,2},{4,5},{5,4},{6,7},{7,6},{8,9},{9,8},{10,11... | collective-permute-start | bytes 1179656 | tf_op jit(solution)/shard_map/ppermute | solution.py:327
  4.5 12.2 %collective-permute-start.12 = (bf16[4,8,48,128]{3,2,1,0:T(8,128)(2,1)S(1)}, bf16[4,8,48,128]{3,2,1,0:T(8,128)(2,1)S(1)}, u32[]{:S(2)}, u32[]{:S(2)}) collective-permute-start(bf16[4,8,48,128]{3,2,1,0:T(8,128)(2,1)S(1)} %get-tuple-element.61), channel_id=1, source_target_pairs={{4,8},{8,4},{5,9},{9,5},{6,10},{10,6},{7,11},{11,7},{20,24},{24,20... | collective-permute-start | bytes 1179656 | tf_op jit(solution)/shard_map/ppermute | solution.py:327
  5.2 15.4 %collective-permute-start.13 = (bf16[4,8,48,128]{3,2,1,0:T(8,128)(2,1)S(1)}, bf16[4,8,48,128]{3,2,1,0:T(8,128)(2,1)S(1)}, u32[]{:S(2)}, u32[]{:S(2)}) collective-permute-start(bf16[4,8,48,128]{3,2,1,0:T(8,128)(2,1)S(1)} %get-tuple-element.62), channel_id=1, source_target_pairs={{0,4},{4,0},{8,12},{12,8},{1,5},{5,1},{9,13},{13,9},{2,6},{6,2},{1... | collective-permute-start | bytes 1179656 | tf_op jit(solution)/shard_map/ppermute | solution.py:327
  11.7 10.6 %collective-permute-start = (bf16[8,4,48,128]{3,2,1,0:T(8,128)(2,1)S(1)}, bf16[8,4,48,128]{3,2,1,0:T(8,128)(2,1)S(1)}, u32[]{:S(2)}, u32[]{:S(2)}) collective-permute-start(bf16[8,4,48,128]{3,2,1,0:T(8,128)(2,1)S(1)} %get-tuple-element.46), channel_id=1, source_target_pairs={{0,1},{1,0},{2,3},{3,2},{4,5},{5,4},{6,7},{7,6},{8,9},{9,8},{10,11... | collective-permute-start | bytes 1179656 | tf_op jit(solution)/shard_map/ppermute | solution.py:327
  11.8 16.4 %collective-permute-start.1 = (bf16[4,8,48,128]{3,2,1,0:T(8,128)(2,1)S(1)}, bf16[4,8,48,128]{3,2,1,0:T(8,128)(2,1)S(1)}, u32[]{:S(2)}, u32[]{:S(2)}) collective-permute-start(bf16[4,8,48,128]{3,2,1,0:T(8,128)(2,1)S(1)} %get-tuple-element.50), channel_id=1, source_target_pairs={{4,8},{8,4},{5,9},{9,5},{6,10},{10,6},{7,11},{11,7},{20,24},{24,20... | collective-permute-start | bytes 1179656 | tf_op jit(solution)/shard_map/ppermute | solution.py:327
  12.5 16.5 %collective-permute-start.2 = (bf16[4,8,48,128]{3,2,1,0:T(8,128)(2,1)S(1)}, bf16[4,8,48,128]{3,2,1,0:T(8,128)(2,1)S(1)}, u32[]{:S(2)}, u32[]{:S(2)}) collective-permute-start(bf16[4,8,48,128]{3,2,1,0:T(8,128)(2,1)S(1)} %get-tuple-element.51), channel_id=1, source_target_pairs={{0,4},{4,0},{8,12},{12,8},{1,5},{5,1},{9,13},{13,9},{2,6},{6,2},{1... | collective-permute-start | bytes 1179656 | tf_op jit(solution)/shard_map/ppermute | solution.py:327
  21.6 9.2 %collective-permute-start.14 = (bf16[8,4,48,128]{3,2,1,0:T(8,128)(2,1)S(1)}, bf16[8,4,48,128]{3,2,1,0:T(8,128)(2,1)S(1)}, u32[]{:S(2)}, u32[]{:S(2)}) collective-permute-start(bf16[8,4,48,128]{3,2,1,0:T(8,128)(2,1)S(1)} %get-tuple-element.64), channel_id=1, source_target_pairs={{0,1},{1,0},{2,3},{3,2},{4,5},{5,4},{6,7},{7,6},{8,9},{9,8},{10,11... | collective-permute-start | bytes 1179656 | tf_op jit(solution)/shard_map/ppermute | solution.py:327
  21.6 14.7 %collective-permute-start.15 = (bf16[4,8,48,128]{3,2,1,0:T(8,128)(2,1)S(1)}, bf16[4,8,48,128]{3,2,1,0:T(8,128)(2,1)S(1)}, u32[]{:S(2)}, u32[]{:S(2)}) collective-permute-start(bf16[4,8,48,128]{3,2,1,0:T(8,128)(2,1)S(1)} %get-tuple-element.65), channel_id=1, source_target_pairs={{4,8},{8,4},{5,9},{9,5},{6,10},{10,6},{7,11},{11,7},{20,24},{24,20... | collective-permute-start | bytes 1179656 | tf_op jit(solution)/shard_map/ppermute | solution.py:327
  22.4 15.1 %collective-permute-start.16 = (bf16[4,8,48,128]{3,2,1,0:T(8,128)(2,1)S(1)}, bf16[4,8,48,128]{3,2,1,0:T(8,128)(2,1)S(1)}, u32[]{:S(2)}, u32[]{:S(2)}) collective-permute-start(bf16[4,8,48,128]{3,2,1,0:T(8,128)(2,1)S(1)} %get-tuple-element.66), channel_id=1, source_target_pairs={{0,4},{4,0},{8,12},{12,8},{1,5},{5,1},{9,13},{13,9},{2,6},{6,2},{1... | collective-permute-start | bytes 1179656 | tf_op jit(solution)/shard_map/ppermute | solution.py:327
  30.0 9.2 %collective-permute-start.3 = (bf16[8,4,48,128]{3,2,1,0:T(8,128)(2,1)S(1)}, bf16[8,4,48,128]{3,2,1,0:T(8,128)(2,1)S(1)}, u32[]{:S(2)}, u32[]{:S(2)}) collective-permute-start(bf16[8,4,48,128]{3,2,1,0:T(8,128)(2,1)S(1)} %get-tuple-element.53), channel_id=1, source_target_pairs={{0,1},{1,0},{2,3},{3,2},{4,5},{5,4},{6,7},{7,6},{8,9},{9,8},{10,11... | collective-permute-start | bytes 1179656 | tf_op jit(solution)/shard_map/ppermute | solution.py:327
  30.1 14.6 %collective-permute-start.4 = (bf16[4,8,48,128]{3,2,1,0:T(8,128)(2,1)S(1)}, bf16[4,8,48,128]{3,2,1,0:T(8,128)(2,1)S(1)}, u32[]{:S(2)}, u32[]{:S(2)}) collective-permute-start(bf16[4,8,48,128]{3,2,1,0:T(8,128)(2,1)S(1)} %get-tuple-element.54), channel_id=1, source_target_pairs={{4,8},{8,4},{5,9},{9,5},{6,10},{10,6},{7,11},{11,7},{20,24},{24,20... | collective-permute-start | bytes 1179656 | tf_op jit(solution)/shard_map/ppermute | solution.py:327
  30.8 15.1 %collective-permute-start.5 = (bf16[4,8,48,128]{3,2,1,0:T(8,128)(2,1)S(1)}, bf16[4,8,48,128]{3,2,1,0:T(8,128)(2,1)S(1)}, u32[]{:S(2)}, u32[]{:S(2)}) collective-permute-start(bf16[4,8,48,128]{3,2,1,0:T(8,128)(2,1)S(1)} %get-tuple-element.55), channel_id=1, source_target_pairs={{0,4},{4,0},{8,12},{12,8},{1,5},{5,1},{9,13},{13,9},{2,6},{6,2},{1... | collective-permute-start | bytes 1179656 | tf_op jit(solution)/shard_map/ppermute | solution.py:327
  38.4 9.2 %collective-permute-start.17 = (bf16[8,4,48,128]{3,2,1,0:T(8,128)(2,1)S(1)}, bf16[8,4,48,128]{3,2,1,0:T(8,128)(2,1)S(1)}, u32[]{:S(2)}, u32[]{:S(2)}) collective-permute-start(bf16[8,4,48,128]{3,2,1,0:T(8,128)(2,1)S(1)} %get-tuple-element.68), channel_id=1, source_target_pairs={{0,1},{1,0},{2,3},{3,2},{4,5},{5,4},{6,7},{7,6},{8,9},{9,8},{10,11... | collective-permute-start | bytes 1179656 | tf_op jit(solution)/shard_map/ppermute | solution.py:327
  38.5 14.7 %collective-permute-start.18 = (bf16[4,8,48,128]{3,2,1,0:T(8,128)(2,1)S(1)}, bf16[4,8,48,128]{3,2,1,0:T(8,128)(2,1)S(1)}, u32[]{:S(2)}, u32[]{:S(2)}) collective-permute-start(bf16[4,8,48,128]{3,2,1,0:T(8,128)(2,1)S(1)} %get-tuple-element.69), channel_id=1, source_target_pairs={{4,8},{8,4},{5,9},{9,5},{6,10},{10,6},{7,11},{11,7},{20,24},{24,20... | collective-permute-start | bytes 1179656 | tf_op jit(solution)/shard_map/ppermute | solution.py:327
  39.2 15.1 %collective-permute-start.19 = (bf16[4,8,48,128]{3,2,1,0:T(8,128)(2,1)S(1)}, bf16[4,8,48,128]{3,2,1,0:T(8,128)(2,1)S(1)}, u32[]{:S(2)}, u32[]{:S(2)}) collective-permute-start(bf16[4,8,48,128]{3,2,1,0:T(8,128)(2,1)S(1)} %get-tuple-element.70), channel_id=1, source_target_pairs={{0,4},{4,0},{8,12},{12,8},{1,5},{5,1},{9,13},{13,9},{2,6},{6,2},{1... | collective-permute-start | bytes 1179656 | tf_op jit(solution)/shard_map/ppermute | solution.py:327
  46.8 9.8 %collective-permute-start.6 = (bf16[8,4,48,128]{3,2,1,0:T(8,128)(2,1)S(1)}, bf16[8,4,48,128]{3,2,1,0:T(8,128)(2,1)S(1)}, u32[]{:S(2)}, u32[]{:S(2)}) collective-permute-start(bf16[8,4,48,128]{3,2,1,0:T(8,128)(2,1)S(1)} %get-tuple-element.57), channel_id=1, source_target_pairs={{0,1},{1,0},{2,3},{3,2},{4,5},{5,4},{6,7},{7,6},{8,9},{9,8},{10,11... | collective-permute-start | bytes 1179656 | tf_op jit(solution)/shard_map/ppermute | solution.py:327
  46.9 11.9 %collective-permute-start.7 = (bf16[4,8,48,128]{3,2,1,0:T(8,128)(2,1)S(1)}, bf16[4,8,48,128]{3,2,1,0:T(8,128)(2,1)S(1)}, u32[]{:S(2)}, u32[]{:S(2)}) collective-permute-start(bf16[4,8,48,128]{3,2,1,0:T(8,128)(2,1)S(1)} %get-tuple-element.58), channel_id=1, source_target_pairs={{4,8},{8,4},{5,9},{9,5},{6,10},{10,6},{7,11},{11,7},{20,24},{24,20... | collective-permute-start | bytes 1179656 | tf_op jit(solution)/shard_map/ppermute | solution.py:327
  47.6 14.7 %collective-permute-start.8 = (bf16[4,8,48,128]{3,2,1,0:T(8,128)(2,1)S(1)}, bf16[4,8,48,128]{3,2,1,0:T(8,128)(2,1)S(1)}, u32[]{:S(2)}, u32[]{:S(2)}) collective-permute-start(bf16[4,8,48,128]{3,2,1,0:T(8,128)(2,1)S(1)} %get-tuple-element.59), channel_id=1, source_target_pairs={{0,4},{4,0},{8,12},{12,8},{1,5},{5,1},{9,13},{13,9},{2,6},{6,2},{1... | collective-permute-start | bytes 1179656 | tf_op jit(solution)/shard_map/ppermute | solution.py:327
  55.1 14.5 %collective-permute-start.20 = (bf16[4,8,48,128]{3,2,1,0:T(8,128)(2,1)S(1)}, bf16[4,8,48,128]{3,2,1,0:T(8,128)(2,1)S(1)}, u32[]{:S(2)}, u32[]{:S(2)}) collective-permute-start(bf16[4,8,48,128]{3,2,1,0:T(8,128)(2,1)S(1)} %get-tuple-element.71.refs_4_), channel_id=1, source_target_pairs={{0,2},{2,0},{1,3},{3,1},{4,6},{6,4},{5,7},{7,5},{8,10},{10,8},{9,1... | collective-permute-start | bytes 1179656 | tf_op jit(solution)/shard_map/ppermute | solution.py:327
  62.7 9.2 %collective-permute-start.9 = (bf16[2,8,48,128]{3,2,1,0:T(8,128)(2,1)S(1)}, bf16[2,8,48,128]{3,2,1,0:T(8,128)(2,1)S(1)}, u32[]{:S(2)}, u32[]{:S(2)}) collective-permute-start(bf16[2,8,48,128]{3,2,1,0:T(8,128)(2,1)S(1)} %shard_map.58.refs_1_), channel_id=1, source_target_pairs={{0,2},{2,0},{1,3},{3,1},{4,6},{6,4},{5,7},{7,5},{8,10},{10,8},{9,1... | collective-permute-start | bytes 589832 | tf_op jit(solution)/shard_map/ppermute | solution.py:327
  64.6 9.3 %collective-permute-start.10 = (bf16[2,8,48,128]{3,2,1,0:T(8,128)(2,1)S(1)}, bf16[2,8,48,128]{3,2,1,0:T(8,128)(2,1)S(1)}, u32[]{:S(2)}, u32[]{:S(2)}) collective-permute-start(bf16[2,8,48,128]{3,2,1,0:T(8,128)(2,1)S(1)} %shard_map.59.refs_2_), channel_id=1, source_target_pairs={{0,2},{2,0},{1,3},{3,1},{4,6},{6,4},{5,7},{7,5},{8,10},{10,8},{9,1... | collective-permute-start | bytes 589832 | tf_op jit(solution)/shard_map/ppermute | solution.py:327
  75.9 8.2 %collective-permute-start.24 = (bf16[272,128]{1,0:T(8,128)(2,1)S(1)}, bf16[272,128]{1,0:T(8,128)(2,1)S(1)}, u32[]{:S(2)}, u32[]{:S(2)}) collective-permute-start(bf16[272,128]{1,0:T(8,128)(2,1)S(1)} %get-tuple-element.83), channel_id=1, source_target_pairs={{0,8},{4,12},{8,0},{12,4},{1,9},{5,13},{9,1},{13,5},{2,10},{6,14},... | collective-permute-start | bytes 208904 | tf_op jit(solution)/shard_map/ppermute | solution.py:626
  77.5 5.9 %collective-permute-start.25 = (bf16[144,128]{1,0:T(8,128)(2,1)S(1)}, bf16[144,128]{1,0:T(8,128)(2,1)S(1)}, u32[]{:S(2)}, u32[]{:S(2)}) collective-permute-start(bf16[144,128]{1,0:T(8,128)(2,1)S(1)} %get-tuple-element.84), channel_id=1, source_target_pairs={{0,12},{4,8},{8,4},{12,0},{1,13},{5,9},{9,5},{13,1},{2,14},{6,10},... | collective-permute-start | bytes 110600 | tf_op jit(solution)/shard_map/ppermute | solution.py:626
  79.7 4.4 %collective-permute-start.26 = (bf16[144,128]{1,0:T(8,128)(2,1)S(1)}, bf16[144,128]{1,0:T(8,128)(2,1)S(1)}, u32[]{:S(2)}, u32[]{:S(2)}) collective-permute-start(bf16[144,128]{1,0:T(8,128)(2,1)S(1)} %get-tuple-element.85), channel_id=1, source_target_pairs={{0,4},{4,0},{8,12},{12,8},{1,5},{5,1},{9,13},{13,9},{2,6},{6,2},{1... | collective-permute-start | bytes 110600 | tf_op jit(solution)/shard_map/ppermute | solution.py:626
  (9 other events, 35.9 us)

commit v24 on v22

--- a/solution.py
+++ b/solution.py
@@ -679,14 +679,12 @@
                 previous[c], now[c] = now[c], u
                 halos[c] = exchange(*edges)
             elif paired:
-                if c > 0:
-                    kept, *sent = rim_step(base, odd, even, courant, "half")
-                else:
-                    sent = [
-                        part_step(base, odd, even, courant, True, begin, RADIUS // 2)
-                        for begin in (0, RADIUS // 2)
-                    ]
-                    kept = part_step(base, odd, even, courant, False)
+                count = RADIUS if c > 0 else RADIUS // 2
+                sent = [
+                    part_step(base, odd, even, courant, True, begin, count)
+                    for begin in range(0, RADIUS, count)
+                ]
+                kept = part_step(base, odd, even, courant, False)
                 finals.append(([kept], sent, [chip_swap(a) for a in sent]))
             else:
                 finals += rim_step(base, odd, even, courant, "all")

time: 91.3 us -> 91 us (level)
    pallas_call x3 -> x5, Pallas kernels: 1.25 us -> 2.32 us  [part_step(): call(functools.partial(part_body, sent, begin), in_specs=whole_vmem(4), o...]
    pallas_call x5 -> x4, Pallas kernels: 4.81 us -> 3.96 us  [rim_step(): call(functools.partial(rim_body, kind), in_specs=whole_vmem(4), out_specs...]
  transfers between devices with their start and end apart: 29 -> 29, of which waited for: 14 -> 14; matrix products, arithmetic and copies ran while one was open for 0% -> 0% of each run, Pallas kernels for 23% -> 24%
where the time goes in v24:
time: 91 us; the launch traced here: 90.7 us
  starting transfers between devices  37.3 us (41%)
  waiting for transfers between devices  26.1 us (29%)
  Pallas kernels  24.1 us (26%)
  local copies, waits for them, and re-layouts  2.18 us (2%)
  between operations  1 us (1%)
    ppermute x25, starting transfers between devices, swap(): lax.ppermute(x, axis, [p for a, b in pairs for p in ((a, b), (b, a))])  31.6 us
    ppermute x25, waiting for transfers between devices, swap(): lax.ppermute(x, axis, [p for a, b in pairs for p in ((a, b), (b, a))])  20 us
    pallas_call x6, Pallas kernels, local_step(): call(functools.partial(local_body, chunk, moment, previous is not None),...  12.7 us
    ppermute x3, waiting for transfers between devices, coupled(): lax.ppermute(blocks[d - 1], 'slab', [(i, i ^ d) for i in range(slabs)])  4.38 us
    pallas_call x4, Pallas kernels, rim_step(): call(functools.partial(rim_body, kind), in_specs=whole_vmem(4), out_specs...  3.96 us
    ppermute x3, starting transfers between devices, coupled(): lax.ppermute(blocks[d - 1], 'slab', [(i, i ^ d) for i in range(slabs)])  3.85 us
    pallas_call x5, Pallas kernels, part_step(): call(functools.partial(part_body, sent, begin), in_specs=whole_vmem(4), o...  2.32 us
    pallas_call x2, Pallas kernels, first_field(): call(functools.partial(first_body, chunk), in_specs=whole_vmem(2), out_sp...  2.1 us
  transfers between devices with their start and end apart: 29, of which 14 were waited for; matrix products, arithmetic and copies ran while one was open for 0% of the time, Pallas kernels for 24%

profile of v24, /device:TPU:0, one launch (start us, length us, event | category | flops | bytes accessed | tf_op | source)
XLA Modules:
  0.0 90.7 jit_solution(12915287163701692638)
XLA Ops:
  5.1 5.5 %collective-permute-start.13 = (bf16[4,8,48,128]{3,2,1,0:T(8,128)(2,1)S(1)}, bf16[4,8,48,128]{3,2,1,0:T(8,128)(2,1)S(1)}, u32[]{:S(2)}, u32[]{:S(2)}) collective-permute-start(bf16[4,8,48,128]{3,2,1,0:T(8,128)(2,1)S(1)} %get-tuple-element.60), channel_id=1, source_target_pairs={{0,4},{4,0},{8,12},{12,8},{1,5},{5,1},{9,13},{13,9},{2,6},{6,2},{1... | collective-permute-start | bytes 1179656 | tf_op jit(solution)/shard_map/ppermute | solution.py:326
  12.4 1.9 %collective-permute-start.2 = (bf16[4,8,48,128]{3,2,1,0:T(8,128)(2,1)S(1)}, bf16[4,8,48,128]{3,2,1,0:T(8,128)(2,1)S(1)}, u32[]{:S(2)}, u32[]{:S(2)}) collective-permute-start(bf16[4,8,48,128]{3,2,1,0:T(8,128)(2,1)S(1)} %get-tuple-element.49), channel_id=1, source_target_pairs={{0,4},{4,0},{8,12},{12,8},{1,5},{5,1},{9,13},{13,9},{2,6},{6,2},{1... | collective-permute-start | bytes 1179656 | tf_op jit(solution)/shard_map/ppermute | solution.py:326
  14.5 2.1 %shard_map.60.refs_0_ = f32[8,8,48,128]{3,2,1,0:T(8,128)S(1)} custom-call(f32[8,8,64,128]{3,2,1,0:T(8,128)S(1)} %get-tuple-element.45._.refs_0_.refs_5_, bf16[8,4,48,128]{3,2,1,0:T(8,128)(2,1)S(1)} %collective-permute-done.11.refs_1_, bf16[8,8,48,256]{3,2,1,0:T(8,128)(2,1)S(1)} %copy-done.1, f32[128,128]{1,0:T(8,128)S(1)} %get-tuple-element.46.refs_3_.c_ref, ...), custom_call_target="tpu_custom_call" | custom-call | flops 1 | bytes 1 | tf_op jit(solution)/shard_map/pallas_call | solution.py:202
  16.6 3.9 %collective-permute-done.13.refs_2_ = bf16[4,8,48,128]{3,2,1,0:T(8,128)(2,1)S(1)} collective-permute-done((bf16[4,8,48,128]{3,2,1,0:T(8,128)(2,1)S(1)}, bf16[4,8,48,128]{3,2,1,0:T(8,128)(2,1)S(1)}, u32[]{:S(2)}, u32[]{:S(2)}) %collective-permute-start.13) | collective-permute-done | bytes 393248 | tf_op jit(solution)/shard_map/ppermute | solution.py:326
  22.2 3.8 %collective-permute-start.16 = (bf16[4,8,48,128]{3,2,1,0:T(8,128)(2,1)S(1)}, bf16[4,8,48,128]{3,2,1,0:T(8,128)(2,1)S(1)}, u32[]{:S(2)}, u32[]{:S(2)}) collective-permute-start(bf16[4,8,48,128]{3,2,1,0:T(8,128)(2,1)S(1)} %get-tuple-element.64), channel_id=1, source_target_pairs={{0,4},{4,0},{8,12},{12,8},{1,5},{5,1},{9,13},{13,9},{2,6},{6,2},{1... | collective-permute-start | bytes 1179656 | tf_op jit(solution)/shard_map/ppermute | solution.py:326
  26.0 2.0 %shard_map.53.refs_0_ = f32[8,8,48,128]{3,2,1,0:T(8,128)S(1)} custom-call(f32[8,8,64,128]{3,2,1,0:T(8,128)S(1)} %get-tuple-element.43.refs_0_.refs_5_, bf16[8,4,48,128]{3,2,1,0:T(8,128)(2,1)S(1)} %collective-permute-done.refs_1_, bf16[8,8,48,256]{3,2,1,0:T(8,128)(2,1)S(1)} %copy-done.1, f32[128,128]{1,0:T(8,128)S(1)} %get-tuple-element.46.refs_3_.c_ref, ...), custom_call_target="tpu_custom_call" | custom-call | flops 1 | bytes 1 | tf_op jit(solution)/shard_map/pallas_call | solution.py:202
  30.6 3.4 %collective-permute-start.5 = (bf16[4,8,48,128]{3,2,1,0:T(8,128)(2,1)S(1)}, bf16[4,8,48,128]{3,2,1,0:T(8,128)(2,1)S(1)}, u32[]{:S(2)}, u32[]{:S(2)}) collective-permute-start(bf16[4,8,48,128]{3,2,1,0:T(8,128)(2,1)S(1)} %get-tuple-element.53), channel_id=1, source_target_pairs={{0,4},{4,0},{8,12},{12,8},{1,5},{5,1},{9,13},{13,9},{2,6},{6,2},{1... | collective-permute-start | bytes 1179656 | tf_op jit(solution)/shard_map/ppermute | solution.py:326
  34.0 2.1 %shard_map.62.refs_0_ = f32[8,8,48,128]{3,2,1,0:T(8,128)S(1)} custom-call(f32[8,8,64,128]{3,2,1,0:T(8,128)S(1)} %get-tuple-element.61.refs_0_.refs_5_, bf16[8,4,48,128]{3,2,1,0:T(8,128)(2,1)S(1)} %collective-permute-done.14.refs_1_, bf16[8,8,48,256]{3,2,1,0:T(8,128)(2,1)S(1)} %copy-done.1, f32[128,128]{1,0:T(8,128)S(1)} %get-tuple-element.46.refs_3_.c_ref, ...), custom_call_target="tpu_custom_call" | custom-call | flops 1 | bytes 1 | tf_op jit(solution)/shard_map/pallas_call | solution.py:202
  39.1 3.4 %collective-permute-start.19 = (bf16[4,8,48,128]{3,2,1,0:T(8,128)(2,1)S(1)}, bf16[4,8,48,128]{3,2,1,0:T(8,128)(2,1)S(1)}, u32[]{:S(2)}, u32[]{:S(2)}) collective-permute-start(bf16[4,8,48,128]{3,2,1,0:T(8,128)(2,1)S(1)} %get-tuple-element.68), channel_id=1, source_target_pairs={{0,4},{4,0},{8,12},{12,8},{1,5},{5,1},{9,13},{13,9},{2,6},{6,2},{1... | collective-permute-start | bytes 1179656 | tf_op jit(solution)/shard_map/ppermute | solution.py:326
  42.4 2.1 %shard_map.55.refs_0_ = f32[8,8,48,128]{3,2,1,0:T(8,128)S(1)} custom-call(f32[8,8,64,128]{3,2,1,0:T(8,128)S(1)} %get-tuple-element.50.refs_0_.refs_5_, bf16[8,4,48,128]{3,2,1,0:T(8,128)(2,1)S(1)} %collective-permute-done.3.refs_1_, bf16[8,8,48,256]{3,2,1,0:T(8,128)(2,1)S(1)} %copy-done.1, f32[128,128]{1,0:T(8,128)S(1)} %get-tuple-element.46.refs_3_.c_ref, ...), custom_call_target="tpu_custom_call" | custom-call | flops 1 | bytes 1 | tf_op jit(solution)/shard_map/pallas_call | solution.py:202
  47.5 3.4 %collective-permute-start.8 = (bf16[4,8,48,128]{3,2,1,0:T(8,128)(2,1)S(1)}, bf16[4,8,48,128]{3,2,1,0:T(8,128)(2,1)S(1)}, u32[]{:S(2)}, u32[]{:S(2)}) collective-permute-start(bf16[4,8,48,128]{3,2,1,0:T(8,128)(2,1)S(1)} %get-tuple-element.57), channel_id=1, source_target_pairs={{0,4},{4,0},{8,12},{12,8},{1,5},{5,1},{9,13},{13,9},{2,6},{6,2},{1... | collective-permute-start | bytes 1179656 | tf_op jit(solution)/shard_map/ppermute | solution.py:326
  50.9 2.1 %shard_map.64.base_ref = f32[8,8,48,128]{3,2,1,0:T(8,128)S(1)} custom-call(f32[8,8,64,128]{3,2,1,0:T(8,128)S(1)} %get-tuple-element.65.refs_0_, bf16[8,4,48,128]{3,2,1,0:T(8,128)(2,1)S(1)} %collective-permute-done.17.refs_1_, bf16[8,8,48,256]{3,2,1,0:T(8,128)(2,1)S(1)} %copy-done.1, f32[128,128]{1,0:T(8,128)S(1)} %get-tuple-element.46.refs_3_.c_ref, ...), custom_call_target="tpu_custom_call" | custom-call | flops 1 | bytes 1 | tf_op jit(solution)/shard_map/pallas_call | solution.py:202
  54.7 1.6 %collective-permute-start.20 = (bf16[4,8,48,128]{3,2,1,0:T(8,128)(2,1)S(1)}, bf16[4,8,48,128]{3,2,1,0:T(8,128)(2,1)S(1)}, u32[]{:S(2)}, u32[]{:S(2)}) collective-permute-start(bf16[4,8,48,128]{3,2,1,0:T(8,128)(2,1)S(1)} %shard_map.65.refs_4_), channel_id=1, source_target_pairs={{0,2},{2,0},{1,3},{3,1},{4,6},{6,4},{5,7},{7,5},{8,10},{10,8},{9,1... | collective-permute-start | bytes 1179656 | tf_op jit(solution)/shard_map/ppermute | solution.py:326
  56.2 2.1 %shard_map.57.base_ref = f32[8,8,48,128]{3,2,1,0:T(8,128)S(1)} custom-call(f32[8,8,64,128]{3,2,1,0:T(8,128)S(1)} %get-tuple-element.54.refs_0_, bf16[8,4,48,128]{3,2,1,0:T(8,128)(2,1)S(1)} %collective-permute-done.6.refs_1_, bf16[8,8,48,256]{3,2,1,0:T(8,128)(2,1)S(1)} %copy-done.1, f32[128,128]{1,0:T(8,128)S(1)} %get-tuple-element.46.refs_3_.c_ref, ...), custom_call_target="tpu_custom_call" | custom-call | flops 1 | bytes 1 | tf_op jit(solution)/shard_map/pallas_call | solution.py:202
  58.4 3.8 %collective-permute-done.8.even_ref = bf16[4,8,48,128]{3,2,1,0:T(8,128)(2,1)S(1)} collective-permute-done((bf16[4,8,48,128]{3,2,1,0:T(8,128)(2,1)S(1)}, bf16[4,8,48,128]{3,2,1,0:T(8,128)(2,1)S(1)}, u32[]{:S(2)}, u32[]{:S(2)}) %collective-permute-start.8) | collective-permute-done | bytes 393248 | tf_op jit(solution)/shard_map/ppermute | solution.py:326
  62.5 1.6 %collective-permute-start.9 = (bf16[2,8,48,128]{3,2,1,0:T(8,128)(2,1)S(1)}, bf16[2,8,48,128]{3,2,1,0:T(8,128)(2,1)S(1)}, u32[]{:S(2)}, u32[]{:S(2)}) collective-permute-start(bf16[2,8,48,128]{3,2,1,0:T(8,128)(2,1)S(1)} %shard_map.58.refs_1_), channel_id=1, source_target_pairs={{0,2},{2,0},{1,3},{3,1},{4,6},{6,4},{5,7},{7,5},{8,10},{10,8},{9,1... | collective-permute-start | bytes 589832 | tf_op jit(solution)/shard_map/ppermute | solution.py:326
  68.3 1.8 %collective-permute-start.22 = (bf16[128,128]{1,0:T(8,128)(2,1)S(1)}, bf16[128,128]{1,0:T(8,128)(2,1)S(1)}, u32[]{:S(2)}, u32[]{:S(2)}) collective-permute-start(bf16[128,128]{1,0:T(8,128)(2,1)S(1)} %get-tuple-element.73), channel_id=1, source_target_pairs={{0,4},{4,0},{8,12},{12,8},{1,5},{5,1},{9,13},{13,9},{2,6},{6,2},{1... | collective-permute-start | bytes 98312 | tf_op jit(solution)/shard_map/ppermute | solution.py:620
  70.6 1.7 %collective-permute-done.22.refs_4_.inner_got_ref = bf16[128,128]{1,0:T(8,128)(2,1)S(1)} collective-permute-done((bf16[128,128]{1,0:T(8,128)(2,1)S(1)}, bf16[128,128]{1,0:T(8,128)(2,1)S(1)}, u32[]{:S(2)}, u32[]{:S(2)}) %collective-permute-start.22) | collective-permute-done | bytes 32800 | tf_op jit(solution)/shard_map/ppermute | solution.py:620
  73.9 1.4 %collective-permute-done.23.got_ref = f32[384,128]{1,0:T(8,128)S(1)} collective-permute-done((f32[384,128]{1,0:T(8,128)S(1)}, f32[384,128]{1,0:T(8,128)S(1)}, u32[]{:S(2)}, u32[]{:S(2)}) %collective-permute-start.23) | collective-permute-done | bytes 196640 | tf_op jit(solution)/shard_map/ppermute | solution.py:326
  75.4 1.6 %collective-permute-start.24 = (bf16[272,128]{1,0:T(8,128)(2,1)S(1)}, bf16[272,128]{1,0:T(8,128)(2,1)S(1)}, u32[]{:S(2)}, u32[]{:S(2)}) collective-permute-start(bf16[272,128]{1,0:T(8,128)(2,1)S(1)} %get-tuple-element.79), channel_id=1, source_target_pairs={{0,8},{4,12},{8,0},{12,4},{1,9},{5,13},{9,1},{13,5},{2,10},{6,14},... | collective-permute-start | bytes 208904 | tf_op jit(solution)/shard_map/ppermute | solution.py:625
  77.0 2.2 %collective-permute-start.25 = (bf16[144,128]{1,0:T(8,128)(2,1)S(1)}, bf16[144,128]{1,0:T(8,128)(2,1)S(1)}, u32[]{:S(2)}, u32[]{:S(2)}) collective-permute-start(bf16[144,128]{1,0:T(8,128)(2,1)S(1)} %get-tuple-element.80), channel_id=1, source_target_pairs={{0,12},{4,8},{8,4},{12,0},{1,13},{5,9},{9,5},{13,1},{2,14},{6,10},... | collective-permute-start | bytes 110600 | tf_op jit(solution)/shard_map/ppermute | solution.py:625
  79.3 3.6 %collective-permute-done.25.refs_1_ = bf16[144,128]{1,0:T(8,128)(2,1)S(1)} collective-permute-done((bf16[144,128]{1,0:T(8,128)(2,1)S(1)}, bf16[144,128]{1,0:T(8,128)(2,1)S(1)}, u32[]{:S(2)}, u32[]{:S(2)}) %collective-permute-start.25) | collective-permute-done | bytes 36896 | tf_op jit(solution)/shard_map/ppermute | solution.py:625
  83.7 1.5 %collective-permute-start.27 = (bf16[272,128]{1,0:T(8,128)(2,1)S(1)}, bf16[272,128]{1,0:T(8,128)(2,1)S(1)}, u32[]{:S(2)}, u32[]{:S(2)}) collective-permute-start(bf16[272,128]{1,0:T(8,128)(2,1)S(1)} %shard_map.73.mine_ref), channel_id=1, source_target_pairs={{0,2},{2,0},{1,3},{3,1},{4,6},{6,4},{5,7},{7,5},{8,10},{10,8},{9,1... | collective-permute-start | bytes 208904 | tf_op jit(solution)/shard_map/ppermute | solution.py:326
  85.2 2.9 %collective-permute-done.27.other_ref = bf16[272,128]{1,0:T(8,128)(2,1)S(1)} collective-permute-done((bf16[272,128]{1,0:T(8,128)(2,1)S(1)}, bf16[272,128]{1,0:T(8,128)(2,1)S(1)}, u32[]{:S(2)}, u32[]{:S(2)}) %collective-permute-start.27) | collective-permute-done | bytes 69664 | tf_op jit(solution)/shard_map/ppermute | solution.py:326
  (69 shorter events, 28.2 us)
Async XLA Ops:
  3.9 8.5 %collective-permute-start.11 = (bf16[8,4,48,128]{3,2,1,0:T(8,128)(2,1)S(1)}, bf16[8,4,48,128]{3,2,1,0:T(8,128)(2,1)S(1)}, u32[]{:S(2)}, u32[]{:S(2)}) collective-permute-start(bf16[8,4,48,128]{3,2,1,0:T(8,128)(2,1)S(1)} %get-tuple-element.58), channel_id=1, source_target_pairs={{0,1},{1,0},{2,3},{3,2},{4,5},{5,4},{6,7},{7,6},{8,9},{9,8},{10,11... | collective-permute-start | bytes 1179656 | tf_op jit(solution)/shard_map/ppermute | solution.py:326
  4.4 12.2 %collective-permute-start.12 = (bf16[4,8,48,128]{3,2,1,0:T(8,128)(2,1)S(1)}, bf16[4,8,48,128]{3,2,1,0:T(8,128)(2,1)S(1)}, u32[]{:S(2)}, u32[]{:S(2)}) collective-permute-start(bf16[4,8,48,128]{3,2,1,0:T(8,128)(2,1)S(1)} %get-tuple-element.59), channel_id=1, source_target_pairs={{4,8},{8,4},{5,9},{9,5},{6,10},{10,6},{7,11},{11,7},{20,24},{24,20... | collective-permute-start | bytes 1179656 | tf_op jit(solution)/shard_map/ppermute | solution.py:326
  5.1 15.4 %collective-permute-start.13 = (bf16[4,8,48,128]{3,2,1,0:T(8,128)(2,1)S(1)}, bf16[4,8,48,128]{3,2,1,0:T(8,128)(2,1)S(1)}, u32[]{:S(2)}, u32[]{:S(2)}) collective-permute-start(bf16[4,8,48,128]{3,2,1,0:T(8,128)(2,1)S(1)} %get-tuple-element.60), channel_id=1, source_target_pairs={{0,4},{4,0},{8,12},{12,8},{1,5},{5,1},{9,13},{13,9},{2,6},{6,2},{1... | collective-permute-start | bytes 1179656 | tf_op jit(solution)/shard_map/ppermute | solution.py:326
  11.6 10.6 %collective-permute-start = (bf16[8,4,48,128]{3,2,1,0:T(8,128)(2,1)S(1)}, bf16[8,4,48,128]{3,2,1,0:T(8,128)(2,1)S(1)}, u32[]{:S(2)}, u32[]{:S(2)}) collective-permute-start(bf16[8,4,48,128]{3,2,1,0:T(8,128)(2,1)S(1)} %get-tuple-element.44), channel_id=1, source_target_pairs={{0,1},{1,0},{2,3},{3,2},{4,5},{5,4},{6,7},{7,6},{8,9},{9,8},{10,11... | collective-permute-start | bytes 1179656 | tf_op jit(solution)/shard_map/ppermute | solution.py:326
  11.7 16.4 %collective-permute-start.1 = (bf16[4,8,48,128]{3,2,1,0:T(8,128)(2,1)S(1)}, bf16[4,8,48,128]{3,2,1,0:T(8,128)(2,1)S(1)}, u32[]{:S(2)}, u32[]{:S(2)}) collective-permute-start(bf16[4,8,48,128]{3,2,1,0:T(8,128)(2,1)S(1)} %get-tuple-element.48), channel_id=1, source_target_pairs={{4,8},{8,4},{5,9},{9,5},{6,10},{10,6},{7,11},{11,7},{20,24},{24,20... | collective-permute-start | bytes 1179656 | tf_op jit(solution)/shard_map/ppermute | solution.py:326
  12.4 16.5 %collective-permute-start.2 = (bf16[4,8,48,128]{3,2,1,0:T(8,128)(2,1)S(1)}, bf16[4,8,48,128]{3,2,1,0:T(8,128)(2,1)S(1)}, u32[]{:S(2)}, u32[]{:S(2)}) collective-permute-start(bf16[4,8,48,128]{3,2,1,0:T(8,128)(2,1)S(1)} %get-tuple-element.49), channel_id=1, source_target_pairs={{0,4},{4,0},{8,12},{12,8},{1,5},{5,1},{9,13},{13,9},{2,6},{6,2},{1... | collective-permute-start | bytes 1179656 | tf_op jit(solution)/shard_map/ppermute | solution.py:326
  21.4 9.2 %collective-permute-start.14 = (bf16[8,4,48,128]{3,2,1,0:T(8,128)(2,1)S(1)}, bf16[8,4,48,128]{3,2,1,0:T(8,128)(2,1)S(1)}, u32[]{:S(2)}, u32[]{:S(2)}) collective-permute-start(bf16[8,4,48,128]{3,2,1,0:T(8,128)(2,1)S(1)} %get-tuple-element.62), channel_id=1, source_target_pairs={{0,1},{1,0},{2,3},{3,2},{4,5},{5,4},{6,7},{7,6},{8,9},{9,8},{10,11... | collective-permute-start | bytes 1179656 | tf_op jit(solution)/shard_map/ppermute | solution.py:326
  21.5 14.7 %collective-permute-start.15 = (bf16[4,8,48,128]{3,2,1,0:T(8,128)(2,1)S(1)}, bf16[4,8,48,128]{3,2,1,0:T(8,128)(2,1)S(1)}, u32[]{:S(2)}, u32[]{:S(2)}) collective-permute-start(bf16[4,8,48,128]{3,2,1,0:T(8,128)(2,1)S(1)} %get-tuple-element.63), channel_id=1, source_target_pairs={{4,8},{8,4},{5,9},{9,5},{6,10},{10,6},{7,11},{11,7},{20,24},{24,20... | collective-permute-start | bytes 1179656 | tf_op jit(solution)/shard_map/ppermute | solution.py:326
  22.2 15.1 %collective-permute-start.16 = (bf16[4,8,48,128]{3,2,1,0:T(8,128)(2,1)S(1)}, bf16[4,8,48,128]{3,2,1,0:T(8,128)(2,1)S(1)}, u32[]{:S(2)}, u32[]{:S(2)}) collective-permute-start(bf16[4,8,48,128]{3,2,1,0:T(8,128)(2,1)S(1)} %get-tuple-element.64), channel_id=1, source_target_pairs={{0,4},{4,0},{8,12},{12,8},{1,5},{5,1},{9,13},{13,9},{2,6},{6,2},{1... | collective-permute-start | bytes 1179656 | tf_op jit(solution)/shard_map/ppermute | solution.py:326
  29.9 9.2 %collective-permute-start.3 = (bf16[8,4,48,128]{3,2,1,0:T(8,128)(2,1)S(1)}, bf16[8,4,48,128]{3,2,1,0:T(8,128)(2,1)S(1)}, u32[]{:S(2)}, u32[]{:S(2)}) collective-permute-start(bf16[8,4,48,128]{3,2,1,0:T(8,128)(2,1)S(1)} %get-tuple-element.51), channel_id=1, source_target_pairs={{0,1},{1,0},{2,3},{3,2},{4,5},{5,4},{6,7},{7,6},{8,9},{9,8},{10,11... | collective-permute-start | bytes 1179656 | tf_op jit(solution)/shard_map/ppermute | solution.py:326
  29.9 14.6 %collective-permute-start.4 = (bf16[4,8,48,128]{3,2,1,0:T(8,128)(2,1)S(1)}, bf16[4,8,48,128]{3,2,1,0:T(8,128)(2,1)S(1)}, u32[]{:S(2)}, u32[]{:S(2)}) collective-permute-start(bf16[4,8,48,128]{3,2,1,0:T(8,128)(2,1)S(1)} %get-tuple-element.52), channel_id=1, source_target_pairs={{4,8},{8,4},{5,9},{9,5},{6,10},{10,6},{7,11},{11,7},{20,24},{24,20... | collective-permute-start | bytes 1179656 | tf_op jit(solution)/shard_map/ppermute | solution.py:326
  30.6 15.1 %collective-permute-start.5 = (bf16[4,8,48,128]{3,2,1,0:T(8,128)(2,1)S(1)}, bf16[4,8,48,128]{3,2,1,0:T(8,128)(2,1)S(1)}, u32[]{:S(2)}, u32[]{:S(2)}) collective-permute-start(bf16[4,8,48,128]{3,2,1,0:T(8,128)(2,1)S(1)} %get-tuple-element.53), channel_id=1, source_target_pairs={{0,4},{4,0},{8,12},{12,8},{1,5},{5,1},{9,13},{13,9},{2,6},{6,2},{1... | collective-permute-start | bytes 1179656 | tf_op jit(solution)/shard_map/ppermute | solution.py:326
  38.3 9.2 %collective-permute-start.17 = (bf16[8,4,48,128]{3,2,1,0:T(8,128)(2,1)S(1)}, bf16[8,4,48,128]{3,2,1,0:T(8,128)(2,1)S(1)}, u32[]{:S(2)}, u32[]{:S(2)}) collective-permute-start(bf16[8,4,48,128]{3,2,1,0:T(8,128)(2,1)S(1)} %get-tuple-element.66), channel_id=1, source_target_pairs={{0,1},{1,0},{2,3},{3,2},{4,5},{5,4},{6,7},{7,6},{8,9},{9,8},{10,11... | collective-permute-start | bytes 1179656 | tf_op jit(solution)/shard_map/ppermute | solution.py:326
  38.4 14.7 %collective-permute-start.18 = (bf16[4,8,48,128]{3,2,1,0:T(8,128)(2,1)S(1)}, bf16[4,8,48,128]{3,2,1,0:T(8,128)(2,1)S(1)}, u32[]{:S(2)}, u32[]{:S(2)}) collective-permute-start(bf16[4,8,48,128]{3,2,1,0:T(8,128)(2,1)S(1)} %get-tuple-element.67), channel_id=1, source_target_pairs={{4,8},{8,4},{5,9},{9,5},{6,10},{10,6},{7,11},{11,7},{20,24},{24,20... | collective-permute-start | bytes 1179656 | tf_op jit(solution)/shard_map/ppermute | solution.py:326
  39.1 15.1 %collective-permute-start.19 = (bf16[4,8,48,128]{3,2,1,0:T(8,128)(2,1)S(1)}, bf16[4,8,48,128]{3,2,1,0:T(8,128)(2,1)S(1)}, u32[]{:S(2)}, u32[]{:S(2)}) collective-permute-start(bf16[4,8,48,128]{3,2,1,0:T(8,128)(2,1)S(1)} %get-tuple-element.68), channel_id=1, source_target_pairs={{0,4},{4,0},{8,12},{12,8},{1,5},{5,1},{9,13},{13,9},{2,6},{6,2},{1... | collective-permute-start | bytes 1179656 | tf_op jit(solution)/shard_map/ppermute | solution.py:326
  46.7 9.5 %collective-permute-start.6 = (bf16[8,4,48,128]{3,2,1,0:T(8,128)(2,1)S(1)}, bf16[8,4,48,128]{3,2,1,0:T(8,128)(2,1)S(1)}, u32[]{:S(2)}, u32[]{:S(2)}) collective-permute-start(bf16[8,4,48,128]{3,2,1,0:T(8,128)(2,1)S(1)} %get-tuple-element.55), channel_id=1, source_target_pairs={{0,1},{1,0},{2,3},{3,2},{4,5},{5,4},{6,7},{7,6},{8,9},{9,8},{10,11... | collective-permute-start | bytes 1179656 | tf_op jit(solution)/shard_map/ppermute | solution.py:326
  46.8 11.6 %collective-permute-start.7 = (bf16[4,8,48,128]{3,2,1,0:T(8,128)(2,1)S(1)}, bf16[4,8,48,128]{3,2,1,0:T(8,128)(2,1)S(1)}, u32[]{:S(2)}, u32[]{:S(2)}) collective-permute-start(bf16[4,8,48,128]{3,2,1,0:T(8,128)(2,1)S(1)} %get-tuple-element.56), channel_id=1, source_target_pairs={{4,8},{8,4},{5,9},{9,5},{6,10},{10,6},{7,11},{11,7},{20,24},{24,20... | collective-permute-start | bytes 1179656 | tf_op jit(solution)/shard_map/ppermute | solution.py:326
  47.5 14.7 %collective-permute-start.8 = (bf16[4,8,48,128]{3,2,1,0:T(8,128)(2,1)S(1)}, bf16[4,8,48,128]{3,2,1,0:T(8,128)(2,1)S(1)}, u32[]{:S(2)}, u32[]{:S(2)}) collective-permute-start(bf16[4,8,48,128]{3,2,1,0:T(8,128)(2,1)S(1)} %get-tuple-element.57), channel_id=1, source_target_pairs={{0,4},{4,0},{8,12},{12,8},{1,5},{5,1},{9,13},{13,9},{2,6},{6,2},{1... | collective-permute-start | bytes 1179656 | tf_op jit(solution)/shard_map/ppermute | solution.py:326
  54.7 15.4 %collective-permute-start.20 = (bf16[4,8,48,128]{3,2,1,0:T(8,128)(2,1)S(1)}, bf16[4,8,48,128]{3,2,1,0:T(8,128)(2,1)S(1)}, u32[]{:S(2)}, u32[]{:S(2)}) collective-permute-start(bf16[4,8,48,128]{3,2,1,0:T(8,128)(2,1)S(1)} %shard_map.65.refs_4_), channel_id=1, source_target_pairs={{0,2},{2,0},{1,3},{3,1},{4,6},{6,4},{5,7},{7,5},{8,10},{10,8},{9,1... | collective-permute-start | bytes 1179656 | tf_op jit(solution)/shard_map/ppermute | solution.py:326
  62.5 9.7 %collective-permute-start.9 = (bf16[2,8,48,128]{3,2,1,0:T(8,128)(2,1)S(1)}, bf16[2,8,48,128]{3,2,1,0:T(8,128)(2,1)S(1)}, u32[]{:S(2)}, u32[]{:S(2)}) collective-permute-start(bf16[2,8,48,128]{3,2,1,0:T(8,128)(2,1)S(1)} %shard_map.58.refs_1_), channel_id=1, source_target_pairs={{0,2},{2,0},{1,3},{3,1},{4,6},{6,4},{5,7},{7,5},{8,10},{10,8},{9,1... | collective-permute-start | bytes 589832 | tf_op jit(solution)/shard_map/ppermute | solution.py:326
  64.5 9.0 %collective-permute-start.10 = (bf16[2,8,48,128]{3,2,1,0:T(8,128)(2,1)S(1)}, bf16[2,8,48,128]{3,2,1,0:T(8,128)(2,1)S(1)}, u32[]{:S(2)}, u32[]{:S(2)}) collective-permute-start(bf16[2,8,48,128]{3,2,1,0:T(8,128)(2,1)S(1)} %shard_map.59.refs_2_), channel_id=1, source_target_pairs={{0,2},{2,0},{1,3},{3,1},{4,6},{6,4},{5,7},{7,5},{8,10},{10,8},{9,1... | collective-permute-start | bytes 589832 | tf_op jit(solution)/shard_map/ppermute | solution.py:326
  75.4 8.2 %collective-permute-start.24 = (bf16[272,128]{1,0:T(8,128)(2,1)S(1)}, bf16[272,128]{1,0:T(8,128)(2,1)S(1)}, u32[]{:S(2)}, u32[]{:S(2)}) collective-permute-start(bf16[272,128]{1,0:T(8,128)(2,1)S(1)} %get-tuple-element.79), channel_id=1, source_target_pairs={{0,8},{4,12},{8,0},{12,4},{1,9},{5,13},{9,1},{13,5},{2,10},{6,14},... | collective-permute-start | bytes 208904 | tf_op jit(solution)/shard_map/ppermute | solution.py:625
  77.0 5.9 %collective-permute-start.25 = (bf16[144,128]{1,0:T(8,128)(2,1)S(1)}, bf16[144,128]{1,0:T(8,128)(2,1)S(1)}, u32[]{:S(2)}, u32[]{:S(2)}) collective-permute-start(bf16[144,128]{1,0:T(8,128)(2,1)S(1)} %get-tuple-element.80), channel_id=1, source_target_pairs={{0,12},{4,8},{8,4},{12,0},{1,13},{5,9},{9,5},{13,1},{2,14},{6,10},... | collective-permute-start | bytes 110600 | tf_op jit(solution)/shard_map/ppermute | solution.py:625
  79.3 4.4 %collective-permute-start.26 = (bf16[144,128]{1,0:T(8,128)(2,1)S(1)}, bf16[144,128]{1,0:T(8,128)(2,1)S(1)}, u32[]{:S(2)}, u32[]{:S(2)}) collective-permute-start(bf16[144,128]{1,0:T(8,128)(2,1)S(1)} %get-tuple-element.81), channel_id=1, source_target_pairs={{0,4},{4,0},{8,12},{12,8},{1,5},{5,1},{9,13},{13,9},{2,6},{6,2},{1... | collective-permute-start | bytes 110600 | tf_op jit(solution)/shard_map/ppermute | solution.py:625
  (9 other events, 46.5 us)
